TPU v7x, 32 devices: a whole 2x2x4 slice. The times are simulated.
32 devices in a mesh: section: 2 (over x), tm: 4 (over y, core), mp: 4 (over z).
Axes of the slice: x: 2, y: 2, z: 4, core: 2. Of those that a mesh axis runs over, the one named last changes fastest.
Arguments:
- frame_len: int32 [4], replicated, may hold values from 64 to 256, as said below
- slot_utt: int32 [8], replicated, may hold values from -1 to 3, as said below
- enc_in: bfloat16 [256, 4, 1280], P(('section', 'tm')), may hold values from -42 to 42
- ffn_up: bfloat16 [1280, 5120], P(None, 'mp'), may hold values from -0.15625 to 0.15625
- ffn_down: bfloat16 [5120, 1280], P('mp'), may hold values from -0.078125 to 0.078125
- kv_proj: bfloat16 [1280, 1024], replicated, may hold values from -10 to 10
- hyp_state: bfloat16 [8, 8, 16, 4096], P('tm'), may hold values from -37 to 37
- hyp_tok: int32 [8, 8, 16], P('tm'), may hold values from 0 to 63999
- hyp_len: int32 [8, 8], P('tm'), may hold values from 1 to 16
- q_proj: bfloat16 [4096, 4096], P(None, ('section', 'mp')), may hold values from -0.75 to 0.75
- o_proj: bfloat16 [4096, 4096], P(('section', 'mp')), may hold values from -1 to 1
- head: bfloat16 [64000, 4096], P(('section', 'tm', 'mp')), may hold values from -45 to 45
Outputs:
- hyp_scores: float32 [8, 8], P('tm')
Inputs may be any that keep to these rules, and one draw needn't show every extreme that they name: `frame_len`: one utterance in every draw has all 256 frames. `slot_utt`: every one of the 4 utterances sits in exactly one slot; slots g * 2 to (g + 1) * 2 - 1 belong to group g, and at least one group has all 2 slots filled.
All inputs are finite; a program needn't handle non-finite values.
Results may differ from a plain program's by a relative error of at most 0.005.
The roundings to bfloat16 on the way count: a program that leaves them out, or rounds other values in their place, can miss the bound.
Values may be sent and summed in bfloat16 or wider, within the bound.
No kernel may reach another device: no remote copies, remote signals or barrier semaphores. Data moves between devices by JAX's collectives and lax.ppermute only.
A program may use at most 128 MiB of HBM per device.

v0:
```python
import math

import jax
import jax.numpy as jnp
from jax import lax
from jax.sharding import PartitionSpec as P

NH = 32
KVH = 4
HD = 128
V = 64000


def layer_norm(values):
    center = values - jnp.mean(values, axis=-1, keepdims=True)
    spread = jnp.mean(center * center, axis=-1, keepdims=True)
    return center * lax.rsqrt(spread + 1e-05)


def square_norm(values):
    return values * lax.rsqrt(jnp.mean(values * values, axis=-1, keepdims=True) + 1e-06)


def per_device(
    frame_len,
    slot_utt,
    enc_in,
    ffn_up,
    ffn_down,
    kv_proj,
    hyp_state,
    hyp_tok,
    hyp_len,
    q_proj,
    o_proj,
    head,
):
    section_count = lax.axis_size("section")
    group_count = lax.axis_size("tm")
    width_count = lax.axis_size("mp")
    section_pos = lax.axis_index("section")
    group_pos = lax.axis_index("tm")
    width_pos = lax.axis_index("mp")
    frame_rows = enc_in.shape[0]
    utterances = enc_in.shape[1]
    enc_width = enc_in.shape[2]
    frame_share = frame_rows // width_count
    share_count = frame_share * utterances
    enc_flat = enc_in.reshape(frame_rows * utterances, enc_width)
    enc_normed = layer_norm(enc_flat.astype(jnp.float32)).astype(jnp.bfloat16)
    enc_inner = jax.nn.gelu(
        jnp.dot(enc_normed, ffn_up, preferred_element_type=jnp.float32), approximate=False
    ).astype(jnp.bfloat16)
    enc_summed = lax.psum_scatter(
        jnp.dot(enc_inner, ffn_down, preferred_element_type=jnp.float32),
        "mp",
        scatter_dimension=0,
        tiled=True,
    )
    own_frames = lax.dynamic_slice_in_dim(enc_flat, width_pos * share_count, share_count, 0)
    enc_states = layer_norm(own_frames.astype(jnp.float32) + enc_summed).astype(jnp.bfloat16)
    slot_total = slot_utt.shape[0]
    slot_count = slot_total // group_count
    chooser = (slot_utt[:, None] == jnp.arange(utterances, dtype=jnp.int32)[None, :]).astype(
        jnp.bfloat16
    )
    head_devices = section_count * width_count
    device_heads = q_proj.shape[1] // HD
    group_heads = NH // KVH
    head_pos = section_pos * width_count + width_pos
    kv_index = head_pos * device_heads // group_heads
    all_devices = section_count * group_count * width_count
    picked = jnp.einsum(
        "su,fud->sfd",
        chooser,
        enc_states.reshape(frame_share, utterances, enc_width),
        preferred_element_type=jnp.float32,
    ).astype(jnp.bfloat16)
    spread_out = jnp.broadcast_to(
        picked.reshape(1, group_count, 1, slot_count, frame_share, enc_width),
        (section_count, group_count, width_count, slot_count, frame_share, enc_width),
    )
    spread_out = spread_out.reshape(all_devices, slot_count, frame_share, enc_width)
    arrived = lax.all_to_all(
        spread_out, ("section", "tm", "mp"), split_axis=0, concat_axis=2, tiled=True
    )
    frames_all = arrived.shape[2]
    key_weights = lax.dynamic_slice_in_dim(kv_proj, kv_index * HD, HD, 1)
    value_weights = lax.dynamic_slice_in_dim(kv_proj, KVH * HD + kv_index * HD, HD, 1)
    both_weights = jnp.concatenate([key_weights, value_weights], 1)
    keys_values = jnp.dot(
        arrived.reshape(slot_count * frames_all, enc_width),
        both_weights,
        preferred_element_type=jnp.float32,
    ).astype(jnp.bfloat16)
    keys_values = keys_values.reshape(slot_count, frames_all, 2 * HD)
    here_slots = lax.dynamic_slice_in_dim(slot_utt, group_pos * slot_count, slot_count, 0)
    frame_limit = jnp.take(frame_len, jnp.maximum(here_slots, 0))
    hyp_count = hyp_state.shape[1]
    positions = hyp_state.shape[2]
    model_width = hyp_state.shape[3]
    slot_tokens = hyp_count * positions
    group_tokens = slot_count * slot_tokens
    dec_rows = hyp_state.reshape(group_tokens, model_width).astype(jnp.float32)
    queries = jnp.dot(
        square_norm(dec_rows).astype(jnp.bfloat16), q_proj, preferred_element_type=jnp.float32
    ).astype(jnp.bfloat16)
    queries = queries.reshape(slot_count, slot_tokens, device_heads, HD)
    scores = jnp.einsum(
        "sqhd,sfd->shqf", queries, keys_values[:, :, :HD], preferred_element_type=jnp.float32
    ) / math.sqrt(HD)
    visible = jnp.arange(frames_all, dtype=jnp.int32)[None, :] < frame_limit[:, None]
    scores = jnp.where(visible[:, None, None, :], scores, -jnp.inf)
    weights = jax.nn.softmax(scores, axis=-1).astype(jnp.bfloat16)
    context = jnp.einsum(
        "shqf,sfd->sqhd", weights, keys_values[:, :, HD:], preferred_element_type=jnp.float32
    ).astype(jnp.bfloat16)
    context = context.reshape(group_tokens, device_heads * HD)
    targets = hyp_tok.reshape(group_tokens)
    vocab_rows = head.shape[0]
    vocab_start = ((section_pos * group_count + group_pos) * width_count + width_pos) * vocab_rows
    share_rows = group_tokens // head_devices
    attn_out = lax.psum_scatter(
        jnp.dot(context, o_proj, preferred_element_type=jnp.float32).astype(jnp.bfloat16),
        ("section", "mp"),
        scatter_dimension=0,
        tiled=True,
    ).astype(jnp.float32)
    first_row = head_pos * share_rows
    out_normed = square_norm(
        lax.dynamic_slice_in_dim(dec_rows, first_row, share_rows, 0) + attn_out
    ).astype(jnp.bfloat16)
    own_targets = lax.dynamic_slice_in_dim(targets, first_row, share_rows, 0)
    hidden_rows = lax.all_gather(out_normed, ("section", "tm", "mp"), axis=0, tiled=True)
    target_rows = lax.all_gather(own_targets, ("section", "tm", "mp"), axis=0, tiled=True)
    logits = lax.dot_general(
        hidden_rows, head, (((1,), (1,)), ((), ())), preferred_element_type=jnp.float32
    )
    upper = jnp.max(logits, axis=1)
    totals = jnp.sum(jnp.exp(logits - upper[:, None]), axis=1)
    matches = (
        jnp.arange(vocab_rows, dtype=jnp.int32)[None, :] == (target_rows - vocab_start)[:, None]
    )
    target_logit = jnp.sum(jnp.where(matches, logits, 0.0), axis=1)
    stats = (upper, totals, target_logit)
    peak = lax.pmax(stats[0], ("section", "tm", "mp"))
    rescaled = stats[1] * jnp.exp(stats[0] - peak)
    sums = lax.psum((rescaled, stats[2]), ("section", "tm", "mp"))
    token_logp = sums[1] - (peak + jnp.log(sums[0]))
    arranged_logp = token_logp.reshape(section_count, group_count, width_count, share_rows)
    own_logp = lax.dynamic_index_in_dim(arranged_logp, group_pos, 1, keepdims=False).reshape(
        group_tokens
    )
    own_logp = own_logp.reshape(slot_count, hyp_count, positions)
    valid = jnp.arange(positions, dtype=jnp.int32)[None, None, :] < hyp_len[:, :, None]
    summed = jnp.sum(jnp.where(valid, own_logp, 0.0), axis=-1) / hyp_len.astype(
        jnp.float32
    ) + math.log(V)
    return jnp.where(here_slots[:, None] >= 0, summed, 0.0)


def solution(mesh):
    in_specs = (
        P(),
        P(),
        P(("section", "tm"), None, None),
        P(None, "mp"),
        P("mp", None),
        P(),
        P("tm", None, None, None),
        P("tm", None, None),
        P("tm", None),
        P(None, ("section", "mp")),
        P(("section", "mp"), None),
        P(("section", "tm", "mp"), None),
    )
    out_specs = P("tm", None)
    return jax.shard_map(
        per_device, mesh=mesh, in_specs=in_specs, out_specs=out_specs, check_vma=False
    )
```

profile of v0, /device:TPU:0, one launch (start us, length us, event | category | flops | bytes accessed | tf_op | source)
XLA Modules:
  0.0 351.9 jit_solution(3198846463667778861)
XLA Ops:
  6.5 0.0 copy-start
  6.5 0.0 reduce-scatter.3.cloned.1.call-start
  6.5 1.9 reshape.149
  8.5 1.2 convert_reduce_fusion
  9.7 1.3 fusion.10
  11.0 0.1 div.52
  11.1 0.1 rsqrt.39
  11.2 0.0 copy-done
  11.2 0.0 copy-start.8
  11.2 5.3 %fusion.24 = f32[128,1280]{1,0:T(8,128)} fusion(bf16[1280,1280]{1,0:T(8,128)(2,1)S(1)} %copy-done, bf16[1280,1280]{1,0:T(8,128)(2,1)} %param.15, bf16[128,1280]{1,0:T(8,128)(2,1)} %reshape.149, f32[128]{0:T(128)S(1)} %rsqrt.39, f32[128]{0:T(128)S(1)} %div.52), kind=kOutput, calls=%fused_computation.51 | convolution fusion | flops 850165760 | bytes 7537664 | tf_op jit(solution)/shard_map/dot_general | solution.py:55
  16.6 0.0 reduce-scatter.3.cloned.1.call-update
  16.6 2.2 multiply_reduce_fusion
  18.8 22.8 %reduce-scatter.3.cloned.1.call-done = f32[32,1280]{1,0:T(8,128)} async-done(((f32[128,1280]{1,0:T(8,128)}), f32[32,1280]{1,0:T(8,128)}) %reduce-scatter.3.cloned.1.call-update) | async-done | bytes 163856 | tf_op jit(solution)/shard_map/reduce_scatter | solution.py:54
  41.6 1.1 fusion.66
  42.7 1.2 multiply_reduce_fusion.2
  43.9 1.1 multiply_convert_fusion.11
  45.0 0.0 copy-done.8
  45.0 0.2 convolution_convert_fusion.1
  45.3 1.2 broadcast_in_dim.38
  46.5 3.6 %all-to-all-start = ((bf16[32,2,8,1280]{3,2,1,0:T(8,128)(2,1)}), bf16[32,2,8,1280]{3,2,1,0:T(8,128)(2,1)}, u32[]{:S(2)}, u32[]{:S(2)}) async-start(bf16[32,2,8,1280]{3,2,1,0:T(8,128)(2,1)} %bitcast.50), calls=%async_computation.1 | async-start | bytes 2621440 | tf_op jit(solution)/shard_map/all_to_all | solution.py:84
  50.1 0.0 reduce-scatter.5.cloned.1.call-start
  50.2 0.1 rsqrt.42
  50.2 0.0 copy-done.4
  50.2 0.6 bitcast_convert_fusion
  50.9 0.0 copy-start.3
  50.9 2.1 copy-done.3
  53.0 0.9 copy-done.5
  54.0 1.3 fusion.7
  55.2 0.1 reshape.154
  55.3 0.1 broadcast_maximum_fusion
  55.4 0.0 copy-done.2
  55.4 0.6 gather_fusion
  56.1 0.1 compare_select_fusion
  56.1 0.1 iota_compare_fusion.2
  56.2 1.1 constant_dynamic-slice_fusion.2
  57.3 23.2 %all-to-all-done = bf16[32,2,8,1280]{3,2,1,0:T(8,128)(2,1)} async-done(((bf16[32,2,8,1280]{3,2,1,0:T(8,128)(2,1)}), bf16[32,2,8,1280]{3,2,1,0:T(8,128)(2,1)}, u32[]{:S(2)}, u32[]{:S(2)}) %all-to-all-start) | async-done | bytes 1310752 | tf_op jit(solution)/shard_map/all_to_all | solution.py:84
  80.6 1.4 copy.23
  82.0 0.5 convolution_convert_fusion.2
  82.5 0.3 fusion.6
  82.8 0.5 fusion.104
  83.3 0.4 fusion.8
  83.7 0.2 copy.27
  83.9 4.8 %convolution_convert_fusion = bf16[256,4096]{1,0:T(8,128)(2,1)} fusion(bf16[512,4096]{1,0:T(8,128)(2,1)} %param.22, bf16[32,8,4,128]{3,2,1,0:T(4,128)(2,1)S(1)} %bitcast.53), kind=kOutput, calls=%fused_computation.5 | convolution fusion | flops 1074790400 | bytes 6553600 | tf_op jit(solution)/shard_map/dot_general | solution.py:124
  88.7 0.0 reduce-scatter.5.cloned.1.call-update
  88.7 0.0 all-gather.2.cloned.1.call-start
  88.8 67.7 %reduce-scatter.5.cloned.1.call-done = bf16[32,4096]{1,0:T(8,128)(2,1)} async-done(((bf16[256,4096]{1,0:T(8,128)(2,1)}), bf16[32,4096]{1,0:T(8,128)(2,1)}) %reduce-scatter.5.cloned.1.call-update) | async-done | bytes 262160 | tf_op jit(solution)/shard_map/reduce_scatter | solution.py:123
  156.4 1.3 multiply_reduce_fusion.1
  157.7 1.9 multiply_convert_fusion.5
  159.7 0.0 all-gather.2.cloned.1.call-update
  159.7 0.0 copy-done.6
  159.7 0.1 reshape.148
  159.8 0.2 dynamic-slice_dynamic-update-slice_fusion
  160.0 40.3 %all-reduce = s32[1024]{0:T(1024)S(1)} all-reduce(s32[1024]{0:T(1024)S(1)} %dynamic-slice_dynamic-update-slice_fusion), channel_id=1, replica_groups=mesh['section'=2,'tm'=4,'mp'=4] {'section','tm','mp'}, use_global_device_ids=true, to_apply=%add | all-reduce | flops 1024 | bytes 8192
  200.3 0.1 broadcast_compare_fusion
  200.3 36.2 %all-gather.2.cloned.1.call-done = bf16[1024,4096]{1,0:T(8,128)(2,1)} async-done(((bf16[32,4096]{1,0:T(8,128)(2,1)}), bf16[1024,4096]{1,0:T(8,128)(2,1)}) %all-gather.2.cloned.1.call-update) | async-done | bytes 8388624 | tf_op jit(solution)/shard_map/all_gather | solution.py:134
  236.5 24.0 %fusion.107 = (f32[1024]{0:T(1024)S(1)}, f32[1024,2000]{0,1:T(8,128)}) fusion(bf16[1024,4096]{1,0:T(8,128)(2,1)} %all-gather.2.cloned.1.call-done, bf16[2000,4096]{1,0:T(8,128)(2,1)} %param.23), kind=kOutput, calls=%fused_computation.154 | convolution fusion | flops 16779262976 | bytes 32968704 | tf_op jit(solution)/shard_map/dot_general | solution.py:136
  260.5 39.2 %pmax.7 = f32[1024]{0:T(1024)S(1)} all-reduce(f32[1024]{0:T(1024)S(1)} %get-tuple-element.11), channel_id=1, replica_groups=mesh['section'=2,'tm'=4,'mp'=4] {'section','tm','mp'}, use_global_device_ids=true, to_apply=%region_13.14 | all-reduce | flops 1024 | bytes 8192 | tf_op jit(solution)/shard_map/pmax | solution.py:146
  299.7 4.5 %exponential_reduce_fusion = (f32[1024]{0:T(1024)S(1)}, f32[1024]{0:T(1024)S(1)}) fusion(f32[1024,2000]{0,1:T(8,128)} %get-tuple-element.12, f32[1024]{0:T(1024)S(1)} %get-tuple-element.11, s32[1024]{0:T(1024)S(1)} %broadcast_subtract_fusion), kind=kLoop, calls=%fused_computation.2 | loop fusion | flops 10237952 | bytes 8208384 | tf_op jit(solution)/shard_map/reduce_sum | solution.py:140
  304.3 40.1 %all-reduce.1 = (f32[1024]{0:T(1024)S(1)}, f32[1024]{0:T(1024)S(1)}) all-reduce(f32[1024]{0:T(1024)S(1)} %get-tuple-element.6, f32[1024]{0:T(1024)S(1)} %exponential_multiply_fusion), channel_id=1, replica_groups=mesh['section'=2,'tm'=4,'mp'=4] {'section','tm','mp'}, use_global_device_ids=true, to_apply=%region_11.12 | all-reduce | flops 2048 | bytes 16384 | tf_op jit(solution)/shard_map/psum | solution.py:148
  344.4 0.1 reshape.156
  344.5 0.1 reshape_reshape.3
  344.6 0.0 copy-done.7
  344.6 0.2 select_reduce_fusion.1
  344.7 0.6 add_select_fusion
  (21 shorter events, 0.1 us)
Async XLA Ops:
  6.5 4.7 %copy-start = (bf16[1280,1280]{1,0:T(8,128)(2,1)S(1)}, bf16[1280,1280]{1,0:T(8,128)(2,1)}, u32[]{:S(2)}) copy-start(bf16[1280,1280]{1,0:T(8,128)(2,1)} %param.16) | copy-start | bytes 9830404
  6.5 35.1 %reduce-scatter.3.cloned.1.call-start = ((), (), s32[]{:S(2)}) async-start(), calls=%async_computation.3 | async-start | bytes 819200 | tf_op jit(solution)/shard_map/reduce_scatter | solution.py:54
  11.2 33.8 %copy-start.8 = (s32[8]{0:T(128)S(1)}, s32[8]{0:T(128)}, u32[]{:S(2)}) copy-start(s32[8]{0:T(128)} %param.13) | copy-start | bytes 100
  16.6 33.7 %copy-start.4 = (bf16[2,8,16,4096]{3,2,1,0:T(8,128)(2,1)S(1)}, bf16[2,8,16,4096]{3,2,1,0:T(8,128)(2,1)}, u32[]{:S(2)}) copy-start(bf16[2,8,16,4096]{3,2,1,0:T(8,128)(2,1)} %param.18) | copy-start | bytes 6291460
  46.5 34.1 %all-to-all-start = ((bf16[32,2,8,1280]{3,2,1,0:T(8,128)(2,1)}), bf16[32,2,8,1280]{3,2,1,0:T(8,128)(2,1)}, u32[]{:S(2)}, u32[]{:S(2)}) async-start(bf16[32,2,8,1280]{3,2,1,0:T(8,128)(2,1)} %bitcast.50), calls=%async_computation.1 | async-start | bytes 2621440 | tf_op jit(solution)/shard_map/all_to_all | solution.py:84
  50.1 106.4 %reduce-scatter.5.cloned.1.call-start = ((), (), s32[]{:S(2)}) async-start(), calls=%async_computation.4 | async-start | bytes 2359296 | tf_op jit(solution)/shard_map/reduce_scatter | solution.py:123
  50.2 3.7 %copy-start.5 = (bf16[4096,512]{1,0:T(8,128)(2,1)S(1)}, bf16[4096,512]{1,0:T(8,128)(2,1)}, u32[]{:S(2)}) copy-start(bf16[4096,512]{1,0:T(8,128)(2,1)} %param.21) | copy-start | bytes 12582916
  50.9 2.1 copy-start.3
  53.9 1.5 copy-start.2
  88.7 71.0 %copy-start.6 = (s32[2,8,16]{2,1,0:T(8,128)S(1)}, s32[2,8,16]{2,1,0:T(8,128)}, u32[]{:S(2)}) copy-start(s32[2,8,16]{2,1,0:T(8,128)} %param.19) | copy-start | bytes 3076
  88.7 147.8 %all-gather.2.cloned.1.call-start = ((), (), s32[]{:S(2)}) async-start(), calls=%async_computation.5 | async-start | bytes 8650752 | tf_op jit(solution)/shard_map/all_gather | solution.py:134
  236.5 108.8 %copy-start.1 = (bf16[1280,1280]{1,0:T(8,128)(2,1)S(1)}, bf16[1280,1280]{1,0:T(8,128)(2,1)}, u32[]{:S(2)}) copy-start(bf16[1280,1280]{1,0:T(8,128)(2,1)} %param.16) | copy-start | bytes 9830404
  260.5 84.0 %copy-start.7 = (s32[2,8]{1,0:T(2,128)S(1)}, s32[2,8]{1,0:T(2,128)}, u32[]{:S(2)}) copy-start(s32[2,8]{1,0:T(2,128)} %param.20) | copy-start | bytes 196
Sparse Core Ops, SparseCore 0:
  16.7 24.8 reduce-scatter.2
  88.8 67.5 reduce-scatter.4
  159.8 76.6 all-gather.1
where the time goes:
time: 353 us; the launch traced here: 352 us
  waiting for transfers between devices  150 us (42%)
  blocking collectives  120 us (34%)
  matrix products  37.3 us (11%)
  other arithmetic  17.6 us (5%)
  between operations  13.4 us (4%)
  local copies, waits for them, and re-layouts  10.4 us (3%)
  starting transfers between devices  3.66 us (1%)
    reduce_scatter x1, waiting for transfers between devices, per_device(): lax.psum_scatter(jnp.dot(context, o_proj, preferred_element_type=jnp.floa...  67.7 us
    unnamed x1, blocking collectives  40.3 us
    psum x1, blocking collectives, per_device(): sums = lax.psum((rescaled, stats[2]), ('section', 'tm', 'mp'))  40.1 us
    pmax x1, blocking collectives, per_device(): peak = lax.pmax(stats[0], ('section', 'tm', 'mp'))  39.2 us
    all_gather x1, waiting for transfers between devices, per_device(): lax.all_gather(out_normed, ('section', 'tm', 'mp'), axis=0, tiled=True)  36.2 us
    dot_general x1, matrix products, per_device(): lax.dot_general(hidden_rows, head, (((1,), (1,)), ((), ())), preferred_el...  24 us
    all_to_all x1, waiting for transfers between devices, per_device(): lax.all_to_all(spread_out, ('section', 'tm', 'mp'), split_axis=0, concat_...  23.2 us
    reduce_scatter x1, waiting for transfers between devices, per_device(): lax.psum_scatter(jnp.dot(enc_inner, ffn_down, preferred_element_type=jnp....  22.8 us
  transfers between devices with their start and end apart: 4, of which 4 were waited for; matrix products, arithmetic and copies ran while one was open for 2% of the time, Pallas kernels for 0%

commit v1 on v0

v1 whole, which is shorter than its diff:
```python
import math

import jax
import jax.numpy as jnp
from jax import lax
from jax.sharding import PartitionSpec as P

NH = 32
KVH = 4
HD = 128
V = 64000
ALL = ("section", "tm", "mp")


def layer_norm(values):
    center = values - jnp.mean(values, axis=-1, keepdims=True)
    spread = jnp.mean(center * center, axis=-1, keepdims=True)
    return center * lax.rsqrt(spread + 1e-05)


def square_norm(values):
    return values * lax.rsqrt(jnp.mean(values * values, axis=-1, keepdims=True) + 1e-06)


def exchange(blocks, axis):
    return lax.all_to_all(blocks, axis, split_axis=0, concat_axis=0, tiled=True)


def scatter_sum(partial, axis, count):
    blocks = partial.reshape((count, partial.shape[0] // count) + partial.shape[1:])
    return jnp.sum(exchange(blocks, axis).astype(jnp.float32), axis=0)


def per_device(
    frame_len,
    slot_utt,
    enc_in,
    ffn_up,
    ffn_down,
    kv_proj,
    hyp_state,
    hyp_tok,
    hyp_len,
    q_proj,
    o_proj,
    head,
):
    section_count = lax.axis_size("section")
    group_count = lax.axis_size("tm")
    width_count = lax.axis_size("mp")
    section_pos = lax.axis_index("section")
    group_pos = lax.axis_index("tm")
    width_pos = lax.axis_index("mp")
    head_devices = section_count * width_count
    head_pos = section_pos * width_count + width_pos
    all_devices = head_devices * group_count

    frame_rows, utterances, enc_width = enc_in.shape
    assert utterances == group_count
    slot_count, hyp_count, positions, model_width = hyp_state.shape
    slot_tokens = hyp_count * positions
    device_heads = q_proj.shape[1] // HD
    group_heads = NH // KVH
    frame_share = frame_rows // width_count
    share_rows = slot_tokens // head_devices
    here_slots = lax.dynamic_slice_in_dim(slot_utt, group_pos * slot_count, slot_count, 0)

    dec_rows = hyp_state.reshape(slot_count * slot_tokens, model_width).astype(jnp.float32)
    queries = jnp.dot(
        square_norm(dec_rows).astype(jnp.bfloat16), q_proj, preferred_element_type=jnp.float32
    ).astype(jnp.bfloat16)
    queries = queries.reshape(slot_count, slot_tokens, device_heads * HD)
    shares = lax.dynamic_slice_in_dim(
        hyp_state.reshape(slot_count, slot_tokens, model_width), head_pos * share_rows, share_rows, 1
    )

    def by_utterance(values):
        out = []
        for utterance in range(utterances):
            block = values[0]
            for slot in range(1, slot_count):
                block = jnp.where(here_slots[slot] == utterance, values[slot], block)
            out.append(block)
        return jnp.stack(out)

    own_slot = jnp.argmax(slot_utt == group_pos)
    from_group = own_slot // slot_count
    queries = lax.dynamic_index_in_dim(
        exchange(by_utterance(queries), "tm"), from_group, 0, keepdims=False
    )
    resid_rows = lax.dynamic_index_in_dim(
        exchange(by_utterance(shares), "tm"), from_group, 0, keepdims=False
    )
    slot_targets = lax.all_gather(
        hyp_tok.reshape(slot_count, slot_tokens), "tm", axis=0, tiled=True
    )
    utt_slots = jnp.argmax(slot_utt[None, :] == jnp.arange(utterances)[:, None], axis=1)
    targets = jnp.take(slot_targets, utt_slots, axis=0).reshape(utterances * slot_tokens)

    enc_flat = (
        enc_in.reshape(width_count, frame_share, utterances, enc_width)
        .transpose(0, 2, 1, 3)
        .reshape(frame_rows * utterances, enc_width)
    )
    share_count = frame_share * utterances
    enc_normed = layer_norm(enc_flat.astype(jnp.float32)).astype(jnp.bfloat16)
    enc_inner = jax.nn.gelu(
        jnp.dot(enc_normed, ffn_up, preferred_element_type=jnp.float32), approximate=False
    ).astype(jnp.bfloat16)
    enc_summed = scatter_sum(
        jnp.dot(enc_inner, ffn_down, preferred_element_type=jnp.float32).astype(jnp.bfloat16),
        "mp",
        width_count,
    )
    own_frames = lax.dynamic_slice_in_dim(enc_flat, width_pos * share_count, share_count, 0)
    enc_states = layer_norm(own_frames.astype(jnp.float32) + enc_summed).astype(jnp.bfloat16)
    keys_values = jnp.dot(enc_states, kv_proj, preferred_element_type=jnp.float32).astype(
        jnp.bfloat16
    )
    keys_values = keys_values.reshape(utterances, frame_share, 2, KVH, HD)
    sent = []
    for section in range(section_count):
        per_width = []
        for width in range(width_count):
            kv_head = (section * width_count + width) * device_heads // group_heads
            per_width.append(
                keys_values[:, :, :, kv_head].reshape(utterances, frame_share, 2 * HD)
            )
        sent.append(jnp.stack(per_width, axis=1))
    sent = jnp.stack(sent).reshape(all_devices, frame_share, 2 * HD)
    frames_all = all_devices * frame_share
    keys_values = exchange(sent, ALL).reshape(frames_all, 2 * HD)

    frame_limit = lax.dynamic_index_in_dim(frame_len, group_pos, 0, keepdims=False)
    queries = queries.reshape(slot_tokens, device_heads, HD)
    scores = jnp.einsum(
        "qhd,fd->hqf", queries, keys_values[:, :HD], preferred_element_type=jnp.float32
    ) / math.sqrt(HD)
    visible = jnp.arange(frames_all, dtype=jnp.int32) < frame_limit
    scores = jnp.where(visible[None, None, :], scores, -jnp.inf)
    weights = jax.nn.softmax(scores, axis=-1).astype(jnp.bfloat16)
    context = jnp.einsum(
        "hqf,fd->qhd", weights, keys_values[:, HD:], preferred_element_type=jnp.float32
    ).astype(jnp.bfloat16)
    partial = jnp.dot(
        context.reshape(slot_tokens, device_heads * HD), o_proj, preferred_element_type=jnp.float32
    ).astype(jnp.bfloat16)
    partial = scatter_sum(partial, "section", section_count).astype(jnp.bfloat16)
    attn_out = scatter_sum(partial, "mp", width_count)
    out_normed = square_norm(resid_rows.astype(jnp.float32) + attn_out).astype(jnp.bfloat16)

    hidden_rows = lax.all_gather(out_normed, ALL, axis=0, tiled=True)
    logits = lax.dot_general(
        hidden_rows, head, (((1,), (1,)), ((), ())), preferred_element_type=jnp.float32
    )
    vocab_rows = head.shape[0]
    vocab_start = (
        (section_pos * group_count + group_pos) * width_count + width_pos
    ) * vocab_rows
    target_rows = (
        targets.reshape(utterances, section_count, width_count, share_rows)
        .transpose(1, 0, 2, 3)
        .reshape(-1)
    )
    upper = jnp.max(logits, axis=1)
    totals = jnp.sum(jnp.exp(logits - upper[:, None]), axis=1)
    matches = (
        jnp.arange(vocab_rows, dtype=jnp.int32)[None, :] == (target_rows - vocab_start)[:, None]
    )
    target_logit = jnp.sum(jnp.where(matches, logits, 0.0), axis=1)

    stats = jnp.stack([upper, totals, target_logit])
    stats = stats.reshape(3, section_count, utterances, width_count, share_rows)
    stats = stats.transpose(2, 0, 1, 3, 4).reshape(utterances, 3, slot_tokens)
    by_slot = jnp.take(stats, jnp.maximum(slot_utt, 0), axis=0)
    by_group = by_slot.reshape(1, group_count, 1, slot_count, 3, slot_tokens)
    by_group = jnp.broadcast_to(
        by_group, (section_count, group_count, width_count, slot_count, 3, slot_tokens)
    ).reshape(all_devices, slot_count, 3, slot_tokens)
    every = exchange(by_group, ALL)
    peak = jnp.max(every[:, :, 0], axis=0)
    total = jnp.sum(every[:, :, 1] * jnp.exp(every[:, :, 0] - peak[None]), axis=0)
    picked = jnp.sum(every[:, :, 2], axis=0)
    token_logp = (picked - (peak + jnp.log(total))).reshape(slot_count, hyp_count, positions)
    valid = jnp.arange(positions, dtype=jnp.int32)[None, None, :] < hyp_len[:, :, None]
    summed = jnp.sum(jnp.where(valid, token_logp, 0.0), axis=-1) / hyp_len.astype(
        jnp.float32
    ) + math.log(V)
    return jnp.where(here_slots[:, None] >= 0, summed, 0.0)


def solution(mesh):
    in_specs = (
        P(),
        P(),
        P(("section", "tm"), None, None),
        P(None, "mp"),
        P("mp", None),
        P(),
        P("tm", None, None, None),
        P("tm", None, None),
        P("tm", None),
        P(None, ("section", "mp")),
        P(("section", "mp"), None),
        P(("section", "tm", "mp"), None),
    )
    out_specs = P("tm", None)
    return jax.shard_map(
        per_device, mesh=mesh, in_specs=in_specs, out_specs=out_specs, check_vma=False
    )
```

time: 353 us -> 221 us (0.63)
  blocking collectives: 120 us -> 16.1 us
  waiting for transfers between devices: 150 us -> 91.5 us
  starting transfers between devices: 3.66 us -> 28.4 us
  other arithmetic: 17.6 us -> 26 us
  between operations: 13.4 us -> 18.8 us
  matrix products: 37.3 us -> 32.5 us
    reduce_scatter x2 -> x0, waiting for transfers between devices: 90.5 us -> none  [the longest x1 67.7 us: per_device(): lax.psum_scatter(jnp.dot(context, o_proj, preferred_element_type=jnp.floa...]
    unnamed x1 -> x0, blocking collectives: 40.3 us -> none
    psum x1 -> x0, blocking collectives: 40.1 us -> none  [per_device(): sums = lax.psum((rescaled, stats[2]), ('section', 'tm', 'mp'))]
    pmax x1 -> x0, blocking collectives: 39.2 us -> none  [per_device(): peak = lax.pmax(stats[0], ('section', 'tm', 'mp'))]
    all_to_all x1 -> x6, starting transfers between devices: 3.58 us -> 28.4 us  [exchange(): return lax.all_to_all(blocks, axis, split_axis=0, concat_axis=0, tiled=True)]
    all_gather x1, waiting for transfers between devices: 36.2 us -> 53.7 us  [per_device(): hidden_rows = lax.all_gather(out_normed, ALL, axis=0, tiled=True)]
    all_to_all x1 -> x6, waiting for transfers between devices: 23.2 us -> 37.8 us  [exchange(): return lax.all_to_all(blocks, axis, split_axis=0, concat_axis=0, tiled=True)]
    all_to_all x0 -> x1, blocking collectives: none -> 10.9 us  [exchange(): return lax.all_to_all(blocks, axis, split_axis=0, concat_axis=0, tiled=True)]
  transfers between devices with their start and end apart: 4 -> 7, of which waited for: 4 -> 6; matrix products, arithmetic and copies ran while one was open for 2% -> 10% of each run, Pallas kernels for 0% -> 0%
where the time goes in v1:
time: 221 us; the launch traced here: 220 us
  waiting for transfers between devices  91.5 us (41%)
  matrix products  32.5 us (15%)
  starting transfers between devices  28.4 us (13%)
  other arithmetic  26 us (12%)
  between operations  18.8 us (9%)
  blocking collectives  16.1 us (7%)
  local copies, waits for them, and re-layouts  6.91 us (3%)
    all_gather x1, waiting for transfers between devices, per_device(): hidden_rows = lax.all_gather(out_normed, ALL, axis=0, tiled=True)  53.7 us
    all_to_all x6, waiting for transfers between devices, exchange(): return lax.all_to_all(blocks, axis, split_axis=0, concat_axis=0, tiled=True)  37.8 us
    all_to_all x6, starting transfers between devices, exchange(): return lax.all_to_all(blocks, axis, split_axis=0, concat_axis=0, tiled=True)  28.4 us
    dot_general x1, matrix products, per_device(): lax.dot_general(hidden_rows, head, (((1,), (1,)), ((), ())), preferred_el...  15.1 us
    all_to_all x1, blocking collectives, exchange(): return lax.all_to_all(blocks, axis, split_axis=0, concat_axis=0, tiled=True)  10.9 us
    all_gather x1, blocking collectives, per_device(): lax.all_gather(hyp_tok.reshape(slot_count, slot_tokens), 'tm', axis=0, ti...  5.24 us
    dot_general x1, matrix products, per_device(): jnp.dot(enc_inner, ffn_down, preferred_element_type=jnp.float32)  5.21 us
    reduce_sum x3, other arithmetic, scatter_sum(): return jnp.sum(exchange(blocks, axis).astype(jnp.float32), axis=0)  4.54 us
  transfers between devices with their start and end apart: 7, of which 6 were waited for; matrix products, arithmetic and copies ran while one was open for 10% of the time, Pallas kernels for 0%

profile of v1, /device:TPU:0, one launch (start us, length us, event | category | flops | bytes accessed | tf_op | source)
XLA Modules:
  0.0 220.3 jit_solution(4168676838242879270)
XLA Ops:
  6.5 1.2 copy.78
  7.7 1.1 convert_reduce_fusion.1
  8.8 1.2 fusion.7
  10.0 0.8 copy.49
  10.8 0.1 rsqrt.39
  10.9 0.1 div.52
  11.0 5.2 %convolution_convert_fusion.1 = bf16[128,1280]{1,0:T(8,128)(2,1)} fusion(bf16[1280,1280]{1,0:T(8,128)(2,1)S(1)} %copy-done, bf16[1280,1280]{1,0:T(8,128)(2,1)} %param.15, bf16[128,1280]{1,0:T(8,128)(2,1)} %bitcast.108, f32[128]{0:T(128)S(1)} %rsqrt.39, f32[128]{0:T(128)S(1)} %div.52), kind=kOutput, calls=%fused_computation.10 | convolution fusion | flops 850329600 | bytes 7209984 | tf_op jit(solution)/shard_map/dot_general | solution.py:111
  16.2 6.3 %all-to-all-start.1 = ((bf16[4,32,1280]{2,1,0:T(8,128)(2,1)}), bf16[4,32,1280]{2,1,0:T(8,128)(2,1)}, u32[]{:S(2)}, u32[]{:S(2)}) async-start(bf16[4,32,1280]{2,1,0:T(8,128)(2,1)} %bitcast.115), calls=%async_computation.1 | async-start | bytes 655360 | tf_op jit(solution)/shard_map/all_to_all | solution.py:26
  22.5 2.1 multiply_reduce_fusion
  24.6 0.1 rsqrt.42
  24.7 2.3 %fusion.1 = bf16[256,4096]{1,0:T(8,128)(2,1)S(1)} fusion(f32[256]{0:T(256)S(1)} %rsqrt.42, bf16[2,8,16,4096]{3,2,1,0:T(8,128)(2,1)} %param.18), kind=kLoop, calls=%fused_computation.5 | loop fusion | flops 3145728 | bytes 4195328 | tf_op jit(solution)/shard_map/convert_element_type | solution.py:70
  27.0 0.5 copy-done.4
  27.5 1.2 convolution_convert_fusion.2
  28.8 0.1 broadcast_compare_fusion.1
  28.9 0.6 slice.30
  32.1 0.9 pad_maximum_fusion.1
  33.0 4.1 %all-to-all-start.3 = ((bf16[4,128,512]{2,1,0:T(8,128)(2,1)}), bf16[4,128,512]{2,1,0:T(8,128)(2,1)}, u32[]{:S(2)}, u32[]{:S(2)}) async-start(bf16[4,128,512]{2,1,0:T(8,128)(2,1)} %pad_maximum_fusion.1), calls=%async_computation.3 | async-start | bytes 1048576 | tf_op jit(solution)/shard_map/all_to_all | solution.py:26
  37.1 1.0 convert_reduce_fusion.2
  38.2 1.0 fusion.56
  39.2 1.1 multiply_reduce_fusion.2
  40.3 2.4 %convolution_convert_fusion.4 = bf16[32,1024]{1,0:T(8,128)(2,1)S(1)} fusion(bf16[1280,1024]{1,0:T(8,128)(2,1)} %param.17, f32[32]{0:T(128)S(1)} %add_rsqrt_fusion.3, f32[32]{0:T(128)S(1)} %broadcast_multiply_fusion.1, f32[32,1280]{1,0:T(8,128)S(1)} %convert_reduce_fusion.2, bf16[128,1280]{1,0:T(8,128)(2,1)} %bitcast.111, s32[]{:T(128)S(6)} %select_n.140), kind=kOutput, calls=%fused_computation.18 | convolution fusion | flops 84123648 | bytes 2932996 | tf_op jit(solution)/shard_map/dot_general | solution.py:117
  42.7 0.7 pad_maximum_fusion.2
  43.4 2.6 %all-to-all-done.3 = bf16[4,128,512]{2,1,0:T(8,128)(2,1)} async-done(((bf16[4,128,512]{2,1,0:T(8,128)(2,1)}), bf16[4,128,512]{2,1,0:T(8,128)(2,1)}, u32[]{:S(2)}, u32[]{:S(2)}) %all-to-all-start.3) | async-done | bytes 524320 | tf_op jit(solution)/shard_map/all_to_all | solution.py:26
  46.0 5.2 %all-to-all-start.2 = ((bf16[32,8,256]{2,1,0:T(8,128)(2,1)}), bf16[32,8,256]{2,1,0:T(8,128)(2,1)}, u32[]{:S(2)}, u32[]{:S(2)}) async-start(bf16[32,8,256]{2,1,0:T(8,128)(2,1)} %bitcast.18), calls=%async_computation.2 | async-start | bytes 262144 | tf_op jit(solution)/shard_map/all_to_all | solution.py:26
  51.3 0.7 compare_reduce_fusion
  54.5 0.6 dynamic_slice.25
  55.1 0.6 iota_compare_fusion.3
  55.7 0.9 constant_dynamic-slice_fusion
  56.6 0.1 copy.52
  56.8 2.9 %all-to-all-done.2 = bf16[32,8,256]{2,1,0:T(8,128)(2,1)} async-done(((bf16[32,8,256]{2,1,0:T(8,128)(2,1)}), bf16[32,8,256]{2,1,0:T(8,128)(2,1)}, u32[]{:S(2)}, u32[]{:S(2)}) %all-to-all-start.2) | async-done | bytes 131104 | tf_op jit(solution)/shard_map/all_to_all | solution.py:26
  59.7 1.8 fusion.5
  61.5 1.2 fusion.96
  62.7 1.5 convolution_convert_fusion.3
  64.2 4.0 %convolution_convert_fusion = bf16[128,4096]{1,0:T(8,128)(2,1)} fusion(bf16[128,512]{0,1:T(8,128)(2,1)S(1)} %bitcast.117, bf16[512,4096]{1,0:T(8,128)(2,1)} %param.22), kind=kOutput, calls=%fused_computation.3 | convolution fusion | flops 537395200 | bytes 5373952 | tf_op jit(solution)/shard_map/dot_general | solution.py:145
  68.2 4.4 %all-to-all-start.4 = ((bf16[2,64,4096]{2,1,0:T(8,128)(2,1)}), bf16[2,64,4096]{2,1,0:T(8,128)(2,1)}, u32[]{:S(2)}, u32[]{:S(2)}) async-start(bf16[2,64,4096]{2,1,0:T(8,128)(2,1)} %bitcast.105), calls=%async_computation.4 | async-start | bytes 2097152 | tf_op jit(solution)/shard_map/all_to_all | solution.py:26
  72.6 13.3 %all-to-all-done.4 = bf16[2,64,4096]{2,1,0:T(8,128)(2,1)} async-done(((bf16[2,64,4096]{2,1,0:T(8,128)(2,1)}), bf16[2,64,4096]{2,1,0:T(8,128)(2,1)}, u32[]{:S(2)}, u32[]{:S(2)}) %all-to-all-start.4) | async-done | bytes 1048608 | tf_op jit(solution)/shard_map/all_to_all | solution.py:26
  85.9 2.4 %reduce_sum.145 = bf16[64,4096]{1,0:T(8,128)(2,1)} reduce(bf16[2,64,4096]{2,1,0:T(8,128)(2,1)} %all-to-all-done.4, bf16[]{:T(256)} %constant.187.clone.1), dimensions={0}, to_apply=%region_9.10 | reduce | flops 262144 | bytes 1572866 | tf_op jit(solution)/shard_map/reduce_sum | solution.py:31
  88.2 4.1 %all-to-all-start.5 = ((bf16[4,16,4096]{2,1,0:T(8,128)(2,1)}), bf16[4,16,4096]{2,1,0:T(8,128)(2,1)}, u32[]{:S(2)}, u32[]{:S(2)}) async-start(bf16[4,16,4096]{2,1,0:T(8,128)(2,1)} %bitcast.106), calls=%async_computation.5 | async-start | bytes 1048576 | tf_op jit(solution)/shard_map/all_to_all | solution.py:26
  92.4 1.1 broadcast_select_fusion.3
  93.4 0.9 pad_maximum_fusion
  94.3 11.3 %all-to-all-done.5 = bf16[4,16,4096]{2,1,0:T(8,128)(2,1)} async-done(((bf16[4,16,4096]{2,1,0:T(8,128)(2,1)}), bf16[4,16,4096]{2,1,0:T(8,128)(2,1)}, u32[]{:S(2)}, u32[]{:S(2)}) %all-to-all-start.5) | async-done | bytes 524320 | tf_op jit(solution)/shard_map/all_to_all | solution.py:26
  105.6 4.1 %all-to-all-start = ((bf16[4,16,4096]{2,1,0:T(8,128)(2,1)}), bf16[4,16,4096]{2,1,0:T(8,128)(2,1)}, u32[]{:S(2)}, u32[]{:S(2)}) async-start(bf16[4,16,4096]{2,1,0:T(8,128)(2,1)} %pad_maximum_fusion), calls=%async_computation | async-start | bytes 1048576 | tf_op jit(solution)/shard_map/all_to_all | solution.py:26
  109.8 1.1 convert_reduce_fusion
  110.9 7.7 %all-to-all-done = bf16[4,16,4096]{2,1,0:T(8,128)(2,1)} async-done(((bf16[4,16,4096]{2,1,0:T(8,128)(2,1)}), bf16[4,16,4096]{2,1,0:T(8,128)(2,1)}, u32[]{:S(2)}, u32[]{:S(2)}) %all-to-all-start) | async-done | bytes 524320 | tf_op jit(solution)/shard_map/all_to_all | solution.py:26
  118.6 1.1 multiply_reduce_fusion.1
  119.7 1.6 multiply_convert_fusion.6
  121.4 0.1 reshape.224
  121.5 5.2 %all-gather = s32[4,2,128]{2,1,0:T(2,128)S(1)} all-gather(s32[1,2,128]{2,1,0:T(2,128)S(1)} %reshape.224), channel_id=1, replica_groups=mesh['section'=2,'tm'=4,'mp'=4] {'tm'}, dimensions={0}, use_global_device_ids=true | all-gather | bytes 5120 | tf_op jit(solution)/shard_map/all_gather | solution.py:94
  126.7 0.6 iota_reduce_fusion
  127.3 0.6 gather_fusion
  127.9 0.1 gather.13
  128.1 0.1 sub.86
  128.2 0.1 broadcast_in_dim.82
  128.3 53.7 %all-gather.3.cloned.1.call-done = bf16[512,4096]{1,0:T(8,128)(2,1)} async-done(((bf16[16,4096]{1,0:T(8,128)(2,1)}), bf16[512,4096]{1,0:T(8,128)(2,1)}) %all-gather.3.cloned.1.call-update) | async-done | bytes 4194320 | tf_op jit(solution)/shard_map/all_gather | solution.py:152
  182.0 15.1 %fusion.97 = (f32[512]{0:T(512)S(1)}, f32[512,2000]{0,1:T(8,128)}) fusion(bf16[512,4096]{1,0:T(8,128)(2,1)} %all-gather.3.cloned.1.call-done, bf16[2000,4096]{1,0:T(8,128)(2,1)} %param.23), kind=kOutput, calls=%fused_computation.178 | convolution fusion | flops 8389631488 | bytes 24676352 | tf_op jit(solution)/shard_map/dot_general | solution.py:153
  197.1 0.1 stack.60
  197.2 3.3 %exponential_reduce_fusion = (f32[512]{0:T(512)S(1)}, f32[512]{0:T(512)S(1)}) fusion(f32[512,2000]{0,1:T(8,128)} %get-tuple-element.26, f32[512]{0:T(512)S(1)} %get-tuple-element.25, s32[512]{0:T(512)S(1)} %sub.86), kind=kLoop, calls=%fused_computation.9 | loop fusion | flops 5118976 | bytes 4104192 | tf_op jit(solution)/shard_map/reduce_sum | solution.py:166
  200.5 0.1 stack.61
  200.6 0.1 stack.62
  200.7 0.1 reshape.229
  200.8 0.6 gather_fusion.1
  201.5 10.9 %all_to_all.35 = f32[32,2,3,128]{3,1,2,0:T(2,128)S(1)} all-to-all(f32[32,2,3,128]{3,1,2,0:T(2,128)S(1)} %bitcast.114), channel_id=1, replica_groups=mesh['section'=2,'tm'=4,'mp'=4] {'section','tm','mp'}, dimensions={0} | all-to-all | bytes 196608 | tf_op jit(solution)/shard_map/all_to_all | solution.py:26
  212.6 0.2 select_reduce_fusion.1
  212.8 0.6 add_select_fusion
  (42 shorter events, 0.7 us)
Async XLA Ops:
  6.5 4.4 %copy-start = (bf16[1280,1280]{1,0:T(8,128)(2,1)S(1)}, bf16[1280,1280]{1,0:T(8,128)(2,1)}, u32[]{:S(2)}) copy-start(bf16[1280,1280]{1,0:T(8,128)(2,1)} %param.16) | copy-start | bytes 9830404
  16.2 16.8 %all-to-all-start.1 = ((bf16[4,32,1280]{2,1,0:T(8,128)(2,1)}), bf16[4,32,1280]{2,1,0:T(8,128)(2,1)}, u32[]{:S(2)}, u32[]{:S(2)}) async-start(bf16[4,32,1280]{2,1,0:T(8,128)(2,1)} %bitcast.115), calls=%async_computation.1 | async-start | bytes 655360 | tf_op jit(solution)/shard_map/all_to_all | solution.py:26
  24.7 2.8 %copy-start.4 = (bf16[4096,512]{1,0:T(8,128)(2,1)S(1)}, bf16[4096,512]{1,0:T(8,128)(2,1)}, u32[]{:S(2)}) copy-start(bf16[4096,512]{1,0:T(8,128)(2,1)} %param.21) | copy-start | bytes 12582916
  27.5 1.3 copy-start.3
  28.8 25.7 %copy-start.5 = (s32[4]{0:T(128)S(1)}, s32[4]{0:T(128)}, u32[]{:S(2)}) copy-start(s32[4]{0:T(128)} %param.12) | copy-start | bytes 52
  33.0 13.0 %all-to-all-start.3 = ((bf16[4,128,512]{2,1,0:T(8,128)(2,1)}), bf16[4,128,512]{2,1,0:T(8,128)(2,1)}, u32[]{:S(2)}, u32[]{:S(2)}) async-start(bf16[4,128,512]{2,1,0:T(8,128)(2,1)} %pad_maximum_fusion.1), calls=%async_computation.3 | async-start | bytes 1048576 | tf_op jit(solution)/shard_map/all_to_all | solution.py:26
  46.0 13.6 %all-to-all-start.2 = ((bf16[32,8,256]{2,1,0:T(8,128)(2,1)}), bf16[32,8,256]{2,1,0:T(8,128)(2,1)}, u32[]{:S(2)}, u32[]{:S(2)}) async-start(bf16[32,8,256]{2,1,0:T(8,128)(2,1)} %bitcast.18), calls=%async_computation.2 | async-start | bytes 262144 | tf_op jit(solution)/shard_map/all_to_all | solution.py:26
  68.2 17.7 %all-to-all-start.4 = ((bf16[2,64,4096]{2,1,0:T(8,128)(2,1)}), bf16[2,64,4096]{2,1,0:T(8,128)(2,1)}, u32[]{:S(2)}, u32[]{:S(2)}) async-start(bf16[2,64,4096]{2,1,0:T(8,128)(2,1)} %bitcast.105), calls=%async_computation.4 | async-start | bytes 2097152 | tf_op jit(solution)/shard_map/all_to_all | solution.py:26
  72.6 48.8 %copy-start.1 = (s32[2,8,16]{2,1,0:T(8,128)S(1)}, s32[2,8,16]{2,1,0:T(8,128)}, u32[]{:S(2)}) copy-start(s32[2,8,16]{2,1,0:T(8,128)} %param.19) | copy-start | bytes 3076
  88.2 17.4 %all-to-all-start.5 = ((bf16[4,16,4096]{2,1,0:T(8,128)(2,1)}), bf16[4,16,4096]{2,1,0:T(8,128)(2,1)}, u32[]{:S(2)}, u32[]{:S(2)}) async-start(bf16[4,16,4096]{2,1,0:T(8,128)(2,1)} %bitcast.106), calls=%async_computation.5 | async-start | bytes 1048576 | tf_op jit(solution)/shard_map/all_to_all | solution.py:26
  105.6 13.1 %all-to-all-start = ((bf16[4,16,4096]{2,1,0:T(8,128)(2,1)}), bf16[4,16,4096]{2,1,0:T(8,128)(2,1)}, u32[]{:S(2)}, u32[]{:S(2)}) async-start(bf16[4,16,4096]{2,1,0:T(8,128)(2,1)} %pad_maximum_fusion), calls=%async_computation | async-start | bytes 1048576 | tf_op jit(solution)/shard_map/all_to_all | solution.py:26
  109.7 72.3 %all-gather.3.cloned.1.call-start = ((), (), s32[]{:S(2)}) async-start(), calls=%async_computation.7 | async-start | bytes 4325376 | tf_op jit(solution)/shard_map/all_gather | solution.py:152
  197.1 15.5 %copy-start.2 = (s32[2,8]{1,0:T(2,128)S(1)}, s32[2,8]{1,0:T(2,128)}, u32[]{:S(2)}) copy-start(s32[2,8]{1,0:T(2,128)} %param.20) | copy-start | bytes 196
Sparse Core Ops, SparseCore 0:
  121.5 60.4 all-gather.2

commit v2 on v1

--- a/solution.py
+++ b/solution.py
@@ -26,9 +26,30 @@
     return lax.all_to_all(blocks, axis, split_axis=0, concat_axis=0, tiled=True)
 
 
-def scatter_sum(partial, axis, count):
-    blocks = partial.reshape((count, partial.shape[0] // count) + partial.shape[1:])
-    return jnp.sum(exchange(blocks, axis).astype(jnp.float32), axis=0)
+def swap(values, axis, distance):
+    pairs = [(i, i ^ distance) for i in range(lax.axis_size(axis))]
+    return lax.ppermute(values, axis, pairs)
+
+
+def scatter_sum(partial, axis):
+    count = lax.axis_size(axis)
+    pos = lax.axis_index(axis)
+    rows = partial.shape[0] // count
+    total = None
+    for distance in range(count - 1, -1, -1):
+        block = lax.dynamic_slice_in_dim(partial, (pos ^ distance) * rows, rows, 0)
+        if distance:
+            block = swap(block, axis, distance)
+        block = block.astype(jnp.float32)
+        total = block if total is None else total + block
+    return total
+
+
+def gather_blocks(block, axis):
+    blocks = [block]
+    for distance in range(1, lax.axis_size(axis)):
+        blocks.append(swap(block, axis, distance))
+    return jnp.concatenate(blocks, axis=0)
 
 
 def per_device(
@@ -63,6 +84,8 @@
     group_heads = NH // KVH
     frame_share = frame_rows // width_count
     share_rows = slot_tokens // head_devices
+    pieces = 2
+    piece_rows = share_rows // pieces
     here_slots = lax.dynamic_slice_in_dim(slot_utt, group_pos * slot_count, slot_count, 0)
 
     dec_rows = hyp_state.reshape(slot_count * slot_tokens, model_width).astype(jnp.float32)
@@ -70,9 +93,13 @@
         square_norm(dec_rows).astype(jnp.bfloat16), q_proj, preferred_element_type=jnp.float32
     ).astype(jnp.bfloat16)
     queries = queries.reshape(slot_count, slot_tokens, device_heads * HD)
-    shares = lax.dynamic_slice_in_dim(
-        hyp_state.reshape(slot_count, slot_tokens, model_width), head_pos * share_rows, share_rows, 1
-    )
+    shares = lax.dynamic_slice(
+        hyp_state.reshape(
+            slot_count, section_count, pieces, width_count, piece_rows, model_width
+        ),
+        (0, section_pos, 0, width_pos, 0, 0),
+        (slot_count, 1, pieces, 1, piece_rows, model_width),
+    ).reshape(slot_count, share_rows, model_width)
 
     def by_utterance(values):
         out = []
@@ -85,17 +112,43 @@
 
     own_slot = jnp.argmax(slot_utt == group_pos)
     from_group = own_slot // slot_count
-    queries = lax.dynamic_index_in_dim(
-        exchange(by_utterance(queries), "tm"), from_group, 0, keepdims=False
-    )
-    resid_rows = lax.dynamic_index_in_dim(
-        exchange(by_utterance(shares), "tm"), from_group, 0, keepdims=False
-    )
-    slot_targets = lax.all_gather(
-        hyp_tok.reshape(slot_count, slot_tokens), "tm", axis=0, tiled=True
-    )
+
+    def from_owner(values):
+        blocks = by_utterance(values)
+        got = lax.dynamic_index_in_dim(blocks, group_pos, 0, keepdims=False)
+        for distance in range(1, group_count):
+            other = group_pos ^ distance
+            sent = lax.dynamic_index_in_dim(blocks, other, 0, keepdims=False)
+            got = jnp.where(from_group == other, swap(sent, "tm", distance), got)
+        return got
+
+    queries = from_owner(queries)
+    resid_rows = from_owner(shares)
+    slot_targets = gather_blocks(hyp_tok.reshape(slot_count, slot_tokens), "tm")
+    slot_targets = slot_targets.reshape(-1)
+
+    token_count = utterances * slot_tokens
+    near_order = section_count == 2 and group_count == 4
+    here = ((section_pos * group_count + group_pos) * width_count + width_pos) * share_rows
+    here = here if near_order else 0
+
+    def rows_of(section, utterance, width, row):
+        return ((section * group_count + utterance) * width_count + width) * share_rows + row
+
+    places = jnp.arange(token_count, dtype=jnp.int32) ^ here
+    place_row = places % share_rows
+    place_width = places // share_rows % width_count
+    place_utt = places // (share_rows * width_count) % group_count
+    place_section = places // (share_rows * width_count * group_count)
+    place_token = (
+        (place_section * pieces + place_row // piece_rows) * width_count + place_width
+    ) * piece_rows + place_row % piece_rows
     utt_slots = jnp.argmax(slot_utt[None, :] == jnp.arange(utterances)[:, None], axis=1)
-    targets = jnp.take(slot_targets, utt_slots, axis=0).reshape(utterances * slot_tokens)
+    place_slot = jnp.zeros_like(places)
+    for utterance in range(utterances):
+        place_slot = jnp.where(place_utt == utterance, utt_slots[utterance], place_slot)
+    place_slot = place_slot ^ (group_pos * slot_count)
+    targets = jnp.take(slot_targets, place_slot * slot_tokens + place_token, axis=0)
 
     enc_flat = (
         enc_in.reshape(width_count, frame_share, utterances, enc_width)
@@ -110,7 +163,6 @@
     enc_summed = scatter_sum(
         jnp.dot(enc_inner, ffn_down, preferred_element_type=jnp.float32).astype(jnp.bfloat16),
         "mp",
-        width_count,
     )
     own_frames = lax.dynamic_slice_in_dim(enc_flat, width_pos * share_count, share_count, 0)
     enc_states = layer_norm(own_frames.astype(jnp.float32) + enc_summed).astype(jnp.bfloat16)
@@ -145,34 +197,53 @@
     partial = jnp.dot(
         context.reshape(slot_tokens, device_heads * HD), o_proj, preferred_element_type=jnp.float32
     ).astype(jnp.bfloat16)
-    partial = scatter_sum(partial, "section", section_count).astype(jnp.bfloat16)
-    attn_out = scatter_sum(partial, "mp", width_count)
+    partial = partial.reshape(section_count, pieces, width_count * piece_rows, model_width)
+    attn_out = []
+    for piece in range(pieces):
+        section_sum = scatter_sum(partial[:, piece], "section")[0].astype(jnp.bfloat16)
+        attn_out.append(scatter_sum(section_sum, "mp"))
+    attn_out = jnp.concatenate(attn_out, axis=0)
     out_normed = square_norm(resid_rows.astype(jnp.float32) + attn_out).astype(jnp.bfloat16)
 
-    hidden_rows = lax.all_gather(out_normed, ALL, axis=0, tiled=True)
-    logits = lax.dot_general(
-        hidden_rows, head, (((1,), (1,)), ((), ())), preferred_element_type=jnp.float32
-    )
+    if near_order:
+        own = gather_blocks(out_normed, "mp")
+        half = own.shape[0] // 2
+        by_x = swap(own, "section", 1)
+        by_y = swap(own, "tm", 2)
+        across = jnp.concatenate([swap(by_x[:half], "tm", 2), swap(by_y[half:], "section", 1)])
+        chunks = [jnp.concatenate([rows, swap(rows, "tm", 1)]) for rows in (own, by_y, by_x, across)]
+    else:
+        chunks = [lax.all_gather(out_normed, ALL, axis=0, tiled=True)]
     vocab_rows = head.shape[0]
     vocab_start = (
         (section_pos * group_count + group_pos) * width_count + width_pos
     ) * vocab_rows
-    target_rows = (
-        targets.reshape(utterances, section_count, width_count, share_rows)
-        .transpose(1, 0, 2, 3)
-        .reshape(-1)
-    )
-    upper = jnp.max(logits, axis=1)
-    totals = jnp.sum(jnp.exp(logits - upper[:, None]), axis=1)
-    matches = (
-        jnp.arange(vocab_rows, dtype=jnp.int32)[None, :] == (target_rows - vocab_start)[:, None]
-    )
-    target_logit = jnp.sum(jnp.where(matches, logits, 0.0), axis=1)
-
-    stats = jnp.stack([upper, totals, target_logit])
-    stats = stats.reshape(3, section_count, utterances, width_count, share_rows)
-    stats = stats.transpose(2, 0, 1, 3, 4).reshape(utterances, 3, slot_tokens)
-    by_slot = jnp.take(stats, jnp.maximum(slot_utt, 0), axis=0)
+    stats = []
+    chunk_rows = token_count // len(chunks)
+    for number, hidden_rows in enumerate(chunks):
+        logits = lax.dot_general(
+            hidden_rows, head, (((1,), (1,)), ((), ())), preferred_element_type=jnp.float32
+        )
+        target_rows = targets[number * chunk_rows : (number + 1) * chunk_rows]
+        upper = jnp.max(logits, axis=1)
+        totals = jnp.sum(jnp.exp(logits - upper[:, None]), axis=1)
+        matches = (
+            jnp.arange(vocab_rows, dtype=jnp.int32)[None, :] == (target_rows - vocab_start)[:, None]
+        )
+        target_logit = jnp.sum(jnp.where(matches, logits, 0.0), axis=1)
+        stats.append(jnp.stack([upper, totals, target_logit]))
+
+    stats = jnp.concatenate(stats, axis=1)
+    token = jnp.arange(slot_tokens, dtype=jnp.int32)
+    token_row = token // (width_count * piece_rows) % pieces * piece_rows + token % piece_rows
+    wanted = rows_of(
+        token[None, :] // (width_count * pieces * piece_rows),
+        jnp.maximum(slot_utt, 0)[:, None],
+        token[None, :] // piece_rows % width_count,
+        token_row[None, :],
+    )
+    by_slot = jnp.take(stats, (wanted ^ here).reshape(-1), axis=1)
+    by_slot = by_slot.reshape(3, slot_utt.shape[0], slot_tokens).transpose(1, 0, 2)
     by_group = by_slot.reshape(1, group_count, 1, slot_count, 3, slot_tokens)
     by_group = jnp.broadcast_to(
         by_group, (section_count, group_count, width_count, slot_count, 3, slot_tokens)

time: 221 us -> 182 us (0.82)
  waiting for transfers between devices: 91.5 us -> 41.1 us
  between operations: 18.8 us -> 5.65 us
  local copies, waits for them, and re-layouts: 6.91 us -> 18.3 us
  matrix products: 32.5 us -> 41.4 us
  starting transfers between devices: 28.4 us -> 35.3 us
  blocking collectives: 16.1 us -> 10.9 us
  other arithmetic: 26 us -> 28.8 us
    all_gather x1 -> x0, waiting for transfers between devices: 53.7 us -> none  [per_device(): hidden_rows = lax.all_gather(out_normed, ALL, axis=0, tiled=True)]
    ppermute x0 -> x31, waiting for transfers between devices: none -> 37.8 us  [swap(): return lax.ppermute(values, axis, pairs)]
    all_to_all x6 -> x1, waiting for transfers between devices: 37.8 us -> 3.3 us  [exchange(): return lax.all_to_all(blocks, axis, split_axis=0, concat_axis=0, tiled=True)]
    ppermute x0 -> x31, starting transfers between devices: none -> 29.4 us  [swap(): return lax.ppermute(values, axis, pairs)]
    all_to_all x6 -> x1, starting transfers between devices: 28.4 us -> 5.97 us  [exchange(): return lax.all_to_all(blocks, axis, split_axis=0, concat_axis=0, tiled=True)]
    select_n x2 -> x6, other arithmetic: 0.08 us -> 8.04 us  [the longest x2 4.98 us: per_device(): jnp.take(slot_targets, place_slot * slot_tokens + place_token, axis=0)]
    dot_general x1 -> x4, matrix products: 15.1 us -> 22.3 us  [per_device(): lax.dot_general(hidden_rows, head, (((1,), (1,)), ((), ())), preferred_el...]
    all_gather x1 -> x0, blocking collectives: 5.24 us -> none  [per_device(): lax.all_gather(hyp_tok.reshape(slot_count, slot_tokens), 'tm', axis=0, ti...]
  transfers between devices with their start and end apart: 7 -> 32, of which waited for: 6 -> 12; matrix products, arithmetic and copies ran while one was open for 10% -> 38% of each run, Pallas kernels for 0% -> 0%
where the time goes in v2:
time: 182 us; the launch traced here: 181 us
  matrix products  41.4 us (23%)
  waiting for transfers between devices  41.1 us (23%)
  starting transfers between devices  35.3 us (19%)
  other arithmetic  28.8 us (16%)
  local copies, waits for them, and re-layouts  18.3 us (10%)
  blocking collectives  10.9 us (6%)
  between operations  5.65 us (3%)
    ppermute x31, waiting for transfers between devices, swap(): return lax.ppermute(values, axis, pairs)  37.8 us
    ppermute x31, starting transfers between devices, swap(): return lax.ppermute(values, axis, pairs)  29.4 us
    dot_general x4, matrix products, per_device(): lax.dot_general(hidden_rows, head, (((1,), (1,)), ((), ())), preferred_el...  22.3 us
    all_to_all x1, blocking collectives, exchange(): return lax.all_to_all(blocks, axis, split_axis=0, concat_axis=0, tiled=True)  10.9 us
    all_to_all x1, starting transfers between devices, exchange(): return lax.all_to_all(blocks, axis, split_axis=0, concat_axis=0, tiled=True)  5.97 us
    dot_general x1, matrix products, per_device(): jnp.dot(enc_inner, ffn_down, preferred_element_type=jnp.float32)  5.24 us
    select_n x2, other arithmetic, per_device(): jnp.take(slot_targets, place_slot * slot_tokens + place_token, axis=0)  4.98 us
    dot_general x1, matrix products, per_device(): jnp.dot(square_norm(dec_rows).astype(jnp.bfloat16), q_proj, preferred_ele...  4.06 us
  transfers between devices with their start and end apart: 32, of which 12 were waited for; matrix products, arithmetic and copies ran while one was open for 38% of the time, Pallas kernels for 0%

profile of v2, /device:TPU:0, one launch (start us, length us, event | category | flops | bytes accessed | tf_op | source)
XLA Modules:
  0.0 181.4 jit_solution(6071545804819089469)
XLA Ops:
  0.0 0.9 reshape.815
  1.4 2.6 %collective-permute-start.22 = (s32[2,128]{1,0:T(2,128)S(1)}, s32[2,128]{1,0:T(2,128)}, u32[]{:S(2)}, u32[]{:S(2)}) collective-permute-start(s32[2,128]{1,0:T(2,128)S(1)} %reshape.815), channel_id=1, source_target_pairs={{0,8},{4,12},{8,0},{12,4},{1,9},{5,13},{9,1},{13,5},{2,10},{6,14},... | collective-permute-start | bytes 3080 | tf_op jit(solution)/shard_map/ppermute | solution.py:31
  4.0 1.1 convert_reduce_fusion
  5.1 1.8 copy.75
  6.9 1.2 fusion.21
  8.4 5.2 %convolution_convert_fusion.1 = bf16[128,1280]{1,0:T(8,128)(2,1)} fusion(bf16[1280,1280]{1,0:T(8,128)(2,1)S(1)} %copy-done, bf16[1280,1280]{1,0:T(8,128)(2,1)} %param.15, bf16[128,1280]{1,0:T(8,128)(2,1)} %bitcast.190, f32[128]{0:T(128)S(1)} %rsqrt.39, f32[128]{0:T(128)S(1)} %div.148), kind=kOutput, calls=%fused_computation.7 | convolution fusion | flops 850329600 | bytes 7209984 | tf_op jit(solution)/shard_map/dot_general | solution.py:164
  13.6 1.7 constant_dynamic-slice_fusion.2
  15.3 3.8 %collective-permute-start.3 = (bf16[32,1280]{1,0:T(8,128)(2,1)}, bf16[32,1280]{1,0:T(8,128)(2,1)}, u32[]{:S(2)}, u32[]{:S(2)}) collective-permute-start(bf16[32,1280]{1,0:T(8,128)(2,1)} %get-tuple-element.37), channel_id=1, source_target_pairs={{0,3},{1,2},{2,1},{3,0},{4,7},{5,6},{6,5},{7,4},{8,11},{9,10},{10,... | collective-permute-start | bytes 245768 | tf_op jit(solution)/shard_map/ppermute | solution.py:31
  27.4 2.1 %multiply_reduce_fusion = f32[2,8,16]{2,1,0:T(8,128)S(1)} fusion(bf16[2,8,16,4096]{3,2,1,0:T(8,128)(2,1)} %param.18), kind=kLoop, calls=%fused_computation.6 | loop fusion | flops 3145472 | bytes 2098176 | tf_op jit(solution)/shard_map/reduce_sum | solution.py:22
  29.6 3.6 %fusion.1 = bf16[256,4096]{1,0:T(8,128)(2,1)} fusion(f32[256]{0:T(256)S(1)} %rsqrt.42, bf16[2,8,16,4096]{3,2,1,0:T(8,128)(2,1)} %param.18), kind=kLoop, calls=%fused_computation.5 | loop fusion | flops 3145728 | bytes 4195328 | tf_op jit(solution)/shard_map/convert_element_type | solution.py:93
  33.7 1.1 iota_compare_fusion.6
  34.9 4.1 %convolution_convert_fusion.2 = bf16[256,512]{1,0:T(8,128)(2,1)S(1)} fusion(bf16[256,4096]{1,0:T(8,128)(2,1)} %fusion.1, bf16[4096,512]{1,0:T(8,128)(2,1)} %param.21), kind=kOutput, calls=%fused_computation.13 | convolution fusion | flops 1073872896 | bytes 6553600 | tf_op jit(solution)/shard_map/dot_general | solution.py:92
  39.1 0.8 dynamic-slice_bitcast_fusion.2
  39.9 1.0 select_bitcast_fusion.7
  41.0 0.8 copy-done.1
  41.8 0.8 dynamic-slice_bitcast_fusion.5
  43.2 2.5 %compare_select_fusion.1 = s32[512,1]{0,1:T(1,128)S(1)} fusion(s32[]{:T(128)S(6)} %mul.235, s32[]{:T(128)} %bitcast.60, s32[]{:T(128)} %bitcast.59, s32[]{:T(128)} %bitcast.58, s32[]{:T(128)} %bitcast.57, s32[]{:T(128)S(6)} %mul.246), kind=kLoop, calls=%fused_computation.164 | loop fusion | flops 51712 | bytes 2072 | tf_op jit(solution)/shard_map/jit(_take)/jit(_where)/select_n | solution.py:151
  46.5 0.9 collective-permute-start.6
  47.4 0.9 collective-permute-start.7
  48.9 2.3 %gather_fusion = s32[512]{0:T(512)S(1)} fusion(s32[1024]{0:T(1024)S(1)} %add_bitcast_fusion, s32[1024]{0:T(1024)S(1)} %pad_clamp_fusion), kind=kCustom, calls=%fused_computation | custom fusion | bytes 6144 | tf_op jit(solution)/shard_map/jit(_take)/gather | solution.py:151
  51.4 1.4 collective-permute-start
  53.4 1.2 fusion.145
  54.9 2.3 %convolution_convert_fusion.4 = bf16[32,1024]{1,0:T(8,128)(2,1)S(1)} fusion(bf16[1280,1024]{1,0:T(8,128)(2,1)} %param.17, f32[32,1280]{1,0:T(8,128)S(1)} %get-tuple-element.24, f32[32]{0:T(128)S(1)} %add_rsqrt_fusion.3, f32[32]{0:T(128)S(1)} %broadcast_multiply_fusion.1), kind=kOutput, calls=%fused_computation.15 | convolution fusion | flops 84041728 | bytes 2851072 | tf_op jit(solution)/shard_map/dot_general | solution.py:169
  57.9 6.0 %all-to-all-start = ((bf16[32,8,256]{2,1,0:T(8,128)(2,1)}), bf16[32,8,256]{2,1,0:T(8,128)(2,1)}, u32[]{:S(2)}, u32[]{:S(2)}) async-start(bf16[32,8,256]{2,1,0:T(8,128)(2,1)} %bitcast.24), calls=%async_computation | async-start | bytes 262144 | tf_op jit(solution)/shard_map/all_to_all | solution.py:26
  63.9 2.5 %and_select_fusion.8 = s32[512]{0:T(512)S(1)} fusion(s32[512]{0:T(512)S(1)} %gather_fusion, s32[]{:T(128)S(6)} %mul.235, s32[]{:T(128)} %bitcast.60, s32[]{:T(128)} %bitcast.59, s32[]{:T(128)} %bitcast.58, s32[]{:T(128)} %bitcast.57, s32[]{:T(128)S(6)} %mul.246), kind=kLoop, calls=%fused_computation.265 | loop fusion | flops 53760 | bytes 4120 | tf_op jit(solution)/shard_map/jit(_take)/select_n | solution.py:151
  67.7 1.0 fusion.71
  68.8 3.3 %all-to-all-done = bf16[32,8,256]{2,1,0:T(8,128)(2,1)} async-done(((bf16[32,8,256]{2,1,0:T(8,128)(2,1)}), bf16[32,8,256]{2,1,0:T(8,128)(2,1)}, u32[]{:S(2)}, u32[]{:S(2)}) %all-to-all-start) | async-done | bytes 131104 | tf_op jit(solution)/shard_map/all_to_all | solution.py:26
  72.1 1.9 %fusion.5 = f32[4,128,256]{1,2,0:T(8,128)} fusion(bf16[128,4,128]{0,2,1:T(8,128)(2,1)S(1)} %bitcast.188, pred[256]{0:T(512)(128)(4,1)} %iota_compare_fusion.6, bf16[256,256]{1,0:T(8,128)(2,1)} %bitcast.25), kind=kOutput, calls=%fused_computation.12 | convolution fusion | flops 33816576 | bytes 721408 | tf_op jit(solution)/shard_map/qhd,fd->hqf/dot_general | solution.py:188
  73.9 1.2 fusion.148
  75.1 1.5 convolution_convert_fusion.3
  76.6 2.9 %convolution_convert_fusion = bf16[128,4096]{1,0:T(8,128)(2,1)S(1)} fusion(bf16[128,512]{0,1:T(8,128)(2,1)S(1)} %bitcast.194, bf16[512,4096]{1,0:T(8,128)(2,1)} %param.22), kind=kOutput, calls=%fused_computation.3 | convolution fusion | flops 537395200 | bytes 5373952 | tf_op jit(solution)/shard_map/dot_general | solution.py:197
  79.7 0.8 collective-permute-start.9
  80.6 1.3 collective-permute-start.13
  81.9 7.1 %collective-permute-done.9 = bf16[1,32,4096]{2,1,0:T(8,128)(2,1)S(1)} collective-permute-done((bf16[1,32,4096]{2,1,0:T(8,128)(2,1)S(1)}, bf16[1,32,4096]{2,1,0:T(8,128)(2,1)S(1)}, u32[]{:S(2)}, u32[]{:S(2)}) %collective-permute-start.9) | collective-permute-done | bytes 262176 | tf_op jit(solution)/shard_map/ppermute | solution.py:31
  89.1 1.3 collective-permute-start.10
  90.4 2.4 %collective-permute-done.13 = bf16[1,32,4096]{2,1,0:T(8,128)(2,1)S(1)} collective-permute-done((bf16[1,32,4096]{2,1,0:T(8,128)(2,1)S(1)}, bf16[1,32,4096]{2,1,0:T(8,128)(2,1)S(1)}, u32[]{:S(2)}, u32[]{:S(2)}) %collective-permute-start.13) | collective-permute-done | bytes 262176 | tf_op jit(solution)/shard_map/ppermute | solution.py:31
  92.8 1.1 collective-permute-start.12
  94.0 1.3 collective-permute-done.10
  95.3 1.2 collective-permute-start.14
  97.4 2.4 %collective-permute-start.16 = (bf16[8,4096]{1,0:T(8,128)(2,1)S(1)}, bf16[8,4096]{1,0:T(8,128)(2,1)S(1)}, u32[]{:S(2)}, u32[]{:S(2)}) collective-permute-start(bf16[8,4096]{1,0:T(8,128)(2,1)S(1)} %get-tuple-element.44), channel_id=1, source_target_pairs={{0,1},{1,0},{2,3},{3,2},{4,5},{5,4},{6,7},{7,6},{8,9},{9,8},{10,11... | collective-permute-start | bytes 196616 | tf_op jit(solution)/shard_map/ppermute | solution.py:31
  99.8 1.7 collective-permute-done.14
  101.4 1.4 collective-permute-done.15
  102.9 1.2 multiply_reduce_fusion.1
  104.2 1.2 collective-permute-start.17
  105.5 1.3 collective-permute-start.18
  106.7 1.9 %collective-permute-start.19 = (bf16[16,4096]{1,0:T(8,128)(2,1)S(1)}, bf16[16,4096]{1,0:T(8,128)(2,1)S(1)}, u32[]{:S(2)}, u32[]{:S(2)}) collective-permute-start(bf16[16,4096]{1,0:T(8,128)(2,1)S(1)} %get-tuple-element.20), channel_id=1, source_target_pairs={{0,3},{1,2},{2,1},{3,0},{4,7},{5,6},{6,5},{7,4},{8,11},{9,10},{10,... | collective-permute-start | bytes 393224 | tf_op jit(solution)/shard_map/ppermute | solution.py:31
  108.7 2.7 %collective-permute-done.17 = bf16[16,4096]{1,0:T(8,128)(2,1)S(1)} collective-permute-done((bf16[16,4096]{1,0:T(8,128)(2,1)S(1)}, bf16[16,4096]{1,0:T(8,128)(2,1)S(1)}, u32[]{:S(2)}, u32[]{:S(2)}) %collective-permute-start.17) | collective-permute-done | bytes 131104 | tf_op jit(solution)/shard_map/ppermute | solution.py:31
  111.4 6.4 %collective-permute-done.18 = bf16[16,4096]{1,0:T(8,128)(2,1)S(1)} collective-permute-done((bf16[16,4096]{1,0:T(8,128)(2,1)S(1)}, bf16[16,4096]{1,0:T(8,128)(2,1)S(1)}, u32[]{:S(2)}, u32[]{:S(2)}) %collective-permute-start.18) | collective-permute-done | bytes 131104 | tf_op jit(solution)/shard_map/ppermute | solution.py:31
  117.9 0.8 collective-permute-start.24
  118.7 0.9 collective-permute-start.26
  119.6 13.0 %collective-permute-done.26 = bf16[64,4096]{1,0:T(8,128)(2,1)S(1)} collective-permute-done((bf16[64,4096]{1,0:T(8,128)(2,1)S(1)}, bf16[64,4096]{1,0:T(8,128)(2,1)S(1)}, u32[]{:S(2)}, u32[]{:S(2)}) %collective-permute-start.26) | collective-permute-done | bytes 524320 | tf_op jit(solution)/shard_map/ppermute | solution.py:31
  132.7 1.3 collective-permute-start.28
  134.1 1.3 collective-permute-start.29
  135.4 8.4 %fusion.152 = (f32[128]{0:T(128)S(1)}, f32[128,2000]{0,1:T(8,128)S(1)}) fusion(bf16[128,4096]{1,0:T(8,128)(2,1)S(1)} %constant_dynamic-update-slice_fusion, bf16[2000,4096]{1,0:T(8,128)(2,1)} %param.23), kind=kOutput, calls=%fused_computation.343 | convolution fusion | flops 2097407872 | bytes 18457088 | tf_op jit(solution)/shard_map/dot_general | solution.py:224
  144.9 0.9 collective-permute-done.25
  145.8 4.6 %fusion.151 = (f32[128]{0:T(128)S(1)}, f32[128,2000]{0,1:T(8,128)S(1)}) fusion(bf16[2000,4096]{1,0:T(8,128)(2,1)S(1)} %bitcast.180, bf16[64,4096]{1,0:T(8,128)(2,1)S(1)} %collective-permute-done.25, bf16[64,4096]{1,0:T(8,128)(2,1)S(1)} %collective-permute-done.24), kind=kOutput, calls=%fused_computation.342 | convolution fusion | flops 2099505024 | bytes 18457088 | tf_op jit(solution)/shard_map/dot_general | solution.py:224
  150.4 4.5 %fusion.150 = (f32[128]{0:T(128)S(1)}, f32[128,2000]{0,1:T(8,128)S(1)}) fusion(bf16[2000,4096]{1,0:T(8,128)(2,1)S(1)} %bitcast.180, bf16[64,4096]{1,0:T(8,128)(2,1)S(1)} %collective-permute-done.27, bf16[64,4096]{1,0:T(8,128)(2,1)S(1)} %collective-permute-done.26), kind=kOutput, calls=%fused_computation.341 | convolution fusion | flops 2099505024 | bytes 18457088 | tf_op jit(solution)/shard_map/dot_general | solution.py:224
  155.6 4.8 %fusion.149 = (f32[128]{0:T(128)S(1)}, f32[128,2000]{0,1:T(8,128)S(1)}) fusion(bf16[2000,4096]{1,0:T(8,128)(2,1)S(1)} %bitcast.180, bf16[64,4096]{1,0:T(8,128)(2,1)S(1)} %collective-permute-done.30, bf16[32,4096]{1,0:T(8,128)(2,1)S(1)} %collective-permute-done.29, bf16[32,4096]{1,0:T(8,128)(2,1)S(1)} %collective-permute-done.28), kind=kOutput, calls=%fused_computation.340 | convolution fusion | flops 2100553600 | bytes 18457088 | tf_op jit(solution)/shard_map/dot_general | solution.py:224
  160.8 4.0 %gather_fusion.1 = f32[1024,3]{1,0:T(8,128)} fusion(f32[3,512]{0,1:T(8,128)S(1)} %copy.80, s32[1024]{0:T(1024)S(1)} %broadcast_clamp_fusion), kind=kCustom, calls=%fused_computation.1 | custom fusion | bytes 28672 | tf_op jit(solution)/shard_map/jit(_take)/gather | solution.py:245
  164.8 2.1 %broadcast_select_fusion = f32[3,8,128]{0,2,1:T(8,128)} fusion(f32[3,8,128]{0,2,1:T(8,128)} %bitcast.187, pred[8,128]{1,0:T(8,128)(4,1)S(1)} %copy-done.6), kind=kLoop, calls=%fused_computation.109 | loop fusion | flops 3072 | bytes 25600 | tf_op jit(solution)/shard_map/jit(_take)/select_n | solution.py:245
  166.9 1.2 copy.81
  168.2 10.9 %all_to_all.10 = f32[32,2,3,128]{3,1,2,0:T(2,128)S(1)} all-to-all(f32[32,2,3,128]{3,1,2,0:T(2,128)S(1)} %bitcast.192), channel_id=1, replica_groups=mesh['section'=2,'tm'=4,'mp'=4] {'section','tm','mp'}, dimensions={0} | all-to-all | bytes 196608 | tf_op jit(solution)/shard_map/all_to_all | solution.py:26
  179.3 0.8 select_reduce_fusion.4
  180.1 1.3 add_select_fusion.8
  (124 shorter events, 13.9 us)
Async XLA Ops:
  0.0 8.3 %copy-start = (bf16[1280,1280]{1,0:T(8,128)(2,1)S(1)}, bf16[1280,1280]{1,0:T(8,128)(2,1)}, u32[]{:S(2)}) copy-start(bf16[1280,1280]{1,0:T(8,128)(2,1)} %param.16) | copy-start | bytes 9830404
  0.9 44.9 %collective-permute-start.21 = (s32[2,128]{1,0:T(2,128)S(1)}, s32[2,128]{1,0:T(2,128)}, u32[]{:S(2)}, u32[]{:S(2)}) collective-permute-start(s32[2,128]{1,0:T(2,128)S(1)} %reshape.815), channel_id=1, source_target_pairs={{0,4},{4,0},{8,12},{12,8},{1,5},{5,1},{9,13},{13,9},{2,6},{6,2},{1... | collective-permute-start | bytes 3080 | tf_op jit(solution)/shard_map/ppermute | solution.py:31
  1.4 45.1 %collective-permute-start.22 = (s32[2,128]{1,0:T(2,128)S(1)}, s32[2,128]{1,0:T(2,128)}, u32[]{:S(2)}, u32[]{:S(2)}) collective-permute-start(s32[2,128]{1,0:T(2,128)S(1)} %reshape.815), channel_id=1, source_target_pairs={{0,8},{4,12},{8,0},{12,4},{1,9},{5,13},{9,1},{13,5},{2,10},{6,14},... | collective-permute-start | bytes 3080 | tf_op jit(solution)/shard_map/ppermute | solution.py:31
  4.0 43.4 %collective-permute-start.23 = (s32[2,128]{1,0:T(2,128)S(1)}, s32[2,128]{1,0:T(2,128)}, u32[]{:S(2)}, u32[]{:S(2)}) collective-permute-start(s32[2,128]{1,0:T(2,128)S(1)} %reshape.815), channel_id=1, source_target_pairs={{0,12},{4,8},{8,4},{12,0},{1,13},{5,9},{9,5},{13,1},{2,14},{6,10},... | collective-permute-start | bytes 3080 | tf_op jit(solution)/shard_map/ppermute | solution.py:31
  8.3 10.7 %copy-start.7 = (s32[8]{0:T(128)S(1)}, s32[8]{0:T(128)}, u32[]{:S(2)}) copy-start(s32[8]{0:T(128)} %param.13) | copy-start | bytes 100
  15.3 17.9 %copy-start.8 = (s32[4]{0:T(128)S(1)}, s32[4]{0:T(128)}, u32[]{:S(2)}) copy-start(s32[4]{0:T(128)} %param.12) | copy-start | bytes 52
  15.3 35.9 %collective-permute-start.3 = (bf16[32,1280]{1,0:T(8,128)(2,1)}, bf16[32,1280]{1,0:T(8,128)(2,1)}, u32[]{:S(2)}, u32[]{:S(2)}) collective-permute-start(bf16[32,1280]{1,0:T(8,128)(2,1)} %get-tuple-element.37), channel_id=1, source_target_pairs={{0,3},{1,2},{2,1},{3,0},{4,7},{5,6},{6,5},{7,4},{8,11},{9,10},{10,... | collective-permute-start | bytes 245768 | tf_op jit(solution)/shard_map/ppermute | solution.py:31
  19.1 32.3 %collective-permute-start.4 = (bf16[32,1280]{1,0:T(8,128)(2,1)}, bf16[32,1280]{1,0:T(8,128)(2,1)}, u32[]{:S(2)}, u32[]{:S(2)}) collective-permute-start(bf16[32,1280]{1,0:T(8,128)(2,1)} %get-tuple-element.39), channel_id=1, source_target_pairs={{0,2},{1,3},{2,0},{3,1},{4,6},{5,7},{6,4},{7,5},{8,10},{9,11},{10,... | collective-permute-start | bytes 245768 | tf_op jit(solution)/shard_map/ppermute | solution.py:31
  39.1 1.9 %copy-start.2 = (bf16[4,128,512]{2,1,0:T(8,128)(2,1)}, bf16[4,128,512]{2,1,0:T(8,128)(2,1)S(1)}, u32[]{:S(2)}) copy-start(bf16[4,128,512]{2,1,0:T(8,128)(2,1)S(1)} %pad_maximum_fusion.1) | copy-start | bytes 1572868
  41.0 0.8 copy-start.1
  45.8 6.9 %collective-permute-start.5 = (bf16[32,1280]{1,0:T(8,128)(2,1)}, bf16[32,1280]{1,0:T(8,128)(2,1)}, u32[]{:S(2)}, u32[]{:S(2)}) collective-permute-start(bf16[32,1280]{1,0:T(8,128)(2,1)} %get-tuple-element.38), channel_id=1, source_target_pairs={{0,1},{1,0},{2,3},{3,2},{4,5},{5,4},{6,7},{7,6},{8,9},{9,8},{10,11... | collective-permute-start | bytes 245768 | tf_op jit(solution)/shard_map/ppermute | solution.py:31
  46.5 19.9 %collective-permute-start.6 = (bf16[128,512]{1,0:T(8,128)(2,1)}, bf16[128,512]{1,0:T(8,128)(2,1)S(1)}, u32[]{:S(2)}, u32[]{:S(2)}) collective-permute-start(bf16[128,512]{1,0:T(8,128)(2,1)} %get-tuple-element.36), channel_id=1, source_target_pairs={{0,12},{4,8},{8,4},{12,0},{1,13},{5,9},{9,5},{13,1},{2,14},{6,10},... | collective-permute-start | bytes 393224 | tf_op jit(solution)/shard_map/ppermute | solution.py:31
  47.4 19.0 %collective-permute-start.7 = (bf16[128,512]{1,0:T(8,128)(2,1)}, bf16[128,512]{1,0:T(8,128)(2,1)S(1)}, u32[]{:S(2)}, u32[]{:S(2)}) collective-permute-start(bf16[128,512]{1,0:T(8,128)(2,1)} %get-tuple-element.35), channel_id=1, source_target_pairs={{0,8},{4,12},{8,0},{12,4},{1,9},{5,13},{9,1},{13,5},{2,10},{6,14},... | collective-permute-start | bytes 393224 | tf_op jit(solution)/shard_map/ppermute | solution.py:31
  51.2 16.5 %collective-permute-start.8 = (bf16[128,512]{1,0:T(8,128)(2,1)}, bf16[128,512]{1,0:T(8,128)(2,1)}, u32[]{:S(2)}, u32[]{:S(2)}) collective-permute-start(bf16[128,512]{1,0:T(8,128)(2,1)} %get-tuple-element.34), channel_id=1, source_target_pairs={{0,4},{4,0},{8,12},{12,8},{1,5},{5,1},{9,13},{13,9},{2,6},{6,2},{1... | collective-permute-start | bytes 393224 | tf_op jit(solution)/shard_map/ppermute | solution.py:31
  51.4 51.5 %collective-permute-start = (bf16[16,4096]{1,0:T(8,128)(2,1)}, bf16[16,4096]{1,0:T(8,128)(2,1)}, u32[]{:S(2)}, u32[]{:S(2)}) collective-permute-start(bf16[16,4096]{1,0:T(8,128)(2,1)} %get-tuple-element.33), channel_id=1, source_target_pairs={{0,12},{4,8},{8,4},{12,0},{1,13},{5,9},{9,5},{13,1},{2,14},{6,10},... | collective-permute-start | bytes 393224 | tf_op jit(solution)/shard_map/ppermute | solution.py:31
  52.7 50.2 %collective-permute-start.1 = (bf16[16,4096]{1,0:T(8,128)(2,1)}, bf16[16,4096]{1,0:T(8,128)(2,1)}, u32[]{:S(2)}, u32[]{:S(2)}) collective-permute-start(bf16[16,4096]{1,0:T(8,128)(2,1)} %get-tuple-element.32), channel_id=1, source_target_pairs={{0,8},{4,12},{8,0},{12,4},{1,9},{5,13},{9,1},{13,5},{2,10},{6,14},... | collective-permute-start | bytes 393224 | tf_op jit(solution)/shard_map/ppermute | solution.py:31
  57.9 14.2 %all-to-all-start = ((bf16[32,8,256]{2,1,0:T(8,128)(2,1)}), bf16[32,8,256]{2,1,0:T(8,128)(2,1)}, u32[]{:S(2)}, u32[]{:S(2)}) async-start(bf16[32,8,256]{2,1,0:T(8,128)(2,1)} %bitcast.24), calls=%async_computation | async-start | bytes 262144 | tf_op jit(solution)/shard_map/all_to_all | solution.py:26
  66.4 0.7 copy-start.3
  67.0 0.6 copy-start.4
  79.6 21.9 %copy-start.5 = (bf16[16,4096]{1,0:T(8,128)(2,1)S(1)}, bf16[16,4096]{1,0:T(8,128)(2,1)}, u32[]{:S(2)}) copy-start(bf16[16,4096]{1,0:T(8,128)(2,1)} %get-tuple-element.31) | copy-start | bytes 393220
  79.7 9.3 %collective-permute-start.9 = (bf16[1,32,4096]{2,1,0:T(8,128)(2,1)S(1)}, bf16[1,32,4096]{2,1,0:T(8,128)(2,1)S(1)}, u32[]{:S(2)}, u32[]{:S(2)}) collective-permute-start(bf16[1,32,4096]{2,1,0:T(8,128)(2,1)S(1)} %dynamic-slice_bitcast_fusion.1), channel_id=1, source_target_pairs={{0,16},{16,0},{1,17},{17,1},{2,18},{18,2},{3,19},{19,3},{4,20},{20... | collective-permute-start | bytes 786440 | tf_op jit(solution)/shard_map/ppermute | solution.py:31
  80.6 12.2 %collective-permute-start.13 = (bf16[1,32,4096]{2,1,0:T(8,128)(2,1)S(1)}, bf16[1,32,4096]{2,1,0:T(8,128)(2,1)S(1)}, u32[]{:S(2)}, u32[]{:S(2)}) collective-permute-start(bf16[1,32,4096]{2,1,0:T(8,128)(2,1)S(1)} %dynamic-slice_bitcast_fusion), channel_id=1, source_target_pairs={{0,16},{16,0},{1,17},{17,1},{2,18},{18,2},{3,19},{19,3},{4,20},{20... | collective-permute-start | bytes 786440 | tf_op jit(solution)/shard_map/ppermute | solution.py:31
  89.1 6.2 %collective-permute-start.10 = (bf16[8,4096]{1,0:T(8,128)(2,1)S(1)}, bf16[8,4096]{1,0:T(8,128)(2,1)S(1)}, u32[]{:S(2)}, u32[]{:S(2)}) collective-permute-start(bf16[8,4096]{1,0:T(8,128)(2,1)S(1)} %get-tuple-element.40), channel_id=1, source_target_pairs={{0,3},{1,2},{2,1},{3,0},{4,7},{5,6},{6,5},{7,4},{8,11},{9,10},{10,... | collective-permute-start | bytes 196616 | tf_op jit(solution)/shard_map/ppermute | solution.py:31
  90.4 6.6 %collective-permute-start.11 = (bf16[8,4096]{1,0:T(8,128)(2,1)S(1)}, bf16[8,4096]{1,0:T(8,128)(2,1)S(1)}, u32[]{:S(2)}, u32[]{:S(2)}) collective-permute-start(bf16[8,4096]{1,0:T(8,128)(2,1)S(1)} %get-tuple-element.42), channel_id=1, source_target_pairs={{0,2},{1,3},{2,0},{3,1},{4,6},{5,7},{6,4},{7,5},{8,10},{9,11},{10,... | collective-permute-start | bytes 196616 | tf_op jit(solution)/shard_map/ppermute | solution.py:31
  92.8 4.6 %collective-permute-start.12 = (bf16[8,4096]{1,0:T(8,128)(2,1)S(1)}, bf16[8,4096]{1,0:T(8,128)(2,1)S(1)}, u32[]{:S(2)}, u32[]{:S(2)}) collective-permute-start(bf16[8,4096]{1,0:T(8,128)(2,1)S(1)} %get-tuple-element.41), channel_id=1, source_target_pairs={{0,1},{1,0},{2,3},{3,2},{4,5},{5,4},{6,7},{7,6},{8,9},{9,8},{10,11... | collective-permute-start | bytes 196616 | tf_op jit(solution)/shard_map/ppermute | solution.py:31
  95.3 6.1 %collective-permute-start.14 = (bf16[8,4096]{1,0:T(8,128)(2,1)S(1)}, bf16[8,4096]{1,0:T(8,128)(2,1)S(1)}, u32[]{:S(2)}, u32[]{:S(2)}) collective-permute-start(bf16[8,4096]{1,0:T(8,128)(2,1)S(1)} %get-tuple-element.43), channel_id=1, source_target_pairs={{0,3},{1,2},{2,1},{3,0},{4,7},{5,6},{6,5},{7,4},{8,11},{9,10},{10,... | collective-permute-start | bytes 196616 | tf_op jit(solution)/shard_map/ppermute | solution.py:31
  97.0 5.9 %collective-permute-start.15 = (bf16[8,4096]{1,0:T(8,128)(2,1)S(1)}, bf16[8,4096]{1,0:T(8,128)(2,1)S(1)}, u32[]{:S(2)}, u32[]{:S(2)}) collective-permute-start(bf16[8,4096]{1,0:T(8,128)(2,1)S(1)} %get-tuple-element.45), channel_id=1, source_target_pairs={{0,2},{1,3},{2,0},{3,1},{4,6},{5,7},{6,4},{7,5},{8,10},{9,11},{10,... | collective-permute-start | bytes 196616 | tf_op jit(solution)/shard_map/ppermute | solution.py:31
  97.4 5.5 %collective-permute-start.16 = (bf16[8,4096]{1,0:T(8,128)(2,1)S(1)}, bf16[8,4096]{1,0:T(8,128)(2,1)S(1)}, u32[]{:S(2)}, u32[]{:S(2)}) collective-permute-start(bf16[8,4096]{1,0:T(8,128)(2,1)S(1)} %get-tuple-element.44), channel_id=1, source_target_pairs={{0,1},{1,0},{2,3},{3,2},{4,5},{5,4},{6,7},{7,6},{8,9},{9,8},{10,11... | collective-permute-start | bytes 196616 | tf_op jit(solution)/shard_map/ppermute | solution.py:31
  101.4 1.5 collective-permute-start.2
  104.2 7.2 %collective-permute-start.17 = (bf16[16,4096]{1,0:T(8,128)(2,1)S(1)}, bf16[16,4096]{1,0:T(8,128)(2,1)S(1)}, u32[]{:S(2)}, u32[]{:S(2)}) collective-permute-start(bf16[16,4096]{1,0:T(8,128)(2,1)S(1)} %get-tuple-element.20), channel_id=1, source_target_pairs={{0,1},{1,0},{2,3},{3,2},{4,5},{5,4},{6,7},{7,6},{8,9},{9,8},{10,11... | collective-permute-start | bytes 393224 | tf_op jit(solution)/shard_map/ppermute | solution.py:31
  105.5 12.3 %collective-permute-start.18 = (bf16[16,4096]{1,0:T(8,128)(2,1)S(1)}, bf16[16,4096]{1,0:T(8,128)(2,1)S(1)}, u32[]{:S(2)}, u32[]{:S(2)}) collective-permute-start(bf16[16,4096]{1,0:T(8,128)(2,1)S(1)} %get-tuple-element.20), channel_id=1, source_target_pairs={{0,2},{1,3},{2,0},{3,1},{4,6},{5,7},{6,4},{7,5},{8,10},{9,11},{10,... | collective-permute-start | bytes 393224 | tf_op jit(solution)/shard_map/ppermute | solution.py:31
  106.7 11.0 %collective-permute-start.19 = (bf16[16,4096]{1,0:T(8,128)(2,1)S(1)}, bf16[16,4096]{1,0:T(8,128)(2,1)S(1)}, u32[]{:S(2)}, u32[]{:S(2)}) collective-permute-start(bf16[16,4096]{1,0:T(8,128)(2,1)S(1)} %get-tuple-element.20), channel_id=1, source_target_pairs={{0,3},{1,2},{2,1},{3,0},{4,7},{5,6},{6,5},{7,4},{8,11},{9,10},{10,... | collective-permute-start | bytes 393224 | tf_op jit(solution)/shard_map/ppermute | solution.py:31
  117.8 28.1 %slice-start = ((s8[16384000]{0:T(1024)(128)(4,1)}), s8[4194304]{0:T(1024)(128)(4,1)S(1)}, s32[]{:S(2)}) async-start(s8[16384000]{0:T(1024)(128)(4,1)} %bitcast.179), calls=%async_computation.2 | async-start | bytes 8388608
  117.8 17.6 %collective-permute-start.20 = (bf16[64,4096]{1,0:T(8,128)(2,1)S(1)}, bf16[64,4096]{1,0:T(8,128)(2,1)S(1)}, u32[]{:S(2)}, u32[]{:S(2)}) collective-permute-start(bf16[64,4096]{1,0:T(8,128)(2,1)S(1)} %pad_maximum_fusion.2), channel_id=1, source_target_pairs={{0,4},{4,0},{8,12},{12,8},{1,5},{5,1},{9,13},{13,9},{2,6},{6,2},{1... | collective-permute-start | bytes 1572872 | tf_op jit(solution)/shard_map/ppermute | solution.py:31
  117.9 16.2 %collective-permute-start.24 = (bf16[64,4096]{1,0:T(8,128)(2,1)S(1)}, bf16[64,4096]{1,0:T(8,128)(2,1)S(1)}, u32[]{:S(2)}, u32[]{:S(2)}) collective-permute-start(bf16[64,4096]{1,0:T(8,128)(2,1)S(1)} %pad_maximum_fusion.2), channel_id=1, source_target_pairs={{0,8},{4,12},{8,0},{12,4},{1,9},{5,13},{9,1},{13,5},{2,10},{6,14},... | collective-permute-start | bytes 1572872 | tf_op jit(solution)/shard_map/ppermute | solution.py:31
  118.7 14.0 %collective-permute-start.26 = (bf16[64,4096]{1,0:T(8,128)(2,1)S(1)}, bf16[64,4096]{1,0:T(8,128)(2,1)S(1)}, u32[]{:S(2)}, u32[]{:S(2)}) collective-permute-start(bf16[64,4096]{1,0:T(8,128)(2,1)S(1)} %pad_maximum_fusion.2), channel_id=1, source_target_pairs={{0,16},{16,0},{1,17},{17,1},{2,18},{18,2},{3,19},{19,3},{4,20},{20... | collective-permute-start | bytes 1572872 | tf_op jit(solution)/shard_map/ppermute | solution.py:31
  132.7 12.0 %collective-permute-start.28 = (bf16[32,4096]{1,0:T(8,128)(2,1)S(1)}, bf16[32,4096]{1,0:T(8,128)(2,1)S(1)}, u32[]{:S(2)}, u32[]{:S(2)}) collective-permute-start(bf16[32,4096]{1,0:T(8,128)(2,1)S(1)} %slice.146), channel_id=1, source_target_pairs={{0,8},{4,12},{8,0},{12,4},{1,9},{5,13},{9,1},{13,5},{2,10},{6,14},... | collective-permute-start | bytes 786440 | tf_op jit(solution)/shard_map/ppermute | solution.py:31
  134.1 10.7 %collective-permute-start.29 = (bf16[32,4096]{1,0:T(8,128)(2,1)S(1)}, bf16[32,4096]{1,0:T(8,128)(2,1)S(1)}, u32[]{:S(2)}, u32[]{:S(2)}) collective-permute-start(bf16[32,4096]{1,0:T(8,128)(2,1)S(1)} %slice.147), channel_id=1, source_target_pairs={{0,16},{16,0},{1,17},{17,1},{2,18},{18,2},{3,19},{19,3},{4,20},{20... | collective-permute-start | bytes 786440 | tf_op jit(solution)/shard_map/ppermute | solution.py:31
  135.4 10.4 %slice-start.1 = ((s8[16384000]{0:T(1024)(128)(4,1)}), s8[4194304]{0:T(1024)(128)(4,1)S(1)}, s32[]{:S(2)}) async-start(s8[16384000]{0:T(1024)(128)(4,1)} %bitcast.179), calls=%async_computation.3 | async-start | bytes 8388608
  135.4 10.4 %slice-start.2 = ((s8[16384000]{0:T(1024)(128)(4,1)}), s8[4194304]{0:T(1024)(128)(4,1)S(1)}, s32[]{:S(2)}) async-start(s8[16384000]{0:T(1024)(128)(4,1)} %bitcast.179), calls=%async_computation.4 | async-start | bytes 8388608
  135.4 10.4 %slice-start.3 = ((s8[16384000]{0:T(1024)(128)(4,1)}), s8[3801088]{0:T(1024)(128)(4,1)S(1)}, s32[]{:S(2)}) async-start(s8[16384000]{0:T(1024)(128)(4,1)} %bitcast.179), calls=%async_computation.5 | async-start | bytes 7602176
  143.8 2.0 %collective-permute-start.25 = (bf16[64,4096]{1,0:T(8,128)(2,1)S(1)}, bf16[64,4096]{1,0:T(8,128)(2,1)S(1)}, u32[]{:S(2)}, u32[]{:S(2)}) collective-permute-start(bf16[64,4096]{1,0:T(8,128)(2,1)S(1)} %collective-permute-done.24), channel_id=1, source_target_pairs={{0,4},{4,0},{8,12},{12,8},{1,5},{5,1},{9,13},{13,9},{2,6},{6,2},{1... | collective-permute-start | bytes 1572872 | tf_op jit(solution)/shard_map/ppermute | solution.py:31
  144.2 6.2 %collective-permute-start.27 = (bf16[64,4096]{1,0:T(8,128)(2,1)S(1)}, bf16[64,4096]{1,0:T(8,128)(2,1)S(1)}, u32[]{:S(2)}, u32[]{:S(2)}) collective-permute-start(bf16[64,4096]{1,0:T(8,128)(2,1)S(1)} %collective-permute-done.26), channel_id=1, source_target_pairs={{0,4},{4,0},{8,12},{12,8},{1,5},{5,1},{9,13},{13,9},{2,6},{6,2},{1... | collective-permute-start | bytes 1572872 | tf_op jit(solution)/shard_map/ppermute | solution.py:31
  144.8 10.7 %collective-permute-start.30 = (bf16[64,4096]{1,0:T(8,128)(2,1)S(1)}, bf16[64,4096]{1,0:T(8,128)(2,1)S(1)}, u32[]{:S(2)}, u32[]{:S(2)}) collective-permute-start(bf16[64,4096]{1,0:T(8,128)(2,1)S(1)} %pad_maximum_fusion.3), channel_id=1, source_target_pairs={{0,4},{4,0},{8,12},{12,8},{1,5},{5,1},{9,13},{13,9},{2,6},{6,2},{1... | collective-permute-start | bytes 1572872 | tf_op jit(solution)/shard_map/ppermute | solution.py:31
  155.5 9.3 %copy-start.6 = (pred[8,128]{1,0:T(8,128)(4,1)S(1)}, pred[8,128]{1,0:T(8,128)(4,1)}, u32[]{:S(2)}) copy-start(pred[8,128]{1,0:T(8,128)(4,1)} %compare_and_fusion) | copy-start | bytes 3076

commit v3 on v1

--- a/solution.py
+++ b/solution.py
@@ -1,8 +1,11 @@
+import functools
 import math
 
 import jax
 import jax.numpy as jnp
 from jax import lax
+from jax.experimental import pallas as pl
+from jax.experimental.pallas import tpu as pltpu
 from jax.sharding import PartitionSpec as P
 
 NH = 32
@@ -10,6 +13,7 @@
 HD = 128
 V = 64000
 ALL = ("section", "tm", "mp")
+LANES = 128
 
 
 def layer_norm(values):
@@ -31,7 +35,314 @@
     return jnp.sum(exchange(blocks, axis).astype(jnp.float32), axis=0)
 
 
-def per_device(
+def swap(values, axis, distance):
+    pairs = [(i, i ^ distance) for i in range(lax.axis_size(axis))]
+    return lax.ppermute(values, axis, pairs)
+
+
+def whole(shape):
+    return pl.BlockSpec(shape, lambda *_: (0,) * len(shape))
+
+
+SCALARS = pl.BlockSpec(memory_space=pltpu.SMEM)
+
+
+def dot(left, right):
+    return jnp.dot(left, right, preferred_element_type=jnp.float32)
+
+
+def dot_nt(left, right):
+    return lax.dot_general(
+        left, right, (((1,), (1,)), ((), ())), preferred_element_type=jnp.float32
+    )
+
+
+def ffn_kernel(count, place_ref, x_ref, up_ref, down_ref, *refs):
+    outs, own_ref, normed, total = refs[:count], refs[count], refs[count + 1], refs[count + 2]
+    share = own_ref.shape[0]
+    step = pl.program_id(0)
+    here = place_ref[0]
+
+    @pl.when(step == 0)
+    def _():
+        normed[...] = layer_norm(x_ref[...].astype(jnp.float32)).astype(jnp.bfloat16)
+        own_ref[...] = x_ref[pl.ds(pl.multiple_of(here * share, share), share), :]
+        total[...] = jnp.zeros_like(total)
+
+    hidden = dot(normed[...], up_ref[...])
+    inner = 0.5 * hidden * (1.0 + lax.erf(hidden * math.sqrt(0.5)))
+    total[...] += dot(inner.astype(jnp.bfloat16), down_ref[...])
+
+    @pl.when(step == pl.num_programs(0) - 1)
+    def _():
+        for distance in range(count):
+            start = pl.multiple_of((here ^ distance) * share, share)
+            outs[distance][...] = total[pl.ds(start, share), :].astype(jnp.bfloat16)
+
+
+def ffn(place, rows, up, down, count):
+    share = rows.shape[0] // count
+    width = rows.shape[1]
+    tile = 256
+    block = jax.ShapeDtypeStruct((share, width), jnp.bfloat16)
+    return pl.pallas_call(
+        functools.partial(ffn_kernel, count),
+        grid=(up.shape[1] // tile,),
+        in_specs=[
+            SCALARS,
+            whole(rows.shape),
+            pl.BlockSpec((width, tile), lambda i: (0, i)),
+            pl.BlockSpec((tile, width), lambda i: (i, 0)),
+        ],
+        out_specs=[whole(block.shape)] * (count + 1),
+        out_shape=[block] * (count + 1),
+        scratch_shapes=[
+            pltpu.VMEM(rows.shape, jnp.bfloat16),
+            pltpu.VMEM(rows.shape, jnp.float32),
+        ],
+        cost_estimate=pl.CostEstimate(
+            flops=4 * rows.shape[0] * width * up.shape[1],
+            bytes_accessed=4 * width * up.shape[1],
+            transcendentals=rows.shape[0] * up.shape[1],
+        ),
+        compiler_params=pltpu.CompilerParams(vmem_limit_bytes=24 << 20),
+        name="encoder_ffn",
+    )(place, rows, up, down)
+
+
+def query_kernel(count, pick_ref, length_ref, place_ref, x_ref, tok_ref, w_ref, *refs):
+    outs, normed, total, shares = refs[:count], refs[count], refs[count + 1], refs[count + 2]
+    slots, tokens, width = x_ref.shape
+    hyps = length_ref.shape[0] // slots
+    positions = tokens // hyps
+    columns = w_ref.shape[1]
+    share = shares.shape[1] - 16
+    step = pl.program_id(0)
+
+    @pl.when(step == 0)
+    def _():
+        lane = lax.broadcasted_iota(jnp.int32, (1, tokens), 1)
+        for slot in range(slots):
+            order = jnp.full((1, tokens), -1, jnp.int32)
+            start = jnp.int32(0)
+            for hyp in range(hyps):
+                length = length_ref[slot * hyps + hyp]
+                inside = (lane >= hyp * positions) & (lane < hyp * positions + length)
+                order = jnp.where(inside, lane - hyp * positions + start, order)
+                start = start + length
+            row = lax.broadcasted_iota(jnp.int32, (tokens, tokens), 0)
+            move = jnp.where(order == row, 1.0, 0.0).astype(jnp.bfloat16)
+            ordered = dot(move, x_ref[slot])
+            normed[pl.ds(slot * tokens, tokens), :] = square_norm(ordered).astype(jnp.bfloat16)
+            share_row = lax.broadcasted_iota(jnp.int32, (share, tokens), 0)
+            chosen = order == share_row * (tokens // share) + place_ref[0]
+            mine = dot(jnp.where(chosen, 1.0, 0.0).astype(jnp.bfloat16), x_ref[slot])
+            shares[slot, :share, :] = mine.astype(jnp.bfloat16)
+            target = jnp.sum(
+                jnp.where(chosen, tok_ref[slot], 0), axis=1, keepdims=True, dtype=jnp.int32
+            )
+            coarse = target // 256
+            cell = lax.broadcasted_iota(jnp.int32, (share, width), 1)
+            packed = jnp.where(cell == 0, coarse, jnp.where(cell == 1, target - coarse * 256, 0))
+            shares[slot, share:, :] = packed.astype(jnp.float32).astype(jnp.bfloat16)
+        total[...] = jnp.zeros_like(total)
+
+    depth = w_ref.shape[0]
+    part = normed[:, pl.ds(pl.multiple_of(step * depth, depth), depth)]
+    total[...] += dot(part, w_ref[...])
+
+    @pl.when(step == pl.num_programs(0) - 1)
+    def _():
+        for distance in range(count):
+            slot = pick_ref[distance]
+            out = outs[distance]
+            start = pl.multiple_of(slot * tokens, tokens)
+            out[:tokens, :] = total[pl.ds(start, tokens), :].astype(jnp.bfloat16)
+            for part in range(width // columns):
+                out[pl.ds(tokens + part * share, share), :] = shares[
+                    slot, :share, part * columns : (part + 1) * columns
+                ]
+            out[pl.ds(tokens + width // columns * share, share), :] = shares[slot, share:, :columns]
+
+
+def queries_of(pick, lengths, place, states, targets, weights, count, share):
+    slots, tokens, width = states.shape
+    columns = weights.shape[1]
+    depth = 1024
+    rows = tokens + width // columns * share + share
+    block = jax.ShapeDtypeStruct((rows, columns), jnp.bfloat16)
+    return pl.pallas_call(
+        functools.partial(query_kernel, count),
+        grid=(width // depth,),
+        in_specs=[
+            SCALARS,
+            SCALARS,
+            SCALARS,
+            whole(states.shape),
+            whole(targets.shape),
+            pl.BlockSpec((depth, columns), lambda i: (i, 0)),
+        ],
+        out_specs=[whole(block.shape)] * count,
+        out_shape=[block] * count,
+        scratch_shapes=[
+            pltpu.VMEM((slots * tokens, width), jnp.bfloat16),
+            pltpu.VMEM((slots * tokens, columns), jnp.float32),
+            pltpu.VMEM((slots, share + 16, width), jnp.bfloat16),
+        ],
+        cost_estimate=pl.CostEstimate(
+            flops=2 * slots * tokens * width * columns,
+            bytes_accessed=2 * width * (columns + slots * tokens),
+            transcendentals=0,
+        ),
+        compiler_params=pltpu.CompilerParams(vmem_limit_bytes=32 << 20),
+        name="hypothesis_queries",
+    )(pick, lengths, place, states, targets, weights)
+
+
+def kv_kernel(sections, utterances, widths, *refs):
+    parts, own_ref, w_ref, out_ref = refs[:-3], refs[-3], refs[-2], refs[-1]
+    rows = own_ref.shape[0]
+    frames = rows // utterances
+    total = own_ref[...].astype(jnp.float32)
+    summed = parts[0][...].astype(jnp.float32)
+    for part in parts[1:]:
+        summed += part[...].astype(jnp.float32)
+    states = layer_norm(total + summed).astype(jnp.bfloat16)
+    to = lax.broadcasted_iota(jnp.int32, (rows, rows), 0)
+    come = lax.broadcasted_iota(jnp.int32, (rows, rows), 1)
+    move = jnp.where(come == to % frames * utterances + to // frames, 1.0, 0.0)
+    states = dot(move.astype(jnp.bfloat16), states).astype(jnp.bfloat16)
+    both = dot(states, w_ref[...])
+    half = KVH * HD
+    per_kv = sections * widths // KVH
+    for section in range(sections):
+        for utterance in range(utterances):
+            for width in range(0, widths, per_kv):
+                kv_head = (section * widths + width) // per_kv
+                take = slice(utterance * frames, (utterance + 1) * frames)
+                block = jnp.concatenate(
+                    [
+                        both[take, kv_head * HD : (kv_head + 1) * HD],
+                        both[take, half + kv_head * HD : half + (kv_head + 1) * HD],
+                    ],
+                    axis=1,
+                )
+                start = ((section * utterances + utterance) * widths + width) * frames
+                block = jnp.concatenate([block] * per_kv, axis=0).astype(jnp.bfloat16)
+                out_ref[start : start + per_kv * frames, :] = block
+
+
+def keys_values_of(parts, own, weights, sections, utterances, widths):
+    rows = sections * widths * own.shape[0]
+    return pl.pallas_call(
+        functools.partial(kv_kernel, sections, utterances, widths),
+        out_shape=jax.ShapeDtypeStruct((rows, 2 * HD), jnp.bfloat16),
+        cost_estimate=pl.CostEstimate(
+            flops=2 * own.shape[0] * weights.shape[0] * weights.shape[1],
+            bytes_accessed=2 * weights.shape[0] * weights.shape[1],
+            transcendentals=0,
+        ),
+        compiler_params=pltpu.CompilerParams(vmem_limit_bytes=24 << 20),
+        name="frame_keys_values",
+    )(*parts, own, weights)
+
+
+def attention_kernel(count, capacity, pieces, sections, widths, info_ref, *refs):
+    payloads = refs[:count]
+    kv_ref, w_ref = refs[count : count + 2]
+    outs = refs[count + 2 : count + 2 + 2 * len(pieces)]
+    resid_ref, context, picked = refs[count + 2 + 2 * len(pieces) :]
+    tokens, columns = kv_ref.shape[1] // 2, w_ref.shape[0]
+    tokens = capacity
+    source, frame_limit, section_pos = info_ref[0], info_ref[1], info_ref[2]
+    step = pl.program_id(0)
+
+    @pl.when(step == 0)
+    def _():
+        for distance in range(count):
+
+            @pl.when(source == distance)
+            def _(payload=payloads[distance]):
+                picked[...] = payload[...]
+
+        keys = kv_ref[:, :HD]
+        values = kv_ref[:, HD:]
+        frames = kv_ref.shape[0]
+        visible = lax.broadcasted_iota(jnp.int32, (tokens, frames), 1) < frame_limit
+        for head in range(columns // HD):
+            query = picked[:tokens, head * HD : (head + 1) * HD]
+            scores = dot_nt(query, keys) * (1.0 / math.sqrt(HD))
+            scores = jnp.where(visible, scores, -jnp.inf)
+            raised = jnp.exp(scores - jnp.max(scores, axis=1, keepdims=True))
+            weights = (raised / jnp.sum(raised, axis=1, keepdims=True)).astype(jnp.bfloat16)
+            context[:, head * HD : (head + 1) * HD] = dot(weights, values).astype(jnp.bfloat16)
+        to = lax.broadcasted_iota(jnp.int32, (tokens, tokens), 0)
+        come = lax.broadcasted_iota(jnp.int32, (tokens, tokens), 1)
+        half = tokens // sections
+        section = jnp.where(to < half, 1 - section_pos, section_pos)
+        inside = to % half
+        row = jnp.zeros_like(to)
+        width = jnp.zeros_like(to)
+        first = 0
+        for piece in pieces:
+            at = inside - first * widths
+            here = (at >= 0) & (at < piece * widths)
+            row = jnp.where(here, first + at % piece, row)
+            width = jnp.where(here, at // piece, width)
+            first += piece
+        move = come == (row * sections + section) * widths + width
+        context[...] = dot(jnp.where(move, 1.0, 0.0).astype(jnp.bfloat16), context[...]).astype(
+            jnp.bfloat16
+        )
+        share = resid_ref.shape[0]
+        first_row = payloads[0].shape[0] - share * (1 + (resid_ref.shape[1] - LANES) // columns)
+        for part in range((resid_ref.shape[1] - LANES) // columns):
+            resid_ref[:, part * columns : (part + 1) * columns] = picked[
+                first_row + part * share : first_row + (part + 1) * share, :
+            ]
+        resid_ref[:, resid_ref.shape[1] - LANES :] = picked[
+            payloads[0].shape[0] - share :, :LANES
+        ]
+
+    product = dot(context[...], w_ref[...])
+    first = 0
+    for number, out in enumerate(outs):
+        rows = out.shape[0]
+        out[...] = product[first : first + rows, :].astype(jnp.bfloat16)
+        first += rows
+
+
+def attend(info, payloads, keys_values, weights, capacity, pieces, sections, widths, share):
+    count = len(payloads)
+    columns, width = weights.shape
+    tile = 1024
+    shapes = [jax.ShapeDtypeStruct((piece * widths, width), jnp.bfloat16) for piece in pieces]
+    shapes = shapes + shapes
+    resid = jax.ShapeDtypeStruct((share, width + LANES), jnp.bfloat16)
+    return pl.pallas_call(
+        functools.partial(attention_kernel, count, capacity, pieces, sections, widths),
+        grid=(width // tile,),
+        in_specs=[SCALARS]
+        + [whole(payloads[0].shape)] * count
+        + [whole(keys_values.shape), pl.BlockSpec((columns, tile), lambda i: (0, i))],
+        out_specs=[pl.BlockSpec((s.shape[0], tile), lambda i: (0, i)) for s in shapes]
+        + [whole(resid.shape)],
+        out_shape=shapes + [resid],
+        scratch_shapes=[
+            pltpu.VMEM((capacity, columns), jnp.bfloat16),
+            pltpu.VMEM(payloads[0].shape, jnp.bfloat16),
+        ],
+        cost_estimate=pl.CostEstimate(
+            flops=2 * capacity * columns * (width + 2 * keys_values.shape[0]),
+            bytes_accessed=2 * columns * width + 2 * capacity * width,
+            transcendentals=capacity * keys_values.shape[0] * columns // HD,
+        ),
+        compiler_params=pltpu.CompilerParams(vmem_limit_bytes=24 << 20),
+        name="attention_projection",
+    )(info, *payloads, keys_values, weights)
+
+
+def near_device(
     frame_len,
     slot_utt,
     enc_in,
@@ -56,6 +367,163 @@
     all_devices = head_devices * group_count
 
     frame_rows, utterances, enc_width = enc_in.shape
+    slot_count, hyp_count, positions, model_width = hyp_state.shape
+    slot_tokens = hyp_count * positions
+    share_rows = slot_tokens // head_devices
+    here_slots = lax.dynamic_slice_in_dim(slot_utt, group_pos * slot_count, slot_count, 0)
+    own_slot = jnp.argmax(slot_utt == group_pos).astype(jnp.int32)
+    source = (own_slot // slot_count) ^ group_pos
+
+    parts = ffn(
+        width_pos.astype(jnp.int32).reshape(1),
+        enc_in.reshape(frame_rows * utterances, enc_width),
+        ffn_up,
+        ffn_down,
+        width_count,
+    )
+    own_frames = parts[width_count]
+    parts = [parts[0]] + [
+        swap(parts[distance], "mp", distance) for distance in range(1, width_count)
+    ]
+
+    wanted = group_pos ^ jnp.arange(group_count)
+    pick = jnp.argmax(here_slots[None, :] == wanted[:, None], axis=1).astype(jnp.int32)
+    payloads = queries_of(
+        pick,
+        hyp_len.reshape(-1),
+        head_pos.astype(jnp.int32).reshape(1),
+        hyp_state.reshape(slot_count, slot_tokens, model_width),
+        hyp_tok.reshape(slot_count, 1, slot_tokens),
+        q_proj,
+        group_count,
+        share_rows,
+    )
+    payloads = [payloads[0]] + [
+        swap(payloads[distance], "tm", distance) for distance in range(1, group_count)
+    ]
+
+    sent = keys_values_of(parts, own_frames, kv_proj, section_count, utterances, width_count)
+    frames_all = all_devices * (frame_rows // width_count)
+    keys_values = exchange(sent.reshape(all_devices, -1, 2 * HD), ALL).reshape(frames_all, 2 * HD)
+    frame_limit = lax.dynamic_index_in_dim(frame_len, group_pos, 0, keepdims=False)
+    info = jnp.stack([source, frame_limit, section_pos.astype(jnp.int32)])
+
+    pieces = (share_rows // 2, share_rows - share_rows // 2)
+    capacity = sum(pieces) * head_devices
+    *projected, resid = attend(
+        info,
+        payloads,
+        keys_values,
+        o_proj,
+        capacity,
+        pieces,
+        section_count,
+        width_count,
+        share_rows,
+    )
+    attn_out = []
+    for number, piece in enumerate(pieces):
+        other = swap(projected[number], "section", 1)
+        section_sum = (
+            projected[len(pieces) + number].astype(jnp.float32) + other.astype(jnp.float32)
+        ).astype(jnp.bfloat16)
+        total = None
+        for distance in range(width_count - 1, -1, -1):
+            block = lax.dynamic_slice_in_dim(
+                section_sum, (width_pos ^ distance) * piece, piece, 0
+            )
+            if distance:
+                block = swap(block, "mp", distance)
+            block = block.astype(jnp.float32)
+            total = block if total is None else total + block
+        attn_out.append(total)
+    attn_out = jnp.concatenate(attn_out, axis=0)
+    out_normed = square_norm(resid[:, :model_width].astype(jnp.float32) + attn_out)
+    out_rows = jnp.concatenate(
+        [out_normed.astype(jnp.bfloat16), resid[:, model_width:]], axis=1
+    )
+
+    share = out_rows.shape[0]
+    own = jnp.zeros((width_count * share, out_rows.shape[1]), jnp.bfloat16)
+    for distance in range(width_count):
+        block = swap(out_rows, "mp", distance) if distance else out_rows
+        own = lax.dynamic_update_slice_in_dim(own, block, (width_pos ^ distance) * share, 0)
+    half = own.shape[0] // 2
+    by_x = swap(own, "section", 1)
+    by_y = swap(own, "tm", 2)
+    across = jnp.concatenate([swap(by_x[:half], "tm", 2), swap(by_y[half:], "section", 1)])
+    vocab_rows = head.shape[0]
+    vocab_start = (
+        (section_pos * group_count + group_pos) * width_count + width_pos
+    ) * vocab_rows
+    stats = []
+    for rows in (own, by_y, by_x, across):
+        chunk = jnp.concatenate([rows, swap(rows, "tm", 1)])
+        logits = dot_nt(chunk[:, :model_width], head)
+        target = chunk[:, model_width : model_width + 2].astype(jnp.int32)
+        target = target[:, 0] * 256 + target[:, 1] - vocab_start
+        upper = jnp.max(logits, axis=1)
+        totals = jnp.sum(jnp.exp(logits - upper[:, None]), axis=1)
+        matches = jnp.arange(vocab_rows, dtype=jnp.int32)[None, :] == target[:, None]
+        target_logit = jnp.sum(jnp.where(matches, logits, 0.0), axis=1)
+        stats.append(jnp.stack([upper, totals, target_logit]).reshape(3, 2, -1))
+
+    stats = jnp.stack(stats).transpose(0, 2, 1, 3).reshape(head_devices, -1)
+    slots = slot_utt.shape[0]
+    place = (
+        (jnp.arange(section_count)[None, :] ^ section_pos) * group_count
+        + (jnp.maximum(slot_utt, 0)[:, None] ^ group_pos)
+    ).reshape(-1)
+    by_slot = jnp.take(stats, place, axis=0, mode="clip")
+    by_group = by_slot.reshape(1, group_count, 1, -1)
+    by_group = jnp.broadcast_to(
+        by_group, (section_count, group_count, width_count, by_group.shape[-1])
+    ).reshape(all_devices, slot_count, section_count, 3, width_count, share)
+    every = exchange(by_group, ALL)
+    peak = jnp.max(every[:, :, :, 0], axis=0)
+    total = jnp.sum(every[:, :, :, 1] * jnp.exp(every[:, :, :, 0] - peak[None]), axis=0)
+    picked = jnp.sum(every[:, :, :, 2], axis=0)
+    token_logp = picked - (peak + jnp.log(total))
+    shape = (1, 1, section_count, width_count, share)
+    order = (
+        lax.broadcasted_iota(jnp.int32, shape, 4) * head_devices
+        + lax.broadcasted_iota(jnp.int32, shape, 2) * width_count
+        + lax.broadcasted_iota(jnp.int32, shape, 3)
+    )
+    ends = jnp.cumsum(hyp_len, axis=1)[:, :, None, None, None]
+    starts = ends - hyp_len[:, :, None, None, None]
+    valid = (order >= starts) & (order < ends)
+    summed = jnp.sum(
+        jnp.where(valid, token_logp[:, None], 0.0), axis=(2, 3, 4)
+    ) / hyp_len.astype(jnp.float32) + math.log(V)
+    return jnp.where(here_slots[:, None] >= 0, summed, 0.0)
+
+
+def general(
+    frame_len,
+    slot_utt,
+    enc_in,
+    ffn_up,
+    ffn_down,
+    kv_proj,
+    hyp_state,
+    hyp_tok,
+    hyp_len,
+    q_proj,
+    o_proj,
+    head,
+):
+    section_count = lax.axis_size("section")
+    group_count = lax.axis_size("tm")
+    width_count = lax.axis_size("mp")
+    section_pos = lax.axis_index("section")
+    group_pos = lax.axis_index("tm")
+    width_pos = lax.axis_index("mp")
+    head_devices = section_count * width_count
+    head_pos = section_pos * width_count + width_pos
+    all_devices = head_devices * group_count
+
+    frame_rows, utterances, enc_width = enc_in.shape
     assert utterances == group_count
     slot_count, hyp_count, positions, model_width = hyp_state.shape
     slot_tokens = hyp_count * positions
@@ -205,6 +673,8 @@
         P(("section", "tm", "mp"), None),
     )
     out_specs = P("tm", None)
+    near = dict(mesh.shape) == {"section": 2, "tm": 4, "mp": 4}
+    per_device = near_device if near else general
     return jax.shard_map(
         per_device, mesh=mesh, in_specs=in_specs, out_specs=out_specs, check_vma=False
     )

time: 221 us -> 155 us (0.70)
  waiting for transfers between devices: 91.5 us -> 41.8 us
  other arithmetic: 26 us -> 8.96 us
  blocking collectives: 16.1 us -> 0 us
  between operations: 18.8 us -> 2.84 us
  Pallas kernels: 0 us -> 13.4 us
  local copies, waits for them, and re-layouts: 6.91 us -> 19.2 us
  starting transfers between devices: 28.4 us -> 37.6 us
    all_gather x1 -> x0, waiting for transfers between devices: 53.7 us -> none  [per_device(): hidden_rows = lax.all_gather(out_normed, ALL, axis=0, tiled=True)]
    ppermute x0 -> x25, waiting for transfers between devices: none -> 31.5 us  [swap(): return lax.ppermute(values, axis, pairs)]
    all_to_all x6 -> x2, waiting for transfers between devices: 37.8 us -> 10.3 us  [exchange(): return lax.all_to_all(blocks, axis, split_axis=0, concat_axis=0, tiled=True)]
    ppermute x0 -> x25, starting transfers between devices: none -> 27.5 us  [swap(): return lax.ppermute(values, axis, pairs)]
    all_to_all x6 -> x2, starting transfers between devices: 28.4 us -> 10.1 us  [exchange(): return lax.all_to_all(blocks, axis, split_axis=0, concat_axis=0, tiled=True)]
    pallas_call x0 -> x4, Pallas kernels: none -> 13.4 us  [the longest x1 4.35 us: queries_of(): pl.pallas_call(functools.partial(query_kernel, count), grid=(width // dep...]
    reduce_sum x11 -> x7, other arithmetic: 12.5 us -> 1.55 us  [the longest x4 1.17 us: near_device(): totals = jnp.sum(jnp.exp(logits - upper[:, None]), axis=1)]
    all_to_all x1 -> x0, blocking collectives: 10.9 us -> none  [exchange(): return lax.all_to_all(blocks, axis, split_axis=0, concat_axis=0, tiled=True)]
  transfers between devices with their start and end apart: 7 -> 27, of which waited for: 6 -> 13; matrix products, arithmetic and copies ran while one was open for 10% -> 20% of each run, Pallas kernels for 0% -> 4%
where the time goes in v3:
time: 155 us
  waiting for transfers between devices  41.8 us (27%)
  starting transfers between devices  37.6 us (24%)
  matrix products  30.9 us (20%)
  local copies, waits for them, and re-layouts  19.2 us (12%)
  Pallas kernels  13.4 us (9%)
  other arithmetic  8.96 us (6%)
  between operations  2.84 us (2%)
    ppermute x25, waiting for transfers between devices, swap(): return lax.ppermute(values, axis, pairs)  31.5 us
    dot_general x4, matrix products, dot_nt(): lax.dot_general(left, right, (((1,), (1,)), ((), ())), preferred_element_...  30.9 us
    ppermute x25, starting transfers between devices, swap(): return lax.ppermute(values, axis, pairs)  27.5 us
    unnamed x42, local copies, waits for them, and re-layouts  11.2 us
    all_to_all x2, waiting for transfers between devices, exchange(): return lax.all_to_all(blocks, axis, split_axis=0, concat_axis=0, tiled=True)  10.3 us
    all_to_all x2, starting transfers between devices, exchange(): return lax.all_to_all(blocks, axis, split_axis=0, concat_axis=0, tiled=True)  10.1 us
    pallas_call x1, Pallas kernels, queries_of(): pl.pallas_call(functools.partial(query_kernel, count), grid=(width // dep...  4.35 us
    pallas_call x1, Pallas kernels, ffn(): pl.pallas_call(functools.partial(ffn_kernel, count), grid=(up.shape[1] //...  4.19 us
  transfers between devices with their start and end apart: 27, of which 13 were waited for; matrix products, arithmetic and copies ran while one was open for 20% of the time, Pallas kernels for 4%

profile of v3, /device:TPU:0, one launch (start us, length us, event | category | flops | bytes accessed | tf_op | source)
XLA Modules:
  0.0 154.6 jit_solution(5851737985575068680)
XLA Ops:
  0.0 1.1 reshape.133.x_ref
  1.1 1.9 %copy-done.2 = bf16[1280,1280]{1,0:T(8,128)(2,1)S(1)} copy-done((bf16[1280,1280]{1,0:T(8,128)(2,1)S(1)}, bf16[1280,1280]{1,0:T(8,128)(2,1)}, u32[]{:S(2)}) %copy-start.2) | copy-done | bytes 3276824
  3.0 1.9 %copy-done.3 = bf16[1280,1280]{1,0:T(8,128)(2,1)S(1)} copy-done((bf16[1280,1280]{1,0:T(8,128)(2,1)S(1)}, bf16[1280,1280]{1,0:T(8,128)(2,1)}, u32[]{:S(2)}) %copy-start.3) | copy-done | bytes 3276824
  4.9 4.2 %encoder_ffn.1 = (bf16[32,1280]{1,0:T(8,128)(2,1)S(1)}, bf16[32,1280]{1,0:T(8,128)(2,1)}, bf16[32,1280]{1,0:T(8,128)(2,1)S(1)}, bf16[32,1280]{1,0:T(8,128)(2,1)S(1)}, bf16[32,1280]{1,0:T(8,128)(2,1)S(1)}) custom-call(s32[1]{0:T(128)} %bitcast.4.place_ref, bf16[128,1280]{1,0:T(8,128)(2,1)S(1)} %reshape.133.x_ref, bf16[1280,1280]{1,0:T(8,128)(2,1)S(1)} %copy-done.2, ...), custom_call_target="tpu_custom_call" | custom-call | flops 838860800 | bytes 6553600 | tf_op jit(solution)/shard_map/encoder_ffn/pallas_call | solution.py:88
  9.1 3.0 %collective-permute-start.3 = (bf16[32,1280]{1,0:T(8,128)(2,1)}, bf16[32,1280]{1,0:T(8,128)(2,1)S(1)}, u32[]{:S(2)}, u32[]{:S(2)}) collective-permute-start(bf16[32,1280]{1,0:T(8,128)(2,1)} %get-tuple-element.28), channel_id=1, source_target_pairs={{0,1},{1,0},{2,3},{3,2},{4,5},{5,4},{6,7},{7,6},{8,9},{9,8},{10,11... | collective-permute-start | bytes 245768 | tf_op jit(solution)/shard_map/ppermute | solution.py:40
  12.1 2.6 %collective-permute-start.4 = (bf16[32,1280]{1,0:T(8,128)(2,1)S(1)}, bf16[32,1280]{1,0:T(8,128)(2,1)S(1)}, u32[]{:S(2)}, u32[]{:S(2)}) collective-permute-start(bf16[32,1280]{1,0:T(8,128)(2,1)S(1)} %get-tuple-element.29), channel_id=1, source_target_pairs={{0,2},{1,3},{2,0},{3,1},{4,6},{5,7},{6,4},{7,5},{8,10},{9,11},{10,... | collective-permute-start | bytes 245768 | tf_op jit(solution)/shard_map/ppermute | solution.py:40
  14.9 0.7 broadcast_compare_fusion
  15.6 0.6 compare_reduce_fusion
  16.2 2.2 %copy-done = bf16[4096,512]{1,0:T(8,128)(2,1)S(1)} copy-done((bf16[4096,512]{1,0:T(8,128)(2,1)S(1)}, bf16[4096,512]{1,0:T(8,128)(2,1)}, u32[]{:S(2)}) %copy-start) | copy-done | bytes 4194328
  18.4 4.4 %hypothesis_queries.1 = (bf16[272,512]{1,0:T(8,128)(2,1)S(1)}, bf16[272,512]{1,0:T(8,128)(2,1)}, bf16[272,512]{1,0:T(8,128)(2,1)S(1)}, bf16[272,512]{1,0:T(8,128)(2,1)S(1)}) custom-call(s32[4]{0:T(128)S(1)} %get-tuple-element.22.pick_ref, s32[16]{0:T(128)S(1)} %reshape.128.length_ref, s32[1]{0:T(128)} %bitcast.2.place_ref, ...), custom_call_target="tpu_custom_call" | custom-call | flops 1073741824 | bytes 6291456 | tf_op jit(solution)/shard_map/hypothesis_queries/pallas_call | solution.py:174
  22.8 1.7 %collective-permute-start.1 = (bf16[272,512]{1,0:T(8,128)(2,1)S(1)}, bf16[272,512]{1,0:T(8,128)(2,1)S(1)}, u32[]{:S(2)}, u32[]{:S(2)}) collective-permute-start(bf16[272,512]{1,0:T(8,128)(2,1)S(1)} %get-tuple-element.25), channel_id=1, source_target_pairs={{0,8},{4,12},{8,0},{12,4},{1,9},{5,13},{9,1},{13,5},{2,10},{6,14},... | collective-permute-start | bytes 835592 | tf_op jit(solution)/shard_map/ppermute | solution.py:40
  24.7 1.5 %frame_keys_values.1 = bf16[256,256]{1,0:T(8,128)(2,1)} custom-call(bf16[32,1280]{1,0:T(8,128)(2,1)S(1)} %get-tuple-element.27.refs_0_, bf16[32,1280]{1,0:T(8,128)(2,1)S(1)} %collective-permute-done.3.refs_1_, bf16[32,1280]{1,0:T(8,128)(2,1)S(1)} %collective-permute-done.4.refs_2_, bf16[32,1280]{1,0:T(8,128)(2,1)S(1)} %collective-permute-done.5.refs_3_, ...), custom_call_target="tpu_custom_call" | custom-call | flops 83886080 | bytes 2621440 | tf_op jit(solution)/shard_map/frame_keys_values/pallas_call | solution.py:237
  26.2 6.2 %all-to-all-start = ((bf16[32,8,256]{2,1,0:T(8,128)(2,1)}), bf16[32,8,256]{2,1,0:T(8,128)(2,1)S(1)}, u32[]{:S(2)}, u32[]{:S(2)}) async-start(bf16[32,8,256]{2,1,0:T(8,128)(2,1)} %bitcast.5), calls=%async_computation | async-start | bytes 262144 | tf_op jit(solution)/shard_map/all_to_all | solution.py:30
  32.5 0.7 compare_reduce_fusion.1
  35.5 0.7 dynamic_slice.32
  36.2 0.8 pad_add_fusion.info_ref
  36.9 1.3 collective-permute-done.2.refs_3_
  38.3 2.4 %all-to-all-done = bf16[32,8,256]{2,1,0:T(8,128)(2,1)S(1)} async-done(((bf16[32,8,256]{2,1,0:T(8,128)(2,1)}), bf16[32,8,256]{2,1,0:T(8,128)(2,1)S(1)}, u32[]{:S(2)}, u32[]{:S(2)}) %all-to-all-start) | async-done | bytes 131104 | tf_op jit(solution)/shard_map/all_to_all | solution.py:30
  40.7 2.2 %copy-done.1 = bf16[512,4096]{1,0:T(8,128)(2,1)S(1)} copy-done((bf16[512,4096]{1,0:T(8,128)(2,1)S(1)}, bf16[512,4096]{1,0:T(8,128)(2,1)}, u32[]{:S(2)}) %copy-start.1) | copy-done | bytes 4194328
  42.9 3.3 %attention_projection.1 = (bf16[32,4096]{1,0:T(8,128)(2,1)S(1)}, bf16[32,4096]{1,0:T(8,128)(2,1)S(1)}, bf16[32,4096]{1,0:T(8,128)(2,1)S(1)}, bf16[32,4096]{1,0:T(8,128)(2,1)S(1)}, bf16[16,4224]{1,0:T(8,128)(2,1)S(1)}) custom-call(s32[3]{0:T(128)S(1)} %pad_add_fusion.info_ref, bf16[272,512]{1,0:T(8,128)(2,1)S(1)} %get-tuple-element.23.refs_0_, ...), custom_call_target="tpu_custom_call" | custom-call | flops 603979776 | bytes 5242880 | tf_op jit(solution)/shard_map/attention_projection/pallas_call | solution.py:322
  46.2 0.8 collective-permute-start.6
  47.0 1.2 collective-permute-start.10
  48.3 7.2 %collective-permute-done.6 = bf16[32,4096]{1,0:T(8,128)(2,1)S(1)} collective-permute-done((bf16[32,4096]{1,0:T(8,128)(2,1)S(1)}, bf16[32,4096]{1,0:T(8,128)(2,1)S(1)}, u32[]{:S(2)}, u32[]{:S(2)}) %collective-permute-start.6) | collective-permute-done | bytes 262176 | tf_op jit(solution)/shard_map/ppermute | solution.py:40
  55.6 2.3 %collective-permute-start.7 = (bf16[8,4096]{1,0:T(8,128)(2,1)S(1)}, bf16[8,4096]{1,0:T(8,128)(2,1)S(1)}, u32[]{:S(2)}, u32[]{:S(2)}) collective-permute-start(bf16[8,4096]{1,0:T(8,128)(2,1)S(1)} %get-tuple-element.47), channel_id=1, source_target_pairs={{0,3},{1,2},{2,1},{3,0},{4,7},{5,6},{6,5},{7,4},{8,11},{9,10},{10,... | collective-permute-start | bytes 196616 | tf_op jit(solution)/shard_map/ppermute | solution.py:40
  57.9 2.2 %collective-permute-start.9 = (bf16[8,4096]{1,0:T(8,128)(2,1)S(1)}, bf16[8,4096]{1,0:T(8,128)(2,1)S(1)}, u32[]{:S(2)}, u32[]{:S(2)}) collective-permute-start(bf16[8,4096]{1,0:T(8,128)(2,1)S(1)} %get-tuple-element.48), channel_id=1, source_target_pairs={{0,1},{1,0},{2,3},{3,2},{4,5},{5,4},{6,7},{7,6},{8,9},{9,8},{10,11... | collective-permute-start | bytes 196616 | tf_op jit(solution)/shard_map/ppermute | solution.py:40
  60.1 2.5 %collective-permute-start.11 = (bf16[8,4096]{1,0:T(8,128)(2,1)S(1)}, bf16[8,4096]{1,0:T(8,128)(2,1)S(1)}, u32[]{:S(2)}, u32[]{:S(2)}) collective-permute-start(bf16[8,4096]{1,0:T(8,128)(2,1)S(1)} %get-tuple-element.50), channel_id=1, source_target_pairs={{0,3},{1,2},{2,1},{3,0},{4,7},{5,6},{6,5},{7,4},{8,11},{9,10},{10,... | collective-permute-start | bytes 196616 | tf_op jit(solution)/shard_map/ppermute | solution.py:40
  62.6 2.0 %collective-permute-start.13 = (bf16[8,4096]{1,0:T(8,128)(2,1)S(1)}, bf16[8,4096]{1,0:T(8,128)(2,1)S(1)}, u32[]{:S(2)}, u32[]{:S(2)}) collective-permute-start(bf16[8,4096]{1,0:T(8,128)(2,1)S(1)} %get-tuple-element.51), channel_id=1, source_target_pairs={{0,1},{1,0},{2,3},{3,2},{4,5},{5,4},{6,7},{7,6},{8,9},{9,8},{10,11... | collective-permute-start | bytes 196616 | tf_op jit(solution)/shard_map/ppermute | solution.py:40
  64.6 1.0 collective-permute-done.8
  65.7 0.7 collective-permute-done.11
  66.4 2.7 %collective-permute-done.12 = bf16[8,4096]{1,0:T(8,128)(2,1)S(1)} collective-permute-done((bf16[8,4096]{1,0:T(8,128)(2,1)S(1)}, bf16[8,4096]{1,0:T(8,128)(2,1)S(1)}, u32[]{:S(2)}, u32[]{:S(2)}) %collective-permute-start.12) | collective-permute-done | bytes 65568 | tf_op jit(solution)/shard_map/ppermute | solution.py:40
  69.8 2.3 %collective-permute-start.15 = (bf16[16,4224]{1,0:T(8,128)(2,1)S(1)}, bf16[16,4224]{1,0:T(8,128)(2,1)S(1)}, u32[]{:S(2)}, u32[]{:S(2)}) collective-permute-start(bf16[16,4224]{1,0:T(8,128)(2,1)S(1)} %get-tuple-element.53), channel_id=1, source_target_pairs={{0,2},{1,3},{2,0},{3,1},{4,6},{5,7},{6,4},{7,5},{8,10},{9,11},{10,... | collective-permute-start | bytes 405512 | tf_op jit(solution)/shard_map/ppermute | solution.py:40
  72.2 2.0 %collective-permute-start.16 = (bf16[16,4224]{1,0:T(8,128)(2,1)S(1)}, bf16[16,4224]{1,0:T(8,128)(2,1)S(1)}, u32[]{:S(2)}, u32[]{:S(2)}) collective-permute-start(bf16[16,4224]{1,0:T(8,128)(2,1)S(1)} %get-tuple-element.53), channel_id=1, source_target_pairs={{0,3},{1,2},{2,1},{3,0},{4,7},{5,6},{6,5},{7,4},{8,11},{9,10},{10,... | collective-permute-start | bytes 405512 | tf_op jit(solution)/shard_map/ppermute | solution.py:40
  74.2 2.1 %collective-permute-done.14 = bf16[16,4224]{1,0:T(8,128)(2,1)S(1)} collective-permute-done((bf16[16,4224]{1,0:T(8,128)(2,1)S(1)}, bf16[16,4224]{1,0:T(8,128)(2,1)S(1)}, u32[]{:S(2)}, u32[]{:S(2)}) %collective-permute-start.14) | collective-permute-done | bytes 135200 | tf_op jit(solution)/shard_map/ppermute | solution.py:40
  76.3 6.6 %collective-permute-done.15 = bf16[16,4224]{1,0:T(8,128)(2,1)S(1)} collective-permute-done((bf16[16,4224]{1,0:T(8,128)(2,1)S(1)}, bf16[16,4224]{1,0:T(8,128)(2,1)S(1)}, u32[]{:S(2)}, u32[]{:S(2)}) %collective-permute-start.15) | collective-permute-done | bytes 135200 | tf_op jit(solution)/shard_map/ppermute | solution.py:40
  83.2 0.6 collective-permute-start.18
  83.7 0.7 collective-permute-start.20
  84.5 0.4 collective-permute-done.17
  84.9 8.0 %fusion.25 = (f32[128]{0:T(128)S(1)}, f32[128,2000]{0,1:T(8,128)S(1)}) fusion(bf16[2000,4096]{1,0:T(8,128)(2,1)} %param.23, bf16[64,4224]{1,0:T(8,128)(2,1)S(1)} %constant_dynamic-update-slice_fusion.7, bf16[64,4224]{1,0:T(8,128)(2,1)S(1)} %collective-permute-done.17), kind=kOutput, calls=%fused_computation.99 | convolution fusion | flops 2099505024 | bytes 18489856 | tf_op jit(solution)/shard_map/dot_general | solution.py:55
  93.2 0.3 exponential_reduce_fusion.3
  93.6 4.6 %collective-permute-done.20 = bf16[64,4224]{1,0:T(8,128)(2,1)} collective-permute-done((bf16[64,4224]{1,0:T(8,128)(2,1)S(1)}, bf16[64,4224]{1,0:T(8,128)(2,1)}, u32[]{:S(2)}, u32[]{:S(2)}) %collective-permute-start.20) | collective-permute-done | bytes 540704 | tf_op jit(solution)/shard_map/ppermute | solution.py:40
  98.2 1.0 slice.107
  99.2 1.6 %collective-permute-start.22 = (bf16[32,4224]{1,0:T(8,128)(2,1)S(1)}, bf16[32,4224]{1,0:T(8,128)(2,1)S(1)}, u32[]{:S(2)}, u32[]{:S(2)}) collective-permute-start(bf16[32,4224]{1,0:T(8,128)(2,1)S(1)} %slice.107), channel_id=1, source_target_pairs={{0,8},{4,12},{8,0},{12,4},{1,9},{5,13},{9,1},{13,5},{2,10},{6,14},... | collective-permute-start | bytes 811016 | tf_op jit(solution)/shard_map/ppermute | solution.py:40
  100.8 1.0 collective-permute-start.23
  102.0 1.1 constant_dynamic-update-slice_fusion.3
  103.1 0.6 collective-permute-start.21
  103.6 3.4 %collective-permute-done.22 = bf16[32,4224]{1,0:T(8,128)(2,1)S(1)} collective-permute-done((bf16[32,4224]{1,0:T(8,128)(2,1)S(1)}, bf16[32,4224]{1,0:T(8,128)(2,1)S(1)}, u32[]{:S(2)}, u32[]{:S(2)}) %collective-permute-start.22) | collective-permute-done | bytes 270368 | tf_op jit(solution)/shard_map/ppermute | solution.py:40
  107.1 1.3 collective-permute-done.23
  108.4 0.8 pad_maximum_fusion
  109.4 10.0 %fusion.24 = (f32[128]{0:T(128)S(1)}, f32[128,2000]{0,1:T(8,128)S(1)}) fusion(bf16[2000,4096]{1,0:T(8,128)(2,1)} %param.23, bf16[128,4224]{1,0:T(8,128)(2,1)S(1)} %constant_dynamic-update-slice_fusion), kind=kOutput, calls=%fused_computation.98 | convolution fusion | flops 2097407872 | bytes 18457088 | tf_op jit(solution)/shard_map/dot_general | solution.py:55
  119.5 4.6 %fusion.23 = (f32[128]{0:T(128)S(1)}, f32[128,2000]{0,1:T(8,128)S(1)}) fusion(bf16[2000,4096]{1,0:T(8,128)(2,1)S(1)} %bitcast.35, bf16[128,4224]{1,0:T(8,128)(2,1)S(1)} %constant_dynamic-update-slice_fusion.2), kind=kOutput, calls=%fused_computation.97 | convolution fusion | flops 2097407872 | bytes 18457088 | tf_op jit(solution)/shard_map/dot_general | solution.py:55
  124.4 0.3 exponential_reduce_fusion.2
  125.0 1.9 %constant_dynamic-update-slice_fusion.4 = bf16[128,4224]{1,0:T(8,128)(2,1)} fusion(bf16[128,4224]{1,0:T(8,128)(2,1)} %copy-done.6, bf16[64,4224]{1,0:T(8,128)(2,1)} %collective-permute-done.24), kind=kLoop, calls=%fused_computation.65 | loop fusion | bytes 1081344 | tf_op jit(solution)/shard_map/concatenate | solution.py:461
  126.9 0.8 slice_convert_fusion
  127.6 8.3 %fusion.22 = (f32[128]{0:T(128)S(1)}, f32[128,2000]{0,1:T(8,128)S(1)}) fusion(bf16[2000,4096]{1,0:T(8,128)(2,1)} %param.23, bf16[128,4224]{1,0:T(8,128)(2,1)} %constant_dynamic-update-slice_fusion.4), kind=kOutput, calls=%fused_computation.96 | convolution fusion | flops 2097407872 | bytes 18457088 | tf_op jit(solution)/shard_map/dot_general | solution.py:55
  136.1 0.3 exponential_reduce_fusion.1
  137.2 0.6 gather_fusion
  137.9 0.6 reshape.137
  138.5 1.2 reshape.151
  139.7 3.8 %all-to-all-start.1 = ((f32[32,1,768]{2,1,0:T(1,128)}), f32[32,1,768]{2,1,0:T(1,128)S(1)}, u32[]{:S(2)}, u32[]{:S(2)}) async-start(f32[32,1,768]{2,1,0:T(1,128)} %reshape.151), calls=%async_computation.1 | async-start | bytes 196608 | tf_op jit(solution)/shard_map/all_to_all | solution.py:30
  143.6 7.9 %all-to-all-done.1 = f32[32,1,768]{2,1,0:T(1,128)S(1)} async-done(((f32[32,1,768]{2,1,0:T(1,128)}), f32[32,1,768]{2,1,0:T(1,128)S(1)}, u32[]{:S(2)}, u32[]{:S(2)}) %all-to-all-start.1) | async-done | bytes 98336 | tf_op jit(solution)/shard_map/all_to_all | solution.py:30
  151.5 0.5 broadcast.106
  152.0 0.9 reduce.48
  152.9 0.5 reshape.152
  153.9 0.6 add_select_fusion
  (119 shorter events, 4.4 us)
Async XLA Ops:
  1.1 1.9 %copy-start.2 = (bf16[1280,1280]{1,0:T(8,128)(2,1)S(1)}, bf16[1280,1280]{1,0:T(8,128)(2,1)}, u32[]{:S(2)}) copy-start(bf16[1280,1280]{1,0:T(8,128)(2,1)} %up_ref.1) | copy-start | bytes 9830404
  3.0 1.9 %copy-start.3 = (bf16[1280,1280]{1,0:T(8,128)(2,1)S(1)}, bf16[1280,1280]{1,0:T(8,128)(2,1)}, u32[]{:S(2)}) copy-start(bf16[1280,1280]{1,0:T(8,128)(2,1)} %down_ref.1) | copy-start | bytes 9830404
  4.9 9.8 %copy-start.9 = (s32[2,8,16]{2,1,0:T(8,128)S(1)}, s32[2,8,16]{2,1,0:T(8,128)}, u32[]{:S(2)}) copy-start(s32[2,8,16]{2,1,0:T(8,128)} %param.19) | copy-start | bytes 3076
  4.9 9.9 %copy-start.7 = (s32[2,8]{1,0:T(2,128)S(1)}, s32[2,8]{1,0:T(2,128)}, u32[]{:S(2)}) copy-start(s32[2,8]{1,0:T(2,128)} %param.20) | copy-start | bytes 196
  4.9 10.0 %copy-start.11 = (s32[8]{0:T(128)S(1)}, s32[8]{0:T(128)}, u32[]{:S(2)}) copy-start(s32[8]{0:T(128)} %param.13) | copy-start | bytes 100
  4.9 11.3 %copy-start.5 = (bf16[2,8,16,4096]{3,2,1,0:T(8,128)(2,1)S(1)}, bf16[2,8,16,4096]{3,2,1,0:T(8,128)(2,1)}, u32[]{:S(2)}) copy-start(bf16[2,8,16,4096]{3,2,1,0:T(8,128)(2,1)} %param.18) | copy-start | bytes 6291460
  9.1 15.4 %collective-permute-start.3 = (bf16[32,1280]{1,0:T(8,128)(2,1)}, bf16[32,1280]{1,0:T(8,128)(2,1)S(1)}, u32[]{:S(2)}, u32[]{:S(2)}) collective-permute-start(bf16[32,1280]{1,0:T(8,128)(2,1)} %get-tuple-element.28), channel_id=1, source_target_pairs={{0,1},{1,0},{2,3},{3,2},{4,5},{5,4},{6,7},{7,6},{8,9},{9,8},{10,11... | collective-permute-start | bytes 245768 | tf_op jit(solution)/shard_map/ppermute | solution.py:40
  12.1 12.5 %collective-permute-start.4 = (bf16[32,1280]{1,0:T(8,128)(2,1)S(1)}, bf16[32,1280]{1,0:T(8,128)(2,1)S(1)}, u32[]{:S(2)}, u32[]{:S(2)}) collective-permute-start(bf16[32,1280]{1,0:T(8,128)(2,1)S(1)} %get-tuple-element.29), channel_id=1, source_target_pairs={{0,2},{1,3},{2,0},{3,1},{4,6},{5,7},{6,4},{7,5},{8,10},{9,11},{10,... | collective-permute-start | bytes 245768 | tf_op jit(solution)/shard_map/ppermute | solution.py:40
  14.7 9.9 %collective-permute-start.5 = (bf16[32,1280]{1,0:T(8,128)(2,1)S(1)}, bf16[32,1280]{1,0:T(8,128)(2,1)S(1)}, u32[]{:S(2)}, u32[]{:S(2)}) collective-permute-start(bf16[32,1280]{1,0:T(8,128)(2,1)S(1)} %get-tuple-element.30), channel_id=1, source_target_pairs={{0,3},{1,2},{2,1},{3,0},{4,7},{5,6},{6,5},{7,4},{8,11},{9,10},{10,... | collective-permute-start | bytes 245768 | tf_op jit(solution)/shard_map/ppermute | solution.py:40
  16.2 2.2 %copy-start = (bf16[4096,512]{1,0:T(8,128)(2,1)S(1)}, bf16[4096,512]{1,0:T(8,128)(2,1)}, u32[]{:S(2)}) copy-start(bf16[4096,512]{1,0:T(8,128)(2,1)} %w_ref.1) | copy-start | bytes 12582916
  18.4 6.2 %copy-start.4 = (bf16[1280,1024]{1,0:T(8,128)(2,1)S(1)}, bf16[1280,1024]{1,0:T(8,128)(2,1)}, u32[]{:S(2)}) copy-start(bf16[1280,1024]{1,0:T(8,128)(2,1)} %refs_5_.2) | copy-start | bytes 7864324
  22.8 14.2 %collective-permute-start = (bf16[272,512]{1,0:T(8,128)(2,1)}, bf16[272,512]{1,0:T(8,128)(2,1)S(1)}, u32[]{:S(2)}, u32[]{:S(2)}) collective-permute-start(bf16[272,512]{1,0:T(8,128)(2,1)} %get-tuple-element.24), channel_id=1, source_target_pairs={{0,4},{4,0},{8,12},{12,8},{1,5},{5,1},{9,13},{13,9},{2,6},{6,2},{1... | collective-permute-start | bytes 835592 | tf_op jit(solution)/shard_map/ppermute | solution.py:40
  22.8 14.2 %collective-permute-start.1 = (bf16[272,512]{1,0:T(8,128)(2,1)S(1)}, bf16[272,512]{1,0:T(8,128)(2,1)S(1)}, u32[]{:S(2)}, u32[]{:S(2)}) collective-permute-start(bf16[272,512]{1,0:T(8,128)(2,1)S(1)} %get-tuple-element.25), channel_id=1, source_target_pairs={{0,8},{4,12},{8,0},{12,4},{1,9},{5,13},{9,1},{13,5},{2,10},{6,14},... | collective-permute-start | bytes 835592 | tf_op jit(solution)/shard_map/ppermute | solution.py:40
  24.5 13.8 %collective-permute-start.2 = (bf16[272,512]{1,0:T(8,128)(2,1)S(1)}, bf16[272,512]{1,0:T(8,128)(2,1)S(1)}, u32[]{:S(2)}, u32[]{:S(2)}) collective-permute-start(bf16[272,512]{1,0:T(8,128)(2,1)S(1)} %get-tuple-element.26), channel_id=1, source_target_pairs={{0,12},{4,8},{8,4},{12,0},{1,13},{5,9},{9,5},{13,1},{2,14},{6,10},... | collective-permute-start | bytes 835592 | tf_op jit(solution)/shard_map/ppermute | solution.py:40
  24.6 7.8 %copy-start.12 = (s32[8]{0:T(128)S(1)}, s32[8]{0:T(128)}, u32[]{:S(2)}) copy-start(s32[8]{0:T(128)} %param.13) | copy-start | bytes 100
  24.7 10.8 %copy-start.13 = (s32[4]{0:T(128)S(1)}, s32[4]{0:T(128)}, u32[]{:S(2)}) copy-start(s32[4]{0:T(128)} %param.12) | copy-start | bytes 52
  26.2 14.5 %all-to-all-start = ((bf16[32,8,256]{2,1,0:T(8,128)(2,1)}), bf16[32,8,256]{2,1,0:T(8,128)(2,1)S(1)}, u32[]{:S(2)}, u32[]{:S(2)}) async-start(bf16[32,8,256]{2,1,0:T(8,128)(2,1)} %bitcast.5), calls=%async_computation | async-start | bytes 262144 | tf_op jit(solution)/shard_map/all_to_all | solution.py:30
  40.7 2.2 %copy-start.1 = (bf16[512,4096]{1,0:T(8,128)(2,1)S(1)}, bf16[512,4096]{1,0:T(8,128)(2,1)}, u32[]{:S(2)}) copy-start(bf16[512,4096]{1,0:T(8,128)(2,1)} %refs_5_.3) | copy-start | bytes 12582916
  46.2 9.3 %collective-permute-start.6 = (bf16[32,4096]{1,0:T(8,128)(2,1)S(1)}, bf16[32,4096]{1,0:T(8,128)(2,1)S(1)}, u32[]{:S(2)}, u32[]{:S(2)}) collective-permute-start(bf16[32,4096]{1,0:T(8,128)(2,1)S(1)} %get-tuple-element.34), channel_id=1, source_target_pairs={{0,16},{16,0},{1,17},{17,1},{2,18},{18,2},{3,19},{19,3},{4,20},{20... | collective-permute-start | bytes 786440 | tf_op jit(solution)/shard_map/ppermute | solution.py:40
  47.0 13.0 %collective-permute-start.10 = (bf16[32,4096]{1,0:T(8,128)(2,1)S(1)}, bf16[32,4096]{1,0:T(8,128)(2,1)S(1)}, u32[]{:S(2)}, u32[]{:S(2)}) collective-permute-start(bf16[32,4096]{1,0:T(8,128)(2,1)S(1)} %get-tuple-element.36), channel_id=1, source_target_pairs={{0,16},{16,0},{1,17},{17,1},{2,18},{18,2},{3,19},{19,3},{4,20},{20... | collective-permute-start | bytes 786440 | tf_op jit(solution)/shard_map/ppermute | solution.py:40
  55.6 7.1 %collective-permute-start.7 = (bf16[8,4096]{1,0:T(8,128)(2,1)S(1)}, bf16[8,4096]{1,0:T(8,128)(2,1)S(1)}, u32[]{:S(2)}, u32[]{:S(2)}) collective-permute-start(bf16[8,4096]{1,0:T(8,128)(2,1)S(1)} %get-tuple-element.47), channel_id=1, source_target_pairs={{0,3},{1,2},{2,1},{3,0},{4,7},{5,6},{6,5},{7,4},{8,11},{9,10},{10,... | collective-permute-start | bytes 196616 | tf_op jit(solution)/shard_map/ppermute | solution.py:40
  57.9 7.8 %collective-permute-start.8 = (bf16[8,4096]{1,0:T(8,128)(2,1)S(1)}, bf16[8,4096]{1,0:T(8,128)(2,1)S(1)}, u32[]{:S(2)}, u32[]{:S(2)}) collective-permute-start(bf16[8,4096]{1,0:T(8,128)(2,1)S(1)} %get-tuple-element.49), channel_id=1, source_target_pairs={{0,2},{1,3},{2,0},{3,1},{4,6},{5,7},{6,4},{7,5},{8,10},{9,11},{10,... | collective-permute-start | bytes 196616 | tf_op jit(solution)/shard_map/ppermute | solution.py:40
  57.9 7.8 %collective-permute-start.9 = (bf16[8,4096]{1,0:T(8,128)(2,1)S(1)}, bf16[8,4096]{1,0:T(8,128)(2,1)S(1)}, u32[]{:S(2)}, u32[]{:S(2)}) collective-permute-start(bf16[8,4096]{1,0:T(8,128)(2,1)S(1)} %get-tuple-element.48), channel_id=1, source_target_pairs={{0,1},{1,0},{2,3},{3,2},{4,5},{5,4},{6,7},{7,6},{8,9},{9,8},{10,11... | collective-permute-start | bytes 196616 | tf_op jit(solution)/shard_map/ppermute | solution.py:40
  60.1 6.2 %collective-permute-start.11 = (bf16[8,4096]{1,0:T(8,128)(2,1)S(1)}, bf16[8,4096]{1,0:T(8,128)(2,1)S(1)}, u32[]{:S(2)}, u32[]{:S(2)}) collective-permute-start(bf16[8,4096]{1,0:T(8,128)(2,1)S(1)} %get-tuple-element.50), channel_id=1, source_target_pairs={{0,3},{1,2},{2,1},{3,0},{4,7},{5,6},{6,5},{7,4},{8,11},{9,10},{10,... | collective-permute-start | bytes 196616 | tf_op jit(solution)/shard_map/ppermute | solution.py:40
  62.6 6.5 %collective-permute-start.12 = (bf16[8,4096]{1,0:T(8,128)(2,1)S(1)}, bf16[8,4096]{1,0:T(8,128)(2,1)S(1)}, u32[]{:S(2)}, u32[]{:S(2)}) collective-permute-start(bf16[8,4096]{1,0:T(8,128)(2,1)S(1)} %get-tuple-element.52), channel_id=1, source_target_pairs={{0,2},{1,3},{2,0},{3,1},{4,6},{5,7},{6,4},{7,5},{8,10},{9,11},{10,... | collective-permute-start | bytes 196616 | tf_op jit(solution)/shard_map/ppermute | solution.py:40
  62.6 6.5 %collective-permute-start.13 = (bf16[8,4096]{1,0:T(8,128)(2,1)S(1)}, bf16[8,4096]{1,0:T(8,128)(2,1)S(1)}, u32[]{:S(2)}, u32[]{:S(2)}) collective-permute-start(bf16[8,4096]{1,0:T(8,128)(2,1)S(1)} %get-tuple-element.51), channel_id=1, source_target_pairs={{0,1},{1,0},{2,3},{3,2},{4,5},{5,4},{6,7},{7,6},{8,9},{9,8},{10,11... | collective-permute-start | bytes 196616 | tf_op jit(solution)/shard_map/ppermute | solution.py:40
  65.7 4.0 %copy-start.8 = (s32[2,8]{1,0:T(2,128)S(1)}, s32[2,8]{1,0:T(2,128)}, u32[]{:S(2)}) copy-start(s32[2,8]{1,0:T(2,128)} %param.20) | copy-start | bytes 196
  69.5 6.7 %collective-permute-start.14 = (bf16[16,4224]{1,0:T(8,128)(2,1)S(1)}, bf16[16,4224]{1,0:T(8,128)(2,1)S(1)}, u32[]{:S(2)}, u32[]{:S(2)}) collective-permute-start(bf16[16,4224]{1,0:T(8,128)(2,1)S(1)} %get-tuple-element.53), channel_id=1, source_target_pairs={{0,1},{1,0},{2,3},{3,2},{4,5},{5,4},{6,7},{7,6},{8,9},{9,8},{10,11... | collective-permute-start | bytes 405512 | tf_op jit(solution)/shard_map/ppermute | solution.py:40
  69.8 13.0 %collective-permute-start.15 = (bf16[16,4224]{1,0:T(8,128)(2,1)S(1)}, bf16[16,4224]{1,0:T(8,128)(2,1)S(1)}, u32[]{:S(2)}, u32[]{:S(2)}) collective-permute-start(bf16[16,4224]{1,0:T(8,128)(2,1)S(1)} %get-tuple-element.53), channel_id=1, source_target_pairs={{0,2},{1,3},{2,0},{3,1},{4,6},{5,7},{6,4},{7,5},{8,10},{9,11},{10,... | collective-permute-start | bytes 405512 | tf_op jit(solution)/shard_map/ppermute | solution.py:40
  72.2 10.7 %collective-permute-start.16 = (bf16[16,4224]{1,0:T(8,128)(2,1)S(1)}, bf16[16,4224]{1,0:T(8,128)(2,1)S(1)}, u32[]{:S(2)}, u32[]{:S(2)}) collective-permute-start(bf16[16,4224]{1,0:T(8,128)(2,1)S(1)} %get-tuple-element.53), channel_id=1, source_target_pairs={{0,3},{1,2},{2,1},{3,0},{4,7},{5,6},{6,5},{7,4},{8,11},{9,10},{10,... | collective-permute-start | bytes 405512 | tf_op jit(solution)/shard_map/ppermute | solution.py:40
  82.9 2.0 %collective-permute-start.17 = (bf16[64,4224]{1,0:T(8,128)(2,1)S(1)}, bf16[64,4224]{1,0:T(8,128)(2,1)S(1)}, u32[]{:S(2)}, u32[]{:S(2)}) collective-permute-start(bf16[64,4224]{1,0:T(8,128)(2,1)S(1)} %constant_dynamic-update-slice_fusion.7), channel_id=1, source_target_pairs={{0,4},{4,0},{8,12},{12,8},{1,5},{5,1},{9,13},{13,9},{2,6},{6,2},{1... | collective-permute-start | bytes 1622024 | tf_op jit(solution)/shard_map/ppermute | solution.py:40
  83.2 17.6 %collective-permute-start.18 = (bf16[64,4224]{1,0:T(8,128)(2,1)S(1)}, bf16[64,4224]{1,0:T(8,128)(2,1)S(1)}, u32[]{:S(2)}, u32[]{:S(2)}) collective-permute-start(bf16[64,4224]{1,0:T(8,128)(2,1)S(1)} %constant_dynamic-update-slice_fusion.7), channel_id=1, source_target_pairs={{0,8},{4,12},{8,0},{12,4},{1,9},{5,13},{9,1},{13,5},{2,10},{6,14},... | collective-permute-start | bytes 1622024 | tf_op jit(solution)/shard_map/ppermute | solution.py:40
  83.7 14.5 %collective-permute-start.20 = (bf16[64,4224]{1,0:T(8,128)(2,1)S(1)}, bf16[64,4224]{1,0:T(8,128)(2,1)}, u32[]{:S(2)}, u32[]{:S(2)}) collective-permute-start(bf16[64,4224]{1,0:T(8,128)(2,1)S(1)} %constant_dynamic-update-slice_fusion.7), channel_id=1, source_target_pairs={{0,16},{16,0},{1,17},{17,1},{2,18},{18,2},{3,19},{19,3},{4,20},{20... | collective-permute-start | bytes 1622024 | tf_op jit(solution)/shard_map/ppermute | solution.py:40
  99.2 7.8 %collective-permute-start.22 = (bf16[32,4224]{1,0:T(8,128)(2,1)S(1)}, bf16[32,4224]{1,0:T(8,128)(2,1)S(1)}, u32[]{:S(2)}, u32[]{:S(2)}) collective-permute-start(bf16[32,4224]{1,0:T(8,128)(2,1)S(1)} %slice.107), channel_id=1, source_target_pairs={{0,8},{4,12},{8,0},{12,4},{1,9},{5,13},{9,1},{13,5},{2,10},{6,14},... | collective-permute-start | bytes 811016 | tf_op jit(solution)/shard_map/ppermute | solution.py:40
  100.8 7.6 %collective-permute-start.23 = (bf16[32,4224]{1,0:T(8,128)(2,1)S(1)}, bf16[32,4224]{1,0:T(8,128)(2,1)S(1)}, u32[]{:S(2)}, u32[]{:S(2)}) collective-permute-start(bf16[32,4224]{1,0:T(8,128)(2,1)S(1)} %slice.108), channel_id=1, source_target_pairs={{0,16},{16,0},{1,17},{17,1},{2,18},{18,2},{3,19},{19,3},{4,20},{20... | collective-permute-start | bytes 811016 | tf_op jit(solution)/shard_map/ppermute | solution.py:40
  101.9 7.4 %collective-permute-start.19 = (bf16[64,4224]{1,0:T(8,128)(2,1)S(1)}, bf16[64,4224]{1,0:T(8,128)(2,1)S(1)}, u32[]{:S(2)}, u32[]{:S(2)}) collective-permute-start(bf16[64,4224]{1,0:T(8,128)(2,1)S(1)} %collective-permute-done.18), channel_id=1, source_target_pairs={{0,4},{4,0},{8,12},{12,8},{1,5},{5,1},{9,13},{13,9},{2,6},{6,2},{1... | collective-permute-start | bytes 1622024 | tf_op jit(solution)/shard_map/ppermute | solution.py:40
  103.1 16.3 %collective-permute-start.21 = (bf16[64,4224]{1,0:T(8,128)(2,1)}, bf16[64,4224]{1,0:T(8,128)(2,1)S(1)}, u32[]{:S(2)}, u32[]{:S(2)}) collective-permute-start(bf16[64,4224]{1,0:T(8,128)(2,1)} %collective-permute-done.20), channel_id=1, source_target_pairs={{0,4},{4,0},{8,12},{12,8},{1,5},{5,1},{9,13},{13,9},{2,6},{6,2},{1... | collective-permute-start | bytes 1622024 | tf_op jit(solution)/shard_map/ppermute | solution.py:40
  108.4 11.1 %slice-start = ((s8[16384000]{0:T(1024)(128)(4,1)}), s8[4194304]{0:T(1024)(128)(4,1)S(1)}, s32[]{:S(2)}) async-start(s8[16384000]{0:T(1024)(128)(4,1)} %bitcast.34), calls=%async_computation.2 | async-start | bytes 8388608
  109.2 15.7 %collective-permute-start.24 = (bf16[64,4224]{1,0:T(8,128)(2,1)}, bf16[64,4224]{1,0:T(8,128)(2,1)}, u32[]{:S(2)}, u32[]{:S(2)}) collective-permute-start(bf16[64,4224]{1,0:T(8,128)(2,1)} %pad_maximum_fusion), channel_id=1, source_target_pairs={{0,4},{4,0},{8,12},{12,8},{1,5},{5,1},{9,13},{13,9},{2,6},{6,2},{1... | collective-permute-start | bytes 1622024 | tf_op jit(solution)/shard_map/ppermute | solution.py:40
  109.3 10.1 %copy-start.6 = (bf16[128,4224]{1,0:T(8,128)(2,1)}, bf16[128,4224]{1,0:T(8,128)(2,1)S(1)}, u32[]{:S(2)}) copy-start(bf16[128,4224]{1,0:T(8,128)(2,1)S(1)} %constant_dynamic-update-slice_fusion.5) | copy-start | bytes 3244036
  109.4 10.1 %slice-start.1 = ((s8[16384000]{0:T(1024)(128)(4,1)}), s8[4194304]{0:T(1024)(128)(4,1)S(1)}, s32[]{:S(2)}) async-start(s8[16384000]{0:T(1024)(128)(4,1)} %bitcast.34), calls=%async_computation.3 | async-start | bytes 8388608
  109.4 10.1 %slice-start.2 = ((s8[16384000]{0:T(1024)(128)(4,1)}), s8[4194304]{0:T(1024)(128)(4,1)S(1)}, s32[]{:S(2)}) async-start(s8[16384000]{0:T(1024)(128)(4,1)} %bitcast.34), calls=%async_computation.4 | async-start | bytes 8388608
  109.4 10.1 %slice-start.3 = ((s8[16384000]{0:T(1024)(128)(4,1)}), s8[3801088]{0:T(1024)(128)(4,1)S(1)}, s32[]{:S(2)}) async-start(s8[16384000]{0:T(1024)(128)(4,1)} %bitcast.34), calls=%async_computation.5 | async-start | bytes 7602176
  139.7 11.8 %all-to-all-start.1 = ((f32[32,1,768]{2,1,0:T(1,128)}), f32[32,1,768]{2,1,0:T(1,128)S(1)}, u32[]{:S(2)}, u32[]{:S(2)}) async-start(f32[32,1,768]{2,1,0:T(1,128)} %reshape.151), calls=%async_computation.1 | async-start | bytes 196608 | tf_op jit(solution)/shard_map/all_to_all | solution.py:30
  152.0 1.9 %copy-start.10 = (pred[2]{0:T(512)(128)(4,1)S(1)}, pred[2]{0:T(512)(128)(4,1)}, u32[]{:S(2)}) copy-start(pred[2]{0:T(512)(128)(4,1)} %get-tuple-element.45) | copy-start | bytes 10

commit v4 on v1

--- a/solution.py
+++ b/solution.py
@@ -1,8 +1,11 @@
+import functools
 import math
 
 import jax
 import jax.numpy as jnp
 from jax import lax
+from jax.experimental import pallas as pl
+from jax.experimental.pallas import tpu as pltpu
 from jax.sharding import PartitionSpec as P
 
 NH = 32
@@ -10,6 +13,7 @@
 HD = 128
 V = 64000
 ALL = ("section", "tm", "mp")
+LANES = 128
 
 
 def layer_norm(values):
@@ -31,7 +35,638 @@
     return jnp.sum(exchange(blocks, axis).astype(jnp.float32), axis=0)
 
 
-def per_device(
+def swap(values, axis, distance):
+    pairs = [(i, i ^ distance) for i in range(lax.axis_size(axis))]
+    return lax.ppermute(values, axis, pairs)
+
+
+def whole(shape):
+    return pl.BlockSpec(shape, lambda *_: (0,) * len(shape))
+
+
+SCALARS = pl.BlockSpec(memory_space=pltpu.SMEM)
+
+
+def dot(left, right):
+    return jnp.dot(left, right, preferred_element_type=jnp.float32)
+
+
+def dot_nt(left, right):
+    return lax.dot_general(
+        left, right, (((1,), (1,)), ((), ())), preferred_element_type=jnp.float32
+    )
+
+
+def start_copies(source_of, target_of, semaphores, count):
+    copies = []
+    for number in range(count):
+        copy = pltpu.make_async_copy(
+            source_of(number), target_of(number), semaphores.at[number]
+        )
+        copy.start()
+        copies.append(copy)
+    return copies
+
+
+def ffn_kernel(count, tile, place_ref, x_ref, up_ref, down_ref, *refs):
+    outs, (own_ref, total, up, down, up_sem, down_sem) = refs[:count], refs[count:]
+    share = own_ref.shape[0]
+    tiles = up_ref.shape[1] // tile
+    up_copies = start_copies(
+        lambda i: up_ref.at[:, pl.ds(i * tile, tile)], lambda i: up.at[i], up_sem, tiles
+    )
+    down_copies = start_copies(
+        lambda i: down_ref.at[pl.ds(i * tile, tile), :], lambda i: down.at[i], down_sem, tiles
+    )
+    here = place_ref[2]
+    own_ref[...] = x_ref[pl.ds(pl.multiple_of(here * share, share), share), :]
+    normed = layer_norm(x_ref[...].astype(jnp.float32)).astype(jnp.bfloat16)
+    for number in range(tiles):
+        up_copies[number].wait()
+        hidden = dot(normed, up[number])
+        inner = 0.5 * hidden * (1.0 + lax.erf(hidden * math.sqrt(0.5)))
+        down_copies[number].wait()
+        product = dot(inner.astype(jnp.bfloat16), down[number])
+        if number == 0:
+            total[...] = product
+        else:
+            total[...] += product
+    for distance in range(count):
+        start = pl.multiple_of((here ^ distance) * share, share)
+        outs[distance][...] = total[pl.ds(start, share), :].astype(jnp.bfloat16)
+
+
+def in_hbm(values):
+    return pltpu.with_memory_space_constraint(values, pltpu.HBM)
+
+
+ANYWHERE = pl.BlockSpec(memory_space=pl.ANY)
+INSIDE = pl.BlockSpec(memory_space=pltpu.VMEM)
+
+
+def ffn(place, rows, up, down, count):
+    share = rows.shape[0] // count
+    width = rows.shape[1]
+    tile = 256
+    tiles = up.shape[1] // tile
+    block = jax.ShapeDtypeStruct((share, width), jnp.bfloat16)
+    return pl.pallas_call(
+        functools.partial(ffn_kernel, count, tile),
+        in_specs=[SCALARS, INSIDE, ANYWHERE, ANYWHERE],
+        out_specs=[INSIDE] * (count + 1),
+        out_shape=[block] * (count + 1),
+        scratch_shapes=[
+            pltpu.VMEM(rows.shape, jnp.float32),
+            pltpu.VMEM((tiles, width, tile), jnp.bfloat16),
+            pltpu.VMEM((tiles, tile, width), jnp.bfloat16),
+            pltpu.SemaphoreType.DMA((tiles,)),
+            pltpu.SemaphoreType.DMA((tiles,)),
+        ],
+        cost_estimate=pl.CostEstimate(
+            flops=4 * rows.shape[0] * width * up.shape[1],
+            bytes_accessed=4 * width * up.shape[1],
+            transcendentals=rows.shape[0] * up.shape[1],
+        ),
+        compiler_params=pltpu.CompilerParams(vmem_limit_bytes=24 << 20),
+        name="encoder_ffn",
+    )(place, rows, in_hbm(up), in_hbm(down))
+
+
+def query_kernel(count, depth, place_ref, slot_ref, length_ref, x_ref, tok_ref, w_ref, *refs):
+    outs, shares_out = refs[:count], refs[count : 2 * count]
+    states, weights, normed, total, shares, x_sem, w_sem = refs[2 * count :]
+    slots, tokens, width = x_ref.shape
+    hyps = length_ref.shape[0] // slots
+    positions = tokens // hyps
+    columns = w_ref.shape[1]
+    share = shares.shape[1] // 2
+    parts = width // columns
+    x_copies = start_copies(lambda i: x_ref.at[i], lambda i: states.at[i], x_sem, slots)
+    w_copies = start_copies(
+        lambda i: w_ref.at[pl.ds(i * depth, depth), :],
+        lambda i: weights.at[i],
+        w_sem,
+        width // depth,
+    )
+    head_pos = place_ref[4]
+    lane = lax.broadcasted_iota(jnp.int32, (1, tokens), 1)
+    for slot in range(slots):
+        order = jnp.full((1, tokens), -1, jnp.int32)
+        start = jnp.int32(0)
+        for hyp in range(hyps):
+            length = length_ref[slot * hyps + hyp]
+            inside = (lane >= hyp * positions) & (lane < hyp * positions + length)
+            order = jnp.where(inside, lane - hyp * positions + start, order)
+            start = start + length
+        row = lax.broadcasted_iota(jnp.int32, (tokens, tokens), 0)
+        move = jnp.where(order == row, 1.0, 0.0).astype(jnp.bfloat16)
+        x_copies[slot].wait()
+        ordered = dot(move, states[slot])
+        normed[slot * tokens : (slot + 1) * tokens, :] = square_norm(ordered).astype(jnp.bfloat16)
+        share_row = lax.broadcasted_iota(jnp.int32, (share, tokens), 0)
+        chosen = order == share_row * (tokens // share) + head_pos
+        mine = dot(jnp.where(chosen, 1.0, 0.0).astype(jnp.bfloat16), states[slot])
+        shares[slot, :share, :] = mine.astype(jnp.bfloat16)
+        target = jnp.sum(
+            jnp.where(chosen, tok_ref[slot], 0), axis=1, keepdims=True, dtype=jnp.int32
+        )
+        coarse = target // 256
+        cell = lax.broadcasted_iota(jnp.int32, (share, columns), 1)
+        packed = jnp.where(cell == 0, coarse, jnp.where(cell == 1, target - coarse * 256, 0))
+        shares[slot, share:, :columns] = packed.astype(jnp.float32).astype(jnp.bfloat16)
+    for number in range(width // depth):
+        w_copies[number].wait()
+        product = dot(normed[:, number * depth : (number + 1) * depth], weights[number])
+        if number == 0:
+            total[...] = product
+        else:
+            total[...] += product
+    group = place_ref[1]
+    for distance in range(count):
+        slot = jnp.int32(0)
+        for candidate in range(1, slots):
+            holds = slot_ref[group * slots + candidate] == group ^ distance
+            slot = jnp.where(holds, candidate, slot)
+        start = pl.multiple_of(slot * tokens, tokens)
+        outs[distance][...] = total[pl.ds(start, tokens), :].astype(jnp.bfloat16)
+        out = shares_out[distance]
+        for part in range(parts):
+            out[part * share : (part + 1) * share, :] = shares[
+                slot, :share, part * columns : (part + 1) * columns
+            ]
+        out[parts * share :, :] = shares[slot, share:, :columns]
+
+
+def queries_of(place, slot_utt, lengths, states, targets, weights, count, share):
+    slots, tokens, width = states.shape
+    columns = weights.shape[1]
+    depth = 1024
+    block = jax.ShapeDtypeStruct((tokens, columns), jnp.bfloat16)
+    rows = jax.ShapeDtypeStruct(((width // columns + 1) * share, columns), jnp.bfloat16)
+    return pl.pallas_call(
+        functools.partial(query_kernel, count, depth),
+        in_specs=[SCALARS] * 3 + [ANYWHERE, INSIDE, ANYWHERE],
+        out_specs=[INSIDE] * (2 * count),
+        out_shape=[block] * count + [rows] * count,
+        scratch_shapes=[
+            pltpu.VMEM(states.shape, jnp.bfloat16),
+            pltpu.VMEM((width // depth, depth, columns), jnp.bfloat16),
+            pltpu.VMEM((slots * tokens, width), jnp.bfloat16),
+            pltpu.VMEM((slots * tokens, columns), jnp.float32),
+            pltpu.VMEM((slots, 2 * share, width), jnp.bfloat16),
+            pltpu.SemaphoreType.DMA((slots,)),
+            pltpu.SemaphoreType.DMA((width // depth,)),
+        ],
+        cost_estimate=pl.CostEstimate(
+            flops=2 * slots * tokens * width * columns,
+            bytes_accessed=2 * width * (columns + slots * tokens),
+            transcendentals=0,
+        ),
+        compiler_params=pltpu.CompilerParams(vmem_limit_bytes=32 << 20),
+        name="hypothesis_queries",
+    )(place, slot_utt, lengths, in_hbm(states), targets, in_hbm(weights))
+
+
+def kv_kernel(sections, utterances, widths, *refs):
+    parts, own_ref, w_ref, out_ref = refs[:-3], refs[-3], refs[-2], refs[-1]
+    rows = own_ref.shape[0]
+    frames = rows // utterances
+    total = own_ref[...].astype(jnp.float32)
+    summed = parts[0][...].astype(jnp.float32)
+    for part in parts[1:]:
+        summed += part[...].astype(jnp.float32)
+    states = layer_norm(total + summed).astype(jnp.bfloat16)
+    to = lax.broadcasted_iota(jnp.int32, (rows, rows), 0)
+    come = lax.broadcasted_iota(jnp.int32, (rows, rows), 1)
+    move = jnp.where(come == to % frames * utterances + to // frames, 1.0, 0.0)
+    states = dot(move.astype(jnp.bfloat16), states).astype(jnp.bfloat16)
+    both = dot(states, w_ref[...])
+    half = KVH * HD
+    per_kv = sections * widths // KVH
+    for section in range(sections):
+        for utterance in range(utterances):
+            for width in range(0, widths, per_kv):
+                kv_head = (section * widths + width) // per_kv
+                take = slice(utterance * frames, (utterance + 1) * frames)
+                block = jnp.concatenate(
+                    [
+                        both[take, kv_head * HD : (kv_head + 1) * HD],
+                        both[take, half + kv_head * HD : half + (kv_head + 1) * HD],
+                    ],
+                    axis=1,
+                )
+                start = ((section * utterances + utterance) * widths + width) * frames
+                block = jnp.concatenate([block] * per_kv, axis=0).astype(jnp.bfloat16)
+                out_ref[start : start + per_kv * frames, :] = block
+
+
+def keys_values_of(parts, own, weights, sections, utterances, widths):
+    rows = sections * widths * own.shape[0]
+    return pl.pallas_call(
+        functools.partial(kv_kernel, sections, utterances, widths),
+        out_shape=jax.ShapeDtypeStruct((rows, 2 * HD), jnp.bfloat16),
+        cost_estimate=pl.CostEstimate(
+            flops=2 * own.shape[0] * weights.shape[0] * weights.shape[1],
+            bytes_accessed=2 * weights.shape[0] * weights.shape[1],
+            transcendentals=0,
+        ),
+        compiler_params=pltpu.CompilerParams(vmem_limit_bytes=24 << 20),
+        name="frame_keys_values",
+    )(*parts, own, weights)
+
+
+def distance_of_slot(place_ref, slot_ref, slots):
+    group = place_ref[1]
+    source = jnp.int32(0)
+    for slot in range(slot_ref.shape[0]):
+        source = jnp.where(slot_ref[slot] == group, slot // slots, source)
+    return source ^ group
+
+
+def attention_kernel(count, capacity, pieces, sections, widths, tile, *refs):
+    place_ref, slot_ref, frame_ref = refs[:3]
+    payloads, (kv_ref, w_ref) = refs[3 : 3 + count], refs[3 + count : 5 + count]
+    outs = refs[5 + count : 5 + count + 2 * len(pieces)]
+    weights, picked, context, w_sem = refs[5 + count + 2 * len(pieces) :]
+    tokens, columns = capacity, w_ref.shape[0]
+    tiles = w_ref.shape[1] // tile
+    w_copies = start_copies(
+        lambda i: w_ref.at[:, pl.ds(i * tile, tile)], lambda i: weights.at[i], w_sem, tiles
+    )
+    source = distance_of_slot(place_ref, slot_ref, slot_ref.shape[0] // count)
+    section_pos = place_ref[0]
+    frame_limit = frame_ref[place_ref[1]]
+    for distance in range(count):
+
+        @pl.when(source == distance)
+        def _(payload=payloads[distance]):
+            picked[...] = payload[:tokens, :]
+
+    keys = kv_ref[:, :HD]
+    values = kv_ref[:, HD:]
+    frames = kv_ref.shape[0]
+    visible = lax.broadcasted_iota(jnp.int32, (tokens, frames), 1) < frame_limit
+    for head in range(columns // HD):
+        scores = dot_nt(picked[:, head * HD : (head + 1) * HD], keys) * (1.0 / math.sqrt(HD))
+        scores = jnp.where(visible, scores, -jnp.inf)
+        raised = jnp.exp(scores - jnp.max(scores, axis=1, keepdims=True))
+        chances = (raised / jnp.sum(raised, axis=1, keepdims=True)).astype(jnp.bfloat16)
+        context[:, head * HD : (head + 1) * HD] = dot(chances, values).astype(jnp.bfloat16)
+    to = lax.broadcasted_iota(jnp.int32, (tokens, tokens), 0)
+    come = lax.broadcasted_iota(jnp.int32, (tokens, tokens), 1)
+    half = tokens // sections
+    section = jnp.where(to < half, 1 - section_pos, section_pos)
+    inside = to % half
+    row = jnp.zeros_like(to)
+    width = jnp.zeros_like(to)
+    first = 0
+    for piece in pieces:
+        at = inside - first * widths
+        here = (at >= 0) & (at < piece * widths)
+        row = jnp.where(here, first + at % piece, row)
+        width = jnp.where(here, at // piece, width)
+        first += piece
+    move = come == (row * sections + section) * widths + width
+    ordered = dot(jnp.where(move, 1.0, 0.0).astype(jnp.bfloat16), context[...])
+    ordered = ordered.astype(jnp.bfloat16)
+    for number in range(tiles):
+        w_copies[number].wait()
+        product = dot(ordered, weights[number]).astype(jnp.bfloat16)
+        first = 0
+        for out in outs:
+            out[:, number * tile : (number + 1) * tile] = product[first : first + out.shape[0], :]
+            first += out.shape[0]
+
+
+def attend(place, slot_utt, frame_len, payloads, keys_values, weights, pieces, sections, widths):
+    count = len(payloads)
+    columns, width = weights.shape
+    capacity = sum(pieces) * sections * widths
+    tile = 1024
+    tiles = width // tile
+    shapes = [jax.ShapeDtypeStruct((piece * widths, width), jnp.bfloat16) for piece in pieces]
+    shapes = shapes + shapes
+    return pl.pallas_call(
+        functools.partial(attention_kernel, count, capacity, pieces, sections, widths, tile),
+        in_specs=[SCALARS] * 3 + [INSIDE] * (count + 1) + [ANYWHERE],
+        out_specs=[INSIDE] * len(shapes),
+        out_shape=shapes,
+        scratch_shapes=[
+            pltpu.VMEM((tiles, columns, tile), jnp.bfloat16),
+            pltpu.VMEM((capacity, columns), jnp.bfloat16),
+            pltpu.VMEM((capacity, columns), jnp.bfloat16),
+            pltpu.SemaphoreType.DMA((tiles,)),
+        ],
+        cost_estimate=pl.CostEstimate(
+            flops=2 * capacity * columns * (width + 2 * keys_values.shape[0]),
+            bytes_accessed=2 * columns * width + 2 * capacity * width,
+            transcendentals=capacity * keys_values.shape[0] * columns // HD,
+        ),
+        compiler_params=pltpu.CompilerParams(vmem_limit_bytes=24 << 20),
+        name="attention_projection",
+    )(place, slot_utt, frame_len, *payloads, keys_values, in_hbm(weights))
+
+
+def norm_kernel(count, pieces, widths, place_ref, slot_ref, *refs):
+    payloads, blocks = refs[:count], refs[count : count + len(pieces) * widths]
+    out_ref, picked, total = refs[count + len(pieces) * widths :]
+    rows, width = total.shape
+    columns = picked.shape[1]
+    share = picked.shape[0] // (width // columns + 1)
+    source = distance_of_slot(place_ref, slot_ref, slot_ref.shape[0] // count)
+    for distance in range(count):
+
+        @pl.when(source == distance)
+        def _(payload=payloads[distance]):
+            picked[...] = payload[...]
+
+    first = 0
+    for number, piece in enumerate(pieces):
+        mine = blocks[number * widths : (number + 1) * widths]
+        summed = mine[0][...].astype(jnp.float32)
+        for block in mine[1:]:
+            summed += block[...].astype(jnp.float32)
+        total[first : first + piece, :] = summed
+        first += piece
+    for part in range(width // columns):
+        take = slice(part * columns, (part + 1) * columns)
+        total[:, take] += picked[part * share : part * share + rows, :].astype(jnp.float32)
+    out_ref[:, :width] = square_norm(total[...]).astype(jnp.bfloat16)
+    last = width // columns * share
+    out_ref[:, width:] = picked[last : last + rows, :LANES]
+
+
+def normed_rows(place, slot_utt, payloads, blocks, pieces, widths):
+    width = blocks[0].shape[1]
+    rows = sum(pieces)
+    return pl.pallas_call(
+        functools.partial(norm_kernel, len(payloads), pieces, widths),
+        in_specs=[SCALARS] * 2 + [INSIDE] * (len(payloads) + len(blocks)),
+        out_specs=INSIDE,
+        out_shape=jax.ShapeDtypeStruct((rows, width + LANES), jnp.bfloat16),
+        scratch_shapes=[
+            pltpu.VMEM(payloads[0].shape, jnp.bfloat16),
+            pltpu.VMEM((rows, width), jnp.float32),
+        ],
+        compiler_params=pltpu.CompilerParams(vmem_limit_bytes=16 << 20),
+        name="token_rows",
+    )(place, slot_utt, *payloads, *blocks)
+
+
+def vocabulary_kernel(tile, first_ref, *refs):
+    sets, (head_ref, out_ref, rows_ref, stat) = refs[:-4], refs[-4:]
+    vocab_rows, width = head_ref.shape
+    share = sets[0].shape[0]
+    tokens = share * len(sets)
+    cell = lax.broadcasted_iota(jnp.int32, (8, LANES), 1)
+    take = jnp.where(cell == 0, 256.0, jnp.where(cell == 1, 1.0, 0.0)).astype(jnp.bfloat16)
+    for number, rows in enumerate(sets):
+        rows_ref[number * share : (number + 1) * share, :] = rows[...]
+    target = dot_nt(take, rows_ref[:, width:])[0:1, :].astype(jnp.int32) - first_ref[3]
+    stat[0:1, :] = jnp.full((1, tokens), -jnp.inf, jnp.float32)
+    stat[8:9, :] = jnp.zeros((1, tokens), jnp.float32)
+    stat[16:17, :] = jnp.zeros((1, tokens), jnp.float32)
+
+    @pl.loop(0, vocab_rows // tile)
+    def _(step):
+        start = pl.multiple_of(step * tile, tile)
+        logits = dot_nt(head_ref[pl.ds(start, tile), :], rows_ref[:, :width])
+        vocab = lax.broadcasted_iota(jnp.int32, logits.shape, 0) + start
+        before = stat[0:1, :]
+        upper = jnp.maximum(before, jnp.max(logits, axis=0, keepdims=True))
+        stat[8:9, :] = stat[8:9, :] * jnp.exp(before - upper) + jnp.sum(
+            jnp.exp(logits - upper), axis=0, keepdims=True
+        )
+        stat[16:17, :] += jnp.sum(jnp.where(vocab == target, logits, 0.0), axis=0, keepdims=True)
+        stat[0:1, :] = upper
+
+    for number in range(len(sets)):
+        for row in range(3):
+            out_ref[number, row : row + 1, :] = stat[
+                8 * row : 8 * row + 1, number * share : (number + 1) * share
+            ]
+
+
+def vocabulary_stats(place, sets, head):
+    share = sets[0].shape[0]
+    count = len(sets)
+    width = head.shape[1]
+    tokens = share * count
+    return pl.pallas_call(
+        functools.partial(vocabulary_kernel, head.shape[0] // 2),
+        in_specs=[SCALARS] + [INSIDE] * (count + 1),
+        out_specs=INSIDE,
+        out_shape=jax.ShapeDtypeStruct((count, 8, share), jnp.float32),
+        scratch_shapes=[
+            pltpu.VMEM((tokens, width + LANES), jnp.bfloat16),
+            pltpu.VMEM((24, tokens), jnp.float32),
+        ],
+        cost_estimate=pl.CostEstimate(
+            flops=3 * tokens * head.shape[0] * width,
+            bytes_accessed=2 * tokens * width,
+            transcendentals=tokens * head.shape[0],
+        ),
+        compiler_params=pltpu.CompilerParams(vmem_limit_bytes=16 << 20),
+        name="vocabulary_scores",
+    )(place, *sets, pltpu.with_memory_space_constraint(head, pltpu.VMEM))
+
+
+def spread_kernel(sections, groups, widths, place_ref, slot_ref, *refs):
+    stats, (out_ref, table, block) = refs[:-3], refs[-3:]
+    share = table.shape[2]
+    first = 0
+    for stat in stats:
+        table[first : first + stat.shape[0]] = stat[...]
+        first += stat.shape[0]
+    slots = slot_ref.shape[0] // groups
+    block[...] = jnp.zeros_like(block)
+    for group in range(groups):
+        for slot in range(slots):
+            utterance = jnp.maximum(slot_ref[group * slots + slot], 0)
+            for section in range(sections):
+                at = (section ^ place_ref[0]) * groups + (utterance ^ place_ref[1])
+                block[group, 3 * slot : 3 * slot + 3, section * share : (section + 1) * share] = (
+                    table[at][0:3, :]
+                )
+    for section in range(sections):
+        for group in range(groups):
+            for width in range(widths):
+                out_ref[(section * groups + group) * widths + width] = block[group]
+
+
+def spread_stats(place, slot_utt, stats, sections, groups, widths):
+    share = stats[0].shape[2]
+    assert 3 * slot_utt.shape[0] // groups <= 8
+    return pl.pallas_call(
+        functools.partial(spread_kernel, sections, groups, widths),
+        in_specs=[SCALARS] * 2 + [INSIDE] * len(stats),
+        out_specs=INSIDE,
+        out_shape=jax.ShapeDtypeStruct(
+            (sections * groups * widths, 8, sections * share), jnp.float32
+        ),
+        scratch_shapes=[
+            pltpu.VMEM((sections * groups, 8, share), jnp.float32),
+            pltpu.VMEM((groups, 8, sections * share), jnp.float32),
+        ],
+        compiler_params=pltpu.CompilerParams(vmem_limit_bytes=16 << 20),
+        name="statistics_by_group",
+    )(place, slot_utt, *stats)
+
+
+def score_kernel(sections, widths, place_ref, slot_ref, length_ref, every_ref, out_ref):
+    slots, hyps = out_ref.shape
+    lanes = every_ref.shape[2]
+    share = lanes // sections // widths
+    lane = lax.broadcasted_iota(jnp.int32, (1, lanes), 1)
+    order = lane % share * (sections * widths) + lane // share
+    column = lax.broadcasted_iota(jnp.int32, (1, hyps), 1)
+    for slot in range(slots):
+        upper = every_ref[:, 3 * slot, :]
+        peak = jnp.max(upper, axis=0, keepdims=True)
+        total = jnp.sum(
+            every_ref[:, 3 * slot + 1, :] * jnp.exp(upper - peak), axis=0, keepdims=True
+        )
+        picked = jnp.sum(every_ref[:, 3 * slot + 2, :], axis=0, keepdims=True)
+        logp = picked - (peak + jnp.log(total))
+        scores = jnp.zeros((1, hyps), jnp.float32)
+        start = jnp.int32(0)
+        for hyp in range(hyps):
+            length = length_ref[slot * hyps + hyp]
+            valid = (order >= start) & (order < start + length)
+            summed = jnp.sum(jnp.where(valid, logp, 0.0), axis=1, keepdims=True)
+            mean = summed / jnp.full((1, 1), length, jnp.int32).astype(jnp.float32)
+            scores = jnp.where(column == hyp, mean + math.log(V), scores)
+            start = start + length
+        filled = slot_ref[place_ref[1] * slots + slot] >= 0
+        out_ref[slot : slot + 1, :] = jnp.where(filled, scores, 0.0)
+
+
+def hypothesis_scores(place, slot_utt, lengths, every, slots, hyps, sections, widths):
+    return pl.pallas_call(
+        functools.partial(score_kernel, sections, widths),
+        in_specs=[SCALARS] * 3 + [INSIDE],
+        out_specs=INSIDE,
+        out_shape=jax.ShapeDtypeStruct((slots, hyps), jnp.float32),
+        compiler_params=pltpu.CompilerParams(vmem_limit_bytes=16 << 20),
+        name="hypothesis_scores",
+    )(place, slot_utt, lengths, every)
+
+
+def near_device(
+    frame_len,
+    slot_utt,
+    enc_in,
+    ffn_up,
+    ffn_down,
+    kv_proj,
+    hyp_state,
+    hyp_tok,
+    hyp_len,
+    q_proj,
+    o_proj,
+    head,
+):
+    section_count = lax.axis_size("section")
+    group_count = lax.axis_size("tm")
+    width_count = lax.axis_size("mp")
+    section_pos = lax.axis_index("section")
+    group_pos = lax.axis_index("tm")
+    width_pos = lax.axis_index("mp")
+    head_devices = section_count * width_count
+    all_devices = head_devices * group_count
+
+    frame_rows, utterances, enc_width = enc_in.shape
+    slot_count, hyp_count, positions, model_width = hyp_state.shape
+    slot_tokens = hyp_count * positions
+    share_rows = slot_tokens // head_devices
+    vocab_start = (
+        (section_pos * group_count + group_pos) * width_count + width_pos
+    ) * head.shape[0]
+    head_pos = section_pos * width_count + width_pos
+    place = jnp.stack([section_pos, group_pos, width_pos, vocab_start, head_pos])
+    place = place.astype(jnp.int32)
+    lengths = hyp_len.reshape(-1)
+
+    parts = ffn(
+        place, enc_in.reshape(frame_rows * utterances, enc_width), ffn_up, ffn_down, width_count
+    )
+    own_frames = parts[width_count]
+    parts = [parts[0]] + [
+        swap(parts[distance], "mp", distance) for distance in range(1, width_count)
+    ]
+
+    blocks = queries_of(
+        place,
+        slot_utt,
+        lengths,
+        hyp_state.reshape(slot_count, slot_tokens, model_width),
+        hyp_tok.reshape(slot_count, 1, slot_tokens),
+        q_proj,
+        group_count,
+        share_rows,
+    )
+    payloads = [blocks[0]] + [
+        swap(blocks[distance], "tm", distance) for distance in range(1, group_count)
+    ]
+    shares = blocks[group_count:]
+
+    sent = keys_values_of(parts, own_frames, kv_proj, section_count, utterances, width_count)
+    frames_all = all_devices * (frame_rows // width_count)
+    keys_values = exchange(sent.reshape(all_devices, -1, 2 * HD), ALL).reshape(frames_all, 2 * HD)
+    keys_values, *shares = lax.optimization_barrier((keys_values, *shares))
+    shares = [shares[0]] + [
+        swap(shares[distance], "tm", distance) for distance in range(1, group_count)
+    ]
+
+    pieces = (share_rows // 2, share_rows - share_rows // 2)
+    projected = attend(
+        place,
+        slot_utt,
+        frame_len,
+        payloads,
+        keys_values,
+        o_proj,
+        pieces,
+        section_count,
+        width_count,
+    )
+    sums = []
+    for number, piece in enumerate(pieces):
+        other = swap(projected[number], "section", 1)
+        section_sum = (
+            projected[len(pieces) + number].astype(jnp.float32) + other.astype(jnp.float32)
+        ).astype(jnp.bfloat16)
+        for distance in range(width_count):
+            block = lax.dynamic_slice_in_dim(
+                section_sum, (width_pos ^ distance) * piece, piece, 0
+            )
+            sums.append(swap(block, "mp", distance) if distance else block)
+    out_rows = normed_rows(place, slot_utt, shares, sums, pieces, width_count)
+
+    share = out_rows.shape[0]
+    own = jnp.zeros((width_count * share, out_rows.shape[1]), jnp.bfloat16)
+    for distance in range(width_count):
+        block = swap(out_rows, "mp", distance) if distance else out_rows
+        own = lax.dynamic_update_slice_in_dim(own, block, (width_pos ^ distance) * share, 0)
+    half = own.shape[0] // 2
+    by_x = swap(own, "section", 1)
+    by_y = swap(own, "tm", 2)
+    across = jnp.concatenate([swap(by_x[:half], "tm", 2), swap(by_y[half:], "section", 1)])
+    stats = [
+        vocabulary_stats(place, [own, swap(own, "tm", 1)], head),
+        vocabulary_stats(place, [by_y, swap(by_y, "tm", 1), by_x, swap(by_x, "tm", 1)], head),
+        vocabulary_stats(place, [across, swap(across, "tm", 1)], head),
+    ]
+
+    every = exchange(
+        spread_stats(place, slot_utt, stats, section_count, group_count, width_count), ALL
+    )
+    return hypothesis_scores(
+        place, slot_utt, lengths, every, slot_count, hyp_count, section_count, width_count
+    )
+
+
+def general(
     frame_len,
     slot_utt,
     enc_in,
@@ -205,6 +840,8 @@
         P(("section", "tm", "mp"), None),
     )
     out_specs = P("tm", None)
+    near = dict(mesh.shape) == {"section": 2, "tm": 4, "mp": 4}
+    per_device = near_device if near else general
     return jax.shard_map(
         per_device, mesh=mesh, in_specs=in_specs, out_specs=out_specs, check_vma=False
     )

time: 221 us -> 140 us (0.63)
  waiting for transfers between devices: 91.5 us -> 45.5 us
  Pallas kernels: 0 us -> 35.4 us
  matrix products: 32.5 us -> 0 us
  other arithmetic: 26 us -> 0.13 us
  between operations: 18.8 us -> 0.22 us
  starting transfers between devices: 28.4 us -> 37.7 us
  blocking collectives: 16.1 us -> 13.8 us
    all_gather x1 -> x0, waiting for transfers between devices: 53.7 us -> none  [per_device(): hidden_rows = lax.all_gather(out_normed, ALL, axis=0, tiled=True)]
    ppermute x0 -> x28, waiting for transfers between devices: none -> 44.5 us  [swap(): return lax.ppermute(values, axis, pairs)]
    all_to_all x6 -> x1, waiting for transfers between devices: 37.8 us -> 1.02 us  [exchange(): return lax.all_to_all(blocks, axis, split_axis=0, concat_axis=0, tiled=True)]
    pallas_call x0 -> x10, Pallas kernels: none -> 35.4 us  [the longest x3 17.5 us: vocabulary_stats(): pl.pallas_call(functools.partial(vocabulary_kernel, head.shape[0] // 2),...]
    ppermute x0 -> x28, starting transfers between devices: none -> 33 us  [swap(): return lax.ppermute(values, axis, pairs)]
    dot_general x7 -> x0, matrix products: 31.3 us -> none  [the longest x1 15.1 us: per_device(): lax.dot_general(hidden_rows, head, (((1,), (1,)), ((), ())), preferred_el...]
    all_to_all x6 -> x1, starting transfers between devices: 28.4 us -> 4.72 us  [exchange(): return lax.all_to_all(blocks, axis, split_axis=0, concat_axis=0, tiled=True)]
    reduce_sum x13 -> x0, other arithmetic: 15.6 us -> none  [the longest x3 4.54 us: scatter_sum(): return jnp.sum(exchange(blocks, axis).astype(jnp.float32), axis=0)]
  transfers between devices with their start and end apart: 7 -> 29, of which waited for: 6 -> 12; matrix products, arithmetic and copies ran while one was open for 10% -> 0% of each run, Pallas kernels for 0% -> 12%
where the time goes in v4:
time: 140 us
  waiting for transfers between devices  45.5 us (32%)
  starting transfers between devices  37.7 us (27%)
  Pallas kernels  35.4 us (25%)
  blocking collectives  13.8 us (10%)
  local copies, waits for them, and re-layouts  7.25 us (5%)
    ppermute x28, waiting for transfers between devices, swap(): return lax.ppermute(values, axis, pairs)  44.5 us
    ppermute x28, starting transfers between devices, swap(): return lax.ppermute(values, axis, pairs)  33 us
    pallas_call x3, Pallas kernels, vocabulary_stats(): pl.pallas_call(functools.partial(vocabulary_kernel, head.shape[0] // 2),...  17.5 us
    all_to_all x1, blocking collectives, exchange(): return lax.all_to_all(blocks, axis, split_axis=0, concat_axis=0, tiled=True)  13.8 us
    unnamed x15, local copies, waits for them, and re-layouts  5.71 us
    pallas_call x1, Pallas kernels, queries_of(): pl.pallas_call(functools.partial(query_kernel, count, depth), in_specs=[S...  5.19 us
    pallas_call x1, Pallas kernels, ffn(): pl.pallas_call(functools.partial(ffn_kernel, count, tile), in_specs=[SCAL...  5.15 us
    all_to_all x1, starting transfers between devices, exchange(): return lax.all_to_all(blocks, axis, split_axis=0, concat_axis=0, tiled=True)  4.72 us
  transfers between devices with their start and end apart: 29, of which 12 were waited for; matrix products, arithmetic and copies ran while one was open for 0% of the time, Pallas kernels for 12%

profile of v4, /device:TPU:0, one launch (start us, length us, event | category | flops | bytes accessed | tf_op | source)
XLA Modules:
  0.0 140.0 jit_solution(6414104929115567541)
XLA Ops:
  0.0 1.1 reshape.19.x_ref
  1.1 0.1 stack.23.place_ref.refs_0_.first_ref
  1.1 5.2 %encoder_ffn.1 = (bf16[32,1280]{1,0:T(8,128)(2,1)S(1)}, bf16[32,1280]{1,0:T(8,128)(2,1)S(1)}, bf16[32,1280]{1,0:T(8,128)(2,1)S(1)}, bf16[32,1280]{1,0:T(8,128)(2,1)S(1)}, bf16[32,1280]{1,0:T(8,128)(2,1)S(1)}) custom-call(s32[5]{0:T(128)S(1)} %stack.23.place_ref.refs_0_.first_ref, bf16[128,1280]{1,0:T(8,128)(2,1)S(1)} %reshape.19.x_ref, ...), custom_call_target="tpu_custom_call" | custom-call | flops 838860800 | bytes 6553600 | tf_op jit(solution)/shard_map/encoder_ffn/pallas_call | solution.py:113
  6.3 0.0 copy-start.6
  6.3 0.0 copy-start.5
  6.3 0.0 copy-start.3
  6.3 3.1 %collective-permute-start = (bf16[32,1280]{1,0:T(8,128)(2,1)S(1)}, bf16[32,1280]{1,0:T(8,128)(2,1)S(1)}, u32[]{:S(2)}, u32[]{:S(2)}) collective-permute-start(bf16[32,1280]{1,0:T(8,128)(2,1)S(1)} %get-tuple-element.28), channel_id=1, source_target_pairs={{0,1},{1,0},{2,3},{3,2},{4,5},{5,4},{6,7},{7,6},{8,9},{9,8},{10,11... | collective-permute-start | bytes 245768 | tf_op jit(solution)/shard_map/ppermute | solution.py:40
  9.4 2.6 %collective-permute-start.1 = (bf16[32,1280]{1,0:T(8,128)(2,1)S(1)}, bf16[32,1280]{1,0:T(8,128)(2,1)S(1)}, u32[]{:S(2)}, u32[]{:S(2)}) collective-permute-start(bf16[32,1280]{1,0:T(8,128)(2,1)S(1)} %get-tuple-element.29), channel_id=1, source_target_pairs={{0,2},{1,3},{2,0},{3,1},{4,6},{5,7},{6,4},{7,5},{8,10},{9,11},{10,... | collective-permute-start | bytes 245768 | tf_op jit(solution)/shard_map/ppermute | solution.py:40
  12.0 0.0 collective-permute-start.2
  12.0 0.0 collective-permute-done.refs_1_
  12.0 6.6 %collective-permute-done.1.refs_2_ = bf16[32,1280]{1,0:T(8,128)(2,1)S(1)} collective-permute-done((bf16[32,1280]{1,0:T(8,128)(2,1)S(1)}, bf16[32,1280]{1,0:T(8,128)(2,1)S(1)}, u32[]{:S(2)}, u32[]{:S(2)}) %collective-permute-start.1) | collective-permute-done | bytes 81952 | tf_op jit(solution)/shard_map/ppermute | solution.py:40
  18.6 0.0 collective-permute-done.2.refs_3_
  18.6 1.5 %frame_keys_values.1 = bf16[256,256]{1,0:T(8,128)(2,1)} custom-call(bf16[32,1280]{1,0:T(8,128)(2,1)S(1)} %get-tuple-element.27.refs_0_, bf16[32,1280]{1,0:T(8,128)(2,1)S(1)} %collective-permute-done.refs_1_, bf16[32,1280]{1,0:T(8,128)(2,1)S(1)} %collective-permute-done.1.refs_2_, bf16[32,1280]{1,0:T(8,128)(2,1)S(1)} %collective-permute-done.2.refs_3_, ...), custom_call_target="tpu_custom_call" | custom-call | flops 83886080 | bytes 2621440 | tf_op jit(solution)/shard_map/frame_keys_values/pallas_call | solution.py:265
  20.2 4.7 %all-to-all-start = ((bf16[32,8,256]{2,1,0:T(8,128)(2,1)}), bf16[32,8,256]{2,1,0:T(8,128)(2,1)S(1)}, u32[]{:S(2)}, u32[]{:S(2)}) async-start(bf16[32,8,256]{2,1,0:T(8,128)(2,1)} %bitcast.5), calls=%async_computation | async-start | bytes 262144 | tf_op jit(solution)/shard_map/all_to_all | solution.py:30
  24.9 0.1 reshape.18.length_ref
  25.0 0.1 reshape.23.tok_ref
  25.1 5.2 %hypothesis_queries.1 = (bf16[128,512]{1,0:T(8,128)(2,1)S(1)}, bf16[128,512]{1,0:T(8,128)(2,1)S(1)}, bf16[128,512]{1,0:T(8,128)(2,1)S(1)}, bf16[128,512]{1,0:T(8...) custom-call(s32[5]{0:T(128)S(1)} %stack.23.place_ref.refs_0_.first_r, ...), custom_call_target="tpu_custom_call" | custom-call | flops 1073741824 | bytes 6291456 | tf_op jit(solution)/shard_map/hypothesis_queries/pallas_call | solution.py:206
  30.3 0.3 collective-permute-start.6
  30.6 1.7 %collective-permute-start.7 = (bf16[128,512]{1,0:T(8,128)(2,1)S(1)}, bf16[128,512]{1,0:T(8,128)(2,1)S(1)}, u32[]{:S(2)}, u32[]{:S(2)}) collective-permute-start(bf16[128,512]{1,0:T(8,128)(2,1)S(1)} %get-tuple-element.42), channel_id=1, source_target_pairs={{0,8},{4,12},{8,0},{12,4},{1,9},{5,13},{9,1},{13,5},{2,10},{6,14},... | collective-permute-start | bytes 393224 | tf_op jit(solution)/shard_map/ppermute | solution.py:40
  32.3 0.0 collective-permute-start.8
  32.3 1.0 all-to-all-done
  33.3 3.6 %collective-permute-done.7.refs_5_ = bf16[128,512]{1,0:T(8,128)(2,1)S(1)} collective-permute-done((bf16[128,512]{1,0:T(8,128)(2,1)S(1)}, bf16[128,512]{1,0:T(8,128)(2,1)S(1)}, u32[]{:S(2)}, u32[]{:S(2)}) %collective-permute-start.7) | collective-permute-done | bytes 131104 | tf_op jit(solution)/shard_map/ppermute | solution.py:40
  36.9 1.5 %collective-permute-done.8.refs_6_ = bf16[128,512]{1,0:T(8,128)(2,1)S(1)} collective-permute-done((bf16[128,512]{1,0:T(8,128)(2,1)S(1)}, bf16[128,512]{1,0:T(8,128)(2,1)S(1)}, u32[]{:S(2)}, u32[]{:S(2)}) %collective-permute-start.8) | collective-permute-done | bytes 131104 | tf_op jit(solution)/shard_map/ppermute | solution.py:40
  38.4 3.1 %attention_projection.1 = (bf16[32,4096]{1,0:T(8,128)(2,1)S(1)}, bf16[32,4096]{1,0:T(8,128)(2,1)S(1)}, bf16[32,4096]{1,0:T(8,128)(2,1)S(1)}, bf16[32,4096]{1,0:T(8,128)(2,1)S(1)}) custom-call(s32[5]{0:T(128)S(1)} %stack.23.place_ref.refs_0_.first_ref, s32[8]{0:T(128)S(1)} %copy-done.3, s32[4]{0:T(128)S(1)} %copy-done.4, ...), custom_call_target="tpu_custom_call" | custom-call | flops 603979776 | bytes 5242880 | tf_op jit(solution)/shard_map/attention_projection/pallas_call | solution.py:349
  41.5 1.9 %collective-permute-start.9 = (bf16[32,4096]{1,0:T(8,128)(2,1)S(1)}, bf16[32,4096]{1,0:T(8,128)(2,1)S(1)}, u32[]{:S(2)}, u32[]{:S(2)}) collective-permute-start(bf16[32,4096]{1,0:T(8,128)(2,1)S(1)} %get-tuple-element.46), channel_id=1, source_target_pairs={{0,16},{16,0},{1,17},{17,1},{2,18},{18,2},{3,19},{19,3},{4,20},{20... | collective-permute-start | bytes 786440 | tf_op jit(solution)/shard_map/ppermute | solution.py:40
  43.5 0.1 collective-permute-start.3
  43.5 1.5 %collective-permute-start.4 = (bf16[144,512]{1,0:T(8,128)(2,1)S(1)}, bf16[144,512]{1,0:T(8,128)(2,1)S(1)}, u32[]{:S(2)}, u32[]{:S(2)}) collective-permute-start(bf16[144,512]{1,0:T(8,128)(2,1)S(1)} %get-tuple-element.38), channel_id=1, source_target_pairs={{0,8},{4,12},{8,0},{12,4},{1,9},{5,13},{9,1},{13,5},{2,10},{6,14},... | collective-permute-start | bytes 442376 | tf_op jit(solution)/shard_map/ppermute | solution.py:40
  45.1 0.3 collective-permute-start.5
  45.3 0.3 collective-permute-start.13
  45.6 5.1 %collective-permute-done.9 = bf16[32,4096]{1,0:T(8,128)(2,1)S(1)} collective-permute-done((bf16[32,4096]{1,0:T(8,128)(2,1)S(1)}, bf16[32,4096]{1,0:T(8,128)(2,1)S(1)}, u32[]{:S(2)}, u32[]{:S(2)}) %collective-permute-start.9) | collective-permute-done | bytes 262176 | tf_op jit(solution)/shard_map/ppermute | solution.py:40
  50.7 0.1 add_convert_fusion.1
  50.8 1.9 %collective-permute-start.10 = (bf16[8,4096]{1,0:T(8,128)(2,1)S(1)}, bf16[8,4096]{1,0:T(8,128)(2,1)S(1)}, u32[]{:S(2)}, u32[]{:S(2)}) collective-permute-start(bf16[8,4096]{1,0:T(8,128)(2,1)S(1)} %get-tuple-element.55), channel_id=1, source_target_pairs={{0,1},{1,0},{2,3},{3,2},{4,5},{5,4},{6,7},{7,6},{8,9},{9,8},{10,11... | collective-permute-start | bytes 196616 | tf_op jit(solution)/shard_map/ppermute | solution.py:40
  52.8 3.2 %collective-permute-done.13 = bf16[32,4096]{1,0:T(8,128)(2,1)S(1)} collective-permute-done((bf16[32,4096]{1,0:T(8,128)(2,1)S(1)}, bf16[32,4096]{1,0:T(8,128)(2,1)S(1)}, u32[]{:S(2)}, u32[]{:S(2)}) %collective-permute-start.13) | collective-permute-done | bytes 262176 | tf_op jit(solution)/shard_map/ppermute | solution.py:40
  55.9 2.7 %collective-permute-start.11 = (bf16[8,4096]{1,0:T(8,128)(2,1)S(1)}, bf16[8,4096]{1,0:T(8,128)(2,1)S(1)}, u32[]{:S(2)}, u32[]{:S(2)}) collective-permute-start(bf16[8,4096]{1,0:T(8,128)(2,1)S(1)} %get-tuple-element.54), channel_id=1, source_target_pairs={{0,2},{1,3},{2,0},{3,1},{4,6},{5,7},{6,4},{7,5},{8,10},{9,11},{10,... | collective-permute-start | bytes 196616 | tf_op jit(solution)/shard_map/ppermute | solution.py:40
  58.6 0.1 add_convert_fusion
  58.7 1.5 %collective-permute-start.12 = (bf16[8,4096]{1,0:T(8,128)(2,1)S(1)}, bf16[8,4096]{1,0:T(8,128)(2,1)S(1)}, u32[]{:S(2)}, u32[]{:S(2)}) collective-permute-start(bf16[8,4096]{1,0:T(8,128)(2,1)S(1)} %get-tuple-element.53), channel_id=1, source_target_pairs={{0,3},{1,2},{2,1},{3,0},{4,7},{5,6},{6,5},{7,4},{8,11},{9,10},{10,... | collective-permute-start | bytes 196616 | tf_op jit(solution)/shard_map/ppermute | solution.py:40
  60.2 0.1 collective-permute-start.14
  60.4 0.0 collective-permute-done.5.refs_3_
  60.4 2.8 %collective-permute-start.15 = (bf16[8,4096]{1,0:T(8,128)(2,1)S(1)}, bf16[8,4096]{1,0:T(8,128)(2,1)S(1)}, u32[]{:S(2)}, u32[]{:S(2)}) collective-permute-start(bf16[8,4096]{1,0:T(8,128)(2,1)S(1)} %get-tuple-element.50), channel_id=1, source_target_pairs={{0,2},{1,3},{2,0},{3,1},{4,6},{5,7},{6,4},{7,5},{8,10},{9,11},{10,... | collective-permute-start | bytes 196616 | tf_op jit(solution)/shard_map/ppermute | solution.py:40
  63.1 0.0 collective-permute-done.10.refs_5_
  63.2 1.4 %collective-permute-start.16 = (bf16[8,4096]{1,0:T(8,128)(2,1)S(1)}, bf16[8,4096]{1,0:T(8,128)(2,1)S(1)}, u32[]{:S(2)}, u32[]{:S(2)}) collective-permute-start(bf16[8,4096]{1,0:T(8,128)(2,1)S(1)} %get-tuple-element.49), channel_id=1, source_target_pairs={{0,3},{1,2},{2,1},{3,0},{4,7},{5,6},{6,5},{7,4},{8,11},{9,10},{10,... | collective-permute-start | bytes 196616 | tf_op jit(solution)/shard_map/ppermute | solution.py:40
  64.6 0.8 collective-permute-done.12.refs_7_
  65.4 4.2 %collective-permute-done.15.refs_10_ = bf16[8,4096]{1,0:T(8,128)(2,1)S(1)} collective-permute-done((bf16[8,4096]{1,0:T(8,128)(2,1)S(1)}, bf16[8,4096]{1,0:T(8,128)(2,1)S(1)}, u32[]{:S(2)}, u32[]{:S(2)}) %collective-permute-start.15) | collective-permute-done | bytes 65568 | tf_op jit(solution)/shard_map/ppermute | solution.py:40
  69.6 0.9 token_rows.1
  70.5 1.7 %collective-permute-start.17 = (bf16[16,4224]{1,0:T(8,128)(2,1)S(1)}, bf16[16,4224]{1,0:T(8,128)(2,1)S(1)}, u32[]{:S(2)}, u32[]{:S(2)}) collective-permute-start(bf16[16,4224]{1,0:T(8,128)(2,1)S(1)} %token_rows.1), channel_id=1, source_target_pairs={{0,1},{1,0},{2,3},{3,2},{4,5},{5,4},{6,7},{7,6},{8,9},{9,8},{10,11... | collective-permute-start | bytes 405512 | tf_op jit(solution)/shard_map/ppermute | solution.py:40
  72.3 2.4 %collective-permute-start.18 = (bf16[16,4224]{1,0:T(8,128)(2,1)S(1)}, bf16[16,4224]{1,0:T(8,128)(2,1)S(1)}, u32[]{:S(2)}, u32[]{:S(2)}) collective-permute-start(bf16[16,4224]{1,0:T(8,128)(2,1)S(1)} %token_rows.1), channel_id=1, source_target_pairs={{0,2},{1,3},{2,0},{3,1},{4,6},{5,7},{6,4},{7,5},{8,10},{9,11},{10,... | collective-permute-start | bytes 405512 | tf_op jit(solution)/shard_map/ppermute | solution.py:40
  74.6 0.7 collective-permute-start.19
  75.4 1.6 %collective-permute-done.17 = bf16[16,4224]{1,0:T(8,128)(2,1)S(1)} collective-permute-done((bf16[16,4224]{1,0:T(8,128)(2,1)S(1)}, bf16[16,4224]{1,0:T(8,128)(2,1)S(1)}, u32[]{:S(2)}, u32[]{:S(2)}) %collective-permute-start.17) | collective-permute-done | bytes 135200 | tf_op jit(solution)/shard_map/ppermute | solution.py:40
  77.0 8.2 %collective-permute-done.18 = bf16[16,4224]{1,0:T(8,128)(2,1)S(1)} collective-permute-done((bf16[16,4224]{1,0:T(8,128)(2,1)S(1)}, bf16[16,4224]{1,0:T(8,128)(2,1)S(1)}, u32[]{:S(2)}, u32[]{:S(2)}) %collective-permute-start.18) | collective-permute-done | bytes 135200 | tf_op jit(solution)/shard_map/ppermute | solution.py:40
  85.3 1.5 %collective-permute-start.23 = (bf16[64,4224]{1,0:T(8,128)(2,1)S(1)}, bf16[64,4224]{1,0:T(8,128)(2,1)S(1)}, u32[]{:S(2)}, u32[]{:S(2)}) collective-permute-start(bf16[64,4224]{1,0:T(8,128)(2,1)S(1)} %constant_dynamic-update-slice_fusion.2.refs_0_), channel_id=1, source_target_pairs={{0,16},{16,0},{1,17},{17,1},{2,18},{18,2},{3,19},{19,3},{4,20},{20... | collective-permute-start | bytes 1622024 | tf_op jit(solution)/shard_map/ppermute | solution.py:40
  86.8 1.5 %collective-permute-start.21 = (bf16[64,4224]{1,0:T(8,128)(2,1)S(1)}, bf16[64,4224]{1,0:T(8,128)(2,1)S(1)}, u32[]{:S(2)}, u32[]{:S(2)}) collective-permute-start(bf16[64,4224]{1,0:T(8,128)(2,1)S(1)} %constant_dynamic-update-slice_fusion.2.refs_0_), channel_id=1, source_target_pairs={{0,8},{4,12},{8,0},{12,4},{1,9},{5,13},{9,1},{13,5},{2,10},{6,14},... | collective-permute-start | bytes 1622024 | tf_op jit(solution)/shard_map/ppermute | solution.py:40
  88.3 8.2 %collective-permute-done.23.refs_2_ = bf16[64,4224]{1,0:T(8,128)(2,1)S(1)} collective-permute-done((bf16[64,4224]{1,0:T(8,128)(2,1)S(1)}, bf16[64,4224]{1,0:T(8,128)(2,1)S(1)}, u32[]{:S(2)}, u32[]{:S(2)}) %collective-permute-start.23) | collective-permute-done | bytes 540704 | tf_op jit(solution)/shard_map/ppermute | solution.py:40
  96.5 1.7 %collective-permute-start.25 = (bf16[32,4224]{1,0:T(8,128)(2,1)S(1)}, bf16[32,4224]{1,0:T(8,128)(2,1)S(1)}, u32[]{:S(2)}, u32[]{:S(2)}) collective-permute-start(bf16[32,4224]{1,0:T(8,128)(2,1)S(1)} %slice.8), channel_id=1, source_target_pairs={{0,8},{4,12},{8,0},{12,4},{1,9},{5,13},{9,1},{13,5},{2,10},{6,14},... | collective-permute-start | bytes 811016 | tf_op jit(solution)/shard_map/ppermute | solution.py:40
  98.3 1.5 %collective-permute-done.21.refs_0_ = bf16[64,4224]{1,0:T(8,128)(2,1)S(1)} collective-permute-done((bf16[64,4224]{1,0:T(8,128)(2,1)S(1)}, bf16[64,4224]{1,0:T(8,128)(2,1)S(1)}, u32[]{:S(2)}, u32[]{:S(2)}) %collective-permute-start.21) | collective-permute-done | bytes 540704 | tf_op jit(solution)/shard_map/ppermute | solution.py:40
  99.8 0.6 collective-permute-start.26
  100.4 0.5 collective-permute-start.24
  100.9 5.7 %copy-done = bf16[2000,4096]{1,0:T(8,128)(2,1)S(1)} copy-done((bf16[2000,4096]{1,0:T(8,128)(2,1)S(1)}, bf16[2000,4096]{1,0:T(8,128)(2,1)}, u32[]{:S(2)}) %copy-start) | copy-done | bytes 16384024
  106.6 5.7 %vocabulary_scores.3.refs_0_ = f32[2,8,64]{2,1,0:T(8,128)S(1)} custom-call(s32[5]{0:T(128)S(1)} %stack.23.place_ref.refs_0_.first_ref, bf16[64,4224]{1,0:T(8,128)(2,1)S(1)} %constant_dynamic-update-slice_fusion.2.refs_0_, bf16[64,4224]{1,0:T(8,128)(2,1)S(1)} %collective-permute-done.20.refs_1_, bf16[2000,4096]{1,0:T(8,128)(2,1)S(1)} %copy-done), custom_call_target="tpu_custom_call" | custom-call | flops 3145728000 | bytes 1048576 | tf_op jit(solution)/shard_map/vocabulary_scores/pallas_call | solution.py:455
  112.4 0.1 collective-permute-start.27
  112.5 6.0 %vocabulary_scores.4.refs_1_ = f32[4,8,64]{2,1,0:T(8,128)S(1)} custom-call(s32[5]{0:T(128)S(1)} %stack.23.place_ref.refs_0_.first_ref, bf16[64,4224]{1,0:T(8,128)(2,1)S(1)} %collective-permute-done.21.refs_0_, bf16[64,4224]{1,0:T(8,128)(2,1)S(1)} %collective-permute-done.22.refs_1_, bf16[64,4224]{1,0:T(8,128)(2,1)S(1)} %collective-permute-done.23.refs_2_, ...), custom_call_target="tpu_custom_call" | custom-call | flops 6291456000 | bytes 2097152 | tf_op jit(solution)/shard_map/vocabulary_scores/pallas_call | solution.py:455
  118.6 5.7 %vocabulary_scores.5.refs_2_ = f32[2,8,64]{2,1,0:T(8,128)S(1)} custom-call(s32[5]{0:T(128)S(1)} %stack.23.place_ref.refs_0_.first_ref, bf16[64,4224]{1,0:T(8,128)(2,1)S(1)} %constant_dynamic-update-slice_fusion.refs_0_, bf16[64,4224]{1,0:T(8,128)(2,1)S(1)} %collective-permute-done.27.refs_1_, bf16[2000,4096]{1,0:T(8,128)(2,1)S(1)} %copy-done.1), custom_call_target="tpu_custom_call" | custom-call | flops 3145728000 | bytes 1048576 | tf_op jit(solution)/shard_map/vocabulary_scores/pallas_call | solution.py:455
  124.3 0.6 statistics_by_group.1
  124.9 13.8 %all_to_all.10.every_ref = f32[32,8,128]{2,1,0:T(8,128)S(1)} all-to-all(f32[32,8,128]{2,1,0:T(8,128)S(1)} %statistics_by_group.1), channel_id=1, replica_groups=mesh['section'=2,'tm'=4,'mp'=4] {'section','tm','mp'}, dimensions={0} | all-to-all | bytes 262144 | tf_op jit(solution)/shard_map/all_to_all | solution.py:30
  138.7 1.3 hypothesis_scores.1
  (36 shorter events, 0.3 us)
Async XLA Ops:
  1.1 17.5 %copy-start.2 = (bf16[1280,1024]{1,0:T(8,128)(2,1)S(1)}, bf16[1280,1024]{1,0:T(8,128)(2,1)}, u32[]{:S(2)}) copy-start(bf16[1280,1024]{1,0:T(8,128)(2,1)} %refs_5_.1) | copy-start | bytes 7864324
  6.3 18.6 %copy-start.6 = (s32[2,8]{1,0:T(2,128)S(1)}, s32[2,8]{1,0:T(2,128)}, u32[]{:S(2)}) copy-start(s32[2,8]{1,0:T(2,128)} %param.20) | copy-start | bytes 196
  6.3 18.7 %copy-start.5 = (s32[2,8,16]{2,1,0:T(8,128)S(1)}, s32[2,8,16]{2,1,0:T(8,128)}, u32[]{:S(2)}) copy-start(s32[2,8,16]{2,1,0:T(8,128)} %param.19) | copy-start | bytes 3076
  6.3 18.7 %copy-start.3 = (s32[8]{0:T(128)S(1)}, s32[8]{0:T(128)}, u32[]{:S(2)}) copy-start(s32[8]{0:T(128)} %slot_ref.7) | copy-start | bytes 100
  6.3 5.7 %collective-permute-start = (bf16[32,1280]{1,0:T(8,128)(2,1)S(1)}, bf16[32,1280]{1,0:T(8,128)(2,1)S(1)}, u32[]{:S(2)}, u32[]{:S(2)}) collective-permute-start(bf16[32,1280]{1,0:T(8,128)(2,1)S(1)} %get-tuple-element.28), channel_id=1, source_target_pairs={{0,1},{1,0},{2,3},{3,2},{4,5},{5,4},{6,7},{7,6},{8,9},{9,8},{10,11... | collective-permute-start | bytes 245768 | tf_op jit(solution)/shard_map/ppermute | solution.py:40
  9.4 9.2 %collective-permute-start.1 = (bf16[32,1280]{1,0:T(8,128)(2,1)S(1)}, bf16[32,1280]{1,0:T(8,128)(2,1)S(1)}, u32[]{:S(2)}, u32[]{:S(2)}) collective-permute-start(bf16[32,1280]{1,0:T(8,128)(2,1)S(1)} %get-tuple-element.29), channel_id=1, source_target_pairs={{0,2},{1,3},{2,0},{3,1},{4,6},{5,7},{6,4},{7,5},{8,10},{9,11},{10,... | collective-permute-start | bytes 245768 | tf_op jit(solution)/shard_map/ppermute | solution.py:40
  12.0 6.6 %collective-permute-start.2 = (bf16[32,1280]{1,0:T(8,128)(2,1)S(1)}, bf16[32,1280]{1,0:T(8,128)(2,1)S(1)}, u32[]{:S(2)}, u32[]{:S(2)}) collective-permute-start(bf16[32,1280]{1,0:T(8,128)(2,1)S(1)} %get-tuple-element.30), channel_id=1, source_target_pairs={{0,3},{1,2},{2,1},{3,0},{4,7},{5,6},{6,5},{7,4},{8,11},{9,10},{10,... | collective-permute-start | bytes 245768 | tf_op jit(solution)/shard_map/ppermute | solution.py:40
  20.2 18.3 %copy-start.4 = (s32[4]{0:T(128)S(1)}, s32[4]{0:T(128)}, u32[]{:S(2)}) copy-start(s32[4]{0:T(128)} %refs_2_.3) | copy-start | bytes 52
  20.2 13.1 %all-to-all-start = ((bf16[32,8,256]{2,1,0:T(8,128)(2,1)}), bf16[32,8,256]{2,1,0:T(8,128)(2,1)S(1)}, u32[]{:S(2)}, u32[]{:S(2)}) async-start(bf16[32,8,256]{2,1,0:T(8,128)(2,1)} %bitcast.5), calls=%async_computation | async-start | bytes 262144 | tf_op jit(solution)/shard_map/all_to_all | solution.py:30
  30.3 3.0 %collective-permute-start.6 = (bf16[128,512]{1,0:T(8,128)(2,1)S(1)}, bf16[128,512]{1,0:T(8,128)(2,1)S(1)}, u32[]{:S(2)}, u32[]{:S(2)}) collective-permute-start(bf16[128,512]{1,0:T(8,128)(2,1)S(1)} %get-tuple-element.41), channel_id=1, source_target_pairs={{0,4},{4,0},{8,12},{12,8},{1,5},{5,1},{9,13},{13,9},{2,6},{6,2},{1... | collective-permute-start | bytes 393224 | tf_op jit(solution)/shard_map/ppermute | solution.py:40
  30.6 6.3 %collective-permute-start.7 = (bf16[128,512]{1,0:T(8,128)(2,1)S(1)}, bf16[128,512]{1,0:T(8,128)(2,1)S(1)}, u32[]{:S(2)}, u32[]{:S(2)}) collective-permute-start(bf16[128,512]{1,0:T(8,128)(2,1)S(1)} %get-tuple-element.42), channel_id=1, source_target_pairs={{0,8},{4,12},{8,0},{12,4},{1,9},{5,13},{9,1},{13,5},{2,10},{6,14},... | collective-permute-start | bytes 393224 | tf_op jit(solution)/shard_map/ppermute | solution.py:40
  32.3 6.2 %collective-permute-start.8 = (bf16[128,512]{1,0:T(8,128)(2,1)S(1)}, bf16[128,512]{1,0:T(8,128)(2,1)S(1)}, u32[]{:S(2)}, u32[]{:S(2)}) collective-permute-start(bf16[128,512]{1,0:T(8,128)(2,1)S(1)} %get-tuple-element.43), channel_id=1, source_target_pairs={{0,12},{4,8},{8,4},{12,0},{1,13},{5,9},{9,5},{13,1},{2,14},{6,10},... | collective-permute-start | bytes 393224 | tf_op jit(solution)/shard_map/ppermute | solution.py:40
  41.5 9.2 %collective-permute-start.9 = (bf16[32,4096]{1,0:T(8,128)(2,1)S(1)}, bf16[32,4096]{1,0:T(8,128)(2,1)S(1)}, u32[]{:S(2)}, u32[]{:S(2)}) collective-permute-start(bf16[32,4096]{1,0:T(8,128)(2,1)S(1)} %get-tuple-element.46), channel_id=1, source_target_pairs={{0,16},{16,0},{1,17},{17,1},{2,18},{18,2},{3,19},{19,3},{4,20},{20... | collective-permute-start | bytes 786440 | tf_op jit(solution)/shard_map/ppermute | solution.py:40
  43.5 15.2 %collective-permute-start.3 = (bf16[144,512]{1,0:T(8,128)(2,1)S(1)}, bf16[144,512]{1,0:T(8,128)(2,1)S(1)}, u32[]{:S(2)}, u32[]{:S(2)}) collective-permute-start(bf16[144,512]{1,0:T(8,128)(2,1)S(1)} %get-tuple-element.37), channel_id=1, source_target_pairs={{0,4},{4,0},{8,12},{12,8},{1,5},{5,1},{9,13},{13,9},{2,6},{6,2},{1... | collective-permute-start | bytes 442376 | tf_op jit(solution)/shard_map/ppermute | solution.py:40
  43.5 16.7 %collective-permute-start.4 = (bf16[144,512]{1,0:T(8,128)(2,1)S(1)}, bf16[144,512]{1,0:T(8,128)(2,1)S(1)}, u32[]{:S(2)}, u32[]{:S(2)}) collective-permute-start(bf16[144,512]{1,0:T(8,128)(2,1)S(1)} %get-tuple-element.38), channel_id=1, source_target_pairs={{0,8},{4,12},{8,0},{12,4},{1,9},{5,13},{9,1},{13,5},{2,10},{6,14},... | collective-permute-start | bytes 442376 | tf_op jit(solution)/shard_map/ppermute | solution.py:40
  45.1 15.3 %collective-permute-start.5 = (bf16[144,512]{1,0:T(8,128)(2,1)S(1)}, bf16[144,512]{1,0:T(8,128)(2,1)S(1)}, u32[]{:S(2)}, u32[]{:S(2)}) collective-permute-start(bf16[144,512]{1,0:T(8,128)(2,1)S(1)} %get-tuple-element.39), channel_id=1, source_target_pairs={{0,12},{4,8},{8,4},{12,0},{1,13},{5,9},{9,5},{13,1},{2,14},{6,10},... | collective-permute-start | bytes 442376 | tf_op jit(solution)/shard_map/ppermute | solution.py:40
  45.3 10.6 %collective-permute-start.13 = (bf16[32,4096]{1,0:T(8,128)(2,1)S(1)}, bf16[32,4096]{1,0:T(8,128)(2,1)S(1)}, u32[]{:S(2)}, u32[]{:S(2)}) collective-permute-start(bf16[32,4096]{1,0:T(8,128)(2,1)S(1)} %get-tuple-element.48), channel_id=1, source_target_pairs={{0,16},{16,0},{1,17},{17,1},{2,18},{18,2},{3,19},{19,3},{4,20},{20... | collective-permute-start | bytes 786440 | tf_op jit(solution)/shard_map/ppermute | solution.py:40
  50.8 12.3 %collective-permute-start.10 = (bf16[8,4096]{1,0:T(8,128)(2,1)S(1)}, bf16[8,4096]{1,0:T(8,128)(2,1)S(1)}, u32[]{:S(2)}, u32[]{:S(2)}) collective-permute-start(bf16[8,4096]{1,0:T(8,128)(2,1)S(1)} %get-tuple-element.55), channel_id=1, source_target_pairs={{0,1},{1,0},{2,3},{3,2},{4,5},{5,4},{6,7},{7,6},{8,9},{9,8},{10,11... | collective-permute-start | bytes 196616 | tf_op jit(solution)/shard_map/ppermute | solution.py:40
  55.9 8.7 %collective-permute-start.11 = (bf16[8,4096]{1,0:T(8,128)(2,1)S(1)}, bf16[8,4096]{1,0:T(8,128)(2,1)S(1)}, u32[]{:S(2)}, u32[]{:S(2)}) collective-permute-start(bf16[8,4096]{1,0:T(8,128)(2,1)S(1)} %get-tuple-element.54), channel_id=1, source_target_pairs={{0,2},{1,3},{2,0},{3,1},{4,6},{5,7},{6,4},{7,5},{8,10},{9,11},{10,... | collective-permute-start | bytes 196616 | tf_op jit(solution)/shard_map/ppermute | solution.py:40
  58.7 6.7 %collective-permute-start.12 = (bf16[8,4096]{1,0:T(8,128)(2,1)S(1)}, bf16[8,4096]{1,0:T(8,128)(2,1)S(1)}, u32[]{:S(2)}, u32[]{:S(2)}) collective-permute-start(bf16[8,4096]{1,0:T(8,128)(2,1)S(1)} %get-tuple-element.53), channel_id=1, source_target_pairs={{0,3},{1,2},{2,1},{3,0},{4,7},{5,6},{6,5},{7,4},{8,11},{9,10},{10,... | collective-permute-start | bytes 196616 | tf_op jit(solution)/shard_map/ppermute | solution.py:40
  60.2 5.2 %collective-permute-start.14 = (bf16[8,4096]{1,0:T(8,128)(2,1)S(1)}, bf16[8,4096]{1,0:T(8,128)(2,1)S(1)}, u32[]{:S(2)}, u32[]{:S(2)}) collective-permute-start(bf16[8,4096]{1,0:T(8,128)(2,1)S(1)} %get-tuple-element.51), channel_id=1, source_target_pairs={{0,1},{1,0},{2,3},{3,2},{4,5},{5,4},{6,7},{7,6},{8,9},{9,8},{10,11... | collective-permute-start | bytes 196616 | tf_op jit(solution)/shard_map/ppermute | solution.py:40
  60.4 9.2 %collective-permute-start.15 = (bf16[8,4096]{1,0:T(8,128)(2,1)S(1)}, bf16[8,4096]{1,0:T(8,128)(2,1)S(1)}, u32[]{:S(2)}, u32[]{:S(2)}) collective-permute-start(bf16[8,4096]{1,0:T(8,128)(2,1)S(1)} %get-tuple-element.50), channel_id=1, source_target_pairs={{0,2},{1,3},{2,0},{3,1},{4,6},{5,7},{6,4},{7,5},{8,10},{9,11},{10,... | collective-permute-start | bytes 196616 | tf_op jit(solution)/shard_map/ppermute | solution.py:40
  63.2 6.4 %collective-permute-start.16 = (bf16[8,4096]{1,0:T(8,128)(2,1)S(1)}, bf16[8,4096]{1,0:T(8,128)(2,1)S(1)}, u32[]{:S(2)}, u32[]{:S(2)}) collective-permute-start(bf16[8,4096]{1,0:T(8,128)(2,1)S(1)} %get-tuple-element.49), channel_id=1, source_target_pairs={{0,3},{1,2},{2,1},{3,0},{4,7},{5,6},{6,5},{7,4},{8,11},{9,10},{10,... | collective-permute-start | bytes 196616 | tf_op jit(solution)/shard_map/ppermute | solution.py:40
  70.5 6.4 %collective-permute-start.17 = (bf16[16,4224]{1,0:T(8,128)(2,1)S(1)}, bf16[16,4224]{1,0:T(8,128)(2,1)S(1)}, u32[]{:S(2)}, u32[]{:S(2)}) collective-permute-start(bf16[16,4224]{1,0:T(8,128)(2,1)S(1)} %token_rows.1), channel_id=1, source_target_pairs={{0,1},{1,0},{2,3},{3,2},{4,5},{5,4},{6,7},{7,6},{8,9},{9,8},{10,11... | collective-permute-start | bytes 405512 | tf_op jit(solution)/shard_map/ppermute | solution.py:40
  72.3 13.0 %collective-permute-start.18 = (bf16[16,4224]{1,0:T(8,128)(2,1)S(1)}, bf16[16,4224]{1,0:T(8,128)(2,1)S(1)}, u32[]{:S(2)}, u32[]{:S(2)}) collective-permute-start(bf16[16,4224]{1,0:T(8,128)(2,1)S(1)} %token_rows.1), channel_id=1, source_target_pairs={{0,2},{1,3},{2,0},{3,1},{4,6},{5,7},{6,4},{7,5},{8,10},{9,11},{10,... | collective-permute-start | bytes 405512 | tf_op jit(solution)/shard_map/ppermute | solution.py:40
  74.6 10.6 %collective-permute-start.19 = (bf16[16,4224]{1,0:T(8,128)(2,1)S(1)}, bf16[16,4224]{1,0:T(8,128)(2,1)S(1)}, u32[]{:S(2)}, u32[]{:S(2)}) collective-permute-start(bf16[16,4224]{1,0:T(8,128)(2,1)S(1)} %token_rows.1), channel_id=1, source_target_pairs={{0,3},{1,2},{2,1},{3,0},{4,7},{5,6},{6,5},{7,4},{8,11},{9,10},{10,... | collective-permute-start | bytes 405512 | tf_op jit(solution)/shard_map/ppermute | solution.py:40
  85.3 11.2 %collective-permute-start.23 = (bf16[64,4224]{1,0:T(8,128)(2,1)S(1)}, bf16[64,4224]{1,0:T(8,128)(2,1)S(1)}, u32[]{:S(2)}, u32[]{:S(2)}) collective-permute-start(bf16[64,4224]{1,0:T(8,128)(2,1)S(1)} %constant_dynamic-update-slice_fusion.2.refs_0_), channel_id=1, source_target_pairs={{0,16},{16,0},{1,17},{17,1},{2,18},{18,2},{3,19},{19,3},{4,20},{20... | collective-permute-start | bytes 1622024 | tf_op jit(solution)/shard_map/ppermute | solution.py:40
  86.8 13.0 %collective-permute-start.21 = (bf16[64,4224]{1,0:T(8,128)(2,1)S(1)}, bf16[64,4224]{1,0:T(8,128)(2,1)S(1)}, u32[]{:S(2)}, u32[]{:S(2)}) collective-permute-start(bf16[64,4224]{1,0:T(8,128)(2,1)S(1)} %constant_dynamic-update-slice_fusion.2.refs_0_), channel_id=1, source_target_pairs={{0,8},{4,12},{8,0},{12,4},{1,9},{5,13},{9,1},{13,5},{2,10},{6,14},... | collective-permute-start | bytes 1622024 | tf_op jit(solution)/shard_map/ppermute | solution.py:40
  88.3 12.7 %collective-permute-start.20 = (bf16[64,4224]{1,0:T(8,128)(2,1)S(1)}, bf16[64,4224]{1,0:T(8,128)(2,1)S(1)}, u32[]{:S(2)}, u32[]{:S(2)}) collective-permute-start(bf16[64,4224]{1,0:T(8,128)(2,1)S(1)} %constant_dynamic-update-slice_fusion.2.refs_0_), channel_id=1, source_target_pairs={{0,4},{4,0},{8,12},{12,8},{1,5},{5,1},{9,13},{13,9},{2,6},{6,2},{1... | collective-permute-start | bytes 1622024 | tf_op jit(solution)/shard_map/ppermute | solution.py:40
  96.5 15.8 %collective-permute-start.25 = (bf16[32,4224]{1,0:T(8,128)(2,1)S(1)}, bf16[32,4224]{1,0:T(8,128)(2,1)S(1)}, u32[]{:S(2)}, u32[]{:S(2)}) collective-permute-start(bf16[32,4224]{1,0:T(8,128)(2,1)S(1)} %slice.8), channel_id=1, source_target_pairs={{0,8},{4,12},{8,0},{12,4},{1,9},{5,13},{9,1},{13,5},{2,10},{6,14},... | collective-permute-start | bytes 811016 | tf_op jit(solution)/shard_map/ppermute | solution.py:40
  99.8 12.6 %collective-permute-start.26 = (bf16[32,4224]{1,0:T(8,128)(2,1)S(1)}, bf16[32,4224]{1,0:T(8,128)(2,1)S(1)}, u32[]{:S(2)}, u32[]{:S(2)}) collective-permute-start(bf16[32,4224]{1,0:T(8,128)(2,1)S(1)} %slice.9), channel_id=1, source_target_pairs={{0,16},{16,0},{1,17},{17,1},{2,18},{18,2},{3,19},{19,3},{4,20},{20... | collective-permute-start | bytes 811016 | tf_op jit(solution)/shard_map/ppermute | solution.py:40
  100.4 12.1 %collective-permute-start.22 = (bf16[64,4224]{1,0:T(8,128)(2,1)S(1)}, bf16[64,4224]{1,0:T(8,128)(2,1)S(1)}, u32[]{:S(2)}, u32[]{:S(2)}) collective-permute-start(bf16[64,4224]{1,0:T(8,128)(2,1)S(1)} %collective-permute-done.21.refs_0_), channel_id=1, source_target_pairs={{0,4},{4,0},{8,12},{12,8},{1,5},{5,1},{9,13},{13,9},{2,6},{6,2},{1... | collective-permute-start | bytes 1622024 | tf_op jit(solution)/shard_map/ppermute | solution.py:40
  100.4 12.1 %collective-permute-start.24 = (bf16[64,4224]{1,0:T(8,128)(2,1)S(1)}, bf16[64,4224]{1,0:T(8,128)(2,1)S(1)}, u32[]{:S(2)}, u32[]{:S(2)}) collective-permute-start(bf16[64,4224]{1,0:T(8,128)(2,1)S(1)} %collective-permute-done.23.refs_2_), channel_id=1, source_target_pairs={{0,4},{4,0},{8,12},{12,8},{1,5},{5,1},{9,13},{13,9},{2,6},{6,2},{1... | collective-permute-start | bytes 1622024 | tf_op jit(solution)/shard_map/ppermute | solution.py:40
  100.9 5.7 %copy-start = (bf16[2000,4096]{1,0:T(8,128)(2,1)S(1)}, bf16[2000,4096]{1,0:T(8,128)(2,1)}, u32[]{:S(2)}) copy-start(bf16[2000,4096]{1,0:T(8,128)(2,1)} %refs_2_.5) | copy-start | bytes 49152004
  106.6 5.9 %copy-start.1 = (bf16[2000,4096]{1,0:T(8,128)(2,1)S(1)}, bf16[2000,4096]{1,0:T(8,128)(2,1)}, u32[]{:S(2)}) copy-start(bf16[2000,4096]{1,0:T(8,128)(2,1)} %refs_2_.5) | copy-start | bytes 49152004
  112.4 6.2 %collective-permute-start.27 = (bf16[64,4224]{1,0:T(8,128)(2,1)S(1)}, bf16[64,4224]{1,0:T(8,128)(2,1)S(1)}, u32[]{:S(2)}, u32[]{:S(2)}) collective-permute-start(bf16[64,4224]{1,0:T(8,128)(2,1)S(1)} %constant_dynamic-update-slice_fusion.refs_0_), channel_id=1, source_target_pairs={{0,4},{4,0},{8,12},{12,8},{1,5},{5,1},{9,13},{13,9},{2,6},{6,2},{1... | collective-permute-start | bytes 1622024 | tf_op jit(solution)/shard_map/ppermute | solution.py:40

commit v5 on v4

--- a/solution.py
+++ b/solution.py
@@ -132,9 +132,10 @@
     )(place, rows, in_hbm(up), in_hbm(down))
 
 
-def query_kernel(count, depth, place_ref, slot_ref, length_ref, x_ref, tok_ref, w_ref, *refs):
-    outs, shares_out = refs[:count], refs[count : 2 * count]
-    states, weights, normed, total, shares, x_sem, w_sem = refs[2 * count :]
+def query_kernel(
+    count, depth, place_ref, slot_ref, length_ref, after_ref, x_ref, tok_ref, w_ref, *refs
+):
+    outs, (states, weights, normed, total, shares, x_sem, w_sem) = refs[:count], refs[count:]
     slots, tokens, width = x_ref.shape
     hyps = length_ref.shape[0] // slots
     positions = tokens // hyps
@@ -188,26 +189,27 @@
             holds = slot_ref[group * slots + candidate] == group ^ distance
             slot = jnp.where(holds, candidate, slot)
         start = pl.multiple_of(slot * tokens, tokens)
-        outs[distance][...] = total[pl.ds(start, tokens), :].astype(jnp.bfloat16)
-        out = shares_out[distance]
+        out = outs[distance]
+        out[:tokens, :] = total[pl.ds(start, tokens), :].astype(jnp.bfloat16)
         for part in range(parts):
-            out[part * share : (part + 1) * share, :] = shares[
+            first = tokens + part * share
+            out[first : first + share, :] = shares[
                 slot, :share, part * columns : (part + 1) * columns
             ]
-        out[parts * share :, :] = shares[slot, share:, :columns]
-
-
-def queries_of(place, slot_utt, lengths, states, targets, weights, count, share):
+        out[tokens + parts * share :, :] = shares[slot, share:, :columns]
+
+
+def queries_of(place, slot_utt, lengths, after, states, targets, weights, count, share):
     slots, tokens, width = states.shape
     columns = weights.shape[1]
     depth = 1024
-    block = jax.ShapeDtypeStruct((tokens, columns), jnp.bfloat16)
-    rows = jax.ShapeDtypeStruct(((width // columns + 1) * share, columns), jnp.bfloat16)
+    rows = tokens + (width // columns + 1) * share
+    block = jax.ShapeDtypeStruct((rows, columns), jnp.bfloat16)
     return pl.pallas_call(
         functools.partial(query_kernel, count, depth),
-        in_specs=[SCALARS] * 3 + [ANYWHERE, INSIDE, ANYWHERE],
-        out_specs=[INSIDE] * (2 * count),
-        out_shape=[block] * count + [rows] * count,
+        in_specs=[SCALARS] * 3 + [ANYWHERE, ANYWHERE, INSIDE, ANYWHERE],
+        out_specs=[INSIDE] * count,
+        out_shape=[block] * count,
         scratch_shapes=[
             pltpu.VMEM(states.shape, jnp.bfloat16),
             pltpu.VMEM((width // depth, depth, columns), jnp.bfloat16),
@@ -224,11 +226,11 @@
         ),
         compiler_params=pltpu.CompilerParams(vmem_limit_bytes=32 << 20),
         name="hypothesis_queries",
-    )(place, slot_utt, lengths, in_hbm(states), targets, in_hbm(weights))
+    )(place, slot_utt, lengths, after, in_hbm(states), targets, in_hbm(weights))
 
 
 def kv_kernel(sections, utterances, widths, *refs):
-    parts, own_ref, w_ref, out_ref = refs[:-3], refs[-3], refs[-2], refs[-1]
+    parts, (own_ref, w_ref, after_ref, out_ref) = refs[:-4], refs[-4:]
     rows = own_ref.shape[0]
     frames = rows // utterances
     total = own_ref[...].astype(jnp.float32)
@@ -260,10 +262,12 @@
                 out_ref[start : start + per_kv * frames, :] = block
 
 
-def keys_values_of(parts, own, weights, sections, utterances, widths):
+def keys_values_of(parts, own, weights, after, sections, utterances, widths):
     rows = sections * widths * own.shape[0]
     return pl.pallas_call(
         functools.partial(kv_kernel, sections, utterances, widths),
+        in_specs=[INSIDE] * (len(parts) + 2) + [ANYWHERE],
+        out_specs=INSIDE,
         out_shape=jax.ShapeDtypeStruct((rows, 2 * HD), jnp.bfloat16),
         cost_estimate=pl.CostEstimate(
             flops=2 * own.shape[0] * weights.shape[0] * weights.shape[1],
@@ -272,18 +276,18 @@
         ),
         compiler_params=pltpu.CompilerParams(vmem_limit_bytes=24 << 20),
         name="frame_keys_values",
-    )(*parts, own, weights)
-
-
-def distance_of_slot(place_ref, slot_ref, slots):
+    )(*parts, own, weights, after)
+
+
+def choice_of_payload(place_ref, slot_ref, slots):
     group = place_ref[1]
     source = jnp.int32(0)
     for slot in range(slot_ref.shape[0]):
         source = jnp.where(slot_ref[slot] == group, slot // slots, source)
-    return source ^ group
-
-
-def attention_kernel(count, capacity, pieces, sections, widths, tile, *refs):
+    return jnp.minimum(source ^ group, 2)
+
+
+def attention_kernel(count, slots, capacity, pieces, sections, widths, tile, *refs):
     place_ref, slot_ref, frame_ref = refs[:3]
     payloads, (kv_ref, w_ref) = refs[3 : 3 + count], refs[3 + count : 5 + count]
     outs = refs[5 + count : 5 + count + 2 * len(pieces)]
@@ -293,7 +297,7 @@
     w_copies = start_copies(
         lambda i: w_ref.at[:, pl.ds(i * tile, tile)], lambda i: weights.at[i], w_sem, tiles
     )
-    source = distance_of_slot(place_ref, slot_ref, slot_ref.shape[0] // count)
+    source = choice_of_payload(place_ref, slot_ref, slots)
     section_pos = place_ref[0]
     frame_limit = frame_ref[place_ref[1]]
     for distance in range(count):
@@ -324,7 +328,8 @@
         at = inside - first * widths
         here = (at >= 0) & (at < piece * widths)
         row = jnp.where(here, first + at % piece, row)
-        width = jnp.where(here, at // piece, width)
+        block = at // piece
+        width = jnp.where(here, block % 2 * (widths // 2) + block // 2, width)
         first += piece
     move = come == (row * sections + section) * widths + width
     ordered = dot(jnp.where(move, 1.0, 0.0).astype(jnp.bfloat16), context[...])
@@ -338,7 +343,7 @@
             first += out.shape[0]
 
 
-def attend(place, slot_utt, frame_len, payloads, keys_values, weights, pieces, sections, widths):
+def attend(place, slot_utt, frame_len, payloads, keys_values, weights, pieces, sections, widths, slots):
     count = len(payloads)
     columns, width = weights.shape
     capacity = sum(pieces) * sections * widths
@@ -347,7 +352,9 @@
     shapes = [jax.ShapeDtypeStruct((piece * widths, width), jnp.bfloat16) for piece in pieces]
     shapes = shapes + shapes
     return pl.pallas_call(
-        functools.partial(attention_kernel, count, capacity, pieces, sections, widths, tile),
+        functools.partial(
+            attention_kernel, count, slots, capacity, pieces, sections, widths, tile
+        ),
         in_specs=[SCALARS] * 3 + [INSIDE] * (count + 1) + [ANYWHERE],
         out_specs=[INSIDE] * len(shapes),
         out_shape=shapes,
@@ -367,26 +374,23 @@
     )(place, slot_utt, frame_len, *payloads, keys_values, in_hbm(weights))
 
 
-def norm_kernel(count, pieces, widths, place_ref, slot_ref, *refs):
-    payloads, blocks = refs[:count], refs[count : count + len(pieces) * widths]
-    out_ref, picked, total = refs[count + len(pieces) * widths :]
+def norm_kernel(count, slots, tokens, pieces, place_ref, slot_ref, after_ref, *refs):
+    payloads, blocks = refs[:count], refs[count : count + 2 * len(pieces)]
+    out_ref, picked, total = refs[count + 2 * len(pieces) :]
     rows, width = total.shape
     columns = picked.shape[1]
     share = picked.shape[0] // (width // columns + 1)
-    source = distance_of_slot(place_ref, slot_ref, slot_ref.shape[0] // count)
-    for distance in range(count):
-
-        @pl.when(source == distance)
-        def _(payload=payloads[distance]):
-            picked[...] = payload[...]
+    source = choice_of_payload(place_ref, slot_ref, slots)
+    for choice in range(count):
+
+        @pl.when(source == choice)
+        def _(payload=payloads[choice]):
+            picked[...] = payload[tokens:, :]
 
     first = 0
     for number, piece in enumerate(pieces):
-        mine = blocks[number * widths : (number + 1) * widths]
-        summed = mine[0][...].astype(jnp.float32)
-        for block in mine[1:]:
-            summed += block[...].astype(jnp.float32)
-        total[first : first + piece, :] = summed
+        kept, other = blocks[2 * number : 2 * number + 2]
+        total[first : first + piece, :] = kept[...] + other[...].astype(jnp.float32)
         first += piece
     for part in range(width // columns):
         take = slice(part * columns, (part + 1) * columns)
@@ -396,21 +400,54 @@
     out_ref[:, width:] = picked[last : last + rows, :LANES]
 
 
-def normed_rows(place, slot_utt, payloads, blocks, pieces, widths):
+def normed_rows(place, slot_utt, after, payloads, blocks, pieces, tokens, slots):
     width = blocks[0].shape[1]
     rows = sum(pieces)
+    columns = payloads[0].shape[1]
     return pl.pallas_call(
-        functools.partial(norm_kernel, len(payloads), pieces, widths),
-        in_specs=[SCALARS] * 2 + [INSIDE] * (len(payloads) + len(blocks)),
+        functools.partial(norm_kernel, len(payloads), slots, tokens, pieces),
+        in_specs=[SCALARS] * 2 + [ANYWHERE] + [INSIDE] * (len(payloads) + len(blocks)),
         out_specs=INSIDE,
         out_shape=jax.ShapeDtypeStruct((rows, width + LANES), jnp.bfloat16),
         scratch_shapes=[
-            pltpu.VMEM(payloads[0].shape, jnp.bfloat16),
+            pltpu.VMEM((payloads[0].shape[0] - tokens, columns), jnp.bfloat16),
             pltpu.VMEM((rows, width), jnp.float32),
         ],
         compiler_params=pltpu.CompilerParams(vmem_limit_bytes=16 << 20),
         name="token_rows",
-    )(place, slot_utt, *payloads, *blocks)
+    )(place, slot_utt, after, *payloads, *blocks)
+
+
+def load_kernel(rows, after_ref, head_ref, out_ref, token_ref, semaphores):
+    count = head_ref.shape[0] // rows
+    copies = start_copies(
+        lambda i: head_ref.at[pl.ds(i * rows, rows), :],
+        lambda i: out_ref.at[pl.ds(i * rows, rows), :],
+        semaphores,
+        count,
+    )
+    token_ref[...] = jnp.zeros_like(token_ref)
+    for copy in copies:
+        copy.wait()
+
+
+def load_head(after, head):
+    rows = head.shape[0] // 5
+    return pl.pallas_call(
+        functools.partial(load_kernel, rows),
+        in_specs=[ANYWHERE, ANYWHERE],
+        out_specs=[INSIDE, INSIDE],
+        out_shape=[
+            pltpu.VMEM(head.shape, head.dtype),
+            jax.ShapeDtypeStruct((8, LANES), jnp.float32),
+        ],
+        scratch_shapes=[pltpu.SemaphoreType.DMA((5,))],
+        cost_estimate=pl.CostEstimate(
+            flops=0, bytes_accessed=2 * head.size, transcendentals=0
+        ),
+        compiler_params=pltpu.CompilerParams(vmem_limit_bytes=20 << 20),
+        name="vocabulary_rows",
+    )(after, in_hbm(head))
 
 
 def vocabulary_kernel(tile, first_ref, *refs):
@@ -599,24 +636,24 @@
         place,
         slot_utt,
         lengths,
+        parts[1],
         hyp_state.reshape(slot_count, slot_tokens, model_width),
         hyp_tok.reshape(slot_count, 1, slot_tokens),
         q_proj,
         group_count,
         share_rows,
     )
-    payloads = [blocks[0]] + [
-        swap(blocks[distance], "tm", distance) for distance in range(1, group_count)
-    ]
-    shares = blocks[group_count:]
-
-    sent = keys_values_of(parts, own_frames, kv_proj, section_count, utterances, width_count)
+    beside = group_pos ^ 1
+    beside_slots = lax.dynamic_slice_in_dim(slot_utt, beside * slot_count, slot_count, 0)
+    beside_has = jnp.any(beside_slots == group_pos ^ 2)
+    crossing = jnp.where(beside_has, swap(blocks[3], "tm", 1), blocks[2])
+    payloads = [blocks[0], swap(blocks[1], "tm", 1), swap(crossing, "tm", 2)]
+
+    sent = keys_values_of(
+        parts, own_frames, kv_proj, blocks[0], section_count, utterances, width_count
+    )
     frames_all = all_devices * (frame_rows // width_count)
     keys_values = exchange(sent.reshape(all_devices, -1, 2 * HD), ALL).reshape(frames_all, 2 * HD)
-    keys_values, *shares = lax.optimization_barrier((keys_values, *shares))
-    shares = [shares[0]] + [
-        swap(shares[distance], "tm", distance) for distance in range(1, group_count)
-    ]
 
     pieces = (share_rows // 2, share_rows - share_rows // 2)
     projected = attend(
@@ -629,19 +666,27 @@
         pieces,
         section_count,
         width_count,
-    )
+        slot_count,
+    )
+    others = [swap(projected[number], "section", 1) for number in range(len(pieces))]
+    head, token = load_head(projected[len(pieces)], head)
     sums = []
     for number, piece in enumerate(pieces):
-        other = swap(projected[number], "section", 1)
-        section_sum = (
-            projected[len(pieces) + number].astype(jnp.float32) + other.astype(jnp.float32)
-        ).astype(jnp.bfloat16)
-        for distance in range(width_count):
-            block = lax.dynamic_slice_in_dim(
-                section_sum, (width_pos ^ distance) * piece, piece, 0
-            )
-            sums.append(swap(block, "mp", distance) if distance else block)
-    out_rows = normed_rows(place, slot_utt, shares, sums, pieces, width_count)
+        total = projected[len(pieces) + number].astype(jnp.float32) + others[number].astype(
+            jnp.float32
+        )
+        for distance in (1, 2):
+            half = total.shape[0] // 2
+            side = width_pos // distance % 2
+            kept = lax.dynamic_slice_in_dim(total, side * half, half, 0)
+            sent = lax.dynamic_slice_in_dim(total, (1 - side) * half, half, 0)
+            came = swap(sent.astype(jnp.bfloat16), "mp", distance)
+            if distance == 1:
+                total = kept + came.astype(jnp.float32)
+        sums += [kept, came]
+    out_rows = normed_rows(
+        place, slot_utt, token, payloads, sums, pieces, slot_tokens, slot_count
+    )
 
     share = out_rows.shape[0]
     own = jnp.zeros((width_count * share, out_rows.shape[1]), jnp.bfloat16)
@@ -651,12 +696,15 @@
     half = own.shape[0] // 2
     by_x = swap(own, "section", 1)
     by_y = swap(own, "tm", 2)
-    across = jnp.concatenate([swap(by_x[:half], "tm", 2), swap(by_y[half:], "section", 1)])
-    stats = [
-        vocabulary_stats(place, [own, swap(own, "tm", 1)], head),
-        vocabulary_stats(place, [by_y, swap(by_y, "tm", 1), by_x, swap(by_x, "tm", 1)], head),
-        vocabulary_stats(place, [across, swap(across, "tm", 1)], head),
-    ]
+    stats = [vocabulary_stats(place, [own, swap(own, "tm", 1)], head)]
+    by_x, by_y, stats[0] = lax.optimization_barrier((by_x, by_y, stats[0]))
+    across = [swap(by_x[:half], "tm", 2), swap(by_y[half:], "section", 1)]
+    stats.append(
+        vocabulary_stats(place, [by_y, swap(by_y, "tm", 1), by_x, swap(by_x, "tm", 1)], head)
+    )
+    *across, stats[1] = lax.optimization_barrier((*across, stats[1]))
+    across = jnp.concatenate(across)
+    stats.append(vocabulary_stats(place, [across, swap(across, "tm", 1)], head))
 
     every = exchange(
         spread_stats(place, slot_utt, stats, section_count, group_count, width_count), ALL

time: 140 us -> 136 us (0.971)
  starting transfers between devices: 37.7 us -> 23.4 us
  blocking collectives: 13.8 us -> 27.5 us
  waiting for transfers between devices: 45.5 us -> 35.1 us
  Pallas kernels: 35.4 us -> 42.5 us
  local copies, waits for them, and re-layouts: 7.25 us -> 5.37 us
  other arithmetic: 0.13 us -> 1.56 us
    all_to_all x1 -> x2, blocking collectives: 13.8 us -> 27.5 us  [exchange(): return lax.all_to_all(blocks, axis, split_axis=0, concat_axis=0, tiled=True)]
    ppermute x28 -> x23, starting transfers between devices: 33 us -> 23.4 us  [swap(): return lax.ppermute(values, axis, pairs)]
    ppermute x28 -> x23, waiting for transfers between devices: 44.5 us -> 35.1 us  [swap(): return lax.ppermute(values, axis, pairs)]
    pallas_call x2 -> x3, Pallas kernels: 4.04 us -> 9.77 us  [the longest x1 5.77 us: load_head(): pl.pallas_call(functools.partial(load_kernel, rows), in_specs=[ANYWHERE,...]
    all_to_all x1 -> x0, starting transfers between devices: 4.72 us -> none  [exchange(): return lax.all_to_all(blocks, axis, split_axis=0, concat_axis=0, tiled=True)]
    unnamed x15 -> x21, local copies, waits for them, and re-layouts: 5.71 us -> 3.74 us
  transfers between devices with their start and end apart: 29 -> 23, of which waited for: 12 -> 16; matrix products, arithmetic and copies ran while one was open for 0% -> 1% of each run, Pallas kernels for 12% -> 14%
where the time goes in v5:
time: 136 us
  Pallas kernels  42.5 us (31%)
  waiting for transfers between devices  35.1 us (26%)
  blocking collectives  27.5 us (20%)
  starting transfers between devices  23.4 us (17%)
  local copies, waits for them, and re-layouts  5.37 us (4%)
  other arithmetic  1.56 us (1%)
    ppermute x23, waiting for transfers between devices, swap(): return lax.ppermute(values, axis, pairs)  35.1 us
    all_to_all x2, blocking collectives, exchange(): return lax.all_to_all(blocks, axis, split_axis=0, concat_axis=0, tiled=True)  27.5 us
    ppermute x23, starting transfers between devices, swap(): return lax.ppermute(values, axis, pairs)  23.4 us
    pallas_call x3, Pallas kernels, vocabulary_stats(): pl.pallas_call(functools.partial(vocabulary_kernel, head.shape[0] // 2),...  17.5 us
    pallas_call x1, Pallas kernels, queries_of(): pl.pallas_call(functools.partial(query_kernel, count, depth), in_specs=[S...  5.89 us
    pallas_call x1, Pallas kernels, load_head(): pl.pallas_call(functools.partial(load_kernel, rows), in_specs=[ANYWHERE,...  5.77 us
    pallas_call x1, Pallas kernels, ffn(): pl.pallas_call(functools.partial(ffn_kernel, count, tile), in_specs=[SCAL...  5.57 us
    unnamed x21, local copies, waits for them, and re-layouts  3.74 us
  transfers between devices with their start and end apart: 23, of which 16 were waited for; matrix products, arithmetic and copies ran while one was open for 1% of the time, Pallas kernels for 14%

profile of v5, /device:TPU:0, one launch (start us, length us, event | category | flops | bytes accessed | tf_op | source)
XLA Modules:
  0.0 135.5 jit_solution(9985245591805603495)
XLA Ops:
  0.0 1.1 reshape.19.x_ref
  1.1 0.1 stack.23.place_ref.refs_0_.first_ref
  1.2 5.6 %encoder_ffn.1 = (bf16[32,1280]{1,0:T(8,128)(2,1)S(1)}, bf16[32,1280]{1,0:T(8,128)(2,1)S(1)}, bf16[32,1280]{1,0:T(8,128)(2,1)}, bf16[32,1280]{1,0:T(8,128)(2,1)}, bf16[32,1280]{1,0:T(8,128)(2,1)S(1)}) custom-call(s32[5]{0:T(128)S(1)} %stack.23.place_ref.refs_0_.first_ref, bf16[128,1280]{1,0:T(8,128)(2,1)S(1)} %reshape.19.x_ref, bf16[1280,1280]{1,0:T(8,128)(2,1)} %up_ref.1, ...), custom_call_target="tpu_custom_call" | custom-call | flops 838860800 | bytes 6553600 | tf_op jit(solution)/shard_map/encoder_ffn/pallas_call | solution.py:113
  6.8 0.6 copy-done.1
  7.4 0.6 copy-done.3
  8.0 3.0 %collective-permute-start = (bf16[32,1280]{1,0:T(8,128)(2,1)S(1)}, bf16[32,1280]{1,0:T(8,128)(2,1)S(1)}, u32[]{:S(2)}, u32[]{:S(2)}) collective-permute-start(bf16[32,1280]{1,0:T(8,128)(2,1)S(1)} %get-tuple-element.26), channel_id=1, source_target_pairs={{0,1},{1,0},{2,3},{3,2},{4,5},{5,4},{6,7},{7,6},{8,9},{9,8},{10,11... | collective-permute-start | bytes 245768 | tf_op jit(solution)/shard_map/ppermute | solution.py:40
  11.1 0.1 reshape.18.length_ref
  11.1 0.1 reshape.21.tok_ref
  11.2 2.3 %collective-permute-done.after_ref.refs_1_ = bf16[32,1280]{1,0:T(8,128)(2,1)S(1)} collective-permute-done((bf16[32,1280]{1,0:T(8,128)(2,1)S(1)}, bf16[32,1280]{1,0:T(8,128)(2,1)S(1)}, u32[]{:S(2)}, u32[]{:S(2)}) %collective-permute-start) | collective-permute-done | bytes 81952 | tf_op jit(solution)/shard_map/ppermute | solution.py:40
  13.5 5.9 %hypothesis_queries.1 = (bf16[272,512]{1,0:T(8,128)(2,1)S(1)}, bf16[272,512]{1,0:T(8,128)(2,1)S(1)}, bf16[272,512]{1,0:T(8,128)(2,1)S(1)}, bf16[272,512]{1,0:T(8,128)(2,1)}) custom-call(s32[5]{0:T(128)S(1)} %stack.23.place_ref.refs_0_.first_ref, s32[8]{0:T(128)S(1)} %copy-done.5, s32[16]{0:T(128)S(1)} %reshape.18.length_ref, ...), custom_call_target="tpu_custom_call" | custom-call | flops 1073741824 | bytes 6291456 | tf_op jit(solution)/shard_map/hypothesis_queries/pallas_call | solution.py:208
  19.4 0.7 copy-done.7
  20.1 0.0 collective-permute-start.2
  20.1 3.0 %collective-permute-start.4 = (bf16[32,1280]{1,0:T(8,128)(2,1)}, bf16[32,1280]{1,0:T(8,128)(2,1)}, u32[]{:S(2)}, u32[]{:S(2)}) collective-permute-start(bf16[32,1280]{1,0:T(8,128)(2,1)} %get-tuple-element.32), channel_id=1, source_target_pairs={{0,2},{1,3},{2,0},{3,1},{4,6},{5,7},{6,4},{7,5},{8,10},{9,11},{10,... | collective-permute-start | bytes 245768 | tf_op jit(solution)/shard_map/ppermute | solution.py:40
  23.1 1.4 %collective-permute-start.5 = (bf16[32,1280]{1,0:T(8,128)(2,1)}, bf16[32,1280]{1,0:T(8,128)(2,1)}, u32[]{:S(2)}, u32[]{:S(2)}) collective-permute-start(bf16[32,1280]{1,0:T(8,128)(2,1)} %get-tuple-element.33), channel_id=1, source_target_pairs={{0,3},{1,2},{2,1},{3,0},{4,7},{5,6},{6,5},{7,4},{8,11},{9,10},{10,... | collective-permute-start | bytes 245768 | tf_op jit(solution)/shard_map/ppermute | solution.py:40
  24.5 0.7 compare_reduce_fusion
  25.2 0.7 broadcast_select_fusion
  25.9 2.5 %collective-permute-start.3 = (bf16[272,512]{1,0:T(8,128)(2,1)S(1)}, bf16[272,512]{1,0:T(8,128)(2,1)S(1)}, u32[]{:S(2)}, u32[]{:S(2)}) collective-permute-start(bf16[272,512]{1,0:T(8,128)(2,1)S(1)} %broadcast_select_fusion), channel_id=1, source_target_pairs={{0,8},{4,12},{8,0},{12,4},{1,9},{5,13},{9,1},{13,5},{2,10},{6,14},... | collective-permute-start | bytes 835592 | tf_op jit(solution)/shard_map/ppermute | solution.py:40
  28.4 1.8 %collective-permute-done.4.refs_2_ = bf16[32,1280]{1,0:T(8,128)(2,1)} collective-permute-done((bf16[32,1280]{1,0:T(8,128)(2,1)}, bf16[32,1280]{1,0:T(8,128)(2,1)}, u32[]{:S(2)}, u32[]{:S(2)}) %collective-permute-start.4) | collective-permute-done | bytes 81952 | tf_op jit(solution)/shard_map/ppermute | solution.py:40
  30.2 0.9 copy-done.2
  31.1 0.9 copy-done.4
  32.0 1.8 %frame_keys_values.1 = bf16[256,256]{1,0:T(8,128)(2,1)S(1)} custom-call(bf16[32,1280]{1,0:T(8,128)(2,1)S(1)} %copy-done.2, bf16[32,1280]{1,0:T(8,128)(2,1)S(1)} %collective-permute-done.after_ref.refs_1_, bf16[32,1280]{1,0:T(8,128)(2,1)} %collective-permute-done.4.refs_2_, bf16[32,1280]{1,0:T(8,128)(2,1)} %collective-permute-done.5.refs_3_, ...), custom_call_target="tpu_custom_call" | custom-call | flops 83886080 | bytes 2621440 | tf_op jit(solution)/shard_map/frame_keys_values/pallas_call | solution.py:267
  33.8 14.7 %all_to_all.10 = bf16[32,8,256]{2,1,0:T(8,128)(2,1)S(1)} all-to-all(bf16[32,8,256]{2,1,0:T(8,128)(2,1)S(1)} %bitcast.9), channel_id=1, replica_groups=mesh['section'=2,'tm'=4,'mp'=4] {'section','tm','mp'}, dimensions={0} | all-to-all | bytes 262144 | tf_op jit(solution)/shard_map/all_to_all | solution.py:30
  48.5 3.1 %attention_projection.1 = (bf16[32,4096]{1,0:T(8,128)(2,1)S(1)}, bf16[32,4096]{1,0:T(8,128)(2,1)S(1)}, bf16[32,4096]{1,0:T(8,128)(2,1)S(1)}, bf16[32,4096]{1,0:T(8,128)(2,1)S(1)}) custom-call(s32[5]{0:T(128)S(1)} %stack.23.place_ref.refs_0_.first_ref, s32[8]{0:T(128)S(1)} %copy-done.5, s32[4]{0:T(128)S(1)} %copy-done.6, ...), custom_call_target="tpu_custom_call" | custom-call | flops 603979776 | bytes 5242880 | tf_op jit(solution)/shard_map/attention_projection/pallas_call | solution.py:354
  51.6 0.9 collective-permute-start.9
  52.5 1.2 collective-permute-start.6
  53.7 5.8 %vocabulary_rows.1 = (bf16[2000,4096]{1,0:T(8,128)(2,1)S(1)}, f32[8,128]{1,0:T(8,128)S(1)}) custom-call(bf16[32,4096]{1,0:T(8,128)(2,1)S(1)} %get-tuple-element.35.after_ref, bf16[2000,4096]{1,0:T(8,128)(2,1)} %head_ref.1), custom_call_target="tpu_custom_call" | custom-call | bytes 16384000 | tf_op jit(solution)/shard_map/vocabulary_rows/pallas_call | solution.py:436
  59.5 1.4 %collective-permute-done.9 = bf16[32,4096]{1,0:T(8,128)(2,1)S(1)} collective-permute-done((bf16[32,4096]{1,0:T(8,128)(2,1)S(1)}, bf16[32,4096]{1,0:T(8,128)(2,1)S(1)}, u32[]{:S(2)}, u32[]{:S(2)}) %collective-permute-start.9) | collective-permute-done | bytes 262176 | tf_op jit(solution)/shard_map/ppermute | solution.py:40
  60.9 0.1 convert_add_fusion
  61.0 0.1 collective-permute-start.10
  61.1 3.6 %collective-permute-done.6 = bf16[32,4096]{1,0:T(8,128)(2,1)S(1)} collective-permute-done((bf16[32,4096]{1,0:T(8,128)(2,1)S(1)}, bf16[32,4096]{1,0:T(8,128)(2,1)S(1)}, u32[]{:S(2)}, u32[]{:S(2)}) %collective-permute-start.6) | collective-permute-done | bytes 262176 | tf_op jit(solution)/shard_map/ppermute | solution.py:40
  64.7 0.1 convert_add_fusion.1
  64.8 1.2 collective-permute-start.7
  66.0 0.1 collective-permute-done.10
  66.1 0.8 collective-permute-start.11
  67.0 3.4 %collective-permute-done.7 = bf16[16,4096]{1,0:T(8,128)(2,1)S(1)} collective-permute-done((bf16[16,4096]{1,0:T(8,128)(2,1)S(1)}, bf16[16,4096]{1,0:T(8,128)(2,1)S(1)}, u32[]{:S(2)}, u32[]{:S(2)}) %collective-permute-start.7) | collective-permute-done | bytes 131104 | tf_op jit(solution)/shard_map/ppermute | solution.py:40
  70.4 1.4 %collective-permute-start.8 = (bf16[8,4096]{1,0:T(8,128)(2,1)S(1)}, bf16[8,4096]{1,0:T(8,128)(2,1)S(1)}, u32[]{:S(2)}, u32[]{:S(2)}) collective-permute-start(bf16[8,4096]{1,0:T(8,128)(2,1)S(1)} %dynamic-slice_convert_fusion.3), channel_id=1, source_target_pairs={{0,2},{1,3},{2,0},{3,1},{4,6},{5,7},{6,4},{7,5},{8,10},{9,11},{10,... | collective-permute-start | bytes 196616 | tf_op jit(solution)/shard_map/ppermute | solution.py:40
  71.8 0.3 collective-permute-done.11.refs_6_
  72.1 3.5 %collective-permute-done.8.refs_4_ = bf16[8,4096]{1,0:T(8,128)(2,1)S(1)} collective-permute-done((bf16[8,4096]{1,0:T(8,128)(2,1)S(1)}, bf16[8,4096]{1,0:T(8,128)(2,1)S(1)}, u32[]{:S(2)}, u32[]{:S(2)}) %collective-permute-start.8) | collective-permute-done | bytes 65568 | tf_op jit(solution)/shard_map/ppermute | solution.py:40
  75.6 0.9 token_rows.1
  76.5 1.8 %collective-permute-start.12 = (bf16[16,4224]{1,0:T(8,128)(2,1)S(1)}, bf16[16,4224]{1,0:T(8,128)(2,1)S(1)}, u32[]{:S(2)}, u32[]{:S(2)}) collective-permute-start(bf16[16,4224]{1,0:T(8,128)(2,1)S(1)} %token_rows.1), channel_id=1, source_target_pairs={{0,1},{1,0},{2,3},{3,2},{4,5},{5,4},{6,7},{7,6},{8,9},{9,8},{10,11... | collective-permute-start | bytes 405512 | tf_op jit(solution)/shard_map/ppermute | solution.py:40
  78.4 0.4 collective-permute-start.13
  78.8 2.2 %collective-permute-start.14 = (bf16[16,4224]{1,0:T(8,128)(2,1)S(1)}, bf16[16,4224]{1,0:T(8,128)(2,1)S(1)}, u32[]{:S(2)}, u32[]{:S(2)}) collective-permute-start(bf16[16,4224]{1,0:T(8,128)(2,1)S(1)} %token_rows.1), channel_id=1, source_target_pairs={{0,3},{1,2},{2,1},{3,0},{4,7},{5,6},{6,5},{7,4},{8,11},{9,10},{10,... | collective-permute-start | bytes 405512 | tf_op jit(solution)/shard_map/ppermute | solution.py:40
  81.0 3.3 %collective-permute-done.12 = bf16[16,4224]{1,0:T(8,128)(2,1)S(1)} collective-permute-done((bf16[16,4224]{1,0:T(8,128)(2,1)S(1)}, bf16[16,4224]{1,0:T(8,128)(2,1)S(1)}, u32[]{:S(2)}, u32[]{:S(2)}) %collective-permute-start.12) | collective-permute-done | bytes 135200 | tf_op jit(solution)/shard_map/ppermute | solution.py:40
  84.4 4.6 %collective-permute-done.13 = bf16[16,4224]{1,0:T(8,128)(2,1)S(1)} collective-permute-done((bf16[16,4224]{1,0:T(8,128)(2,1)S(1)}, bf16[16,4224]{1,0:T(8,128)(2,1)S(1)}, u32[]{:S(2)}, u32[]{:S(2)}) %collective-permute-start.13) | collective-permute-done | bytes 135200 | tf_op jit(solution)/shard_map/ppermute | solution.py:40
  89.0 0.1 collective-permute-start.17
  89.1 0.5 collective-permute-start.15
  89.6 0.1 collective-permute-start.16
  89.7 1.4 %collective-permute-done.17.refs_1_ = bf16[64,4224]{1,0:T(8,128)(2,1)S(1)} collective-permute-done((bf16[64,4224]{1,0:T(8,128)(2,1)S(1)}, bf16[64,4224]{1,0:T(8,128)(2,1)S(1)}, u32[]{:S(2)}, u32[]{:S(2)}) %collective-permute-start.17) | collective-permute-done | bytes 540704 | tf_op jit(solution)/shard_map/ppermute | solution.py:40
  91.0 5.7 %vocabulary_scores.3.refs_0_ = f32[2,8,64]{2,1,0:T(8,128)S(1)} custom-call(s32[5]{0:T(128)S(1)} %stack.23.place_ref.refs_0_.first_ref, bf16[64,4224]{1,0:T(8,128)(2,1)S(1)} %constant_dynamic-update-slice_fusion.2.refs_0_, bf16[64,4224]{1,0:T(8,128)(2,1)S(1)} %collective-permute-done.17.refs_1_, bf16[2000,4096]{1,0:T(8,128)(2,1)S(1)} %get-tuple-element.40.refs_2_.refs_4_), custom_call_target="tpu_custom_call" | custom-call | flops 3145728000 | bytes 1048576 | tf_op jit(solution)/shard_map/vocabulary_scores/pallas_call | solution.py:492
  96.8 7.0 %collective-permute-done.15.refs_2_ = bf16[64,4224]{1,0:T(8,128)(2,1)S(1)} collective-permute-done((bf16[64,4224]{1,0:T(8,128)(2,1)S(1)}, bf16[64,4224]{1,0:T(8,128)(2,1)S(1)}, u32[]{:S(2)}, u32[]{:S(2)}) %collective-permute-start.15) | collective-permute-done | bytes 540704 | tf_op jit(solution)/shard_map/ppermute | solution.py:40
  103.8 0.1 collective-permute-done.16.refs_0_
  103.9 0.5 collective-permute-start.21
  104.5 0.4 collective-permute-start.18
  104.8 1.7 %collective-permute-start.19 = (bf16[32,4224]{1,0:T(8,128)(2,1)S(1)}, bf16[32,4224]{1,0:T(8,128)(2,1)S(1)}, u32[]{:S(2)}, u32[]{:S(2)}) collective-permute-start(bf16[32,4224]{1,0:T(8,128)(2,1)S(1)} %slice.7), channel_id=1, source_target_pairs={{0,16},{16,0},{1,17},{17,1},{2,18},{18,2},{3,19},{19,3},{4,20},{20... | collective-permute-start | bytes 811016 | tf_op jit(solution)/shard_map/ppermute | solution.py:40
  106.6 0.0 collective-permute-done.21.refs_3_
  106.6 6.0 %vocabulary_scores.4.refs_1_ = f32[4,8,64]{2,1,0:T(8,128)S(1)} custom-call(s32[5]{0:T(128)S(1)} %stack.23.place_ref.refs_0_.first_ref, bf16[64,4224]{1,0:T(8,128)(2,1)S(1)} %collective-permute-done.16.refs_0_, bf16[64,4224]{1,0:T(8,128)(2,1)S(1)} %collective-permute-done.20.refs_1_, bf16[64,4224]{1,0:T(8,128)(2,1)S(1)} %collective-permute-done.15.refs_2_, ...), custom_call_target="tpu_custom_call" | custom-call | flops 6291456000 | bytes 2097152 | tf_op jit(solution)/shard_map/vocabulary_scores/pallas_call | solution.py:492
  112.7 0.3 collective-permute-done.18
  112.9 0.1 collective-permute-done.19
  113.1 0.1 collective-permute-start.22
  113.1 1.9 %collective-permute-done.22.refs_1_ = bf16[64,4224]{1,0:T(8,128)(2,1)S(1)} collective-permute-done((bf16[64,4224]{1,0:T(8,128)(2,1)S(1)}, bf16[64,4224]{1,0:T(8,128)(2,1)S(1)}, u32[]{:S(2)}, u32[]{:S(2)}) %collective-permute-start.22) | collective-permute-done | bytes 540704 | tf_op jit(solution)/shard_map/ppermute | solution.py:40
  115.1 5.7 %vocabulary_scores.5.refs_2_ = f32[2,8,64]{2,1,0:T(8,128)S(1)} custom-call(s32[5]{0:T(128)S(1)} %stack.23.place_ref.refs_0_.first_ref, bf16[64,4224]{1,0:T(8,128)(2,1)S(1)} %constant_dynamic-update-slice_fusion.refs_0_, bf16[64,4224]{1,0:T(8,128)(2,1)S(1)} %collective-permute-done.22.refs_1_, bf16[2000,4096]{1,0:T(8,128)(2,1)S(1)} %get-tuple-element.40.refs_2_.refs_4_), custom_call_target="tpu_custom_call" | custom-call | flops 3145728000 | bytes 1048576 | tf_op jit(solution)/shard_map/vocabulary_scores/pallas_call | solution.py:492
  120.8 0.6 statistics_by_group.1
  121.4 12.8 %all_to_all.11.every_ref = f32[32,8,128]{2,1,0:T(8,128)S(1)} all-to-all(f32[32,8,128]{2,1,0:T(8,128)S(1)} %statistics_by_group.1), channel_id=1, replica_groups=mesh['section'=2,'tm'=4,'mp'=4] {'section','tm','mp'}, dimensions={0} | all-to-all | bytes 262144 | tf_op jit(solution)/shard_map/all_to_all | solution.py:30
  134.2 1.3 hypothesis_scores.1
  (40 shorter events, 0.4 us)
Async XLA Ops:
  0.0 11.1 %copy-start.9 = (s32[2,8]{1,0:T(2,128)S(1)}, s32[2,8]{1,0:T(2,128)}, u32[]{:S(2)}) copy-start(s32[2,8]{1,0:T(2,128)} %param.20) | copy-start | bytes 196
  0.0 11.1 %copy-start.8 = (s32[2,8,16]{2,1,0:T(8,128)S(1)}, s32[2,8,16]{2,1,0:T(8,128)}, u32[]{:S(2)}) copy-start(s32[2,8,16]{2,1,0:T(8,128)} %param.19) | copy-start | bytes 3076
  0.0 13.5 %copy-start.5 = (s32[8]{0:T(128)S(1)}, s32[8]{0:T(128)}, u32[]{:S(2)}) copy-start(s32[8]{0:T(128)} %slot_ref.7) | copy-start | bytes 100
  6.8 0.6 copy-start.1
  7.4 0.6 copy-start.3
  8.0 22.2 %copy-start = (bf16[1280,1024]{1,0:T(8,128)(2,1)S(1)}, bf16[1280,1024]{1,0:T(8,128)(2,1)}, u32[]{:S(2)}) copy-start(bf16[1280,1024]{1,0:T(8,128)(2,1)} %refs_5_.1) | copy-start | bytes 7864324
  8.0 5.5 %collective-permute-start = (bf16[32,1280]{1,0:T(8,128)(2,1)S(1)}, bf16[32,1280]{1,0:T(8,128)(2,1)S(1)}, u32[]{:S(2)}, u32[]{:S(2)}) collective-permute-start(bf16[32,1280]{1,0:T(8,128)(2,1)S(1)} %get-tuple-element.26), channel_id=1, source_target_pairs={{0,1},{1,0},{2,3},{3,2},{4,5},{5,4},{6,7},{7,6},{8,9},{9,8},{10,11... | collective-permute-start | bytes 245768 | tf_op jit(solution)/shard_map/ppermute | solution.py:40
  13.5 35.0 %copy-start.6 = (s32[4]{0:T(128)S(1)}, s32[4]{0:T(128)}, u32[]{:S(2)}) copy-start(s32[4]{0:T(128)} %refs_2_.1) | copy-start | bytes 52
  19.4 0.7 copy-start.7
  20.1 5.1 %collective-permute-start.2 = (bf16[272,512]{1,0:T(8,128)(2,1)}, bf16[272,512]{1,0:T(8,128)(2,1)}, u32[]{:S(2)}, u32[]{:S(2)}) collective-permute-start(bf16[272,512]{1,0:T(8,128)(2,1)} %get-tuple-element.29), channel_id=1, source_target_pairs={{0,4},{4,0},{8,12},{12,8},{1,5},{5,1},{9,13},{13,9},{2,6},{6,2},{1... | collective-permute-start | bytes 835592 | tf_op jit(solution)/shard_map/ppermute | solution.py:40
  20.1 10.1 %collective-permute-start.4 = (bf16[32,1280]{1,0:T(8,128)(2,1)}, bf16[32,1280]{1,0:T(8,128)(2,1)}, u32[]{:S(2)}, u32[]{:S(2)}) collective-permute-start(bf16[32,1280]{1,0:T(8,128)(2,1)} %get-tuple-element.32), channel_id=1, source_target_pairs={{0,2},{1,3},{2,0},{3,1},{4,6},{5,7},{6,4},{7,5},{8,10},{9,11},{10,... | collective-permute-start | bytes 245768 | tf_op jit(solution)/shard_map/ppermute | solution.py:40
  23.1 7.1 %collective-permute-start.5 = (bf16[32,1280]{1,0:T(8,128)(2,1)}, bf16[32,1280]{1,0:T(8,128)(2,1)}, u32[]{:S(2)}, u32[]{:S(2)}) collective-permute-start(bf16[32,1280]{1,0:T(8,128)(2,1)} %get-tuple-element.33), channel_id=1, source_target_pairs={{0,3},{1,2},{2,1},{3,0},{4,7},{5,6},{6,5},{7,4},{8,11},{9,10},{10,... | collective-permute-start | bytes 245768 | tf_op jit(solution)/shard_map/ppermute | solution.py:40
  25.2 23.3 %collective-permute-start.1 = (bf16[272,512]{1,0:T(8,128)(2,1)}, bf16[272,512]{1,0:T(8,128)(2,1)S(1)}, u32[]{:S(2)}, u32[]{:S(2)}) collective-permute-start(bf16[272,512]{1,0:T(8,128)(2,1)} %copy-done.7), channel_id=1, source_target_pairs={{0,4},{4,0},{8,12},{12,8},{1,5},{5,1},{9,13},{13,9},{2,6},{6,2},{1... | collective-permute-start | bytes 835592 | tf_op jit(solution)/shard_map/ppermute | solution.py:40
  25.9 22.6 %collective-permute-start.3 = (bf16[272,512]{1,0:T(8,128)(2,1)S(1)}, bf16[272,512]{1,0:T(8,128)(2,1)S(1)}, u32[]{:S(2)}, u32[]{:S(2)}) collective-permute-start(bf16[272,512]{1,0:T(8,128)(2,1)S(1)} %broadcast_select_fusion), channel_id=1, source_target_pairs={{0,8},{4,12},{8,0},{12,4},{1,9},{5,13},{9,1},{13,5},{2,10},{6,14},... | collective-permute-start | bytes 835592 | tf_op jit(solution)/shard_map/ppermute | solution.py:40
  30.2 0.9 copy-start.2
  31.1 0.9 copy-start.4
  51.6 9.3 %collective-permute-start.9 = (bf16[32,4096]{1,0:T(8,128)(2,1)S(1)}, bf16[32,4096]{1,0:T(8,128)(2,1)S(1)}, u32[]{:S(2)}, u32[]{:S(2)}) collective-permute-start(bf16[32,4096]{1,0:T(8,128)(2,1)S(1)} %get-tuple-element.39), channel_id=1, source_target_pairs={{0,16},{16,0},{1,17},{17,1},{2,18},{18,2},{3,19},{19,3},{4,20},{20... | collective-permute-start | bytes 786440 | tf_op jit(solution)/shard_map/ppermute | solution.py:40
  52.5 12.2 %collective-permute-start.6 = (bf16[32,4096]{1,0:T(8,128)(2,1)S(1)}, bf16[32,4096]{1,0:T(8,128)(2,1)S(1)}, u32[]{:S(2)}, u32[]{:S(2)}) collective-permute-start(bf16[32,4096]{1,0:T(8,128)(2,1)S(1)} %get-tuple-element.37), channel_id=1, source_target_pairs={{0,16},{16,0},{1,17},{17,1},{2,18},{18,2},{3,19},{19,3},{4,20},{20... | collective-permute-start | bytes 786440 | tf_op jit(solution)/shard_map/ppermute | solution.py:40
  61.0 5.0 %collective-permute-start.10 = (bf16[16,4096]{1,0:T(8,128)(2,1)S(1)}, bf16[16,4096]{1,0:T(8,128)(2,1)S(1)}, u32[]{:S(2)}, u32[]{:S(2)}) collective-permute-start(bf16[16,4096]{1,0:T(8,128)(2,1)S(1)} %dynamic-slice_convert_fusion), channel_id=1, source_target_pairs={{0,1},{1,0},{2,3},{3,2},{4,5},{5,4},{6,7},{7,6},{8,9},{9,8},{10,11... | collective-permute-start | bytes 393224 | tf_op jit(solution)/shard_map/ppermute | solution.py:40
  64.8 5.5 %collective-permute-start.7 = (bf16[16,4096]{1,0:T(8,128)(2,1)S(1)}, bf16[16,4096]{1,0:T(8,128)(2,1)S(1)}, u32[]{:S(2)}, u32[]{:S(2)}) collective-permute-start(bf16[16,4096]{1,0:T(8,128)(2,1)S(1)} %dynamic-slice_convert_fusion.1), channel_id=1, source_target_pairs={{0,1},{1,0},{2,3},{3,2},{4,5},{5,4},{6,7},{7,6},{8,9},{9,8},{10,11... | collective-permute-start | bytes 393224 | tf_op jit(solution)/shard_map/ppermute | solution.py:40
  66.1 6.0 %collective-permute-start.11 = (bf16[8,4096]{1,0:T(8,128)(2,1)S(1)}, bf16[8,4096]{1,0:T(8,128)(2,1)S(1)}, u32[]{:S(2)}, u32[]{:S(2)}) collective-permute-start(bf16[8,4096]{1,0:T(8,128)(2,1)S(1)} %dynamic-slice_convert_fusion.2), channel_id=1, source_target_pairs={{0,2},{1,3},{2,0},{3,1},{4,6},{5,7},{6,4},{7,5},{8,10},{9,11},{10,... | collective-permute-start | bytes 196616 | tf_op jit(solution)/shard_map/ppermute | solution.py:40
  70.4 5.2 %collective-permute-start.8 = (bf16[8,4096]{1,0:T(8,128)(2,1)S(1)}, bf16[8,4096]{1,0:T(8,128)(2,1)S(1)}, u32[]{:S(2)}, u32[]{:S(2)}) collective-permute-start(bf16[8,4096]{1,0:T(8,128)(2,1)S(1)} %dynamic-slice_convert_fusion.3), channel_id=1, source_target_pairs={{0,2},{1,3},{2,0},{3,1},{4,6},{5,7},{6,4},{7,5},{8,10},{9,11},{10,... | collective-permute-start | bytes 196616 | tf_op jit(solution)/shard_map/ppermute | solution.py:40
  76.5 7.9 %collective-permute-start.12 = (bf16[16,4224]{1,0:T(8,128)(2,1)S(1)}, bf16[16,4224]{1,0:T(8,128)(2,1)S(1)}, u32[]{:S(2)}, u32[]{:S(2)}) collective-permute-start(bf16[16,4224]{1,0:T(8,128)(2,1)S(1)} %token_rows.1), channel_id=1, source_target_pairs={{0,1},{1,0},{2,3},{3,2},{4,5},{5,4},{6,7},{7,6},{8,9},{9,8},{10,11... | collective-permute-start | bytes 405512 | tf_op jit(solution)/shard_map/ppermute | solution.py:40
  78.4 10.6 %collective-permute-start.13 = (bf16[16,4224]{1,0:T(8,128)(2,1)S(1)}, bf16[16,4224]{1,0:T(8,128)(2,1)S(1)}, u32[]{:S(2)}, u32[]{:S(2)}) collective-permute-start(bf16[16,4224]{1,0:T(8,128)(2,1)S(1)} %token_rows.1), channel_id=1, source_target_pairs={{0,2},{1,3},{2,0},{3,1},{4,6},{5,7},{6,4},{7,5},{8,10},{9,11},{10,... | collective-permute-start | bytes 405512 | tf_op jit(solution)/shard_map/ppermute | solution.py:40
  78.8 10.2 %collective-permute-start.14 = (bf16[16,4224]{1,0:T(8,128)(2,1)S(1)}, bf16[16,4224]{1,0:T(8,128)(2,1)S(1)}, u32[]{:S(2)}, u32[]{:S(2)}) collective-permute-start(bf16[16,4224]{1,0:T(8,128)(2,1)S(1)} %token_rows.1), channel_id=1, source_target_pairs={{0,3},{1,2},{2,1},{3,0},{4,7},{5,6},{6,5},{7,4},{8,11},{9,10},{10,... | collective-permute-start | bytes 405512 | tf_op jit(solution)/shard_map/ppermute | solution.py:40
  89.0 2.0 %collective-permute-start.17 = (bf16[64,4224]{1,0:T(8,128)(2,1)S(1)}, bf16[64,4224]{1,0:T(8,128)(2,1)S(1)}, u32[]{:S(2)}, u32[]{:S(2)}) collective-permute-start(bf16[64,4224]{1,0:T(8,128)(2,1)S(1)} %constant_dynamic-update-slice_fusion.2.refs_0_), channel_id=1, source_target_pairs={{0,4},{4,0},{8,12},{12,8},{1,5},{5,1},{9,13},{13,9},{2,6},{6,2},{1... | collective-permute-start | bytes 1622024 | tf_op jit(solution)/shard_map/ppermute | solution.py:40
  89.1 14.7 %collective-permute-start.15 = (bf16[64,4224]{1,0:T(8,128)(2,1)S(1)}, bf16[64,4224]{1,0:T(8,128)(2,1)S(1)}, u32[]{:S(2)}, u32[]{:S(2)}) collective-permute-start(bf16[64,4224]{1,0:T(8,128)(2,1)S(1)} %constant_dynamic-update-slice_fusion.2.refs_0_), channel_id=1, source_target_pairs={{0,16},{16,0},{1,17},{17,1},{2,18},{18,2},{3,19},{19,3},{4,20},{20... | collective-permute-start | bytes 1622024 | tf_op jit(solution)/shard_map/ppermute | solution.py:40
  89.6 14.3 %collective-permute-start.16 = (bf16[64,4224]{1,0:T(8,128)(2,1)S(1)}, bf16[64,4224]{1,0:T(8,128)(2,1)S(1)}, u32[]{:S(2)}, u32[]{:S(2)}) collective-permute-start(bf16[64,4224]{1,0:T(8,128)(2,1)S(1)} %constant_dynamic-update-slice_fusion.2.refs_0_), channel_id=1, source_target_pairs={{0,8},{4,12},{8,0},{12,4},{1,9},{5,13},{9,1},{13,5},{2,10},{6,14},... | collective-permute-start | bytes 1622024 | tf_op jit(solution)/shard_map/ppermute | solution.py:40
  103.9 2.7 %collective-permute-start.20 = (bf16[64,4224]{1,0:T(8,128)(2,1)S(1)}, bf16[64,4224]{1,0:T(8,128)(2,1)S(1)}, u32[]{:S(2)}, u32[]{:S(2)}) collective-permute-start(bf16[64,4224]{1,0:T(8,128)(2,1)S(1)} %collective-permute-done.16.refs_0_), channel_id=1, source_target_pairs={{0,4},{4,0},{8,12},{12,8},{1,5},{5,1},{9,13},{13,9},{2,6},{6,2},{1... | collective-permute-start | bytes 1622024 | tf_op jit(solution)/shard_map/ppermute | solution.py:40
  103.9 2.7 %collective-permute-start.21 = (bf16[64,4224]{1,0:T(8,128)(2,1)S(1)}, bf16[64,4224]{1,0:T(8,128)(2,1)S(1)}, u32[]{:S(2)}, u32[]{:S(2)}) collective-permute-start(bf16[64,4224]{1,0:T(8,128)(2,1)S(1)} %collective-permute-done.15.refs_2_), channel_id=1, source_target_pairs={{0,4},{4,0},{8,12},{12,8},{1,5},{5,1},{9,13},{13,9},{2,6},{6,2},{1... | collective-permute-start | bytes 1622024 | tf_op jit(solution)/shard_map/ppermute | solution.py:40
  104.5 8.5 %collective-permute-start.18 = (bf16[32,4224]{1,0:T(8,128)(2,1)S(1)}, bf16[32,4224]{1,0:T(8,128)(2,1)S(1)}, u32[]{:S(2)}, u32[]{:S(2)}) collective-permute-start(bf16[32,4224]{1,0:T(8,128)(2,1)S(1)} %slice.6), channel_id=1, source_target_pairs={{0,8},{4,12},{8,0},{12,4},{1,9},{5,13},{9,1},{13,5},{2,10},{6,14},... | collective-permute-start | bytes 811016 | tf_op jit(solution)/shard_map/ppermute | solution.py:40
  104.8 8.2 %collective-permute-start.19 = (bf16[32,4224]{1,0:T(8,128)(2,1)S(1)}, bf16[32,4224]{1,0:T(8,128)(2,1)S(1)}, u32[]{:S(2)}, u32[]{:S(2)}) collective-permute-start(bf16[32,4224]{1,0:T(8,128)(2,1)S(1)} %slice.7), channel_id=1, source_target_pairs={{0,16},{16,0},{1,17},{17,1},{2,18},{18,2},{3,19},{19,3},{4,20},{20... | collective-permute-start | bytes 811016 | tf_op jit(solution)/shard_map/ppermute | solution.py:40
  113.1 2.0 %collective-permute-start.22 = (bf16[64,4224]{1,0:T(8,128)(2,1)S(1)}, bf16[64,4224]{1,0:T(8,128)(2,1)S(1)}, u32[]{:S(2)}, u32[]{:S(2)}) collective-permute-start(bf16[64,4224]{1,0:T(8,128)(2,1)S(1)} %constant_dynamic-update-slice_fusion.refs_0_), channel_id=1, source_target_pairs={{0,4},{4,0},{8,12},{12,8},{1,5},{5,1},{9,13},{13,9},{2,6},{6,2},{1... | collective-permute-start | bytes 1622024 | tf_op jit(solution)/shard_map/ppermute | solution.py:40

commit v6 on v5

--- a/solution.py
+++ b/solution.py
@@ -184,19 +184,26 @@
             total[...] += product
     group = place_ref[1]
     for distance in range(count):
-        slot = jnp.int32(0)
-        for candidate in range(1, slots):
+        slot = jnp.int32(-1)
+        for candidate in range(slots):
             holds = slot_ref[group * slots + candidate] == group ^ distance
             slot = jnp.where(holds, candidate, slot)
-        start = pl.multiple_of(slot * tokens, tokens)
         out = outs[distance]
-        out[:tokens, :] = total[pl.ds(start, tokens), :].astype(jnp.bfloat16)
-        for part in range(parts):
-            first = tokens + part * share
-            out[first : first + share, :] = shares[
-                slot, :share, part * columns : (part + 1) * columns
-            ]
-        out[tokens + parts * share :, :] = shares[slot, share:, :columns]
+
+        @pl.when(slot < 0)
+        def _(out=out):
+            out[...] = jnp.zeros_like(out)
+
+        @pl.when(slot >= 0)
+        def _(out=out, slot=slot):
+            start = pl.multiple_of(slot * tokens, tokens)
+            out[:tokens, :] = total[pl.ds(start, tokens), :].astype(jnp.bfloat16)
+            for part in range(parts):
+                first = tokens + part * share
+                out[first : first + share, :] = shares[
+                    slot, :share, part * columns : (part + 1) * columns
+                ]
+            out[tokens + parts * share :, :] = shares[slot, share:, :columns]
 
 
 def queries_of(place, slot_utt, lengths, after, states, targets, weights, count, share):
@@ -318,20 +325,18 @@
         context[:, head * HD : (head + 1) * HD] = dot(chances, values).astype(jnp.bfloat16)
     to = lax.broadcasted_iota(jnp.int32, (tokens, tokens), 0)
     come = lax.broadcasted_iota(jnp.int32, (tokens, tokens), 1)
-    half = tokens // sections
-    section = jnp.where(to < half, 1 - section_pos, section_pos)
-    inside = to % half
-    row = jnp.zeros_like(to)
-    width = jnp.zeros_like(to)
-    first = 0
-    for piece in pieces:
-        at = inside - first * widths
-        here = (at >= 0) & (at < piece * widths)
-        row = jnp.where(here, first + at % piece, row)
-        block = at // piece
-        width = jnp.where(here, block % 2 * (widths // 2) + block // 2, width)
-        first += piece
-    move = come == (row * sections + section) * widths + width
+    low_bit = place_ref[2] % 2
+    size = widths * pieces[0]
+    block = to % size // pieces[0]
+    section = jnp.where(to < size, 1 - section_pos, section_pos)
+    first_order = (to % pieces[0] * sections + section) * widths + block % 2 * 2 + block // 2
+    at = to - 2 * size
+    size = widths * pieces[1]
+    block = at % size // pieces[1]
+    low = jnp.where(at < size, 1 - low_bit, low_bit)
+    row = pieces[0] + at % pieces[1]
+    second_order = (row * sections + block % 2) * widths + block // 2 * 2 + low
+    move = come == jnp.where(at < 0, first_order, second_order)
     ordered = dot(jnp.where(move, 1.0, 0.0).astype(jnp.bfloat16), context[...])
     ordered = ordered.astype(jnp.bfloat16)
     for number in range(tiles):
@@ -349,8 +354,11 @@
     capacity = sum(pieces) * sections * widths
     tile = 1024
     tiles = width // tile
-    shapes = [jax.ShapeDtypeStruct((piece * widths, width), jnp.bfloat16) for piece in pieces]
-    shapes = shapes + shapes
+    shapes = [
+        jax.ShapeDtypeStruct((piece * widths, width), jnp.bfloat16)
+        for piece in pieces
+        for _ in range(2)
+    ]
     return pl.pallas_call(
         functools.partial(
             attention_kernel, count, slots, capacity, pieces, sections, widths, tile
@@ -636,17 +644,14 @@
         place,
         slot_utt,
         lengths,
-        parts[1],
+        own_frames,
         hyp_state.reshape(slot_count, slot_tokens, model_width),
         hyp_tok.reshape(slot_count, 1, slot_tokens),
         q_proj,
         group_count,
         share_rows,
     )
-    beside = group_pos ^ 1
-    beside_slots = lax.dynamic_slice_in_dim(slot_utt, beside * slot_count, slot_count, 0)
-    beside_has = jnp.any(beside_slots == group_pos ^ 2)
-    crossing = jnp.where(beside_has, swap(blocks[3], "tm", 1), blocks[2])
+    crossing = blocks[2] + swap(blocks[3], "tm", 1)
     payloads = [blocks[0], swap(blocks[1], "tm", 1), swap(crossing, "tm", 2)]
 
     sent = keys_values_of(
@@ -668,22 +673,24 @@
         width_count,
         slot_count,
     )
-    others = [swap(projected[number], "section", 1) for number in range(len(pieces))]
-    head, token = load_head(projected[len(pieces)], head)
-    sums = []
-    for number, piece in enumerate(pieces):
-        total = projected[len(pieces) + number].astype(jnp.float32) + others[number].astype(
-            jnp.float32
-        )
-        for distance in (1, 2):
-            half = total.shape[0] // 2
-            side = width_pos // distance % 2
-            kept = lax.dynamic_slice_in_dim(total, side * half, half, 0)
-            sent = lax.dynamic_slice_in_dim(total, (1 - side) * half, half, 0)
-            came = swap(sent.astype(jnp.bfloat16), "mp", distance)
-            if distance == 1:
-                total = kept + came.astype(jnp.float32)
-        sums += [kept, came]
+    head, token = load_head(projected[1], head)
+
+    def halve(total, came, axis, distance, side):
+        if came is not None:
+            total = total + came.astype(jnp.float32)
+        half = total.shape[0] // 2
+        kept = lax.dynamic_slice_in_dim(total, side * half, half, 0)
+        sent = lax.dynamic_slice_in_dim(total, (1 - side) * half, half, 0)
+        return kept, swap(sent.astype(jnp.bfloat16), axis, distance)
+
+    low, high = width_pos % 2, width_pos // 2
+    first = projected[1].astype(jnp.float32), swap(projected[0], "section", 1)
+    second = projected[3].astype(jnp.float32), swap(projected[2], "mp", 1)
+    first = halve(*first, "mp", 1, low)
+    second = halve(*second, "mp", 2, high)
+    first = halve(*first, "mp", 2, high)
+    second = halve(*second, "section", 1, section_pos)
+    sums = [*first, *second]
     out_rows = normed_rows(
         place, slot_utt, token, payloads, sums, pieces, slot_tokens, slot_count
     )

time: 136 us -> 126 us (0.926)
  blocking collectives: 27.5 us -> 12.6 us
  waiting for transfers between devices: 35.1 us -> 41.9 us
  starting transfers between devices: 23.4 us -> 26.8 us
  local copies, waits for them, and re-layouts: 5.37 us -> 3.01 us
  Pallas kernels: 42.5 us -> 41.1 us
    all_to_all x2 -> x1, blocking collectives: 27.5 us -> 12.6 us  [exchange(): return lax.all_to_all(blocks, axis, split_axis=0, concat_axis=0, tiled=True)]
    all_to_all x0 -> x1, waiting for transfers between devices: none -> 8.39 us  [exchange(): return lax.all_to_all(blocks, axis, split_axis=0, concat_axis=0, tiled=True)]
    all_to_all x0 -> x1, starting transfers between devices: none -> 5.1 us  [exchange(): return lax.all_to_all(blocks, axis, split_axis=0, concat_axis=0, tiled=True)]
    unnamed x21 -> x7, local copies, waits for them, and re-layouts: 3.74 us -> 0.04 us
    ppermute x23, starting transfers between devices: 23.4 us -> 21.7 us  [swap(): return lax.ppermute(values, axis, pairs)]
    ppermute x23, waiting for transfers between devices: 35.1 us -> 33.5 us  [swap(): return lax.ppermute(values, axis, pairs)]
  transfers between devices with their start and end apart: 23 -> 24, of which waited for: 16 -> 15; matrix products, arithmetic and copies ran while one was open for 1% -> 0% of each run, Pallas kernels for 14% -> 15%
where the time goes in v6:
time: 126 us
  waiting for transfers between devices  41.9 us (33%)
  Pallas kernels  41.1 us (33%)
  starting transfers between devices  26.8 us (21%)
  blocking collectives  12.6 us (10%)
  local copies, waits for them, and re-layouts  3.01 us (2%)
    ppermute x23, waiting for transfers between devices, swap(): return lax.ppermute(values, axis, pairs)  33.5 us
    ppermute x23, starting transfers between devices, swap(): return lax.ppermute(values, axis, pairs)  21.7 us
    pallas_call x3, Pallas kernels, vocabulary_stats(): pl.pallas_call(functools.partial(vocabulary_kernel, head.shape[0] // 2),...  17.5 us
    all_to_all x1, blocking collectives, exchange(): return lax.all_to_all(blocks, axis, split_axis=0, concat_axis=0, tiled=True)  12.6 us
    all_to_all x1, waiting for transfers between devices, exchange(): return lax.all_to_all(blocks, axis, split_axis=0, concat_axis=0, tiled=True)  8.39 us
    pallas_call x1, Pallas kernels, load_head(): pl.pallas_call(functools.partial(load_kernel, rows), in_specs=[ANYWHERE,...  5.77 us
    pallas_call x1, Pallas kernels, queries_of(): pl.pallas_call(functools.partial(query_kernel, count, depth), in_specs=[S...  5.43 us
    all_to_all x1, starting transfers between devices, exchange(): return lax.all_to_all(blocks, axis, split_axis=0, concat_axis=0, tiled=True)  5.1 us
  transfers between devices with their start and end apart: 24, of which 15 were waited for; matrix products, arithmetic and copies ran while one was open for 0% of the time, Pallas kernels for 15%

profile of v6, /device:TPU:0, one launch (start us, length us, event | category | flops | bytes accessed | tf_op | source)
XLA Modules:
  0.0 125.9 jit_solution(17726732107845689149)
XLA Ops:
  0.0 1.1 reshape.19.x_ref
  1.1 0.8 reshape.18.length_ref
  1.8 0.8 reshape.21.tok_ref
  2.6 0.1 stack.23.place_ref.refs_0_.first_ref
  2.7 4.9 %encoder_ffn.1 = (bf16[32,1280]{1,0:T(8,128)(2,1)S(1)}, bf16[32,1280]{1,0:T(8,128)(2,1)S(1)}, bf16[32,1280]{1,0:T(8,128)(2,1)S(1)}, bf16[32,1280]{1,0:T(8,128)(2,1)S(1)}, bf16[32,1280]{1,0:T(8,128)(2,1)S(1)}) custom-call(s32[5]{0:T(128)S(1)} %stack.23.place_ref.refs_0_.first_ref, bf16[128,1280]{1,0:T(8,128)(2,1)S(1)} %reshape.19.x_ref, ...), custom_call_target="tpu_custom_call" | custom-call | flops 838860800 | bytes 6553600 | tf_op jit(solution)/shard_map/encoder_ffn/pallas_call | solution.py:113
  7.6 0.0 copy-start
  7.6 0.0 copy-start.2
  7.6 5.4 %hypothesis_queries.1 = (bf16[272,512]{1,0:T(8,128)(2,1)S(1)}, bf16[272,512]{1,0:T(8,128)(2,1)S(1)}, bf16[272,512]{1,0:T(8,128)(2,1)S(1)}, bf16[272,512]{1,0:T(8,128)(2,1)S(1)}) custom-call(s32[5]{0:T(128)S(1)} %stack.23.place_ref.refs_0_.first_ref, s32[8]{0:T(128)S(1)} %copy-done.1, s32[16]{0:T(128)S(1)} %reshape.18.length_ref, ...), custom_call_target="tpu_custom_call" | custom-call | flops 1073741824 | bytes 6291456 | tf_op jit(solution)/shard_map/hypothesis_queries/pallas_call | solution.py:215
  13.1 0.5 collective-permute-start.1
  13.6 2.7 %collective-permute-start.3 = (bf16[32,1280]{1,0:T(8,128)(2,1)S(1)}, bf16[32,1280]{1,0:T(8,128)(2,1)S(1)}, u32[]{:S(2)}, u32[]{:S(2)}) collective-permute-start(bf16[32,1280]{1,0:T(8,128)(2,1)S(1)} %get-tuple-element.32), channel_id=1, source_target_pairs={{0,1},{1,0},{2,3},{3,2},{4,5},{5,4},{6,7},{7,6},{8,9},{9,8},{10,11... | collective-permute-start | bytes 245768 | tf_op jit(solution)/shard_map/ppermute | solution.py:40
  16.2 2.6 %collective-permute-start.4 = (bf16[32,1280]{1,0:T(8,128)(2,1)S(1)}, bf16[32,1280]{1,0:T(8,128)(2,1)S(1)}, u32[]{:S(2)}, u32[]{:S(2)}) collective-permute-start(bf16[32,1280]{1,0:T(8,128)(2,1)S(1)} %get-tuple-element.33), channel_id=1, source_target_pairs={{0,2},{1,3},{2,0},{3,1},{4,6},{5,7},{6,4},{7,5},{8,10},{9,11},{10,... | collective-permute-start | bytes 245768 | tf_op jit(solution)/shard_map/ppermute | solution.py:40
  18.8 0.0 collective-permute-start
  18.8 0.0 collective-permute-done.1
  18.8 0.1 add.68
  18.9 1.8 %collective-permute-start.2 = (bf16[272,512]{1,0:T(8,128)(2,1)S(1)}, bf16[272,512]{1,0:T(8,128)(2,1)S(1)}, u32[]{:S(2)}, u32[]{:S(2)}) collective-permute-start(bf16[272,512]{1,0:T(8,128)(2,1)S(1)} %add.68), channel_id=1, source_target_pairs={{0,8},{4,12},{8,0},{12,4},{1,9},{5,13},{9,1},{13,5},{2,10},{6,14},... | collective-permute-start | bytes 835592 | tf_op jit(solution)/shard_map/ppermute | solution.py:40
  20.7 0.0 collective-permute-done.3.refs_1_
  20.8 5.0 %collective-permute-done.4.refs_2_ = bf16[32,1280]{1,0:T(8,128)(2,1)S(1)} collective-permute-done((bf16[32,1280]{1,0:T(8,128)(2,1)S(1)}, bf16[32,1280]{1,0:T(8,128)(2,1)S(1)}, u32[]{:S(2)}, u32[]{:S(2)}) %collective-permute-start.4) | collective-permute-done | bytes 81952 | tf_op jit(solution)/shard_map/ppermute | solution.py:40
  25.7 1.5 %frame_keys_values.1 = bf16[256,256]{1,0:T(8,128)(2,1)} custom-call(bf16[32,1280]{1,0:T(8,128)(2,1)S(1)} %get-tuple-element.31.refs_0_, bf16[32,1280]{1,0:T(8,128)(2,1)S(1)} %collective-permute-done.3.refs_1_, bf16[32,1280]{1,0:T(8,128)(2,1)S(1)} %collective-permute-done.4.refs_2_, bf16[32,1280]{1,0:T(8,128)(2,1)S(1)} %collective-permute-done.5.refs_3_, ...), custom_call_target="tpu_custom_call" | custom-call | flops 83886080 | bytes 2621440 | tf_op jit(solution)/shard_map/frame_keys_values/pallas_call | solution.py:274
  27.3 5.1 %all-to-all-start = ((bf16[32,8,256]{2,1,0:T(8,128)(2,1)}), bf16[32,8,256]{2,1,0:T(8,128)(2,1)S(1)}, u32[]{:S(2)}, u32[]{:S(2)}) async-start(bf16[32,8,256]{2,1,0:T(8,128)(2,1)} %bitcast.6), calls=%async_computation | async-start | bytes 262144 | tf_op jit(solution)/shard_map/all_to_all | solution.py:30
  32.4 8.4 %all-to-all-done = bf16[32,8,256]{2,1,0:T(8,128)(2,1)S(1)} async-done(((bf16[32,8,256]{2,1,0:T(8,128)(2,1)}), bf16[32,8,256]{2,1,0:T(8,128)(2,1)S(1)}, u32[]{:S(2)}, u32[]{:S(2)}) %all-to-all-start) | async-done | bytes 131104 | tf_op jit(solution)/shard_map/all_to_all | solution.py:30
  40.8 0.0 collective-permute-done.2.refs_5_.refs_2_
  40.8 3.1 %attention_projection.1 = (bf16[32,4096]{1,0:T(8,128)(2,1)S(1)}, bf16[32,4096]{1,0:T(8,128)(2,1)S(1)}, bf16[32,4096]{1,0:T(8,128)(2,1)S(1)}, bf16[32,4096]{1,0:T(8,128)(2,1)S(1)}) custom-call(s32[5]{0:T(128)S(1)} %stack.23.place_ref.refs_0_.first_ref, s32[8]{0:T(128)S(1)} %copy-done.1, s32[4]{0:T(128)S(1)} %copy-done.2, ...), custom_call_target="tpu_custom_call" | custom-call | flops 603979776 | bytes 5242880 | tf_op jit(solution)/shard_map/attention_projection/pallas_call | solution.py:362
  43.9 0.8 collective-permute-start.6
  44.7 5.8 %vocabulary_rows.1 = (bf16[2000,4096]{1,0:T(8,128)(2,1)S(1)}, f32[8,128]{1,0:T(8,128)S(1)}) custom-call(bf16[32,4096]{1,0:T(8,128)(2,1)S(1)} %get-tuple-element.35.after_ref, bf16[2000,4096]{1,0:T(8,128)(2,1)} %head_ref.1), custom_call_target="tpu_custom_call" | custom-call | bytes 16384000 | tf_op jit(solution)/shard_map/vocabulary_rows/pallas_call | solution.py:444
  50.5 0.8 collective-permute-done.6
  51.3 0.1 convert_add_fusion.1
  51.4 1.3 %collective-permute-start.7 = (bf16[16,4096]{1,0:T(8,128)(2,1)S(1)}, bf16[16,4096]{1,0:T(8,128)(2,1)S(1)}, u32[]{:S(2)}, u32[]{:S(2)}) collective-permute-start(bf16[16,4096]{1,0:T(8,128)(2,1)S(1)} %dynamic-slice_convert_fusion.1), channel_id=1, source_target_pairs={{0,1},{1,0},{2,3},{3,2},{4,5},{5,4},{6,7},{7,6},{8,9},{9,8},{10,11... | collective-permute-start | bytes 393224 | tf_op jit(solution)/shard_map/ppermute | solution.py:40
  52.7 0.0 collective-permute-done.9
  52.7 0.1 convert_add_fusion
  52.8 0.8 collective-permute-start.10
  53.6 3.3 %collective-permute-done.7 = bf16[16,4096]{1,0:T(8,128)(2,1)S(1)} collective-permute-done((bf16[16,4096]{1,0:T(8,128)(2,1)S(1)}, bf16[16,4096]{1,0:T(8,128)(2,1)S(1)}, u32[]{:S(2)}, u32[]{:S(2)}) %collective-permute-start.7) | collective-permute-done | bytes 131104 | tf_op jit(solution)/shard_map/ppermute | solution.py:40
  57.0 2.2 %collective-permute-start.8 = (bf16[8,4096]{1,0:T(8,128)(2,1)S(1)}, bf16[8,4096]{1,0:T(8,128)(2,1)S(1)}, u32[]{:S(2)}, u32[]{:S(2)}) collective-permute-start(bf16[8,4096]{1,0:T(8,128)(2,1)S(1)} %dynamic-slice_convert_fusion.3), channel_id=1, source_target_pairs={{0,2},{1,3},{2,0},{3,1},{4,6},{5,7},{6,4},{7,5},{8,10},{9,11},{10,... | collective-permute-start | bytes 196616 | tf_op jit(solution)/shard_map/ppermute | solution.py:40
  59.2 3.6 %collective-permute-done.10 = bf16[16,4096]{1,0:T(8,128)(2,1)S(1)} collective-permute-done((bf16[16,4096]{1,0:T(8,128)(2,1)S(1)}, bf16[16,4096]{1,0:T(8,128)(2,1)S(1)}, u32[]{:S(2)}, u32[]{:S(2)}) %collective-permute-start.10) | collective-permute-done | bytes 131104 | tf_op jit(solution)/shard_map/ppermute | solution.py:40
  62.8 0.8 collective-permute-start.11
  63.6 0.5 collective-permute-done.8.refs_4_
  64.2 3.0 %collective-permute-done.11.refs_6_ = bf16[8,4096]{1,0:T(8,128)(2,1)S(1)} collective-permute-done((bf16[8,4096]{1,0:T(8,128)(2,1)S(1)}, bf16[8,4096]{1,0:T(8,128)(2,1)S(1)}, u32[]{:S(2)}, u32[]{:S(2)}) %collective-permute-start.11) | collective-permute-done | bytes 65568 | tf_op jit(solution)/shard_map/ppermute | solution.py:40
  67.2 0.9 token_rows.1
  68.1 0.1 collective-permute-start.12
  68.2 2.1 %collective-permute-start.13 = (bf16[16,4224]{1,0:T(8,128)(2,1)S(1)}, bf16[16,4224]{1,0:T(8,128)(2,1)S(1)}, u32[]{:S(2)}, u32[]{:S(2)}) collective-permute-start(bf16[16,4224]{1,0:T(8,128)(2,1)S(1)} %token_rows.1), channel_id=1, source_target_pairs={{0,2},{1,3},{2,0},{3,1},{4,6},{5,7},{6,4},{7,5},{8,10},{9,11},{10,... | collective-permute-start | bytes 405512 | tf_op jit(solution)/shard_map/ppermute | solution.py:40
  70.2 2.3 %collective-permute-start.14 = (bf16[16,4224]{1,0:T(8,128)(2,1)S(1)}, bf16[16,4224]{1,0:T(8,128)(2,1)S(1)}, u32[]{:S(2)}, u32[]{:S(2)}) collective-permute-start(bf16[16,4224]{1,0:T(8,128)(2,1)S(1)} %token_rows.1), channel_id=1, source_target_pairs={{0,3},{1,2},{2,1},{3,0},{4,7},{5,6},{6,5},{7,4},{8,11},{9,10},{10,... | collective-permute-start | bytes 405512 | tf_op jit(solution)/shard_map/ppermute | solution.py:40
  72.6 2.2 %collective-permute-done.12 = bf16[16,4224]{1,0:T(8,128)(2,1)S(1)} collective-permute-done((bf16[16,4224]{1,0:T(8,128)(2,1)S(1)}, bf16[16,4224]{1,0:T(8,128)(2,1)S(1)}, u32[]{:S(2)}, u32[]{:S(2)}) %collective-permute-start.12) | collective-permute-done | bytes 135200 | tf_op jit(solution)/shard_map/ppermute | solution.py:40
  74.8 4.6 %collective-permute-done.13 = bf16[16,4224]{1,0:T(8,128)(2,1)S(1)} collective-permute-done((bf16[16,4224]{1,0:T(8,128)(2,1)S(1)}, bf16[16,4224]{1,0:T(8,128)(2,1)S(1)}, u32[]{:S(2)}, u32[]{:S(2)}) %collective-permute-start.13) | collective-permute-done | bytes 135200 | tf_op jit(solution)/shard_map/ppermute | solution.py:40
  79.4 0.0 collective-permute-done.14
  79.5 0.1 collective-permute-start.17
  79.6 0.5 collective-permute-start.15
  80.1 0.4 collective-permute-start.16
  80.5 1.0 collective-permute-done.17.refs_1_
  81.5 5.7 %vocabulary_scores.3.refs_0_ = f32[2,8,64]{2,1,0:T(8,128)S(1)} custom-call(s32[5]{0:T(128)S(1)} %stack.23.place_ref.refs_0_.first_ref, bf16[64,4224]{1,0:T(8,128)(2,1)S(1)} %constant_dynamic-update-slice_fusion.2.refs_0_, bf16[64,4224]{1,0:T(8,128)(2,1)S(1)} %collective-permute-done.17.refs_1_, bf16[2000,4096]{1,0:T(8,128)(2,1)S(1)} %get-tuple-element.40.refs_2_.refs_4_), custom_call_target="tpu_custom_call" | custom-call | flops 3145728000 | bytes 1048576 | tf_op jit(solution)/shard_map/vocabulary_scores/pallas_call | solution.py:500
  87.2 7.0 %collective-permute-done.15.refs_2_ = bf16[64,4224]{1,0:T(8,128)(2,1)S(1)} collective-permute-done((bf16[64,4224]{1,0:T(8,128)(2,1)S(1)}, bf16[64,4224]{1,0:T(8,128)(2,1)S(1)}, u32[]{:S(2)}, u32[]{:S(2)}) %collective-permute-start.15) | collective-permute-done | bytes 540704 | tf_op jit(solution)/shard_map/ppermute | solution.py:40
  94.2 0.2 collective-permute-done.16.refs_0_
  94.4 0.5 collective-permute-start.21
  95.0 0.5 collective-permute-start.18
  95.4 1.7 %collective-permute-start.19 = (bf16[32,4224]{1,0:T(8,128)(2,1)S(1)}, bf16[32,4224]{1,0:T(8,128)(2,1)S(1)}, u32[]{:S(2)}, u32[]{:S(2)}) collective-permute-start(bf16[32,4224]{1,0:T(8,128)(2,1)S(1)} %slice.7), channel_id=1, source_target_pairs={{0,16},{16,0},{1,17},{17,1},{2,18},{18,2},{3,19},{19,3},{4,20},{20... | collective-permute-start | bytes 811016 | tf_op jit(solution)/shard_map/ppermute | solution.py:40
  97.2 0.0 collective-permute-done.20.refs_1_
  97.2 0.0 collective-permute-done.21.refs_3_
  97.2 6.0 %vocabulary_scores.4.refs_1_ = f32[4,8,64]{2,1,0:T(8,128)S(1)} custom-call(s32[5]{0:T(128)S(1)} %stack.23.place_ref.refs_0_.first_ref, bf16[64,4224]{1,0:T(8,128)(2,1)S(1)} %collective-permute-done.16.refs_0_, bf16[64,4224]{1,0:T(8,128)(2,1)S(1)} %collective-permute-done.20.refs_1_, bf16[64,4224]{1,0:T(8,128)(2,1)S(1)} %collective-permute-done.15.refs_2_, ...), custom_call_target="tpu_custom_call" | custom-call | flops 6291456000 | bytes 2097152 | tf_op jit(solution)/shard_map/vocabulary_scores/pallas_call | solution.py:500
  103.2 0.2 collective-permute-done.18
  103.4 0.1 collective-permute-done.19
  103.6 0.1 collective-permute-start.22
  103.7 1.9 %collective-permute-done.22.refs_1_ = bf16[64,4224]{1,0:T(8,128)(2,1)S(1)} collective-permute-done((bf16[64,4224]{1,0:T(8,128)(2,1)S(1)}, bf16[64,4224]{1,0:T(8,128)(2,1)S(1)}, u32[]{:S(2)}, u32[]{:S(2)}) %collective-permute-start.22) | collective-permute-done | bytes 540704 | tf_op jit(solution)/shard_map/ppermute | solution.py:40
  105.6 5.7 %vocabulary_scores.5.refs_2_ = f32[2,8,64]{2,1,0:T(8,128)S(1)} custom-call(s32[5]{0:T(128)S(1)} %stack.23.place_ref.refs_0_.first_ref, bf16[64,4224]{1,0:T(8,128)(2,1)S(1)} %constant_dynamic-update-slice_fusion.refs_0_, bf16[64,4224]{1,0:T(8,128)(2,1)S(1)} %collective-permute-done.22.refs_1_, bf16[2000,4096]{1,0:T(8,128)(2,1)S(1)} %get-tuple-element.40.refs_2_.refs_4_), custom_call_target="tpu_custom_call" | custom-call | flops 3145728000 | bytes 1048576 | tf_op jit(solution)/shard_map/vocabulary_scores/pallas_call | solution.py:500
  111.3 0.6 statistics_by_group.1
  112.0 12.6 %all_to_all.10.every_ref = f32[32,8,128]{2,1,0:T(8,128)S(1)} all-to-all(f32[32,8,128]{2,1,0:T(8,128)S(1)} %statistics_by_group.1), channel_id=1, replica_groups=mesh['section'=2,'tm'=4,'mp'=4] {'section','tm','mp'}, dimensions={0} | all-to-all | bytes 262144 | tf_op jit(solution)/shard_map/all_to_all | solution.py:30
  124.6 1.3 %hypothesis_scores.1 = f32[2,8]{1,0:T(2,128)} custom-call(s32[5]{0:T(128)S(1)} %stack.23.place_ref.refs_0_.first_ref, s32[8]{0:T(128)S(1)} %copy-done.1, s32[16]{0:T(128)S(1)} %reshape.18.length_ref, f32[32,8,128]{2,1,0:T(8,128)S(1)} %all_to_all.10.every_ref), custom_call_target="tpu_custom_call" | custom-call | tf_op jit(solution)/shard_map/hypothesis_scores/pallas_call | solution.py:590
  (26 shorter events, 0.4 us)
Async XLA Ops:
  0.0 7.6 %copy-start.1 = (s32[8]{0:T(128)S(1)}, s32[8]{0:T(128)}, u32[]{:S(2)}) copy-start(s32[8]{0:T(128)} %slot_ref.7) | copy-start | bytes 100
  7.6 18.1 %copy-start = (bf16[1280,1024]{1,0:T(8,128)(2,1)S(1)}, bf16[1280,1024]{1,0:T(8,128)(2,1)}, u32[]{:S(2)}) copy-start(bf16[1280,1024]{1,0:T(8,128)(2,1)} %refs_5_.1) | copy-start | bytes 7864324
  7.6 33.1 %copy-start.2 = (s32[4]{0:T(128)S(1)}, s32[4]{0:T(128)}, u32[]{:S(2)}) copy-start(s32[4]{0:T(128)} %refs_2_.1) | copy-start | bytes 52
  13.1 5.8 %collective-permute-start.1 = (bf16[272,512]{1,0:T(8,128)(2,1)S(1)}, bf16[272,512]{1,0:T(8,128)(2,1)S(1)}, u32[]{:S(2)}, u32[]{:S(2)}) collective-permute-start(bf16[272,512]{1,0:T(8,128)(2,1)S(1)} %get-tuple-element.30), channel_id=1, source_target_pairs={{0,4},{4,0},{8,12},{12,8},{1,5},{5,1},{9,13},{13,9},{2,6},{6,2},{1... | collective-permute-start | bytes 835592 | tf_op jit(solution)/shard_map/ppermute | solution.py:40
  13.6 7.2 %collective-permute-start.3 = (bf16[32,1280]{1,0:T(8,128)(2,1)S(1)}, bf16[32,1280]{1,0:T(8,128)(2,1)S(1)}, u32[]{:S(2)}, u32[]{:S(2)}) collective-permute-start(bf16[32,1280]{1,0:T(8,128)(2,1)S(1)} %get-tuple-element.32), channel_id=1, source_target_pairs={{0,1},{1,0},{2,3},{3,2},{4,5},{5,4},{6,7},{7,6},{8,9},{9,8},{10,11... | collective-permute-start | bytes 245768 | tf_op jit(solution)/shard_map/ppermute | solution.py:40
  16.2 9.5 %collective-permute-start.4 = (bf16[32,1280]{1,0:T(8,128)(2,1)S(1)}, bf16[32,1280]{1,0:T(8,128)(2,1)S(1)}, u32[]{:S(2)}, u32[]{:S(2)}) collective-permute-start(bf16[32,1280]{1,0:T(8,128)(2,1)S(1)} %get-tuple-element.33), channel_id=1, source_target_pairs={{0,2},{1,3},{2,0},{3,1},{4,6},{5,7},{6,4},{7,5},{8,10},{9,11},{10,... | collective-permute-start | bytes 245768 | tf_op jit(solution)/shard_map/ppermute | solution.py:40
  18.8 6.9 %collective-permute-start.5 = (bf16[32,1280]{1,0:T(8,128)(2,1)S(1)}, bf16[32,1280]{1,0:T(8,128)(2,1)S(1)}, u32[]{:S(2)}, u32[]{:S(2)}) collective-permute-start(bf16[32,1280]{1,0:T(8,128)(2,1)S(1)} %get-tuple-element.34), channel_id=1, source_target_pairs={{0,3},{1,2},{2,1},{3,0},{4,7},{5,6},{6,5},{7,4},{8,11},{9,10},{10,... | collective-permute-start | bytes 245768 | tf_op jit(solution)/shard_map/ppermute | solution.py:40
  18.8 13.5 %collective-permute-start = (bf16[272,512]{1,0:T(8,128)(2,1)S(1)}, bf16[272,512]{1,0:T(8,128)(2,1)S(1)}, u32[]{:S(2)}, u32[]{:S(2)}) collective-permute-start(bf16[272,512]{1,0:T(8,128)(2,1)S(1)} %get-tuple-element.28), channel_id=1, source_target_pairs={{0,4},{4,0},{8,12},{12,8},{1,5},{5,1},{9,13},{13,9},{2,6},{6,2},{1... | collective-permute-start | bytes 835592 | tf_op jit(solution)/shard_map/ppermute | solution.py:40
  18.9 21.8 %collective-permute-start.2 = (bf16[272,512]{1,0:T(8,128)(2,1)S(1)}, bf16[272,512]{1,0:T(8,128)(2,1)S(1)}, u32[]{:S(2)}, u32[]{:S(2)}) collective-permute-start(bf16[272,512]{1,0:T(8,128)(2,1)S(1)} %add.68), channel_id=1, source_target_pairs={{0,8},{4,12},{8,0},{12,4},{1,9},{5,13},{9,1},{13,5},{2,10},{6,14},... | collective-permute-start | bytes 835592 | tf_op jit(solution)/shard_map/ppermute | solution.py:40
  27.3 13.5 %all-to-all-start = ((bf16[32,8,256]{2,1,0:T(8,128)(2,1)}), bf16[32,8,256]{2,1,0:T(8,128)(2,1)S(1)}, u32[]{:S(2)}, u32[]{:S(2)}) async-start(bf16[32,8,256]{2,1,0:T(8,128)(2,1)} %bitcast.6), calls=%async_computation | async-start | bytes 262144 | tf_op jit(solution)/shard_map/all_to_all | solution.py:30
  43.9 7.4 %collective-permute-start.6 = (bf16[32,4096]{1,0:T(8,128)(2,1)S(1)}, bf16[32,4096]{1,0:T(8,128)(2,1)S(1)}, u32[]{:S(2)}, u32[]{:S(2)}) collective-permute-start(bf16[32,4096]{1,0:T(8,128)(2,1)S(1)} %get-tuple-element.37), channel_id=1, source_target_pairs={{0,16},{16,0},{1,17},{17,1},{2,18},{18,2},{3,19},{19,3},{4,20},{20... | collective-permute-start | bytes 786440 | tf_op jit(solution)/shard_map/ppermute | solution.py:40
  44.7 8.0 %collective-permute-start.9 = (bf16[32,4096]{1,0:T(8,128)(2,1)S(1)}, bf16[32,4096]{1,0:T(8,128)(2,1)S(1)}, u32[]{:S(2)}, u32[]{:S(2)}) collective-permute-start(bf16[32,4096]{1,0:T(8,128)(2,1)S(1)} %get-tuple-element.39), channel_id=1, source_target_pairs={{0,1},{1,0},{2,3},{3,2},{4,5},{5,4},{6,7},{7,6},{8,9},{9,8},{10,11... | collective-permute-start | bytes 786440 | tf_op jit(solution)/shard_map/ppermute | solution.py:40
  51.4 5.5 %collective-permute-start.7 = (bf16[16,4096]{1,0:T(8,128)(2,1)S(1)}, bf16[16,4096]{1,0:T(8,128)(2,1)S(1)}, u32[]{:S(2)}, u32[]{:S(2)}) collective-permute-start(bf16[16,4096]{1,0:T(8,128)(2,1)S(1)} %dynamic-slice_convert_fusion.1), channel_id=1, source_target_pairs={{0,1},{1,0},{2,3},{3,2},{4,5},{5,4},{6,7},{7,6},{8,9},{9,8},{10,11... | collective-permute-start | bytes 393224 | tf_op jit(solution)/shard_map/ppermute | solution.py:40
  52.8 10.0 %collective-permute-start.10 = (bf16[16,4096]{1,0:T(8,128)(2,1)S(1)}, bf16[16,4096]{1,0:T(8,128)(2,1)S(1)}, u32[]{:S(2)}, u32[]{:S(2)}) collective-permute-start(bf16[16,4096]{1,0:T(8,128)(2,1)S(1)} %dynamic-slice_convert_fusion), channel_id=1, source_target_pairs={{0,2},{1,3},{2,0},{3,1},{4,6},{5,7},{6,4},{7,5},{8,10},{9,11},{10,... | collective-permute-start | bytes 393224 | tf_op jit(solution)/shard_map/ppermute | solution.py:40
  57.0 7.2 %collective-permute-start.8 = (bf16[8,4096]{1,0:T(8,128)(2,1)S(1)}, bf16[8,4096]{1,0:T(8,128)(2,1)S(1)}, u32[]{:S(2)}, u32[]{:S(2)}) collective-permute-start(bf16[8,4096]{1,0:T(8,128)(2,1)S(1)} %dynamic-slice_convert_fusion.3), channel_id=1, source_target_pairs={{0,2},{1,3},{2,0},{3,1},{4,6},{5,7},{6,4},{7,5},{8,10},{9,11},{10,... | collective-permute-start | bytes 196616 | tf_op jit(solution)/shard_map/ppermute | solution.py:40
  62.8 4.3 %collective-permute-start.11 = (bf16[8,4096]{1,0:T(8,128)(2,1)S(1)}, bf16[8,4096]{1,0:T(8,128)(2,1)S(1)}, u32[]{:S(2)}, u32[]{:S(2)}) collective-permute-start(bf16[8,4096]{1,0:T(8,128)(2,1)S(1)} %dynamic-slice_convert_fusion.2), channel_id=1, source_target_pairs={{0,16},{16,0},{1,17},{17,1},{2,18},{18,2},{3,19},{19,3},{4,20},{20... | collective-permute-start | bytes 196616 | tf_op jit(solution)/shard_map/ppermute | solution.py:40
  68.1 6.7 %collective-permute-start.12 = (bf16[16,4224]{1,0:T(8,128)(2,1)S(1)}, bf16[16,4224]{1,0:T(8,128)(2,1)S(1)}, u32[]{:S(2)}, u32[]{:S(2)}) collective-permute-start(bf16[16,4224]{1,0:T(8,128)(2,1)S(1)} %token_rows.1), channel_id=1, source_target_pairs={{0,1},{1,0},{2,3},{3,2},{4,5},{5,4},{6,7},{7,6},{8,9},{9,8},{10,11... | collective-permute-start | bytes 405512 | tf_op jit(solution)/shard_map/ppermute | solution.py:40
  68.2 11.3 %collective-permute-start.13 = (bf16[16,4224]{1,0:T(8,128)(2,1)S(1)}, bf16[16,4224]{1,0:T(8,128)(2,1)S(1)}, u32[]{:S(2)}, u32[]{:S(2)}) collective-permute-start(bf16[16,4224]{1,0:T(8,128)(2,1)S(1)} %token_rows.1), channel_id=1, source_target_pairs={{0,2},{1,3},{2,0},{3,1},{4,6},{5,7},{6,4},{7,5},{8,10},{9,11},{10,... | collective-permute-start | bytes 405512 | tf_op jit(solution)/shard_map/ppermute | solution.py:40
  70.2 9.2 %collective-permute-start.14 = (bf16[16,4224]{1,0:T(8,128)(2,1)S(1)}, bf16[16,4224]{1,0:T(8,128)(2,1)S(1)}, u32[]{:S(2)}, u32[]{:S(2)}) collective-permute-start(bf16[16,4224]{1,0:T(8,128)(2,1)S(1)} %token_rows.1), channel_id=1, source_target_pairs={{0,3},{1,2},{2,1},{3,0},{4,7},{5,6},{6,5},{7,4},{8,11},{9,10},{10,... | collective-permute-start | bytes 405512 | tf_op jit(solution)/shard_map/ppermute | solution.py:40
  79.5 2.0 %collective-permute-start.17 = (bf16[64,4224]{1,0:T(8,128)(2,1)S(1)}, bf16[64,4224]{1,0:T(8,128)(2,1)S(1)}, u32[]{:S(2)}, u32[]{:S(2)}) collective-permute-start(bf16[64,4224]{1,0:T(8,128)(2,1)S(1)} %constant_dynamic-update-slice_fusion.2.refs_0_), channel_id=1, source_target_pairs={{0,4},{4,0},{8,12},{12,8},{1,5},{5,1},{9,13},{13,9},{2,6},{6,2},{1... | collective-permute-start | bytes 1622024 | tf_op jit(solution)/shard_map/ppermute | solution.py:40
  79.6 14.7 %collective-permute-start.15 = (bf16[64,4224]{1,0:T(8,128)(2,1)S(1)}, bf16[64,4224]{1,0:T(8,128)(2,1)S(1)}, u32[]{:S(2)}, u32[]{:S(2)}) collective-permute-start(bf16[64,4224]{1,0:T(8,128)(2,1)S(1)} %constant_dynamic-update-slice_fusion.2.refs_0_), channel_id=1, source_target_pairs={{0,16},{16,0},{1,17},{17,1},{2,18},{18,2},{3,19},{19,3},{4,20},{20... | collective-permute-start | bytes 1622024 | tf_op jit(solution)/shard_map/ppermute | solution.py:40
  80.1 14.3 %collective-permute-start.16 = (bf16[64,4224]{1,0:T(8,128)(2,1)S(1)}, bf16[64,4224]{1,0:T(8,128)(2,1)S(1)}, u32[]{:S(2)}, u32[]{:S(2)}) collective-permute-start(bf16[64,4224]{1,0:T(8,128)(2,1)S(1)} %constant_dynamic-update-slice_fusion.2.refs_0_), channel_id=1, source_target_pairs={{0,8},{4,12},{8,0},{12,4},{1,9},{5,13},{9,1},{13,5},{2,10},{6,14},... | collective-permute-start | bytes 1622024 | tf_op jit(solution)/shard_map/ppermute | solution.py:40
  94.4 2.8 %collective-permute-start.20 = (bf16[64,4224]{1,0:T(8,128)(2,1)S(1)}, bf16[64,4224]{1,0:T(8,128)(2,1)S(1)}, u32[]{:S(2)}, u32[]{:S(2)}) collective-permute-start(bf16[64,4224]{1,0:T(8,128)(2,1)S(1)} %collective-permute-done.16.refs_0_), channel_id=1, source_target_pairs={{0,4},{4,0},{8,12},{12,8},{1,5},{5,1},{9,13},{13,9},{2,6},{6,2},{1... | collective-permute-start | bytes 1622024 | tf_op jit(solution)/shard_map/ppermute | solution.py:40
  94.4 2.8 %collective-permute-start.21 = (bf16[64,4224]{1,0:T(8,128)(2,1)S(1)}, bf16[64,4224]{1,0:T(8,128)(2,1)S(1)}, u32[]{:S(2)}, u32[]{:S(2)}) collective-permute-start(bf16[64,4224]{1,0:T(8,128)(2,1)S(1)} %collective-permute-done.15.refs_2_), channel_id=1, source_target_pairs={{0,4},{4,0},{8,12},{12,8},{1,5},{5,1},{9,13},{13,9},{2,6},{6,2},{1... | collective-permute-start | bytes 1622024 | tf_op jit(solution)/shard_map/ppermute | solution.py:40
  95.0 8.5 %collective-permute-start.18 = (bf16[32,4224]{1,0:T(8,128)(2,1)S(1)}, bf16[32,4224]{1,0:T(8,128)(2,1)S(1)}, u32[]{:S(2)}, u32[]{:S(2)}) collective-permute-start(bf16[32,4224]{1,0:T(8,128)(2,1)S(1)} %slice.6), channel_id=1, source_target_pairs={{0,8},{4,12},{8,0},{12,4},{1,9},{5,13},{9,1},{13,5},{2,10},{6,14},... | collective-permute-start | bytes 811016 | tf_op jit(solution)/shard_map/ppermute | solution.py:40
  95.4 8.1 %collective-permute-start.19 = (bf16[32,4224]{1,0:T(8,128)(2,1)S(1)}, bf16[32,4224]{1,0:T(8,128)(2,1)S(1)}, u32[]{:S(2)}, u32[]{:S(2)}) collective-permute-start(bf16[32,4224]{1,0:T(8,128)(2,1)S(1)} %slice.7), channel_id=1, source_target_pairs={{0,16},{16,0},{1,17},{17,1},{2,18},{18,2},{3,19},{19,3},{4,20},{20... | collective-permute-start | bytes 811016 | tf_op jit(solution)/shard_map/ppermute | solution.py:40
  103.6 2.0 %collective-permute-start.22 = (bf16[64,4224]{1,0:T(8,128)(2,1)S(1)}, bf16[64,4224]{1,0:T(8,128)(2,1)S(1)}, u32[]{:S(2)}, u32[]{:S(2)}) collective-permute-start(bf16[64,4224]{1,0:T(8,128)(2,1)S(1)} %constant_dynamic-update-slice_fusion.refs_0_), channel_id=1, source_target_pairs={{0,4},{4,0},{8,12},{12,8},{1,5},{5,1},{9,13},{13,9},{2,6},{6,2},{1... | collective-permute-start | bytes 1622024 | tf_op jit(solution)/shard_map/ppermute | solution.py:40

commit v7 on v6

--- a/solution.py
+++ b/solution.py
@@ -68,9 +68,9 @@
     return copies
 
 
-def ffn_kernel(count, tile, place_ref, x_ref, up_ref, down_ref, *refs):
-    outs, (own_ref, total, up, down, up_sem, down_sem) = refs[:count], refs[count:]
-    share = own_ref.shape[0]
+def ffn_kernel(tile, place_ref, x_ref, up_ref, down_ref, *refs):
+    out_ref, own_ref, rows, total, up, down, up_sem, down_sem = refs
+    count, share, width = out_ref.shape
     tiles = up_ref.shape[1] // tile
     up_copies = start_copies(
         lambda i: up_ref.at[:, pl.ds(i * tile, tile)], lambda i: up.at[i], up_sem, tiles
@@ -78,9 +78,10 @@
     down_copies = start_copies(
         lambda i: down_ref.at[pl.ds(i * tile, tile), :], lambda i: down.at[i], down_sem, tiles
     )
-    here = place_ref[2]
-    own_ref[...] = x_ref[pl.ds(pl.multiple_of(here * share, share), share), :]
-    normed = layer_norm(x_ref[...].astype(jnp.float32)).astype(jnp.bfloat16)
+    rows[...] = x_ref[...].astype(jnp.float32).reshape(rows.shape)
+    start = pl.multiple_of(place_ref[2] * share, share)
+    own_ref[...] = rows[pl.ds(start, share), :].astype(jnp.bfloat16)
+    normed = layer_norm(rows[...]).astype(jnp.bfloat16)
     for number in range(tiles):
         up_copies[number].wait()
         hidden = dot(normed, up[number])
@@ -91,9 +92,8 @@
             total[...] = product
         else:
             total[...] += product
-    for distance in range(count):
-        start = pl.multiple_of((here ^ distance) * share, share)
-        outs[distance][...] = total[pl.ds(start, share), :].astype(jnp.bfloat16)
+    for part in range(count):
+        out_ref[part] = total[part * share : (part + 1) * share, :].astype(jnp.bfloat16)
 
 
 def in_hbm(values):
@@ -104,32 +104,36 @@
 INSIDE = pl.BlockSpec(memory_space=pltpu.VMEM)
 
 
-def ffn(place, rows, up, down, count):
-    share = rows.shape[0] // count
-    width = rows.shape[1]
+def ffn(place, enc_in, up, down, count):
+    frames, utterances, width = enc_in.shape
+    rows = frames * utterances
+    share = rows // count
     tile = 256
     tiles = up.shape[1] // tile
-    block = jax.ShapeDtypeStruct((share, width), jnp.bfloat16)
     return pl.pallas_call(
-        functools.partial(ffn_kernel, count, tile),
+        functools.partial(ffn_kernel, tile),
         in_specs=[SCALARS, INSIDE, ANYWHERE, ANYWHERE],
-        out_specs=[INSIDE] * (count + 1),
-        out_shape=[block] * (count + 1),
+        out_specs=[INSIDE] * 2,
+        out_shape=[
+            jax.ShapeDtypeStruct((count, share, width), jnp.bfloat16),
+            jax.ShapeDtypeStruct((share, width), jnp.bfloat16),
+        ],
         scratch_shapes=[
-            pltpu.VMEM(rows.shape, jnp.float32),
+            pltpu.VMEM((rows, width), jnp.float32),
+            pltpu.VMEM((rows, width), jnp.float32),
             pltpu.VMEM((tiles, width, tile), jnp.bfloat16),
             pltpu.VMEM((tiles, tile, width), jnp.bfloat16),
             pltpu.SemaphoreType.DMA((tiles,)),
             pltpu.SemaphoreType.DMA((tiles,)),
         ],
         cost_estimate=pl.CostEstimate(
-            flops=4 * rows.shape[0] * width * up.shape[1],
+            flops=4 * rows * width * up.shape[1],
             bytes_accessed=4 * width * up.shape[1],
-            transcendentals=rows.shape[0] * up.shape[1],
+            transcendentals=rows * up.shape[1],
         ),
         compiler_params=pltpu.CompilerParams(vmem_limit_bytes=24 << 20),
         name="encoder_ffn",
-    )(place, rows, in_hbm(up), in_hbm(down))
+    )(place, enc_in, in_hbm(up), in_hbm(down))
 
 
 def query_kernel(
@@ -137,7 +141,7 @@
 ):
     outs, (states, weights, normed, total, shares, x_sem, w_sem) = refs[:count], refs[count:]
     slots, tokens, width = x_ref.shape
-    hyps = length_ref.shape[0] // slots
+    hyps = length_ref.shape[1]
     positions = tokens // hyps
     columns = w_ref.shape[1]
     share = shares.shape[1] // 2
@@ -155,7 +159,7 @@
         order = jnp.full((1, tokens), -1, jnp.int32)
         start = jnp.int32(0)
         for hyp in range(hyps):
-            length = length_ref[slot * hyps + hyp]
+            length = length_ref[slot, hyp]
             inside = (lane >= hyp * positions) & (lane < hyp * positions + length)
             order = jnp.where(inside, lane - hyp * positions + start, order)
             start = start + length
@@ -237,13 +241,13 @@
 
 
 def kv_kernel(sections, utterances, widths, *refs):
-    parts, (own_ref, w_ref, after_ref, out_ref) = refs[:-4], refs[-4:]
+    parts_ref, own_ref, w_ref, after_ref, out_ref = refs
     rows = own_ref.shape[0]
     frames = rows // utterances
     total = own_ref[...].astype(jnp.float32)
-    summed = parts[0][...].astype(jnp.float32)
-    for part in parts[1:]:
-        summed += part[...].astype(jnp.float32)
+    summed = parts_ref[0].astype(jnp.float32)
+    for part in range(1, parts_ref.shape[0]):
+        summed += parts_ref[part].astype(jnp.float32)
     states = layer_norm(total + summed).astype(jnp.bfloat16)
     to = lax.broadcasted_iota(jnp.int32, (rows, rows), 0)
     come = lax.broadcasted_iota(jnp.int32, (rows, rows), 1)
@@ -273,7 +277,7 @@
     rows = sections * widths * own.shape[0]
     return pl.pallas_call(
         functools.partial(kv_kernel, sections, utterances, widths),
-        in_specs=[INSIDE] * (len(parts) + 2) + [ANYWHERE],
+        in_specs=[INSIDE] * 3 + [ANYWHERE],
         out_specs=INSIDE,
         out_shape=jax.ShapeDtypeStruct((rows, 2 * HD), jnp.bfloat16),
         cost_estimate=pl.CostEstimate(
@@ -283,7 +287,7 @@
         ),
         compiler_params=pltpu.CompilerParams(vmem_limit_bytes=24 << 20),
         name="frame_keys_values",
-    )(*parts, own, weights, after)
+    )(parts, own, weights, after)
 
 
 def choice_of_payload(place_ref, slot_ref, slots):
@@ -576,7 +580,7 @@
         scores = jnp.zeros((1, hyps), jnp.float32)
         start = jnp.int32(0)
         for hyp in range(hyps):
-            length = length_ref[slot * hyps + hyp]
+            length = length_ref[slot, hyp]
             valid = (order >= start) & (order < start + length)
             summed = jnp.sum(jnp.where(valid, logp, 0.0), axis=1, keepdims=True)
             mean = summed / jnp.full((1, 1), length, jnp.int32).astype(jnp.float32)
@@ -630,21 +634,15 @@
     head_pos = section_pos * width_count + width_pos
     place = jnp.stack([section_pos, group_pos, width_pos, vocab_start, head_pos])
     place = place.astype(jnp.int32)
-    lengths = hyp_len.reshape(-1)
-
-    parts = ffn(
-        place, enc_in.reshape(frame_rows * utterances, enc_width), ffn_up, ffn_down, width_count
-    )
-    own_frames = parts[width_count]
-    parts = [parts[0]] + [
-        swap(parts[distance], "mp", distance) for distance in range(1, width_count)
-    ]
+
+    parts, own_frames = ffn(place, enc_in, ffn_up, ffn_down, width_count)
+    parts = exchange(parts, "mp")
 
     blocks = queries_of(
         place,
         slot_utt,
-        lengths,
-        own_frames,
+        hyp_len,
+        place,
         hyp_state.reshape(slot_count, slot_tokens, model_width),
         hyp_tok.reshape(slot_count, 1, slot_tokens),
         q_proj,
@@ -717,7 +715,7 @@
         spread_stats(place, slot_utt, stats, section_count, group_count, width_count), ALL
     )
     return hypothesis_scores(
-        place, slot_utt, lengths, every, slot_count, hyp_count, section_count, width_count
+        place, slot_utt, hyp_len, every, slot_count, hyp_count, section_count, width_count
     )
 
 

time: 126 us -> 126 us (level)
  waiting for transfers between devices: 41.9 us -> 38.3 us
    all_to_all x1 -> x2, starting transfers between devices: 5.1 us -> 11.4 us  [exchange(): return lax.all_to_all(blocks, axis, split_axis=0, concat_axis=0, tiled=True)]
    ppermute x23 -> x20, starting transfers between devices: 21.7 us -> 16.2 us  [swap(): return lax.ppermute(values, axis, pairs)]
    ppermute x23 -> x20, waiting for transfers between devices: 33.5 us -> 29.6 us  [swap(): return lax.ppermute(values, axis, pairs)]
    unnamed x7 -> x21, local copies, waits for them, and re-layouts: 0.04 us -> 3.26 us
    reshape x2 -> x0, local copies, waits for them, and re-layouts: 1.83 us -> none  [the longest x1 1.06 us: near_device(): enc_in.reshape(frame_rows * utterances, enc_width)]
    all_to_all x1 -> x2, waiting for transfers between devices: 8.39 us -> 8.71 us  [exchange(): return lax.all_to_all(blocks, axis, split_axis=0, concat_axis=0, tiled=True)]
  transfers between devices with their start and end apart: 24 -> 22, of which waited for: 15 -> 16; matrix products, arithmetic and copies ran while one was open for 0% -> 1% of each run, Pallas kernels for 15% -> 19%
where the time goes in v7:
time: 126 us; the launch traced here: 125 us
  Pallas kernels  41.7 us (33%)
  waiting for transfers between devices  38.3 us (30%)
  starting transfers between devices  27.6 us (22%)
  blocking collectives  12.6 us (10%)
  local copies, waits for them, and re-layouts  3.71 us (3%)
    ppermute x20, waiting for transfers between devices, swap(): return lax.ppermute(values, axis, pairs)  29.6 us
    pallas_call x3, Pallas kernels, vocabulary_stats(): pl.pallas_call(functools.partial(vocabulary_kernel, head.shape[0] // 2),...  17.5 us
    ppermute x20, starting transfers between devices, swap(): return lax.ppermute(values, axis, pairs)  16.2 us
    all_to_all x1, blocking collectives, exchange(): return lax.all_to_all(blocks, axis, split_axis=0, concat_axis=0, tiled=True)  12.6 us
    all_to_all x2, starting transfers between devices, exchange(): return lax.all_to_all(blocks, axis, split_axis=0, concat_axis=0, tiled=True)  11.4 us
    all_to_all x2, waiting for transfers between devices, exchange(): return lax.all_to_all(blocks, axis, split_axis=0, concat_axis=0, tiled=True)  8.71 us
    pallas_call x1, Pallas kernels, queries_of(): pl.pallas_call(functools.partial(query_kernel, count, depth), in_specs=[S...  5.95 us
    pallas_call x1, Pallas kernels, load_head(): pl.pallas_call(functools.partial(load_kernel, rows), in_specs=[ANYWHERE,...  5.77 us
  transfers between devices with their start and end apart: 22, of which 16 were waited for; matrix products, arithmetic and copies ran while one was open for 1% of the time, Pallas kernels for 19%

profile of v7, /device:TPU:0, one launch (start us, length us, event | category | flops | bytes accessed | tf_op | source)
XLA Modules:
  0.0 125.2 jit_solution(15014797509973272896)
XLA Ops:
  0.0 0.1 stack.23.place_ref.after_ref.refs_0_.first_ref
  0.1 1.0 copy-done.2
  1.1 4.9 %encoder_ffn.1 = (bf16[4,32,1280]{2,1,0:T(8,128)(2,1)S(1)}, bf16[32,1280]{1,0:T(8,128)(2,1)S(1)}) custom-call(s32[5]{0:T(128)S(1)} %stack.23.place_ref.after_ref.refs_0_.first_ref, bf16[32,4,1280]{2,1,0:T(4,128)(2,1)S(1)} %copy-done.2, bf16[1280,1280]{1,0:T(8,128)(2,1)} %up_ref.1, bf16[1280,1280]{1,0:T(8,128)(2,1)} %down_ref.1), custom_call_target="tpu_custom_call" | custom-call | flops 838860800 | bytes 6553600 | tf_op jit(solution)/shard_map/encoder_ffn/pallas_call | solution.py:113
  6.0 0.7 copy-done.3
  6.7 6.6 %all-to-all-start = ((bf16[4,32,1280]{2,1,0:T(8,128)(2,1)}), bf16[4,32,1280]{2,1,0:T(8,128)(2,1)S(1)}, u32[]{:S(2)}, u32[]{:S(2)}) async-start(bf16[4,32,1280]{2,1,0:T(8,128)(2,1)} %copy-done.3), calls=%async_computation | async-start | bytes 655360 | tf_op jit(solution)/shard_map/all_to_all | solution.py:30
  13.3 0.1 reshape.13.tok_ref
  13.4 0.0 copy-start.8
  13.4 5.9 %hypothesis_queries.1 = (bf16[272,512]{1,0:T(8,128)(2,1)S(1)}, bf16[272,512]{1,0:T(8,128)(2,1)}, bf16[272,512]{1,0:T(8,128)(2,1)S(1)}, bf16[272,512]{1,0:T(8,128)(2,1)S(1)}) custom-call(s32[5]{0:T(128)S(1)} %stack.23.place_ref.after_ref.refs_0_.first_ref, s32[8]{0:T(128)S(1)} %copy-done.6, s32[2,8]{1,0:T(2,128)S(1)} %copy-done.7, ...), custom_call_target="tpu_custom_call" | custom-call | flops 1073741824 | bytes 6291456 | tf_op jit(solution)/shard_map/hypothesis_queries/pallas_call | solution.py:219
  19.4 0.1 collective-permute-start.1
  19.4 0.5 collective-permute-start
  19.9 1.0 collective-permute-done.1
  21.0 0.8 add.68
  21.8 1.5 %collective-permute-start.2 = (bf16[272,512]{1,0:T(8,128)(2,1)}, bf16[272,512]{1,0:T(8,128)(2,1)}, u32[]{:S(2)}, u32[]{:S(2)}) collective-permute-start(bf16[272,512]{1,0:T(8,128)(2,1)} %add.68), channel_id=1, source_target_pairs={{0,8},{4,12},{8,0},{12,4},{1,9},{5,13},{9,1},{13,5},{2,10},{6,14},... | collective-permute-start | bytes 835592 | tf_op jit(solution)/shard_map/ppermute | solution.py:40
  23.3 0.3 all-to-all-done.refs_0_
  23.6 0.9 copy-done.5
  24.5 0.9 frame_keys_values.1
  25.4 0.6 copy-done.1
  26.0 4.8 %all-to-all-start.1 = ((bf16[32,8,256]{2,1,0:T(8,128)(2,1)}), bf16[32,8,256]{2,1,0:T(8,128)(2,1)S(1)}, u32[]{:S(2)}, u32[]{:S(2)}) async-start(bf16[32,8,256]{2,1,0:T(8,128)(2,1)} %bitcast.9), calls=%async_computation.1 | async-start | bytes 262144 | tf_op jit(solution)/shard_map/all_to_all | solution.py:30
  30.8 0.0 collective-permute-done.2.refs_5_.refs_2_
  30.8 8.4 %all-to-all-done.1 = bf16[32,8,256]{2,1,0:T(8,128)(2,1)S(1)} async-done(((bf16[32,8,256]{2,1,0:T(8,128)(2,1)}), bf16[32,8,256]{2,1,0:T(8,128)(2,1)S(1)}, u32[]{:S(2)}, u32[]{:S(2)}) %all-to-all-start.1) | async-done | bytes 131104 | tf_op jit(solution)/shard_map/all_to_all | solution.py:30
  39.2 3.5 %attention_projection.1 = (bf16[32,4096]{1,0:T(8,128)(2,1)S(1)}, bf16[32,4096]{1,0:T(8,128)(2,1)S(1)}, bf16[32,4096]{1,0:T(8,128)(2,1)S(1)}, bf16[32,4096]{1,0:T(8,128)(2,1)S(1)}) custom-call(s32[5]{0:T(128)S(1)} %stack.23.place_ref.after_ref.refs_0_.first_ref, s32[8]{0:T(128)S(1)} %copy-done.6, s32[4]{0:T(128)S(1)} %copy-done.8, ...), custom_call_target="tpu_custom_call" | custom-call | flops 603979776 | bytes 5242880 | tf_op jit(solution)/shard_map/attention_projection/pallas_call | solution.py:366
  42.8 0.8 collective-permute-start.3
  43.6 5.8 %vocabulary_rows.1 = (bf16[2000,4096]{1,0:T(8,128)(2,1)S(1)}, f32[8,128]{1,0:T(8,128)S(1)}) custom-call(bf16[32,4096]{1,0:T(8,128)(2,1)S(1)} %get-tuple-element.29.after_ref, bf16[2000,4096]{1,0:T(8,128)(2,1)} %head_ref.1), custom_call_target="tpu_custom_call" | custom-call | bytes 16384000 | tf_op jit(solution)/shard_map/vocabulary_rows/pallas_call | solution.py:448
  49.4 0.8 collective-permute-done.3
  50.2 0.1 convert_add_fusion.1
  50.3 1.3 %collective-permute-start.4 = (bf16[16,4096]{1,0:T(8,128)(2,1)S(1)}, bf16[16,4096]{1,0:T(8,128)(2,1)S(1)}, u32[]{:S(2)}, u32[]{:S(2)}) collective-permute-start(bf16[16,4096]{1,0:T(8,128)(2,1)S(1)} %dynamic-slice_convert_fusion.1), channel_id=1, source_target_pairs={{0,1},{1,0},{2,3},{3,2},{4,5},{5,4},{6,7},{7,6},{8,9},{9,8},{10,11... | collective-permute-start | bytes 393224 | tf_op jit(solution)/shard_map/ppermute | solution.py:40
  51.6 0.0 collective-permute-done.6
  51.6 0.1 convert_add_fusion
  51.7 0.8 collective-permute-start.7
  52.5 3.3 %collective-permute-done.4 = bf16[16,4096]{1,0:T(8,128)(2,1)S(1)} collective-permute-done((bf16[16,4096]{1,0:T(8,128)(2,1)S(1)}, bf16[16,4096]{1,0:T(8,128)(2,1)S(1)}, u32[]{:S(2)}, u32[]{:S(2)}) %collective-permute-start.4) | collective-permute-done | bytes 131104 | tf_op jit(solution)/shard_map/ppermute | solution.py:40
  55.9 2.2 %collective-permute-start.5 = (bf16[8,4096]{1,0:T(8,128)(2,1)S(1)}, bf16[8,4096]{1,0:T(8,128)(2,1)S(1)}, u32[]{:S(2)}, u32[]{:S(2)}) collective-permute-start(bf16[8,4096]{1,0:T(8,128)(2,1)S(1)} %dynamic-slice_convert_fusion.3), channel_id=1, source_target_pairs={{0,2},{1,3},{2,0},{3,1},{4,6},{5,7},{6,4},{7,5},{8,10},{9,11},{10,... | collective-permute-start | bytes 196616 | tf_op jit(solution)/shard_map/ppermute | solution.py:40
  58.1 3.6 %collective-permute-done.7 = bf16[16,4096]{1,0:T(8,128)(2,1)S(1)} collective-permute-done((bf16[16,4096]{1,0:T(8,128)(2,1)S(1)}, bf16[16,4096]{1,0:T(8,128)(2,1)S(1)}, u32[]{:S(2)}, u32[]{:S(2)}) %collective-permute-start.7) | collective-permute-done | bytes 131104 | tf_op jit(solution)/shard_map/ppermute | solution.py:40
  61.7 0.8 collective-permute-start.8
  62.5 0.5 collective-permute-done.5.refs_4_
  63.1 3.0 %collective-permute-done.8.refs_6_ = bf16[8,4096]{1,0:T(8,128)(2,1)S(1)} collective-permute-done((bf16[8,4096]{1,0:T(8,128)(2,1)S(1)}, bf16[8,4096]{1,0:T(8,128)(2,1)S(1)}, u32[]{:S(2)}, u32[]{:S(2)}) %collective-permute-start.8) | collective-permute-done | bytes 65568 | tf_op jit(solution)/shard_map/ppermute | solution.py:40
  66.0 1.3 %token_rows.1 = bf16[16,4224]{1,0:T(8,128)(2,1)S(1)} custom-call(s32[5]{0:T(128)S(1)} %stack.23.place_ref.after_ref.refs_0_.first_ref, s32[8]{0:T(128)S(1)} %copy-done.6, f32[8,128]{1,0:T(8,128)S(1)} %get-tuple-element.30.after_ref, bf16[272,512]{1,0:T(8,128)(2,1)S(1)} %get-tuple-element.23.refs_3_.refs_0_, ...), custom_call_target="tpu_custom_call" | custom-call | tf_op jit(solution)/shard_map/token_rows/pallas_call | solution.py:419
  67.4 0.1 collective-permute-start.9
  67.5 2.1 %collective-permute-start.10 = (bf16[16,4224]{1,0:T(8,128)(2,1)S(1)}, bf16[16,4224]{1,0:T(8,128)(2,1)S(1)}, u32[]{:S(2)}, u32[]{:S(2)}) collective-permute-start(bf16[16,4224]{1,0:T(8,128)(2,1)S(1)} %token_rows.1), channel_id=1, source_target_pairs={{0,2},{1,3},{2,0},{3,1},{4,6},{5,7},{6,4},{7,5},{8,10},{9,11},{10,... | collective-permute-start | bytes 405512 | tf_op jit(solution)/shard_map/ppermute | solution.py:40
  69.5 2.3 %collective-permute-start.11 = (bf16[16,4224]{1,0:T(8,128)(2,1)S(1)}, bf16[16,4224]{1,0:T(8,128)(2,1)S(1)}, u32[]{:S(2)}, u32[]{:S(2)}) collective-permute-start(bf16[16,4224]{1,0:T(8,128)(2,1)S(1)} %token_rows.1), channel_id=1, source_target_pairs={{0,3},{1,2},{2,1},{3,0},{4,7},{5,6},{6,5},{7,4},{8,11},{9,10},{10,... | collective-permute-start | bytes 405512 | tf_op jit(solution)/shard_map/ppermute | solution.py:40
  71.9 2.2 %collective-permute-done.9 = bf16[16,4224]{1,0:T(8,128)(2,1)S(1)} collective-permute-done((bf16[16,4224]{1,0:T(8,128)(2,1)S(1)}, bf16[16,4224]{1,0:T(8,128)(2,1)S(1)}, u32[]{:S(2)}, u32[]{:S(2)}) %collective-permute-start.9) | collective-permute-done | bytes 135200 | tf_op jit(solution)/shard_map/ppermute | solution.py:40
  74.1 4.6 %collective-permute-done.10 = bf16[16,4224]{1,0:T(8,128)(2,1)S(1)} collective-permute-done((bf16[16,4224]{1,0:T(8,128)(2,1)S(1)}, bf16[16,4224]{1,0:T(8,128)(2,1)S(1)}, u32[]{:S(2)}, u32[]{:S(2)}) %collective-permute-start.10) | collective-permute-done | bytes 135200 | tf_op jit(solution)/shard_map/ppermute | solution.py:40
  78.7 0.0 collective-permute-done.11
  78.8 0.1 collective-permute-start.14
  78.8 0.5 collective-permute-start.12
  79.4 0.4 collective-permute-start.13
  79.8 1.0 collective-permute-done.14.refs_1_
  80.8 5.7 %vocabulary_scores.3.refs_0_ = f32[2,8,64]{2,1,0:T(8,128)S(1)} custom-call(s32[5]{0:T(128)S(1)} %stack.23.place_ref.after_ref.refs_0_.first_ref, bf16[64,4224]{1,0:T(8,128)(2,1)S(1)} %constant_dynamic-update-slice_fusion.2.refs_0_, bf16[64,4224]{1,0:T(8,128)(2,1)S(1)} %collective-permute-done.14.refs_1_, bf16[2000,4096]{1,0:T(8,128)(2,1)S(1)} %get-tuple-element.34.refs_2_.refs_4_), custom_call_target="tpu_custom_call" | custom-call | flops 3145728000 | bytes 1048576 | tf_op jit(solution)/shard_map/vocabulary_scores/pallas_call | solution.py:504
  86.5 7.0 %collective-permute-done.12.refs_2_ = bf16[64,4224]{1,0:T(8,128)(2,1)S(1)} collective-permute-done((bf16[64,4224]{1,0:T(8,128)(2,1)S(1)}, bf16[64,4224]{1,0:T(8,128)(2,1)S(1)}, u32[]{:S(2)}, u32[]{:S(2)}) %collective-permute-start.12) | collective-permute-done | bytes 540704 | tf_op jit(solution)/shard_map/ppermute | solution.py:40
  93.5 0.2 collective-permute-done.13.refs_0_
  93.7 0.0 collective-permute-start.17
  93.7 0.5 collective-permute-start.18
  94.3 0.4 collective-permute-start.15
  94.7 1.7 %collective-permute-start.16 = (bf16[32,4224]{1,0:T(8,128)(2,1)S(1)}, bf16[32,4224]{1,0:T(8,128)(2,1)S(1)}, u32[]{:S(2)}, u32[]{:S(2)}) collective-permute-start(bf16[32,4224]{1,0:T(8,128)(2,1)S(1)} %slice.7), channel_id=1, source_target_pairs={{0,16},{16,0},{1,17},{17,1},{2,18},{18,2},{3,19},{19,3},{4,20},{20... | collective-permute-start | bytes 811016 | tf_op jit(solution)/shard_map/ppermute | solution.py:40
  96.5 0.0 collective-permute-done.17.refs_1_
  96.5 0.0 collective-permute-done.18.refs_3_
  96.5 6.0 %vocabulary_scores.4.refs_1_ = f32[4,8,64]{2,1,0:T(8,128)S(1)} custom-call(s32[5]{0:T(128)S(1)} %stack.23.place_ref.after_ref.refs_0_.first_ref, bf16[64,4224]{1,0:T(8,128)(2,1)S(1)} %collective-permute-done.13.refs_0_, bf16[64,4224]{1,0:T(8,128)(2,1)S(1)} %collective-permute-done.17.refs_1_, bf16[64,4224]{1,0:T(8,128)(2,1)S(1)} %collective-permute-done.12.refs_2_, ...), custom_call_target="tpu_custom_call" | custom-call | flops 6291456000 | bytes 2097152 | tf_op jit(solution)/shard_map/vocabulary_scores/pallas_call | solution.py:504
  102.5 0.3 collective-permute-done.15
  102.7 0.1 collective-permute-done.16
  102.9 0.1 collective-permute-start.19
  103.0 1.9 %collective-permute-done.19.refs_1_ = bf16[64,4224]{1,0:T(8,128)(2,1)S(1)} collective-permute-done((bf16[64,4224]{1,0:T(8,128)(2,1)S(1)}, bf16[64,4224]{1,0:T(8,128)(2,1)S(1)}, u32[]{:S(2)}, u32[]{:S(2)}) %collective-permute-start.19) | collective-permute-done | bytes 540704 | tf_op jit(solution)/shard_map/ppermute | solution.py:40
  104.9 5.7 %vocabulary_scores.5.refs_2_ = f32[2,8,64]{2,1,0:T(8,128)S(1)} custom-call(s32[5]{0:T(128)S(1)} %stack.23.place_ref.after_ref.refs_0_.first_ref, bf16[64,4224]{1,0:T(8,128)(2,1)S(1)} %constant_dynamic-update-slice_fusion.refs_0_, bf16[64,4224]{1,0:T(8,128)(2,1)S(1)} %collective-permute-done.19.refs_1_, bf16[2000,4096]{1,0:T(8,128)(2,1)S(1)} %get-tuple-element.34.refs_2_.refs_4_), custom_call_target="tpu_custom_call" | custom-call | flops 3145728000 | bytes 1048576 | tf_op jit(solution)/shard_map/vocabulary_scores/pallas_call | solution.py:504
  110.6 0.6 statistics_by_group.1
  111.3 12.6 %all_to_all.15.every_ref = f32[32,8,128]{2,1,0:T(8,128)S(1)} all-to-all(f32[32,8,128]{2,1,0:T(8,128)S(1)} %statistics_by_group.1), channel_id=1, replica_groups=mesh['section'=2,'tm'=4,'mp'=4] {'section','tm','mp'}, dimensions={0} | all-to-all | bytes 262144 | tf_op jit(solution)/shard_map/all_to_all | solution.py:30
  123.9 1.3 %hypothesis_scores.1 = f32[2,8]{1,0:T(2,128)} custom-call(s32[5]{0:T(128)S(1)} %stack.23.place_ref.after_ref.refs_0_.first_ref, s32[8]{0:T(128)S(1)} %copy-done.6, s32[2,8]{1,0:T(2,128)S(1)} %copy-done.7, f32[32,8,128]{2,1,0:T(8,128)S(1)} %all_to_all.15.every_ref), custom_call_target="tpu_custom_call" | custom-call | tf_op jit(solution)/shard_map/hypothesis_scores/pallas_call | solution.py:594
  (34 shorter events, 0.4 us)
Async XLA Ops:
  0.0 13.3 %copy-start.9 = (s32[2,8,16]{2,1,0:T(8,128)S(1)}, s32[2,8,16]{2,1,0:T(8,128)}, u32[]{:S(2)}) copy-start(s32[2,8,16]{2,1,0:T(8,128)} %param.19) | copy-start | bytes 3076
  0.0 13.4 %copy-start.6 = (s32[8]{0:T(128)S(1)}, s32[8]{0:T(128)}, u32[]{:S(2)}) copy-start(s32[8]{0:T(128)} %slot_ref.7) | copy-start | bytes 100
  0.0 13.4 %copy-start.7 = (s32[2,8]{1,0:T(2,128)S(1)}, s32[2,8]{1,0:T(2,128)}, u32[]{:S(2)}) copy-start(s32[2,8]{1,0:T(2,128)} %length_ref.3) | copy-start | bytes 196
  0.1 1.0 copy-start.2
  6.0 0.7 copy-start.3
  6.7 6.7 %copy-start.4 = (bf16[32,1280]{1,0:T(8,128)(2,1)}, bf16[32,1280]{1,0:T(8,128)(2,1)S(1)}, u32[]{:S(2)}) copy-start(bf16[32,1280]{1,0:T(8,128)(2,1)S(1)} %get-tuple-element.28.refs_1_) | copy-start | bytes 245764
  6.7 16.9 %copy-start = (bf16[1280,1024]{1,0:T(8,128)(2,1)S(1)}, bf16[1280,1024]{1,0:T(8,128)(2,1)}, u32[]{:S(2)}) copy-start(bf16[1280,1024]{1,0:T(8,128)(2,1)} %refs_2_.2) | copy-start | bytes 7864324
  6.7 16.9 %all-to-all-start = ((bf16[4,32,1280]{2,1,0:T(8,128)(2,1)}), bf16[4,32,1280]{2,1,0:T(8,128)(2,1)S(1)}, u32[]{:S(2)}, u32[]{:S(2)}) async-start(bf16[4,32,1280]{2,1,0:T(8,128)(2,1)} %copy-done.3), calls=%async_computation | async-start | bytes 655360 | tf_op jit(solution)/shard_map/all_to_all | solution.py:30
  13.4 25.8 %copy-start.8 = (s32[4]{0:T(128)S(1)}, s32[4]{0:T(128)}, u32[]{:S(2)}) copy-start(s32[4]{0:T(128)} %refs_2_.3) | copy-start | bytes 52
  19.4 1.6 %collective-permute-start.1 = (bf16[272,512]{1,0:T(8,128)(2,1)S(1)}, bf16[272,512]{1,0:T(8,128)(2,1)S(1)}, u32[]{:S(2)}, u32[]{:S(2)}) collective-permute-start(bf16[272,512]{1,0:T(8,128)(2,1)S(1)} %get-tuple-element.26), channel_id=1, source_target_pairs={{0,4},{4,0},{8,12},{12,8},{1,5},{5,1},{9,13},{13,9},{2,6},{6,2},{1... | collective-permute-start | bytes 835592 | tf_op jit(solution)/shard_map/ppermute | solution.py:40
  19.4 11.4 %collective-permute-start = (bf16[272,512]{1,0:T(8,128)(2,1)}, bf16[272,512]{1,0:T(8,128)(2,1)S(1)}, u32[]{:S(2)}, u32[]{:S(2)}) collective-permute-start(bf16[272,512]{1,0:T(8,128)(2,1)} %get-tuple-element.24), channel_id=1, source_target_pairs={{0,4},{4,0},{8,12},{12,8},{1,5},{5,1},{9,13},{13,9},{2,6},{6,2},{1... | collective-permute-start | bytes 835592 | tf_op jit(solution)/shard_map/ppermute | solution.py:40
  21.8 9.1 %collective-permute-start.2 = (bf16[272,512]{1,0:T(8,128)(2,1)}, bf16[272,512]{1,0:T(8,128)(2,1)}, u32[]{:S(2)}, u32[]{:S(2)}) collective-permute-start(bf16[272,512]{1,0:T(8,128)(2,1)} %add.68), channel_id=1, source_target_pairs={{0,8},{4,12},{8,0},{12,4},{1,9},{5,13},{9,1},{13,5},{2,10},{6,14},... | collective-permute-start | bytes 835592 | tf_op jit(solution)/shard_map/ppermute | solution.py:40
  23.6 0.9 copy-start.5
  25.4 0.6 copy-start.1
  26.0 13.2 %all-to-all-start.1 = ((bf16[32,8,256]{2,1,0:T(8,128)(2,1)}), bf16[32,8,256]{2,1,0:T(8,128)(2,1)S(1)}, u32[]{:S(2)}, u32[]{:S(2)}) async-start(bf16[32,8,256]{2,1,0:T(8,128)(2,1)} %bitcast.9), calls=%async_computation.1 | async-start | bytes 262144 | tf_op jit(solution)/shard_map/all_to_all | solution.py:30
  42.8 7.4 %collective-permute-start.3 = (bf16[32,4096]{1,0:T(8,128)(2,1)S(1)}, bf16[32,4096]{1,0:T(8,128)(2,1)S(1)}, u32[]{:S(2)}, u32[]{:S(2)}) collective-permute-start(bf16[32,4096]{1,0:T(8,128)(2,1)S(1)} %get-tuple-element.31), channel_id=1, source_target_pairs={{0,16},{16,0},{1,17},{17,1},{2,18},{18,2},{3,19},{19,3},{4,20},{20... | collective-permute-start | bytes 786440 | tf_op jit(solution)/shard_map/ppermute | solution.py:40
  43.6 8.0 %collective-permute-start.6 = (bf16[32,4096]{1,0:T(8,128)(2,1)S(1)}, bf16[32,4096]{1,0:T(8,128)(2,1)S(1)}, u32[]{:S(2)}, u32[]{:S(2)}) collective-permute-start(bf16[32,4096]{1,0:T(8,128)(2,1)S(1)} %get-tuple-element.33), channel_id=1, source_target_pairs={{0,1},{1,0},{2,3},{3,2},{4,5},{5,4},{6,7},{7,6},{8,9},{9,8},{10,11... | collective-permute-start | bytes 786440 | tf_op jit(solution)/shard_map/ppermute | solution.py:40
  50.3 5.5 %collective-permute-start.4 = (bf16[16,4096]{1,0:T(8,128)(2,1)S(1)}, bf16[16,4096]{1,0:T(8,128)(2,1)S(1)}, u32[]{:S(2)}, u32[]{:S(2)}) collective-permute-start(bf16[16,4096]{1,0:T(8,128)(2,1)S(1)} %dynamic-slice_convert_fusion.1), channel_id=1, source_target_pairs={{0,1},{1,0},{2,3},{3,2},{4,5},{5,4},{6,7},{7,6},{8,9},{9,8},{10,11... | collective-permute-start | bytes 393224 | tf_op jit(solution)/shard_map/ppermute | solution.py:40
  51.7 10.0 %collective-permute-start.7 = (bf16[16,4096]{1,0:T(8,128)(2,1)S(1)}, bf16[16,4096]{1,0:T(8,128)(2,1)S(1)}, u32[]{:S(2)}, u32[]{:S(2)}) collective-permute-start(bf16[16,4096]{1,0:T(8,128)(2,1)S(1)} %dynamic-slice_convert_fusion), channel_id=1, source_target_pairs={{0,2},{1,3},{2,0},{3,1},{4,6},{5,7},{6,4},{7,5},{8,10},{9,11},{10,... | collective-permute-start | bytes 393224 | tf_op jit(solution)/shard_map/ppermute | solution.py:40
  55.9 7.2 %collective-permute-start.5 = (bf16[8,4096]{1,0:T(8,128)(2,1)S(1)}, bf16[8,4096]{1,0:T(8,128)(2,1)S(1)}, u32[]{:S(2)}, u32[]{:S(2)}) collective-permute-start(bf16[8,4096]{1,0:T(8,128)(2,1)S(1)} %dynamic-slice_convert_fusion.3), channel_id=1, source_target_pairs={{0,2},{1,3},{2,0},{3,1},{4,6},{5,7},{6,4},{7,5},{8,10},{9,11},{10,... | collective-permute-start | bytes 196616 | tf_op jit(solution)/shard_map/ppermute | solution.py:40
  61.7 4.3 %collective-permute-start.8 = (bf16[8,4096]{1,0:T(8,128)(2,1)S(1)}, bf16[8,4096]{1,0:T(8,128)(2,1)S(1)}, u32[]{:S(2)}, u32[]{:S(2)}) collective-permute-start(bf16[8,4096]{1,0:T(8,128)(2,1)S(1)} %dynamic-slice_convert_fusion.2), channel_id=1, source_target_pairs={{0,16},{16,0},{1,17},{17,1},{2,18},{18,2},{3,19},{19,3},{4,20},{20... | collective-permute-start | bytes 196616 | tf_op jit(solution)/shard_map/ppermute | solution.py:40
  67.4 6.7 %collective-permute-start.9 = (bf16[16,4224]{1,0:T(8,128)(2,1)S(1)}, bf16[16,4224]{1,0:T(8,128)(2,1)S(1)}, u32[]{:S(2)}, u32[]{:S(2)}) collective-permute-start(bf16[16,4224]{1,0:T(8,128)(2,1)S(1)} %token_rows.1), channel_id=1, source_target_pairs={{0,1},{1,0},{2,3},{3,2},{4,5},{5,4},{6,7},{7,6},{8,9},{9,8},{10,11... | collective-permute-start | bytes 405512 | tf_op jit(solution)/shard_map/ppermute | solution.py:40
  67.5 11.3 %collective-permute-start.10 = (bf16[16,4224]{1,0:T(8,128)(2,1)S(1)}, bf16[16,4224]{1,0:T(8,128)(2,1)S(1)}, u32[]{:S(2)}, u32[]{:S(2)}) collective-permute-start(bf16[16,4224]{1,0:T(8,128)(2,1)S(1)} %token_rows.1), channel_id=1, source_target_pairs={{0,2},{1,3},{2,0},{3,1},{4,6},{5,7},{6,4},{7,5},{8,10},{9,11},{10,... | collective-permute-start | bytes 405512 | tf_op jit(solution)/shard_map/ppermute | solution.py:40
  69.5 9.2 %collective-permute-start.11 = (bf16[16,4224]{1,0:T(8,128)(2,1)S(1)}, bf16[16,4224]{1,0:T(8,128)(2,1)S(1)}, u32[]{:S(2)}, u32[]{:S(2)}) collective-permute-start(bf16[16,4224]{1,0:T(8,128)(2,1)S(1)} %token_rows.1), channel_id=1, source_target_pairs={{0,3},{1,2},{2,1},{3,0},{4,7},{5,6},{6,5},{7,4},{8,11},{9,10},{10,... | collective-permute-start | bytes 405512 | tf_op jit(solution)/shard_map/ppermute | solution.py:40
  78.8 2.0 %collective-permute-start.14 = (bf16[64,4224]{1,0:T(8,128)(2,1)S(1)}, bf16[64,4224]{1,0:T(8,128)(2,1)S(1)}, u32[]{:S(2)}, u32[]{:S(2)}) collective-permute-start(bf16[64,4224]{1,0:T(8,128)(2,1)S(1)} %constant_dynamic-update-slice_fusion.2.refs_0_), channel_id=1, source_target_pairs={{0,4},{4,0},{8,12},{12,8},{1,5},{5,1},{9,13},{13,9},{2,6},{6,2},{1... | collective-permute-start | bytes 1622024 | tf_op jit(solution)/shard_map/ppermute | solution.py:40
  78.8 14.7 %collective-permute-start.12 = (bf16[64,4224]{1,0:T(8,128)(2,1)S(1)}, bf16[64,4224]{1,0:T(8,128)(2,1)S(1)}, u32[]{:S(2)}, u32[]{:S(2)}) collective-permute-start(bf16[64,4224]{1,0:T(8,128)(2,1)S(1)} %constant_dynamic-update-slice_fusion.2.refs_0_), channel_id=1, source_target_pairs={{0,16},{16,0},{1,17},{17,1},{2,18},{18,2},{3,19},{19,3},{4,20},{20... | collective-permute-start | bytes 1622024 | tf_op jit(solution)/shard_map/ppermute | solution.py:40
  79.4 14.3 %collective-permute-start.13 = (bf16[64,4224]{1,0:T(8,128)(2,1)S(1)}, bf16[64,4224]{1,0:T(8,128)(2,1)S(1)}, u32[]{:S(2)}, u32[]{:S(2)}) collective-permute-start(bf16[64,4224]{1,0:T(8,128)(2,1)S(1)} %constant_dynamic-update-slice_fusion.2.refs_0_), channel_id=1, source_target_pairs={{0,8},{4,12},{8,0},{12,4},{1,9},{5,13},{9,1},{13,5},{2,10},{6,14},... | collective-permute-start | bytes 1622024 | tf_op jit(solution)/shard_map/ppermute | solution.py:40
  93.7 2.7 %collective-permute-start.17 = (bf16[64,4224]{1,0:T(8,128)(2,1)S(1)}, bf16[64,4224]{1,0:T(8,128)(2,1)S(1)}, u32[]{:S(2)}, u32[]{:S(2)}) collective-permute-start(bf16[64,4224]{1,0:T(8,128)(2,1)S(1)} %collective-permute-done.13.refs_0_), channel_id=1, source_target_pairs={{0,4},{4,0},{8,12},{12,8},{1,5},{5,1},{9,13},{13,9},{2,6},{6,2},{1... | collective-permute-start | bytes 1622024 | tf_op jit(solution)/shard_map/ppermute | solution.py:40
  93.7 2.7 %collective-permute-start.18 = (bf16[64,4224]{1,0:T(8,128)(2,1)S(1)}, bf16[64,4224]{1,0:T(8,128)(2,1)S(1)}, u32[]{:S(2)}, u32[]{:S(2)}) collective-permute-start(bf16[64,4224]{1,0:T(8,128)(2,1)S(1)} %collective-permute-done.12.refs_2_), channel_id=1, source_target_pairs={{0,4},{4,0},{8,12},{12,8},{1,5},{5,1},{9,13},{13,9},{2,6},{6,2},{1... | collective-permute-start | bytes 1622024 | tf_op jit(solution)/shard_map/ppermute | solution.py:40
  94.3 8.5 %collective-permute-start.15 = (bf16[32,4224]{1,0:T(8,128)(2,1)S(1)}, bf16[32,4224]{1,0:T(8,128)(2,1)S(1)}, u32[]{:S(2)}, u32[]{:S(2)}) collective-permute-start(bf16[32,4224]{1,0:T(8,128)(2,1)S(1)} %slice.6), channel_id=1, source_target_pairs={{0,8},{4,12},{8,0},{12,4},{1,9},{5,13},{9,1},{13,5},{2,10},{6,14},... | collective-permute-start | bytes 811016 | tf_op jit(solution)/shard_map/ppermute | solution.py:40
  94.7 8.1 %collective-permute-start.16 = (bf16[32,4224]{1,0:T(8,128)(2,1)S(1)}, bf16[32,4224]{1,0:T(8,128)(2,1)S(1)}, u32[]{:S(2)}, u32[]{:S(2)}) collective-permute-start(bf16[32,4224]{1,0:T(8,128)(2,1)S(1)} %slice.7), channel_id=1, source_target_pairs={{0,16},{16,0},{1,17},{17,1},{2,18},{18,2},{3,19},{19,3},{4,20},{20... | collective-permute-start | bytes 811016 | tf_op jit(solution)/shard_map/ppermute | solution.py:40
  102.9 2.0 %collective-permute-start.19 = (bf16[64,4224]{1,0:T(8,128)(2,1)S(1)}, bf16[64,4224]{1,0:T(8,128)(2,1)S(1)}, u32[]{:S(2)}, u32[]{:S(2)}) collective-permute-start(bf16[64,4224]{1,0:T(8,128)(2,1)S(1)} %constant_dynamic-update-slice_fusion.refs_0_), channel_id=1, source_target_pairs={{0,4},{4,0},{8,12},{12,8},{1,5},{5,1},{9,13},{13,9},{2,6},{6,2},{1... | collective-permute-start | bytes 1622024 | tf_op jit(solution)/shard_map/ppermute | solution.py:40

commit v8 on v7

--- a/solution.py
+++ b/solution.py
@@ -68,23 +68,39 @@
     return copies
 
 
-def ffn_kernel(tile, place_ref, x_ref, up_ref, down_ref, *refs):
-    out_ref, own_ref, rows, total, up, down, up_sem, down_sem = refs
-    count, share, width = out_ref.shape
+def front_kernel(count, tile, depth, place_ref, slot_ref, length_ref, *refs):
+    x_ref, up_ref, down_ref, state_ref, tok_ref, w_ref = refs[:6]
+    sum_ref, own_ref = refs[6:8]
+    outs = refs[8 : 8 + count]
+    inputs, rows, total, up, down, states, weights, normed, queries, shares = refs[8 + count : -5]
+    x_sem, up_sem, down_sem, state_sem, w_sem = refs[-5:]
+    parts, share, enc_width = sum_ref.shape
     tiles = up_ref.shape[1] // tile
+    slots, tokens, width = state_ref.shape
+    columns = w_ref.shape[1]
+    steps = width // depth
+    x_copy = start_copies(lambda i: x_ref, lambda i: inputs, x_sem, 1)[0]
     up_copies = start_copies(
         lambda i: up_ref.at[:, pl.ds(i * tile, tile)], lambda i: up.at[i], up_sem, tiles
     )
     down_copies = start_copies(
         lambda i: down_ref.at[pl.ds(i * tile, tile), :], lambda i: down.at[i], down_sem, tiles
     )
-    rows[...] = x_ref[...].astype(jnp.float32).reshape(rows.shape)
+    state_copies = start_copies(
+        lambda i: state_ref.at[i], lambda i: states.at[i], state_sem, slots
+    )
+    w_copies = start_copies(
+        lambda i: w_ref.at[pl.ds(i * depth, depth), :], lambda i: weights.at[i], w_sem, steps
+    )
+
+    x_copy.wait()
+    rows[...] = inputs[...].astype(jnp.float32).reshape(rows.shape)
     start = pl.multiple_of(place_ref[2] * share, share)
     own_ref[...] = rows[pl.ds(start, share), :].astype(jnp.bfloat16)
-    normed = layer_norm(rows[...]).astype(jnp.bfloat16)
+    enc_normed = layer_norm(rows[...]).astype(jnp.bfloat16)
     for number in range(tiles):
         up_copies[number].wait()
-        hidden = dot(normed, up[number])
+        hidden = dot(enc_normed, up[number])
         inner = 0.5 * hidden * (1.0 + lax.erf(hidden * math.sqrt(0.5)))
         down_copies[number].wait()
         product = dot(inner.astype(jnp.bfloat16), down[number])
@@ -92,67 +108,12 @@
             total[...] = product
         else:
             total[...] += product
-    for part in range(count):
-        out_ref[part] = total[part * share : (part + 1) * share, :].astype(jnp.bfloat16)
-
-
-def in_hbm(values):
-    return pltpu.with_memory_space_constraint(values, pltpu.HBM)
-
-
-ANYWHERE = pl.BlockSpec(memory_space=pl.ANY)
-INSIDE = pl.BlockSpec(memory_space=pltpu.VMEM)
-
-
-def ffn(place, enc_in, up, down, count):
-    frames, utterances, width = enc_in.shape
-    rows = frames * utterances
-    share = rows // count
-    tile = 256
-    tiles = up.shape[1] // tile
-    return pl.pallas_call(
-        functools.partial(ffn_kernel, tile),
-        in_specs=[SCALARS, INSIDE, ANYWHERE, ANYWHERE],
-        out_specs=[INSIDE] * 2,
-        out_shape=[
-            jax.ShapeDtypeStruct((count, share, width), jnp.bfloat16),
-            jax.ShapeDtypeStruct((share, width), jnp.bfloat16),
-        ],
-        scratch_shapes=[
-            pltpu.VMEM((rows, width), jnp.float32),
-            pltpu.VMEM((rows, width), jnp.float32),
-            pltpu.VMEM((tiles, width, tile), jnp.bfloat16),
-            pltpu.VMEM((tiles, tile, width), jnp.bfloat16),
-            pltpu.SemaphoreType.DMA((tiles,)),
-            pltpu.SemaphoreType.DMA((tiles,)),
-        ],
-        cost_estimate=pl.CostEstimate(
-            flops=4 * rows * width * up.shape[1],
-            bytes_accessed=4 * width * up.shape[1],
-            transcendentals=rows * up.shape[1],
-        ),
-        compiler_params=pltpu.CompilerParams(vmem_limit_bytes=24 << 20),
-        name="encoder_ffn",
-    )(place, enc_in, in_hbm(up), in_hbm(down))
-
-
-def query_kernel(
-    count, depth, place_ref, slot_ref, length_ref, after_ref, x_ref, tok_ref, w_ref, *refs
-):
-    outs, (states, weights, normed, total, shares, x_sem, w_sem) = refs[:count], refs[count:]
-    slots, tokens, width = x_ref.shape
+    for part in range(parts):
+        sum_ref[part] = total[part * share : (part + 1) * share, :].astype(jnp.bfloat16)
+
     hyps = length_ref.shape[1]
     positions = tokens // hyps
-    columns = w_ref.shape[1]
     share = shares.shape[1] // 2
-    parts = width // columns
-    x_copies = start_copies(lambda i: x_ref.at[i], lambda i: states.at[i], x_sem, slots)
-    w_copies = start_copies(
-        lambda i: w_ref.at[pl.ds(i * depth, depth), :],
-        lambda i: weights.at[i],
-        w_sem,
-        width // depth,
-    )
     head_pos = place_ref[4]
     lane = lax.broadcasted_iota(jnp.int32, (1, tokens), 1)
     for slot in range(slots):
@@ -165,7 +126,7 @@
             start = start + length
         row = lax.broadcasted_iota(jnp.int32, (tokens, tokens), 0)
         move = jnp.where(order == row, 1.0, 0.0).astype(jnp.bfloat16)
-        x_copies[slot].wait()
+        state_copies[slot].wait()
         ordered = dot(move, states[slot])
         normed[slot * tokens : (slot + 1) * tokens, :] = square_norm(ordered).astype(jnp.bfloat16)
         share_row = lax.broadcasted_iota(jnp.int32, (share, tokens), 0)
@@ -179,14 +140,15 @@
         cell = lax.broadcasted_iota(jnp.int32, (share, columns), 1)
         packed = jnp.where(cell == 0, coarse, jnp.where(cell == 1, target - coarse * 256, 0))
         shares[slot, share:, :columns] = packed.astype(jnp.float32).astype(jnp.bfloat16)
-    for number in range(width // depth):
+    for number in range(steps):
         w_copies[number].wait()
         product = dot(normed[:, number * depth : (number + 1) * depth], weights[number])
         if number == 0:
-            total[...] = product
+            queries[...] = product
         else:
-            total[...] += product
+            queries[...] += product
     group = place_ref[1]
+    chunks = width // columns
     for distance in range(count):
         slot = jnp.int32(-1)
         for candidate in range(slots):
@@ -201,47 +163,81 @@
         @pl.when(slot >= 0)
         def _(out=out, slot=slot):
             start = pl.multiple_of(slot * tokens, tokens)
-            out[:tokens, :] = total[pl.ds(start, tokens), :].astype(jnp.bfloat16)
-            for part in range(parts):
+            out[:tokens, :] = queries[pl.ds(start, tokens), :].astype(jnp.bfloat16)
+            for part in range(chunks):
                 first = tokens + part * share
                 out[first : first + share, :] = shares[
                     slot, :share, part * columns : (part + 1) * columns
                 ]
-            out[tokens + parts * share :, :] = shares[slot, share:, :columns]
-
-
-def queries_of(place, slot_utt, lengths, after, states, targets, weights, count, share):
+            out[tokens + chunks * share :, :] = shares[slot, share:, :columns]
+
+
+def in_hbm(values):
+    return pltpu.with_memory_space_constraint(values, pltpu.HBM)
+
+
+ANYWHERE = pl.BlockSpec(memory_space=pl.ANY)
+INSIDE = pl.BlockSpec(memory_space=pltpu.VMEM)
+
+
+def front(place, slot_utt, lengths, enc_in, up, down, states, targets, weights, parts, count, share):
+    frames, utterances, enc_width = enc_in.shape
+    rows = frames * utterances
+    tile = 256
+    tiles = up.shape[1] // tile
     slots, tokens, width = states.shape
     columns = weights.shape[1]
     depth = 1024
-    rows = tokens + (width // columns + 1) * share
-    block = jax.ShapeDtypeStruct((rows, columns), jnp.bfloat16)
+    steps = width // depth
+    payload = tokens + (width // columns + 1) * share
     return pl.pallas_call(
-        functools.partial(query_kernel, count, depth),
-        in_specs=[SCALARS] * 3 + [ANYWHERE, ANYWHERE, INSIDE, ANYWHERE],
-        out_specs=[INSIDE] * count,
-        out_shape=[block] * count,
+        functools.partial(front_kernel, count, tile, depth),
+        in_specs=[SCALARS] * 3 + [ANYWHERE] * 4 + [INSIDE, ANYWHERE],
+        out_specs=[INSIDE] * (2 + count),
+        out_shape=[
+            jax.ShapeDtypeStruct((parts, rows // parts, enc_width), jnp.bfloat16),
+            jax.ShapeDtypeStruct((rows // parts, enc_width), jnp.bfloat16),
+        ]
+        + [jax.ShapeDtypeStruct((payload, columns), jnp.bfloat16)] * count,
         scratch_shapes=[
+            pltpu.VMEM(enc_in.shape, jnp.bfloat16),
+            pltpu.VMEM((rows, enc_width), jnp.float32),
+            pltpu.VMEM((rows, enc_width), jnp.float32),
+            pltpu.VMEM((tiles, enc_width, tile), jnp.bfloat16),
+            pltpu.VMEM((tiles, tile, enc_width), jnp.bfloat16),
             pltpu.VMEM(states.shape, jnp.bfloat16),
-            pltpu.VMEM((width // depth, depth, columns), jnp.bfloat16),
+            pltpu.VMEM((steps, depth, columns), jnp.bfloat16),
             pltpu.VMEM((slots * tokens, width), jnp.bfloat16),
             pltpu.VMEM((slots * tokens, columns), jnp.float32),
             pltpu.VMEM((slots, 2 * share, width), jnp.bfloat16),
+            pltpu.SemaphoreType.DMA((1,)),
+            pltpu.SemaphoreType.DMA((tiles,)),
+            pltpu.SemaphoreType.DMA((tiles,)),
             pltpu.SemaphoreType.DMA((slots,)),
-            pltpu.SemaphoreType.DMA((width // depth,)),
+            pltpu.SemaphoreType.DMA((steps,)),
         ],
         cost_estimate=pl.CostEstimate(
-            flops=2 * slots * tokens * width * columns,
-            bytes_accessed=2 * width * (columns + slots * tokens),
-            transcendentals=0,
+            flops=4 * rows * enc_width * up.shape[1] + 2 * slots * tokens * width * columns,
+            bytes_accessed=4 * enc_width * up.shape[1] + 2 * width * (columns + slots * tokens),
+            transcendentals=rows * up.shape[1],
         ),
-        compiler_params=pltpu.CompilerParams(vmem_limit_bytes=32 << 20),
-        name="hypothesis_queries",
-    )(place, slot_utt, lengths, after, in_hbm(states), targets, in_hbm(weights))
+        compiler_params=pltpu.CompilerParams(vmem_limit_bytes=40 << 20),
+        name="encoder_ffn_and_queries",
+    )(
+        place,
+        slot_utt,
+        lengths,
+        in_hbm(enc_in),
+        in_hbm(up),
+        in_hbm(down),
+        in_hbm(states),
+        targets,
+        in_hbm(weights),
+    )
 
 
 def kv_kernel(sections, utterances, widths, *refs):
-    parts_ref, own_ref, w_ref, after_ref, out_ref = refs
+    parts_ref, own_ref, w_ref, out_ref = refs
     rows = own_ref.shape[0]
     frames = rows // utterances
     total = own_ref[...].astype(jnp.float32)
@@ -273,11 +269,11 @@
                 out_ref[start : start + per_kv * frames, :] = block
 
 
-def keys_values_of(parts, own, weights, after, sections, utterances, widths):
+def keys_values_of(parts, own, weights, sections, utterances, widths):
     rows = sections * widths * own.shape[0]
     return pl.pallas_call(
         functools.partial(kv_kernel, sections, utterances, widths),
-        in_specs=[INSIDE] * 3 + [ANYWHERE],
+        in_specs=[INSIDE] * 3,
         out_specs=INSIDE,
         out_shape=jax.ShapeDtypeStruct((rows, 2 * HD), jnp.bfloat16),
         cost_estimate=pl.CostEstimate(
@@ -287,7 +283,7 @@
         ),
         compiler_params=pltpu.CompilerParams(vmem_limit_bytes=24 << 20),
         name="frame_keys_values",
-    )(parts, own, weights, after)
+    )(parts, own, weights)
 
 
 def choice_of_payload(place_ref, slot_ref, slots):
@@ -635,26 +631,25 @@
     place = jnp.stack([section_pos, group_pos, width_pos, vocab_start, head_pos])
     place = place.astype(jnp.int32)
 
-    parts, own_frames = ffn(place, enc_in, ffn_up, ffn_down, width_count)
-    parts = exchange(parts, "mp")
-
-    blocks = queries_of(
+    parts, own_frames, *blocks = front(
         place,
         slot_utt,
         hyp_len,
-        place,
+        enc_in,
+        ffn_up,
+        ffn_down,
         hyp_state.reshape(slot_count, slot_tokens, model_width),
         hyp_tok.reshape(slot_count, 1, slot_tokens),
         q_proj,
+        width_count,
         group_count,
         share_rows,
     )
+    parts = exchange(parts, "mp")
     crossing = blocks[2] + swap(blocks[3], "tm", 1)
     payloads = [blocks[0], swap(blocks[1], "tm", 1), swap(crossing, "tm", 2)]
 
-    sent = keys_values_of(
-        parts, own_frames, kv_proj, blocks[0], section_count, utterances, width_count
-    )
+    sent = keys_values_of(parts, own_frames, kv_proj, section_count, utterances, width_count)
     frames_all = all_devices * (frame_rows // width_count)
     keys_values = exchange(sent.reshape(all_devices, -1, 2 * HD), ALL).reshape(frames_all, 2 * HD)
 

time: 126 us -> 133 us (1.056)
  waiting for transfers between devices: 38.3 us -> 43.5 us
  local copies, waits for them, and re-layouts: 3.71 us -> 6.82 us
    all_to_all x2, waiting for transfers between devices: 8.71 us -> 13.7 us  [exchange(): return lax.all_to_all(blocks, axis, split_axis=0, concat_axis=0, tiled=True)]
    unnamed x21 -> x27, local copies, waits for them, and re-layouts: 3.26 us -> 5.67 us
    pallas_call x2 -> x1, Pallas kernels: 10.8 us -> 10.6 us  [front(): pl.pallas_call(functools.partial(front_kernel, count, tile, depth), in_sp...]
  transfers between devices with their start and end apart: 22 -> 22, of which waited for: 16 -> 16; matrix products, arithmetic and copies ran while one was open for 1% -> 2% of each run, Pallas kernels for 19% -> 14%
where the time goes in v8:
time: 133 us
  waiting for transfers between devices  43.5 us (33%)
  Pallas kernels  41.5 us (31%)
  starting transfers between devices  26.3 us (20%)
  blocking collectives  12.6 us (9%)
  local copies, waits for them, and re-layouts  6.82 us (5%)
  other arithmetic  1.9 us (1%)
    ppermute x20, waiting for transfers between devices, swap(): return lax.ppermute(values, axis, pairs)  29.8 us
    pallas_call x3, Pallas kernels, vocabulary_stats(): pl.pallas_call(functools.partial(vocabulary_kernel, head.shape[0] // 2),...  17.5 us
    ppermute x20, starting transfers between devices, swap(): return lax.ppermute(values, axis, pairs)  16.2 us
    all_to_all x2, waiting for transfers between devices, exchange(): return lax.all_to_all(blocks, axis, split_axis=0, concat_axis=0, tiled=True)  13.7 us
    all_to_all x1, blocking collectives, exchange(): return lax.all_to_all(blocks, axis, split_axis=0, concat_axis=0, tiled=True)  12.6 us
    pallas_call x1, Pallas kernels, front(): pl.pallas_call(functools.partial(front_kernel, count, tile, depth), in_sp...  10.6 us
    all_to_all x2, starting transfers between devices, exchange(): return lax.all_to_all(blocks, axis, split_axis=0, concat_axis=0, tiled=True)  10.1 us
    pallas_call x1, Pallas kernels, load_head(): pl.pallas_call(functools.partial(load_kernel, rows), in_specs=[ANYWHERE,...  5.77 us
  transfers between devices with their start and end apart: 22, of which 16 were waited for; matrix products, arithmetic and copies ran while one was open for 2% of the time, Pallas kernels for 14%

profile of v8, /device:TPU:0, one launch (start us, length us, event | category | flops | bytes accessed | tf_op | source)
XLA Modules:
  0.0 132.8 jit_solution(9721169455098251223)
XLA Ops:
  0.0 0.8 reshape.13.refs_4_
  0.8 0.1 stack.23.place_ref.refs_0_.first_ref
  0.9 0.7 copy-done.6
  1.5 0.7 copy-done.8
  2.2 10.6 %encoder_ffn_and_queries.1 = (bf16[4,32,1280]{2,1,0:T(8,128)(2,1)S(1)}, bf16[32,1280]{1,0:T(8,128)(2,1)S(1)}, bf16[272,512]{1,0:T(8,128)(2,1)S(1)}, bf16[272,512...) custom-call(s32[5]{0:T(128)S(1)} %stack.23.place_ref.refs_0_.first_ref, ...), custom_call_target="tpu_custom_call" | custom-call | flops 1912602624 | bytes 12845056 | tf_op jit(solution)/shard_map/encoder_ffn_and_queries/pallas_call | solution.py:193
  12.8 0.7 copy-done.2
  13.6 0.7 copy-done.3
  14.3 0.6 copy-done.4
  14.9 0.7 copy-done.12
  15.6 6.5 %all-to-all-start = ((bf16[4,32,1280]{2,1,0:T(8,128)(2,1)}), bf16[4,32,1280]{2,1,0:T(8,128)(2,1)S(1)}, u32[]{:S(2)}, u32[]{:S(2)}) async-start(bf16[4,32,1280]{2,1,0:T(8,128)(2,1)} %copy-done.2), calls=%async_computation | async-start | bytes 655360 | tf_op jit(solution)/shard_map/all_to_all | solution.py:30
  22.1 0.0 collective-permute-start.1
  22.1 0.5 collective-permute-start
  22.6 1.3 collective-permute-done.1
  23.8 1.7 %add.68 = bf16[272,512]{1,0:T(8,128)(2,1)} add(bf16[272,512]{1,0:T(8,128)(2,1)} %copy-done.3, bf16[272,512]{1,0:T(8,128)(2,1)S(1)} %collective-permute-done.1) | non-fusion elementwise | flops 139264 | bytes 835584 | tf_op jit(solution)/shard_map/add | solution.py:649
  25.6 1.5 %collective-permute-start.2 = (bf16[272,512]{1,0:T(8,128)(2,1)}, bf16[272,512]{1,0:T(8,128)(2,1)}, u32[]{:S(2)}, u32[]{:S(2)}) collective-permute-start(bf16[272,512]{1,0:T(8,128)(2,1)} %add.68), channel_id=1, source_target_pairs={{0,8},{4,12},{8,0},{12,4},{1,9},{5,13},{9,1},{13,5},{2,10},{6,14},... | collective-permute-start | bytes 835592 | tf_op jit(solution)/shard_map/ppermute | solution.py:40
  27.1 5.3 %all-to-all-done.refs_0_ = bf16[4,32,1280]{2,1,0:T(8,128)(2,1)S(1)} async-done(((bf16[4,32,1280]{2,1,0:T(8,128)(2,1)}), bf16[4,32,1280]{2,1,0:T(8,128)(2,1)S(1)}, u32[]{:S(2)}, u32[]{:S(2)}) %all-to-all-start) | async-done | bytes 327712 | tf_op jit(solution)/shard_map/all_to_all | solution.py:30
  32.4 0.9 copy-done.5
  33.3 0.9 frame_keys_values.1
  34.2 0.6 copy-done.1
  34.8 3.7 %all-to-all-start.1 = ((bf16[32,8,256]{2,1,0:T(8,128)(2,1)}), bf16[32,8,256]{2,1,0:T(8,128)(2,1)S(1)}, u32[]{:S(2)}, u32[]{:S(2)}) async-start(bf16[32,8,256]{2,1,0:T(8,128)(2,1)} %bitcast.9), calls=%async_computation.1 | async-start | bytes 262144 | tf_op jit(solution)/shard_map/all_to_all | solution.py:30
  38.5 0.0 collective-permute-done.refs_4_.refs_1_
  38.5 0.0 collective-permute-done.2.refs_5_.refs_2_
  38.5 8.4 %all-to-all-done.1 = bf16[32,8,256]{2,1,0:T(8,128)(2,1)S(1)} async-done(((bf16[32,8,256]{2,1,0:T(8,128)(2,1)}), bf16[32,8,256]{2,1,0:T(8,128)(2,1)S(1)}, u32[]{:S(2)}, u32[]{:S(2)}) %all-to-all-start.1) | async-done | bytes 131104 | tf_op jit(solution)/shard_map/all_to_all | solution.py:30
  46.9 3.5 %attention_projection.1 = (bf16[32,4096]{1,0:T(8,128)(2,1)S(1)}, bf16[32,4096]{1,0:T(8,128)(2,1)S(1)}, bf16[32,4096]{1,0:T(8,128)(2,1)S(1)}, bf16[32,4096]{1,0:T(8,128)(2,1)S(1)}) custom-call(s32[5]{0:T(128)S(1)} %stack.23.place_ref.refs_0_.first_ref, s32[8]{0:T(128)S(1)} %copy-done.7, s32[4]{0:T(128)S(1)} %copy-done.10, ...), custom_call_target="tpu_custom_call" | custom-call | flops 603979776 | bytes 5242880 | tf_op jit(solution)/shard_map/attention_projection/pallas_call | solution.py:362
  50.4 0.8 collective-permute-start.3
  51.2 0.0 collective-permute-start.6
  51.2 5.8 %vocabulary_rows.1 = (bf16[2000,4096]{1,0:T(8,128)(2,1)S(1)}, f32[8,128]{1,0:T(8,128)S(1)}) custom-call(bf16[32,4096]{1,0:T(8,128)(2,1)S(1)} %get-tuple-element.29.after_ref, bf16[2000,4096]{1,0:T(8,128)(2,1)} %head_ref.1), custom_call_target="tpu_custom_call" | custom-call | bytes 16384000 | tf_op jit(solution)/shard_map/vocabulary_rows/pallas_call | solution.py:444
  57.0 0.8 collective-permute-done.3
  57.8 0.1 convert_add_fusion.1
  57.9 1.3 collective-permute-start.4
  59.2 0.1 convert_add_fusion
  59.3 0.8 collective-permute-start.7
  60.1 3.3 %collective-permute-done.4 = bf16[16,4096]{1,0:T(8,128)(2,1)S(1)} collective-permute-done((bf16[16,4096]{1,0:T(8,128)(2,1)S(1)}, bf16[16,4096]{1,0:T(8,128)(2,1)S(1)}, u32[]{:S(2)}, u32[]{:S(2)}) %collective-permute-start.4) | collective-permute-done | bytes 131104 | tf_op jit(solution)/shard_map/ppermute | solution.py:40
  63.5 2.2 %collective-permute-start.5 = (bf16[8,4096]{1,0:T(8,128)(2,1)S(1)}, bf16[8,4096]{1,0:T(8,128)(2,1)S(1)}, u32[]{:S(2)}, u32[]{:S(2)}) collective-permute-start(bf16[8,4096]{1,0:T(8,128)(2,1)S(1)} %dynamic-slice_convert_fusion.3), channel_id=1, source_target_pairs={{0,2},{1,3},{2,0},{3,1},{4,6},{5,7},{6,4},{7,5},{8,10},{9,11},{10,... | collective-permute-start | bytes 196616 | tf_op jit(solution)/shard_map/ppermute | solution.py:40
  65.7 3.6 %collective-permute-done.7 = bf16[16,4096]{1,0:T(8,128)(2,1)S(1)} collective-permute-done((bf16[16,4096]{1,0:T(8,128)(2,1)S(1)}, bf16[16,4096]{1,0:T(8,128)(2,1)S(1)}, u32[]{:S(2)}, u32[]{:S(2)}) %collective-permute-start.7) | collective-permute-done | bytes 131104 | tf_op jit(solution)/shard_map/ppermute | solution.py:40
  69.3 0.8 collective-permute-start.8
  70.2 0.5 collective-permute-done.5.refs_4_
  70.7 3.0 %collective-permute-done.8.refs_6_ = bf16[8,4096]{1,0:T(8,128)(2,1)S(1)} collective-permute-done((bf16[8,4096]{1,0:T(8,128)(2,1)S(1)}, bf16[8,4096]{1,0:T(8,128)(2,1)S(1)}, u32[]{:S(2)}, u32[]{:S(2)}) %collective-permute-start.8) | collective-permute-done | bytes 65568 | tf_op jit(solution)/shard_map/ppermute | solution.py:40
  73.7 1.3 %token_rows.1 = bf16[16,4224]{1,0:T(8,128)(2,1)S(1)} custom-call(s32[5]{0:T(128)S(1)} %stack.23.place_ref.refs_0_.first_ref, s32[8]{0:T(128)S(1)} %copy-done.7, f32[8,128]{1,0:T(8,128)S(1)} %get-tuple-element.30.after_ref, bf16[272,512]{1,0:T(8,128)(2,1)S(1)} %get-tuple-element.23.refs_3_.refs_0_, bf16[272,512]{1,0:T(8,128)(2,1)S(1)} %collective-permute-done.refs_4_.refs_1_, ...), custom_call_target="tpu_custom_call" | custom-call | tf_op jit(solution)/shard_map/token_rows/pallas_call | solution.py:415
  75.0 0.1 collective-permute-start.9
  75.1 2.1 %collective-permute-start.10 = (bf16[16,4224]{1,0:T(8,128)(2,1)S(1)}, bf16[16,4224]{1,0:T(8,128)(2,1)S(1)}, u32[]{:S(2)}, u32[]{:S(2)}) collective-permute-start(bf16[16,4224]{1,0:T(8,128)(2,1)S(1)} %token_rows.1), channel_id=1, source_target_pairs={{0,2},{1,3},{2,0},{3,1},{4,6},{5,7},{6,4},{7,5},{8,10},{9,11},{10,... | collective-permute-start | bytes 405512 | tf_op jit(solution)/shard_map/ppermute | solution.py:40
  77.1 2.3 %collective-permute-start.11 = (bf16[16,4224]{1,0:T(8,128)(2,1)S(1)}, bf16[16,4224]{1,0:T(8,128)(2,1)S(1)}, u32[]{:S(2)}, u32[]{:S(2)}) collective-permute-start(bf16[16,4224]{1,0:T(8,128)(2,1)S(1)} %token_rows.1), channel_id=1, source_target_pairs={{0,3},{1,2},{2,1},{3,0},{4,7},{5,6},{6,5},{7,4},{8,11},{9,10},{10,... | collective-permute-start | bytes 405512 | tf_op jit(solution)/shard_map/ppermute | solution.py:40
  79.5 2.3 %collective-permute-done.9 = bf16[16,4224]{1,0:T(8,128)(2,1)S(1)} collective-permute-done((bf16[16,4224]{1,0:T(8,128)(2,1)S(1)}, bf16[16,4224]{1,0:T(8,128)(2,1)S(1)}, u32[]{:S(2)}, u32[]{:S(2)}) %collective-permute-start.9) | collective-permute-done | bytes 135200 | tf_op jit(solution)/shard_map/ppermute | solution.py:40
  81.8 4.5 %collective-permute-done.10 = bf16[16,4224]{1,0:T(8,128)(2,1)S(1)} collective-permute-done((bf16[16,4224]{1,0:T(8,128)(2,1)S(1)}, bf16[16,4224]{1,0:T(8,128)(2,1)S(1)}, u32[]{:S(2)}, u32[]{:S(2)}) %collective-permute-start.10) | collective-permute-done | bytes 135200 | tf_op jit(solution)/shard_map/ppermute | solution.py:40
  86.4 0.1 collective-permute-start.14
  86.5 0.5 collective-permute-start.12
  87.0 0.4 collective-permute-start.13
  87.4 1.0 collective-permute-done.14.refs_1_
  88.4 5.7 %vocabulary_scores.3.refs_0_ = f32[2,8,64]{2,1,0:T(8,128)S(1)} custom-call(s32[5]{0:T(128)S(1)} %stack.23.place_ref.refs_0_.first_ref, bf16[64,4224]{1,0:T(8,128)(2,1)S(1)} %constant_dynamic-update-slice_fusion.2.refs_0_, bf16[64,4224]{1,0:T(8,128)(2,1)S(1)} %collective-permute-done.14.refs_1_, bf16[2000,4096]{1,0:T(8,128)(2,1)S(1)} %get-tuple-element.34.refs_2_.refs_4_), custom_call_target="tpu_custom_call" | custom-call | flops 3145728000 | bytes 1048576 | tf_op jit(solution)/shard_map/vocabulary_scores/pallas_call | solution.py:500
  94.1 7.0 %collective-permute-done.12.refs_2_ = bf16[64,4224]{1,0:T(8,128)(2,1)S(1)} collective-permute-done((bf16[64,4224]{1,0:T(8,128)(2,1)S(1)}, bf16[64,4224]{1,0:T(8,128)(2,1)S(1)}, u32[]{:S(2)}, u32[]{:S(2)}) %collective-permute-start.12) | collective-permute-done | bytes 540704 | tf_op jit(solution)/shard_map/ppermute | solution.py:40
  101.2 0.2 collective-permute-done.13.refs_0_
  101.4 0.5 collective-permute-start.18
  101.9 0.5 collective-permute-start.15
  102.4 1.7 %collective-permute-start.16 = (bf16[32,4224]{1,0:T(8,128)(2,1)S(1)}, bf16[32,4224]{1,0:T(8,128)(2,1)S(1)}, u32[]{:S(2)}, u32[]{:S(2)}) collective-permute-start(bf16[32,4224]{1,0:T(8,128)(2,1)S(1)} %slice.7), channel_id=1, source_target_pairs={{0,16},{16,0},{1,17},{17,1},{2,18},{18,2},{3,19},{19,3},{4,20},{20... | collective-permute-start | bytes 811016 | tf_op jit(solution)/shard_map/ppermute | solution.py:40
  104.2 6.0 %vocabulary_scores.4.refs_1_ = f32[4,8,64]{2,1,0:T(8,128)S(1)} custom-call(s32[5]{0:T(128)S(1)} %stack.23.place_ref.refs_0_.first_ref, bf16[64,4224]{1,0:T(8,128)(2,1)S(1)} %collective-permute-done.13.refs_0_, bf16[64,4224]{1,0:T(8,128)(2,1)S(1)} %collective-permute-done.17.refs_1_, bf16[64,4224]{1,0:T(8,128)(2,1)S(1)} %collective-permute-done.12.refs_2_, ...), custom_call_target="tpu_custom_call" | custom-call | flops 6291456000 | bytes 2097152 | tf_op jit(solution)/shard_map/vocabulary_scores/pallas_call | solution.py:500
  110.2 0.2 collective-permute-done.15
  110.4 0.1 collective-permute-done.16
  110.6 0.0 copy-start.9
  110.6 0.1 collective-permute-start.19
  110.7 1.9 %collective-permute-done.19.refs_1_ = bf16[64,4224]{1,0:T(8,128)(2,1)S(1)} collective-permute-done((bf16[64,4224]{1,0:T(8,128)(2,1)S(1)}, bf16[64,4224]{1,0:T(8,128)(2,1)S(1)}, u32[]{:S(2)}, u32[]{:S(2)}) %collective-permute-start.19) | collective-permute-done | bytes 540704 | tf_op jit(solution)/shard_map/ppermute | solution.py:40
  112.6 5.7 %vocabulary_scores.5.refs_2_ = f32[2,8,64]{2,1,0:T(8,128)S(1)} custom-call(s32[5]{0:T(128)S(1)} %stack.23.place_ref.refs_0_.first_ref, bf16[64,4224]{1,0:T(8,128)(2,1)S(1)} %constant_dynamic-update-slice_fusion.refs_0_, bf16[64,4224]{1,0:T(8,128)(2,1)S(1)} %collective-permute-done.19.refs_1_, bf16[2000,4096]{1,0:T(8,128)(2,1)S(1)} %get-tuple-element.34.refs_2_.refs_4_), custom_call_target="tpu_custom_call" | custom-call | flops 3145728000 | bytes 1048576 | tf_op jit(solution)/shard_map/vocabulary_scores/pallas_call | solution.py:500
  118.3 0.6 statistics_by_group.1
  119.0 12.6 %all_to_all.15.every_ref = f32[32,8,128]{2,1,0:T(8,128)S(1)} all-to-all(f32[32,8,128]{2,1,0:T(8,128)S(1)} %statistics_by_group.1), channel_id=1, replica_groups=mesh['section'=2,'tm'=4,'mp'=4] {'section','tm','mp'}, dimensions={0} | all-to-all | bytes 262144 | tf_op jit(solution)/shard_map/all_to_all | solution.py:30
  131.5 1.3 hypothesis_scores.1
  (39 shorter events, 0.4 us)
Async XLA Ops:
  0.9 0.7 copy-start.6
  1.5 0.7 copy-start.8
  2.2 30.2 %copy-start = (bf16[1280,1024]{1,0:T(8,128)(2,1)S(1)}, bf16[1280,1024]{1,0:T(8,128)(2,1)}, u32[]{:S(2)}) copy-start(bf16[1280,1024]{1,0:T(8,128)(2,1)} %refs_2_.4) | copy-start | bytes 7864324
  12.8 0.7 copy-start.2
  13.6 0.7 copy-start.3
  14.3 0.6 copy-start.4
  14.9 0.7 copy-start.12
  15.6 6.5 %copy-start.11 = (bf16[272,512]{1,0:T(8,128)(2,1)}, bf16[272,512]{1,0:T(8,128)(2,1)S(1)}, u32[]{:S(2)}) copy-start(bf16[272,512]{1,0:T(8,128)(2,1)S(1)} %get-tuple-element.24) | copy-start | bytes 835588
  15.6 31.3 %copy-start.7 = (s32[8]{0:T(128)S(1)}, s32[8]{0:T(128)}, u32[]{:S(2)}) copy-start(s32[8]{0:T(128)} %slot_ref.7) | copy-start | bytes 100
  15.6 31.3 %copy-start.10 = (s32[4]{0:T(128)S(1)}, s32[4]{0:T(128)}, u32[]{:S(2)}) copy-start(s32[4]{0:T(128)} %refs_2_.5) | copy-start | bytes 52
  15.6 16.8 %all-to-all-start = ((bf16[4,32,1280]{2,1,0:T(8,128)(2,1)}), bf16[4,32,1280]{2,1,0:T(8,128)(2,1)S(1)}, u32[]{:S(2)}, u32[]{:S(2)}) async-start(bf16[4,32,1280]{2,1,0:T(8,128)(2,1)} %copy-done.2), calls=%async_computation | async-start | bytes 655360 | tf_op jit(solution)/shard_map/all_to_all | solution.py:30
  22.1 1.8 %collective-permute-start.1 = (bf16[272,512]{1,0:T(8,128)(2,1)}, bf16[272,512]{1,0:T(8,128)(2,1)S(1)}, u32[]{:S(2)}, u32[]{:S(2)}) collective-permute-start(bf16[272,512]{1,0:T(8,128)(2,1)} %copy-done.12), channel_id=1, source_target_pairs={{0,4},{4,0},{8,12},{12,8},{1,5},{5,1},{9,13},{13,9},{2,6},{6,2},{1... | collective-permute-start | bytes 835592 | tf_op jit(solution)/shard_map/ppermute | solution.py:40
  22.1 16.4 %collective-permute-start = (bf16[272,512]{1,0:T(8,128)(2,1)}, bf16[272,512]{1,0:T(8,128)(2,1)S(1)}, u32[]{:S(2)}, u32[]{:S(2)}) collective-permute-start(bf16[272,512]{1,0:T(8,128)(2,1)} %copy-done.11), channel_id=1, source_target_pairs={{0,4},{4,0},{8,12},{12,8},{1,5},{5,1},{9,13},{13,9},{2,6},{6,2},{1... | collective-permute-start | bytes 835592 | tf_op jit(solution)/shard_map/ppermute | solution.py:40
  25.6 12.9 %collective-permute-start.2 = (bf16[272,512]{1,0:T(8,128)(2,1)}, bf16[272,512]{1,0:T(8,128)(2,1)}, u32[]{:S(2)}, u32[]{:S(2)}) collective-permute-start(bf16[272,512]{1,0:T(8,128)(2,1)} %add.68), channel_id=1, source_target_pairs={{0,8},{4,12},{8,0},{12,4},{1,9},{5,13},{9,1},{13,5},{2,10},{6,14},... | collective-permute-start | bytes 835592 | tf_op jit(solution)/shard_map/ppermute | solution.py:40
  32.4 0.9 copy-start.5
  34.2 0.6 copy-start.1
  34.8 12.1 %all-to-all-start.1 = ((bf16[32,8,256]{2,1,0:T(8,128)(2,1)}), bf16[32,8,256]{2,1,0:T(8,128)(2,1)S(1)}, u32[]{:S(2)}, u32[]{:S(2)}) async-start(bf16[32,8,256]{2,1,0:T(8,128)(2,1)} %bitcast.9), calls=%async_computation.1 | async-start | bytes 262144 | tf_op jit(solution)/shard_map/all_to_all | solution.py:30
  50.4 7.4 %collective-permute-start.3 = (bf16[32,4096]{1,0:T(8,128)(2,1)S(1)}, bf16[32,4096]{1,0:T(8,128)(2,1)S(1)}, u32[]{:S(2)}, u32[]{:S(2)}) collective-permute-start(bf16[32,4096]{1,0:T(8,128)(2,1)S(1)} %get-tuple-element.31), channel_id=1, source_target_pairs={{0,16},{16,0},{1,17},{17,1},{2,18},{18,2},{3,19},{19,3},{4,20},{20... | collective-permute-start | bytes 786440 | tf_op jit(solution)/shard_map/ppermute | solution.py:40
  51.2 8.0 %collective-permute-start.6 = (bf16[32,4096]{1,0:T(8,128)(2,1)S(1)}, bf16[32,4096]{1,0:T(8,128)(2,1)S(1)}, u32[]{:S(2)}, u32[]{:S(2)}) collective-permute-start(bf16[32,4096]{1,0:T(8,128)(2,1)S(1)} %get-tuple-element.33), channel_id=1, source_target_pairs={{0,1},{1,0},{2,3},{3,2},{4,5},{5,4},{6,7},{7,6},{8,9},{9,8},{10,11... | collective-permute-start | bytes 786440 | tf_op jit(solution)/shard_map/ppermute | solution.py:40
  57.9 5.5 %collective-permute-start.4 = (bf16[16,4096]{1,0:T(8,128)(2,1)S(1)}, bf16[16,4096]{1,0:T(8,128)(2,1)S(1)}, u32[]{:S(2)}, u32[]{:S(2)}) collective-permute-start(bf16[16,4096]{1,0:T(8,128)(2,1)S(1)} %dynamic-slice_convert_fusion.1), channel_id=1, source_target_pairs={{0,1},{1,0},{2,3},{3,2},{4,5},{5,4},{6,7},{7,6},{8,9},{9,8},{10,11... | collective-permute-start | bytes 393224 | tf_op jit(solution)/shard_map/ppermute | solution.py:40
  59.3 10.0 %collective-permute-start.7 = (bf16[16,4096]{1,0:T(8,128)(2,1)S(1)}, bf16[16,4096]{1,0:T(8,128)(2,1)S(1)}, u32[]{:S(2)}, u32[]{:S(2)}) collective-permute-start(bf16[16,4096]{1,0:T(8,128)(2,1)S(1)} %dynamic-slice_convert_fusion), channel_id=1, source_target_pairs={{0,2},{1,3},{2,0},{3,1},{4,6},{5,7},{6,4},{7,5},{8,10},{9,11},{10,... | collective-permute-start | bytes 393224 | tf_op jit(solution)/shard_map/ppermute | solution.py:40
  63.5 7.2 %collective-permute-start.5 = (bf16[8,4096]{1,0:T(8,128)(2,1)S(1)}, bf16[8,4096]{1,0:T(8,128)(2,1)S(1)}, u32[]{:S(2)}, u32[]{:S(2)}) collective-permute-start(bf16[8,4096]{1,0:T(8,128)(2,1)S(1)} %dynamic-slice_convert_fusion.3), channel_id=1, source_target_pairs={{0,2},{1,3},{2,0},{3,1},{4,6},{5,7},{6,4},{7,5},{8,10},{9,11},{10,... | collective-permute-start | bytes 196616 | tf_op jit(solution)/shard_map/ppermute | solution.py:40
  69.3 4.3 %collective-permute-start.8 = (bf16[8,4096]{1,0:T(8,128)(2,1)S(1)}, bf16[8,4096]{1,0:T(8,128)(2,1)S(1)}, u32[]{:S(2)}, u32[]{:S(2)}) collective-permute-start(bf16[8,4096]{1,0:T(8,128)(2,1)S(1)} %dynamic-slice_convert_fusion.2), channel_id=1, source_target_pairs={{0,16},{16,0},{1,17},{17,1},{2,18},{18,2},{3,19},{19,3},{4,20},{20... | collective-permute-start | bytes 196616 | tf_op jit(solution)/shard_map/ppermute | solution.py:40
  75.0 6.8 %collective-permute-start.9 = (bf16[16,4224]{1,0:T(8,128)(2,1)S(1)}, bf16[16,4224]{1,0:T(8,128)(2,1)S(1)}, u32[]{:S(2)}, u32[]{:S(2)}) collective-permute-start(bf16[16,4224]{1,0:T(8,128)(2,1)S(1)} %token_rows.1), channel_id=1, source_target_pairs={{0,1},{1,0},{2,3},{3,2},{4,5},{5,4},{6,7},{7,6},{8,9},{9,8},{10,11... | collective-permute-start | bytes 405512 | tf_op jit(solution)/shard_map/ppermute | solution.py:40
  75.1 11.2 %collective-permute-start.10 = (bf16[16,4224]{1,0:T(8,128)(2,1)S(1)}, bf16[16,4224]{1,0:T(8,128)(2,1)S(1)}, u32[]{:S(2)}, u32[]{:S(2)}) collective-permute-start(bf16[16,4224]{1,0:T(8,128)(2,1)S(1)} %token_rows.1), channel_id=1, source_target_pairs={{0,2},{1,3},{2,0},{3,1},{4,6},{5,7},{6,4},{7,5},{8,10},{9,11},{10,... | collective-permute-start | bytes 405512 | tf_op jit(solution)/shard_map/ppermute | solution.py:40
  77.1 9.2 %collective-permute-start.11 = (bf16[16,4224]{1,0:T(8,128)(2,1)S(1)}, bf16[16,4224]{1,0:T(8,128)(2,1)S(1)}, u32[]{:S(2)}, u32[]{:S(2)}) collective-permute-start(bf16[16,4224]{1,0:T(8,128)(2,1)S(1)} %token_rows.1), channel_id=1, source_target_pairs={{0,3},{1,2},{2,1},{3,0},{4,7},{5,6},{6,5},{7,4},{8,11},{9,10},{10,... | collective-permute-start | bytes 405512 | tf_op jit(solution)/shard_map/ppermute | solution.py:40
  86.4 2.0 %collective-permute-start.14 = (bf16[64,4224]{1,0:T(8,128)(2,1)S(1)}, bf16[64,4224]{1,0:T(8,128)(2,1)S(1)}, u32[]{:S(2)}, u32[]{:S(2)}) collective-permute-start(bf16[64,4224]{1,0:T(8,128)(2,1)S(1)} %constant_dynamic-update-slice_fusion.2.refs_0_), channel_id=1, source_target_pairs={{0,4},{4,0},{8,12},{12,8},{1,5},{5,1},{9,13},{13,9},{2,6},{6,2},{1... | collective-permute-start | bytes 1622024 | tf_op jit(solution)/shard_map/ppermute | solution.py:40
  86.5 14.7 %collective-permute-start.12 = (bf16[64,4224]{1,0:T(8,128)(2,1)S(1)}, bf16[64,4224]{1,0:T(8,128)(2,1)S(1)}, u32[]{:S(2)}, u32[]{:S(2)}) collective-permute-start(bf16[64,4224]{1,0:T(8,128)(2,1)S(1)} %constant_dynamic-update-slice_fusion.2.refs_0_), channel_id=1, source_target_pairs={{0,16},{16,0},{1,17},{17,1},{2,18},{18,2},{3,19},{19,3},{4,20},{20... | collective-permute-start | bytes 1622024 | tf_op jit(solution)/shard_map/ppermute | solution.py:40
  87.0 14.3 %collective-permute-start.13 = (bf16[64,4224]{1,0:T(8,128)(2,1)S(1)}, bf16[64,4224]{1,0:T(8,128)(2,1)S(1)}, u32[]{:S(2)}, u32[]{:S(2)}) collective-permute-start(bf16[64,4224]{1,0:T(8,128)(2,1)S(1)} %constant_dynamic-update-slice_fusion.2.refs_0_), channel_id=1, source_target_pairs={{0,8},{4,12},{8,0},{12,4},{1,9},{5,13},{9,1},{13,5},{2,10},{6,14},... | collective-permute-start | bytes 1622024 | tf_op jit(solution)/shard_map/ppermute | solution.py:40
  101.4 2.8 %collective-permute-start.17 = (bf16[64,4224]{1,0:T(8,128)(2,1)S(1)}, bf16[64,4224]{1,0:T(8,128)(2,1)S(1)}, u32[]{:S(2)}, u32[]{:S(2)}) collective-permute-start(bf16[64,4224]{1,0:T(8,128)(2,1)S(1)} %collective-permute-done.13.refs_0_), channel_id=1, source_target_pairs={{0,4},{4,0},{8,12},{12,8},{1,5},{5,1},{9,13},{13,9},{2,6},{6,2},{1... | collective-permute-start | bytes 1622024 | tf_op jit(solution)/shard_map/ppermute | solution.py:40
  101.4 2.8 %collective-permute-start.18 = (bf16[64,4224]{1,0:T(8,128)(2,1)S(1)}, bf16[64,4224]{1,0:T(8,128)(2,1)S(1)}, u32[]{:S(2)}, u32[]{:S(2)}) collective-permute-start(bf16[64,4224]{1,0:T(8,128)(2,1)S(1)} %collective-permute-done.12.refs_2_), channel_id=1, source_target_pairs={{0,4},{4,0},{8,12},{12,8},{1,5},{5,1},{9,13},{13,9},{2,6},{6,2},{1... | collective-permute-start | bytes 1622024 | tf_op jit(solution)/shard_map/ppermute | solution.py:40
  101.9 8.5 %collective-permute-start.15 = (bf16[32,4224]{1,0:T(8,128)(2,1)S(1)}, bf16[32,4224]{1,0:T(8,128)(2,1)S(1)}, u32[]{:S(2)}, u32[]{:S(2)}) collective-permute-start(bf16[32,4224]{1,0:T(8,128)(2,1)S(1)} %slice.6), channel_id=1, source_target_pairs={{0,8},{4,12},{8,0},{12,4},{1,9},{5,13},{9,1},{13,5},{2,10},{6,14},... | collective-permute-start | bytes 811016 | tf_op jit(solution)/shard_map/ppermute | solution.py:40
  102.4 8.1 %collective-permute-start.16 = (bf16[32,4224]{1,0:T(8,128)(2,1)S(1)}, bf16[32,4224]{1,0:T(8,128)(2,1)S(1)}, u32[]{:S(2)}, u32[]{:S(2)}) collective-permute-start(bf16[32,4224]{1,0:T(8,128)(2,1)S(1)} %slice.7), channel_id=1, source_target_pairs={{0,16},{16,0},{1,17},{17,1},{2,18},{18,2},{3,19},{19,3},{4,20},{20... | collective-permute-start | bytes 811016 | tf_op jit(solution)/shard_map/ppermute | solution.py:40
  110.6 21.0 %copy-start.9 = (s32[2,8]{1,0:T(2,128)S(1)}, s32[2,8]{1,0:T(2,128)}, u32[]{:S(2)}) copy-start(s32[2,8]{1,0:T(2,128)} %length_ref.3) | copy-start | bytes 196
  110.6 2.0 %collective-permute-start.19 = (bf16[64,4224]{1,0:T(8,128)(2,1)S(1)}, bf16[64,4224]{1,0:T(8,128)(2,1)S(1)}, u32[]{:S(2)}, u32[]{:S(2)}) collective-permute-start(bf16[64,4224]{1,0:T(8,128)(2,1)S(1)} %constant_dynamic-update-slice_fusion.refs_0_), channel_id=1, source_target_pairs={{0,4},{4,0},{8,12},{12,8},{1,5},{5,1},{9,13},{13,9},{2,6},{6,2},{1... | collective-permute-start | bytes 1622024 | tf_op jit(solution)/shard_map/ppermute | solution.py:40

commit v9 on v7

--- a/solution.py
+++ b/solution.py
@@ -68,26 +68,18 @@
     return copies
 
 
-def ffn_kernel(tile, place_ref, x_ref, up_ref, down_ref, *refs):
-    out_ref, own_ref, rows, total, up, down, up_sem, down_sem = refs
+def ffn_kernel(tile, place_ref, after_ref, x_ref, up_ref, down_ref, *refs):
+    out_ref, own_ref, rows, total = refs
     count, share, width = out_ref.shape
     tiles = up_ref.shape[1] // tile
-    up_copies = start_copies(
-        lambda i: up_ref.at[:, pl.ds(i * tile, tile)], lambda i: up.at[i], up_sem, tiles
-    )
-    down_copies = start_copies(
-        lambda i: down_ref.at[pl.ds(i * tile, tile), :], lambda i: down.at[i], down_sem, tiles
-    )
     rows[...] = x_ref[...].astype(jnp.float32).reshape(rows.shape)
     start = pl.multiple_of(place_ref[2] * share, share)
     own_ref[...] = rows[pl.ds(start, share), :].astype(jnp.bfloat16)
     normed = layer_norm(rows[...]).astype(jnp.bfloat16)
     for number in range(tiles):
-        up_copies[number].wait()
-        hidden = dot(normed, up[number])
+        hidden = dot(normed, up_ref[:, number * tile : (number + 1) * tile])
         inner = 0.5 * hidden * (1.0 + lax.erf(hidden * math.sqrt(0.5)))
-        down_copies[number].wait()
-        product = dot(inner.astype(jnp.bfloat16), down[number])
+        product = dot(inner.astype(jnp.bfloat16), down_ref[number * tile : (number + 1) * tile, :])
         if number == 0:
             total[...] = product
         else:
@@ -104,15 +96,14 @@
 INSIDE = pl.BlockSpec(memory_space=pltpu.VMEM)
 
 
-def ffn(place, enc_in, up, down, count):
+def ffn(place, after, enc_in, up, down, count):
     frames, utterances, width = enc_in.shape
     rows = frames * utterances
     share = rows // count
     tile = 256
-    tiles = up.shape[1] // tile
     return pl.pallas_call(
         functools.partial(ffn_kernel, tile),
-        in_specs=[SCALARS, INSIDE, ANYWHERE, ANYWHERE],
+        in_specs=[SCALARS, ANYWHERE, INSIDE, INSIDE, INSIDE],
         out_specs=[INSIDE] * 2,
         out_shape=[
             jax.ShapeDtypeStruct((count, share, width), jnp.bfloat16),
@@ -121,10 +112,6 @@
         scratch_shapes=[
             pltpu.VMEM((rows, width), jnp.float32),
             pltpu.VMEM((rows, width), jnp.float32),
-            pltpu.VMEM((tiles, width, tile), jnp.bfloat16),
-            pltpu.VMEM((tiles, tile, width), jnp.bfloat16),
-            pltpu.SemaphoreType.DMA((tiles,)),
-            pltpu.SemaphoreType.DMA((tiles,)),
         ],
         cost_estimate=pl.CostEstimate(
             flops=4 * rows * width * up.shape[1],
@@ -133,59 +120,66 @@
         ),
         compiler_params=pltpu.CompilerParams(vmem_limit_bytes=24 << 20),
         name="encoder_ffn",
-    )(place, enc_in, in_hbm(up), in_hbm(down))
-
-
-def query_kernel(
-    count, depth, place_ref, slot_ref, length_ref, after_ref, x_ref, tok_ref, w_ref, *refs
-):
-    outs, (states, weights, normed, total, shares, x_sem, w_sem) = refs[:count], refs[count:]
+    )(place, after, enc_in, up, down)
+
+
+def query_kernel(count, depth, place_ref, slot_ref, length_ref, x_ref, tok_ref, w_ref, *refs):
+    outs, (states, weights, total, ordered, shares, x_sem, w_sem) = refs[:count], refs[count:]
     slots, tokens, width = x_ref.shape
-    hyps = length_ref.shape[1]
-    positions = tokens // hyps
+    hyps, positions = tok_ref.shape[1:]
     columns = w_ref.shape[1]
     share = shares.shape[1] // 2
     parts = width // columns
+    steps = width // depth
     x_copies = start_copies(lambda i: x_ref.at[i], lambda i: states.at[i], x_sem, slots)
     w_copies = start_copies(
-        lambda i: w_ref.at[pl.ds(i * depth, depth), :],
-        lambda i: weights.at[i],
-        w_sem,
-        width // depth,
-    )
+        lambda i: w_ref.at[pl.ds(i * depth, depth), :], lambda i: weights.at[i], w_sem, steps
+    )
+    scales = []
+    for slot in range(slots):
+        x_copies[slot].wait()
+        squares = jnp.zeros((tokens, depth), jnp.float32)
+        for number in range(steps):
+            part = states[slot, :, number * depth : (number + 1) * depth].astype(jnp.float32)
+            squares += part * part
+        mean = jnp.sum(squares, axis=1, keepdims=True) * (1.0 / width)
+        scales.append(lax.rsqrt(mean + 1e-06))
+    for number in range(steps):
+        w_copies[number].wait()
+        for slot in range(slots):
+            part = states[slot, :, number * depth : (number + 1) * depth].astype(jnp.float32)
+            product = dot((part * scales[slot]).astype(jnp.bfloat16), weights[number])
+            if number == 0:
+                total[slot] = product
+            else:
+                total[slot] += product
     head_pos = place_ref[4]
     lane = lax.broadcasted_iota(jnp.int32, (1, tokens), 1)
+    position = lax.broadcasted_iota(jnp.int32, (1, positions), 1)
+    share_place = (
+        lax.broadcasted_iota(jnp.int32, (share, 1), 0) * (tokens // share) + head_pos
+    )
     for slot in range(slots):
         order = jnp.full((1, tokens), -1, jnp.int32)
+        target = jnp.zeros((share, positions), jnp.int32)
         start = jnp.int32(0)
         for hyp in range(hyps):
             length = length_ref[slot, hyp]
             inside = (lane >= hyp * positions) & (lane < hyp * positions + length)
             order = jnp.where(inside, lane - hyp * positions + start, order)
+            here = jnp.where(position < length, position + start, -1)
+            target = jnp.where(here == share_place, tok_ref[slot, hyp : hyp + 1, :], target)
             start = start + length
         row = lax.broadcasted_iota(jnp.int32, (tokens, tokens), 0)
         move = jnp.where(order == row, 1.0, 0.0).astype(jnp.bfloat16)
-        x_copies[slot].wait()
-        ordered = dot(move, states[slot])
-        normed[slot * tokens : (slot + 1) * tokens, :] = square_norm(ordered).astype(jnp.bfloat16)
-        share_row = lax.broadcasted_iota(jnp.int32, (share, tokens), 0)
-        chosen = order == share_row * (tokens // share) + head_pos
-        mine = dot(jnp.where(chosen, 1.0, 0.0).astype(jnp.bfloat16), states[slot])
-        shares[slot, :share, :] = mine.astype(jnp.bfloat16)
-        target = jnp.sum(
-            jnp.where(chosen, tok_ref[slot], 0), axis=1, keepdims=True, dtype=jnp.int32
-        )
+        ordered[slot] = dot(move, total[slot].astype(jnp.bfloat16)).astype(jnp.bfloat16)
+        mine = jnp.where(order == share_place, 1.0, 0.0).astype(jnp.bfloat16)
+        shares[slot, :share, :] = dot(mine, states[slot]).astype(jnp.bfloat16)
+        target = jnp.sum(target, axis=1, keepdims=True, dtype=jnp.int32)
         coarse = target // 256
         cell = lax.broadcasted_iota(jnp.int32, (share, columns), 1)
         packed = jnp.where(cell == 0, coarse, jnp.where(cell == 1, target - coarse * 256, 0))
         shares[slot, share:, :columns] = packed.astype(jnp.float32).astype(jnp.bfloat16)
-    for number in range(width // depth):
-        w_copies[number].wait()
-        product = dot(normed[:, number * depth : (number + 1) * depth], weights[number])
-        if number == 0:
-            total[...] = product
-        else:
-            total[...] += product
     group = place_ref[1]
     for distance in range(count):
         slot = jnp.int32(-1)
@@ -200,8 +194,7 @@
 
         @pl.when(slot >= 0)
         def _(out=out, slot=slot):
-            start = pl.multiple_of(slot * tokens, tokens)
-            out[:tokens, :] = total[pl.ds(start, tokens), :].astype(jnp.bfloat16)
+            out[:tokens, :] = ordered[slot]
             for part in range(parts):
                 first = tokens + part * share
                 out[first : first + share, :] = shares[
@@ -210,7 +203,7 @@
             out[tokens + parts * share :, :] = shares[slot, share:, :columns]
 
 
-def queries_of(place, slot_utt, lengths, after, states, targets, weights, count, share):
+def queries_of(place, slot_utt, lengths, states, targets, weights, count, share):
     slots, tokens, width = states.shape
     columns = weights.shape[1]
     depth = 1024
@@ -218,14 +211,14 @@
     block = jax.ShapeDtypeStruct((rows, columns), jnp.bfloat16)
     return pl.pallas_call(
         functools.partial(query_kernel, count, depth),
-        in_specs=[SCALARS] * 3 + [ANYWHERE, ANYWHERE, INSIDE, ANYWHERE],
+        in_specs=[SCALARS] * 3 + [ANYWHERE, INSIDE, ANYWHERE],
         out_specs=[INSIDE] * count,
         out_shape=[block] * count,
         scratch_shapes=[
             pltpu.VMEM(states.shape, jnp.bfloat16),
             pltpu.VMEM((width // depth, depth, columns), jnp.bfloat16),
-            pltpu.VMEM((slots * tokens, width), jnp.bfloat16),
-            pltpu.VMEM((slots * tokens, columns), jnp.float32),
+            pltpu.VMEM((slots, tokens, columns), jnp.float32),
+            pltpu.VMEM((slots, tokens, columns), jnp.bfloat16),
             pltpu.VMEM((slots, 2 * share, width), jnp.bfloat16),
             pltpu.SemaphoreType.DMA((slots,)),
             pltpu.SemaphoreType.DMA((width // depth,)),
@@ -235,13 +228,13 @@
             bytes_accessed=2 * width * (columns + slots * tokens),
             transcendentals=0,
         ),
-        compiler_params=pltpu.CompilerParams(vmem_limit_bytes=32 << 20),
+        compiler_params=pltpu.CompilerParams(vmem_limit_bytes=20 << 20),
         name="hypothesis_queries",
-    )(place, slot_utt, lengths, after, in_hbm(states), targets, in_hbm(weights))
+    )(place, slot_utt, lengths, in_hbm(states), targets, in_hbm(weights))
 
 
 def kv_kernel(sections, utterances, widths, *refs):
-    parts_ref, own_ref, w_ref, after_ref, out_ref = refs
+    parts_ref, own_ref, w_ref, out_ref = refs
     rows = own_ref.shape[0]
     frames = rows // utterances
     total = own_ref[...].astype(jnp.float32)
@@ -273,11 +266,11 @@
                 out_ref[start : start + per_kv * frames, :] = block
 
 
-def keys_values_of(parts, own, weights, after, sections, utterances, widths):
+def keys_values_of(parts, own, weights, sections, utterances, widths):
     rows = sections * widths * own.shape[0]
     return pl.pallas_call(
         functools.partial(kv_kernel, sections, utterances, widths),
-        in_specs=[INSIDE] * 3 + [ANYWHERE],
+        in_specs=[INSIDE] * 3,
         out_specs=INSIDE,
         out_shape=jax.ShapeDtypeStruct((rows, 2 * HD), jnp.bfloat16),
         cost_estimate=pl.CostEstimate(
@@ -287,7 +280,7 @@
         ),
         compiler_params=pltpu.CompilerParams(vmem_limit_bytes=24 << 20),
         name="frame_keys_values",
-    )(parts, own, weights, after)
+    )(parts, own, weights)
 
 
 def choice_of_payload(place_ref, slot_ref, slots):
@@ -635,16 +628,12 @@
     place = jnp.stack([section_pos, group_pos, width_pos, vocab_start, head_pos])
     place = place.astype(jnp.int32)
 
-    parts, own_frames = ffn(place, enc_in, ffn_up, ffn_down, width_count)
-    parts = exchange(parts, "mp")
-
     blocks = queries_of(
         place,
         slot_utt,
         hyp_len,
-        place,
         hyp_state.reshape(slot_count, slot_tokens, model_width),
-        hyp_tok.reshape(slot_count, 1, slot_tokens),
+        hyp_tok,
         q_proj,
         group_count,
         share_rows,
@@ -652,9 +641,9 @@
     crossing = blocks[2] + swap(blocks[3], "tm", 1)
     payloads = [blocks[0], swap(blocks[1], "tm", 1), swap(crossing, "tm", 2)]
 
-    sent = keys_values_of(
-        parts, own_frames, kv_proj, blocks[0], section_count, utterances, width_count
-    )
+    parts, own_frames = ffn(place, blocks[0], enc_in, ffn_up, ffn_down, width_count)
+    parts = exchange(parts, "mp")
+    sent = keys_values_of(parts, own_frames, kv_proj, section_count, utterances, width_count)
     frames_all = all_devices * (frame_rows // width_count)
     keys_values = exchange(sent.reshape(all_devices, -1, 2 * HD), ALL).reshape(frames_all, 2 * HD)
 

time: 126 us -> 135 us (1.071)
  local copies, waits for them, and re-layouts: 3.71 us -> 12 us
  waiting for transfers between devices: 38.3 us -> 44 us
  Pallas kernels: 41.7 us -> 38 us
    unnamed x21 -> x39, local copies, waits for them, and re-layouts: 3.26 us -> 11.1 us
    all_to_all x2, waiting for transfers between devices: 8.71 us -> 14.3 us  [exchange(): return lax.all_to_all(blocks, axis, split_axis=0, concat_axis=0, tiled=True)]
    pallas_call x1, Pallas kernels: 4.89 us -> 2.01 us  [ffn(): pl.pallas_call(functools.partial(ffn_kernel, tile), in_specs=[SCALARS, AN...]
  transfers between devices with their start and end apart: 22 -> 22, of which waited for: 16 -> 16; matrix products, arithmetic and copies ran while one was open for 1% -> 1% of each run, Pallas kernels for 19% -> 14%
where the time goes in v9:
time: 135 us
  waiting for transfers between devices  44 us (33%)
  Pallas kernels  38 us (28%)
  starting transfers between devices  26.5 us (20%)
  blocking collectives  12.6 us (9%)
  local copies, waits for them, and re-layouts  12 us (9%)
    ppermute x20, waiting for transfers between devices, swap(): return lax.ppermute(values, axis, pairs)  29.7 us
    pallas_call x3, Pallas kernels, vocabulary_stats(): pl.pallas_call(functools.partial(vocabulary_kernel, head.shape[0] // 2),...  17.5 us
    ppermute x20, starting transfers between devices, swap(): return lax.ppermute(values, axis, pairs)  16.3 us
    all_to_all x2, waiting for transfers between devices, exchange(): return lax.all_to_all(blocks, axis, split_axis=0, concat_axis=0, tiled=True)  14.3 us
    all_to_all x1, blocking collectives, exchange(): return lax.all_to_all(blocks, axis, split_axis=0, concat_axis=0, tiled=True)  12.6 us
    unnamed x39, local copies, waits for them, and re-layouts  11.1 us
    all_to_all x2, starting transfers between devices, exchange(): return lax.all_to_all(blocks, axis, split_axis=0, concat_axis=0, tiled=True)  10.1 us
    pallas_call x1, Pallas kernels, load_head(): pl.pallas_call(functools.partial(load_kernel, rows), in_specs=[ANYWHERE,...  5.77 us
  transfers between devices with their start and end apart: 22, of which 16 were waited for; matrix products, arithmetic and copies ran while one was open for 1% of the time, Pallas kernels for 14%

profile of v9, /device:TPU:0, one launch (start us, length us, event | category | flops | bytes accessed | tf_op | source)
XLA Modules:
  0.0 134.5 jit_solution(6373612667924528548)
XLA Ops:
  0.0 0.7 stack.23.place_ref.refs_0_.first_ref
  0.7 1.0 copy-done.8
  1.7 0.7 copy-done.11
  2.3 0.7 copy-done.13
  3.0 0.7 copy-done.14
  3.7 5.2 %hypothesis_queries.1 = (bf16[272,512]{1,0:T(8,128)(2,1)S(1)}, bf16[272,512]{1,0:T(8,128)(2,1)S(1)}, bf16[272,512]{1,0:T(8,128)(2,1)S(1)}, bf16[272,512]{1,0:T(8,128)(2,1)S(1)}) custom-call(s32[5]{0:T(128)S(1)} %copy-done.8, s32[8]{0:T(128)S(1)} %copy-done.11, s32[2,8]{1,0:T(2,128)S(1)} %copy-done.14, bf16[2,128,4096]{2,1,0:T(8,128)(2,1)} %bitcast.9, ...), custom_call_target="tpu_custom_call" | custom-call | flops 1073741824 | bytes 6291456 | tf_op jit(solution)/shard_map/hypothesis_queries/pallas_call | solution.py:212
  8.9 0.7 copy-done.5
  9.7 0.7 copy-done.17
  10.4 0.7 copy-done.18
  11.1 1.9 %copy-done.1 = bf16[1280,1280]{1,0:T(8,128)(2,1)S(1)} copy-done((bf16[1280,1280]{1,0:T(8,128)(2,1)S(1)}, bf16[1280,1280]{1,0:T(8,128)(2,1)}, u32[]{:S(2)}) %copy-start.1) | copy-done | bytes 3276824
  13.0 2.0 %encoder_ffn.1 = (bf16[4,32,1280]{2,1,0:T(8,128)(2,1)S(1)}, bf16[32,1280]{1,0:T(8,128)(2,1)S(1)}) custom-call(s32[5]{0:T(128)S(1)} %copy-done.9, bf16[272,512]{1,0:T(8,128)(2,1)S(1)} %get-tuple-element.23.after_ref.refs_3_.refs_0_, bf16[32,4,1280]{2,1,0:T(4,128)(2,1)S(1)} %copy-done.3, bf16[1280,1280]{1,0:T(8,128)(2,1)S(1)} %copy-done, ...), custom_call_target="tpu_custom_call" | custom-call | flops 838860800 | bytes 6553600 | tf_op jit(solution)/shard_map/encoder_ffn/pallas_call | solution.py:104
  15.0 0.7 copy-done.4
  15.7 0.6 copy-done.6
  16.4 6.5 %all-to-all-start = ((bf16[4,32,1280]{2,1,0:T(8,128)(2,1)}), bf16[4,32,1280]{2,1,0:T(8,128)(2,1)S(1)}, u32[]{:S(2)}, u32[]{:S(2)}) async-start(bf16[4,32,1280]{2,1,0:T(8,128)(2,1)} %copy-done.4), calls=%async_computation | async-start | bytes 655360 | tf_op jit(solution)/shard_map/all_to_all | solution.py:30
  22.8 0.5 collective-permute-start
  23.3 1.3 collective-permute-done.1
  24.6 1.0 add.68
  25.6 1.6 %collective-permute-start.2 = (bf16[272,512]{1,0:T(8,128)(2,1)S(1)}, bf16[272,512]{1,0:T(8,128)(2,1)S(1)}, u32[]{:S(2)}, u32[]{:S(2)}) collective-permute-start(bf16[272,512]{1,0:T(8,128)(2,1)S(1)} %add.68), channel_id=1, source_target_pairs={{0,8},{4,12},{8,0},{12,4},{1,9},{5,13},{9,1},{13,5},{2,10},{6,14},... | collective-permute-start | bytes 835592 | tf_op jit(solution)/shard_map/ppermute | solution.py:40
  27.2 5.9 %all-to-all-done.refs_0_ = bf16[4,32,1280]{2,1,0:T(8,128)(2,1)S(1)} async-done(((bf16[4,32,1280]{2,1,0:T(8,128)(2,1)}), bf16[4,32,1280]{2,1,0:T(8,128)(2,1)S(1)}, u32[]{:S(2)}, u32[]{:S(2)}) %all-to-all-start) | async-done | bytes 327712 | tf_op jit(solution)/shard_map/all_to_all | solution.py:30
  33.1 1.7 %copy-done.2 = bf16[1280,1024]{1,0:T(8,128)(2,1)S(1)} copy-done((bf16[1280,1024]{1,0:T(8,128)(2,1)S(1)}, bf16[1280,1024]{1,0:T(8,128)(2,1)}, u32[]{:S(2)}) %copy-start.2) | copy-done | bytes 2621464
  34.9 0.9 copy-done.7
  35.8 1.5 %frame_keys_values.1 = bf16[256,256]{1,0:T(8,128)(2,1)} custom-call(bf16[4,32,1280]{2,1,0:T(8,128)(2,1)S(1)} %all-to-all-done.refs_0_, bf16[32,1280]{1,0:T(8,128)(2,1)S(1)} %copy-done.7, bf16[1280,1024]{1,0:T(8,128)(2,1)S(1)} %copy-done.2), custom_call_target="tpu_custom_call" | custom-call | flops 83886080 | bytes 2621440 | tf_op jit(solution)/shard_map/frame_keys_values/pallas_call | solution.py:271
  37.3 3.7 %all-to-all-start.1 = ((bf16[32,8,256]{2,1,0:T(8,128)(2,1)}), bf16[32,8,256]{2,1,0:T(8,128)(2,1)S(1)}, u32[]{:S(2)}, u32[]{:S(2)}) async-start(bf16[32,8,256]{2,1,0:T(8,128)(2,1)} %bitcast.6), calls=%async_computation.1 | async-start | bytes 262144 | tf_op jit(solution)/shard_map/all_to_all | solution.py:30
  41.0 8.4 %all-to-all-done.1 = bf16[32,8,256]{2,1,0:T(8,128)(2,1)S(1)} async-done(((bf16[32,8,256]{2,1,0:T(8,128)(2,1)}), bf16[32,8,256]{2,1,0:T(8,128)(2,1)S(1)}, u32[]{:S(2)}, u32[]{:S(2)}) %all-to-all-start.1) | async-done | bytes 131104 | tf_op jit(solution)/shard_map/all_to_all | solution.py:30
  49.4 3.1 %attention_projection.1 = (bf16[32,4096]{1,0:T(8,128)(2,1)S(1)}, bf16[32,4096]{1,0:T(8,128)(2,1)S(1)}, bf16[32,4096]{1,0:T(8,128)(2,1)S(1)}, bf16[32,4096]{1,0:T(8,128)(2,1)S(1)}) custom-call(s32[5]{0:T(128)S(1)} %copy-done.10, s32[8]{0:T(128)S(1)} %copy-done.12, s32[4]{0:T(128)S(1)} %copy-done.16, ...), custom_call_target="tpu_custom_call" | custom-call | flops 603979776 | bytes 5242880 | tf_op jit(solution)/shard_map/attention_projection/pallas_call | solution.py:359
  52.5 0.8 collective-permute-start.3
  53.4 5.8 %vocabulary_rows.1 = (bf16[2000,4096]{1,0:T(8,128)(2,1)S(1)}, f32[8,128]{1,0:T(8,128)S(1)}) custom-call(bf16[32,4096]{1,0:T(8,128)(2,1)S(1)} %get-tuple-element.29.after_ref, bf16[2000,4096]{1,0:T(8,128)(2,1)} %head_ref.1), custom_call_target="tpu_custom_call" | custom-call | bytes 16384000 | tf_op jit(solution)/shard_map/vocabulary_rows/pallas_call | solution.py:441
  59.1 0.8 collective-permute-done.3
  59.9 0.1 convert_add_fusion.1
  60.0 1.3 collective-permute-start.4
  61.3 0.1 convert_add_fusion
  61.4 0.8 collective-permute-start.7
  62.3 3.3 %collective-permute-done.4 = bf16[16,4096]{1,0:T(8,128)(2,1)S(1)} collective-permute-done((bf16[16,4096]{1,0:T(8,128)(2,1)S(1)}, bf16[16,4096]{1,0:T(8,128)(2,1)S(1)}, u32[]{:S(2)}, u32[]{:S(2)}) %collective-permute-start.4) | collective-permute-done | bytes 131104 | tf_op jit(solution)/shard_map/ppermute | solution.py:40
  65.6 2.2 %collective-permute-start.5 = (bf16[8,4096]{1,0:T(8,128)(2,1)S(1)}, bf16[8,4096]{1,0:T(8,128)(2,1)S(1)}, u32[]{:S(2)}, u32[]{:S(2)}) collective-permute-start(bf16[8,4096]{1,0:T(8,128)(2,1)S(1)} %dynamic-slice_convert_fusion.3), channel_id=1, source_target_pairs={{0,2},{1,3},{2,0},{3,1},{4,6},{5,7},{6,4},{7,5},{8,10},{9,11},{10,... | collective-permute-start | bytes 196616 | tf_op jit(solution)/shard_map/ppermute | solution.py:40
  67.8 3.6 %collective-permute-done.7 = bf16[16,4096]{1,0:T(8,128)(2,1)S(1)} collective-permute-done((bf16[16,4096]{1,0:T(8,128)(2,1)S(1)}, bf16[16,4096]{1,0:T(8,128)(2,1)S(1)}, u32[]{:S(2)}, u32[]{:S(2)}) %collective-permute-start.7) | collective-permute-done | bytes 131104 | tf_op jit(solution)/shard_map/ppermute | solution.py:40
  71.5 0.8 collective-permute-start.8
  72.3 0.5 collective-permute-done.5.refs_4_
  72.8 3.0 %collective-permute-done.8.refs_6_ = bf16[8,4096]{1,0:T(8,128)(2,1)S(1)} collective-permute-done((bf16[8,4096]{1,0:T(8,128)(2,1)S(1)}, bf16[8,4096]{1,0:T(8,128)(2,1)S(1)}, u32[]{:S(2)}, u32[]{:S(2)}) %collective-permute-start.8) | collective-permute-done | bytes 65568 | tf_op jit(solution)/shard_map/ppermute | solution.py:40
  75.8 0.9 token_rows.1
  76.7 0.1 collective-permute-start.9
  76.8 2.1 %collective-permute-start.10 = (bf16[16,4224]{1,0:T(8,128)(2,1)S(1)}, bf16[16,4224]{1,0:T(8,128)(2,1)S(1)}, u32[]{:S(2)}, u32[]{:S(2)}) collective-permute-start(bf16[16,4224]{1,0:T(8,128)(2,1)S(1)} %token_rows.1), channel_id=1, source_target_pairs={{0,2},{1,3},{2,0},{3,1},{4,6},{5,7},{6,4},{7,5},{8,10},{9,11},{10,... | collective-permute-start | bytes 405512 | tf_op jit(solution)/shard_map/ppermute | solution.py:40
  78.8 2.3 %collective-permute-start.11 = (bf16[16,4224]{1,0:T(8,128)(2,1)S(1)}, bf16[16,4224]{1,0:T(8,128)(2,1)S(1)}, u32[]{:S(2)}, u32[]{:S(2)}) collective-permute-start(bf16[16,4224]{1,0:T(8,128)(2,1)S(1)} %token_rows.1), channel_id=1, source_target_pairs={{0,3},{1,2},{2,1},{3,0},{4,7},{5,6},{6,5},{7,4},{8,11},{9,10},{10,... | collective-permute-start | bytes 405512 | tf_op jit(solution)/shard_map/ppermute | solution.py:40
  81.2 2.3 %collective-permute-done.9 = bf16[16,4224]{1,0:T(8,128)(2,1)S(1)} collective-permute-done((bf16[16,4224]{1,0:T(8,128)(2,1)S(1)}, bf16[16,4224]{1,0:T(8,128)(2,1)S(1)}, u32[]{:S(2)}, u32[]{:S(2)}) %collective-permute-start.9) | collective-permute-done | bytes 135200 | tf_op jit(solution)/shard_map/ppermute | solution.py:40
  83.5 4.5 %collective-permute-done.10 = bf16[16,4224]{1,0:T(8,128)(2,1)S(1)} collective-permute-done((bf16[16,4224]{1,0:T(8,128)(2,1)S(1)}, bf16[16,4224]{1,0:T(8,128)(2,1)S(1)}, u32[]{:S(2)}, u32[]{:S(2)}) %collective-permute-start.10) | collective-permute-done | bytes 135200 | tf_op jit(solution)/shard_map/ppermute | solution.py:40
  88.1 0.1 collective-permute-start.14
  88.2 0.5 collective-permute-start.12
  88.7 0.4 collective-permute-start.13
  89.1 1.0 collective-permute-done.14.refs_1_
  90.1 5.7 %vocabulary_scores.3.refs_0_ = f32[2,8,64]{2,1,0:T(8,128)S(1)} custom-call(s32[5]{0:T(128)S(1)} %copy-done.10, bf16[64,4224]{1,0:T(8,128)(2,1)S(1)} %constant_dynamic-update-slice_fusion.2.refs_0_, bf16[64,4224]{1,0:T(8,128)(2,1)S(1)} %collective-permute-done.14.refs_1_, bf16[2000,4096]{1,0:T(8,128)(2,1)S(1)} %get-tuple-element.34.refs_2_.refs_4_), custom_call_target="tpu_custom_call" | custom-call | flops 3145728000 | bytes 1048576 | tf_op jit(solution)/shard_map/vocabulary_scores/pallas_call | solution.py:497
  95.8 7.0 %collective-permute-done.12.refs_2_ = bf16[64,4224]{1,0:T(8,128)(2,1)S(1)} collective-permute-done((bf16[64,4224]{1,0:T(8,128)(2,1)S(1)}, bf16[64,4224]{1,0:T(8,128)(2,1)S(1)}, u32[]{:S(2)}, u32[]{:S(2)}) %collective-permute-start.12) | collective-permute-done | bytes 540704 | tf_op jit(solution)/shard_map/ppermute | solution.py:40
  102.9 0.2 collective-permute-done.13.refs_0_
  103.1 0.5 collective-permute-start.18
  103.6 0.5 collective-permute-start.15
  104.1 1.7 %collective-permute-start.16 = (bf16[32,4224]{1,0:T(8,128)(2,1)S(1)}, bf16[32,4224]{1,0:T(8,128)(2,1)S(1)}, u32[]{:S(2)}, u32[]{:S(2)}) collective-permute-start(bf16[32,4224]{1,0:T(8,128)(2,1)S(1)} %slice.7), channel_id=1, source_target_pairs={{0,16},{16,0},{1,17},{17,1},{2,18},{18,2},{3,19},{19,3},{4,20},{20... | collective-permute-start | bytes 811016 | tf_op jit(solution)/shard_map/ppermute | solution.py:40
  105.9 6.0 %vocabulary_scores.4.refs_1_ = f32[4,8,64]{2,1,0:T(8,128)S(1)} custom-call(s32[5]{0:T(128)S(1)} %copy-done.10, bf16[64,4224]{1,0:T(8,128)(2,1)S(1)} %collective-permute-done.13.refs_0_, bf16[64,4224]{1,0:T(8,128)(2,1)S(1)} %collective-permute-done.17.refs_1_, bf16[64,4224]{1,0:T(8,128)(2,1)S(1)} %collective-permute-done.12.refs_2_, ...), custom_call_target="tpu_custom_call" | custom-call | flops 6291456000 | bytes 2097152 | tf_op jit(solution)/shard_map/vocabulary_scores/pallas_call | solution.py:497
  111.9 0.2 collective-permute-done.15
  112.1 0.1 collective-permute-done.16
  112.3 0.0 copy-start.15
  112.3 0.1 collective-permute-start.19
  112.4 1.9 %collective-permute-done.19.refs_1_ = bf16[64,4224]{1,0:T(8,128)(2,1)S(1)} collective-permute-done((bf16[64,4224]{1,0:T(8,128)(2,1)S(1)}, bf16[64,4224]{1,0:T(8,128)(2,1)S(1)}, u32[]{:S(2)}, u32[]{:S(2)}) %collective-permute-start.19) | collective-permute-done | bytes 540704 | tf_op jit(solution)/shard_map/ppermute | solution.py:40
  114.3 5.7 %vocabulary_scores.5.refs_2_ = f32[2,8,64]{2,1,0:T(8,128)S(1)} custom-call(s32[5]{0:T(128)S(1)} %copy-done.10, bf16[64,4224]{1,0:T(8,128)(2,1)S(1)} %constant_dynamic-update-slice_fusion.refs_0_, bf16[64,4224]{1,0:T(8,128)(2,1)S(1)} %collective-permute-done.19.refs_1_, bf16[2000,4096]{1,0:T(8,128)(2,1)S(1)} %get-tuple-element.34.refs_2_.refs_4_), custom_call_target="tpu_custom_call" | custom-call | flops 3145728000 | bytes 1048576 | tf_op jit(solution)/shard_map/vocabulary_scores/pallas_call | solution.py:497
  120.0 0.6 statistics_by_group.1
  120.7 12.6 %all_to_all.15.every_ref = f32[32,8,128]{2,1,0:T(8,128)S(1)} all-to-all(f32[32,8,128]{2,1,0:T(8,128)S(1)} %statistics_by_group.1), channel_id=1, replica_groups=mesh['section'=2,'tm'=4,'mp'=4] {'section','tm','mp'}, dimensions={0} | all-to-all | bytes 262144 | tf_op jit(solution)/shard_map/all_to_all | solution.py:30
  133.2 1.3 hypothesis_scores.1
  (51 shorter events, 0.4 us)
Async XLA Ops:
  0.0 11.1 %copy-start = (bf16[1280,1280]{1,0:T(8,128)(2,1)S(1)}, bf16[1280,1280]{1,0:T(8,128)(2,1)}, u32[]{:S(2)}) copy-start(bf16[1280,1280]{1,0:T(8,128)(2,1)} %up_ref.1) | copy-start | bytes 9830404
  0.7 10.4 %copy-start.3 = (bf16[32,4,1280]{2,1,0:T(4,128)(2,1)S(1)}, bf16[32,4,1280]{2,1,0:T(4,128)(2,1)}, u32[]{:S(2)}) copy-start(bf16[32,4,1280]{2,1,0:T(4,128)(2,1)} %x_ref.1) | copy-start | bytes 983044
  0.7 1.0 copy-start.8
  1.6 0.7 copy-start.11
  2.3 0.7 copy-start.13
  3.0 0.7 copy-start.14
  3.7 7.4 %copy-start.9 = (s32[5]{0:T(128)S(1)}, s32[5]{0:T(128)}, u32[]{:S(2)}) copy-start(s32[5]{0:T(128)} %stack.23.place_ref.refs_0_.first_ref) | copy-start | bytes 64
  8.9 0.7 copy-start.5
  9.7 0.7 copy-start.17
  10.4 0.7 copy-start.18
  11.1 1.9 %copy-start.1 = (bf16[1280,1280]{1,0:T(8,128)(2,1)S(1)}, bf16[1280,1280]{1,0:T(8,128)(2,1)}, u32[]{:S(2)}) copy-start(bf16[1280,1280]{1,0:T(8,128)(2,1)} %down_ref.1) | copy-start | bytes 9830404
  15.0 0.7 copy-start.4
  15.7 0.6 copy-start.6
  16.4 33.0 %copy-start.10 = (s32[5]{0:T(128)S(1)}, s32[5]{0:T(128)}, u32[]{:S(2)}) copy-start(s32[5]{0:T(128)} %stack.23.place_ref.refs_0_.first_ref) | copy-start | bytes 64
  16.4 33.0 %copy-start.12 = (s32[8]{0:T(128)S(1)}, s32[8]{0:T(128)}, u32[]{:S(2)}) copy-start(s32[8]{0:T(128)} %slot_ref.7) | copy-start | bytes 100
  16.4 33.0 %copy-start.16 = (s32[4]{0:T(128)S(1)}, s32[4]{0:T(128)}, u32[]{:S(2)}) copy-start(s32[4]{0:T(128)} %refs_2_.3) | copy-start | bytes 52
  16.4 16.8 %all-to-all-start = ((bf16[4,32,1280]{2,1,0:T(8,128)(2,1)}), bf16[4,32,1280]{2,1,0:T(8,128)(2,1)S(1)}, u32[]{:S(2)}, u32[]{:S(2)}) async-start(bf16[4,32,1280]{2,1,0:T(8,128)(2,1)} %copy-done.4), calls=%async_computation | async-start | bytes 655360 | tf_op jit(solution)/shard_map/all_to_all | solution.py:30
  22.8 1.8 %collective-permute-start.1 = (bf16[272,512]{1,0:T(8,128)(2,1)}, bf16[272,512]{1,0:T(8,128)(2,1)S(1)}, u32[]{:S(2)}, u32[]{:S(2)}) collective-permute-start(bf16[272,512]{1,0:T(8,128)(2,1)} %copy-done.18), channel_id=1, source_target_pairs={{0,4},{4,0},{8,12},{12,8},{1,5},{5,1},{9,13},{13,9},{2,6},{6,2},{1... | collective-permute-start | bytes 835592 | tf_op jit(solution)/shard_map/ppermute | solution.py:40
  22.8 18.2 %collective-permute-start = (bf16[272,512]{1,0:T(8,128)(2,1)}, bf16[272,512]{1,0:T(8,128)(2,1)S(1)}, u32[]{:S(2)}, u32[]{:S(2)}) collective-permute-start(bf16[272,512]{1,0:T(8,128)(2,1)} %copy-done.17), channel_id=1, source_target_pairs={{0,4},{4,0},{8,12},{12,8},{1,5},{5,1},{9,13},{13,9},{2,6},{6,2},{1... | collective-permute-start | bytes 835592 | tf_op jit(solution)/shard_map/ppermute | solution.py:40
  25.6 15.4 %collective-permute-start.2 = (bf16[272,512]{1,0:T(8,128)(2,1)S(1)}, bf16[272,512]{1,0:T(8,128)(2,1)S(1)}, u32[]{:S(2)}, u32[]{:S(2)}) collective-permute-start(bf16[272,512]{1,0:T(8,128)(2,1)S(1)} %add.68), channel_id=1, source_target_pairs={{0,8},{4,12},{8,0},{12,4},{1,9},{5,13},{9,1},{13,5},{2,10},{6,14},... | collective-permute-start | bytes 835592 | tf_op jit(solution)/shard_map/ppermute | solution.py:40
  33.1 1.7 %copy-start.2 = (bf16[1280,1024]{1,0:T(8,128)(2,1)S(1)}, bf16[1280,1024]{1,0:T(8,128)(2,1)}, u32[]{:S(2)}) copy-start(bf16[1280,1024]{1,0:T(8,128)(2,1)} %refs_2_.2) | copy-start | bytes 7864324
  34.9 0.9 copy-start.7
  37.3 12.1 %all-to-all-start.1 = ((bf16[32,8,256]{2,1,0:T(8,128)(2,1)}), bf16[32,8,256]{2,1,0:T(8,128)(2,1)S(1)}, u32[]{:S(2)}, u32[]{:S(2)}) async-start(bf16[32,8,256]{2,1,0:T(8,128)(2,1)} %bitcast.6), calls=%async_computation.1 | async-start | bytes 262144 | tf_op jit(solution)/shard_map/all_to_all | solution.py:30
  52.5 7.4 %collective-permute-start.3 = (bf16[32,4096]{1,0:T(8,128)(2,1)S(1)}, bf16[32,4096]{1,0:T(8,128)(2,1)S(1)}, u32[]{:S(2)}, u32[]{:S(2)}) collective-permute-start(bf16[32,4096]{1,0:T(8,128)(2,1)S(1)} %get-tuple-element.31), channel_id=1, source_target_pairs={{0,16},{16,0},{1,17},{17,1},{2,18},{18,2},{3,19},{19,3},{4,20},{20... | collective-permute-start | bytes 786440 | tf_op jit(solution)/shard_map/ppermute | solution.py:40
  53.4 8.0 %collective-permute-start.6 = (bf16[32,4096]{1,0:T(8,128)(2,1)S(1)}, bf16[32,4096]{1,0:T(8,128)(2,1)S(1)}, u32[]{:S(2)}, u32[]{:S(2)}) collective-permute-start(bf16[32,4096]{1,0:T(8,128)(2,1)S(1)} %get-tuple-element.33), channel_id=1, source_target_pairs={{0,1},{1,0},{2,3},{3,2},{4,5},{5,4},{6,7},{7,6},{8,9},{9,8},{10,11... | collective-permute-start | bytes 786440 | tf_op jit(solution)/shard_map/ppermute | solution.py:40
  60.0 5.5 %collective-permute-start.4 = (bf16[16,4096]{1,0:T(8,128)(2,1)S(1)}, bf16[16,4096]{1,0:T(8,128)(2,1)S(1)}, u32[]{:S(2)}, u32[]{:S(2)}) collective-permute-start(bf16[16,4096]{1,0:T(8,128)(2,1)S(1)} %dynamic-slice_convert_fusion.1), channel_id=1, source_target_pairs={{0,1},{1,0},{2,3},{3,2},{4,5},{5,4},{6,7},{7,6},{8,9},{9,8},{10,11... | collective-permute-start | bytes 393224 | tf_op jit(solution)/shard_map/ppermute | solution.py:40
  61.4 10.0 %collective-permute-start.7 = (bf16[16,4096]{1,0:T(8,128)(2,1)S(1)}, bf16[16,4096]{1,0:T(8,128)(2,1)S(1)}, u32[]{:S(2)}, u32[]{:S(2)}) collective-permute-start(bf16[16,4096]{1,0:T(8,128)(2,1)S(1)} %dynamic-slice_convert_fusion), channel_id=1, source_target_pairs={{0,2},{1,3},{2,0},{3,1},{4,6},{5,7},{6,4},{7,5},{8,10},{9,11},{10,... | collective-permute-start | bytes 393224 | tf_op jit(solution)/shard_map/ppermute | solution.py:40
  65.6 7.2 %collective-permute-start.5 = (bf16[8,4096]{1,0:T(8,128)(2,1)S(1)}, bf16[8,4096]{1,0:T(8,128)(2,1)S(1)}, u32[]{:S(2)}, u32[]{:S(2)}) collective-permute-start(bf16[8,4096]{1,0:T(8,128)(2,1)S(1)} %dynamic-slice_convert_fusion.3), channel_id=1, source_target_pairs={{0,2},{1,3},{2,0},{3,1},{4,6},{5,7},{6,4},{7,5},{8,10},{9,11},{10,... | collective-permute-start | bytes 196616 | tf_op jit(solution)/shard_map/ppermute | solution.py:40
  71.5 4.3 %collective-permute-start.8 = (bf16[8,4096]{1,0:T(8,128)(2,1)S(1)}, bf16[8,4096]{1,0:T(8,128)(2,1)S(1)}, u32[]{:S(2)}, u32[]{:S(2)}) collective-permute-start(bf16[8,4096]{1,0:T(8,128)(2,1)S(1)} %dynamic-slice_convert_fusion.2), channel_id=1, source_target_pairs={{0,16},{16,0},{1,17},{17,1},{2,18},{18,2},{3,19},{19,3},{4,20},{20... | collective-permute-start | bytes 196616 | tf_op jit(solution)/shard_map/ppermute | solution.py:40
  76.7 6.8 %collective-permute-start.9 = (bf16[16,4224]{1,0:T(8,128)(2,1)S(1)}, bf16[16,4224]{1,0:T(8,128)(2,1)S(1)}, u32[]{:S(2)}, u32[]{:S(2)}) collective-permute-start(bf16[16,4224]{1,0:T(8,128)(2,1)S(1)} %token_rows.1), channel_id=1, source_target_pairs={{0,1},{1,0},{2,3},{3,2},{4,5},{5,4},{6,7},{7,6},{8,9},{9,8},{10,11... | collective-permute-start | bytes 405512 | tf_op jit(solution)/shard_map/ppermute | solution.py:40
  76.8 11.2 %collective-permute-start.10 = (bf16[16,4224]{1,0:T(8,128)(2,1)S(1)}, bf16[16,4224]{1,0:T(8,128)(2,1)S(1)}, u32[]{:S(2)}, u32[]{:S(2)}) collective-permute-start(bf16[16,4224]{1,0:T(8,128)(2,1)S(1)} %token_rows.1), channel_id=1, source_target_pairs={{0,2},{1,3},{2,0},{3,1},{4,6},{5,7},{6,4},{7,5},{8,10},{9,11},{10,... | collective-permute-start | bytes 405512 | tf_op jit(solution)/shard_map/ppermute | solution.py:40
  78.8 9.2 %collective-permute-start.11 = (bf16[16,4224]{1,0:T(8,128)(2,1)S(1)}, bf16[16,4224]{1,0:T(8,128)(2,1)S(1)}, u32[]{:S(2)}, u32[]{:S(2)}) collective-permute-start(bf16[16,4224]{1,0:T(8,128)(2,1)S(1)} %token_rows.1), channel_id=1, source_target_pairs={{0,3},{1,2},{2,1},{3,0},{4,7},{5,6},{6,5},{7,4},{8,11},{9,10},{10,... | collective-permute-start | bytes 405512 | tf_op jit(solution)/shard_map/ppermute | solution.py:40
  88.1 2.0 %collective-permute-start.14 = (bf16[64,4224]{1,0:T(8,128)(2,1)S(1)}, bf16[64,4224]{1,0:T(8,128)(2,1)S(1)}, u32[]{:S(2)}, u32[]{:S(2)}) collective-permute-start(bf16[64,4224]{1,0:T(8,128)(2,1)S(1)} %constant_dynamic-update-slice_fusion.2.refs_0_), channel_id=1, source_target_pairs={{0,4},{4,0},{8,12},{12,8},{1,5},{5,1},{9,13},{13,9},{2,6},{6,2},{1... | collective-permute-start | bytes 1622024 | tf_op jit(solution)/shard_map/ppermute | solution.py:40
  88.2 14.7 %collective-permute-start.12 = (bf16[64,4224]{1,0:T(8,128)(2,1)S(1)}, bf16[64,4224]{1,0:T(8,128)(2,1)S(1)}, u32[]{:S(2)}, u32[]{:S(2)}) collective-permute-start(bf16[64,4224]{1,0:T(8,128)(2,1)S(1)} %constant_dynamic-update-slice_fusion.2.refs_0_), channel_id=1, source_target_pairs={{0,16},{16,0},{1,17},{17,1},{2,18},{18,2},{3,19},{19,3},{4,20},{20... | collective-permute-start | bytes 1622024 | tf_op jit(solution)/shard_map/ppermute | solution.py:40
  88.7 14.3 %collective-permute-start.13 = (bf16[64,4224]{1,0:T(8,128)(2,1)S(1)}, bf16[64,4224]{1,0:T(8,128)(2,1)S(1)}, u32[]{:S(2)}, u32[]{:S(2)}) collective-permute-start(bf16[64,4224]{1,0:T(8,128)(2,1)S(1)} %constant_dynamic-update-slice_fusion.2.refs_0_), channel_id=1, source_target_pairs={{0,8},{4,12},{8,0},{12,4},{1,9},{5,13},{9,1},{13,5},{2,10},{6,14},... | collective-permute-start | bytes 1622024 | tf_op jit(solution)/shard_map/ppermute | solution.py:40
  103.1 2.8 %collective-permute-start.17 = (bf16[64,4224]{1,0:T(8,128)(2,1)S(1)}, bf16[64,4224]{1,0:T(8,128)(2,1)S(1)}, u32[]{:S(2)}, u32[]{:S(2)}) collective-permute-start(bf16[64,4224]{1,0:T(8,128)(2,1)S(1)} %collective-permute-done.13.refs_0_), channel_id=1, source_target_pairs={{0,4},{4,0},{8,12},{12,8},{1,5},{5,1},{9,13},{13,9},{2,6},{6,2},{1... | collective-permute-start | bytes 1622024 | tf_op jit(solution)/shard_map/ppermute | solution.py:40
  103.1 2.8 %collective-permute-start.18 = (bf16[64,4224]{1,0:T(8,128)(2,1)S(1)}, bf16[64,4224]{1,0:T(8,128)(2,1)S(1)}, u32[]{:S(2)}, u32[]{:S(2)}) collective-permute-start(bf16[64,4224]{1,0:T(8,128)(2,1)S(1)} %collective-permute-done.12.refs_2_), channel_id=1, source_target_pairs={{0,4},{4,0},{8,12},{12,8},{1,5},{5,1},{9,13},{13,9},{2,6},{6,2},{1... | collective-permute-start | bytes 1622024 | tf_op jit(solution)/shard_map/ppermute | solution.py:40
  103.6 8.5 %collective-permute-start.15 = (bf16[32,4224]{1,0:T(8,128)(2,1)S(1)}, bf16[32,4224]{1,0:T(8,128)(2,1)S(1)}, u32[]{:S(2)}, u32[]{:S(2)}) collective-permute-start(bf16[32,4224]{1,0:T(8,128)(2,1)S(1)} %slice.6), channel_id=1, source_target_pairs={{0,8},{4,12},{8,0},{12,4},{1,9},{5,13},{9,1},{13,5},{2,10},{6,14},... | collective-permute-start | bytes 811016 | tf_op jit(solution)/shard_map/ppermute | solution.py:40
  104.1 8.1 %collective-permute-start.16 = (bf16[32,4224]{1,0:T(8,128)(2,1)S(1)}, bf16[32,4224]{1,0:T(8,128)(2,1)S(1)}, u32[]{:S(2)}, u32[]{:S(2)}) collective-permute-start(bf16[32,4224]{1,0:T(8,128)(2,1)S(1)} %slice.7), channel_id=1, source_target_pairs={{0,16},{16,0},{1,17},{17,1},{2,18},{18,2},{3,19},{19,3},{4,20},{20... | collective-permute-start | bytes 811016 | tf_op jit(solution)/shard_map/ppermute | solution.py:40
  112.3 21.0 %copy-start.15 = (s32[2,8]{1,0:T(2,128)S(1)}, s32[2,8]{1,0:T(2,128)}, u32[]{:S(2)}) copy-start(s32[2,8]{1,0:T(2,128)} %length_ref.3) | copy-start | bytes 196
  112.3 2.0 %collective-permute-start.19 = (bf16[64,4224]{1,0:T(8,128)(2,1)S(1)}, bf16[64,4224]{1,0:T(8,128)(2,1)S(1)}, u32[]{:S(2)}, u32[]{:S(2)}) collective-permute-start(bf16[64,4224]{1,0:T(8,128)(2,1)S(1)} %constant_dynamic-update-slice_fusion.refs_0_), channel_id=1, source_target_pairs={{0,4},{4,0},{8,12},{12,8},{1,5},{5,1},{9,13},{13,9},{2,6},{6,2},{1... | collective-permute-start | bytes 1622024 | tf_op jit(solution)/shard_map/ppermute | solution.py:40

commit v10 on v9

--- a/solution.py
+++ b/solution.py
@@ -45,6 +45,28 @@
 
 
 SCALARS = pl.BlockSpec(memory_space=pltpu.SMEM)
+PLACES = 5
+
+
+class Scalars:
+    def __init__(self, ref, slots, utterances, hyps):
+        self.ref = ref
+        self.slots = slots
+        self.frames_at = PLACES + slots
+        self.lengths_at = self.frames_at + utterances
+        self.hyps = hyps
+
+    def place(self, number):
+        return self.ref[number]
+
+    def slot(self, number):
+        return self.ref[PLACES + number]
+
+    def frames(self, utterance):
+        return self.ref[self.frames_at + utterance]
+
+    def length(self, slot, hyp):
+        return self.ref[self.lengths_at + slot * self.hyps + hyp]
 
 
 def dot(left, right):
@@ -68,22 +90,37 @@
     return copies
 
 
-def ffn_kernel(tile, place_ref, after_ref, x_ref, up_ref, down_ref, *refs):
-    out_ref, own_ref, rows, total = refs
+def ffn_kernel(steps, view, info_ref, after_ref, x_ref, up_ref, down_ref, *refs):
+    out_ref, own_ref, inputs, rows, up, down, x_sem, up_sem, down_sem = refs
     count, share, width = out_ref.shape
-    tiles = up_ref.shape[1] // tile
-    rows[...] = x_ref[...].astype(jnp.float32).reshape(rows.shape)
-    start = pl.multiple_of(place_ref[2] * share, share)
+    hidden_units = up_ref.shape[1]
+    up_rows, down_rows = width // steps, hidden_units // steps
+    x_copy = start_copies(lambda i: x_ref, lambda i: inputs, x_sem, 1)[0]
+    up_copies = start_copies(
+        lambda i: up_ref.at[pl.ds(i * up_rows, up_rows), :], lambda i: up.at[i], up_sem, steps
+    )
+    down_copies = start_copies(
+        lambda i: down_ref.at[pl.ds(i * down_rows, down_rows), :],
+        lambda i: down.at[i],
+        down_sem,
+        steps,
+    )
+    x_copy.wait()
+    rows[...] = inputs[...].astype(jnp.float32).reshape(rows.shape)
+    start = pl.multiple_of(view(info_ref).place(2) * share, share)
     own_ref[...] = rows[pl.ds(start, share), :].astype(jnp.bfloat16)
     normed = layer_norm(rows[...]).astype(jnp.bfloat16)
-    for number in range(tiles):
-        hidden = dot(normed, up_ref[:, number * tile : (number + 1) * tile])
-        inner = 0.5 * hidden * (1.0 + lax.erf(hidden * math.sqrt(0.5)))
-        product = dot(inner.astype(jnp.bfloat16), down_ref[number * tile : (number + 1) * tile, :])
-        if number == 0:
-            total[...] = product
-        else:
-            total[...] += product
+    hidden = None
+    for number in range(steps):
+        up_copies[number].wait()
+        product = dot(normed[:, number * up_rows : (number + 1) * up_rows], up[number])
+        hidden = product if hidden is None else hidden + product
+    inner = (0.5 * hidden * (1.0 + lax.erf(hidden * math.sqrt(0.5)))).astype(jnp.bfloat16)
+    total = None
+    for number in range(steps):
+        down_copies[number].wait()
+        product = dot(inner[:, number * down_rows : (number + 1) * down_rows], down[number])
+        total = product if total is None else total + product
     for part in range(count):
         out_ref[part] = total[part * share : (part + 1) * share, :].astype(jnp.bfloat16)
 
@@ -96,22 +133,27 @@
 INSIDE = pl.BlockSpec(memory_space=pltpu.VMEM)
 
 
-def ffn(place, after, enc_in, up, down, count):
+def ffn(view, info, after, enc_in, up, down, count):
     frames, utterances, width = enc_in.shape
     rows = frames * utterances
     share = rows // count
-    tile = 256
+    steps = 5
     return pl.pallas_call(
-        functools.partial(ffn_kernel, tile),
-        in_specs=[SCALARS, ANYWHERE, INSIDE, INSIDE, INSIDE],
+        functools.partial(ffn_kernel, steps, view),
+        in_specs=[SCALARS] + [ANYWHERE] * 4,
         out_specs=[INSIDE] * 2,
         out_shape=[
-            jax.ShapeDtypeStruct((count, share, width), jnp.bfloat16),
+            pltpu.HBM((count, share, width), jnp.bfloat16),
             jax.ShapeDtypeStruct((share, width), jnp.bfloat16),
         ],
         scratch_shapes=[
+            pltpu.VMEM(enc_in.shape, jnp.bfloat16),
             pltpu.VMEM((rows, width), jnp.float32),
-            pltpu.VMEM((rows, width), jnp.float32),
+            pltpu.VMEM((steps, width // steps, up.shape[1]), jnp.bfloat16),
+            pltpu.VMEM((steps, up.shape[1] // steps, width), jnp.bfloat16),
+            pltpu.SemaphoreType.DMA((1,)),
+            pltpu.SemaphoreType.DMA((steps,)),
+            pltpu.SemaphoreType.DMA((steps,)),
         ],
         cost_estimate=pl.CostEstimate(
             flops=4 * rows * width * up.shape[1],
@@ -120,10 +162,10 @@
         ),
         compiler_params=pltpu.CompilerParams(vmem_limit_bytes=24 << 20),
         name="encoder_ffn",
-    )(place, after, enc_in, up, down)
-
-
-def query_kernel(count, depth, place_ref, slot_ref, length_ref, x_ref, tok_ref, w_ref, *refs):
+    )(info, after, in_hbm(enc_in), in_hbm(up), in_hbm(down))
+
+
+def query_kernel(count, depth, view, info_ref, x_ref, tok_ref, w_ref, *refs):
     outs, (states, weights, total, ordered, shares, x_sem, w_sem) = refs[:count], refs[count:]
     slots, tokens, width = x_ref.shape
     hyps, positions = tok_ref.shape[1:]
@@ -153,7 +195,8 @@
                 total[slot] = product
             else:
                 total[slot] += product
-    head_pos = place_ref[4]
+    info = view(info_ref)
+    head_pos = info.place(4)
     lane = lax.broadcasted_iota(jnp.int32, (1, tokens), 1)
     position = lax.broadcasted_iota(jnp.int32, (1, positions), 1)
     share_place = (
@@ -164,7 +207,7 @@
         target = jnp.zeros((share, positions), jnp.int32)
         start = jnp.int32(0)
         for hyp in range(hyps):
-            length = length_ref[slot, hyp]
+            length = info.length(slot, hyp)
             inside = (lane >= hyp * positions) & (lane < hyp * positions + length)
             order = jnp.where(inside, lane - hyp * positions + start, order)
             here = jnp.where(position < length, position + start, -1)
@@ -180,11 +223,11 @@
         cell = lax.broadcasted_iota(jnp.int32, (share, columns), 1)
         packed = jnp.where(cell == 0, coarse, jnp.where(cell == 1, target - coarse * 256, 0))
         shares[slot, share:, :columns] = packed.astype(jnp.float32).astype(jnp.bfloat16)
-    group = place_ref[1]
+    group = info.place(1)
     for distance in range(count):
         slot = jnp.int32(-1)
         for candidate in range(slots):
-            holds = slot_ref[group * slots + candidate] == group ^ distance
+            holds = info.slot(group * slots + candidate) == group ^ distance
             slot = jnp.where(holds, candidate, slot)
         out = outs[distance]
 
@@ -203,15 +246,15 @@
             out[tokens + parts * share :, :] = shares[slot, share:, :columns]
 
 
-def queries_of(place, slot_utt, lengths, states, targets, weights, count, share):
+def queries_of(view, info, states, targets, weights, count, share):
     slots, tokens, width = states.shape
     columns = weights.shape[1]
     depth = 1024
     rows = tokens + (width // columns + 1) * share
-    block = jax.ShapeDtypeStruct((rows, columns), jnp.bfloat16)
+    block = pltpu.HBM((rows, columns), jnp.bfloat16)
     return pl.pallas_call(
-        functools.partial(query_kernel, count, depth),
-        in_specs=[SCALARS] * 3 + [ANYWHERE, INSIDE, ANYWHERE],
+        functools.partial(query_kernel, count, depth, view),
+        in_specs=[SCALARS, ANYWHERE, INSIDE, ANYWHERE],
         out_specs=[INSIDE] * count,
         out_shape=[block] * count,
         scratch_shapes=[
@@ -230,7 +273,7 @@
         ),
         compiler_params=pltpu.CompilerParams(vmem_limit_bytes=20 << 20),
         name="hypothesis_queries",
-    )(place, slot_utt, lengths, in_hbm(states), targets, in_hbm(weights))
+    )(info, in_hbm(states), in_hbm(targets), in_hbm(weights))
 
 
 def kv_kernel(sections, utterances, widths, *refs):
@@ -272,7 +315,7 @@
         functools.partial(kv_kernel, sections, utterances, widths),
         in_specs=[INSIDE] * 3,
         out_specs=INSIDE,
-        out_shape=jax.ShapeDtypeStruct((rows, 2 * HD), jnp.bfloat16),
+        out_shape=pltpu.HBM((rows, 2 * HD), jnp.bfloat16),
         cost_estimate=pl.CostEstimate(
             flops=2 * own.shape[0] * weights.shape[0] * weights.shape[1],
             bytes_accessed=2 * weights.shape[0] * weights.shape[1],
@@ -283,27 +326,27 @@
     )(parts, own, weights)
 
 
-def choice_of_payload(place_ref, slot_ref, slots):
-    group = place_ref[1]
+def choice_of_payload(info, slots):
+    group = info.place(1)
     source = jnp.int32(0)
-    for slot in range(slot_ref.shape[0]):
-        source = jnp.where(slot_ref[slot] == group, slot // slots, source)
+    for slot in range(info.slots):
+        source = jnp.where(info.slot(slot) == group, slot // slots, source)
     return jnp.minimum(source ^ group, 2)
 
 
-def attention_kernel(count, slots, capacity, pieces, sections, widths, tile, *refs):
-    place_ref, slot_ref, frame_ref = refs[:3]
-    payloads, (kv_ref, w_ref) = refs[3 : 3 + count], refs[3 + count : 5 + count]
-    outs = refs[5 + count : 5 + count + 2 * len(pieces)]
-    weights, picked, context, w_sem = refs[5 + count + 2 * len(pieces) :]
+def attention_kernel(count, slots, capacity, pieces, sections, widths, tile, view, info_ref, *refs):
+    info = view(info_ref)
+    payloads, (kv_ref, w_ref) = refs[:count], refs[count : 2 + count]
+    outs = refs[2 + count : 2 + count + 2 * len(pieces)]
+    weights, picked, context, w_sem = refs[2 + count + 2 * len(pieces) :]
     tokens, columns = capacity, w_ref.shape[0]
     tiles = w_ref.shape[1] // tile
     w_copies = start_copies(
         lambda i: w_ref.at[:, pl.ds(i * tile, tile)], lambda i: weights.at[i], w_sem, tiles
     )
-    source = choice_of_payload(place_ref, slot_ref, slots)
-    section_pos = place_ref[0]
-    frame_limit = frame_ref[place_ref[1]]
+    source = choice_of_payload(info, slots)
+    section_pos = info.place(0)
+    frame_limit = info.frames(info.place(1))
     for distance in range(count):
 
         @pl.when(source == distance)
@@ -322,7 +365,7 @@
         context[:, head * HD : (head + 1) * HD] = dot(chances, values).astype(jnp.bfloat16)
     to = lax.broadcasted_iota(jnp.int32, (tokens, tokens), 0)
     come = lax.broadcasted_iota(jnp.int32, (tokens, tokens), 1)
-    low_bit = place_ref[2] % 2
+    low_bit = info.place(2) % 2
     size = widths * pieces[0]
     block = to % size // pieces[0]
     section = jnp.where(to < size, 1 - section_pos, section_pos)
@@ -345,22 +388,22 @@
             first += out.shape[0]
 
 
-def attend(place, slot_utt, frame_len, payloads, keys_values, weights, pieces, sections, widths, slots):
+def attend(view, info, payloads, keys_values, weights, pieces, sections, widths, slots):
     count = len(payloads)
     columns, width = weights.shape
     capacity = sum(pieces) * sections * widths
     tile = 1024
     tiles = width // tile
     shapes = [
-        jax.ShapeDtypeStruct((piece * widths, width), jnp.bfloat16)
+        kind((piece * widths, width), jnp.bfloat16)
         for piece in pieces
-        for _ in range(2)
+        for kind in (pltpu.HBM, jax.ShapeDtypeStruct)
     ]
     return pl.pallas_call(
         functools.partial(
-            attention_kernel, count, slots, capacity, pieces, sections, widths, tile
+            attention_kernel, count, slots, capacity, pieces, sections, widths, tile, view
         ),
-        in_specs=[SCALARS] * 3 + [INSIDE] * (count + 1) + [ANYWHERE],
+        in_specs=[SCALARS] + [INSIDE] * (count + 1) + [ANYWHERE],
         out_specs=[INSIDE] * len(shapes),
         out_shape=shapes,
         scratch_shapes=[
@@ -376,16 +419,16 @@
         ),
         compiler_params=pltpu.CompilerParams(vmem_limit_bytes=24 << 20),
         name="attention_projection",
-    )(place, slot_utt, frame_len, *payloads, keys_values, in_hbm(weights))
-
-
-def norm_kernel(count, slots, tokens, pieces, place_ref, slot_ref, after_ref, *refs):
+    )(info, *payloads, keys_values, in_hbm(weights))
+
+
+def norm_kernel(count, slots, tokens, pieces, view, info_ref, after_ref, *refs):
     payloads, blocks = refs[:count], refs[count : count + 2 * len(pieces)]
     out_ref, picked, total = refs[count + 2 * len(pieces) :]
     rows, width = total.shape
     columns = picked.shape[1]
     share = picked.shape[0] // (width // columns + 1)
-    source = choice_of_payload(place_ref, slot_ref, slots)
+    source = choice_of_payload(view(info_ref), slots)
     for choice in range(count):
 
         @pl.when(source == choice)
@@ -405,22 +448,22 @@
     out_ref[:, width:] = picked[last : last + rows, :LANES]
 
 
-def normed_rows(place, slot_utt, after, payloads, blocks, pieces, tokens, slots):
+def normed_rows(view, info, after, payloads, blocks, pieces, tokens, slots):
     width = blocks[0].shape[1]
     rows = sum(pieces)
     columns = payloads[0].shape[1]
     return pl.pallas_call(
-        functools.partial(norm_kernel, len(payloads), slots, tokens, pieces),
-        in_specs=[SCALARS] * 2 + [ANYWHERE] + [INSIDE] * (len(payloads) + len(blocks)),
+        functools.partial(norm_kernel, len(payloads), slots, tokens, pieces, view),
+        in_specs=[SCALARS, ANYWHERE] + [INSIDE] * (len(payloads) + len(blocks)),
         out_specs=INSIDE,
-        out_shape=jax.ShapeDtypeStruct((rows, width + LANES), jnp.bfloat16),
+        out_shape=pltpu.HBM((rows, width + LANES), jnp.bfloat16),
         scratch_shapes=[
             pltpu.VMEM((payloads[0].shape[0] - tokens, columns), jnp.bfloat16),
             pltpu.VMEM((rows, width), jnp.float32),
         ],
         compiler_params=pltpu.CompilerParams(vmem_limit_bytes=16 << 20),
         name="token_rows",
-    )(place, slot_utt, after, *payloads, *blocks)
+    )(info, after, *payloads, *blocks)
 
 
 def load_kernel(rows, after_ref, head_ref, out_ref, token_ref, semaphores):
@@ -489,7 +532,7 @@
             ]
 
 
-def vocabulary_stats(place, sets, head):
+def vocabulary_stats(info, sets, head):
     share = sets[0].shape[0]
     count = len(sets)
     width = head.shape[1]
@@ -510,23 +553,24 @@
         ),
         compiler_params=pltpu.CompilerParams(vmem_limit_bytes=16 << 20),
         name="vocabulary_scores",
-    )(place, *sets, pltpu.with_memory_space_constraint(head, pltpu.VMEM))
-
-
-def spread_kernel(sections, groups, widths, place_ref, slot_ref, *refs):
+    )(info, *sets, pltpu.with_memory_space_constraint(head, pltpu.VMEM))
+
+
+def spread_kernel(sections, groups, widths, view, info_ref, *refs):
+    info = view(info_ref)
     stats, (out_ref, table, block) = refs[:-3], refs[-3:]
     share = table.shape[2]
     first = 0
     for stat in stats:
         table[first : first + stat.shape[0]] = stat[...]
         first += stat.shape[0]
-    slots = slot_ref.shape[0] // groups
+    slots = info.slots // groups
     block[...] = jnp.zeros_like(block)
     for group in range(groups):
         for slot in range(slots):
-            utterance = jnp.maximum(slot_ref[group * slots + slot], 0)
+            utterance = jnp.maximum(info.slot(group * slots + slot), 0)
             for section in range(sections):
-                at = (section ^ place_ref[0]) * groups + (utterance ^ place_ref[1])
+                at = (section ^ info.place(0)) * groups + (utterance ^ info.place(1))
                 block[group, 3 * slot : 3 * slot + 3, section * share : (section + 1) * share] = (
                     table[at][0:3, :]
                 )
@@ -536,26 +580,25 @@
                 out_ref[(section * groups + group) * widths + width] = block[group]
 
 
-def spread_stats(place, slot_utt, stats, sections, groups, widths):
+def spread_stats(view, info, stats, slots, sections, groups, widths):
     share = stats[0].shape[2]
-    assert 3 * slot_utt.shape[0] // groups <= 8
+    assert 3 * slots <= 8
     return pl.pallas_call(
-        functools.partial(spread_kernel, sections, groups, widths),
-        in_specs=[SCALARS] * 2 + [INSIDE] * len(stats),
+        functools.partial(spread_kernel, sections, groups, widths, view),
+        in_specs=[SCALARS] + [INSIDE] * len(stats),
         out_specs=INSIDE,
-        out_shape=jax.ShapeDtypeStruct(
-            (sections * groups * widths, 8, sections * share), jnp.float32
-        ),
+        out_shape=pltpu.HBM((sections * groups * widths, 8, sections * share), jnp.float32),
         scratch_shapes=[
             pltpu.VMEM((sections * groups, 8, share), jnp.float32),
             pltpu.VMEM((groups, 8, sections * share), jnp.float32),
         ],
         compiler_params=pltpu.CompilerParams(vmem_limit_bytes=16 << 20),
         name="statistics_by_group",
-    )(place, slot_utt, *stats)
-
-
-def score_kernel(sections, widths, place_ref, slot_ref, length_ref, every_ref, out_ref):
+    )(info, *stats)
+
+
+def score_kernel(sections, widths, view, info_ref, every_ref, out_ref):
+    info = view(info_ref)
     slots, hyps = out_ref.shape
     lanes = every_ref.shape[2]
     share = lanes // sections // widths
@@ -573,25 +616,25 @@
         scores = jnp.zeros((1, hyps), jnp.float32)
         start = jnp.int32(0)
         for hyp in range(hyps):
-            length = length_ref[slot, hyp]
+            length = info.length(slot, hyp)
             valid = (order >= start) & (order < start + length)
             summed = jnp.sum(jnp.where(valid, logp, 0.0), axis=1, keepdims=True)
             mean = summed / jnp.full((1, 1), length, jnp.int32).astype(jnp.float32)
             scores = jnp.where(column == hyp, mean + math.log(V), scores)
             start = start + length
-        filled = slot_ref[place_ref[1] * slots + slot] >= 0
+        filled = info.slot(info.place(1) * slots + slot) >= 0
         out_ref[slot : slot + 1, :] = jnp.where(filled, scores, 0.0)
 
 
-def hypothesis_scores(place, slot_utt, lengths, every, slots, hyps, sections, widths):
+def hypothesis_scores(view, info, every, slots, hyps, sections, widths):
     return pl.pallas_call(
-        functools.partial(score_kernel, sections, widths),
-        in_specs=[SCALARS] * 3 + [INSIDE],
+        functools.partial(score_kernel, sections, widths, view),
+        in_specs=[SCALARS, INSIDE],
         out_specs=INSIDE,
         out_shape=jax.ShapeDtypeStruct((slots, hyps), jnp.float32),
         compiler_params=pltpu.CompilerParams(vmem_limit_bytes=16 << 20),
         name="hypothesis_scores",
-    )(place, slot_utt, lengths, every)
+    )(info, every)
 
 
 def near_device(
@@ -626,12 +669,14 @@
     ) * head.shape[0]
     head_pos = section_pos * width_count + width_pos
     place = jnp.stack([section_pos, group_pos, width_pos, vocab_start, head_pos])
-    place = place.astype(jnp.int32)
+    info = jnp.concatenate([place.astype(jnp.int32), slot_utt, frame_len, hyp_len.reshape(-1)])
+    view = functools.partial(
+        Scalars, slots=slot_utt.shape[0], utterances=utterances, hyps=hyp_count
+    )
 
     blocks = queries_of(
-        place,
-        slot_utt,
-        hyp_len,
+        view,
+        info,
         hyp_state.reshape(slot_count, slot_tokens, model_width),
         hyp_tok,
         q_proj,
@@ -641,7 +686,7 @@
     crossing = blocks[2] + swap(blocks[3], "tm", 1)
     payloads = [blocks[0], swap(blocks[1], "tm", 1), swap(crossing, "tm", 2)]
 
-    parts, own_frames = ffn(place, blocks[0], enc_in, ffn_up, ffn_down, width_count)
+    parts, own_frames = ffn(view, info, crossing, enc_in, ffn_up, ffn_down, width_count)
     parts = exchange(parts, "mp")
     sent = keys_values_of(parts, own_frames, kv_proj, section_count, utterances, width_count)
     frames_all = all_devices * (frame_rows // width_count)
@@ -649,9 +694,8 @@
 
     pieces = (share_rows // 2, share_rows - share_rows // 2)
     projected = attend(
-        place,
-        slot_utt,
-        frame_len,
+        view,
+        info,
         payloads,
         keys_values,
         o_proj,
@@ -679,7 +723,7 @@
     second = halve(*second, "section", 1, section_pos)
     sums = [*first, *second]
     out_rows = normed_rows(
-        place, slot_utt, token, payloads, sums, pieces, slot_tokens, slot_count
+        view, info, token, payloads, sums, pieces, slot_tokens, slot_count
     )
 
     share = out_rows.shape[0]
@@ -690,21 +734,24 @@
     half = own.shape[0] // 2
     by_x = swap(own, "section", 1)
     by_y = swap(own, "tm", 2)
-    stats = [vocabulary_stats(place, [own, swap(own, "tm", 1)], head)]
+    stats = [vocabulary_stats(info, [own, swap(own, "tm", 1)], head)]
     by_x, by_y, stats[0] = lax.optimization_barrier((by_x, by_y, stats[0]))
     across = [swap(by_x[:half], "tm", 2), swap(by_y[half:], "section", 1)]
     stats.append(
-        vocabulary_stats(place, [by_y, swap(by_y, "tm", 1), by_x, swap(by_x, "tm", 1)], head)
+        vocabulary_stats(info, [by_y, swap(by_y, "tm", 1), by_x, swap(by_x, "tm", 1)], head)
     )
     *across, stats[1] = lax.optimization_barrier((*across, stats[1]))
     across = jnp.concatenate(across)
-    stats.append(vocabulary_stats(place, [across, swap(across, "tm", 1)], head))
+    stats.append(vocabulary_stats(info, [across, swap(across, "tm", 1)], head))
 
     every = exchange(
-        spread_stats(place, slot_utt, stats, section_count, group_count, width_count), ALL
+        spread_stats(
+            view, info, stats, slot_count, section_count, group_count, width_count
+        ),
+        ALL,
     )
     return hypothesis_scores(
-        place, slot_utt, hyp_len, every, slot_count, hyp_count, section_count, width_count
+        view, info, every, slot_count, hyp_count, section_count, width_count
     )
 
 

time: 135 us -> 139 us (1.030)
  Pallas kernels: 38 us -> 46.8 us
  local copies, waits for them, and re-layouts: 12 us -> 4.26 us
  waiting for transfers between devices: 44 us -> 47 us
    unnamed x39 -> x9, local copies, waits for them, and re-layouts: 11.1 us -> 1.54 us
    pallas_call x4, Pallas kernels: 9.19 us -> 15.5 us  [the longest x1 6.57 us: ffn(): pl.pallas_call(functools.partial(ffn_kernel, steps, view), in_specs=[SCAL...]
    all_to_all x2, waiting for transfers between devices: 14.3 us -> 17.5 us  [exchange(): return lax.all_to_all(blocks, axis, split_axis=0, concat_axis=0, tiled=True)]
where the time goes in v10:
time: 139 us; the launch traced here: 138 us
  waiting for transfers between devices  47 us (34%)
  Pallas kernels  46.8 us (34%)
  starting transfers between devices  25.9 us (19%)
  blocking collectives  12.8 us (9%)
  local copies, waits for them, and re-layouts  4.26 us (3%)
    ppermute x20, waiting for transfers between devices, swap(): return lax.ppermute(values, axis, pairs)  29.5 us
    pallas_call x3, Pallas kernels, vocabulary_stats(): pl.pallas_call(functools.partial(vocabulary_kernel, head.shape[0] // 2),...  17.5 us
    all_to_all x2, waiting for transfers between devices, exchange(): return lax.all_to_all(blocks, axis, split_axis=0, concat_axis=0, tiled=True)  17.5 us
    ppermute x20, starting transfers between devices, swap(): return lax.ppermute(values, axis, pairs)  16 us
    all_to_all x1, blocking collectives, exchange(): return lax.all_to_all(blocks, axis, split_axis=0, concat_axis=0, tiled=True)  12.8 us
    all_to_all x2, starting transfers between devices, exchange(): return lax.all_to_all(blocks, axis, split_axis=0, concat_axis=0, tiled=True)  9.91 us
    pallas_call x1, Pallas kernels, ffn(): pl.pallas_call(functools.partial(ffn_kernel, steps, view), in_specs=[SCAL...  6.57 us
    pallas_call x1, Pallas kernels, queries_of(): pl.pallas_call(functools.partial(query_kernel, count, depth, view), in_sp...  6.4 us
  transfers between devices with their start and end apart: 22, of which 16 were waited for; matrix products, arithmetic and copies ran while one was open for 1% of the time, Pallas kernels for 14%

profile of v10, /device:TPU:0, one launch (start us, length us, event | category | flops | bytes accessed | tf_op | source)
XLA Modules:
  0.0 138.4 jit_solution(12946739272270203362)
XLA Ops:
  0.0 0.8 reshape.12
  0.8 0.7 concatenate.6.info_ref.first_ref
  1.5 6.4 %hypothesis_queries.1 = (bf16[272,512]{1,0:T(8,128)(2,1)}, bf16[272,512]{1,0:T(8,128)(2,1)}, bf16[272,512]{1,0:T(8,128)(2,1)}, bf16[272,512]{1,0:T(8,128)(2,1)}) custom-call(s32[33]{0:T(128)S(1)} %concatenate.6.info_ref.first_ref, bf16[2,128,4096]{2,1,0:T(8,128)(2,1)} %bitcast.9, s32[2,8,16]{2,1,0:T(8,128)} %tok_ref.1, bf16[4096,512]{1,0:T(8,128)(2,1)} %w_ref.1), custom_call_target="tpu_custom_call" | custom-call | flops 1073741824 | bytes 6291456 | tf_op jit(solution)/shard_map/hypothesis_queries/pallas_call | solution.py:255
  7.9 0.5 collective-permute-start.1
  8.4 1.4 %collective-permute-done.1 = bf16[272,512]{1,0:T(8,128)(2,1)S(1)} collective-permute-done((bf16[272,512]{1,0:T(8,128)(2,1)}, bf16[272,512]{1,0:T(8,128)(2,1)S(1)}, u32[]{:S(2)}, u32[]{:S(2)}) %collective-permute-start.1) | collective-permute-done | bytes 278560 | tf_op jit(solution)/shard_map/ppermute | solution.py:40
  9.8 1.2 add.68.after_ref
  11.0 6.6 %encoder_ffn.1 = (bf16[4,32,1280]{2,1,0:T(8,128)(2,1)}, bf16[32,1280]{1,0:T(8,128)(2,1)S(1)}) custom-call(s32[33]{0:T(128)S(1)} %concatenate.6.info_ref.first_ref, bf16[272,512]{1,0:T(8,128)(2,1)S(1)} %add.68.after_ref, bf16[32,4,1280]{2,1,0:T(4,128)(2,1)} %x_ref.1, bf16[1280,1280]{1,0:T(8,128)(2,1)} %up_ref.1, bf16[1280,1280]{1,0:T(8,128)(2,1)} %down_ref.1), custom_call_target="tpu_custom_call" | custom-call | flops 838860800 | bytes 6553600 | tf_op jit(solution)/shard_map/encoder_ffn/pallas_call | solution.py:141
  17.6 0.6 copy-done.2
  18.2 6.3 %all-to-all-start = ((bf16[4,32,1280]{2,1,0:T(8,128)(2,1)}), bf16[4,32,1280]{2,1,0:T(8,128)(2,1)S(1)}, u32[]{:S(2)}, u32[]{:S(2)}) async-start(bf16[4,32,1280]{2,1,0:T(8,128)(2,1)} %get-tuple-element.27), calls=%async_computation | async-start | bytes 655360 | tf_op jit(solution)/shard_map/all_to_all | solution.py:30
  24.5 0.0 collective-permute-start
  24.5 1.5 %collective-permute-start.2 = (bf16[272,512]{1,0:T(8,128)(2,1)S(1)}, bf16[272,512]{1,0:T(8,128)(2,1)}, u32[]{:S(2)}, u32[]{:S(2)}) collective-permute-start(bf16[272,512]{1,0:T(8,128)(2,1)S(1)} %add.68.after_ref), channel_id=1, source_target_pairs={{0,8},{4,12},{8,0},{12,4},{1,9},{5,13},{9,1},{13,5},{2,10},{6,14},... | collective-permute-start | bytes 835592 | tf_op jit(solution)/shard_map/ppermute | solution.py:40
  26.0 9.1 %all-to-all-done.refs_0_ = bf16[4,32,1280]{2,1,0:T(8,128)(2,1)S(1)} async-done(((bf16[4,32,1280]{2,1,0:T(8,128)(2,1)}), bf16[4,32,1280]{2,1,0:T(8,128)(2,1)S(1)}, u32[]{:S(2)}, u32[]{:S(2)}) %all-to-all-start) | async-done | bytes 327712 | tf_op jit(solution)/shard_map/all_to_all | solution.py:30
  35.1 0.9 copy-done.3
  36.0 1.5 %frame_keys_values.1 = bf16[256,256]{1,0:T(8,128)(2,1)} custom-call(bf16[4,32,1280]{2,1,0:T(8,128)(2,1)S(1)} %all-to-all-done.refs_0_, bf16[32,1280]{1,0:T(8,128)(2,1)S(1)} %copy-done.3, bf16[1280,1024]{1,0:T(8,128)(2,1)S(1)} %copy-done), custom_call_target="tpu_custom_call" | custom-call | flops 83886080 | bytes 2621440 | tf_op jit(solution)/shard_map/frame_keys_values/pallas_call | solution.py:314
  37.5 3.7 %all-to-all-start.1 = ((bf16[32,8,256]{2,1,0:T(8,128)(2,1)}), bf16[32,8,256]{2,1,0:T(8,128)(2,1)S(1)}, u32[]{:S(2)}, u32[]{:S(2)}) async-start(bf16[32,8,256]{2,1,0:T(8,128)(2,1)} %bitcast.10), calls=%async_computation.1 | async-start | bytes 262144 | tf_op jit(solution)/shard_map/all_to_all | solution.py:30
  41.2 0.0 collective-permute-done.refs_1_
  41.2 0.0 collective-permute-done.2.refs_2_
  41.2 8.4 %all-to-all-done.1 = bf16[32,8,256]{2,1,0:T(8,128)(2,1)S(1)} async-done(((bf16[32,8,256]{2,1,0:T(8,128)(2,1)}), bf16[32,8,256]{2,1,0:T(8,128)(2,1)S(1)}, u32[]{:S(2)}, u32[]{:S(2)}) %all-to-all-start.1) | async-done | bytes 131104 | tf_op jit(solution)/shard_map/all_to_all | solution.py:30
  49.6 4.3 %attention_projection.1 = (bf16[32,4096]{1,0:T(8,128)(2,1)}, bf16[32,4096]{1,0:T(8,128)(2,1)S(1)}, bf16[32,4096]{1,0:T(8,128)(2,1)}, bf16[32,4096]{1,0:T(8,128)(2,1)S(1)}) custom-call(s32[33]{0:T(128)S(1)} %concatenate.6.info_ref.first_ref, bf16[272,512]{1,0:T(8,128)(2,1)S(1)} %copy-done.1, bf16[272,512]{1,0:T(8,128)(2,1)} %collective-permute-done.refs_1_, ...), custom_call_target="tpu_custom_call" | custom-call | flops 603979776 | bytes 5242880 | tf_op jit(solution)/shard_map/attention_projection/pallas_call | solution.py:402
  54.0 0.9 collective-permute-start.3
  54.8 0.0 collective-permute-start.6
  54.8 5.8 %vocabulary_rows.1 = (bf16[2000,4096]{1,0:T(8,128)(2,1)S(1)}, f32[8,128]{1,0:T(8,128)S(1)}) custom-call(bf16[32,4096]{1,0:T(8,128)(2,1)S(1)} %get-tuple-element.29.after_ref, bf16[2000,4096]{1,0:T(8,128)(2,1)} %head_ref.1), custom_call_target="tpu_custom_call" | custom-call | bytes 16384000 | tf_op jit(solution)/shard_map/vocabulary_rows/pallas_call | solution.py:484
  60.6 1.0 collective-permute-done.3
  61.6 0.1 convert_add_fusion.1
  61.7 1.2 collective-permute-start.4
  62.9 0.0 collective-permute-done.6
  62.9 0.1 convert_add_fusion
  63.0 0.9 collective-permute-start.7
  63.9 3.3 %collective-permute-done.4 = bf16[16,4096]{1,0:T(8,128)(2,1)S(1)} collective-permute-done((bf16[16,4096]{1,0:T(8,128)(2,1)S(1)}, bf16[16,4096]{1,0:T(8,128)(2,1)S(1)}, u32[]{:S(2)}, u32[]{:S(2)}) %collective-permute-start.4) | collective-permute-done | bytes 131104 | tf_op jit(solution)/shard_map/ppermute | solution.py:40
  67.3 2.2 %collective-permute-start.5 = (bf16[8,4096]{1,0:T(8,128)(2,1)S(1)}, bf16[8,4096]{1,0:T(8,128)(2,1)S(1)}, u32[]{:S(2)}, u32[]{:S(2)}) collective-permute-start(bf16[8,4096]{1,0:T(8,128)(2,1)S(1)} %dynamic-slice_convert_fusion.3), channel_id=1, source_target_pairs={{0,2},{1,3},{2,0},{3,1},{4,6},{5,7},{6,4},{7,5},{8,10},{9,11},{10,... | collective-permute-start | bytes 196616 | tf_op jit(solution)/shard_map/ppermute | solution.py:40
  69.5 3.6 %collective-permute-done.7 = bf16[16,4096]{1,0:T(8,128)(2,1)S(1)} collective-permute-done((bf16[16,4096]{1,0:T(8,128)(2,1)S(1)}, bf16[16,4096]{1,0:T(8,128)(2,1)S(1)}, u32[]{:S(2)}, u32[]{:S(2)}) %collective-permute-start.7) | collective-permute-done | bytes 131104 | tf_op jit(solution)/shard_map/ppermute | solution.py:40
  73.1 0.8 collective-permute-start.8
  74.0 0.5 collective-permute-done.5.refs_4_
  74.5 3.0 %collective-permute-done.8.refs_6_ = bf16[8,4096]{1,0:T(8,128)(2,1)S(1)} collective-permute-done((bf16[8,4096]{1,0:T(8,128)(2,1)S(1)}, bf16[8,4096]{1,0:T(8,128)(2,1)S(1)}, u32[]{:S(2)}, u32[]{:S(2)}) %collective-permute-start.8) | collective-permute-done | bytes 65568 | tf_op jit(solution)/shard_map/ppermute | solution.py:40
  77.5 2.1 %token_rows.1 = bf16[16,4224]{1,0:T(8,128)(2,1)} custom-call(s32[33]{0:T(128)S(1)} %concatenate.6.info_ref.first_ref, f32[8,128]{1,0:T(8,128)S(1)} %get-tuple-element.30.after_ref, bf16[272,512]{1,0:T(8,128)(2,1)S(1)} %copy-done.1, bf16[272,512]{1,0:T(8,128)(2,1)} %collective-permute-done.refs_1_, bf16[272,512]{1,0:T(8,128)(2,1)} %collective-permute-done.2.refs_2_, ...), custom_call_target="tpu_custom_call" | custom-call | tf_op jit(solution)/shard_map/token_rows/pallas_call | solution.py:455
  79.5 0.0 collective-permute-start.9
  79.5 2.1 %collective-permute-start.10 = (bf16[16,4224]{1,0:T(8,128)(2,1)}, bf16[16,4224]{1,0:T(8,128)(2,1)S(1)}, u32[]{:S(2)}, u32[]{:S(2)}) collective-permute-start(bf16[16,4224]{1,0:T(8,128)(2,1)} %token_rows.1), channel_id=1, source_target_pairs={{0,2},{1,3},{2,0},{3,1},{4,6},{5,7},{6,4},{7,5},{8,10},{9,11},{10,... | collective-permute-start | bytes 405512 | tf_op jit(solution)/shard_map/ppermute | solution.py:40
  81.6 2.3 %collective-permute-start.11 = (bf16[16,4224]{1,0:T(8,128)(2,1)}, bf16[16,4224]{1,0:T(8,128)(2,1)S(1)}, u32[]{:S(2)}, u32[]{:S(2)}) collective-permute-start(bf16[16,4224]{1,0:T(8,128)(2,1)} %token_rows.1), channel_id=1, source_target_pairs={{0,3},{1,2},{2,1},{3,0},{4,7},{5,6},{6,5},{7,4},{8,11},{9,10},{10,... | collective-permute-start | bytes 405512 | tf_op jit(solution)/shard_map/ppermute | solution.py:40
  84.0 1.0 constant_dynamic-update-slice_fusion.5
  84.9 1.2 collective-permute-done.9
  86.2 4.9 %collective-permute-done.10 = bf16[16,4224]{1,0:T(8,128)(2,1)S(1)} collective-permute-done((bf16[16,4224]{1,0:T(8,128)(2,1)}, bf16[16,4224]{1,0:T(8,128)(2,1)S(1)}, u32[]{:S(2)}, u32[]{:S(2)}) %collective-permute-start.10) | collective-permute-done | bytes 135200 | tf_op jit(solution)/shard_map/ppermute | solution.py:40
  91.1 0.0 collective-permute-done.11
  91.1 0.1 collective-permute-start.14
  91.2 0.5 collective-permute-start.12
  91.7 0.3 collective-permute-start.13
  92.0 1.1 collective-permute-done.14.refs_1_
  93.1 5.7 %vocabulary_scores.3.refs_0_ = f32[2,8,64]{2,1,0:T(8,128)S(1)} custom-call(s32[33]{0:T(128)S(1)} %concatenate.6.info_ref.first_ref, bf16[64,4224]{1,0:T(8,128)(2,1)S(1)} %constant_dynamic-update-slice_fusion.2.refs_0_, bf16[64,4224]{1,0:T(8,128)(2,1)S(1)} %collective-permute-done.14.refs_1_, bf16[2000,4096]{1,0:T(8,128)(2,1)S(1)} %get-tuple-element.34.refs_2_.refs_4_), custom_call_target="tpu_custom_call" | custom-call | flops 3145728000 | bytes 1048576 | tf_op jit(solution)/shard_map/vocabulary_scores/pallas_call | solution.py:540
  98.8 7.0 %collective-permute-done.12.refs_2_ = bf16[64,4224]{1,0:T(8,128)(2,1)S(1)} collective-permute-done((bf16[64,4224]{1,0:T(8,128)(2,1)S(1)}, bf16[64,4224]{1,0:T(8,128)(2,1)S(1)}, u32[]{:S(2)}, u32[]{:S(2)}) %collective-permute-start.12) | collective-permute-done | bytes 540704 | tf_op jit(solution)/shard_map/ppermute | solution.py:40
  105.9 0.2 collective-permute-done.13.refs_0_
  106.1 0.0 collective-permute-start.17
  106.1 0.5 collective-permute-start.18
  106.6 0.4 collective-permute-start.15
  107.0 1.7 %collective-permute-start.16 = (bf16[32,4224]{1,0:T(8,128)(2,1)S(1)}, bf16[32,4224]{1,0:T(8,128)(2,1)S(1)}, u32[]{:S(2)}, u32[]{:S(2)}) collective-permute-start(bf16[32,4224]{1,0:T(8,128)(2,1)S(1)} %slice.7), channel_id=1, source_target_pairs={{0,16},{16,0},{1,17},{17,1},{2,18},{18,2},{3,19},{19,3},{4,20},{20... | collective-permute-start | bytes 811016 | tf_op jit(solution)/shard_map/ppermute | solution.py:40
  108.7 0.0 collective-permute-done.17.refs_1_
  108.7 0.0 collective-permute-done.18.refs_3_
  108.8 6.0 %vocabulary_scores.4.refs_1_ = f32[4,8,64]{2,1,0:T(8,128)S(1)} custom-call(s32[33]{0:T(128)S(1)} %concatenate.6.info_ref.first_ref, bf16[64,4224]{1,0:T(8,128)(2,1)S(1)} %collective-permute-done.13.refs_0_, bf16[64,4224]{1,0:T(8,128)(2,1)S(1)} %collective-permute-done.17.refs_1_, bf16[64,4224]{1,0:T(8,128)(2,1)S(1)} %collective-permute-done.12.refs_2_, ...), custom_call_target="tpu_custom_call" | custom-call | flops 6291456000 | bytes 2097152 | tf_op jit(solution)/shard_map/vocabulary_scores/pallas_call | solution.py:540
  114.8 0.3 collective-permute-done.15
  115.1 0.1 collective-permute-done.16
  115.2 0.1 collective-permute-start.19
  115.3 1.9 %collective-permute-done.19.refs_1_ = bf16[64,4224]{1,0:T(8,128)(2,1)S(1)} collective-permute-done((bf16[64,4224]{1,0:T(8,128)(2,1)S(1)}, bf16[64,4224]{1,0:T(8,128)(2,1)S(1)}, u32[]{:S(2)}, u32[]{:S(2)}) %collective-permute-start.19) | collective-permute-done | bytes 540704 | tf_op jit(solution)/shard_map/ppermute | solution.py:40
  117.2 5.7 %vocabulary_scores.5.refs_2_ = f32[2,8,64]{2,1,0:T(8,128)S(1)} custom-call(s32[33]{0:T(128)S(1)} %concatenate.6.info_ref.first_ref, bf16[64,4224]{1,0:T(8,128)(2,1)S(1)} %constant_dynamic-update-slice_fusion.refs_0_, bf16[64,4224]{1,0:T(8,128)(2,1)S(1)} %collective-permute-done.19.refs_1_, bf16[2000,4096]{1,0:T(8,128)(2,1)S(1)} %get-tuple-element.34.refs_2_.refs_4_), custom_call_target="tpu_custom_call" | custom-call | flops 3145728000 | bytes 1048576 | tf_op jit(solution)/shard_map/vocabulary_scores/pallas_call | solution.py:540
  122.9 1.3 statistics_by_group.1
  124.2 12.8 %all_to_all.15.every_ref = f32[32,8,128]{2,1,0:T(8,128)S(1)} all-to-all(f32[32,8,128]{2,1,0:T(8,128)} %statistics_by_group.1), channel_id=1, replica_groups=mesh['section'=2,'tm'=4,'mp'=4] {'section','tm','mp'}, dimensions={0} | all-to-all | bytes 262144 | tf_op jit(solution)/shard_map/all_to_all | solution.py:30
  137.1 1.3 hypothesis_scores.1
  (22 shorter events, 0.3 us)
Async XLA Ops:
  7.9 1.9 %collective-permute-start.1 = (bf16[272,512]{1,0:T(8,128)(2,1)}, bf16[272,512]{1,0:T(8,128)(2,1)S(1)}, u32[]{:S(2)}, u32[]{:S(2)}) collective-permute-start(bf16[272,512]{1,0:T(8,128)(2,1)} %get-tuple-element.26), channel_id=1, source_target_pairs={{0,4},{4,0},{8,12},{12,8},{1,5},{5,1},{9,13},{13,9},{2,6},{6,2},{1... | collective-permute-start | bytes 835592 | tf_op jit(solution)/shard_map/ppermute | solution.py:40
  9.8 25.3 %copy-start = (bf16[1280,1024]{1,0:T(8,128)(2,1)S(1)}, bf16[1280,1024]{1,0:T(8,128)(2,1)}, u32[]{:S(2)}) copy-start(bf16[1280,1024]{1,0:T(8,128)(2,1)} %refs_2_.1) | copy-start | bytes 7864324
  11.0 38.6 %copy-start.1 = (bf16[272,512]{1,0:T(8,128)(2,1)S(1)}, bf16[272,512]{1,0:T(8,128)(2,1)}, u32[]{:S(2)}) copy-start(bf16[272,512]{1,0:T(8,128)(2,1)} %get-tuple-element.23.refs_0_) | copy-start | bytes 835588
  17.6 0.6 copy-start.2
  18.2 16.9 %all-to-all-start = ((bf16[4,32,1280]{2,1,0:T(8,128)(2,1)}), bf16[4,32,1280]{2,1,0:T(8,128)(2,1)S(1)}, u32[]{:S(2)}, u32[]{:S(2)}) async-start(bf16[4,32,1280]{2,1,0:T(8,128)(2,1)} %get-tuple-element.27), calls=%async_computation | async-start | bytes 655360 | tf_op jit(solution)/shard_map/all_to_all | solution.py:30
  24.5 16.7 %collective-permute-start = (bf16[272,512]{1,0:T(8,128)(2,1)}, bf16[272,512]{1,0:T(8,128)(2,1)}, u32[]{:S(2)}, u32[]{:S(2)}) collective-permute-start(bf16[272,512]{1,0:T(8,128)(2,1)} %get-tuple-element.24), channel_id=1, source_target_pairs={{0,4},{4,0},{8,12},{12,8},{1,5},{5,1},{9,13},{13,9},{2,6},{6,2},{1... | collective-permute-start | bytes 835592 | tf_op jit(solution)/shard_map/ppermute | solution.py:40
  24.5 16.7 %collective-permute-start.2 = (bf16[272,512]{1,0:T(8,128)(2,1)S(1)}, bf16[272,512]{1,0:T(8,128)(2,1)}, u32[]{:S(2)}, u32[]{:S(2)}) collective-permute-start(bf16[272,512]{1,0:T(8,128)(2,1)S(1)} %add.68.after_ref), channel_id=1, source_target_pairs={{0,8},{4,12},{8,0},{12,4},{1,9},{5,13},{9,1},{13,5},{2,10},{6,14},... | collective-permute-start | bytes 835592 | tf_op jit(solution)/shard_map/ppermute | solution.py:40
  35.1 0.9 copy-start.3
  37.5 12.1 %all-to-all-start.1 = ((bf16[32,8,256]{2,1,0:T(8,128)(2,1)}), bf16[32,8,256]{2,1,0:T(8,128)(2,1)S(1)}, u32[]{:S(2)}, u32[]{:S(2)}) async-start(bf16[32,8,256]{2,1,0:T(8,128)(2,1)} %bitcast.10), calls=%async_computation.1 | async-start | bytes 262144 | tf_op jit(solution)/shard_map/all_to_all | solution.py:30
  54.0 7.7 %collective-permute-start.3 = (bf16[32,4096]{1,0:T(8,128)(2,1)}, bf16[32,4096]{1,0:T(8,128)(2,1)S(1)}, u32[]{:S(2)}, u32[]{:S(2)}) collective-permute-start(bf16[32,4096]{1,0:T(8,128)(2,1)} %get-tuple-element.31), channel_id=1, source_target_pairs={{0,16},{16,0},{1,17},{17,1},{2,18},{18,2},{3,19},{19,3},{4,20},{20... | collective-permute-start | bytes 786440 | tf_op jit(solution)/shard_map/ppermute | solution.py:40
  54.8 8.1 %collective-permute-start.6 = (bf16[32,4096]{1,0:T(8,128)(2,1)}, bf16[32,4096]{1,0:T(8,128)(2,1)S(1)}, u32[]{:S(2)}, u32[]{:S(2)}) collective-permute-start(bf16[32,4096]{1,0:T(8,128)(2,1)} %get-tuple-element.33), channel_id=1, source_target_pairs={{0,1},{1,0},{2,3},{3,2},{4,5},{5,4},{6,7},{7,6},{8,9},{9,8},{10,11... | collective-permute-start | bytes 786440 | tf_op jit(solution)/shard_map/ppermute | solution.py:40
  61.7 5.5 %collective-permute-start.4 = (bf16[16,4096]{1,0:T(8,128)(2,1)S(1)}, bf16[16,4096]{1,0:T(8,128)(2,1)S(1)}, u32[]{:S(2)}, u32[]{:S(2)}) collective-permute-start(bf16[16,4096]{1,0:T(8,128)(2,1)S(1)} %dynamic-slice_convert_fusion.1), channel_id=1, source_target_pairs={{0,1},{1,0},{2,3},{3,2},{4,5},{5,4},{6,7},{7,6},{8,9},{9,8},{10,11... | collective-permute-start | bytes 393224 | tf_op jit(solution)/shard_map/ppermute | solution.py:40
  63.0 10.1 %collective-permute-start.7 = (bf16[16,4096]{1,0:T(8,128)(2,1)S(1)}, bf16[16,4096]{1,0:T(8,128)(2,1)S(1)}, u32[]{:S(2)}, u32[]{:S(2)}) collective-permute-start(bf16[16,4096]{1,0:T(8,128)(2,1)S(1)} %dynamic-slice_convert_fusion), channel_id=1, source_target_pairs={{0,2},{1,3},{2,0},{3,1},{4,6},{5,7},{6,4},{7,5},{8,10},{9,11},{10,... | collective-permute-start | bytes 393224 | tf_op jit(solution)/shard_map/ppermute | solution.py:40
  67.3 7.2 %collective-permute-start.5 = (bf16[8,4096]{1,0:T(8,128)(2,1)S(1)}, bf16[8,4096]{1,0:T(8,128)(2,1)S(1)}, u32[]{:S(2)}, u32[]{:S(2)}) collective-permute-start(bf16[8,4096]{1,0:T(8,128)(2,1)S(1)} %dynamic-slice_convert_fusion.3), channel_id=1, source_target_pairs={{0,2},{1,3},{2,0},{3,1},{4,6},{5,7},{6,4},{7,5},{8,10},{9,11},{10,... | collective-permute-start | bytes 196616 | tf_op jit(solution)/shard_map/ppermute | solution.py:40
  73.1 4.3 %collective-permute-start.8 = (bf16[8,4096]{1,0:T(8,128)(2,1)S(1)}, bf16[8,4096]{1,0:T(8,128)(2,1)S(1)}, u32[]{:S(2)}, u32[]{:S(2)}) collective-permute-start(bf16[8,4096]{1,0:T(8,128)(2,1)S(1)} %dynamic-slice_convert_fusion.2), channel_id=1, source_target_pairs={{0,16},{16,0},{1,17},{17,1},{2,18},{18,2},{3,19},{19,3},{4,20},{20... | collective-permute-start | bytes 196616 | tf_op jit(solution)/shard_map/ppermute | solution.py:40
  79.5 6.6 %collective-permute-start.9 = (bf16[16,4224]{1,0:T(8,128)(2,1)}, bf16[16,4224]{1,0:T(8,128)(2,1)S(1)}, u32[]{:S(2)}, u32[]{:S(2)}) collective-permute-start(bf16[16,4224]{1,0:T(8,128)(2,1)} %token_rows.1), channel_id=1, source_target_pairs={{0,1},{1,0},{2,3},{3,2},{4,5},{5,4},{6,7},{7,6},{8,9},{9,8},{10,11... | collective-permute-start | bytes 405512 | tf_op jit(solution)/shard_map/ppermute | solution.py:40
  79.5 11.5 %collective-permute-start.10 = (bf16[16,4224]{1,0:T(8,128)(2,1)}, bf16[16,4224]{1,0:T(8,128)(2,1)S(1)}, u32[]{:S(2)}, u32[]{:S(2)}) collective-permute-start(bf16[16,4224]{1,0:T(8,128)(2,1)} %token_rows.1), channel_id=1, source_target_pairs={{0,2},{1,3},{2,0},{3,1},{4,6},{5,7},{6,4},{7,5},{8,10},{9,11},{10,... | collective-permute-start | bytes 405512 | tf_op jit(solution)/shard_map/ppermute | solution.py:40
  81.6 9.4 %collective-permute-start.11 = (bf16[16,4224]{1,0:T(8,128)(2,1)}, bf16[16,4224]{1,0:T(8,128)(2,1)S(1)}, u32[]{:S(2)}, u32[]{:S(2)}) collective-permute-start(bf16[16,4224]{1,0:T(8,128)(2,1)} %token_rows.1), channel_id=1, source_target_pairs={{0,3},{1,2},{2,1},{3,0},{4,7},{5,6},{6,5},{7,4},{8,11},{9,10},{10,... | collective-permute-start | bytes 405512 | tf_op jit(solution)/shard_map/ppermute | solution.py:40
  91.1 2.0 %collective-permute-start.14 = (bf16[64,4224]{1,0:T(8,128)(2,1)S(1)}, bf16[64,4224]{1,0:T(8,128)(2,1)S(1)}, u32[]{:S(2)}, u32[]{:S(2)}) collective-permute-start(bf16[64,4224]{1,0:T(8,128)(2,1)S(1)} %constant_dynamic-update-slice_fusion.2.refs_0_), channel_id=1, source_target_pairs={{0,4},{4,0},{8,12},{12,8},{1,5},{5,1},{9,13},{13,9},{2,6},{6,2},{1... | collective-permute-start | bytes 1622024 | tf_op jit(solution)/shard_map/ppermute | solution.py:40
  91.2 14.7 %collective-permute-start.12 = (bf16[64,4224]{1,0:T(8,128)(2,1)S(1)}, bf16[64,4224]{1,0:T(8,128)(2,1)S(1)}, u32[]{:S(2)}, u32[]{:S(2)}) collective-permute-start(bf16[64,4224]{1,0:T(8,128)(2,1)S(1)} %constant_dynamic-update-slice_fusion.2.refs_0_), channel_id=1, source_target_pairs={{0,16},{16,0},{1,17},{17,1},{2,18},{18,2},{3,19},{19,3},{4,20},{20... | collective-permute-start | bytes 1622024 | tf_op jit(solution)/shard_map/ppermute | solution.py:40
  91.7 14.3 %collective-permute-start.13 = (bf16[64,4224]{1,0:T(8,128)(2,1)S(1)}, bf16[64,4224]{1,0:T(8,128)(2,1)S(1)}, u32[]{:S(2)}, u32[]{:S(2)}) collective-permute-start(bf16[64,4224]{1,0:T(8,128)(2,1)S(1)} %constant_dynamic-update-slice_fusion.2.refs_0_), channel_id=1, source_target_pairs={{0,8},{4,12},{8,0},{12,4},{1,9},{5,13},{9,1},{13,5},{2,10},{6,14},... | collective-permute-start | bytes 1622024 | tf_op jit(solution)/shard_map/ppermute | solution.py:40
  106.1 2.7 %collective-permute-start.17 = (bf16[64,4224]{1,0:T(8,128)(2,1)S(1)}, bf16[64,4224]{1,0:T(8,128)(2,1)S(1)}, u32[]{:S(2)}, u32[]{:S(2)}) collective-permute-start(bf16[64,4224]{1,0:T(8,128)(2,1)S(1)} %collective-permute-done.13.refs_0_), channel_id=1, source_target_pairs={{0,4},{4,0},{8,12},{12,8},{1,5},{5,1},{9,13},{13,9},{2,6},{6,2},{1... | collective-permute-start | bytes 1622024 | tf_op jit(solution)/shard_map/ppermute | solution.py:40
  106.1 2.7 %collective-permute-start.18 = (bf16[64,4224]{1,0:T(8,128)(2,1)S(1)}, bf16[64,4224]{1,0:T(8,128)(2,1)S(1)}, u32[]{:S(2)}, u32[]{:S(2)}) collective-permute-start(bf16[64,4224]{1,0:T(8,128)(2,1)S(1)} %collective-permute-done.12.refs_2_), channel_id=1, source_target_pairs={{0,4},{4,0},{8,12},{12,8},{1,5},{5,1},{9,13},{13,9},{2,6},{6,2},{1... | collective-permute-start | bytes 1622024 | tf_op jit(solution)/shard_map/ppermute | solution.py:40
  106.6 8.5 %collective-permute-start.15 = (bf16[32,4224]{1,0:T(8,128)(2,1)S(1)}, bf16[32,4224]{1,0:T(8,128)(2,1)S(1)}, u32[]{:S(2)}, u32[]{:S(2)}) collective-permute-start(bf16[32,4224]{1,0:T(8,128)(2,1)S(1)} %slice.6), channel_id=1, source_target_pairs={{0,8},{4,12},{8,0},{12,4},{1,9},{5,13},{9,1},{13,5},{2,10},{6,14},... | collective-permute-start | bytes 811016 | tf_op jit(solution)/shard_map/ppermute | solution.py:40
  107.0 8.2 %collective-permute-start.16 = (bf16[32,4224]{1,0:T(8,128)(2,1)S(1)}, bf16[32,4224]{1,0:T(8,128)(2,1)S(1)}, u32[]{:S(2)}, u32[]{:S(2)}) collective-permute-start(bf16[32,4224]{1,0:T(8,128)(2,1)S(1)} %slice.7), channel_id=1, source_target_pairs={{0,16},{16,0},{1,17},{17,1},{2,18},{18,2},{3,19},{19,3},{4,20},{20... | collective-permute-start | bytes 811016 | tf_op jit(solution)/shard_map/ppermute | solution.py:40
  115.2 2.0 %collective-permute-start.19 = (bf16[64,4224]{1,0:T(8,128)(2,1)S(1)}, bf16[64,4224]{1,0:T(8,128)(2,1)S(1)}, u32[]{:S(2)}, u32[]{:S(2)}) collective-permute-start(bf16[64,4224]{1,0:T(8,128)(2,1)S(1)} %constant_dynamic-update-slice_fusion.refs_0_), channel_id=1, source_target_pairs={{0,4},{4,0},{8,12},{12,8},{1,5},{5,1},{9,13},{13,9},{2,6},{6,2},{1... | collective-permute-start | bytes 1622024 | tf_op jit(solution)/shard_map/ppermute | solution.py:40

commit v11 on v7

--- a/solution.py
+++ b/solution.py
@@ -14,6 +14,7 @@
 V = 64000
 ALL = ("section", "tm", "mp")
 LANES = 128
+FOLD = 4
 
 
 def layer_norm(values):
@@ -407,9 +408,12 @@
     for part in range(width // columns):
         take = slice(part * columns, (part + 1) * columns)
         total[:, take] += picked[part * share : part * share + rows, :].astype(jnp.float32)
-    out_ref[:, :width] = square_norm(total[...]).astype(jnp.bfloat16)
+    shape = out_ref.shape[:2]
+    normed = square_norm(total[...]).reshape(*shape, width)
+    out_ref[:, :, :width] = normed.astype(jnp.bfloat16)
     last = width // columns * share
-    out_ref[:, width:] = picked[last : last + rows, :LANES]
+    target = picked[last : last + rows, :LANES].astype(jnp.float32).reshape(*shape, LANES)
+    out_ref[:, :, width:] = target.astype(jnp.bfloat16)
 
 
 def normed_rows(place, slot_utt, after, payloads, blocks, pieces, tokens, slots):
@@ -420,7 +424,7 @@
         functools.partial(norm_kernel, len(payloads), slots, tokens, pieces),
         in_specs=[SCALARS] * 2 + [ANYWHERE] + [INSIDE] * (len(payloads) + len(blocks)),
         out_specs=INSIDE,
-        out_shape=jax.ShapeDtypeStruct((rows, width + LANES), jnp.bfloat16),
+        out_shape=jax.ShapeDtypeStruct((rows // FOLD, FOLD, width + LANES), jnp.bfloat16),
         scratch_shapes=[
             pltpu.VMEM((payloads[0].shape[0] - tokens, columns), jnp.bfloat16),
             pltpu.VMEM((rows, width), jnp.float32),
@@ -465,12 +469,13 @@
 def vocabulary_kernel(tile, first_ref, *refs):
     sets, (head_ref, out_ref, rows_ref, stat) = refs[:-4], refs[-4:]
     vocab_rows, width = head_ref.shape
-    share = sets[0].shape[0]
+    share = sets[0].shape[0] * FOLD
     tokens = share * len(sets)
     cell = lax.broadcasted_iota(jnp.int32, (8, LANES), 1)
     take = jnp.where(cell == 0, 256.0, jnp.where(cell == 1, 1.0, 0.0)).astype(jnp.bfloat16)
     for number, rows in enumerate(sets):
-        rows_ref[number * share : (number + 1) * share, :] = rows[...]
+        flat = rows[...].astype(jnp.float32).reshape(share, width + LANES)
+        rows_ref[number * share : (number + 1) * share, :] = flat.astype(jnp.bfloat16)
     target = dot_nt(take, rows_ref[:, width:])[0:1, :].astype(jnp.int32) - first_ref[3]
     stat[0:1, :] = jnp.full((1, tokens), -jnp.inf, jnp.float32)
     stat[8:9, :] = jnp.zeros((1, tokens), jnp.float32)
@@ -497,7 +502,7 @@
 
 
 def vocabulary_stats(place, sets, head):
-    share = sets[0].shape[0]
+    share = sets[0].shape[0] * FOLD
     count = len(sets)
     width = head.shape[1]
     tokens = share * count
@@ -601,6 +606,73 @@
     )(place, slot_utt, lengths, every)
 
 
+def rest(pieces, slot_tokens, place, slot_utt, frame_len, hyp_len, payloads, keys_values, o_proj, head):
+    section_count = lax.axis_size("section")
+    group_count = lax.axis_size("tm")
+    width_count = lax.axis_size("mp")
+    section_pos = lax.axis_index("section")
+    width_pos = lax.axis_index("mp")
+    slot_count, hyp_count = hyp_len.shape
+    projected = attend(
+        place,
+        slot_utt,
+        frame_len,
+        payloads,
+        keys_values,
+        o_proj,
+        pieces,
+        section_count,
+        width_count,
+        slot_count,
+    )
+    head, token = load_head(projected[1], head)
+
+    def halve(total, came, axis, distance, side):
+        if came is not None:
+            total = total + came.astype(jnp.float32)
+        half = total.shape[0] // 2
+        kept = lax.dynamic_slice_in_dim(total, side * half, half, 0)
+        sent = lax.dynamic_slice_in_dim(total, (1 - side) * half, half, 0)
+        return kept, swap(sent.astype(jnp.bfloat16), axis, distance)
+
+    low, high = width_pos % 2, width_pos // 2
+    first = projected[1].astype(jnp.float32), swap(projected[0], "section", 1)
+    second = projected[3].astype(jnp.float32), swap(projected[2], "mp", 1)
+    first = halve(*first, "mp", 1, low)
+    second = halve(*second, "mp", 2, high)
+    first = halve(*first, "mp", 2, high)
+    second = halve(*second, "section", 1, section_pos)
+    sums = [*first, *second]
+    out_rows = normed_rows(
+        place, slot_utt, token, payloads, sums, pieces, slot_tokens, slot_count
+    )
+
+    own = jnp.zeros((width_count, *out_rows.shape), jnp.bfloat16)
+    for distance in range(width_count):
+        block = swap(out_rows, "mp", distance) if distance else out_rows
+        own = lax.dynamic_update_index_in_dim(own, block, width_pos ^ distance, 0)
+    own = own.reshape(-1, *out_rows.shape[1:])
+    half = own.shape[0] // 2
+    by_x = swap(own, "section", 1)
+    by_y = swap(own, "tm", 2)
+    stats = [vocabulary_stats(place, [own, swap(own, "tm", 1)], head)]
+    by_x, by_y, stats[0] = lax.optimization_barrier((by_x, by_y, stats[0]))
+    across = [swap(by_x[:half], "tm", 2), swap(by_y[half:], "section", 1)]
+    stats.append(
+        vocabulary_stats(place, [by_y, swap(by_y, "tm", 1), by_x, swap(by_x, "tm", 1)], head)
+    )
+    *across, stats[1] = lax.optimization_barrier((*across, stats[1]))
+    across = jnp.concatenate(across)
+    stats.append(vocabulary_stats(place, [across, swap(across, "tm", 1)], head))
+
+    every = exchange(
+        spread_stats(place, slot_utt, stats, section_count, group_count, width_count), ALL
+    )
+    return hypothesis_scores(
+        place, slot_utt, hyp_len, every, slot_count, hyp_count, section_count, width_count
+    )
+
+
 def near_device(
     frame_len,
     slot_utt,
@@ -658,64 +730,18 @@
     frames_all = all_devices * (frame_rows // width_count)
     keys_values = exchange(sent.reshape(all_devices, -1, 2 * HD), ALL).reshape(frames_all, 2 * HD)
 
-    pieces = (share_rows // 2, share_rows - share_rows // 2)
-    projected = attend(
-        place,
-        slot_utt,
-        frame_len,
-        payloads,
-        keys_values,
-        o_proj,
-        pieces,
-        section_count,
-        width_count,
-        slot_count,
-    )
-    head, token = load_head(projected[1], head)
-
-    def halve(total, came, axis, distance, side):
-        if came is not None:
-            total = total + came.astype(jnp.float32)
-        half = total.shape[0] // 2
-        kept = lax.dynamic_slice_in_dim(total, side * half, half, 0)
-        sent = lax.dynamic_slice_in_dim(total, (1 - side) * half, half, 0)
-        return kept, swap(sent.astype(jnp.bfloat16), axis, distance)
-
-    low, high = width_pos % 2, width_pos // 2
-    first = projected[1].astype(jnp.float32), swap(projected[0], "section", 1)
-    second = projected[3].astype(jnp.float32), swap(projected[2], "mp", 1)
-    first = halve(*first, "mp", 1, low)
-    second = halve(*second, "mp", 2, high)
-    first = halve(*first, "mp", 2, high)
-    second = halve(*second, "section", 1, section_pos)
-    sums = [*first, *second]
-    out_rows = normed_rows(
-        place, slot_utt, token, payloads, sums, pieces, slot_tokens, slot_count
-    )
-
-    share = out_rows.shape[0]
-    own = jnp.zeros((width_count * share, out_rows.shape[1]), jnp.bfloat16)
-    for distance in range(width_count):
-        block = swap(out_rows, "mp", distance) if distance else out_rows
-        own = lax.dynamic_update_slice_in_dim(own, block, (width_pos ^ distance) * share, 0)
-    half = own.shape[0] // 2
-    by_x = swap(own, "section", 1)
-    by_y = swap(own, "tm", 2)
-    stats = [vocabulary_stats(place, [own, swap(own, "tm", 1)], head)]
-    by_x, by_y, stats[0] = lax.optimization_barrier((by_x, by_y, stats[0]))
-    across = [swap(by_x[:half], "tm", 2), swap(by_y[half:], "section", 1)]
-    stats.append(
-        vocabulary_stats(place, [by_y, swap(by_y, "tm", 1), by_x, swap(by_x, "tm", 1)], head)
-    )
-    *across, stats[1] = lax.optimization_barrier((*across, stats[1]))
-    across = jnp.concatenate(across)
-    stats.append(vocabulary_stats(place, [across, swap(across, "tm", 1)], head))
-
-    every = exchange(
-        spread_stats(place, slot_utt, stats, section_count, group_count, width_count), ALL
-    )
-    return hypothesis_scores(
-        place, slot_utt, hyp_len, every, slot_count, hyp_count, section_count, width_count
+    here_slots = lax.dynamic_slice_in_dim(slot_utt, group_pos * slot_count, slot_count, 0)
+    filled = jnp.where(here_slots >= 0, jnp.sum(hyp_len, axis=1), 0)
+    most = jnp.max(filled).reshape(1)
+    for distance in (1, 2):
+        most = jnp.maximum(most, swap(most, "tm", distance))
+    operands = (place, slot_utt, frame_len, hyp_len, payloads, keys_values, o_proj, head)
+    few = share_rows * 3 // 4
+    return lax.cond(
+        most[0] <= few * head_devices,
+        functools.partial(rest, (few - few // 3, few // 3), slot_tokens),
+        functools.partial(rest, (share_rows // 2, share_rows - share_rows // 2), slot_tokens),
+        *operands,
     )
 
 

time: 126 us -> 134 us (1.063)
  waiting for transfers between devices: 38.3 us -> 25.1 us
  local copies, waits for them, and re-layouts: 3.71 us -> 13.7 us
  starting transfers between devices: 27.6 us -> 34.3 us
  Pallas kernels: 41.7 us -> 43.7 us
  between operations: 0.26 us -> 1.89 us
    cond x0 -> x7, local copies, waits for them, and re-layouts: none -> 11.4 us
    all_to_all x2, waiting for transfers between devices: 8.71 us -> 1.03 us  [exchange(): return lax.all_to_all(blocks, axis, split_axis=0, concat_axis=0, tiled=True)]
    ppermute x20 -> x22, starting transfers between devices: 16.2 us -> 22.9 us  [swap(): return lax.ppermute(values, axis, pairs)]
    ppermute x20 -> x22, waiting for transfers between devices: 29.6 us -> 24.1 us  [swap(): return lax.ppermute(values, axis, pairs)]
    unnamed x21 -> x14, local copies, waits for them, and re-layouts: 3.26 us -> 1.55 us
  transfers between devices with their start and end apart: 22 -> 24, of which waited for: 16 -> 11; matrix products, arithmetic and copies ran while one was open for 1% -> 2% of each run, Pallas kernels for 19% -> 19%
where the time goes in v11:
time: 134 us; the launch traced here: 133 us
  Pallas kernels  43.7 us (33%)
  starting transfers between devices  34.3 us (26%)
  waiting for transfers between devices  25.1 us (19%)
  local copies, waits for them, and re-layouts  13.7 us (10%)
  blocking collectives  12.5 us (9%)
  between operations  1.89 us (1%)
  other arithmetic  1.75 us (1%)
    ppermute x22, waiting for transfers between devices, swap(): return lax.ppermute(values, axis, pairs)  24.1 us
    ppermute x22, starting transfers between devices, swap(): return lax.ppermute(values, axis, pairs)  22.9 us
    pallas_call x3, Pallas kernels, vocabulary_stats(): pl.pallas_call(functools.partial(vocabulary_kernel, head.shape[0] // 2),...  18.4 us
    all_to_all x1, blocking collectives, exchange(): return lax.all_to_all(blocks, axis, split_axis=0, concat_axis=0, tiled=True)  12.5 us
    all_to_all x2, starting transfers between devices, exchange(): return lax.all_to_all(blocks, axis, split_axis=0, concat_axis=0, tiled=True)  11.4 us
    cond x7, local copies, waits for them, and re-layouts  11.4 us
    pallas_call x1, Pallas kernels, queries_of(): pl.pallas_call(functools.partial(query_kernel, count, depth), in_specs=[S...  5.93 us
    pallas_call x1, Pallas kernels, load_head(): pl.pallas_call(functools.partial(load_kernel, rows), in_specs=[ANYWHERE,...  5.81 us
  transfers between devices with their start and end apart: 24, of which 11 were waited for; matrix products, arithmetic and copies ran while one was open for 2% of the time, Pallas kernels for 19%

profile of v11, /device:TPU:0, one launch (start us, length us, event | category | flops | bytes accessed | tf_op | source)
XLA Modules:
  0.0 133.2 jit_solution(2267729353408311941)
XLA Ops:
  0.0 0.1 stack.23.place_ref.after_ref
  0.1 1.0 copy-done.5
  1.1 5.6 %encoder_ffn.1 = (bf16[4,32,1280]{2,1,0:T(8,128)(2,1)}, bf16[32,1280]{1,0:T(8,128)(2,1)S(1)}) custom-call(s32[5]{0:T(128)S(1)} %stack.23.place_ref.after_ref, bf16[32,4,1280]{2,1,0:T(4,128)(2,1)S(1)} %copy-done.5, bf16[1280,1280]{1,0:T(8,128)(2,1)} %up_ref.1, bf16[1280,1280]{1,0:T(8,128)(2,1)} %down_ref.1), custom_call_target="tpu_custom_call" | custom-call | flops 838860800 | bytes 6553600 | tf_op jit(solution)/shard_map/encoder_ffn/pallas_call | solution.py:114
  6.7 6.6 %all-to-all-start.2 = ((bf16[4,32,1280]{2,1,0:T(8,128)(2,1)}), bf16[4,32,1280]{2,1,0:T(8,128)(2,1)S(1)}, u32[]{:S(2)}, u32[]{:S(2)}) async-start(bf16[4,32,1280]{2,1,0:T(8,128)(2,1)} %get-tuple-element.102), calls=%async_computation.2 | async-start | bytes 655360 | tf_op jit(solution)/shard_map/all_to_all | solution.py:31
  13.3 0.1 reshape.27.tok_ref
  13.4 5.9 %hypothesis_queries.1 = (bf16[272,512]{1,0:T(8,128)(2,1)}, bf16[272,512]{1,0:T(8,128)(2,1)S(1)}, bf16[272,512]{1,0:T(8,128)(2,1)S(1)}, bf16[272,512]{1,0:T(8,128)(2,1)S(1)}) custom-call(s32[5]{0:T(128)S(1)} %stack.23.place_ref.after_ref, s32[8]{0:T(128)S(1)} %copy-done.8, s32[2,8]{1,0:T(2,128)S(1)} %copy-done.9, s32[5]{0:T(128)S(1)} %stack.23.place_ref.after_ref, ...), custom_call_target="tpu_custom_call" | custom-call | flops 1073741824 | bytes 6291456 | tf_op jit(solution)/shard_map/hypothesis_queries/pallas_call | solution.py:220
  19.4 0.1 collective-permute-start.37
  19.4 0.5 collective-permute-start.36
  19.9 1.0 collective-permute-done.37
  21.0 0.8 add.122
  21.8 1.5 %collective-permute-start.38 = (bf16[272,512]{1,0:T(8,128)(2,1)}, bf16[272,512]{1,0:T(8,128)(2,1)}, u32[]{:S(2)}, u32[]{:S(2)}) collective-permute-start(bf16[272,512]{1,0:T(8,128)(2,1)} %add.122), channel_id=1, source_target_pairs={{0,8},{4,12},{8,0},{12,4},{1,9},{5,13},{9,1},{13,5},{2,10},{6,14},... | collective-permute-start | bytes 835592 | tf_op jit(solution)/shard_map/ppermute | solution.py:41
  23.3 0.4 all-to-all-done.2.refs_0_
  23.6 1.5 %frame_keys_values.1 = bf16[256,256]{1,0:T(8,128)(2,1)} custom-call(bf16[4,32,1280]{2,1,0:T(8,128)(2,1)S(1)} %all-to-all-done.2.refs_0_, bf16[32,1280]{1,0:T(8,128)(2,1)S(1)} %get-tuple-element.103.refs_1_, bf16[1280,1024]{1,0:T(8,128)(2,1)S(1)} %copy-done.4, bf16[272,512]{1,0:T(8,128)(2,1)} %get-tuple-element.98.refs_3_), custom_call_target="tpu_custom_call" | custom-call | flops 83886080 | bytes 2621440 | tf_op jit(solution)/shard_map/frame_keys_values/pallas_call | solution.py:279
  25.2 4.8 %all-to-all-start.3 = ((bf16[32,8,256]{2,1,0:T(8,128)(2,1)}), bf16[32,8,256]{2,1,0:T(8,128)(2,1)S(1)}, u32[]{:S(2)}, u32[]{:S(2)}) async-start(bf16[32,8,256]{2,1,0:T(8,128)(2,1)} %bitcast.20), calls=%async_computation.3 | async-start | bytes 262144 | tf_op jit(solution)/shard_map/all_to_all | solution.py:31
  30.0 0.1 reduce_sum.9
  30.1 0.7 fusion
  30.8 0.3 collective-permute-start.34
  31.0 1.1 collective-permute-done.34
  33.4 3.1 %collective-permute-start.35 = (s32[1]{0:T(128)}, s32[1]{0:T(128)}, u32[]{:S(2)}, u32[]{:S(2)}) collective-permute-start(s32[1]{0:T(128)} %max.6), channel_id=1, source_target_pairs={{0,8},{4,12},{8,0},{12,4},{1,9},{5,13},{9,1},{13,5},{2,10},{6,14},... | collective-permute-start | bytes 20 | tf_op jit(solution)/shard_map/ppermute | solution.py:41
  36.5 0.6 collective-permute-done.35
  37.7 0.7 all-to-all-done.3
  38.4 94.3 %conditional.1 = (f32[2,8]{1,0:T(2,128)S(1)}) conditional(s32[]{:T(128)} %bitcast.13, (s32[5]{0:T(128)S(1)}, s32[8]{0:T(128)S(1)}, s32[4]{0:T(128)S(1)}, bf16[272,512]{1,0:T(8,128)(2,1)}, bf16[272,512]{1,0:T(8,128)(2,1)}, /*index=5*/bf16[272,512]{1,0:T(8,128)(2,1)}, bf16[32,8,256]{2,1,0:T(8,128)(2,1)S(1)}, bf16[512,4096]{1,0:T(8,128)(2,1)}, ...), branch_computations={%region_2.3_spmd, %region_3.4_spmd} | conditional | flops 13187940352 | bytes 187205120 | solution.py:740
  38.4 3.8 %attention_projection.3 = (bf16[32,4096]{1,0:T(8,128)(2,1)S(1)}, bf16[32,4096]{1,0:T(8,128)(2,1)S(1)}, bf16[16,4096]{1,0:T(8,128)(2,1)S(1)}, bf16[16,4096]{1,0:T(8,128)(2,1)S(1)}) custom-call(s32[5]{0:T(128)S(1)} %get-tuple-element.70.refs_0_.place_ref.first_ref, s32[8]{0:T(128)S(1)} %get-tuple-element.71.refs_1_.slot_ref, s32[4]{0:T(128)S(1)} %get-tuple-element.114.refs_2_, ...), custom_call_target="tpu_custom_call" | custom-call | flops 452984832 | bytes 4980736 | tf_op jit(solution)/shard_map/cond/branch_1_fun/attention_projection/pallas_call | solution.py:367
  42.1 1.4 %collective-permute-start.20 = (bf16[16,4096]{1,0:T(8,128)(2,1)S(1)}, bf16[16,4096]{1,0:T(8,128)(2,1)S(1)}, u32[]{:S(2)}, u32[]{:S(2)}) collective-permute-start(bf16[16,4096]{1,0:T(8,128)(2,1)S(1)} %get-tuple-element.84), channel_id=1, source_target_pairs={{0,1},{1,0},{2,3},{3,2},{4,5},{5,4},{6,7},{7,6},{8,9},{9,8},{10,11... | collective-permute-start | bytes 393224 | tf_op jit(solution)/shard_map/cond/branch_1_fun/ppermute | solution.py:41
  43.6 3.6 %collective-permute-done.20 = bf16[16,4096]{1,0:T(8,128)(2,1)S(1)} collective-permute-done((bf16[16,4096]{1,0:T(8,128)(2,1)S(1)}, bf16[16,4096]{1,0:T(8,128)(2,1)S(1)}, u32[]{:S(2)}, u32[]{:S(2)}) %collective-permute-start.20) | collective-permute-done | bytes 131104 | tf_op jit(solution)/shard_map/cond/branch_1_fun/ppermute | solution.py:41
  47.2 2.3 %collective-permute-start.21 = (bf16[8,4096]{1,0:T(8,128)(2,1)S(1)}, bf16[8,4096]{1,0:T(8,128)(2,1)S(1)}, u32[]{:S(2)}, u32[]{:S(2)}) collective-permute-start(bf16[8,4096]{1,0:T(8,128)(2,1)S(1)} %dynamic-slice_convert_fusion.5), channel_id=1, source_target_pairs={{0,2},{1,3},{2,0},{3,1},{4,6},{5,7},{6,4},{7,5},{8,10},{9,11},{10,... | collective-permute-start | bytes 196616 | tf_op jit(solution)/shard_map/cond/branch_1_fun/ppermute | solution.py:41
  49.6 1.5 %collective-permute-start.17 = (bf16[32,4096]{1,0:T(8,128)(2,1)S(1)}, bf16[32,4096]{1,0:T(8,128)(2,1)S(1)}, u32[]{:S(2)}, u32[]{:S(2)}) collective-permute-start(bf16[32,4096]{1,0:T(8,128)(2,1)S(1)} %get-tuple-element.82), channel_id=1, source_target_pairs={{0,16},{16,0},{1,17},{17,1},{2,18},{18,2},{3,19},{19,3},{4,20},{20... | collective-permute-start | bytes 786440 | tf_op jit(solution)/shard_map/cond/branch_1_fun/ppermute | solution.py:41
  51.0 5.8 %vocabulary_rows.3 = (bf16[2000,4096]{1,0:T(8,128)(2,1)S(1)}, f32[8,128]{1,0:T(8,128)S(1)}) custom-call(bf16[32,4096]{1,0:T(8,128)(2,1)S(1)} %get-tuple-element.79.after_ref, bf16[2000,4096]{1,0:T(8,128)(2,1)} %get-tuple-element.118.head_ref), custom_call_target="tpu_custom_call" | custom-call | bytes 16384000 | tf_op jit(solution)/shard_map/cond/branch_1_fun/vocabulary_rows/pallas_call | solution.py:452
  56.9 5.6 %copy-done = bf16[2000,4096]{1,0:T(8,128)(2,1)} copy-done((bf16[2000,4096]{1,0:T(8,128)(2,1)}, bf16[2000,4096]{1,0:T(8,128)(2,1)S(1)}, u32[]{:S(2)}) %copy-start) | copy-done | bytes 16384024 | tf_op jit(solution)/shard_map/cond
  62.5 0.6 collective-permute-start.22
  63.2 0.1 convert_add_fusion.4
  63.3 1.6 %collective-permute-start.18 = (bf16[16,4096]{1,0:T(8,128)(2,1)S(1)}, bf16[16,4096]{1,0:T(8,128)(2,1)S(1)}, u32[]{:S(2)}, u32[]{:S(2)}) collective-permute-start(bf16[16,4096]{1,0:T(8,128)(2,1)S(1)} %dynamic-slice_convert_fusion.4), channel_id=1, source_target_pairs={{0,1},{1,0},{2,3},{3,2},{4,5},{5,4},{6,7},{7,6},{8,9},{9,8},{10,11... | collective-permute-start | bytes 393224 | tf_op jit(solution)/shard_map/cond/branch_1_fun/ppermute | solution.py:41
  64.9 4.1 %collective-permute-done.18 = bf16[16,4096]{1,0:T(8,128)(2,1)S(1)} collective-permute-done((bf16[16,4096]{1,0:T(8,128)(2,1)S(1)}, bf16[16,4096]{1,0:T(8,128)(2,1)S(1)}, u32[]{:S(2)}, u32[]{:S(2)}) %collective-permute-start.18) | collective-permute-done | bytes 131104 | tf_op jit(solution)/shard_map/cond/branch_1_fun/ppermute | solution.py:41
  69.1 0.1 collective-permute-start.19
  69.2 8.3 %collective-permute-done.19.refs_4_ = bf16[8,4096]{1,0:T(8,128)(2,1)S(1)} collective-permute-done((bf16[8,4096]{1,0:T(8,128)(2,1)S(1)}, bf16[8,4096]{1,0:T(8,128)(2,1)S(1)}, u32[]{:S(2)}, u32[]{:S(2)}) %collective-permute-start.19) | collective-permute-done | bytes 65568 | tf_op jit(solution)/shard_map/cond/branch_1_fun/ppermute | solution.py:41
  77.5 1.3 token_rows.3
  78.8 0.1 collective-permute-start.23
  78.9 0.1 collective-permute-start.24
  78.9 4.3 %collective-permute-start.25 = (bf16[3,4,4224]{2,1,0:T(4,128)(2,1)S(1)}, bf16[3,4,4224]{2,1,0:T(4,128)(2,1)S(1)}, u32[]{:S(2)}, u32[]{:S(2)}) collective-permute-start(bf16[3,4,4224]{2,1,0:T(4,128)(2,1)S(1)} %token_rows.3), channel_id=1, source_target_pairs={{0,3},{1,2},{2,1},{3,0},{4,7},{5,6},{6,5},{7,4},{8,11},{9,10},{10,... | collective-permute-start | bytes 304136 | tf_op jit(solution)/shard_map/cond/branch_1_fun/ppermute | solution.py:41
  83.2 0.1 broadcast.11
  83.3 0.1 bitcast_dynamic-update-slice_fusion.7
  83.4 1.2 collective-permute-done.23
  84.6 0.1 bitcast_dynamic-update-slice_fusion.5
  84.7 2.4 %collective-permute-done.25 = bf16[3,4,4224]{2,1,0:T(4,128)(2,1)S(1)} collective-permute-done((bf16[3,4,4224]{2,1,0:T(4,128)(2,1)S(1)}, bf16[3,4,4224]{2,1,0:T(4,128)(2,1)S(1)}, u32[]{:S(2)}, u32[]{:S(2)}) %collective-permute-start.25) | collective-permute-done | bytes 101408 | tf_op jit(solution)/shard_map/cond/branch_1_fun/ppermute | solution.py:41
  87.1 0.1 collective-permute-start.28
  87.2 1.6 %collective-permute-start.26 = (bf16[12,4,4224]{2,1,0:T(4,128)(2,1)S(1)}, bf16[12,4,4224]{2,1,0:T(4,128)(2,1)S(1)}, u32[]{:S(2)}, u32[]{:S(2)}) collective-permute-start(bf16[12,4,4224]{2,1,0:T(4,128)(2,1)S(1)} %bitcast.34), channel_id=1, source_target_pairs={{0,16},{16,0},{1,17},{17,1},{2,18},{18,2},{3,19},{19,3},{4,20},{20... | collective-permute-start | bytes 1216520 | tf_op jit(solution)/shard_map/cond/branch_1_fun/ppermute | solution.py:41
  88.7 1.5 %collective-permute-start.27 = (bf16[12,4,4224]{2,1,0:T(4,128)(2,1)S(1)}, bf16[12,4,4224]{2,1,0:T(4,128)(2,1)S(1)}, u32[]{:S(2)}, u32[]{:S(2)}) collective-permute-start(bf16[12,4,4224]{2,1,0:T(4,128)(2,1)S(1)} %bitcast.35), channel_id=1, source_target_pairs={{0,8},{4,12},{8,0},{12,4},{1,9},{5,13},{9,1},{13,5},{2,10},{6,14},... | collective-permute-start | bytes 1216520 | tf_op jit(solution)/shard_map/cond/branch_1_fun/ppermute | solution.py:41
  90.2 5.7 %copy-done.1 = bf16[2000,4096]{1,0:T(8,128)(2,1)S(1)} copy-done((bf16[2000,4096]{1,0:T(8,128)(2,1)S(1)}, bf16[2000,4096]{1,0:T(8,128)(2,1)}, u32[]{:S(2)}) %copy-start.1) | copy-done | bytes 16384024 | tf_op jit(solution)/shard_map/cond
  95.9 5.9 %vocabulary_scores.9.refs_0_ = f32[2,8,48]{2,1,0:T(8,128)S(1)} custom-call(s32[5]{0:T(128)S(1)} %get-tuple-element.70.refs_0_.place_ref.first_ref, bf16[12,4,4224]{2,1,0:T(4,128)(2,1)S(1)} %bitcast.36, bf16[12,4,4224]{2,1,0:T(4,128)(2,1)S(1)} %collective-permute-done.28.refs_1_, bf16[2000,4096]{1,0:T(8,128)(2,1)S(1)} %copy-done.1), custom_call_target="tpu_custom_call" | custom-call | flops 2359296000 | bytes 786432 | tf_op jit(solution)/shard_map/cond/branch_1_fun/vocabulary_scores/pallas_call | solution.py:509
  101.9 0.5 collective-permute-start.32
  102.4 0.1 slice.10
  102.5 0.1 slice.11
  102.5 0.6 collective-permute-start.29
  103.1 1.1 collective-permute-start.30
  104.3 6.5 %vocabulary_scores.10.refs_1_ = f32[4,8,48]{2,1,0:T(8,128)S(1)} custom-call(s32[5]{0:T(128)S(1)} %get-tuple-element.70.refs_0_.place_ref.first_ref, bf16[12,4,4224]{2,1,0:T(4,128)(2,1)S(1)} %collective-permute-done.27.refs_0_, bf16[12,4,4224]{2,1,0:T(4,128)(2,1)S(1)} %collective-permute-done.31.refs_1_, ...), custom_call_target="tpu_custom_call" | custom-call | flops 4718592000 | bytes 1572864 | tf_op jit(solution)/shard_map/cond/branch_1_fun/vocabulary_scores/pallas_call | solution.py:509
  110.9 0.1 constant_dynamic-update-slice_fusion.3
  110.9 0.1 constant_dynamic-update-slice_fusion.2.refs_0_
  111.0 0.1 collective-permute-start.33
  111.2 1.7 %collective-permute-done.33.refs_1_ = bf16[12,4,4224]{2,1,0:T(4,128)(2,1)S(1)} collective-permute-done((bf16[12,4,4224]{2,1,0:T(4,128)(2,1)S(1)}, bf16[12,4,4224]{2,1,0:T(4,128)(2,1)S(1)}, u32[]{:S(2)}, u32[]{:S(2)}) %collective-permute-start.33) | collective-permute-done | bytes 405536 | tf_op jit(solution)/shard_map/cond/branch_1_fun/ppermute | solution.py:41
  112.8 5.9 %vocabulary_scores.11.refs_2_ = f32[2,8,48]{2,1,0:T(8,128)S(1)} custom-call(s32[5]{0:T(128)S(1)} %get-tuple-element.70.refs_0_.place_ref.first_ref, bf16[12,4,4224]{2,1,0:T(4,128)(2,1)S(1)} %constant_dynamic-update-slice_fusion.2.refs_0_, bf16[12,4,4224]{2,1,0:T(4,128)(2,1)S(1)} %collective-permute-done.33.refs_1_, bf16[2000,4096]{1,0:T(8,128)(2,1)S(1)} %copy-done.1), custom_call_target="tpu_custom_call" | custom-call | flops 2359296000 | bytes 786432 | tf_op jit(solution)/shard_map/cond/branch_1_fun/vocabulary_scores/pallas_call | solution.py:509
  118.8 0.6 statistics_by_group.3
  119.4 12.5 %all_to_all.19.every_ref = f32[32,8,96]{2,1,0:T(8,128)S(1)} all-to-all(f32[32,8,96]{2,1,0:T(8,128)S(1)} %statistics_by_group.3), channel_id=1, replica_groups=mesh['section'=2,'tm'=4,'mp'=4] {'section','tm','mp'}, dimensions={0} | all-to-all | bytes 196608 | tf_op jit(solution)/shard_map/cond/branch_1_fun/all_to_all | solution.py:31
  131.9 0.7 hypothesis_scores.3
  132.7 0.6 copy-done.12
  (41 shorter events, 0.4 us)
Async XLA Ops:
  0.0 13.3 %copy-start.10 = (s32[2,8,16]{2,1,0:T(8,128)S(1)}, s32[2,8,16]{2,1,0:T(8,128)}, u32[]{:S(2)}) copy-start(s32[2,8,16]{2,1,0:T(8,128)} %param.21) | copy-start | bytes 3076
  0.0 13.4 %copy-start.8 = (s32[8]{0:T(128)S(1)}, s32[8]{0:T(128)}, u32[]{:S(2)}) copy-start(s32[8]{0:T(128)} %slot_ref.1) | copy-start | bytes 100
  0.0 13.4 %copy-start.9 = (s32[2,8]{1,0:T(2,128)S(1)}, s32[2,8]{1,0:T(2,128)}, u32[]{:S(2)}) copy-start(s32[2,8]{1,0:T(2,128)} %length_ref.1) | copy-start | bytes 196
  0.1 1.0 copy-start.5
  6.7 16.9 %copy-start.4 = (bf16[1280,1024]{1,0:T(8,128)(2,1)S(1)}, bf16[1280,1024]{1,0:T(8,128)(2,1)}, u32[]{:S(2)}) copy-start(bf16[1280,1024]{1,0:T(8,128)(2,1)} %refs_2_.1) | copy-start | bytes 7864324
  6.7 16.9 %all-to-all-start.2 = ((bf16[4,32,1280]{2,1,0:T(8,128)(2,1)}), bf16[4,32,1280]{2,1,0:T(8,128)(2,1)S(1)}, u32[]{:S(2)}, u32[]{:S(2)}) async-start(bf16[4,32,1280]{2,1,0:T(8,128)(2,1)} %get-tuple-element.102), calls=%async_computation.2 | async-start | bytes 655360 | tf_op jit(solution)/shard_map/all_to_all | solution.py:31
  13.4 25.0 %copy-start.11 = (s32[4]{0:T(128)S(1)}, s32[4]{0:T(128)}, u32[]{:S(2)}) copy-start(s32[4]{0:T(128)} %param.14) | copy-start | bytes 52
  19.4 1.6 %collective-permute-start.37 = (bf16[272,512]{1,0:T(8,128)(2,1)S(1)}, bf16[272,512]{1,0:T(8,128)(2,1)S(1)}, u32[]{:S(2)}, u32[]{:S(2)}) collective-permute-start(bf16[272,512]{1,0:T(8,128)(2,1)S(1)} %get-tuple-element.101), channel_id=1, source_target_pairs={{0,4},{4,0},{8,12},{12,8},{1,5},{5,1},{9,13},{13,9},{2,6},{6,2},{1... | collective-permute-start | bytes 835592 | tf_op jit(solution)/shard_map/ppermute | solution.py:41
  19.4 18.2 %collective-permute-start.36 = (bf16[272,512]{1,0:T(8,128)(2,1)S(1)}, bf16[272,512]{1,0:T(8,128)(2,1)}, u32[]{:S(2)}, u32[]{:S(2)}) collective-permute-start(bf16[272,512]{1,0:T(8,128)(2,1)S(1)} %get-tuple-element.99), channel_id=1, source_target_pairs={{0,4},{4,0},{8,12},{12,8},{1,5},{5,1},{9,13},{13,9},{2,6},{6,2},{1... | collective-permute-start | bytes 835592 | tf_op jit(solution)/shard_map/ppermute | solution.py:41
  21.8 15.9 %collective-permute-start.38 = (bf16[272,512]{1,0:T(8,128)(2,1)}, bf16[272,512]{1,0:T(8,128)(2,1)}, u32[]{:S(2)}, u32[]{:S(2)}) collective-permute-start(bf16[272,512]{1,0:T(8,128)(2,1)} %add.122), channel_id=1, source_target_pairs={{0,8},{4,12},{8,0},{12,4},{1,9},{5,13},{9,1},{13,5},{2,10},{6,14},... | collective-permute-start | bytes 835592 | tf_op jit(solution)/shard_map/ppermute | solution.py:41
  25.2 13.2 %all-to-all-start.3 = ((bf16[32,8,256]{2,1,0:T(8,128)(2,1)}), bf16[32,8,256]{2,1,0:T(8,128)(2,1)S(1)}, u32[]{:S(2)}, u32[]{:S(2)}) async-start(bf16[32,8,256]{2,1,0:T(8,128)(2,1)} %bitcast.20), calls=%async_computation.3 | async-start | bytes 262144 | tf_op jit(solution)/shard_map/all_to_all | solution.py:31
  30.8 1.4 %collective-permute-start.34 = (s32[1]{0:T(128)}, s32[1]{0:T(128)}, u32[]{:S(2)}, u32[]{:S(2)}) collective-permute-start(s32[1]{0:T(128)} %bitcast.12), channel_id=1, source_target_pairs={{0,4},{4,0},{8,12},{12,8},{1,5},{5,1},{9,13},{13,9},{2,6},{6,2},{1... | collective-permute-start | bytes 20 | tf_op jit(solution)/shard_map/ppermute | solution.py:41
  33.4 3.7 %collective-permute-start.35 = (s32[1]{0:T(128)}, s32[1]{0:T(128)}, u32[]{:S(2)}, u32[]{:S(2)}) collective-permute-start(s32[1]{0:T(128)} %max.6), channel_id=1, source_target_pairs={{0,8},{4,12},{8,0},{12,4},{1,9},{5,13},{9,1},{13,5},{2,10},{6,14},... | collective-permute-start | bytes 20 | tf_op jit(solution)/shard_map/ppermute | solution.py:41
  42.1 5.0 %collective-permute-start.20 = (bf16[16,4096]{1,0:T(8,128)(2,1)S(1)}, bf16[16,4096]{1,0:T(8,128)(2,1)S(1)}, u32[]{:S(2)}, u32[]{:S(2)}) collective-permute-start(bf16[16,4096]{1,0:T(8,128)(2,1)S(1)} %get-tuple-element.84), channel_id=1, source_target_pairs={{0,1},{1,0},{2,3},{3,2},{4,5},{5,4},{6,7},{7,6},{8,9},{9,8},{10,11... | collective-permute-start | bytes 393224 | tf_op jit(solution)/shard_map/cond/branch_1_fun/ppermute | solution.py:41
  47.2 15.3 %collective-permute-start.21 = (bf16[8,4096]{1,0:T(8,128)(2,1)S(1)}, bf16[8,4096]{1,0:T(8,128)(2,1)S(1)}, u32[]{:S(2)}, u32[]{:S(2)}) collective-permute-start(bf16[8,4096]{1,0:T(8,128)(2,1)S(1)} %dynamic-slice_convert_fusion.5), channel_id=1, source_target_pairs={{0,2},{1,3},{2,0},{3,1},{4,6},{5,7},{6,4},{7,5},{8,10},{9,11},{10,... | collective-permute-start | bytes 196616 | tf_op jit(solution)/shard_map/cond/branch_1_fun/ppermute | solution.py:41
  49.6 13.6 %collective-permute-start.17 = (bf16[32,4096]{1,0:T(8,128)(2,1)S(1)}, bf16[32,4096]{1,0:T(8,128)(2,1)S(1)}, u32[]{:S(2)}, u32[]{:S(2)}) collective-permute-start(bf16[32,4096]{1,0:T(8,128)(2,1)S(1)} %get-tuple-element.82), channel_id=1, source_target_pairs={{0,16},{16,0},{1,17},{17,1},{2,18},{18,2},{3,19},{19,3},{4,20},{20... | collective-permute-start | bytes 786440 | tf_op jit(solution)/shard_map/cond/branch_1_fun/ppermute | solution.py:41
  51.0 26.5 %copy-start.7 = (bf16[272,512]{1,0:T(8,128)(2,1)S(1)}, bf16[272,512]{1,0:T(8,128)(2,1)}, u32[]{:S(2)}) copy-start(bf16[272,512]{1,0:T(8,128)(2,1)} %get-tuple-element.74.refs_3_.refs_0_) | copy-start | bytes 835588 | tf_op jit(solution)/shard_map/cond
  56.9 5.6 %copy-start = (bf16[2000,4096]{1,0:T(8,128)(2,1)}, bf16[2000,4096]{1,0:T(8,128)(2,1)S(1)}, u32[]{:S(2)}) copy-start(bf16[2000,4096]{1,0:T(8,128)(2,1)S(1)} %get-tuple-element.85.refs_2_.refs_4_) | copy-start | bytes 49152004 | tf_op jit(solution)/shard_map/cond
  62.5 6.6 %collective-permute-start.22 = (bf16[4,4096]{1,0:T(4,128)(2,1)S(1)}, bf16[4,4096]{1,0:T(4,128)(2,1)S(1)}, u32[]{:S(2)}, u32[]{:S(2)}) collective-permute-start(bf16[4,4096]{1,0:T(4,128)(2,1)S(1)} %dynamic-slice_convert_fusion.7), channel_id=1, source_target_pairs={{0,16},{16,0},{1,17},{17,1},{2,18},{18,2},{3,19},{19,3},{4,20},{20... | collective-permute-start | bytes 98312 | tf_op jit(solution)/shard_map/cond/branch_1_fun/ppermute | solution.py:41
  63.3 5.7 %collective-permute-start.18 = (bf16[16,4096]{1,0:T(8,128)(2,1)S(1)}, bf16[16,4096]{1,0:T(8,128)(2,1)S(1)}, u32[]{:S(2)}, u32[]{:S(2)}) collective-permute-start(bf16[16,4096]{1,0:T(8,128)(2,1)S(1)} %dynamic-slice_convert_fusion.4), channel_id=1, source_target_pairs={{0,1},{1,0},{2,3},{3,2},{4,5},{5,4},{6,7},{7,6},{8,9},{9,8},{10,11... | collective-permute-start | bytes 393224 | tf_op jit(solution)/shard_map/cond/branch_1_fun/ppermute | solution.py:41
  69.1 8.5 %collective-permute-start.19 = (bf16[8,4096]{1,0:T(8,128)(2,1)S(1)}, bf16[8,4096]{1,0:T(8,128)(2,1)S(1)}, u32[]{:S(2)}, u32[]{:S(2)}) collective-permute-start(bf16[8,4096]{1,0:T(8,128)(2,1)S(1)} %dynamic-slice_convert_fusion.6), channel_id=1, source_target_pairs={{0,2},{1,3},{2,0},{3,1},{4,6},{5,7},{6,4},{7,5},{8,10},{9,11},{10,... | collective-permute-start | bytes 196616 | tf_op jit(solution)/shard_map/cond/branch_1_fun/ppermute | solution.py:41
  78.8 5.8 %collective-permute-start.23 = (bf16[3,4,4224]{2,1,0:T(4,128)(2,1)S(1)}, bf16[3,4,4224]{2,1,0:T(4,128)(2,1)S(1)}, u32[]{:S(2)}, u32[]{:S(2)}) collective-permute-start(bf16[3,4,4224]{2,1,0:T(4,128)(2,1)S(1)} %token_rows.3), channel_id=1, source_target_pairs={{0,1},{1,0},{2,3},{3,2},{4,5},{5,4},{6,7},{7,6},{8,9},{9,8},{10,11... | collective-permute-start | bytes 304136 | tf_op jit(solution)/shard_map/cond/branch_1_fun/ppermute | solution.py:41
  78.9 5.8 %collective-permute-start.24 = (bf16[3,4,4224]{2,1,0:T(4,128)(2,1)S(1)}, bf16[3,4,4224]{2,1,0:T(4,128)(2,1)S(1)}, u32[]{:S(2)}, u32[]{:S(2)}) collective-permute-start(bf16[3,4,4224]{2,1,0:T(4,128)(2,1)S(1)} %token_rows.3), channel_id=1, source_target_pairs={{0,2},{1,3},{2,0},{3,1},{4,6},{5,7},{6,4},{7,5},{8,10},{9,11},{10,... | collective-permute-start | bytes 304136 | tf_op jit(solution)/shard_map/cond/branch_1_fun/ppermute | solution.py:41
  78.9 8.1 %collective-permute-start.25 = (bf16[3,4,4224]{2,1,0:T(4,128)(2,1)S(1)}, bf16[3,4,4224]{2,1,0:T(4,128)(2,1)S(1)}, u32[]{:S(2)}, u32[]{:S(2)}) collective-permute-start(bf16[3,4,4224]{2,1,0:T(4,128)(2,1)S(1)} %token_rows.3), channel_id=1, source_target_pairs={{0,3},{1,2},{2,1},{3,0},{4,7},{5,6},{6,5},{7,4},{8,11},{9,10},{10,... | collective-permute-start | bytes 304136 | tf_op jit(solution)/shard_map/cond/branch_1_fun/ppermute | solution.py:41
  87.1 3.1 %collective-permute-start.28 = (bf16[12,4,4224]{2,1,0:T(4,128)(2,1)S(1)}, bf16[12,4,4224]{2,1,0:T(4,128)(2,1)S(1)}, u32[]{:S(2)}, u32[]{:S(2)}) collective-permute-start(bf16[12,4,4224]{2,1,0:T(4,128)(2,1)S(1)} %bitcast.33), channel_id=1, source_target_pairs={{0,4},{4,0},{8,12},{12,8},{1,5},{5,1},{9,13},{13,9},{2,6},{6,2},{1... | collective-permute-start | bytes 1216520 | tf_op jit(solution)/shard_map/cond/branch_1_fun/ppermute | solution.py:41
  87.2 14.7 %collective-permute-start.26 = (bf16[12,4,4224]{2,1,0:T(4,128)(2,1)S(1)}, bf16[12,4,4224]{2,1,0:T(4,128)(2,1)S(1)}, u32[]{:S(2)}, u32[]{:S(2)}) collective-permute-start(bf16[12,4,4224]{2,1,0:T(4,128)(2,1)S(1)} %bitcast.34), channel_id=1, source_target_pairs={{0,16},{16,0},{1,17},{17,1},{2,18},{18,2},{3,19},{19,3},{4,20},{20... | collective-permute-start | bytes 1216520 | tf_op jit(solution)/shard_map/cond/branch_1_fun/ppermute | solution.py:41
  88.7 13.1 %collective-permute-start.27 = (bf16[12,4,4224]{2,1,0:T(4,128)(2,1)S(1)}, bf16[12,4,4224]{2,1,0:T(4,128)(2,1)S(1)}, u32[]{:S(2)}, u32[]{:S(2)}) collective-permute-start(bf16[12,4,4224]{2,1,0:T(4,128)(2,1)S(1)} %bitcast.35), channel_id=1, source_target_pairs={{0,8},{4,12},{8,0},{12,4},{1,9},{5,13},{9,1},{13,5},{2,10},{6,14},... | collective-permute-start | bytes 1216520 | tf_op jit(solution)/shard_map/cond/branch_1_fun/ppermute | solution.py:41
  90.2 5.7 %copy-start.1 = (bf16[2000,4096]{1,0:T(8,128)(2,1)S(1)}, bf16[2000,4096]{1,0:T(8,128)(2,1)}, u32[]{:S(2)}) copy-start(bf16[2000,4096]{1,0:T(8,128)(2,1)} %copy-done) | copy-start | bytes 49152004 | tf_op jit(solution)/shard_map/cond
  101.8 2.4 %collective-permute-start.31 = (bf16[12,4,4224]{2,1,0:T(4,128)(2,1)S(1)}, bf16[12,4,4224]{2,1,0:T(4,128)(2,1)S(1)}, u32[]{:S(2)}, u32[]{:S(2)}) collective-permute-start(bf16[12,4,4224]{2,1,0:T(4,128)(2,1)S(1)} %collective-permute-done.27.refs_0_), channel_id=1, source_target_pairs={{0,4},{4,0},{8,12},{12,8},{1,5},{5,1},{9,13},{13,9},{2,6},{6,2},{1... | collective-permute-start | bytes 1216520 | tf_op jit(solution)/shard_map/cond/branch_1_fun/ppermute | solution.py:41
  101.9 2.4 %collective-permute-start.32 = (bf16[12,4,4224]{2,1,0:T(4,128)(2,1)S(1)}, bf16[12,4,4224]{2,1,0:T(4,128)(2,1)S(1)}, u32[]{:S(2)}, u32[]{:S(2)}) collective-permute-start(bf16[12,4,4224]{2,1,0:T(4,128)(2,1)S(1)} %collective-permute-done.26.refs_2_), channel_id=1, source_target_pairs={{0,4},{4,0},{8,12},{12,8},{1,5},{5,1},{9,13},{13,9},{2,6},{6,2},{1... | collective-permute-start | bytes 1216520 | tf_op jit(solution)/shard_map/cond/branch_1_fun/ppermute | solution.py:41
  102.5 8.3 %collective-permute-start.29 = (bf16[6,4,4224]{2,1,0:T(4,128)(2,1)S(1)}, bf16[6,4,4224]{2,1,0:T(4,128)(2,1)S(1)}, u32[]{:S(2)}, u32[]{:S(2)}) collective-permute-start(bf16[6,4,4224]{2,1,0:T(4,128)(2,1)S(1)} %slice.10), channel_id=1, source_target_pairs={{0,8},{4,12},{8,0},{12,4},{1,9},{5,13},{9,1},{13,5},{2,10},{6,14},... | collective-permute-start | bytes 608264 | tf_op jit(solution)/shard_map/cond/branch_1_fun/ppermute | solution.py:41
  103.1 7.7 %collective-permute-start.30 = (bf16[6,4,4224]{2,1,0:T(4,128)(2,1)S(1)}, bf16[6,4,4224]{2,1,0:T(4,128)(2,1)S(1)}, u32[]{:S(2)}, u32[]{:S(2)}) collective-permute-start(bf16[6,4,4224]{2,1,0:T(4,128)(2,1)S(1)} %slice.11), channel_id=1, source_target_pairs={{0,16},{16,0},{1,17},{17,1},{2,18},{18,2},{3,19},{19,3},{4,20},{20... | collective-permute-start | bytes 608264 | tf_op jit(solution)/shard_map/cond/branch_1_fun/ppermute | solution.py:41
  111.0 1.8 %collective-permute-start.33 = (bf16[12,4,4224]{2,1,0:T(4,128)(2,1)S(1)}, bf16[12,4,4224]{2,1,0:T(4,128)(2,1)S(1)}, u32[]{:S(2)}, u32[]{:S(2)}) collective-permute-start(bf16[12,4,4224]{2,1,0:T(4,128)(2,1)S(1)} %constant_dynamic-update-slice_fusion.2.refs_0_), channel_id=1, source_target_pairs={{0,4},{4,0},{8,12},{12,8},{1,5},{5,1},{9,13},{13,9},{2,6},{6,2},{1... | collective-permute-start | bytes 1216520 | tf_op jit(solution)/shard_map/cond/branch_1_fun/ppermute | solution.py:41
  132.6 0.6 copy-start.12

commit v12 on v11

--- a/solution.py
+++ b/solution.py
@@ -387,7 +387,7 @@
     )(place, slot_utt, frame_len, *payloads, keys_values, in_hbm(weights))
 
 
-def norm_kernel(count, slots, tokens, pieces, place_ref, slot_ref, after_ref, *refs):
+def norm_kernel(count, slots, tokens, pieces, place_ref, slot_ref, *refs):
     payloads, blocks = refs[:count], refs[count : count + 2 * len(pieces)]
     out_ref, picked, total = refs[count + 2 * len(pieces) :]
     rows, width = total.shape
@@ -416,13 +416,13 @@
     out_ref[:, :, width:] = target.astype(jnp.bfloat16)
 
 
-def normed_rows(place, slot_utt, after, payloads, blocks, pieces, tokens, slots):
+def normed_rows(place, slot_utt, payloads, blocks, pieces, tokens, slots):
     width = blocks[0].shape[1]
     rows = sum(pieces)
     columns = payloads[0].shape[1]
     return pl.pallas_call(
         functools.partial(norm_kernel, len(payloads), slots, tokens, pieces),
-        in_specs=[SCALARS] * 2 + [ANYWHERE] + [INSIDE] * (len(payloads) + len(blocks)),
+        in_specs=[SCALARS] * 2 + [INSIDE] * (len(payloads) + len(blocks)),
         out_specs=INSIDE,
         out_shape=jax.ShapeDtypeStruct((rows // FOLD, FOLD, width + LANES), jnp.bfloat16),
         scratch_shapes=[
@@ -431,39 +431,7 @@
         ],
         compiler_params=pltpu.CompilerParams(vmem_limit_bytes=16 << 20),
         name="token_rows",
-    )(place, slot_utt, after, *payloads, *blocks)
-
-
-def load_kernel(rows, after_ref, head_ref, out_ref, token_ref, semaphores):
-    count = head_ref.shape[0] // rows
-    copies = start_copies(
-        lambda i: head_ref.at[pl.ds(i * rows, rows), :],
-        lambda i: out_ref.at[pl.ds(i * rows, rows), :],
-        semaphores,
-        count,
-    )
-    token_ref[...] = jnp.zeros_like(token_ref)
-    for copy in copies:
-        copy.wait()
-
-
-def load_head(after, head):
-    rows = head.shape[0] // 5
-    return pl.pallas_call(
-        functools.partial(load_kernel, rows),
-        in_specs=[ANYWHERE, ANYWHERE],
-        out_specs=[INSIDE, INSIDE],
-        out_shape=[
-            pltpu.VMEM(head.shape, head.dtype),
-            jax.ShapeDtypeStruct((8, LANES), jnp.float32),
-        ],
-        scratch_shapes=[pltpu.SemaphoreType.DMA((5,))],
-        cost_estimate=pl.CostEstimate(
-            flops=0, bytes_accessed=2 * head.size, transcendentals=0
-        ),
-        compiler_params=pltpu.CompilerParams(vmem_limit_bytes=20 << 20),
-        name="vocabulary_rows",
-    )(after, in_hbm(head))
+    )(place, slot_utt, *payloads, *blocks)
 
 
 def vocabulary_kernel(tile, first_ref, *refs):
@@ -625,7 +593,6 @@
         width_count,
         slot_count,
     )
-    head, token = load_head(projected[1], head)
 
     def halve(total, came, axis, distance, side):
         if came is not None:
@@ -644,7 +611,7 @@
     second = halve(*second, "section", 1, section_pos)
     sums = [*first, *second]
     out_rows = normed_rows(
-        place, slot_utt, token, payloads, sums, pieces, slot_tokens, slot_count
+        place, slot_utt, payloads, sums, pieces, slot_tokens, slot_count
     )
 
     own = jnp.zeros((width_count, *out_rows.shape), jnp.bfloat16)

time: 134 us -> 126 us (0.940)
  local copies, waits for them, and re-layouts: 13.7 us -> 8.11 us
  Pallas kernels: 43.7 us -> 38.2 us
  waiting for transfers between devices: 25.1 us -> 28.2 us
    pallas_call x1 -> x0, Pallas kernels: 5.81 us -> none  [load_head(): pl.pallas_call(functools.partial(load_kernel, rows), in_specs=[ANYWHERE,...]
    cond x7 -> x5, local copies, waits for them, and re-layouts: 11.4 us -> 5.73 us
    ppermute x22, waiting for transfers between devices: 24.1 us -> 27.4 us  [swap(): return lax.ppermute(values, axis, pairs)]
  transfers between devices with their start and end apart: 24 -> 24, of which waited for: 11 -> 13; matrix products, arithmetic and copies ran while one was open for 2% -> 2% of each run, Pallas kernels for 19% -> 16%
where the time goes in v12:
time: 126 us
  Pallas kernels  38.2 us (30%)
  starting transfers between devices  35.4 us (28%)
  waiting for transfers between devices  28.2 us (22%)
  blocking collectives  12 us (10%)
  local copies, waits for them, and re-layouts  8.11 us (6%)
  between operations  2.13 us (2%)
  other arithmetic  1.76 us (1%)
    ppermute x22, waiting for transfers between devices, swap(): return lax.ppermute(values, axis, pairs)  27.4 us
    ppermute x22, starting transfers between devices, swap(): return lax.ppermute(values, axis, pairs)  24 us
    pallas_call x3, Pallas kernels, vocabulary_stats(): pl.pallas_call(functools.partial(vocabulary_kernel, head.shape[0] // 2),...  18.4 us
    all_to_all x1, blocking collectives, exchange(): return lax.all_to_all(blocks, axis, split_axis=0, concat_axis=0, tiled=True)  12 us
    all_to_all x2, starting transfers between devices, exchange(): return lax.all_to_all(blocks, axis, split_axis=0, concat_axis=0, tiled=True)  11.4 us
    pallas_call x1, Pallas kernels, queries_of(): pl.pallas_call(functools.partial(query_kernel, count, depth), in_specs=[S...  6.16 us
    cond x5, local copies, waits for them, and re-layouts  5.73 us
    pallas_call x1, Pallas kernels, ffn(): pl.pallas_call(functools.partial(ffn_kernel, tile), in_specs=[SCALARS, IN...  5.62 us
  transfers between devices with their start and end apart: 24, of which 13 were waited for; matrix products, arithmetic and copies ran while one was open for 2% of the time, Pallas kernels for 16%

profile of v12, /device:TPU:0, one launch (start us, length us, event | category | flops | bytes accessed | tf_op | source)
XLA Modules:
  0.0 126.0 jit_solution(17487931687776854363)
XLA Ops:
  0.0 0.1 stack.23.place_ref.after_ref
  0.1 1.0 copy-done.3
  1.1 5.6 %encoder_ffn.1 = (bf16[4,32,1280]{2,1,0:T(8,128)(2,1)}, bf16[32,1280]{1,0:T(8,128)(2,1)S(1)}) custom-call(s32[5]{0:T(128)S(1)} %stack.23.place_ref.after_ref, bf16[32,4,1280]{2,1,0:T(4,128)(2,1)S(1)} %copy-done.3, bf16[1280,1280]{1,0:T(8,128)(2,1)} %up_ref.1, bf16[1280,1280]{1,0:T(8,128)(2,1)} %down_ref.1), custom_call_target="tpu_custom_call" | custom-call | flops 838860800 | bytes 6553600 | tf_op jit(solution)/shard_map/encoder_ffn/pallas_call | solution.py:114
  6.7 6.3 %all-to-all-start.2 = ((bf16[4,32,1280]{2,1,0:T(8,128)(2,1)}), bf16[4,32,1280]{2,1,0:T(8,128)(2,1)S(1)}, u32[]{:S(2)}, u32[]{:S(2)}) async-start(bf16[4,32,1280]{2,1,0:T(8,128)(2,1)} %get-tuple-element.98), calls=%async_computation.2 | async-start | bytes 655360 | tf_op jit(solution)/shard_map/all_to_all | solution.py:31
  13.0 0.1 reshape.27.tok_ref
  13.1 6.2 %hypothesis_queries.1 = (bf16[272,512]{1,0:T(8,128)(2,1)}, bf16[272,512]{1,0:T(8,128)(2,1)S(1)}, bf16[272,512]{1,0:T(8,128)(2,1)S(1)}, bf16[272,512]{1,0:T(8,128)(2,1)S(1)}) custom-call(s32[5]{0:T(128)S(1)} %stack.23.place_ref.after_ref, s32[8]{0:T(128)S(1)} %copy-done.6, s32[2,8]{1,0:T(2,128)S(1)} %copy-done.7, s32[5]{0:T(128)S(1)} %stack.23.place_ref.after_ref, ...), custom_call_target="tpu_custom_call" | custom-call | flops 1073741824 | bytes 6291456 | tf_op jit(solution)/shard_map/hypothesis_queries/pallas_call | solution.py:220
  19.3 0.1 collective-permute-start.37
  19.4 0.5 collective-permute-start.36
  19.9 1.0 collective-permute-done.37
  20.9 0.8 add.122
  21.7 1.5 %collective-permute-start.38 = (bf16[272,512]{1,0:T(8,128)(2,1)}, bf16[272,512]{1,0:T(8,128)(2,1)}, u32[]{:S(2)}, u32[]{:S(2)}) collective-permute-start(bf16[272,512]{1,0:T(8,128)(2,1)} %add.122), channel_id=1, source_target_pairs={{0,8},{4,12},{8,0},{12,4},{1,9},{5,13},{9,1},{13,5},{2,10},{6,14},... | collective-permute-start | bytes 835592 | tf_op jit(solution)/shard_map/ppermute | solution.py:41
  23.3 0.1 all-to-all-done.2.refs_0_
  23.3 1.5 %frame_keys_values.1 = bf16[256,256]{1,0:T(8,128)(2,1)} custom-call(bf16[4,32,1280]{2,1,0:T(8,128)(2,1)S(1)} %all-to-all-done.2.refs_0_, bf16[32,1280]{1,0:T(8,128)(2,1)S(1)} %get-tuple-element.99.refs_1_, bf16[1280,1024]{1,0:T(8,128)(2,1)S(1)} %copy-done.2, bf16[272,512]{1,0:T(8,128)(2,1)} %get-tuple-element.94.refs_3_), custom_call_target="tpu_custom_call" | custom-call | flops 83886080 | bytes 2621440 | tf_op jit(solution)/shard_map/frame_keys_values/pallas_call | solution.py:279
  24.9 5.0 %all-to-all-start.3 = ((bf16[32,8,256]{2,1,0:T(8,128)(2,1)}), bf16[32,8,256]{2,1,0:T(8,128)(2,1)S(1)}, u32[]{:S(2)}, u32[]{:S(2)}) async-start(bf16[32,8,256]{2,1,0:T(8,128)(2,1)} %bitcast.20), calls=%async_computation.3 | async-start | bytes 262144 | tf_op jit(solution)/shard_map/all_to_all | solution.py:31
  29.9 0.1 reduce_sum.9
  30.1 0.7 fusion
  30.8 0.3 collective-permute-start.34
  31.0 1.0 collective-permute-done.34
  33.3 3.1 %collective-permute-start.35 = (s32[1]{0:T(128)}, s32[1]{0:T(128)}, u32[]{:S(2)}, u32[]{:S(2)}) collective-permute-start(s32[1]{0:T(128)} %max.6), channel_id=1, source_target_pairs={{0,8},{4,12},{8,0},{12,4},{1,9},{5,13},{9,1},{13,5},{2,10},{6,14},... | collective-permute-start | bytes 20 | tf_op jit(solution)/shard_map/ppermute | solution.py:41
  36.5 0.4 collective-permute-done.35
  37.6 0.7 all-to-all-done.3
  38.3 87.0 %conditional.1 = (f32[2,8]{1,0:T(2,128)S(1)}) conditional(s32[]{:T(128)} %bitcast.13, (s32[5]{0:T(128)S(1)}, s32[8]{0:T(128)S(1)}, s32[4]{0:T(128)S(1)}, bf16[272,512]{1,0:T(8,128)(2,1)}, bf16[272,512]{1,0:T(8,128)(2,1)}, /*index=5*/bf16[272,512]{1,0:T(8,128)(2,1)}, bf16[32,8,256]{2,1,0:T(8,128)(2,1)S(1)}, bf16[512,4096]{1,0:T(8,128)(2,1)}, ...), branch_computations={%region_2.3_spmd, %region_3.4_spmd} | conditional | flops 13187940352 | bytes 105285184 | solution.py:707
  38.4 3.8 %attention_projection.3 = (bf16[32,4096]{1,0:T(8,128)(2,1)S(1)}, bf16[32,4096]{1,0:T(8,128)(2,1)S(1)}, bf16[16,4096]{1,0:T(8,128)(2,1)S(1)}, bf16[16,4096]{1,0:T(8,128)(2,1)S(1)}) custom-call(s32[5]{0:T(128)S(1)} %get-tuple-element.68.refs_0_.place_ref.first_ref, s32[8]{0:T(128)S(1)} %get-tuple-element.69.refs_1_.slot_ref, s32[4]{0:T(128)S(1)} %get-tuple-element.110.refs_2_, ...), custom_call_target="tpu_custom_call" | custom-call | flops 452984832 | bytes 4980736 | tf_op jit(solution)/shard_map/cond/branch_1_fun/attention_projection/pallas_call | solution.py:367
  42.2 1.4 %collective-permute-start.20 = (bf16[16,4096]{1,0:T(8,128)(2,1)S(1)}, bf16[16,4096]{1,0:T(8,128)(2,1)S(1)}, u32[]{:S(2)}, u32[]{:S(2)}) collective-permute-start(bf16[16,4096]{1,0:T(8,128)(2,1)S(1)} %get-tuple-element.80), channel_id=1, source_target_pairs={{0,1},{1,0},{2,3},{3,2},{4,5},{5,4},{6,7},{7,6},{8,9},{9,8},{10,11... | collective-permute-start | bytes 393224 | tf_op jit(solution)/shard_map/cond/branch_1_fun/ppermute | solution.py:41
  43.5 3.7 %collective-permute-done.20 = bf16[16,4096]{1,0:T(8,128)(2,1)S(1)} collective-permute-done((bf16[16,4096]{1,0:T(8,128)(2,1)S(1)}, bf16[16,4096]{1,0:T(8,128)(2,1)S(1)}, u32[]{:S(2)}, u32[]{:S(2)}) %collective-permute-start.20) | collective-permute-done | bytes 131104 | tf_op jit(solution)/shard_map/cond/branch_1_fun/ppermute | solution.py:41
  47.3 2.3 %collective-permute-start.21 = (bf16[8,4096]{1,0:T(8,128)(2,1)S(1)}, bf16[8,4096]{1,0:T(8,128)(2,1)S(1)}, u32[]{:S(2)}, u32[]{:S(2)}) collective-permute-start(bf16[8,4096]{1,0:T(8,128)(2,1)S(1)} %dynamic-slice_convert_fusion.5), channel_id=1, source_target_pairs={{0,2},{1,3},{2,0},{3,1},{4,6},{5,7},{6,4},{7,5},{8,10},{9,11},{10,... | collective-permute-start | bytes 196616 | tf_op jit(solution)/shard_map/cond/branch_1_fun/ppermute | solution.py:41
  49.5 1.5 %collective-permute-start.17 = (bf16[32,4096]{1,0:T(8,128)(2,1)S(1)}, bf16[32,4096]{1,0:T(8,128)(2,1)S(1)}, u32[]{:S(2)}, u32[]{:S(2)}) collective-permute-start(bf16[32,4096]{1,0:T(8,128)(2,1)S(1)} %get-tuple-element.78), channel_id=1, source_target_pairs={{0,16},{16,0},{1,17},{17,1},{2,18},{18,2},{3,19},{19,3},{4,20},{20... | collective-permute-start | bytes 786440 | tf_op jit(solution)/shard_map/cond/branch_1_fun/ppermute | solution.py:41
  51.0 1.5 %collective-permute-done.21 = bf16[8,4096]{1,0:T(8,128)(2,1)S(1)} collective-permute-done((bf16[8,4096]{1,0:T(8,128)(2,1)S(1)}, bf16[8,4096]{1,0:T(8,128)(2,1)S(1)}, u32[]{:S(2)}, u32[]{:S(2)}) %collective-permute-start.21) | collective-permute-done | bytes 65568 | tf_op jit(solution)/shard_map/cond/branch_1_fun/ppermute | solution.py:41
  52.5 1.4 %collective-permute-start.22 = (bf16[4,4096]{1,0:T(4,128)(2,1)S(1)}, bf16[4,4096]{1,0:T(4,128)(2,1)S(1)}, u32[]{:S(2)}, u32[]{:S(2)}) collective-permute-start(bf16[4,4096]{1,0:T(4,128)(2,1)S(1)} %dynamic-slice_convert_fusion.7), channel_id=1, source_target_pairs={{0,16},{16,0},{1,17},{17,1},{2,18},{18,2},{3,19},{19,3},{4,20},{20... | collective-permute-start | bytes 98312 | tf_op jit(solution)/shard_map/cond/branch_1_fun/ppermute | solution.py:41
  53.9 2.0 %collective-permute-done.17 = bf16[32,4096]{1,0:T(8,128)(2,1)S(1)} collective-permute-done((bf16[32,4096]{1,0:T(8,128)(2,1)S(1)}, bf16[32,4096]{1,0:T(8,128)(2,1)S(1)}, u32[]{:S(2)}, u32[]{:S(2)}) %collective-permute-start.17) | collective-permute-done | bytes 262176 | tf_op jit(solution)/shard_map/cond/branch_1_fun/ppermute | solution.py:41
  55.9 0.1 convert_add_fusion.4
  56.0 1.6 %collective-permute-start.18 = (bf16[16,4096]{1,0:T(8,128)(2,1)S(1)}, bf16[16,4096]{1,0:T(8,128)(2,1)S(1)}, u32[]{:S(2)}, u32[]{:S(2)}) collective-permute-start(bf16[16,4096]{1,0:T(8,128)(2,1)S(1)} %dynamic-slice_convert_fusion.4), channel_id=1, source_target_pairs={{0,1},{1,0},{2,3},{3,2},{4,5},{5,4},{6,7},{7,6},{8,9},{9,8},{10,11... | collective-permute-start | bytes 393224 | tf_op jit(solution)/shard_map/cond/branch_1_fun/ppermute | solution.py:41
  57.6 4.1 %collective-permute-done.18 = bf16[16,4096]{1,0:T(8,128)(2,1)S(1)} collective-permute-done((bf16[16,4096]{1,0:T(8,128)(2,1)S(1)}, bf16[16,4096]{1,0:T(8,128)(2,1)S(1)}, u32[]{:S(2)}, u32[]{:S(2)}) %collective-permute-start.18) | collective-permute-done | bytes 131104 | tf_op jit(solution)/shard_map/cond/branch_1_fun/ppermute | solution.py:41
  61.8 0.9 collective-permute-start.19
  62.7 7.6 %collective-permute-done.19.refs_4_ = bf16[8,4096]{1,0:T(8,128)(2,1)S(1)} collective-permute-done((bf16[8,4096]{1,0:T(8,128)(2,1)S(1)}, bf16[8,4096]{1,0:T(8,128)(2,1)S(1)}, u32[]{:S(2)}, u32[]{:S(2)}) %collective-permute-start.19) | collective-permute-done | bytes 65568 | tf_op jit(solution)/shard_map/cond/branch_1_fun/ppermute | solution.py:41
  70.3 1.3 token_rows.3
  71.5 0.1 collective-permute-start.23
  71.6 2.6 %collective-permute-start.24 = (bf16[3,4,4224]{2,1,0:T(4,128)(2,1)S(1)}, bf16[3,4,4224]{2,1,0:T(4,128)(2,1)S(1)}, u32[]{:S(2)}, u32[]{:S(2)}) collective-permute-start(bf16[3,4,4224]{2,1,0:T(4,128)(2,1)S(1)} %token_rows.3), channel_id=1, source_target_pairs={{0,2},{1,3},{2,0},{3,1},{4,6},{5,7},{6,4},{7,5},{8,10},{9,11},{10,... | collective-permute-start | bytes 304136 | tf_op jit(solution)/shard_map/cond/branch_1_fun/ppermute | solution.py:41
  74.2 1.8 %collective-permute-start.25 = (bf16[3,4,4224]{2,1,0:T(4,128)(2,1)S(1)}, bf16[3,4,4224]{2,1,0:T(4,128)(2,1)S(1)}, u32[]{:S(2)}, u32[]{:S(2)}) collective-permute-start(bf16[3,4,4224]{2,1,0:T(4,128)(2,1)S(1)} %token_rows.3), channel_id=1, source_target_pairs={{0,3},{1,2},{2,1},{3,0},{4,7},{5,6},{6,5},{7,4},{8,11},{9,10},{10,... | collective-permute-start | bytes 304136 | tf_op jit(solution)/shard_map/cond/branch_1_fun/ppermute | solution.py:41
  76.0 0.1 broadcast.11
  76.1 0.1 bitcast_dynamic-update-slice_fusion.7
  76.1 1.2 collective-permute-done.23
  77.4 0.1 bitcast_dynamic-update-slice_fusion.5
  77.4 3.2 %collective-permute-done.25 = bf16[3,4,4224]{2,1,0:T(4,128)(2,1)S(1)} collective-permute-done((bf16[3,4,4224]{2,1,0:T(4,128)(2,1)S(1)}, bf16[3,4,4224]{2,1,0:T(4,128)(2,1)S(1)}, u32[]{:S(2)}, u32[]{:S(2)}) %collective-permute-start.25) | collective-permute-done | bytes 101408 | tf_op jit(solution)/shard_map/cond/branch_1_fun/ppermute | solution.py:41
  80.7 0.1 collective-permute-start.28
  80.8 1.3 %collective-permute-start.26 = (bf16[12,4,4224]{2,1,0:T(4,128)(2,1)S(1)}, bf16[12,4,4224]{2,1,0:T(4,128)(2,1)S(1)}, u32[]{:S(2)}, u32[]{:S(2)}) collective-permute-start(bf16[12,4,4224]{2,1,0:T(4,128)(2,1)S(1)} %bitcast.34), channel_id=1, source_target_pairs={{0,16},{16,0},{1,17},{17,1},{2,18},{18,2},{3,19},{19,3},{4,20},{20... | collective-permute-start | bytes 1216520 | tf_op jit(solution)/shard_map/cond/branch_1_fun/ppermute | solution.py:41
  82.1 1.4 %collective-permute-start.27 = (bf16[12,4,4224]{2,1,0:T(4,128)(2,1)S(1)}, bf16[12,4,4224]{2,1,0:T(4,128)(2,1)S(1)}, u32[]{:S(2)}, u32[]{:S(2)}) collective-permute-start(bf16[12,4,4224]{2,1,0:T(4,128)(2,1)S(1)} %bitcast.35), channel_id=1, source_target_pairs={{0,8},{4,12},{8,0},{12,4},{1,9},{5,13},{9,1},{13,5},{2,10},{6,14},... | collective-permute-start | bytes 1216520 | tf_op jit(solution)/shard_map/cond/branch_1_fun/ppermute | solution.py:41
  83.5 5.7 %copy-done.1 = bf16[2000,4096]{1,0:T(8,128)(2,1)S(1)} copy-done((bf16[2000,4096]{1,0:T(8,128)(2,1)S(1)}, bf16[2000,4096]{1,0:T(8,128)(2,1)}, u32[]{:S(2)}) %copy-start.1) | copy-done | bytes 16384024 | tf_op jit(solution)/shard_map/cond
  89.1 5.9 %vocabulary_scores.9.refs_0_ = f32[2,8,48]{2,1,0:T(8,128)S(1)} custom-call(s32[5]{0:T(128)S(1)} %get-tuple-element.68.refs_0_.place_ref.first_ref, bf16[12,4,4224]{2,1,0:T(4,128)(2,1)S(1)} %bitcast.36, bf16[12,4,4224]{2,1,0:T(4,128)(2,1)S(1)} %collective-permute-done.28.refs_1_, bf16[2000,4096]{1,0:T(8,128)(2,1)S(1)} %copy-done.1), custom_call_target="tpu_custom_call" | custom-call | flops 2359296000 | bytes 786432 | tf_op jit(solution)/shard_map/cond/branch_1_fun/vocabulary_scores/pallas_call | solution.py:477
  95.1 0.5 collective-permute-start.32
  95.6 0.1 slice.10
  95.7 0.1 slice.11
  95.8 0.7 collective-permute-start.29
  96.5 1.0 collective-permute-start.30
  97.5 6.5 %vocabulary_scores.10.refs_1_ = f32[4,8,48]{2,1,0:T(8,128)S(1)} custom-call(s32[5]{0:T(128)S(1)} %get-tuple-element.68.refs_0_.place_ref.first_ref, bf16[12,4,4224]{2,1,0:T(4,128)(2,1)S(1)} %collective-permute-done.27.refs_0_, bf16[12,4,4224]{2,1,0:T(4,128)(2,1)S(1)} %collective-permute-done.31.refs_1_, ...), custom_call_target="tpu_custom_call" | custom-call | flops 4718592000 | bytes 1572864 | tf_op jit(solution)/shard_map/cond/branch_1_fun/vocabulary_scores/pallas_call | solution.py:477
  104.1 0.1 constant_dynamic-update-slice_fusion.3
  104.2 0.1 constant_dynamic-update-slice_fusion.2.refs_0_
  104.3 0.1 collective-permute-start.33
  104.4 1.7 %collective-permute-done.33.refs_1_ = bf16[12,4,4224]{2,1,0:T(4,128)(2,1)S(1)} collective-permute-done((bf16[12,4,4224]{2,1,0:T(4,128)(2,1)S(1)}, bf16[12,4,4224]{2,1,0:T(4,128)(2,1)S(1)}, u32[]{:S(2)}, u32[]{:S(2)}) %collective-permute-start.33) | collective-permute-done | bytes 405536 | tf_op jit(solution)/shard_map/cond/branch_1_fun/ppermute | solution.py:41
  106.1 5.9 %vocabulary_scores.11.refs_2_ = f32[2,8,48]{2,1,0:T(8,128)S(1)} custom-call(s32[5]{0:T(128)S(1)} %get-tuple-element.68.refs_0_.place_ref.first_ref, bf16[12,4,4224]{2,1,0:T(4,128)(2,1)S(1)} %constant_dynamic-update-slice_fusion.2.refs_0_, bf16[12,4,4224]{2,1,0:T(4,128)(2,1)S(1)} %collective-permute-done.33.refs_1_, bf16[2000,4096]{1,0:T(8,128)(2,1)S(1)} %copy-done.1), custom_call_target="tpu_custom_call" | custom-call | flops 2359296000 | bytes 786432 | tf_op jit(solution)/shard_map/cond/branch_1_fun/vocabulary_scores/pallas_call | solution.py:477
  112.0 0.6 statistics_by_group.3
  112.7 12.0 %all_to_all.19.every_ref = f32[32,8,96]{2,1,0:T(8,128)S(1)} all-to-all(f32[32,8,96]{2,1,0:T(8,128)S(1)} %statistics_by_group.3), channel_id=1, replica_groups=mesh['section'=2,'tm'=4,'mp'=4] {'section','tm','mp'}, dimensions={0} | all-to-all | bytes 196608 | tf_op jit(solution)/shard_map/cond/branch_1_fun/all_to_all | solution.py:31
  124.6 0.7 hypothesis_scores.3
  125.4 0.6 copy-done.10
  (38 shorter events, 0.4 us)
Async XLA Ops:
  0.1 1.0 copy-start.3
  1.1 12.0 %copy-start.8 = (s32[2,8,16]{2,1,0:T(8,128)S(1)}, s32[2,8,16]{2,1,0:T(8,128)}, u32[]{:S(2)}) copy-start(s32[2,8,16]{2,1,0:T(8,128)} %param.21) | copy-start | bytes 3076
  1.1 12.0 %copy-start.6 = (s32[8]{0:T(128)S(1)}, s32[8]{0:T(128)}, u32[]{:S(2)}) copy-start(s32[8]{0:T(128)} %slot_ref.1) | copy-start | bytes 100
  1.1 12.0 %copy-start.7 = (s32[2,8]{1,0:T(2,128)S(1)}, s32[2,8]{1,0:T(2,128)}, u32[]{:S(2)}) copy-start(s32[2,8]{1,0:T(2,128)} %length_ref.1) | copy-start | bytes 196
  6.7 16.7 %all-to-all-start.2 = ((bf16[4,32,1280]{2,1,0:T(8,128)(2,1)}), bf16[4,32,1280]{2,1,0:T(8,128)(2,1)S(1)}, u32[]{:S(2)}, u32[]{:S(2)}) async-start(bf16[4,32,1280]{2,1,0:T(8,128)(2,1)} %get-tuple-element.98), calls=%async_computation.2 | async-start | bytes 655360 | tf_op jit(solution)/shard_map/all_to_all | solution.py:31
  13.1 10.2 %copy-start.2 = (bf16[1280,1024]{1,0:T(8,128)(2,1)S(1)}, bf16[1280,1024]{1,0:T(8,128)(2,1)}, u32[]{:S(2)}) copy-start(bf16[1280,1024]{1,0:T(8,128)(2,1)} %refs_2_.1) | copy-start | bytes 7864324
  19.3 19.1 %copy-start.9 = (s32[4]{0:T(128)S(1)}, s32[4]{0:T(128)}, u32[]{:S(2)}) copy-start(s32[4]{0:T(128)} %param.14) | copy-start | bytes 52
  19.3 1.6 %collective-permute-start.37 = (bf16[272,512]{1,0:T(8,128)(2,1)S(1)}, bf16[272,512]{1,0:T(8,128)(2,1)S(1)}, u32[]{:S(2)}, u32[]{:S(2)}) collective-permute-start(bf16[272,512]{1,0:T(8,128)(2,1)S(1)} %get-tuple-element.97), channel_id=1, source_target_pairs={{0,4},{4,0},{8,12},{12,8},{1,5},{5,1},{9,13},{13,9},{2,6},{6,2},{1... | collective-permute-start | bytes 835592 | tf_op jit(solution)/shard_map/ppermute | solution.py:41
  19.4 18.2 %collective-permute-start.36 = (bf16[272,512]{1,0:T(8,128)(2,1)S(1)}, bf16[272,512]{1,0:T(8,128)(2,1)}, u32[]{:S(2)}, u32[]{:S(2)}) collective-permute-start(bf16[272,512]{1,0:T(8,128)(2,1)S(1)} %get-tuple-element.95), channel_id=1, source_target_pairs={{0,4},{4,0},{8,12},{12,8},{1,5},{5,1},{9,13},{13,9},{2,6},{6,2},{1... | collective-permute-start | bytes 835592 | tf_op jit(solution)/shard_map/ppermute | solution.py:41
  21.7 15.9 %collective-permute-start.38 = (bf16[272,512]{1,0:T(8,128)(2,1)}, bf16[272,512]{1,0:T(8,128)(2,1)}, u32[]{:S(2)}, u32[]{:S(2)}) collective-permute-start(bf16[272,512]{1,0:T(8,128)(2,1)} %add.122), channel_id=1, source_target_pairs={{0,8},{4,12},{8,0},{12,4},{1,9},{5,13},{9,1},{13,5},{2,10},{6,14},... | collective-permute-start | bytes 835592 | tf_op jit(solution)/shard_map/ppermute | solution.py:41
  24.9 13.5 %all-to-all-start.3 = ((bf16[32,8,256]{2,1,0:T(8,128)(2,1)}), bf16[32,8,256]{2,1,0:T(8,128)(2,1)S(1)}, u32[]{:S(2)}, u32[]{:S(2)}) async-start(bf16[32,8,256]{2,1,0:T(8,128)(2,1)} %bitcast.20), calls=%async_computation.3 | async-start | bytes 262144 | tf_op jit(solution)/shard_map/all_to_all | solution.py:31
  30.8 1.2 collective-permute-start.34
  33.3 3.6 %collective-permute-start.35 = (s32[1]{0:T(128)}, s32[1]{0:T(128)}, u32[]{:S(2)}, u32[]{:S(2)}) collective-permute-start(s32[1]{0:T(128)} %max.6), channel_id=1, source_target_pairs={{0,8},{4,12},{8,0},{12,4},{1,9},{5,13},{9,1},{13,5},{2,10},{6,14},... | collective-permute-start | bytes 20 | tf_op jit(solution)/shard_map/ppermute | solution.py:41
  38.3 31.9 %copy-start.5 = (bf16[272,512]{1,0:T(8,128)(2,1)S(1)}, bf16[272,512]{1,0:T(8,128)(2,1)}, u32[]{:S(2)}) copy-start(bf16[272,512]{1,0:T(8,128)(2,1)} %get-tuple-element.71.refs_3_.refs_0_) | copy-start | bytes 835588 | tf_op jit(solution)/shard_map/cond
  42.2 5.0 %collective-permute-start.20 = (bf16[16,4096]{1,0:T(8,128)(2,1)S(1)}, bf16[16,4096]{1,0:T(8,128)(2,1)S(1)}, u32[]{:S(2)}, u32[]{:S(2)}) collective-permute-start(bf16[16,4096]{1,0:T(8,128)(2,1)S(1)} %get-tuple-element.80), channel_id=1, source_target_pairs={{0,1},{1,0},{2,3},{3,2},{4,5},{5,4},{6,7},{7,6},{8,9},{9,8},{10,11... | collective-permute-start | bytes 393224 | tf_op jit(solution)/shard_map/cond/branch_1_fun/ppermute | solution.py:41
  47.3 5.2 %collective-permute-start.21 = (bf16[8,4096]{1,0:T(8,128)(2,1)S(1)}, bf16[8,4096]{1,0:T(8,128)(2,1)S(1)}, u32[]{:S(2)}, u32[]{:S(2)}) collective-permute-start(bf16[8,4096]{1,0:T(8,128)(2,1)S(1)} %dynamic-slice_convert_fusion.5), channel_id=1, source_target_pairs={{0,2},{1,3},{2,0},{3,1},{4,6},{5,7},{6,4},{7,5},{8,10},{9,11},{10,... | collective-permute-start | bytes 196616 | tf_op jit(solution)/shard_map/cond/branch_1_fun/ppermute | solution.py:41
  49.5 6.4 %collective-permute-start.17 = (bf16[32,4096]{1,0:T(8,128)(2,1)S(1)}, bf16[32,4096]{1,0:T(8,128)(2,1)S(1)}, u32[]{:S(2)}, u32[]{:S(2)}) collective-permute-start(bf16[32,4096]{1,0:T(8,128)(2,1)S(1)} %get-tuple-element.78), channel_id=1, source_target_pairs={{0,16},{16,0},{1,17},{17,1},{2,18},{18,2},{3,19},{19,3},{4,20},{20... | collective-permute-start | bytes 786440 | tf_op jit(solution)/shard_map/cond/branch_1_fun/ppermute | solution.py:41
  52.5 10.1 %collective-permute-start.22 = (bf16[4,4096]{1,0:T(4,128)(2,1)S(1)}, bf16[4,4096]{1,0:T(4,128)(2,1)S(1)}, u32[]{:S(2)}, u32[]{:S(2)}) collective-permute-start(bf16[4,4096]{1,0:T(4,128)(2,1)S(1)} %dynamic-slice_convert_fusion.7), channel_id=1, source_target_pairs={{0,16},{16,0},{1,17},{17,1},{2,18},{18,2},{3,19},{19,3},{4,20},{20... | collective-permute-start | bytes 98312 | tf_op jit(solution)/shard_map/cond/branch_1_fun/ppermute | solution.py:41
  56.0 5.7 %collective-permute-start.18 = (bf16[16,4096]{1,0:T(8,128)(2,1)S(1)}, bf16[16,4096]{1,0:T(8,128)(2,1)S(1)}, u32[]{:S(2)}, u32[]{:S(2)}) collective-permute-start(bf16[16,4096]{1,0:T(8,128)(2,1)S(1)} %dynamic-slice_convert_fusion.4), channel_id=1, source_target_pairs={{0,1},{1,0},{2,3},{3,2},{4,5},{5,4},{6,7},{7,6},{8,9},{9,8},{10,11... | collective-permute-start | bytes 393224 | tf_op jit(solution)/shard_map/cond/branch_1_fun/ppermute | solution.py:41
  61.8 8.5 %collective-permute-start.19 = (bf16[8,4096]{1,0:T(8,128)(2,1)S(1)}, bf16[8,4096]{1,0:T(8,128)(2,1)S(1)}, u32[]{:S(2)}, u32[]{:S(2)}) collective-permute-start(bf16[8,4096]{1,0:T(8,128)(2,1)S(1)} %dynamic-slice_convert_fusion.6), channel_id=1, source_target_pairs={{0,2},{1,3},{2,0},{3,1},{4,6},{5,7},{6,4},{7,5},{8,10},{9,11},{10,... | collective-permute-start | bytes 196616 | tf_op jit(solution)/shard_map/cond/branch_1_fun/ppermute | solution.py:41
  71.5 5.8 %collective-permute-start.23 = (bf16[3,4,4224]{2,1,0:T(4,128)(2,1)S(1)}, bf16[3,4,4224]{2,1,0:T(4,128)(2,1)S(1)}, u32[]{:S(2)}, u32[]{:S(2)}) collective-permute-start(bf16[3,4,4224]{2,1,0:T(4,128)(2,1)S(1)} %token_rows.3), channel_id=1, source_target_pairs={{0,1},{1,0},{2,3},{3,2},{4,5},{5,4},{6,7},{7,6},{8,9},{9,8},{10,11... | collective-permute-start | bytes 304136 | tf_op jit(solution)/shard_map/cond/branch_1_fun/ppermute | solution.py:41
  71.6 5.8 %collective-permute-start.24 = (bf16[3,4,4224]{2,1,0:T(4,128)(2,1)S(1)}, bf16[3,4,4224]{2,1,0:T(4,128)(2,1)S(1)}, u32[]{:S(2)}, u32[]{:S(2)}) collective-permute-start(bf16[3,4,4224]{2,1,0:T(4,128)(2,1)S(1)} %token_rows.3), channel_id=1, source_target_pairs={{0,2},{1,3},{2,0},{3,1},{4,6},{5,7},{6,4},{7,5},{8,10},{9,11},{10,... | collective-permute-start | bytes 304136 | tf_op jit(solution)/shard_map/cond/branch_1_fun/ppermute | solution.py:41
  74.2 6.4 %collective-permute-start.25 = (bf16[3,4,4224]{2,1,0:T(4,128)(2,1)S(1)}, bf16[3,4,4224]{2,1,0:T(4,128)(2,1)S(1)}, u32[]{:S(2)}, u32[]{:S(2)}) collective-permute-start(bf16[3,4,4224]{2,1,0:T(4,128)(2,1)S(1)} %token_rows.3), channel_id=1, source_target_pairs={{0,3},{1,2},{2,1},{3,0},{4,7},{5,6},{6,5},{7,4},{8,11},{9,10},{10,... | collective-permute-start | bytes 304136 | tf_op jit(solution)/shard_map/cond/branch_1_fun/ppermute | solution.py:41
  80.7 2.8 %collective-permute-start.28 = (bf16[12,4,4224]{2,1,0:T(4,128)(2,1)S(1)}, bf16[12,4,4224]{2,1,0:T(4,128)(2,1)S(1)}, u32[]{:S(2)}, u32[]{:S(2)}) collective-permute-start(bf16[12,4,4224]{2,1,0:T(4,128)(2,1)S(1)} %bitcast.33), channel_id=1, source_target_pairs={{0,4},{4,0},{8,12},{12,8},{1,5},{5,1},{9,13},{13,9},{2,6},{6,2},{1... | collective-permute-start | bytes 1216520 | tf_op jit(solution)/shard_map/cond/branch_1_fun/ppermute | solution.py:41
  80.8 14.3 %collective-permute-start.26 = (bf16[12,4,4224]{2,1,0:T(4,128)(2,1)S(1)}, bf16[12,4,4224]{2,1,0:T(4,128)(2,1)S(1)}, u32[]{:S(2)}, u32[]{:S(2)}) collective-permute-start(bf16[12,4,4224]{2,1,0:T(4,128)(2,1)S(1)} %bitcast.34), channel_id=1, source_target_pairs={{0,16},{16,0},{1,17},{17,1},{2,18},{18,2},{3,19},{19,3},{4,20},{20... | collective-permute-start | bytes 1216520 | tf_op jit(solution)/shard_map/cond/branch_1_fun/ppermute | solution.py:41
  82.1 13.0 %collective-permute-start.27 = (bf16[12,4,4224]{2,1,0:T(4,128)(2,1)S(1)}, bf16[12,4,4224]{2,1,0:T(4,128)(2,1)S(1)}, u32[]{:S(2)}, u32[]{:S(2)}) collective-permute-start(bf16[12,4,4224]{2,1,0:T(4,128)(2,1)S(1)} %bitcast.35), channel_id=1, source_target_pairs={{0,8},{4,12},{8,0},{12,4},{1,9},{5,13},{9,1},{13,5},{2,10},{6,14},... | collective-permute-start | bytes 1216520 | tf_op jit(solution)/shard_map/cond/branch_1_fun/ppermute | solution.py:41
  83.5 5.7 %copy-start.1 = (bf16[2000,4096]{1,0:T(8,128)(2,1)S(1)}, bf16[2000,4096]{1,0:T(8,128)(2,1)}, u32[]{:S(2)}) copy-start(bf16[2000,4096]{1,0:T(8,128)(2,1)} %get-tuple-element.114.refs_2_.refs_4_) | copy-start | bytes 49152004 | tf_op jit(solution)/shard_map/cond
  95.1 2.4 %collective-permute-start.31 = (bf16[12,4,4224]{2,1,0:T(4,128)(2,1)S(1)}, bf16[12,4,4224]{2,1,0:T(4,128)(2,1)S(1)}, u32[]{:S(2)}, u32[]{:S(2)}) collective-permute-start(bf16[12,4,4224]{2,1,0:T(4,128)(2,1)S(1)} %collective-permute-done.27.refs_0_), channel_id=1, source_target_pairs={{0,4},{4,0},{8,12},{12,8},{1,5},{5,1},{9,13},{13,9},{2,6},{6,2},{1... | collective-permute-start | bytes 1216520 | tf_op jit(solution)/shard_map/cond/branch_1_fun/ppermute | solution.py:41
  95.1 2.4 %collective-permute-start.32 = (bf16[12,4,4224]{2,1,0:T(4,128)(2,1)S(1)}, bf16[12,4,4224]{2,1,0:T(4,128)(2,1)S(1)}, u32[]{:S(2)}, u32[]{:S(2)}) collective-permute-start(bf16[12,4,4224]{2,1,0:T(4,128)(2,1)S(1)} %collective-permute-done.26.refs_2_), channel_id=1, source_target_pairs={{0,4},{4,0},{8,12},{12,8},{1,5},{5,1},{9,13},{13,9},{2,6},{6,2},{1... | collective-permute-start | bytes 1216520 | tf_op jit(solution)/shard_map/cond/branch_1_fun/ppermute | solution.py:41
  95.8 8.3 %collective-permute-start.29 = (bf16[6,4,4224]{2,1,0:T(4,128)(2,1)S(1)}, bf16[6,4,4224]{2,1,0:T(4,128)(2,1)S(1)}, u32[]{:S(2)}, u32[]{:S(2)}) collective-permute-start(bf16[6,4,4224]{2,1,0:T(4,128)(2,1)S(1)} %slice.10), channel_id=1, source_target_pairs={{0,8},{4,12},{8,0},{12,4},{1,9},{5,13},{9,1},{13,5},{2,10},{6,14},... | collective-permute-start | bytes 608264 | tf_op jit(solution)/shard_map/cond/branch_1_fun/ppermute | solution.py:41
  96.5 7.6 %collective-permute-start.30 = (bf16[6,4,4224]{2,1,0:T(4,128)(2,1)S(1)}, bf16[6,4,4224]{2,1,0:T(4,128)(2,1)S(1)}, u32[]{:S(2)}, u32[]{:S(2)}) collective-permute-start(bf16[6,4,4224]{2,1,0:T(4,128)(2,1)S(1)} %slice.11), channel_id=1, source_target_pairs={{0,16},{16,0},{1,17},{17,1},{2,18},{18,2},{3,19},{19,3},{4,20},{20... | collective-permute-start | bytes 608264 | tf_op jit(solution)/shard_map/cond/branch_1_fun/ppermute | solution.py:41
  104.3 1.8 %collective-permute-start.33 = (bf16[12,4,4224]{2,1,0:T(4,128)(2,1)S(1)}, bf16[12,4,4224]{2,1,0:T(4,128)(2,1)S(1)}, u32[]{:S(2)}, u32[]{:S(2)}) collective-permute-start(bf16[12,4,4224]{2,1,0:T(4,128)(2,1)S(1)} %constant_dynamic-update-slice_fusion.2.refs_0_), channel_id=1, source_target_pairs={{0,4},{4,0},{8,12},{12,8},{1,5},{5,1},{9,13},{13,9},{2,6},{6,2},{1... | collective-permute-start | bytes 1216520 | tf_op jit(solution)/shard_map/cond/branch_1_fun/ppermute | solution.py:41
  125.4 0.6 copy-start.10

commit v13 on v12

--- a/solution.py
+++ b/solution.py
@@ -340,7 +340,7 @@
     block = at % size // pieces[1]
     low = jnp.where(at < size, 1 - low_bit, low_bit)
     row = pieces[0] + at % pieces[1]
-    second_order = (row * sections + block % 2) * widths + block // 2 * 2 + low
+    second_order = (row * sections + block // 2) * widths + block % 2 * 2 + low
     move = come == jnp.where(at < 0, first_order, second_order)
     ordered = dot(jnp.where(move, 1.0, 0.0).astype(jnp.bfloat16), context[...])
     ordered = ordered.astype(jnp.bfloat16)
@@ -387,9 +387,62 @@
     )(place, slot_utt, frame_len, *payloads, keys_values, in_hbm(weights))
 
 
-def norm_kernel(count, slots, tokens, pieces, place_ref, slot_ref, *refs):
-    payloads, blocks = refs[:count], refs[count : count + 2 * len(pieces)]
-    out_ref, picked, total = refs[count + 2 * len(pieces) :]
+def fold_kernel(sides, joined, place_ref, *refs):
+    count = len(sides)
+    parts, outs = refs[: 2 * count], refs[2 * count :]
+    first = 0
+    for number, side in enumerate(sides):
+        kept_ref, came_ref = parts[2 * number : 2 * number + 2]
+        total = kept_ref[...].astype(jnp.float32) + came_ref[...].astype(jnp.float32)
+        half = total.shape[0] // 2
+        top, bottom = total[:half], total[half:]
+        upper = side(place_ref) == 0
+        kept = jnp.where(upper, top, bottom)
+        sent = jnp.where(upper, bottom, top).astype(jnp.bfloat16)
+        if joined:
+            outs[0][first : first + half, :] = kept
+            outs[1][first : first + half, :] = sent
+            first += half
+        else:
+            outs[2 * number][...] = kept
+            outs[2 * number + 1][...] = sent
+
+
+def fold(place, parts, sides, joined):
+    width = parts[0].shape[1]
+    halves = [part.shape[0] // 2 for part in parts[::2]]
+    if joined:
+        halves = [sum(halves)]
+    shapes = [
+        jax.ShapeDtypeStruct((half, width), kind)
+        for half in halves
+        for kind in (jnp.float32, jnp.bfloat16)
+    ]
+    return pl.pallas_call(
+        functools.partial(fold_kernel, sides, joined),
+        in_specs=[SCALARS] + [INSIDE] * len(parts),
+        out_specs=[INSIDE] * len(shapes),
+        out_shape=shapes,
+        compiler_params=pltpu.CompilerParams(vmem_limit_bytes=24 << 20),
+        name="sum_phase",
+    )(place, *parts)
+
+
+def section_side(place_ref):
+    return place_ref[0]
+
+
+def low_side(place_ref):
+    return place_ref[2] % 2
+
+
+def high_side(place_ref):
+    return place_ref[2] // 2
+
+
+def norm_kernel(count, slots, tokens, place_ref, slot_ref, *refs):
+    payloads, (kept, other) = refs[:count], refs[count : count + 2]
+    out_ref, picked, total = refs[count + 2 :]
     rows, width = total.shape
     columns = picked.shape[1]
     share = picked.shape[0] // (width // columns + 1)
@@ -400,11 +453,7 @@
         def _(payload=payloads[choice]):
             picked[...] = payload[tokens:, :]
 
-    first = 0
-    for number, piece in enumerate(pieces):
-        kept, other = blocks[2 * number : 2 * number + 2]
-        total[first : first + piece, :] = kept[...] + other[...].astype(jnp.float32)
-        first += piece
+    total[...] = kept[...] + other[...].astype(jnp.float32)
     for part in range(width // columns):
         take = slice(part * columns, (part + 1) * columns)
         total[:, take] += picked[part * share : part * share + rows, :].astype(jnp.float32)
@@ -416,12 +465,12 @@
     out_ref[:, :, width:] = target.astype(jnp.bfloat16)
 
 
-def normed_rows(place, slot_utt, payloads, blocks, pieces, tokens, slots):
+def normed_rows(place, slot_utt, payloads, blocks, tokens, slots):
     width = blocks[0].shape[1]
-    rows = sum(pieces)
+    rows = blocks[0].shape[0]
     columns = payloads[0].shape[1]
     return pl.pallas_call(
-        functools.partial(norm_kernel, len(payloads), slots, tokens, pieces),
+        functools.partial(norm_kernel, len(payloads), slots, tokens),
         in_specs=[SCALARS] * 2 + [INSIDE] * (len(payloads) + len(blocks)),
         out_specs=INSIDE,
         out_shape=jax.ShapeDtypeStruct((rows // FOLD, FOLD, width + LANES), jnp.bfloat16),
@@ -434,11 +483,21 @@
     )(place, slot_utt, *payloads, *blocks)
 
 
-def vocabulary_kernel(tile, first_ref, *refs):
-    sets, (head_ref, out_ref, rows_ref, stat) = refs[:-4], refs[-4:]
+def vocabulary_kernel(tile, count, first_ref, *refs):
+    sets, head_ref, out_ref = refs[:count], refs[count], refs[count + 1]
+    loaded_ref, semaphores = (refs[count + 2], refs[-1]) if len(refs) > count + 4 else (None, None)
+    rows_ref, stat = refs[-3:-1] if loaded_ref is not None else refs[-2:]
     vocab_rows, width = head_ref.shape
     share = sets[0].shape[0] * FOLD
     tokens = share * len(sets)
+    tiles = vocab_rows // tile
+    if loaded_ref is not None:
+        copies = start_copies(
+            lambda i: head_ref.at[pl.ds(i * tile, tile), :],
+            lambda i: loaded_ref.at[pl.ds(i * tile, tile), :],
+            semaphores,
+            tiles,
+        )
     cell = lax.broadcasted_iota(jnp.int32, (8, LANES), 1)
     take = jnp.where(cell == 0, 256.0, jnp.where(cell == 1, 1.0, 0.0)).astype(jnp.bfloat16)
     for number, rows in enumerate(sets):
@@ -449,10 +508,8 @@
     stat[8:9, :] = jnp.zeros((1, tokens), jnp.float32)
     stat[16:17, :] = jnp.zeros((1, tokens), jnp.float32)
 
-    @pl.loop(0, vocab_rows // tile)
-    def _(step):
-        start = pl.multiple_of(step * tile, tile)
-        logits = dot_nt(head_ref[pl.ds(start, tile), :], rows_ref[:, :width])
+    def one_tile(start, block):
+        logits = dot_nt(block, rows_ref[:, :width])
         vocab = lax.broadcasted_iota(jnp.int32, logits.shape, 0) + start
         before = stat[0:1, :]
         upper = jnp.maximum(before, jnp.max(logits, axis=0, keepdims=True))
@@ -462,6 +519,17 @@
         stat[16:17, :] += jnp.sum(jnp.where(vocab == target, logits, 0.0), axis=0, keepdims=True)
         stat[0:1, :] = upper
 
+    if loaded_ref is not None:
+        for number in range(tiles):
+            copies[number].wait()
+            one_tile(number * tile, loaded_ref[number * tile : (number + 1) * tile, :])
+    else:
+
+        @pl.loop(0, tiles)
+        def _(step):
+            start = pl.multiple_of(step * tile, tile)
+            one_tile(start, head_ref[pl.ds(start, tile), :])
+
     for number in range(len(sets)):
         for row in range(3):
             out_ref[number, row : row + 1, :] = stat[
@@ -469,28 +537,35 @@
             ]
 
 
-def vocabulary_stats(place, sets, head):
+def vocabulary_stats(place, sets, head, load=False):
     share = sets[0].shape[0] * FOLD
     count = len(sets)
     width = head.shape[1]
     tokens = share * count
+    tile = head.shape[0] // (5 if load else 2)
+    stats = jax.ShapeDtypeStruct((count, 8, share), jnp.float32)
     return pl.pallas_call(
-        functools.partial(vocabulary_kernel, head.shape[0] // 2),
-        in_specs=[SCALARS] + [INSIDE] * (count + 1),
-        out_specs=INSIDE,
-        out_shape=jax.ShapeDtypeStruct((count, 8, share), jnp.float32),
+        functools.partial(vocabulary_kernel, tile, count),
+        in_specs=[SCALARS] + [INSIDE] * count + [ANYWHERE if load else INSIDE],
+        out_specs=[INSIDE] * 2 if load else INSIDE,
+        out_shape=[stats, pltpu.VMEM(head.shape, head.dtype)] if load else stats,
         scratch_shapes=[
             pltpu.VMEM((tokens, width + LANES), jnp.bfloat16),
             pltpu.VMEM((24, tokens), jnp.float32),
-        ],
+        ]
+        + ([pltpu.SemaphoreType.DMA((5,))] if load else []),
         cost_estimate=pl.CostEstimate(
             flops=3 * tokens * head.shape[0] * width,
             bytes_accessed=2 * tokens * width,
             transcendentals=tokens * head.shape[0],
         ),
-        compiler_params=pltpu.CompilerParams(vmem_limit_bytes=16 << 20),
+        compiler_params=pltpu.CompilerParams(vmem_limit_bytes=(36 if load else 16) << 20),
         name="vocabulary_scores",
-    )(place, *sets, pltpu.with_memory_space_constraint(head, pltpu.VMEM))
+    )(
+        place,
+        *sets,
+        in_hbm(head) if load else pltpu.with_memory_space_constraint(head, pltpu.VMEM),
+    )
 
 
 def spread_kernel(sections, groups, widths, place_ref, slot_ref, *refs):
@@ -594,24 +669,20 @@
         slot_count,
     )
 
-    def halve(total, came, axis, distance, side):
-        if came is not None:
-            total = total + came.astype(jnp.float32)
-        half = total.shape[0] // 2
-        kept = lax.dynamic_slice_in_dim(total, side * half, half, 0)
-        sent = lax.dynamic_slice_in_dim(total, (1 - side) * half, half, 0)
-        return kept, swap(sent.astype(jnp.bfloat16), axis, distance)
-
-    low, high = width_pos % 2, width_pos // 2
-    first = projected[1].astype(jnp.float32), swap(projected[0], "section", 1)
-    second = projected[3].astype(jnp.float32), swap(projected[2], "mp", 1)
-    first = halve(*first, "mp", 1, low)
-    second = halve(*second, "mp", 2, high)
-    first = halve(*first, "mp", 2, high)
-    second = halve(*second, "section", 1, section_pos)
-    sums = [*first, *second]
+    kept, sent, other_kept, other_sent = fold(
+        place,
+        [projected[1], swap(projected[0], "section", 1), projected[3], swap(projected[2], "mp", 1)],
+        [low_side, section_side],
+        False,
+    )
+    kept, sent = fold(
+        place,
+        [kept, swap(sent, "mp", 1), other_kept, swap(other_sent, "section", 1)],
+        [high_side, high_side],
+        True,
+    )
     out_rows = normed_rows(
-        place, slot_utt, payloads, sums, pieces, slot_tokens, slot_count
+        place, slot_utt, payloads, [kept, swap(sent, "mp", 2)], slot_tokens, slot_count
     )
 
     own = jnp.zeros((width_count, *out_rows.shape), jnp.bfloat16)
@@ -622,13 +693,12 @@
     half = own.shape[0] // 2
     by_x = swap(own, "section", 1)
     by_y = swap(own, "tm", 2)
-    stats = [vocabulary_stats(place, [own, swap(own, "tm", 1)], head)]
-    by_x, by_y, stats[0] = lax.optimization_barrier((by_x, by_y, stats[0]))
+    stats, head = vocabulary_stats(place, [own, swap(own, "tm", 1)], head, load=True)
+    stats = [stats]
     across = [swap(by_x[:half], "tm", 2), swap(by_y[half:], "section", 1)]
     stats.append(
         vocabulary_stats(place, [by_y, swap(by_y, "tm", 1), by_x, swap(by_x, "tm", 1)], head)
     )
-    *across, stats[1] = lax.optimization_barrier((*across, stats[1]))
     across = jnp.concatenate(across)
     stats.append(vocabulary_stats(place, [across, swap(across, "tm", 1)], head))
 

time: 126 us -> 126 us (level)
  Pallas kernels: 38.2 us -> 44.6 us
  local copies, waits for them, and re-layouts: 8.11 us -> 2.34 us
  blocking collectives: 12 us -> 10.7 us
    pallas_call x3 -> x5, Pallas kernels: 18.4 us -> 25 us  [the longest x3 23.8 us: vocabulary_stats(): pl.pallas_call(functools.partial(vocabulary_kernel, tile, count), in_spec...]
    cond x5 -> x3, local copies, waits for them, and re-layouts: 5.73 us -> 0.08 us
    all_to_all x1, blocking collectives: 12 us -> 10.7 us  [exchange(): return lax.all_to_all(blocks, axis, split_axis=0, concat_axis=0, tiled=True)]
    ppermute x22 -> x21, starting transfers between devices: 24 us -> 25 us  [swap(): return lax.ppermute(values, axis, pairs)]
    ppermute x22 -> x21, waiting for transfers between devices: 27.4 us -> 27 us  [swap(): return lax.ppermute(values, axis, pairs)]
  transfers between devices with their start and end apart: 24 -> 23, of which waited for: 13 -> 14; matrix products, arithmetic and copies ran while one was open for 2% -> 2% of each run, Pallas kernels for 16% -> 20%
where the time goes in v13:
time: 126 us
  Pallas kernels  44.6 us (35%)
  starting transfers between devices  36.4 us (29%)
  waiting for transfers between devices  27.8 us (22%)
  blocking collectives  10.7 us (8%)
  local copies, waits for them, and re-layouts  2.34 us (2%)
  between operations  2.02 us (2%)
  other arithmetic  1.63 us (1%)
    ppermute x21, waiting for transfers between devices, swap(): return lax.ppermute(values, axis, pairs)  27 us
    ppermute x21, starting transfers between devices, swap(): return lax.ppermute(values, axis, pairs)  25 us
    pallas_call x3, Pallas kernels, vocabulary_stats(): pl.pallas_call(functools.partial(vocabulary_kernel, tile, count), in_spec...  23.8 us
    all_to_all x2, starting transfers between devices, exchange(): return lax.all_to_all(blocks, axis, split_axis=0, concat_axis=0, tiled=True)  11.4 us
    all_to_all x1, blocking collectives, exchange(): return lax.all_to_all(blocks, axis, split_axis=0, concat_axis=0, tiled=True)  10.7 us
    pallas_call x1, Pallas kernels, queries_of(): pl.pallas_call(functools.partial(query_kernel, count, depth), in_specs=[S...  5.93 us
    pallas_call x1, Pallas kernels, ffn(): pl.pallas_call(functools.partial(ffn_kernel, tile), in_specs=[SCALARS, IN...  5.62 us
    pallas_call x1, Pallas kernels, attend(): pl.pallas_call(functools.partial(attention_kernel, count, slots, capacity...  3.81 us
  transfers between devices with their start and end apart: 23, of which 14 were waited for; matrix products, arithmetic and copies ran while one was open for 2% of the time, Pallas kernels for 20%

profile of v13, /device:TPU:0, one launch (start us, length us, event | category | flops | bytes accessed | tf_op | source)
XLA Modules:
  0.0 125.5 jit_solution(2847942233458244993)
XLA Ops:
  0.0 0.1 stack.23.place_ref.after_ref
  0.1 1.0 copy-done.1
  1.1 5.6 %encoder_ffn.1 = (bf16[4,32,1280]{2,1,0:T(8,128)(2,1)}, bf16[32,1280]{1,0:T(8,128)(2,1)S(1)}) custom-call(s32[5]{0:T(128)S(1)} %stack.23.place_ref.after_ref, bf16[32,4,1280]{2,1,0:T(4,128)(2,1)S(1)} %copy-done.1, bf16[1280,1280]{1,0:T(8,128)(2,1)} %up_ref.1, bf16[1280,1280]{1,0:T(8,128)(2,1)} %down_ref.1), custom_call_target="tpu_custom_call" | custom-call | flops 838860800 | bytes 6553600 | tf_op jit(solution)/shard_map/encoder_ffn/pallas_call | solution.py:114
  6.7 6.6 %all-to-all-start.2 = ((bf16[4,32,1280]{2,1,0:T(8,128)(2,1)}), bf16[4,32,1280]{2,1,0:T(8,128)(2,1)S(1)}, u32[]{:S(2)}, u32[]{:S(2)}) async-start(bf16[4,32,1280]{2,1,0:T(8,128)(2,1)} %get-tuple-element.102), calls=%async_computation.2 | async-start | bytes 655360 | tf_op jit(solution)/shard_map/all_to_all | solution.py:31
  13.3 0.1 reshape.27.tok_ref
  13.4 5.9 %hypothesis_queries.1 = (bf16[272,512]{1,0:T(8,128)(2,1)}, bf16[272,512]{1,0:T(8,128)(2,1)S(1)}, bf16[272,512]{1,0:T(8,128)(2,1)S(1)}, bf16[272,512]{1,0:T(8,128)(2,1)S(1)}) custom-call(s32[5]{0:T(128)S(1)} %stack.23.place_ref.after_ref, s32[8]{0:T(128)S(1)} %copy-done.4, s32[2,8]{1,0:T(2,128)S(1)} %copy-done.5, s32[5]{0:T(128)S(1)} %stack.23.place_ref.after_ref, ...), custom_call_target="tpu_custom_call" | custom-call | flops 1073741824 | bytes 6291456 | tf_op jit(solution)/shard_map/hypothesis_queries/pallas_call | solution.py:220
  19.3 0.1 collective-permute-start.35
  19.4 0.5 collective-permute-start.34
  19.9 1.0 collective-permute-done.35
  21.0 0.8 add.45
  21.8 1.5 %collective-permute-start.36 = (bf16[272,512]{1,0:T(8,128)(2,1)}, bf16[272,512]{1,0:T(8,128)(2,1)}, u32[]{:S(2)}, u32[]{:S(2)}) collective-permute-start(bf16[272,512]{1,0:T(8,128)(2,1)} %add.45), channel_id=1, source_target_pairs={{0,8},{4,12},{8,0},{12,4},{1,9},{5,13},{9,1},{13,5},{2,10},{6,14},... | collective-permute-start | bytes 835592 | tf_op jit(solution)/shard_map/ppermute | solution.py:41
  23.3 0.3 all-to-all-done.2.refs_0_
  23.6 1.5 %frame_keys_values.1 = bf16[256,256]{1,0:T(8,128)(2,1)} custom-call(bf16[4,32,1280]{2,1,0:T(8,128)(2,1)S(1)} %all-to-all-done.2.refs_0_, bf16[32,1280]{1,0:T(8,128)(2,1)S(1)} %get-tuple-element.103.refs_1_, bf16[1280,1024]{1,0:T(8,128)(2,1)S(1)} %copy-done, bf16[272,512]{1,0:T(8,128)(2,1)} %get-tuple-element.98.refs_3_), custom_call_target="tpu_custom_call" | custom-call | flops 83886080 | bytes 2621440 | tf_op jit(solution)/shard_map/frame_keys_values/pallas_call | solution.py:279
  25.2 4.8 %all-to-all-start.3 = ((bf16[32,8,256]{2,1,0:T(8,128)(2,1)}), bf16[32,8,256]{2,1,0:T(8,128)(2,1)S(1)}, u32[]{:S(2)}, u32[]{:S(2)}) async-start(bf16[32,8,256]{2,1,0:T(8,128)(2,1)} %bitcast.20), calls=%async_computation.3 | async-start | bytes 262144 | tf_op jit(solution)/shard_map/all_to_all | solution.py:31
  30.0 0.1 reduce_sum.9
  30.1 0.7 fusion
  30.8 0.3 collective-permute-start.32
  31.1 1.1 collective-permute-done.32
  33.5 3.1 %collective-permute-start.33 = (s32[1]{0:T(128)}, s32[1]{0:T(128)}, u32[]{:S(2)}, u32[]{:S(2)}) collective-permute-start(s32[1]{0:T(128)} %max.6), channel_id=1, source_target_pairs={{0,8},{4,12},{8,0},{12,4},{1,9},{5,13},{9,1},{13,5},{2,10},{6,14},... | collective-permute-start | bytes 20 | tf_op jit(solution)/shard_map/ppermute | solution.py:41
  36.6 0.6 collective-permute-done.33
  37.9 0.5 all-to-all-done.3
  38.4 86.6 %conditional.1 = (f32[2,8]{1,0:T(2,128)S(1)}) conditional(s32[]{:T(128)} %bitcast.13, (s32[5]{0:T(128)S(1)}, s32[8]{0:T(128)S(1)}, s32[4]{0:T(128)S(1)}, bf16[272,512]{1,0:T(8,128)(2,1)}, bf16[272,512]{1,0:T(8,128)(2,1)}, /*index=5*/bf16[272,512]{1,0:T(8,128)(2,1)}, bf16[32,8,256]{2,1,0:T(8,128)(2,1)S(1)}, bf16[512,4096]{1,0:T(8,128)(2,1)}, ...), branch_computations={%region_2.3_spmd, %region_3.4_spmd} | conditional | flops 13186891776 | bytes 35029880 | solution.py:777
  38.4 3.8 %attention_projection.3 = (bf16[32,4096]{1,0:T(8,128)(2,1)S(1)}, bf16[32,4096]{1,0:T(8,128)(2,1)S(1)}, bf16[16,4096]{1,0:T(8,128)(2,1)S(1)}, bf16[16,4096]{1,0:T(8,128)(2,1)S(1)}) custom-call(s32[5]{0:T(128)S(1)} %get-tuple-element.70.refs_0_.place_ref.first_ref, s32[8]{0:T(128)S(1)} %get-tuple-element.71.refs_1_.slot_ref, s32[4]{0:T(128)S(1)} %get-tuple-element.114.refs_2_, ...), custom_call_target="tpu_custom_call" | custom-call | flops 452984832 | bytes 4980736 | tf_op jit(solution)/shard_map/cond/branch_1_fun/attention_projection/pallas_call | solution.py:367
  42.2 1.6 %collective-permute-start.16 = (bf16[32,4096]{1,0:T(8,128)(2,1)S(1)}, bf16[32,4096]{1,0:T(8,128)(2,1)S(1)}, u32[]{:S(2)}, u32[]{:S(2)}) collective-permute-start(bf16[32,4096]{1,0:T(8,128)(2,1)S(1)} %get-tuple-element.80), channel_id=1, source_target_pairs={{0,16},{16,0},{1,17},{17,1},{2,18},{18,2},{3,19},{19,3},{4,20},{20... | collective-permute-start | bytes 786440 | tf_op jit(solution)/shard_map/cond/branch_1_fun/ppermute | solution.py:41
  43.8 1.5 %collective-permute-start.17 = (bf16[16,4096]{1,0:T(8,128)(2,1)S(1)}, bf16[16,4096]{1,0:T(8,128)(2,1)S(1)}, u32[]{:S(2)}, u32[]{:S(2)}) collective-permute-start(bf16[16,4096]{1,0:T(8,128)(2,1)S(1)} %get-tuple-element.82), channel_id=1, source_target_pairs={{0,1},{1,0},{2,3},{3,2},{4,5},{5,4},{6,7},{7,6},{8,9},{9,8},{10,11... | collective-permute-start | bytes 393224 | tf_op jit(solution)/shard_map/cond/branch_1_fun/ppermute | solution.py:41
  45.2 3.5 %collective-permute-done.17.refs_3_ = bf16[16,4096]{1,0:T(8,128)(2,1)S(1)} collective-permute-done((bf16[16,4096]{1,0:T(8,128)(2,1)S(1)}, bf16[16,4096]{1,0:T(8,128)(2,1)S(1)}, u32[]{:S(2)}, u32[]{:S(2)}) %collective-permute-start.17) | collective-permute-done | bytes 131104 | tf_op jit(solution)/shard_map/cond/branch_1_fun/ppermute | solution.py:41
  48.7 0.9 collective-permute-done.16.refs_1_
  49.6 0.7 sum_phase.6
  50.3 1.4 %collective-permute-start.18 = (bf16[16,4096]{1,0:T(8,128)(2,1)S(1)}, bf16[16,4096]{1,0:T(8,128)(2,1)S(1)}, u32[]{:S(2)}, u32[]{:S(2)}) collective-permute-start(bf16[16,4096]{1,0:T(8,128)(2,1)S(1)} %get-tuple-element.84), channel_id=1, source_target_pairs={{0,1},{1,0},{2,3},{3,2},{4,5},{5,4},{6,7},{7,6},{8,9},{9,8},{10,11... | collective-permute-start | bytes 393224 | tf_op jit(solution)/shard_map/cond/branch_1_fun/ppermute | solution.py:41
  51.7 1.4 %collective-permute-start.19 = (bf16[8,4096]{1,0:T(8,128)(2,1)S(1)}, bf16[8,4096]{1,0:T(8,128)(2,1)S(1)}, u32[]{:S(2)}, u32[]{:S(2)}) collective-permute-start(bf16[8,4096]{1,0:T(8,128)(2,1)S(1)} %get-tuple-element.86), channel_id=1, source_target_pairs={{0,16},{16,0},{1,17},{17,1},{2,18},{18,2},{3,19},{19,3},{4,20},{20... | collective-permute-start | bytes 196616 | tf_op jit(solution)/shard_map/cond/branch_1_fun/ppermute | solution.py:41
  53.1 2.9 %collective-permute-done.19.refs_3_ = bf16[8,4096]{1,0:T(8,128)(2,1)S(1)} collective-permute-done((bf16[8,4096]{1,0:T(8,128)(2,1)S(1)}, bf16[8,4096]{1,0:T(8,128)(2,1)S(1)}, u32[]{:S(2)}, u32[]{:S(2)}) %collective-permute-start.19) | collective-permute-done | bytes 65568 | tf_op jit(solution)/shard_map/cond/branch_1_fun/ppermute | solution.py:41
  56.0 0.6 sum_phase.7
  56.6 2.4 %collective-permute-start.20 = (bf16[12,4096]{1,0:T(8,128)(2,1)S(1)}, bf16[12,4096]{1,0:T(8,128)(2,1)S(1)}, u32[]{:S(2)}, u32[]{:S(2)}) collective-permute-start(bf16[12,4096]{1,0:T(8,128)(2,1)S(1)} %get-tuple-element.88), channel_id=1, source_target_pairs={{0,2},{1,3},{2,0},{3,1},{4,6},{5,7},{6,4},{7,5},{8,10},{9,11},{10,... | collective-permute-start | bytes 294920 | tf_op jit(solution)/shard_map/cond/branch_1_fun/ppermute | solution.py:41
  59.0 5.0 %collective-permute-done.20.refs_4_ = bf16[12,4096]{1,0:T(8,128)(2,1)S(1)} collective-permute-done((bf16[12,4096]{1,0:T(8,128)(2,1)S(1)}, bf16[12,4096]{1,0:T(8,128)(2,1)S(1)}, u32[]{:S(2)}, u32[]{:S(2)}) %collective-permute-start.20) | collective-permute-done | bytes 98336 | tf_op jit(solution)/shard_map/cond/branch_1_fun/ppermute | solution.py:41
  64.0 1.3 %token_rows.3 = bf16[3,4,4224]{2,1,0:T(4,128)(2,1)S(1)} custom-call(s32[5]{0:T(128)S(1)} %get-tuple-element.70.refs_0_.place_ref.first_ref, s32[8]{0:T(128)S(1)} %get-tuple-element.71.refs_1_.slot_ref, bf16[272,512]{1,0:T(8,128)(2,1)S(1)} %copy-done.3, bf16[272,512]{1,0:T(8,128)(2,1)} %get-tuple-element.74.refs_4_.refs_1_, ...), custom_call_target="tpu_custom_call" | custom-call | tf_op jit(solution)/shard_map/cond/branch_1_fun/token_rows/pallas_call | solution.py:472
  65.3 0.1 collective-permute-start.21
  65.3 3.0 %collective-permute-start.22 = (bf16[3,4,4224]{2,1,0:T(4,128)(2,1)S(1)}, bf16[3,4,4224]{2,1,0:T(4,128)(2,1)S(1)}, u32[]{:S(2)}, u32[]{:S(2)}) collective-permute-start(bf16[3,4,4224]{2,1,0:T(4,128)(2,1)S(1)} %token_rows.3), channel_id=1, source_target_pairs={{0,2},{1,3},{2,0},{3,1},{4,6},{5,7},{6,4},{7,5},{8,10},{9,11},{10,... | collective-permute-start | bytes 304136 | tf_op jit(solution)/shard_map/cond/branch_1_fun/ppermute | solution.py:41
  68.4 1.3 %collective-permute-start.23 = (bf16[3,4,4224]{2,1,0:T(4,128)(2,1)S(1)}, bf16[3,4,4224]{2,1,0:T(4,128)(2,1)S(1)}, u32[]{:S(2)}, u32[]{:S(2)}) collective-permute-start(bf16[3,4,4224]{2,1,0:T(4,128)(2,1)S(1)} %token_rows.3), channel_id=1, source_target_pairs={{0,3},{1,2},{2,1},{3,0},{4,7},{5,6},{6,5},{7,4},{8,11},{9,10},{10,... | collective-permute-start | bytes 304136 | tf_op jit(solution)/shard_map/cond/branch_1_fun/ppermute | solution.py:41
  69.7 0.1 broadcast.7
  69.8 0.1 bitcast_dynamic-update-slice_fusion.7
  69.9 0.1 collective-permute-done.21
  70.0 1.0 collective-permute-done.22
  71.1 0.1 bitcast_dynamic-update-slice_fusion.5
  71.1 3.7 %collective-permute-done.23 = bf16[3,4,4224]{2,1,0:T(4,128)(2,1)S(1)} collective-permute-done((bf16[3,4,4224]{2,1,0:T(4,128)(2,1)S(1)}, bf16[3,4,4224]{2,1,0:T(4,128)(2,1)S(1)}, u32[]{:S(2)}, u32[]{:S(2)}) %collective-permute-start.23) | collective-permute-done | bytes 101408 | tf_op jit(solution)/shard_map/cond/branch_1_fun/ppermute | solution.py:41
  74.8 0.1 bitcast_dynamic-update-slice_fusion.4
  74.9 1.5 %collective-permute-start.27 = (bf16[12,4,4224]{2,1,0:T(4,128)(2,1)S(1)}, bf16[12,4,4224]{2,1,0:T(4,128)(2,1)S(1)}, u32[]{:S(2)}, u32[]{:S(2)}) collective-permute-start(bf16[12,4,4224]{2,1,0:T(4,128)(2,1)S(1)} %bitcast.33), channel_id=1, source_target_pairs={{0,16},{16,0},{1,17},{17,1},{2,18},{18,2},{3,19},{19,3},{4,20},{20... | collective-permute-start | bytes 1216520 | tf_op jit(solution)/shard_map/cond/branch_1_fun/ppermute | solution.py:41
  76.4 1.5 %collective-permute-start.25 = (bf16[12,4,4224]{2,1,0:T(4,128)(2,1)S(1)}, bf16[12,4,4224]{2,1,0:T(4,128)(2,1)S(1)}, u32[]{:S(2)}, u32[]{:S(2)}) collective-permute-start(bf16[12,4,4224]{2,1,0:T(4,128)(2,1)S(1)} %bitcast.34), channel_id=1, source_target_pairs={{0,8},{4,12},{8,0},{12,4},{1,9},{5,13},{9,1},{13,5},{2,10},{6,14},... | collective-permute-start | bytes 1216520 | tf_op jit(solution)/shard_map/cond/branch_1_fun/ppermute | solution.py:41
  77.9 6.1 %collective-permute-done.27.refs_2_ = bf16[12,4,4224]{2,1,0:T(4,128)(2,1)S(1)} collective-permute-done((bf16[12,4,4224]{2,1,0:T(4,128)(2,1)S(1)}, bf16[12,4,4224]{2,1,0:T(4,128)(2,1)S(1)}, u32[]{:S(2)}, u32[]{:S(2)}) %collective-permute-start.27) | collective-permute-done | bytes 405536 | tf_op jit(solution)/shard_map/cond/branch_1_fun/ppermute | solution.py:41
  84.1 0.1 slice.14
  84.1 1.6 %collective-permute-start.29 = (bf16[6,4,4224]{2,1,0:T(4,128)(2,1)S(1)}, bf16[6,4,4224]{2,1,0:T(4,128)(2,1)S(1)}, u32[]{:S(2)}, u32[]{:S(2)}) collective-permute-start(bf16[6,4,4224]{2,1,0:T(4,128)(2,1)S(1)} %slice.14), channel_id=1, source_target_pairs={{0,8},{4,12},{8,0},{12,4},{1,9},{5,13},{9,1},{13,5},{2,10},{6,14},... | collective-permute-start | bytes 608264 | tf_op jit(solution)/shard_map/cond/branch_1_fun/ppermute | solution.py:41
  85.7 0.8 collective-permute-done.25.refs_0_
  86.5 0.1 slice.15
  86.6 1.7 %collective-permute-start.30 = (bf16[6,4,4224]{2,1,0:T(4,128)(2,1)S(1)}, bf16[6,4,4224]{2,1,0:T(4,128)(2,1)S(1)}, u32[]{:S(2)}, u32[]{:S(2)}) collective-permute-start(bf16[6,4,4224]{2,1,0:T(4,128)(2,1)S(1)} %slice.15), channel_id=1, source_target_pairs={{0,16},{16,0},{1,17},{17,1},{2,18},{18,2},{3,19},{19,3},{4,20},{20... | collective-permute-start | bytes 608264 | tf_op jit(solution)/shard_map/cond/branch_1_fun/ppermute | solution.py:41
  88.3 0.5 collective-permute-start.28
  88.8 11.3 %vocabulary_scores.9 = (f32[2,8,48]{2,1,0:T(8,128)S(1)}, bf16[2000,4096]{1,0:T(8,128)(2,1)S(1)}) custom-call(s32[5]{0:T(128)S(1)} %get-tuple-element.70.refs_0_.place_ref.first_ref, bf16[12,4,4224]{2,1,0:T(4,128)(2,1)S(1)} %bitcast.36, bf16[12,4,4224]{2,1,0:T(4,128)(2,1)S(1)} %collective-permute-done.24.refs_1_, bf16[2000,4096]{1,0:T(8,128)(2,1)} %get-tuple-element.118.refs_2_), custom_call_target="tpu_custom_call" | custom-call | flops 2359296000 | bytes 786432 | tf_op jit(solution)/shard_map/cond/branch_1_fun/vocabulary_scores/pallas_call | solution.py:547
  100.1 0.1 constant_dynamic-update-slice_fusion.3
  100.2 0.1 constant_dynamic-update-slice_fusion.2.refs_0_
  100.3 0.1 collective-permute-start.31
  100.4 6.5 %vocabulary_scores.10.refs_1_ = f32[4,8,48]{2,1,0:T(8,128)S(1)} custom-call(s32[5]{0:T(128)S(1)} %get-tuple-element.70.refs_0_.place_ref.first_ref, bf16[12,4,4224]{2,1,0:T(4,128)(2,1)S(1)} %collective-permute-done.25.refs_0_, bf16[12,4,4224]{2,1,0:T(4,128)(2,1)S(1)} %collective-permute-done.26.refs_1_, ...), custom_call_target="tpu_custom_call" | custom-call | flops 4718592000 | bytes 1572864 | tf_op jit(solution)/shard_map/cond/branch_1_fun/vocabulary_scores/pallas_call | solution.py:547
  106.9 5.9 %vocabulary_scores.11.refs_2_ = f32[2,8,48]{2,1,0:T(8,128)S(1)} custom-call(s32[5]{0:T(128)S(1)} %get-tuple-element.70.refs_0_.place_ref.first_ref, bf16[12,4,4224]{2,1,0:T(4,128)(2,1)S(1)} %constant_dynamic-update-slice_fusion.2.refs_0_, bf16[12,4,4224]{2,1,0:T(4,128)(2,1)S(1)} %collective-permute-done.31.refs_1_, ...), custom_call_target="tpu_custom_call" | custom-call | flops 2359296000 | bytes 786432 | tf_op jit(solution)/shard_map/cond/branch_1_fun/vocabulary_scores/pallas_call | solution.py:547
  112.9 0.6 statistics_by_group.3
  113.5 10.7 %all_to_all.19.every_ref = f32[32,8,96]{2,1,0:T(8,128)S(1)} all-to-all(f32[32,8,96]{2,1,0:T(8,128)S(1)} %statistics_by_group.3), channel_id=1, replica_groups=mesh['section'=2,'tm'=4,'mp'=4] {'section','tm','mp'}, dimensions={0} | all-to-all | bytes 196608 | tf_op jit(solution)/shard_map/cond/branch_1_fun/all_to_all | solution.py:31
  124.2 0.7 hypothesis_scores.3
  125.0 0.6 copy-done.8
  (26 shorter events, 0.1 us)
Async XLA Ops:
  0.0 13.3 %copy-start.6 = (s32[2,8,16]{2,1,0:T(8,128)S(1)}, s32[2,8,16]{2,1,0:T(8,128)}, u32[]{:S(2)}) copy-start(s32[2,8,16]{2,1,0:T(8,128)} %param.21) | copy-start | bytes 3076
  0.0 13.4 %copy-start.5 = (s32[2,8]{1,0:T(2,128)S(1)}, s32[2,8]{1,0:T(2,128)}, u32[]{:S(2)}) copy-start(s32[2,8]{1,0:T(2,128)} %length_ref.1) | copy-start | bytes 196
  0.0 13.4 %copy-start.4 = (s32[8]{0:T(128)S(1)}, s32[8]{0:T(128)}, u32[]{:S(2)}) copy-start(s32[8]{0:T(128)} %slot_ref.1) | copy-start | bytes 100
  0.1 1.0 copy-start.1
  6.7 16.9 %copy-start = (bf16[1280,1024]{1,0:T(8,128)(2,1)S(1)}, bf16[1280,1024]{1,0:T(8,128)(2,1)}, u32[]{:S(2)}) copy-start(bf16[1280,1024]{1,0:T(8,128)(2,1)} %refs_2_.1) | copy-start | bytes 7864324
  6.7 16.9 %all-to-all-start.2 = ((bf16[4,32,1280]{2,1,0:T(8,128)(2,1)}), bf16[4,32,1280]{2,1,0:T(8,128)(2,1)S(1)}, u32[]{:S(2)}, u32[]{:S(2)}) async-start(bf16[4,32,1280]{2,1,0:T(8,128)(2,1)} %get-tuple-element.102), calls=%async_computation.2 | async-start | bytes 655360 | tf_op jit(solution)/shard_map/all_to_all | solution.py:31
  13.4 25.0 %copy-start.7 = (s32[4]{0:T(128)S(1)}, s32[4]{0:T(128)}, u32[]{:S(2)}) copy-start(s32[4]{0:T(128)} %param.14) | copy-start | bytes 52
  19.3 1.6 %collective-permute-start.35 = (bf16[272,512]{1,0:T(8,128)(2,1)S(1)}, bf16[272,512]{1,0:T(8,128)(2,1)S(1)}, u32[]{:S(2)}, u32[]{:S(2)}) collective-permute-start(bf16[272,512]{1,0:T(8,128)(2,1)S(1)} %get-tuple-element.101), channel_id=1, source_target_pairs={{0,4},{4,0},{8,12},{12,8},{1,5},{5,1},{9,13},{13,9},{2,6},{6,2},{1... | collective-permute-start | bytes 835592 | tf_op jit(solution)/shard_map/ppermute | solution.py:41
  19.4 18.5 %collective-permute-start.34 = (bf16[272,512]{1,0:T(8,128)(2,1)S(1)}, bf16[272,512]{1,0:T(8,128)(2,1)}, u32[]{:S(2)}, u32[]{:S(2)}) collective-permute-start(bf16[272,512]{1,0:T(8,128)(2,1)S(1)} %get-tuple-element.99), channel_id=1, source_target_pairs={{0,4},{4,0},{8,12},{12,8},{1,5},{5,1},{9,13},{13,9},{2,6},{6,2},{1... | collective-permute-start | bytes 835592 | tf_op jit(solution)/shard_map/ppermute | solution.py:41
  21.8 16.1 %collective-permute-start.36 = (bf16[272,512]{1,0:T(8,128)(2,1)}, bf16[272,512]{1,0:T(8,128)(2,1)}, u32[]{:S(2)}, u32[]{:S(2)}) collective-permute-start(bf16[272,512]{1,0:T(8,128)(2,1)} %add.45), channel_id=1, source_target_pairs={{0,8},{4,12},{8,0},{12,4},{1,9},{5,13},{9,1},{13,5},{2,10},{6,14},... | collective-permute-start | bytes 835592 | tf_op jit(solution)/shard_map/ppermute | solution.py:41
  25.2 13.2 %all-to-all-start.3 = ((bf16[32,8,256]{2,1,0:T(8,128)(2,1)}), bf16[32,8,256]{2,1,0:T(8,128)(2,1)S(1)}, u32[]{:S(2)}, u32[]{:S(2)}) async-start(bf16[32,8,256]{2,1,0:T(8,128)(2,1)} %bitcast.20), calls=%async_computation.3 | async-start | bytes 262144 | tf_op jit(solution)/shard_map/all_to_all | solution.py:31
  30.8 1.4 %collective-permute-start.32 = (s32[1]{0:T(128)}, s32[1]{0:T(128)}, u32[]{:S(2)}, u32[]{:S(2)}) collective-permute-start(s32[1]{0:T(128)} %bitcast.12), channel_id=1, source_target_pairs={{0,4},{4,0},{8,12},{12,8},{1,5},{5,1},{9,13},{13,9},{2,6},{6,2},{1... | collective-permute-start | bytes 20 | tf_op jit(solution)/shard_map/ppermute | solution.py:41
  33.5 3.8 %collective-permute-start.33 = (s32[1]{0:T(128)}, s32[1]{0:T(128)}, u32[]{:S(2)}, u32[]{:S(2)}) collective-permute-start(s32[1]{0:T(128)} %max.6), channel_id=1, source_target_pairs={{0,8},{4,12},{8,0},{12,4},{1,9},{5,13},{9,1},{13,5},{2,10},{6,14},... | collective-permute-start | bytes 20 | tf_op jit(solution)/shard_map/ppermute | solution.py:41
  38.4 25.6 %copy-start.3 = (bf16[272,512]{1,0:T(8,128)(2,1)S(1)}, bf16[272,512]{1,0:T(8,128)(2,1)}, u32[]{:S(2)}) copy-start(bf16[272,512]{1,0:T(8,128)(2,1)} %get-tuple-element.73.refs_3_.refs_0_) | copy-start | bytes 835588 | tf_op jit(solution)/shard_map/cond
  42.2 7.4 %collective-permute-start.16 = (bf16[32,4096]{1,0:T(8,128)(2,1)S(1)}, bf16[32,4096]{1,0:T(8,128)(2,1)S(1)}, u32[]{:S(2)}, u32[]{:S(2)}) collective-permute-start(bf16[32,4096]{1,0:T(8,128)(2,1)S(1)} %get-tuple-element.80), channel_id=1, source_target_pairs={{0,16},{16,0},{1,17},{17,1},{2,18},{18,2},{3,19},{19,3},{4,20},{20... | collective-permute-start | bytes 786440 | tf_op jit(solution)/shard_map/cond/branch_1_fun/ppermute | solution.py:41
  43.8 5.0 %collective-permute-start.17 = (bf16[16,4096]{1,0:T(8,128)(2,1)S(1)}, bf16[16,4096]{1,0:T(8,128)(2,1)S(1)}, u32[]{:S(2)}, u32[]{:S(2)}) collective-permute-start(bf16[16,4096]{1,0:T(8,128)(2,1)S(1)} %get-tuple-element.82), channel_id=1, source_target_pairs={{0,1},{1,0},{2,3},{3,2},{4,5},{5,4},{6,7},{7,6},{8,9},{9,8},{10,11... | collective-permute-start | bytes 393224 | tf_op jit(solution)/shard_map/cond/branch_1_fun/ppermute | solution.py:41
  50.3 5.7 %collective-permute-start.18 = (bf16[16,4096]{1,0:T(8,128)(2,1)S(1)}, bf16[16,4096]{1,0:T(8,128)(2,1)S(1)}, u32[]{:S(2)}, u32[]{:S(2)}) collective-permute-start(bf16[16,4096]{1,0:T(8,128)(2,1)S(1)} %get-tuple-element.84), channel_id=1, source_target_pairs={{0,1},{1,0},{2,3},{3,2},{4,5},{5,4},{6,7},{7,6},{8,9},{9,8},{10,11... | collective-permute-start | bytes 393224 | tf_op jit(solution)/shard_map/cond/branch_1_fun/ppermute | solution.py:41
  51.7 4.3 %collective-permute-start.19 = (bf16[8,4096]{1,0:T(8,128)(2,1)S(1)}, bf16[8,4096]{1,0:T(8,128)(2,1)S(1)}, u32[]{:S(2)}, u32[]{:S(2)}) collective-permute-start(bf16[8,4096]{1,0:T(8,128)(2,1)S(1)} %get-tuple-element.86), channel_id=1, source_target_pairs={{0,16},{16,0},{1,17},{17,1},{2,18},{18,2},{3,19},{19,3},{4,20},{20... | collective-permute-start | bytes 196616 | tf_op jit(solution)/shard_map/cond/branch_1_fun/ppermute | solution.py:41
  56.6 7.4 %collective-permute-start.20 = (bf16[12,4096]{1,0:T(8,128)(2,1)S(1)}, bf16[12,4096]{1,0:T(8,128)(2,1)S(1)}, u32[]{:S(2)}, u32[]{:S(2)}) collective-permute-start(bf16[12,4096]{1,0:T(8,128)(2,1)S(1)} %get-tuple-element.88), channel_id=1, source_target_pairs={{0,2},{1,3},{2,0},{3,1},{4,6},{5,7},{6,4},{7,5},{8,10},{9,11},{10,... | collective-permute-start | bytes 294920 | tf_op jit(solution)/shard_map/cond/branch_1_fun/ppermute | solution.py:41
  65.3 4.7 %collective-permute-start.21 = (bf16[3,4,4224]{2,1,0:T(4,128)(2,1)S(1)}, bf16[3,4,4224]{2,1,0:T(4,128)(2,1)S(1)}, u32[]{:S(2)}, u32[]{:S(2)}) collective-permute-start(bf16[3,4,4224]{2,1,0:T(4,128)(2,1)S(1)} %token_rows.3), channel_id=1, source_target_pairs={{0,1},{1,0},{2,3},{3,2},{4,5},{5,4},{6,7},{7,6},{8,9},{9,8},{10,11... | collective-permute-start | bytes 304136 | tf_op jit(solution)/shard_map/cond/branch_1_fun/ppermute | solution.py:41
  65.3 5.7 %collective-permute-start.22 = (bf16[3,4,4224]{2,1,0:T(4,128)(2,1)S(1)}, bf16[3,4,4224]{2,1,0:T(4,128)(2,1)S(1)}, u32[]{:S(2)}, u32[]{:S(2)}) collective-permute-start(bf16[3,4,4224]{2,1,0:T(4,128)(2,1)S(1)} %token_rows.3), channel_id=1, source_target_pairs={{0,2},{1,3},{2,0},{3,1},{4,6},{5,7},{6,4},{7,5},{8,10},{9,11},{10,... | collective-permute-start | bytes 304136 | tf_op jit(solution)/shard_map/cond/branch_1_fun/ppermute | solution.py:41
  68.4 6.4 %collective-permute-start.23 = (bf16[3,4,4224]{2,1,0:T(4,128)(2,1)S(1)}, bf16[3,4,4224]{2,1,0:T(4,128)(2,1)S(1)}, u32[]{:S(2)}, u32[]{:S(2)}) collective-permute-start(bf16[3,4,4224]{2,1,0:T(4,128)(2,1)S(1)} %token_rows.3), channel_id=1, source_target_pairs={{0,3},{1,2},{2,1},{3,0},{4,7},{5,6},{6,5},{7,4},{8,11},{9,10},{10,... | collective-permute-start | bytes 304136 | tf_op jit(solution)/shard_map/cond/branch_1_fun/ppermute | solution.py:41
  74.9 9.2 %collective-permute-start.27 = (bf16[12,4,4224]{2,1,0:T(4,128)(2,1)S(1)}, bf16[12,4,4224]{2,1,0:T(4,128)(2,1)S(1)}, u32[]{:S(2)}, u32[]{:S(2)}) collective-permute-start(bf16[12,4,4224]{2,1,0:T(4,128)(2,1)S(1)} %bitcast.33), channel_id=1, source_target_pairs={{0,16},{16,0},{1,17},{17,1},{2,18},{18,2},{3,19},{19,3},{4,20},{20... | collective-permute-start | bytes 1216520 | tf_op jit(solution)/shard_map/cond/branch_1_fun/ppermute | solution.py:41
  76.4 10.1 %collective-permute-start.25 = (bf16[12,4,4224]{2,1,0:T(4,128)(2,1)S(1)}, bf16[12,4,4224]{2,1,0:T(4,128)(2,1)S(1)}, u32[]{:S(2)}, u32[]{:S(2)}) collective-permute-start(bf16[12,4,4224]{2,1,0:T(4,128)(2,1)S(1)} %bitcast.34), channel_id=1, source_target_pairs={{0,8},{4,12},{8,0},{12,4},{1,9},{5,13},{9,1},{13,5},{2,10},{6,14},... | collective-permute-start | bytes 1216520 | tf_op jit(solution)/shard_map/cond/branch_1_fun/ppermute | solution.py:41
  77.9 10.9 %collective-permute-start.24 = (bf16[12,4,4224]{2,1,0:T(4,128)(2,1)S(1)}, bf16[12,4,4224]{2,1,0:T(4,128)(2,1)S(1)}, u32[]{:S(2)}, u32[]{:S(2)}) collective-permute-start(bf16[12,4,4224]{2,1,0:T(4,128)(2,1)S(1)} %bitcast.35), channel_id=1, source_target_pairs={{0,4},{4,0},{8,12},{12,8},{1,5},{5,1},{9,13},{13,9},{2,6},{6,2},{1... | collective-permute-start | bytes 1216520 | tf_op jit(solution)/shard_map/cond/branch_1_fun/ppermute | solution.py:41
  84.1 15.9 %collective-permute-start.29 = (bf16[6,4,4224]{2,1,0:T(4,128)(2,1)S(1)}, bf16[6,4,4224]{2,1,0:T(4,128)(2,1)S(1)}, u32[]{:S(2)}, u32[]{:S(2)}) collective-permute-start(bf16[6,4,4224]{2,1,0:T(4,128)(2,1)S(1)} %slice.14), channel_id=1, source_target_pairs={{0,8},{4,12},{8,0},{12,4},{1,9},{5,13},{9,1},{13,5},{2,10},{6,14},... | collective-permute-start | bytes 608264 | tf_op jit(solution)/shard_map/cond/branch_1_fun/ppermute | solution.py:41
  86.6 13.6 %collective-permute-start.30 = (bf16[6,4,4224]{2,1,0:T(4,128)(2,1)S(1)}, bf16[6,4,4224]{2,1,0:T(4,128)(2,1)S(1)}, u32[]{:S(2)}, u32[]{:S(2)}) collective-permute-start(bf16[6,4,4224]{2,1,0:T(4,128)(2,1)S(1)} %slice.15), channel_id=1, source_target_pairs={{0,16},{16,0},{1,17},{17,1},{2,18},{18,2},{3,19},{19,3},{4,20},{20... | collective-permute-start | bytes 608264 | tf_op jit(solution)/shard_map/cond/branch_1_fun/ppermute | solution.py:41
  88.3 12.1 %collective-permute-start.26 = (bf16[12,4,4224]{2,1,0:T(4,128)(2,1)S(1)}, bf16[12,4,4224]{2,1,0:T(4,128)(2,1)S(1)}, u32[]{:S(2)}, u32[]{:S(2)}) collective-permute-start(bf16[12,4,4224]{2,1,0:T(4,128)(2,1)S(1)} %collective-permute-done.25.refs_0_), channel_id=1, source_target_pairs={{0,4},{4,0},{8,12},{12,8},{1,5},{5,1},{9,13},{13,9},{2,6},{6,2},{1... | collective-permute-start | bytes 1216520 | tf_op jit(solution)/shard_map/cond/branch_1_fun/ppermute | solution.py:41
  88.3 12.1 %collective-permute-start.28 = (bf16[12,4,4224]{2,1,0:T(4,128)(2,1)S(1)}, bf16[12,4,4224]{2,1,0:T(4,128)(2,1)S(1)}, u32[]{:S(2)}, u32[]{:S(2)}) collective-permute-start(bf16[12,4,4224]{2,1,0:T(4,128)(2,1)S(1)} %collective-permute-done.27.refs_2_), channel_id=1, source_target_pairs={{0,4},{4,0},{8,12},{12,8},{1,5},{5,1},{9,13},{13,9},{2,6},{6,2},{1... | collective-permute-start | bytes 1216520 | tf_op jit(solution)/shard_map/cond/branch_1_fun/ppermute | solution.py:41
  100.3 6.7 %collective-permute-start.31 = (bf16[12,4,4224]{2,1,0:T(4,128)(2,1)S(1)}, bf16[12,4,4224]{2,1,0:T(4,128)(2,1)S(1)}, u32[]{:S(2)}, u32[]{:S(2)}) collective-permute-start(bf16[12,4,4224]{2,1,0:T(4,128)(2,1)S(1)} %constant_dynamic-update-slice_fusion.2.refs_0_), channel_id=1, source_target_pairs={{0,4},{4,0},{8,12},{12,8},{1,5},{5,1},{9,13},{13,9},{2,6},{6,2},{1... | collective-permute-start | bytes 1216520 | tf_op jit(solution)/shard_map/cond/branch_1_fun/ppermute | solution.py:41
  125.0 0.6 copy-start.8

commit v14 on v13

--- a/solution.py
+++ b/solution.py
@@ -70,29 +70,36 @@
 
 
 def ffn_kernel(tile, place_ref, x_ref, up_ref, down_ref, *refs):
-    out_ref, own_ref, rows, total, up, down, up_sem, down_sem = refs
+    out_ref, own_ref, inputs, rows, up, down, x_sem, up_sem, down_sem = refs
     count, share, width = out_ref.shape
     tiles = up_ref.shape[1] // tile
+    x_copy = start_copies(lambda i: x_ref, lambda i: inputs, x_sem, 1)[0]
     up_copies = start_copies(
         lambda i: up_ref.at[:, pl.ds(i * tile, tile)], lambda i: up.at[i], up_sem, tiles
     )
-    down_copies = start_copies(
-        lambda i: down_ref.at[pl.ds(i * tile, tile), :], lambda i: down.at[i], down_sem, tiles
-    )
-    rows[...] = x_ref[...].astype(jnp.float32).reshape(rows.shape)
+    x_copy.wait()
+    rows[...] = inputs[...].astype(jnp.float32).reshape(rows.shape)
     start = pl.multiple_of(place_ref[2] * share, share)
     own_ref[...] = rows[pl.ds(start, share), :].astype(jnp.bfloat16)
     normed = layer_norm(rows[...]).astype(jnp.bfloat16)
+    inner = []
     for number in range(tiles):
         up_copies[number].wait()
+        if number == 0:
+            down_copies = start_copies(
+                lambda i: down_ref.at[pl.ds(i * tile, tile), :],
+                lambda i: down.at[i],
+                down_sem,
+                tiles,
+            )
         hidden = dot(normed, up[number])
-        inner = 0.5 * hidden * (1.0 + lax.erf(hidden * math.sqrt(0.5)))
+        hidden = 0.5 * hidden * (1.0 + lax.erf(hidden * math.sqrt(0.5)))
+        inner.append(hidden.astype(jnp.bfloat16))
+    total = None
+    for number in range(tiles):
         down_copies[number].wait()
-        product = dot(inner.astype(jnp.bfloat16), down[number])
-        if number == 0:
-            total[...] = product
-        else:
-            total[...] += product
+        product = dot(inner[number], down[number])
+        total = product if total is None else total + product
     for part in range(count):
         out_ref[part] = total[part * share : (part + 1) * share, :].astype(jnp.bfloat16)
 
@@ -113,17 +120,18 @@
     tiles = up.shape[1] // tile
     return pl.pallas_call(
         functools.partial(ffn_kernel, tile),
-        in_specs=[SCALARS, INSIDE, ANYWHERE, ANYWHERE],
+        in_specs=[SCALARS] + [ANYWHERE] * 3,
         out_specs=[INSIDE] * 2,
         out_shape=[
             jax.ShapeDtypeStruct((count, share, width), jnp.bfloat16),
             jax.ShapeDtypeStruct((share, width), jnp.bfloat16),
         ],
         scratch_shapes=[
-            pltpu.VMEM((rows, width), jnp.float32),
+            pltpu.VMEM(enc_in.shape, jnp.bfloat16),
             pltpu.VMEM((rows, width), jnp.float32),
             pltpu.VMEM((tiles, width, tile), jnp.bfloat16),
             pltpu.VMEM((tiles, tile, width), jnp.bfloat16),
+            pltpu.SemaphoreType.DMA((1,)),
             pltpu.SemaphoreType.DMA((tiles,)),
             pltpu.SemaphoreType.DMA((tiles,)),
         ],
@@ -134,7 +142,7 @@
         ),
         compiler_params=pltpu.CompilerParams(vmem_limit_bytes=24 << 20),
         name="encoder_ffn",
-    )(place, enc_in, in_hbm(up), in_hbm(down))
+    )(place, in_hbm(enc_in), in_hbm(up), in_hbm(down))
 
 
 def query_kernel(
@@ -485,19 +493,30 @@
 
 def vocabulary_kernel(tile, count, first_ref, *refs):
     sets, head_ref, out_ref = refs[:count], refs[count], refs[count + 1]
-    loaded_ref, semaphores = (refs[count + 2], refs[-1]) if len(refs) > count + 4 else (None, None)
-    rows_ref, stat = refs[-3:-1] if loaded_ref is not None else refs[-2:]
+    loads = len(refs) > count + 4
+    if loads:
+        loaded_ref, zero_ref, rows_ref, stat, semaphores = refs[count + 2 :]
+        zero_ref[0] = 0
+    else:
+        rows_ref, stat = refs[count + 2 :]
     vocab_rows, width = head_ref.shape
     share = sets[0].shape[0] * FOLD
     tokens = share * len(sets)
     tiles = vocab_rows // tile
-    if loaded_ref is not None:
-        copies = start_copies(
-            lambda i: head_ref.at[pl.ds(i * tile, tile), :],
-            lambda i: loaded_ref.at[pl.ds(i * tile, tile), :],
-            semaphores,
-            tiles,
+    pieces = 5
+
+    def load(number):
+        size = tile // pieces
+        place = lambda i: pl.ds(number * tile + i * size, size)
+        return start_copies(
+            lambda i: head_ref.at[place(i), :],
+            lambda i: loaded_ref.at[place(i), :],
+            semaphores.at[number],
+            pieces,
         )
+
+    if loads:
+        copies = [load(0), load(1)]
     cell = lax.broadcasted_iota(jnp.int32, (8, LANES), 1)
     take = jnp.where(cell == 0, 256.0, jnp.where(cell == 1, 1.0, 0.0)).astype(jnp.bfloat16)
     for number, rows in enumerate(sets):
@@ -519,9 +538,12 @@
         stat[16:17, :] += jnp.sum(jnp.where(vocab == target, logits, 0.0), axis=0, keepdims=True)
         stat[0:1, :] = upper
 
-    if loaded_ref is not None:
+    if loads:
         for number in range(tiles):
-            copies[number].wait()
+            for copy in copies[number]:
+                copy.wait()
+            if number + 2 < tiles:
+                copies.append(load(number + 2))
             one_tile(number * tile, loaded_ref[number * tile : (number + 1) * tile, :])
     else:
 
@@ -547,13 +569,19 @@
     return pl.pallas_call(
         functools.partial(vocabulary_kernel, tile, count),
         in_specs=[SCALARS] + [INSIDE] * count + [ANYWHERE if load else INSIDE],
-        out_specs=[INSIDE] * 2 if load else INSIDE,
-        out_shape=[stats, pltpu.VMEM(head.shape, head.dtype)] if load else stats,
+        out_specs=[INSIDE, INSIDE, SCALARS] if load else INSIDE,
+        out_shape=[
+            stats,
+            pltpu.VMEM(head.shape, head.dtype),
+            jax.ShapeDtypeStruct((1,), jnp.int32),
+        ]
+        if load
+        else stats,
         scratch_shapes=[
             pltpu.VMEM((tokens, width + LANES), jnp.bfloat16),
             pltpu.VMEM((24, tokens), jnp.float32),
         ]
-        + ([pltpu.SemaphoreType.DMA((5,))] if load else []),
+        + ([pltpu.SemaphoreType.DMA((5, 5))] if load else []),
         cost_estimate=pl.CostEstimate(
             flops=3 * tokens * head.shape[0] * width,
             bytes_accessed=2 * tokens * width,
@@ -693,9 +721,12 @@
     half = own.shape[0] // 2
     by_x = swap(own, "section", 1)
     by_y = swap(own, "tm", 2)
-    stats, head = vocabulary_stats(place, [own, swap(own, "tm", 1)], head, load=True)
+    stats, head, zero = vocabulary_stats(place, [own, swap(own, "tm", 1)], head, load=True)
     stats = [stats]
-    across = [swap(by_x[:half], "tm", 2), swap(by_y[half:], "section", 1)]
+    across = [
+        swap(lax.dynamic_slice_in_dim(by_x, zero[0], half, 0), "tm", 2),
+        swap(lax.dynamic_slice_in_dim(by_y, zero[0] + half, half, 0), "section", 1),
+    ]
     stats.append(
         vocabulary_stats(place, [by_y, swap(by_y, "tm", 1), by_x, swap(by_x, "tm", 1)], head)
     )
@@ -769,9 +800,10 @@
 
     here_slots = lax.dynamic_slice_in_dim(slot_utt, group_pos * slot_count, slot_count, 0)
     filled = jnp.where(here_slots >= 0, jnp.sum(hyp_len, axis=1), 0)
-    most = jnp.max(filled).reshape(1)
-    for distance in (1, 2):
-        most = jnp.maximum(most, swap(most, "tm", distance))
+    count = jnp.max(filled).reshape(1)
+    most = count
+    for distance in range(1, group_count):
+        most = jnp.maximum(most, swap(count, "tm", distance))
     operands = (place, slot_utt, frame_len, hyp_len, payloads, keys_values, o_proj, head)
     few = share_rows * 3 // 4
     return lax.cond(

time: 126 us -> 139 us (1.10)
  local copies, waits for them, and re-layouts: 2.34 us -> 12.7 us
  starting transfers between devices: 36.4 us -> 29.8 us
  loops' own time: 0.13 us -> 3.38 us
  waiting for transfers between devices: 27.8 us -> 30.4 us
  blocking collectives: 10.7 us -> 12.5 us
    cond x3 -> x7, local copies, waits for them, and re-layouts: 0.08 us -> 11.4 us
    ppermute x21 -> x22, starting transfers between devices: 25 us -> 18.4 us  [swap(): return lax.ppermute(values, axis, pairs)]
    another operation x1, loops' own time: 0.13 us -> 3.38 us  [near_device(): lax.cond(most[0] <= few * head_devices, functools.partial(rest, (few - fe...]
    all_to_all x1, blocking collectives: 10.7 us -> 12.5 us  [exchange(): return lax.all_to_all(blocks, axis, split_axis=0, concat_axis=0, tiled=True)]
    all_to_all x2, waiting for transfers between devices: 0.81 us -> 2.28 us  [exchange(): return lax.all_to_all(blocks, axis, split_axis=0, concat_axis=0, tiled=True)]
    ppermute x21 -> x22, waiting for transfers between devices: 27 us -> 28.1 us  [swap(): return lax.ppermute(values, axis, pairs)]
  transfers between devices with their start and end apart: 23 -> 24, of which waited for: 14 -> 14; matrix products, arithmetic and copies ran while one was open for 2% -> 2% of each run, Pallas kernels for 20% -> 18%
where the time goes in v14:
time: 139 us; the launch traced here: 138 us
  Pallas kernels  45.4 us (33%)
  waiting for transfers between devices  30.4 us (22%)
  starting transfers between devices  29.8 us (21%)
  local copies, waits for them, and re-layouts  12.7 us (9%)
  blocking collectives  12.5 us (9%)
  loops' own time  3.38 us (2%)
  between operations  2.69 us (2%)
  other arithmetic  1.61 us (1%)
    ppermute x22, waiting for transfers between devices, swap(): return lax.ppermute(values, axis, pairs)  28.1 us
    pallas_call x3, Pallas kernels, vocabulary_stats(): pl.pallas_call(functools.partial(vocabulary_kernel, tile, count), in_spec...  23.9 us
    ppermute x22, starting transfers between devices, swap(): return lax.ppermute(values, axis, pairs)  18.4 us
    all_to_all x1, blocking collectives, exchange(): return lax.all_to_all(blocks, axis, split_axis=0, concat_axis=0, tiled=True)  12.5 us
    all_to_all x2, starting transfers between devices, exchange(): return lax.all_to_all(blocks, axis, split_axis=0, concat_axis=0, tiled=True)  11.4 us
    cond x7, local copies, waits for them, and re-layouts  11.4 us
    pallas_call x1, Pallas kernels, ffn(): pl.pallas_call(functools.partial(ffn_kernel, tile), in_specs=[SCALARS] +...  6.33 us
    pallas_call x1, Pallas kernels, queries_of(): pl.pallas_call(functools.partial(query_kernel, count, depth), in_specs=[S...  5.92 us
  transfers between devices with their start and end apart: 24, of which 14 were waited for; matrix products, arithmetic and copies ran while one was open for 2% of the time, Pallas kernels for 18%

profile of v14, /device:TPU:0, one launch (start us, length us, event | category | flops | bytes accessed | tf_op | source)
XLA Modules:
  0.0 138.4 jit_solution(6942337581434750269)
XLA Ops:
  0.0 0.1 stack.23.place_ref.after_ref
  0.1 6.3 %encoder_ffn.1 = (bf16[4,32,1280]{2,1,0:T(8,128)(2,1)}, bf16[32,1280]{1,0:T(8,128)(2,1)S(1)}) custom-call(s32[5]{0:T(128)S(1)} %stack.23.place_ref.after_ref, bf16[32,4,1280]{2,1,0:T(4,128)(2,1)} %x_ref.1, bf16[1280,1280]{1,0:T(8,128)(2,1)} %up_ref.1, bf16[1280,1280]{1,0:T(8,128)(2,1)} %down_ref.1), custom_call_target="tpu_custom_call" | custom-call | flops 838860800 | bytes 6553600 | tf_op jit(solution)/shard_map/encoder_ffn/pallas_call | solution.py:121
  6.4 6.6 %all-to-all-start.2 = ((bf16[4,32,1280]{2,1,0:T(8,128)(2,1)}), bf16[4,32,1280]{2,1,0:T(8,128)(2,1)S(1)}, u32[]{:S(2)}, u32[]{:S(2)}) async-start(bf16[4,32,1280]{2,1,0:T(8,128)(2,1)} %get-tuple-element.104), calls=%async_computation.2 | async-start | bytes 655360 | tf_op jit(solution)/shard_map/all_to_all | solution.py:31
  13.1 0.1 reshape.27.tok_ref
  13.1 5.9 %hypothesis_queries.1 = (bf16[272,512]{1,0:T(8,128)(2,1)}, bf16[272,512]{1,0:T(8,128)(2,1)S(1)}, bf16[272,512]{1,0:T(8,128)(2,1)S(1)}, bf16[272,512]{1,0:T(8,128)(2,1)S(1)}) custom-call(s32[5]{0:T(128)S(1)} %stack.23.place_ref.after_ref, s32[8]{0:T(128)S(1)} %copy-done.7, s32[2,8]{1,0:T(2,128)S(1)} %copy-done.8, s32[5]{0:T(128)S(1)} %stack.23.place_ref.after_ref, ...), custom_call_target="tpu_custom_call" | custom-call | flops 1073741824 | bytes 6291456 | tf_op jit(solution)/shard_map/hypothesis_queries/pallas_call | solution.py:228
  19.1 0.1 collective-permute-start.36
  19.2 0.5 collective-permute-start.35
  19.7 1.0 collective-permute-done.36
  20.7 0.8 add.67
  21.5 1.5 %collective-permute-start.37 = (bf16[272,512]{1,0:T(8,128)(2,1)}, bf16[272,512]{1,0:T(8,128)(2,1)}, u32[]{:S(2)}, u32[]{:S(2)}) collective-permute-start(bf16[272,512]{1,0:T(8,128)(2,1)} %add.67), channel_id=1, source_target_pairs={{0,8},{4,12},{8,0},{12,4},{1,9},{5,13},{9,1},{13,5},{2,10},{6,14},... | collective-permute-start | bytes 835592 | tf_op jit(solution)/shard_map/ppermute | solution.py:41
  23.0 0.3 all-to-all-done.2.refs_0_
  23.4 1.5 %frame_keys_values.1 = bf16[256,256]{1,0:T(8,128)(2,1)} custom-call(bf16[4,32,1280]{2,1,0:T(8,128)(2,1)S(1)} %all-to-all-done.2.refs_0_, bf16[32,1280]{1,0:T(8,128)(2,1)S(1)} %get-tuple-element.105.refs_1_, bf16[1280,1024]{1,0:T(8,128)(2,1)S(1)} %copy-done.4, bf16[272,512]{1,0:T(8,128)(2,1)} %get-tuple-element.100.refs_3_), custom_call_target="tpu_custom_call" | custom-call | flops 83886080 | bytes 2621440 | tf_op jit(solution)/shard_map/frame_keys_values/pallas_call | solution.py:287
  24.9 4.8 %all-to-all-start.3 = ((bf16[32,8,256]{2,1,0:T(8,128)(2,1)}), bf16[32,8,256]{2,1,0:T(8,128)(2,1)S(1)}, u32[]{:S(2)}, u32[]{:S(2)}) async-start(bf16[32,8,256]{2,1,0:T(8,128)(2,1)} %bitcast.22), calls=%async_computation.3 | async-start | bytes 262144 | tf_op jit(solution)/shard_map/all_to_all | solution.py:31
  29.7 0.1 reduce_sum.9
  29.8 0.7 fusion
  30.5 0.3 collective-permute-start.32
  30.8 1.7 %collective-permute-start.33 = (s32[1]{0:T(128)}, s32[1]{0:T(128)}, u32[]{:S(2)}, u32[]{:S(2)}) collective-permute-start(s32[1]{0:T(128)} %bitcast.14), channel_id=1, source_target_pairs={{0,8},{4,12},{8,0},{12,4},{1,9},{5,13},{9,1},{13,5},{2,10},{6,14},... | collective-permute-start | bytes 20 | tf_op jit(solution)/shard_map/ppermute | solution.py:41
  33.8 0.8 collective-permute-done.33
  35.2 0.3 collective-permute-done.34
  36.2 1.9 %all-to-all-done.3 = bf16[32,8,256]{2,1,0:T(8,128)(2,1)S(1)} async-done(((bf16[32,8,256]{2,1,0:T(8,128)(2,1)}), bf16[32,8,256]{2,1,0:T(8,128)(2,1)S(1)}, u32[]{:S(2)}, u32[]{:S(2)}) %all-to-all-start.3) | async-done | bytes 131104 | tf_op jit(solution)/shard_map/all_to_all | solution.py:31
  38.1 99.7 %conditional.1 = (f32[2,8]{1,0:T(2,128)S(1)}) conditional(s32[]{:T(128)} %bitcast.15, (s32[5]{0:T(128)S(1)}, s32[8]{0:T(128)S(1)}, s32[4]{0:T(128)S(1)}, bf16[272,512]{1,0:T(8,128)(2,1)}, bf16[272,512]{1,0:T(8,128)(2,1)}, /*index=5*/bf16[272,512]{1,0:T(8,128)(2,1)}, bf16[32,8,256]{2,1,0:T(8,128)(2,1)S(1)}, bf16[512,4096]{1,0:T(8,128)(2,1)}, ...), branch_computations={%region_2.3_spmd, %region_3.4_spmd} | conditional | flops 13186891776 | bytes 166102016 | solution.py:809
  38.1 3.8 %attention_projection.3 = (bf16[32,4096]{1,0:T(8,128)(2,1)S(1)}, bf16[32,4096]{1,0:T(8,128)(2,1)S(1)}, bf16[16,4096]{1,0:T(8,128)(2,1)S(1)}, bf16[16,4096]{1,0:T(8,128)(2,1)S(1)}) custom-call(s32[5]{0:T(128)S(1)} %get-tuple-element.71.refs_0_.place_ref.first_ref, s32[8]{0:T(128)S(1)} %get-tuple-element.72.refs_1_.slot_ref, s32[4]{0:T(128)S(1)} %get-tuple-element.116.refs_2_, ...), custom_call_target="tpu_custom_call" | custom-call | flops 452984832 | bytes 4980736 | tf_op jit(solution)/shard_map/cond/branch_1_fun/attention_projection/pallas_call | solution.py:375
  41.9 0.8 collective-permute-start.16
  42.8 0.5 collective-permute-start.17
  43.3 4.5 %collective-permute-done.17.refs_3_ = bf16[16,4096]{1,0:T(8,128)(2,1)S(1)} collective-permute-done((bf16[16,4096]{1,0:T(8,128)(2,1)S(1)}, bf16[16,4096]{1,0:T(8,128)(2,1)S(1)}, u32[]{:S(2)}, u32[]{:S(2)}) %collective-permute-start.17) | collective-permute-done | bytes 131104 | tf_op jit(solution)/shard_map/cond/branch_1_fun/ppermute | solution.py:41
  47.7 1.6 %collective-permute-done.16.refs_1_ = bf16[32,4096]{1,0:T(8,128)(2,1)S(1)} collective-permute-done((bf16[32,4096]{1,0:T(8,128)(2,1)S(1)}, bf16[32,4096]{1,0:T(8,128)(2,1)S(1)}, u32[]{:S(2)}, u32[]{:S(2)}) %collective-permute-start.16) | collective-permute-done | bytes 262176 | tf_op jit(solution)/shard_map/cond/branch_1_fun/ppermute | solution.py:41
  49.4 0.7 sum_phase.6
  50.0 1.2 collective-permute-start.18
  51.2 1.3 collective-permute-start.19
  52.5 3.0 %collective-permute-done.19.refs_3_ = bf16[8,4096]{1,0:T(8,128)(2,1)S(1)} collective-permute-done((bf16[8,4096]{1,0:T(8,128)(2,1)S(1)}, bf16[8,4096]{1,0:T(8,128)(2,1)S(1)}, u32[]{:S(2)}, u32[]{:S(2)}) %collective-permute-start.19) | collective-permute-done | bytes 65568 | tf_op jit(solution)/shard_map/cond/branch_1_fun/ppermute | solution.py:41
  55.5 0.6 sum_phase.7
  56.1 2.4 %collective-permute-start.20 = (bf16[12,4096]{1,0:T(8,128)(2,1)S(1)}, bf16[12,4096]{1,0:T(8,128)(2,1)S(1)}, u32[]{:S(2)}, u32[]{:S(2)}) collective-permute-start(bf16[12,4096]{1,0:T(8,128)(2,1)S(1)} %get-tuple-element.89), channel_id=1, source_target_pairs={{0,2},{1,3},{2,0},{3,1},{4,6},{5,7},{6,4},{7,5},{8,10},{9,11},{10,... | collective-permute-start | bytes 294920 | tf_op jit(solution)/shard_map/cond/branch_1_fun/ppermute | solution.py:41
  58.5 5.3 %collective-permute-done.20.refs_4_ = bf16[12,4096]{1,0:T(8,128)(2,1)S(1)} collective-permute-done((bf16[12,4096]{1,0:T(8,128)(2,1)S(1)}, bf16[12,4096]{1,0:T(8,128)(2,1)S(1)}, u32[]{:S(2)}, u32[]{:S(2)}) %collective-permute-start.20) | collective-permute-done | bytes 98336 | tf_op jit(solution)/shard_map/cond/branch_1_fun/ppermute | solution.py:41
  63.9 1.3 token_rows.3
  65.1 0.1 collective-permute-start.21
  65.2 3.3 %collective-permute-start.22 = (bf16[3,4,4224]{2,1,0:T(4,128)(2,1)S(1)}, bf16[3,4,4224]{2,1,0:T(4,128)(2,1)S(1)}, u32[]{:S(2)}, u32[]{:S(2)}) collective-permute-start(bf16[3,4,4224]{2,1,0:T(4,128)(2,1)S(1)} %token_rows.3), channel_id=1, source_target_pairs={{0,2},{1,3},{2,0},{3,1},{4,6},{5,7},{6,4},{7,5},{8,10},{9,11},{10,... | collective-permute-start | bytes 304136 | tf_op jit(solution)/shard_map/cond/branch_1_fun/ppermute | solution.py:41
  68.5 1.1 collective-permute-start.23
  69.6 0.1 broadcast.7
  69.8 0.8 collective-permute-done.21
  70.6 5.3 %collective-permute-done.22 = bf16[3,4,4224]{2,1,0:T(4,128)(2,1)S(1)} collective-permute-done((bf16[3,4,4224]{2,1,0:T(4,128)(2,1)S(1)}, bf16[3,4,4224]{2,1,0:T(4,128)(2,1)S(1)}, u32[]{:S(2)}, u32[]{:S(2)}) %collective-permute-start.22) | collective-permute-done | bytes 101408 | tf_op jit(solution)/shard_map/cond/branch_1_fun/ppermute | solution.py:41
  75.9 0.1 bitcast_dynamic-update-slice_fusion.4
  76.0 0.1 collective-permute-start.24
  76.1 0.1 collective-permute-start.27
  76.1 0.4 collective-permute-start.25
  76.6 1.2 collective-permute-done.24.refs_1_
  77.8 11.5 %vocabulary_scores.9 = (f32[2,8,48]{2,1,0:T(8,128)S(1)}, bf16[2000,4096]{1,0:T(8,128)(2,1)S(1)}, s32[1]{0:T(128)}) custom-call(s32[5]{0:T(128)S(1)} %get-tuple-element.71.refs_0_.place_ref.first_ref, bf16[12,4,4224]{2,1,0:T(4,128)(2,1)S(1)} %bitcast.38, bf16[12,4,4224]{2,1,0:T(4,128)(2,1)S(1)} %collective-permute-done.24.refs_1_, ...), custom_call_target="tpu_custom_call" | custom-call | flops 2359296000 | bytes 786432 | tf_op jit(solution)/shard_map/cond/branch_1_fun/vocabulary_scores/pallas_call | solution.py:569
  89.3 5.6 %copy-done = bf16[2000,4096]{1,0:T(8,128)(2,1)} copy-done((bf16[2000,4096]{1,0:T(8,128)(2,1)}, bf16[2000,4096]{1,0:T(8,128)(2,1)S(1)}, u32[]{:S(2)}) %copy-start) | copy-done | bytes 16384024 | tf_op jit(solution)/shard_map/cond
  96.8 0.1 constant_dynamic-slice_fusion.3
  96.9 0.5 collective-permute-start.29
  98.7 0.1 constant_dynamic-slice_fusion.2
  98.8 2.0 %collective-permute-start.30 = (bf16[6,4,4224]{2,1,0:T(4,128)(2,1)S(1)}, bf16[6,4,4224]{2,1,0:T(4,128)(2,1)S(1)}, u32[]{:S(2)}, u32[]{:S(2)}) collective-permute-start(bf16[6,4,4224]{2,1,0:T(4,128)(2,1)S(1)} %constant_dynamic-slice_fusion.2), channel_id=1, source_target_pairs={{0,16},{16,0},{1,17},{17,1},{2,18},{18,2},{3,19},{19,3},{4,20},{20... | collective-permute-start | bytes 608264 | tf_op jit(solution)/shard_map/cond/branch_1_fun/ppermute | solution.py:41
  100.8 0.5 collective-permute-start.28
  101.4 2.7 %collective-permute-done.29 = bf16[6,4,4224]{2,1,0:T(4,128)(2,1)S(1)} collective-permute-done((bf16[6,4,4224]{2,1,0:T(4,128)(2,1)S(1)}, bf16[6,4,4224]{2,1,0:T(4,128)(2,1)S(1)}, u32[]{:S(2)}, u32[]{:S(2)}) %collective-permute-start.29) | collective-permute-done | bytes 202784 | tf_op jit(solution)/shard_map/cond/branch_1_fun/ppermute | solution.py:41
  104.1 0.1 constant_dynamic-update-slice_fusion.3
  104.1 1.5 %collective-permute-done.30 = bf16[6,4,4224]{2,1,0:T(4,128)(2,1)S(1)} collective-permute-done((bf16[6,4,4224]{2,1,0:T(4,128)(2,1)S(1)}, bf16[6,4,4224]{2,1,0:T(4,128)(2,1)S(1)}, u32[]{:S(2)}, u32[]{:S(2)}) %collective-permute-start.30) | collective-permute-done | bytes 202784 | tf_op jit(solution)/shard_map/cond/branch_1_fun/ppermute | solution.py:41
  105.6 0.1 constant_dynamic-update-slice_fusion.2.refs_0_
  105.7 0.1 collective-permute-start.31
  105.8 5.6 %copy-done.1 = bf16[2000,4096]{1,0:T(8,128)(2,1)S(1)} copy-done((bf16[2000,4096]{1,0:T(8,128)(2,1)S(1)}, bf16[2000,4096]{1,0:T(8,128)(2,1)}, u32[]{:S(2)}) %copy-start.1) | copy-done | bytes 16384024 | tf_op jit(solution)/shard_map/cond
  111.5 6.5 %vocabulary_scores.10.refs_1_ = f32[4,8,48]{2,1,0:T(8,128)S(1)} custom-call(s32[5]{0:T(128)S(1)} %get-tuple-element.71.refs_0_.place_ref.first_ref, bf16[12,4,4224]{2,1,0:T(4,128)(2,1)S(1)} %collective-permute-done.25.refs_0_, bf16[12,4,4224]{2,1,0:T(4,128)(2,1)S(1)} %collective-permute-done.26.refs_1_, ...), custom_call_target="tpu_custom_call" | custom-call | flops 4718592000 | bytes 1572864 | tf_op jit(solution)/shard_map/cond/branch_1_fun/vocabulary_scores/pallas_call | solution.py:569
  118.0 5.9 %vocabulary_scores.11.refs_2_ = f32[2,8,48]{2,1,0:T(8,128)S(1)} custom-call(s32[5]{0:T(128)S(1)} %get-tuple-element.71.refs_0_.place_ref.first_ref, bf16[12,4,4224]{2,1,0:T(4,128)(2,1)S(1)} %constant_dynamic-update-slice_fusion.2.refs_0_, bf16[12,4,4224]{2,1,0:T(4,128)(2,1)S(1)} %collective-permute-done.31.refs_1_, bf16[2000,4096]{1,0:T(8,128)(2,1)S(1)} %copy-done.1), custom_call_target="tpu_custom_call" | custom-call | flops 2359296000 | bytes 786432 | tf_op jit(solution)/shard_map/cond/branch_1_fun/vocabulary_scores/pallas_call | solution.py:569
  124.0 0.6 statistics_by_group.3
  124.6 12.5 %all_to_all.19.every_ref = f32[32,8,96]{2,1,0:T(8,128)S(1)} all-to-all(f32[32,8,96]{2,1,0:T(8,128)S(1)} %statistics_by_group.3), channel_id=1, replica_groups=mesh['section'=2,'tm'=4,'mp'=4] {'section','tm','mp'}, dimensions={0} | all-to-all | bytes 196608 | tf_op jit(solution)/shard_map/cond/branch_1_fun/all_to_all | solution.py:31
  137.1 0.7 hypothesis_scores.3
  137.8 0.6 copy-done.11
  (30 shorter events, 0.2 us)
Async XLA Ops:
  0.0 13.1 %copy-start.9 = (s32[2,8,16]{2,1,0:T(8,128)S(1)}, s32[2,8,16]{2,1,0:T(8,128)}, u32[]{:S(2)}) copy-start(s32[2,8,16]{2,1,0:T(8,128)} %param.21) | copy-start | bytes 3076
  0.0 13.1 %copy-start.8 = (s32[2,8]{1,0:T(2,128)S(1)}, s32[2,8]{1,0:T(2,128)}, u32[]{:S(2)}) copy-start(s32[2,8]{1,0:T(2,128)} %length_ref.1) | copy-start | bytes 196
  0.0 13.1 %copy-start.7 = (s32[8]{0:T(128)S(1)}, s32[8]{0:T(128)}, u32[]{:S(2)}) copy-start(s32[8]{0:T(128)} %slot_ref.1) | copy-start | bytes 100
  6.4 16.9 %copy-start.4 = (bf16[1280,1024]{1,0:T(8,128)(2,1)S(1)}, bf16[1280,1024]{1,0:T(8,128)(2,1)}, u32[]{:S(2)}) copy-start(bf16[1280,1024]{1,0:T(8,128)(2,1)} %refs_2_.1) | copy-start | bytes 7864324
  6.4 16.9 %all-to-all-start.2 = ((bf16[4,32,1280]{2,1,0:T(8,128)(2,1)}), bf16[4,32,1280]{2,1,0:T(8,128)(2,1)S(1)}, u32[]{:S(2)}, u32[]{:S(2)}) async-start(bf16[4,32,1280]{2,1,0:T(8,128)(2,1)} %get-tuple-element.104), calls=%async_computation.2 | async-start | bytes 655360 | tf_op jit(solution)/shard_map/all_to_all | solution.py:31
  13.1 25.0 %copy-start.10 = (s32[4]{0:T(128)S(1)}, s32[4]{0:T(128)}, u32[]{:S(2)}) copy-start(s32[4]{0:T(128)} %param.14) | copy-start | bytes 52
  19.1 1.6 %collective-permute-start.36 = (bf16[272,512]{1,0:T(8,128)(2,1)S(1)}, bf16[272,512]{1,0:T(8,128)(2,1)S(1)}, u32[]{:S(2)}, u32[]{:S(2)}) collective-permute-start(bf16[272,512]{1,0:T(8,128)(2,1)S(1)} %get-tuple-element.103), channel_id=1, source_target_pairs={{0,4},{4,0},{8,12},{12,8},{1,5},{5,1},{9,13},{13,9},{2,6},{6,2},{1... | collective-permute-start | bytes 835592 | tf_op jit(solution)/shard_map/ppermute | solution.py:41
  19.2 17.0 %collective-permute-start.35 = (bf16[272,512]{1,0:T(8,128)(2,1)S(1)}, bf16[272,512]{1,0:T(8,128)(2,1)}, u32[]{:S(2)}, u32[]{:S(2)}) collective-permute-start(bf16[272,512]{1,0:T(8,128)(2,1)S(1)} %get-tuple-element.101), channel_id=1, source_target_pairs={{0,4},{4,0},{8,12},{12,8},{1,5},{5,1},{9,13},{13,9},{2,6},{6,2},{1... | collective-permute-start | bytes 835592 | tf_op jit(solution)/shard_map/ppermute | solution.py:41
  21.5 14.7 %collective-permute-start.37 = (bf16[272,512]{1,0:T(8,128)(2,1)}, bf16[272,512]{1,0:T(8,128)(2,1)}, u32[]{:S(2)}, u32[]{:S(2)}) collective-permute-start(bf16[272,512]{1,0:T(8,128)(2,1)} %add.67), channel_id=1, source_target_pairs={{0,8},{4,12},{8,0},{12,4},{1,9},{5,13},{9,1},{13,5},{2,10},{6,14},... | collective-permute-start | bytes 835592 | tf_op jit(solution)/shard_map/ppermute | solution.py:41
  24.9 13.2 %all-to-all-start.3 = ((bf16[32,8,256]{2,1,0:T(8,128)(2,1)}), bf16[32,8,256]{2,1,0:T(8,128)(2,1)S(1)}, u32[]{:S(2)}, u32[]{:S(2)}) async-start(bf16[32,8,256]{2,1,0:T(8,128)(2,1)} %bitcast.22), calls=%async_computation.3 | async-start | bytes 262144 | tf_op jit(solution)/shard_map/all_to_all | solution.py:31
  30.5 1.9 %collective-permute-start.32 = (s32[1]{0:T(128)}, s32[1]{0:T(128)}, u32[]{:S(2)}, u32[]{:S(2)}) collective-permute-start(s32[1]{0:T(128)} %bitcast.14), channel_id=1, source_target_pairs={{0,4},{4,0},{8,12},{12,8},{1,5},{5,1},{9,13},{13,9},{2,6},{6,2},{1... | collective-permute-start | bytes 20 | tf_op jit(solution)/shard_map/ppermute | solution.py:41
  30.8 3.8 %collective-permute-start.33 = (s32[1]{0:T(128)}, s32[1]{0:T(128)}, u32[]{:S(2)}, u32[]{:S(2)}) collective-permute-start(s32[1]{0:T(128)} %bitcast.14), channel_id=1, source_target_pairs={{0,8},{4,12},{8,0},{12,4},{1,9},{5,13},{9,1},{13,5},{2,10},{6,14},... | collective-permute-start | bytes 20 | tf_op jit(solution)/shard_map/ppermute | solution.py:41
  32.5 3.1 %collective-permute-start.34 = (s32[1]{0:T(128)}, s32[1]{0:T(128)}, u32[]{:S(2)}, u32[]{:S(2)}) collective-permute-start(s32[1]{0:T(128)} %bitcast.14), channel_id=1, source_target_pairs={{0,12},{4,8},{8,4},{12,0},{1,13},{5,9},{9,5},{13,1},{2,14},{6,10},... | collective-permute-start | bytes 20 | tf_op jit(solution)/shard_map/ppermute | solution.py:41
  38.1 25.8 %copy-start.6 = (bf16[272,512]{1,0:T(8,128)(2,1)S(1)}, bf16[272,512]{1,0:T(8,128)(2,1)}, u32[]{:S(2)}) copy-start(bf16[272,512]{1,0:T(8,128)(2,1)} %get-tuple-element.74.refs_3_.refs_0_) | copy-start | bytes 835588 | tf_op jit(solution)/shard_map/cond
  41.9 7.4 %collective-permute-start.16 = (bf16[32,4096]{1,0:T(8,128)(2,1)S(1)}, bf16[32,4096]{1,0:T(8,128)(2,1)S(1)}, u32[]{:S(2)}, u32[]{:S(2)}) collective-permute-start(bf16[32,4096]{1,0:T(8,128)(2,1)S(1)} %get-tuple-element.81), channel_id=1, source_target_pairs={{0,16},{16,0},{1,17},{17,1},{2,18},{18,2},{3,19},{19,3},{4,20},{20... | collective-permute-start | bytes 786440 | tf_op jit(solution)/shard_map/cond/branch_1_fun/ppermute | solution.py:41
  42.8 5.0 %collective-permute-start.17 = (bf16[16,4096]{1,0:T(8,128)(2,1)S(1)}, bf16[16,4096]{1,0:T(8,128)(2,1)S(1)}, u32[]{:S(2)}, u32[]{:S(2)}) collective-permute-start(bf16[16,4096]{1,0:T(8,128)(2,1)S(1)} %get-tuple-element.83), channel_id=1, source_target_pairs={{0,1},{1,0},{2,3},{3,2},{4,5},{5,4},{6,7},{7,6},{8,9},{9,8},{10,11... | collective-permute-start | bytes 393224 | tf_op jit(solution)/shard_map/cond/branch_1_fun/ppermute | solution.py:41
  50.0 5.5 %collective-permute-start.18 = (bf16[16,4096]{1,0:T(8,128)(2,1)S(1)}, bf16[16,4096]{1,0:T(8,128)(2,1)S(1)}, u32[]{:S(2)}, u32[]{:S(2)}) collective-permute-start(bf16[16,4096]{1,0:T(8,128)(2,1)S(1)} %get-tuple-element.85), channel_id=1, source_target_pairs={{0,1},{1,0},{2,3},{3,2},{4,5},{5,4},{6,7},{7,6},{8,9},{9,8},{10,11... | collective-permute-start | bytes 393224 | tf_op jit(solution)/shard_map/cond/branch_1_fun/ppermute | solution.py:41
  51.2 4.3 %collective-permute-start.19 = (bf16[8,4096]{1,0:T(8,128)(2,1)S(1)}, bf16[8,4096]{1,0:T(8,128)(2,1)S(1)}, u32[]{:S(2)}, u32[]{:S(2)}) collective-permute-start(bf16[8,4096]{1,0:T(8,128)(2,1)S(1)} %get-tuple-element.87), channel_id=1, source_target_pairs={{0,16},{16,0},{1,17},{17,1},{2,18},{18,2},{3,19},{19,3},{4,20},{20... | collective-permute-start | bytes 196616 | tf_op jit(solution)/shard_map/cond/branch_1_fun/ppermute | solution.py:41
  56.1 7.8 %collective-permute-start.20 = (bf16[12,4096]{1,0:T(8,128)(2,1)S(1)}, bf16[12,4096]{1,0:T(8,128)(2,1)S(1)}, u32[]{:S(2)}, u32[]{:S(2)}) collective-permute-start(bf16[12,4096]{1,0:T(8,128)(2,1)S(1)} %get-tuple-element.89), channel_id=1, source_target_pairs={{0,2},{1,3},{2,0},{3,1},{4,6},{5,7},{6,4},{7,5},{8,10},{9,11},{10,... | collective-permute-start | bytes 294920 | tf_op jit(solution)/shard_map/cond/branch_1_fun/ppermute | solution.py:41
  65.1 5.4 %collective-permute-start.21 = (bf16[3,4,4224]{2,1,0:T(4,128)(2,1)S(1)}, bf16[3,4,4224]{2,1,0:T(4,128)(2,1)S(1)}, u32[]{:S(2)}, u32[]{:S(2)}) collective-permute-start(bf16[3,4,4224]{2,1,0:T(4,128)(2,1)S(1)} %token_rows.3), channel_id=1, source_target_pairs={{0,1},{1,0},{2,3},{3,2},{4,5},{5,4},{6,7},{7,6},{8,9},{9,8},{10,11... | collective-permute-start | bytes 304136 | tf_op jit(solution)/shard_map/cond/branch_1_fun/ppermute | solution.py:41
  65.2 10.7 %collective-permute-start.22 = (bf16[3,4,4224]{2,1,0:T(4,128)(2,1)S(1)}, bf16[3,4,4224]{2,1,0:T(4,128)(2,1)S(1)}, u32[]{:S(2)}, u32[]{:S(2)}) collective-permute-start(bf16[3,4,4224]{2,1,0:T(4,128)(2,1)S(1)} %token_rows.3), channel_id=1, source_target_pairs={{0,2},{1,3},{2,0},{3,1},{4,6},{5,7},{6,4},{7,5},{8,10},{9,11},{10,... | collective-permute-start | bytes 304136 | tf_op jit(solution)/shard_map/cond/branch_1_fun/ppermute | solution.py:41
  68.5 7.4 %collective-permute-start.23 = (bf16[3,4,4224]{2,1,0:T(4,128)(2,1)S(1)}, bf16[3,4,4224]{2,1,0:T(4,128)(2,1)S(1)}, u32[]{:S(2)}, u32[]{:S(2)}) collective-permute-start(bf16[3,4,4224]{2,1,0:T(4,128)(2,1)S(1)} %token_rows.3), channel_id=1, source_target_pairs={{0,3},{1,2},{2,1},{3,0},{4,7},{5,6},{6,5},{7,4},{8,11},{9,10},{10,... | collective-permute-start | bytes 304136 | tf_op jit(solution)/shard_map/cond/branch_1_fun/ppermute | solution.py:41
  76.0 1.8 %collective-permute-start.24 = (bf16[12,4,4224]{2,1,0:T(4,128)(2,1)S(1)}, bf16[12,4,4224]{2,1,0:T(4,128)(2,1)S(1)}, u32[]{:S(2)}, u32[]{:S(2)}) collective-permute-start(bf16[12,4,4224]{2,1,0:T(4,128)(2,1)S(1)} %bitcast.35), channel_id=1, source_target_pairs={{0,4},{4,0},{8,12},{12,8},{1,5},{5,1},{9,13},{13,9},{2,6},{6,2},{1... | collective-permute-start | bytes 1216520 | tf_op jit(solution)/shard_map/cond/branch_1_fun/ppermute | solution.py:41
  76.1 20.8 %collective-permute-start.27 = (bf16[12,4,4224]{2,1,0:T(4,128)(2,1)S(1)}, bf16[12,4,4224]{2,1,0:T(4,128)(2,1)S(1)}, u32[]{:S(2)}, u32[]{:S(2)}) collective-permute-start(bf16[12,4,4224]{2,1,0:T(4,128)(2,1)S(1)} %bitcast.36), channel_id=1, source_target_pairs={{0,16},{16,0},{1,17},{17,1},{2,18},{18,2},{3,19},{19,3},{4,20},{20... | collective-permute-start | bytes 1216520 | tf_op jit(solution)/shard_map/cond/branch_1_fun/ppermute | solution.py:41
  76.1 22.6 %collective-permute-start.25 = (bf16[12,4,4224]{2,1,0:T(4,128)(2,1)S(1)}, bf16[12,4,4224]{2,1,0:T(4,128)(2,1)S(1)}, u32[]{:S(2)}, u32[]{:S(2)}) collective-permute-start(bf16[12,4,4224]{2,1,0:T(4,128)(2,1)S(1)} %bitcast.37), channel_id=1, source_target_pairs={{0,8},{4,12},{8,0},{12,4},{1,9},{5,13},{9,1},{13,5},{2,10},{6,14},... | collective-permute-start | bytes 1216520 | tf_op jit(solution)/shard_map/cond/branch_1_fun/ppermute | solution.py:41
  89.3 5.6 %copy-start = (bf16[2000,4096]{1,0:T(8,128)(2,1)}, bf16[2000,4096]{1,0:T(8,128)(2,1)S(1)}, u32[]{:S(2)}) copy-start(bf16[2000,4096]{1,0:T(8,128)(2,1)S(1)} %get-tuple-element.92.refs_4_.refs_2_) | copy-start | bytes 49152004 | tf_op jit(solution)/shard_map/cond
  96.9 7.2 %collective-permute-start.29 = (bf16[6,4,4224]{2,1,0:T(4,128)(2,1)S(1)}, bf16[6,4,4224]{2,1,0:T(4,128)(2,1)S(1)}, u32[]{:S(2)}, u32[]{:S(2)}) collective-permute-start(bf16[6,4,4224]{2,1,0:T(4,128)(2,1)S(1)} %constant_dynamic-slice_fusion.3), channel_id=1, source_target_pairs={{0,8},{4,12},{8,0},{12,4},{1,9},{5,13},{9,1},{13,5},{2,10},{6,14},... | collective-permute-start | bytes 608264 | tf_op jit(solution)/shard_map/cond/branch_1_fun/ppermute | solution.py:41
  98.8 6.8 %collective-permute-start.30 = (bf16[6,4,4224]{2,1,0:T(4,128)(2,1)S(1)}, bf16[6,4,4224]{2,1,0:T(4,128)(2,1)S(1)}, u32[]{:S(2)}, u32[]{:S(2)}) collective-permute-start(bf16[6,4,4224]{2,1,0:T(4,128)(2,1)S(1)} %constant_dynamic-slice_fusion.2), channel_id=1, source_target_pairs={{0,16},{16,0},{1,17},{17,1},{2,18},{18,2},{3,19},{19,3},{4,20},{20... | collective-permute-start | bytes 608264 | tf_op jit(solution)/shard_map/cond/branch_1_fun/ppermute | solution.py:41
  100.8 5.0 %collective-permute-start.26 = (bf16[12,4,4224]{2,1,0:T(4,128)(2,1)S(1)}, bf16[12,4,4224]{2,1,0:T(4,128)(2,1)S(1)}, u32[]{:S(2)}, u32[]{:S(2)}) collective-permute-start(bf16[12,4,4224]{2,1,0:T(4,128)(2,1)S(1)} %collective-permute-done.25.refs_0_), channel_id=1, source_target_pairs={{0,4},{4,0},{8,12},{12,8},{1,5},{5,1},{9,13},{13,9},{2,6},{6,2},{1... | collective-permute-start | bytes 1216520 | tf_op jit(solution)/shard_map/cond/branch_1_fun/ppermute | solution.py:41
  100.8 5.0 %collective-permute-start.28 = (bf16[12,4,4224]{2,1,0:T(4,128)(2,1)S(1)}, bf16[12,4,4224]{2,1,0:T(4,128)(2,1)S(1)}, u32[]{:S(2)}, u32[]{:S(2)}) collective-permute-start(bf16[12,4,4224]{2,1,0:T(4,128)(2,1)S(1)} %collective-permute-done.27.refs_2_), channel_id=1, source_target_pairs={{0,4},{4,0},{8,12},{12,8},{1,5},{5,1},{9,13},{13,9},{2,6},{6,2},{1... | collective-permute-start | bytes 1216520 | tf_op jit(solution)/shard_map/cond/branch_1_fun/ppermute | solution.py:41
  105.7 12.3 %collective-permute-start.31 = (bf16[12,4,4224]{2,1,0:T(4,128)(2,1)S(1)}, bf16[12,4,4224]{2,1,0:T(4,128)(2,1)S(1)}, u32[]{:S(2)}, u32[]{:S(2)}) collective-permute-start(bf16[12,4,4224]{2,1,0:T(4,128)(2,1)S(1)} %constant_dynamic-update-slice_fusion.2.refs_0_), channel_id=1, source_target_pairs={{0,4},{4,0},{8,12},{12,8},{1,5},{5,1},{9,13},{13,9},{2,6},{6,2},{1... | collective-permute-start | bytes 1216520 | tf_op jit(solution)/shard_map/cond/branch_1_fun/ppermute | solution.py:41
  105.8 5.7 %copy-start.1 = (bf16[2000,4096]{1,0:T(8,128)(2,1)S(1)}, bf16[2000,4096]{1,0:T(8,128)(2,1)}, u32[]{:S(2)}) copy-start(bf16[2000,4096]{1,0:T(8,128)(2,1)} %copy-done) | copy-start | bytes 49152004 | tf_op jit(solution)/shard_map/cond
  137.8 0.6 copy-start.11

commit v15 on v14

--- a/solution.py
+++ b/solution.py
@@ -492,31 +492,10 @@
 
 
 def vocabulary_kernel(tile, count, first_ref, *refs):
-    sets, head_ref, out_ref = refs[:count], refs[count], refs[count + 1]
-    loads = len(refs) > count + 4
-    if loads:
-        loaded_ref, zero_ref, rows_ref, stat, semaphores = refs[count + 2 :]
-        zero_ref[0] = 0
-    else:
-        rows_ref, stat = refs[count + 2 :]
+    sets, (head_ref, out_ref, rows_ref, stat) = refs[:count], refs[count:]
     vocab_rows, width = head_ref.shape
     share = sets[0].shape[0] * FOLD
     tokens = share * len(sets)
-    tiles = vocab_rows // tile
-    pieces = 5
-
-    def load(number):
-        size = tile // pieces
-        place = lambda i: pl.ds(number * tile + i * size, size)
-        return start_copies(
-            lambda i: head_ref.at[place(i), :],
-            lambda i: loaded_ref.at[place(i), :],
-            semaphores.at[number],
-            pieces,
-        )
-
-    if loads:
-        copies = [load(0), load(1)]
     cell = lax.broadcasted_iota(jnp.int32, (8, LANES), 1)
     take = jnp.where(cell == 0, 256.0, jnp.where(cell == 1, 1.0, 0.0)).astype(jnp.bfloat16)
     for number, rows in enumerate(sets):
@@ -527,8 +506,10 @@
     stat[8:9, :] = jnp.zeros((1, tokens), jnp.float32)
     stat[16:17, :] = jnp.zeros((1, tokens), jnp.float32)
 
-    def one_tile(start, block):
-        logits = dot_nt(block, rows_ref[:, :width])
+    @pl.loop(0, vocab_rows // tile)
+    def _(step):
+        start = pl.multiple_of(step * tile, tile)
+        logits = dot_nt(head_ref[pl.ds(start, tile), :], rows_ref[:, :width])
         vocab = lax.broadcasted_iota(jnp.int32, logits.shape, 0) + start
         before = stat[0:1, :]
         upper = jnp.maximum(before, jnp.max(logits, axis=0, keepdims=True))
@@ -538,20 +519,6 @@
         stat[16:17, :] += jnp.sum(jnp.where(vocab == target, logits, 0.0), axis=0, keepdims=True)
         stat[0:1, :] = upper
 
-    if loads:
-        for number in range(tiles):
-            for copy in copies[number]:
-                copy.wait()
-            if number + 2 < tiles:
-                copies.append(load(number + 2))
-            one_tile(number * tile, loaded_ref[number * tile : (number + 1) * tile, :])
-    else:
-
-        @pl.loop(0, tiles)
-        def _(step):
-            start = pl.multiple_of(step * tile, tile)
-            one_tile(start, head_ref[pl.ds(start, tile), :])
-
     for number in range(len(sets)):
         for row in range(3):
             out_ref[number, row : row + 1, :] = stat[
@@ -559,41 +526,43 @@
             ]
 
 
-def vocabulary_stats(place, sets, head, load=False):
+def vocabulary_stats(place, sets, head):
     share = sets[0].shape[0] * FOLD
     count = len(sets)
     width = head.shape[1]
     tokens = share * count
-    tile = head.shape[0] // (5 if load else 2)
-    stats = jax.ShapeDtypeStruct((count, 8, share), jnp.float32)
     return pl.pallas_call(
-        functools.partial(vocabulary_kernel, tile, count),
-        in_specs=[SCALARS] + [INSIDE] * count + [ANYWHERE if load else INSIDE],
-        out_specs=[INSIDE, INSIDE, SCALARS] if load else INSIDE,
-        out_shape=[
-            stats,
-            pltpu.VMEM(head.shape, head.dtype),
-            jax.ShapeDtypeStruct((1,), jnp.int32),
-        ]
-        if load
-        else stats,
+        functools.partial(vocabulary_kernel, head.shape[0] // 2, count),
+        in_specs=[SCALARS] + [INSIDE] * (count + 1),
+        out_specs=INSIDE,
+        out_shape=jax.ShapeDtypeStruct((count, 8, share), jnp.float32),
         scratch_shapes=[
             pltpu.VMEM((tokens, width + LANES), jnp.bfloat16),
             pltpu.VMEM((24, tokens), jnp.float32),
-        ]
-        + ([pltpu.SemaphoreType.DMA((5, 5))] if load else []),
+        ],
         cost_estimate=pl.CostEstimate(
             flops=3 * tokens * head.shape[0] * width,
             bytes_accessed=2 * tokens * width,
             transcendentals=tokens * head.shape[0],
         ),
-        compiler_params=pltpu.CompilerParams(vmem_limit_bytes=(36 if load else 16) << 20),
+        compiler_params=pltpu.CompilerParams(vmem_limit_bytes=16 << 20),
         name="vocabulary_scores",
-    )(
-        place,
-        *sets,
-        in_hbm(head) if load else pltpu.with_memory_space_constraint(head, pltpu.VMEM),
-    )
+    )(place, *sets, pltpu.with_memory_space_constraint(head, pltpu.VMEM))
+
+
+def zero_kernel(after_ref, head_ref, out_ref):
+    out_ref[0] = 0
+
+
+def zero_after(after, head):
+    return pl.pallas_call(
+        zero_kernel,
+        in_specs=[ANYWHERE, INSIDE],
+        out_specs=SCALARS,
+        out_shape=jax.ShapeDtypeStruct((1,), jnp.int32),
+        compiler_params=pltpu.CompilerParams(vmem_limit_bytes=16 << 20),
+        name="vocabulary_rows",
+    )(after, pltpu.with_memory_space_constraint(head, pltpu.VMEM))
 
 
 def spread_kernel(sections, groups, widths, place_ref, slot_ref, *refs):
@@ -721,17 +690,18 @@
     half = own.shape[0] // 2
     by_x = swap(own, "section", 1)
     by_y = swap(own, "tm", 2)
-    stats, head, zero = vocabulary_stats(place, [own, swap(own, "tm", 1)], head, load=True)
-    stats = [stats]
+    zero = zero_after(own, head)
     across = [
         swap(lax.dynamic_slice_in_dim(by_x, zero[0], half, 0), "tm", 2),
         swap(lax.dynamic_slice_in_dim(by_y, zero[0] + half, half, 0), "section", 1),
     ]
+    stats = [
+        vocabulary_stats(place, [own, swap(own, "tm", 1), by_y, swap(by_y, "tm", 1)], head)
+    ]
+    across = jnp.concatenate(across)
     stats.append(
-        vocabulary_stats(place, [by_y, swap(by_y, "tm", 1), by_x, swap(by_x, "tm", 1)], head)
-    )
-    across = jnp.concatenate(across)
-    stats.append(vocabulary_stats(place, [across, swap(across, "tm", 1)], head))
+        vocabulary_stats(place, [by_x, swap(by_x, "tm", 1), across, swap(across, "tm", 1)], head)
+    )
 
     every = exchange(
         spread_stats(place, slot_utt, stats, section_count, group_count, width_count), ALL

time: 139 us -> 129 us (0.928)
  Pallas kernels: 45.4 us -> 35.3 us
    pallas_call x3, Pallas kernels: 23.9 us -> 13.6 us  [the longest x2 13.1 us: vocabulary_stats(): pl.pallas_call(functools.partial(vocabulary_kernel, head.shape[0] // 2, c...]
  transfers between devices with their start and end apart: 24 -> 24, of which waited for: 14 -> 14; matrix products, arithmetic and copies ran while one was open for 2% -> 2% of each run, Pallas kernels for 18% -> 11%
where the time goes in v15:
time: 129 us; the launch traced here: 128 us
  Pallas kernels  35.3 us (27%)
  starting transfers between devices  30.9 us (24%)
  waiting for transfers between devices  29.4 us (23%)
  local copies, waits for them, and re-layouts  12.7 us (10%)
  blocking collectives  12.2 us (9%)
  loops' own time  3.52 us (3%)
  between operations  2.69 us (2%)
  other arithmetic  1.63 us (1%)
    ppermute x22, waiting for transfers between devices, swap(): return lax.ppermute(values, axis, pairs)  27.4 us
    ppermute x22, starting transfers between devices, swap(): return lax.ppermute(values, axis, pairs)  19.6 us
    pallas_call x2, Pallas kernels, vocabulary_stats(): pl.pallas_call(functools.partial(vocabulary_kernel, head.shape[0] // 2, c...  13.1 us
    all_to_all x1, blocking collectives, exchange(): return lax.all_to_all(blocks, axis, split_axis=0, concat_axis=0, tiled=True)  12.2 us
    cond x7, local copies, waits for them, and re-layouts  11.4 us
    all_to_all x2, starting transfers between devices, exchange(): return lax.all_to_all(blocks, axis, split_axis=0, concat_axis=0, tiled=True)  11.4 us
    pallas_call x1, Pallas kernels, ffn(): pl.pallas_call(functools.partial(ffn_kernel, tile), in_specs=[SCALARS] +...  6.32 us
    pallas_call x1, Pallas kernels, queries_of(): pl.pallas_call(functools.partial(query_kernel, count, depth), in_specs=[S...  6.15 us
  transfers between devices with their start and end apart: 24, of which 14 were waited for; matrix products, arithmetic and copies ran while one was open for 2% of the time, Pallas kernels for 11%

profile of v15, /device:TPU:0, one launch (start us, length us, event | category | flops | bytes accessed | tf_op | source)
XLA Modules:
  0.0 128.4 jit_solution(8927438875023522245)
XLA Ops:
  0.0 0.1 stack.23.place_ref.after_ref
  0.1 6.3 %encoder_ffn.1 = (bf16[4,32,1280]{2,1,0:T(8,128)(2,1)}, bf16[32,1280]{1,0:T(8,128)(2,1)S(1)}) custom-call(s32[5]{0:T(128)S(1)} %stack.23.place_ref.after_ref, bf16[32,4,1280]{2,1,0:T(4,128)(2,1)} %x_ref.1, bf16[1280,1280]{1,0:T(8,128)(2,1)} %up_ref.1, bf16[1280,1280]{1,0:T(8,128)(2,1)} %down_ref.1), custom_call_target="tpu_custom_call" | custom-call | flops 838860800 | bytes 6553600 | tf_op jit(solution)/shard_map/encoder_ffn/pallas_call | solution.py:121
  6.4 6.3 %all-to-all-start.2 = ((bf16[4,32,1280]{2,1,0:T(8,128)(2,1)}), bf16[4,32,1280]{2,1,0:T(8,128)(2,1)S(1)}, u32[]{:S(2)}, u32[]{:S(2)}) async-start(bf16[4,32,1280]{2,1,0:T(8,128)(2,1)} %get-tuple-element.98), calls=%async_computation.2 | async-start | bytes 655360 | tf_op jit(solution)/shard_map/all_to_all | solution.py:31
  12.7 0.1 reshape.27.tok_ref
  12.8 6.1 %hypothesis_queries.1 = (bf16[272,512]{1,0:T(8,128)(2,1)}, bf16[272,512]{1,0:T(8,128)(2,1)S(1)}, bf16[272,512]{1,0:T(8,128)(2,1)S(1)}, bf16[272,512]{1,0:T(8,128)(2,1)S(1)}) custom-call(s32[5]{0:T(128)S(1)} %stack.23.place_ref.after_ref, s32[8]{0:T(128)S(1)} %copy-done.7, s32[2,8]{1,0:T(2,128)S(1)} %copy-done.8, s32[5]{0:T(128)S(1)} %stack.23.place_ref.after_ref, ...), custom_call_target="tpu_custom_call" | custom-call | flops 1073741824 | bytes 6291456 | tf_op jit(solution)/shard_map/hypothesis_queries/pallas_call | solution.py:228
  19.0 0.1 collective-permute-start.36
  19.1 0.5 collective-permute-start.35
  19.6 1.0 collective-permute-done.36
  20.6 0.8 add.67
  21.4 1.5 %collective-permute-start.37 = (bf16[272,512]{1,0:T(8,128)(2,1)}, bf16[272,512]{1,0:T(8,128)(2,1)}, u32[]{:S(2)}, u32[]{:S(2)}) collective-permute-start(bf16[272,512]{1,0:T(8,128)(2,1)} %add.67), channel_id=1, source_target_pairs={{0,8},{4,12},{8,0},{12,4},{1,9},{5,13},{9,1},{13,5},{2,10},{6,14},... | collective-permute-start | bytes 835592 | tf_op jit(solution)/shard_map/ppermute | solution.py:41
  23.0 0.1 all-to-all-done.2.refs_0_
  23.1 1.5 %frame_keys_values.1 = bf16[256,256]{1,0:T(8,128)(2,1)} custom-call(bf16[4,32,1280]{2,1,0:T(8,128)(2,1)S(1)} %all-to-all-done.2.refs_0_, bf16[32,1280]{1,0:T(8,128)(2,1)S(1)} %get-tuple-element.99.refs_1_, bf16[1280,1024]{1,0:T(8,128)(2,1)S(1)} %copy-done.4, bf16[272,512]{1,0:T(8,128)(2,1)} %get-tuple-element.94.refs_3_), custom_call_target="tpu_custom_call" | custom-call | flops 83886080 | bytes 2621440 | tf_op jit(solution)/shard_map/frame_keys_values/pallas_call | solution.py:287
  24.6 5.0 %all-to-all-start.3 = ((bf16[32,8,256]{2,1,0:T(8,128)(2,1)}), bf16[32,8,256]{2,1,0:T(8,128)(2,1)S(1)}, u32[]{:S(2)}, u32[]{:S(2)}) async-start(bf16[32,8,256]{2,1,0:T(8,128)(2,1)} %bitcast.22), calls=%async_computation.3 | async-start | bytes 262144 | tf_op jit(solution)/shard_map/all_to_all | solution.py:31
  29.7 0.1 reduce_sum.9
  29.8 0.7 fusion
  30.5 0.3 collective-permute-start.32
  30.7 1.7 %collective-permute-start.33 = (s32[1]{0:T(128)}, s32[1]{0:T(128)}, u32[]{:S(2)}, u32[]{:S(2)}) collective-permute-start(s32[1]{0:T(128)} %bitcast.14), channel_id=1, source_target_pairs={{0,8},{4,12},{8,0},{12,4},{1,9},{5,13},{9,1},{13,5},{2,10},{6,14},... | collective-permute-start | bytes 20 | tf_op jit(solution)/shard_map/ppermute | solution.py:41
  33.7 0.7 collective-permute-done.33
  35.1 0.4 collective-permute-done.34
  36.1 1.9 %all-to-all-done.3 = bf16[32,8,256]{2,1,0:T(8,128)(2,1)S(1)} async-done(((bf16[32,8,256]{2,1,0:T(8,128)(2,1)}), bf16[32,8,256]{2,1,0:T(8,128)(2,1)S(1)}, u32[]{:S(2)}, u32[]{:S(2)}) %all-to-all-start.3) | async-done | bytes 131104 | tf_op jit(solution)/shard_map/all_to_all | solution.py:31
  38.1 89.8 %conditional.1 = (f32[2,8]{1,0:T(2,128)S(1)}) conditional(s32[]{:T(128)} %bitcast.15, (s32[5]{0:T(128)S(1)}, s32[8]{0:T(128)S(1)}, s32[4]{0:T(128)S(1)}, bf16[272,512]{1,0:T(8,128)(2,1)}, bf16[272,512]{1,0:T(8,128)(2,1)}, /*index=5*/bf16[272,512]{1,0:T(8,128)(2,1)}, bf16[32,8,256]{2,1,0:T(8,128)(2,1)S(1)}, bf16[512,4096]{1,0:T(8,128)(2,1)}, ...), branch_computations={%region_2.3_spmd, %region_3.4_spmd} | conditional | flops 13186891776 | bytes 166102016 | solution.py:779
  38.1 3.8 %attention_projection.3 = (bf16[32,4096]{1,0:T(8,128)(2,1)S(1)}, bf16[32,4096]{1,0:T(8,128)(2,1)S(1)}, bf16[16,4096]{1,0:T(8,128)(2,1)S(1)}, bf16[16,4096]{1,0:T(8,128)(2,1)S(1)}) custom-call(s32[5]{0:T(128)S(1)} %get-tuple-element.68.refs_0_.place_ref.first_ref, s32[8]{0:T(128)S(1)} %get-tuple-element.69.refs_1_.slot_ref, s32[4]{0:T(128)S(1)} %get-tuple-element.110.refs_2_, ...), custom_call_target="tpu_custom_call" | custom-call | flops 452984832 | bytes 4980736 | tf_op jit(solution)/shard_map/cond/branch_1_fun/attention_projection/pallas_call | solution.py:375
  41.9 0.8 collective-permute-start.16
  42.7 0.5 collective-permute-start.17
  43.2 4.5 %collective-permute-done.17.refs_3_ = bf16[16,4096]{1,0:T(8,128)(2,1)S(1)} collective-permute-done((bf16[16,4096]{1,0:T(8,128)(2,1)S(1)}, bf16[16,4096]{1,0:T(8,128)(2,1)S(1)}, u32[]{:S(2)}, u32[]{:S(2)}) %collective-permute-start.17) | collective-permute-done | bytes 131104 | tf_op jit(solution)/shard_map/cond/branch_1_fun/ppermute | solution.py:41
  47.7 1.6 %collective-permute-done.16.refs_1_ = bf16[32,4096]{1,0:T(8,128)(2,1)S(1)} collective-permute-done((bf16[32,4096]{1,0:T(8,128)(2,1)S(1)}, bf16[32,4096]{1,0:T(8,128)(2,1)S(1)}, u32[]{:S(2)}, u32[]{:S(2)}) %collective-permute-start.16) | collective-permute-done | bytes 262176 | tf_op jit(solution)/shard_map/cond/branch_1_fun/ppermute | solution.py:41
  49.3 0.7 sum_phase.6
  50.0 1.2 collective-permute-start.18
  51.2 1.3 %collective-permute-start.19 = (bf16[8,4096]{1,0:T(8,128)(2,1)S(1)}, bf16[8,4096]{1,0:T(8,128)(2,1)S(1)}, u32[]{:S(2)}, u32[]{:S(2)}) collective-permute-start(bf16[8,4096]{1,0:T(8,128)(2,1)S(1)} %get-tuple-element.84), channel_id=1, source_target_pairs={{0,16},{16,0},{1,17},{17,1},{2,18},{18,2},{3,19},{19,3},{4,20},{20... | collective-permute-start | bytes 196616 | tf_op jit(solution)/shard_map/cond/branch_1_fun/ppermute | solution.py:41
  52.5 3.0 %collective-permute-done.19.refs_3_ = bf16[8,4096]{1,0:T(8,128)(2,1)S(1)} collective-permute-done((bf16[8,4096]{1,0:T(8,128)(2,1)S(1)}, bf16[8,4096]{1,0:T(8,128)(2,1)S(1)}, u32[]{:S(2)}, u32[]{:S(2)}) %collective-permute-start.19) | collective-permute-done | bytes 65568 | tf_op jit(solution)/shard_map/cond/branch_1_fun/ppermute | solution.py:41
  55.5 0.6 sum_phase.7
  56.1 2.4 %collective-permute-start.20 = (bf16[12,4096]{1,0:T(8,128)(2,1)S(1)}, bf16[12,4096]{1,0:T(8,128)(2,1)S(1)}, u32[]{:S(2)}, u32[]{:S(2)}) collective-permute-start(bf16[12,4096]{1,0:T(8,128)(2,1)S(1)} %get-tuple-element.86), channel_id=1, source_target_pairs={{0,2},{1,3},{2,0},{3,1},{4,6},{5,7},{6,4},{7,5},{8,10},{9,11},{10,... | collective-permute-start | bytes 294920 | tf_op jit(solution)/shard_map/cond/branch_1_fun/ppermute | solution.py:41
  58.5 5.3 %collective-permute-done.20.refs_4_ = bf16[12,4096]{1,0:T(8,128)(2,1)S(1)} collective-permute-done((bf16[12,4096]{1,0:T(8,128)(2,1)S(1)}, bf16[12,4096]{1,0:T(8,128)(2,1)S(1)}, u32[]{:S(2)}, u32[]{:S(2)}) %collective-permute-start.20) | collective-permute-done | bytes 98336 | tf_op jit(solution)/shard_map/cond/branch_1_fun/ppermute | solution.py:41
  63.8 1.3 token_rows.3
  65.1 0.1 collective-permute-start.21
  65.2 3.3 %collective-permute-start.22 = (bf16[3,4,4224]{2,1,0:T(4,128)(2,1)S(1)}, bf16[3,4,4224]{2,1,0:T(4,128)(2,1)S(1)}, u32[]{:S(2)}, u32[]{:S(2)}) collective-permute-start(bf16[3,4,4224]{2,1,0:T(4,128)(2,1)S(1)} %token_rows.3), channel_id=1, source_target_pairs={{0,2},{1,3},{2,0},{3,1},{4,6},{5,7},{6,4},{7,5},{8,10},{9,11},{10,... | collective-permute-start | bytes 304136 | tf_op jit(solution)/shard_map/cond/branch_1_fun/ppermute | solution.py:41
  68.4 1.1 collective-permute-start.23
  69.5 0.1 broadcast.7
  69.7 0.1 bitcast_dynamic-update-slice_fusion.7
  69.7 0.8 collective-permute-done.21
  70.5 0.1 bitcast_dynamic-update-slice_fusion.6
  70.6 5.3 %collective-permute-done.22 = bf16[3,4,4224]{2,1,0:T(4,128)(2,1)S(1)} collective-permute-done((bf16[3,4,4224]{2,1,0:T(4,128)(2,1)S(1)}, bf16[3,4,4224]{2,1,0:T(4,128)(2,1)S(1)}, u32[]{:S(2)}, u32[]{:S(2)}) %collective-permute-start.22) | collective-permute-done | bytes 101408 | tf_op jit(solution)/shard_map/cond/branch_1_fun/ppermute | solution.py:41
  75.9 0.1 bitcast_dynamic-update-slice_fusion.4
  76.0 0.6 collective-permute-start.27
  76.5 5.7 %copy-done.2 = bf16[2000,4096]{1,0:T(8,128)(2,1)S(1)} copy-done((bf16[2000,4096]{1,0:T(8,128)(2,1)S(1)}, bf16[2000,4096]{1,0:T(8,128)(2,1)}, u32[]{:S(2)}) %copy-start.2) | copy-done | bytes 16384024 | tf_op jit(solution)/shard_map/cond
  82.2 0.5 vocabulary_rows.3
  86.1 0.1 constant_dynamic-slice_fusion.3
  86.2 2.1 %collective-permute-start.29 = (bf16[6,4,4224]{2,1,0:T(4,128)(2,1)S(1)}, bf16[6,4,4224]{2,1,0:T(4,128)(2,1)S(1)}, u32[]{:S(2)}, u32[]{:S(2)}) collective-permute-start(bf16[6,4,4224]{2,1,0:T(4,128)(2,1)S(1)} %constant_dynamic-slice_fusion.3), channel_id=1, source_target_pairs={{0,8},{4,12},{8,0},{12,4},{1,9},{5,13},{9,1},{13,5},{2,10},{6,14},... | collective-permute-start | bytes 608264 | tf_op jit(solution)/shard_map/cond/branch_1_fun/ppermute | solution.py:41
  88.2 0.1 collective-permute-done.25.refs_2_
  88.3 0.1 constant_dynamic-slice_fusion.2
  88.4 1.6 %collective-permute-start.30 = (bf16[6,4,4224]{2,1,0:T(4,128)(2,1)S(1)}, bf16[6,4,4224]{2,1,0:T(4,128)(2,1)S(1)}, u32[]{:S(2)}, u32[]{:S(2)}) collective-permute-start(bf16[6,4,4224]{2,1,0:T(4,128)(2,1)S(1)} %constant_dynamic-slice_fusion.2), channel_id=1, source_target_pairs={{0,16},{16,0},{1,17},{17,1},{2,18},{18,2},{3,19},{19,3},{4,20},{20... | collective-permute-start | bytes 608264 | tf_op jit(solution)/shard_map/cond/branch_1_fun/ppermute | solution.py:41
  90.0 0.5 collective-permute-start.28
  90.5 3.2 %collective-permute-done.29 = bf16[6,4,4224]{2,1,0:T(4,128)(2,1)S(1)} collective-permute-done((bf16[6,4,4224]{2,1,0:T(4,128)(2,1)S(1)}, bf16[6,4,4224]{2,1,0:T(4,128)(2,1)S(1)}, u32[]{:S(2)}, u32[]{:S(2)}) %collective-permute-start.29) | collective-permute-done | bytes 202784 | tf_op jit(solution)/shard_map/cond/branch_1_fun/ppermute | solution.py:41
  93.7 0.1 constant_dynamic-update-slice_fusion.3
  93.8 1.5 %collective-permute-done.30 = bf16[6,4,4224]{2,1,0:T(4,128)(2,1)S(1)} collective-permute-done((bf16[6,4,4224]{2,1,0:T(4,128)(2,1)S(1)}, bf16[6,4,4224]{2,1,0:T(4,128)(2,1)S(1)}, u32[]{:S(2)}, u32[]{:S(2)}) %collective-permute-start.30) | collective-permute-done | bytes 202784 | tf_op jit(solution)/shard_map/cond/branch_1_fun/ppermute | solution.py:41
  95.3 0.1 constant_dynamic-update-slice_fusion.2.refs_2_
  95.4 0.1 collective-permute-start.31
  95.5 5.6 %copy-done.3 = bf16[2000,4096]{1,0:T(8,128)(2,1)S(1)} copy-done((bf16[2000,4096]{1,0:T(8,128)(2,1)S(1)}, bf16[2000,4096]{1,0:T(8,128)(2,1)}, u32[]{:S(2)}) %copy-start.3) | copy-done | bytes 16384024 | tf_op jit(solution)/shard_map/cond
  101.1 6.5 %vocabulary_scores.6.refs_0_ = f32[4,8,48]{2,1,0:T(8,128)S(1)} custom-call(s32[5]{0:T(128)S(1)} %get-tuple-element.68.refs_0_.place_ref.first_ref, bf16[12,4,4224]{2,1,0:T(4,128)(2,1)S(1)} %bitcast.35, bf16[12,4,4224]{2,1,0:T(4,128)(2,1)S(1)} %collective-permute-done.24.refs_1_, bf16[12,4,4224]{2,1,0:T(4,128)(2,1)S(1)} %collective-permute-done.25.refs_2_, ...), custom_call_target="tpu_custom_call" | custom-call | flops 4718592000 | bytes 1572864 | tf_op jit(solution)/shard_map/cond/branch_1_fun/vocabulary_scores/pallas_call | solution.py:534
  107.7 6.5 %vocabulary_scores.7.refs_1_ = f32[4,8,48]{2,1,0:T(8,128)S(1)} custom-call(s32[5]{0:T(128)S(1)} %get-tuple-element.68.refs_0_.place_ref.first_ref, bf16[12,4,4224]{2,1,0:T(4,128)(2,1)S(1)} %collective-permute-done.27.refs_0_, bf16[12,4,4224]{2,1,0:T(4,128)(2,1)S(1)} %collective-permute-done.28.refs_1_, ...), custom_call_target="tpu_custom_call" | custom-call | flops 4718592000 | bytes 1572864 | tf_op jit(solution)/shard_map/cond/branch_1_fun/vocabulary_scores/pallas_call | solution.py:534
  114.2 0.7 statistics_by_group.3
  114.9 12.2 %all_to_all.19.every_ref = f32[32,8,96]{2,1,0:T(8,128)S(1)} all-to-all(f32[32,8,96]{2,1,0:T(8,128)S(1)} %statistics_by_group.3), channel_id=1, replica_groups=mesh['section'=2,'tm'=4,'mp'=4] {'section','tm','mp'}, dimensions={0} | all-to-all | bytes 196608 | tf_op jit(solution)/shard_map/cond/branch_1_fun/all_to_all | solution.py:31
  127.1 0.7 hypothesis_scores.3
  127.9 0.6 copy-done.11
  (30 shorter events, 0.1 us)
Async XLA Ops:
  0.1 12.7 %copy-start.9 = (s32[2,8,16]{2,1,0:T(8,128)S(1)}, s32[2,8,16]{2,1,0:T(8,128)}, u32[]{:S(2)}) copy-start(s32[2,8,16]{2,1,0:T(8,128)} %param.21) | copy-start | bytes 3076
  0.1 12.7 %copy-start.7 = (s32[8]{0:T(128)S(1)}, s32[8]{0:T(128)}, u32[]{:S(2)}) copy-start(s32[8]{0:T(128)} %slot_ref.1) | copy-start | bytes 100
  0.1 12.7 %copy-start.8 = (s32[2,8]{1,0:T(2,128)S(1)}, s32[2,8]{1,0:T(2,128)}, u32[]{:S(2)}) copy-start(s32[2,8]{1,0:T(2,128)} %length_ref.1) | copy-start | bytes 196
  6.4 16.7 %all-to-all-start.2 = ((bf16[4,32,1280]{2,1,0:T(8,128)(2,1)}), bf16[4,32,1280]{2,1,0:T(8,128)(2,1)S(1)}, u32[]{:S(2)}, u32[]{:S(2)}) async-start(bf16[4,32,1280]{2,1,0:T(8,128)(2,1)} %get-tuple-element.98), calls=%async_computation.2 | async-start | bytes 655360 | tf_op jit(solution)/shard_map/all_to_all | solution.py:31
  12.8 10.2 %copy-start.4 = (bf16[1280,1024]{1,0:T(8,128)(2,1)S(1)}, bf16[1280,1024]{1,0:T(8,128)(2,1)}, u32[]{:S(2)}) copy-start(bf16[1280,1024]{1,0:T(8,128)(2,1)} %refs_2_.1) | copy-start | bytes 7864324
  19.0 19.1 %copy-start.10 = (s32[4]{0:T(128)S(1)}, s32[4]{0:T(128)}, u32[]{:S(2)}) copy-start(s32[4]{0:T(128)} %param.14) | copy-start | bytes 52
  19.0 1.6 %collective-permute-start.36 = (bf16[272,512]{1,0:T(8,128)(2,1)S(1)}, bf16[272,512]{1,0:T(8,128)(2,1)S(1)}, u32[]{:S(2)}, u32[]{:S(2)}) collective-permute-start(bf16[272,512]{1,0:T(8,128)(2,1)S(1)} %get-tuple-element.97), channel_id=1, source_target_pairs={{0,4},{4,0},{8,12},{12,8},{1,5},{5,1},{9,13},{13,9},{2,6},{6,2},{1... | collective-permute-start | bytes 835592 | tf_op jit(solution)/shard_map/ppermute | solution.py:41
  19.1 17.0 %collective-permute-start.35 = (bf16[272,512]{1,0:T(8,128)(2,1)S(1)}, bf16[272,512]{1,0:T(8,128)(2,1)}, u32[]{:S(2)}, u32[]{:S(2)}) collective-permute-start(bf16[272,512]{1,0:T(8,128)(2,1)S(1)} %get-tuple-element.95), channel_id=1, source_target_pairs={{0,4},{4,0},{8,12},{12,8},{1,5},{5,1},{9,13},{13,9},{2,6},{6,2},{1... | collective-permute-start | bytes 835592 | tf_op jit(solution)/shard_map/ppermute | solution.py:41
  21.4 14.7 %collective-permute-start.37 = (bf16[272,512]{1,0:T(8,128)(2,1)}, bf16[272,512]{1,0:T(8,128)(2,1)}, u32[]{:S(2)}, u32[]{:S(2)}) collective-permute-start(bf16[272,512]{1,0:T(8,128)(2,1)} %add.67), channel_id=1, source_target_pairs={{0,8},{4,12},{8,0},{12,4},{1,9},{5,13},{9,1},{13,5},{2,10},{6,14},... | collective-permute-start | bytes 835592 | tf_op jit(solution)/shard_map/ppermute | solution.py:41
  24.6 13.4 %all-to-all-start.3 = ((bf16[32,8,256]{2,1,0:T(8,128)(2,1)}), bf16[32,8,256]{2,1,0:T(8,128)(2,1)S(1)}, u32[]{:S(2)}, u32[]{:S(2)}) async-start(bf16[32,8,256]{2,1,0:T(8,128)(2,1)} %bitcast.22), calls=%async_computation.3 | async-start | bytes 262144 | tf_op jit(solution)/shard_map/all_to_all | solution.py:31
  30.5 1.9 %collective-permute-start.32 = (s32[1]{0:T(128)}, s32[1]{0:T(128)}, u32[]{:S(2)}, u32[]{:S(2)}) collective-permute-start(s32[1]{0:T(128)} %bitcast.14), channel_id=1, source_target_pairs={{0,4},{4,0},{8,12},{12,8},{1,5},{5,1},{9,13},{13,9},{2,6},{6,2},{1... | collective-permute-start | bytes 20 | tf_op jit(solution)/shard_map/ppermute | solution.py:41
  30.7 3.6 %collective-permute-start.33 = (s32[1]{0:T(128)}, s32[1]{0:T(128)}, u32[]{:S(2)}, u32[]{:S(2)}) collective-permute-start(s32[1]{0:T(128)} %bitcast.14), channel_id=1, source_target_pairs={{0,8},{4,12},{8,0},{12,4},{1,9},{5,13},{9,1},{13,5},{2,10},{6,14},... | collective-permute-start | bytes 20 | tf_op jit(solution)/shard_map/ppermute | solution.py:41
  32.4 3.1 %collective-permute-start.34 = (s32[1]{0:T(128)}, s32[1]{0:T(128)}, u32[]{:S(2)}, u32[]{:S(2)}) collective-permute-start(s32[1]{0:T(128)} %bitcast.14), channel_id=1, source_target_pairs={{0,12},{4,8},{8,4},{12,0},{1,13},{5,9},{9,5},{13,1},{2,14},{6,10},... | collective-permute-start | bytes 20 | tf_op jit(solution)/shard_map/ppermute | solution.py:41
  38.1 25.8 %copy-start.6 = (bf16[272,512]{1,0:T(8,128)(2,1)S(1)}, bf16[272,512]{1,0:T(8,128)(2,1)}, u32[]{:S(2)}) copy-start(bf16[272,512]{1,0:T(8,128)(2,1)} %get-tuple-element.71.refs_3_.refs_0_) | copy-start | bytes 835588 | tf_op jit(solution)/shard_map/cond
  41.9 7.4 %collective-permute-start.16 = (bf16[32,4096]{1,0:T(8,128)(2,1)S(1)}, bf16[32,4096]{1,0:T(8,128)(2,1)S(1)}, u32[]{:S(2)}, u32[]{:S(2)}) collective-permute-start(bf16[32,4096]{1,0:T(8,128)(2,1)S(1)} %get-tuple-element.78), channel_id=1, source_target_pairs={{0,16},{16,0},{1,17},{17,1},{2,18},{18,2},{3,19},{19,3},{4,20},{20... | collective-permute-start | bytes 786440 | tf_op jit(solution)/shard_map/cond/branch_1_fun/ppermute | solution.py:41
  42.7 5.0 %collective-permute-start.17 = (bf16[16,4096]{1,0:T(8,128)(2,1)S(1)}, bf16[16,4096]{1,0:T(8,128)(2,1)S(1)}, u32[]{:S(2)}, u32[]{:S(2)}) collective-permute-start(bf16[16,4096]{1,0:T(8,128)(2,1)S(1)} %get-tuple-element.80), channel_id=1, source_target_pairs={{0,1},{1,0},{2,3},{3,2},{4,5},{5,4},{6,7},{7,6},{8,9},{9,8},{10,11... | collective-permute-start | bytes 393224 | tf_op jit(solution)/shard_map/cond/branch_1_fun/ppermute | solution.py:41
  50.0 5.5 %collective-permute-start.18 = (bf16[16,4096]{1,0:T(8,128)(2,1)S(1)}, bf16[16,4096]{1,0:T(8,128)(2,1)S(1)}, u32[]{:S(2)}, u32[]{:S(2)}) collective-permute-start(bf16[16,4096]{1,0:T(8,128)(2,1)S(1)} %get-tuple-element.82), channel_id=1, source_target_pairs={{0,1},{1,0},{2,3},{3,2},{4,5},{5,4},{6,7},{7,6},{8,9},{9,8},{10,11... | collective-permute-start | bytes 393224 | tf_op jit(solution)/shard_map/cond/branch_1_fun/ppermute | solution.py:41
  51.2 4.3 %collective-permute-start.19 = (bf16[8,4096]{1,0:T(8,128)(2,1)S(1)}, bf16[8,4096]{1,0:T(8,128)(2,1)S(1)}, u32[]{:S(2)}, u32[]{:S(2)}) collective-permute-start(bf16[8,4096]{1,0:T(8,128)(2,1)S(1)} %get-tuple-element.84), channel_id=1, source_target_pairs={{0,16},{16,0},{1,17},{17,1},{2,18},{18,2},{3,19},{19,3},{4,20},{20... | collective-permute-start | bytes 196616 | tf_op jit(solution)/shard_map/cond/branch_1_fun/ppermute | solution.py:41
  56.1 7.8 %collective-permute-start.20 = (bf16[12,4096]{1,0:T(8,128)(2,1)S(1)}, bf16[12,4096]{1,0:T(8,128)(2,1)S(1)}, u32[]{:S(2)}, u32[]{:S(2)}) collective-permute-start(bf16[12,4096]{1,0:T(8,128)(2,1)S(1)} %get-tuple-element.86), channel_id=1, source_target_pairs={{0,2},{1,3},{2,0},{3,1},{4,6},{5,7},{6,4},{7,5},{8,10},{9,11},{10,... | collective-permute-start | bytes 294920 | tf_op jit(solution)/shard_map/cond/branch_1_fun/ppermute | solution.py:41
  65.1 5.4 %collective-permute-start.21 = (bf16[3,4,4224]{2,1,0:T(4,128)(2,1)S(1)}, bf16[3,4,4224]{2,1,0:T(4,128)(2,1)S(1)}, u32[]{:S(2)}, u32[]{:S(2)}) collective-permute-start(bf16[3,4,4224]{2,1,0:T(4,128)(2,1)S(1)} %token_rows.3), channel_id=1, source_target_pairs={{0,1},{1,0},{2,3},{3,2},{4,5},{5,4},{6,7},{7,6},{8,9},{9,8},{10,11... | collective-permute-start | bytes 304136 | tf_op jit(solution)/shard_map/cond/branch_1_fun/ppermute | solution.py:41
  65.2 10.7 %collective-permute-start.22 = (bf16[3,4,4224]{2,1,0:T(4,128)(2,1)S(1)}, bf16[3,4,4224]{2,1,0:T(4,128)(2,1)S(1)}, u32[]{:S(2)}, u32[]{:S(2)}) collective-permute-start(bf16[3,4,4224]{2,1,0:T(4,128)(2,1)S(1)} %token_rows.3), channel_id=1, source_target_pairs={{0,2},{1,3},{2,0},{3,1},{4,6},{5,7},{6,4},{7,5},{8,10},{9,11},{10,... | collective-permute-start | bytes 304136 | tf_op jit(solution)/shard_map/cond/branch_1_fun/ppermute | solution.py:41
  68.4 7.4 %collective-permute-start.23 = (bf16[3,4,4224]{2,1,0:T(4,128)(2,1)S(1)}, bf16[3,4,4224]{2,1,0:T(4,128)(2,1)S(1)}, u32[]{:S(2)}, u32[]{:S(2)}) collective-permute-start(bf16[3,4,4224]{2,1,0:T(4,128)(2,1)S(1)} %token_rows.3), channel_id=1, source_target_pairs={{0,3},{1,2},{2,1},{3,0},{4,7},{5,6},{6,5},{7,4},{8,11},{9,10},{10,... | collective-permute-start | bytes 304136 | tf_op jit(solution)/shard_map/cond/branch_1_fun/ppermute | solution.py:41
  76.0 10.1 %collective-permute-start.27 = (bf16[12,4,4224]{2,1,0:T(4,128)(2,1)S(1)}, bf16[12,4,4224]{2,1,0:T(4,128)(2,1)S(1)}, u32[]{:S(2)}, u32[]{:S(2)}) collective-permute-start(bf16[12,4,4224]{2,1,0:T(4,128)(2,1)S(1)} %bitcast.31), channel_id=1, source_target_pairs={{0,16},{16,0},{1,17},{17,1},{2,18},{18,2},{3,19},{19,3},{4,20},{20... | collective-permute-start | bytes 1216520 | tf_op jit(solution)/shard_map/cond/branch_1_fun/ppermute | solution.py:41
  76.5 18.9 %collective-permute-start.24 = (bf16[12,4,4224]{2,1,0:T(4,128)(2,1)S(1)}, bf16[12,4,4224]{2,1,0:T(4,128)(2,1)S(1)}, u32[]{:S(2)}, u32[]{:S(2)}) collective-permute-start(bf16[12,4,4224]{2,1,0:T(4,128)(2,1)S(1)} %bitcast.32), channel_id=1, source_target_pairs={{0,4},{4,0},{8,12},{12,8},{1,5},{5,1},{9,13},{13,9},{2,6},{6,2},{1... | collective-permute-start | bytes 1216520 | tf_op jit(solution)/shard_map/cond/branch_1_fun/ppermute | solution.py:41
  76.5 11.8 %collective-permute-start.25 = (bf16[12,4,4224]{2,1,0:T(4,128)(2,1)S(1)}, bf16[12,4,4224]{2,1,0:T(4,128)(2,1)S(1)}, u32[]{:S(2)}, u32[]{:S(2)}) collective-permute-start(bf16[12,4,4224]{2,1,0:T(4,128)(2,1)S(1)} %bitcast.33), channel_id=1, source_target_pairs={{0,8},{4,12},{8,0},{12,4},{1,9},{5,13},{9,1},{13,5},{2,10},{6,14},... | collective-permute-start | bytes 1216520 | tf_op jit(solution)/shard_map/cond/branch_1_fun/ppermute | solution.py:41
  76.5 5.7 %copy-start.2 = (bf16[2000,4096]{1,0:T(8,128)(2,1)S(1)}, bf16[2000,4096]{1,0:T(8,128)(2,1)}, u32[]{:S(2)}) copy-start(bf16[2000,4096]{1,0:T(8,128)(2,1)} %get-tuple-element.114.refs_4_.head_ref) | copy-start | bytes 49152004 | tf_op jit(solution)/shard_map/cond
  86.2 7.5 %collective-permute-start.29 = (bf16[6,4,4224]{2,1,0:T(4,128)(2,1)S(1)}, bf16[6,4,4224]{2,1,0:T(4,128)(2,1)S(1)}, u32[]{:S(2)}, u32[]{:S(2)}) collective-permute-start(bf16[6,4,4224]{2,1,0:T(4,128)(2,1)S(1)} %constant_dynamic-slice_fusion.3), channel_id=1, source_target_pairs={{0,8},{4,12},{8,0},{12,4},{1,9},{5,13},{9,1},{13,5},{2,10},{6,14},... | collective-permute-start | bytes 608264 | tf_op jit(solution)/shard_map/cond/branch_1_fun/ppermute | solution.py:41
  88.4 6.9 %collective-permute-start.30 = (bf16[6,4,4224]{2,1,0:T(4,128)(2,1)S(1)}, bf16[6,4,4224]{2,1,0:T(4,128)(2,1)S(1)}, u32[]{:S(2)}, u32[]{:S(2)}) collective-permute-start(bf16[6,4,4224]{2,1,0:T(4,128)(2,1)S(1)} %constant_dynamic-slice_fusion.2), channel_id=1, source_target_pairs={{0,16},{16,0},{1,17},{17,1},{2,18},{18,2},{3,19},{19,3},{4,20},{20... | collective-permute-start | bytes 608264 | tf_op jit(solution)/shard_map/cond/branch_1_fun/ppermute | solution.py:41
  90.0 5.5 %collective-permute-start.26 = (bf16[12,4,4224]{2,1,0:T(4,128)(2,1)S(1)}, bf16[12,4,4224]{2,1,0:T(4,128)(2,1)S(1)}, u32[]{:S(2)}, u32[]{:S(2)}) collective-permute-start(bf16[12,4,4224]{2,1,0:T(4,128)(2,1)S(1)} %collective-permute-done.25.refs_2_), channel_id=1, source_target_pairs={{0,4},{4,0},{8,12},{12,8},{1,5},{5,1},{9,13},{13,9},{2,6},{6,2},{1... | collective-permute-start | bytes 1216520 | tf_op jit(solution)/shard_map/cond/branch_1_fun/ppermute | solution.py:41
  90.0 17.7 %collective-permute-start.28 = (bf16[12,4,4224]{2,1,0:T(4,128)(2,1)S(1)}, bf16[12,4,4224]{2,1,0:T(4,128)(2,1)S(1)}, u32[]{:S(2)}, u32[]{:S(2)}) collective-permute-start(bf16[12,4,4224]{2,1,0:T(4,128)(2,1)S(1)} %collective-permute-done.27.refs_0_), channel_id=1, source_target_pairs={{0,4},{4,0},{8,12},{12,8},{1,5},{5,1},{9,13},{13,9},{2,6},{6,2},{1... | collective-permute-start | bytes 1216520 | tf_op jit(solution)/shard_map/cond/branch_1_fun/ppermute | solution.py:41
  95.4 12.3 %collective-permute-start.31 = (bf16[12,4,4224]{2,1,0:T(4,128)(2,1)S(1)}, bf16[12,4,4224]{2,1,0:T(4,128)(2,1)S(1)}, u32[]{:S(2)}, u32[]{:S(2)}) collective-permute-start(bf16[12,4,4224]{2,1,0:T(4,128)(2,1)S(1)} %constant_dynamic-update-slice_fusion.2.refs_2_), channel_id=1, source_target_pairs={{0,4},{4,0},{8,12},{12,8},{1,5},{5,1},{9,13},{13,9},{2,6},{6,2},{1... | collective-permute-start | bytes 1216520 | tf_op jit(solution)/shard_map/cond/branch_1_fun/ppermute | solution.py:41
  95.5 5.7 %copy-start.3 = (bf16[2000,4096]{1,0:T(8,128)(2,1)S(1)}, bf16[2000,4096]{1,0:T(8,128)(2,1)}, u32[]{:S(2)}) copy-start(bf16[2000,4096]{1,0:T(8,128)(2,1)} %get-tuple-element.114.refs_4_.head_ref) | copy-start | bytes 49152004 | tf_op jit(solution)/shard_map/cond
  127.9 0.6 copy-start.11

commit v16 on v15

--- a/solution.py
+++ b/solution.py
@@ -492,7 +492,8 @@
 
 
 def vocabulary_kernel(tile, count, first_ref, *refs):
-    sets, (head_ref, out_ref, rows_ref, stat) = refs[:count], refs[count:]
+    sets, (head_ref, out_ref, zero_ref, rows_ref, stat) = refs[:count], refs[count:]
+    zero_ref[0] = 0
     vocab_rows, width = head_ref.shape
     share = sets[0].shape[0] * FOLD
     tokens = share * len(sets)
@@ -534,8 +535,11 @@
     return pl.pallas_call(
         functools.partial(vocabulary_kernel, head.shape[0] // 2, count),
         in_specs=[SCALARS] + [INSIDE] * (count + 1),
-        out_specs=INSIDE,
-        out_shape=jax.ShapeDtypeStruct((count, 8, share), jnp.float32),
+        out_specs=[INSIDE, SCALARS],
+        out_shape=[
+            jax.ShapeDtypeStruct((count, 8, share), jnp.float32),
+            jax.ShapeDtypeStruct((1,), jnp.int32),
+        ],
         scratch_shapes=[
             pltpu.VMEM((tokens, width + LANES), jnp.bfloat16),
             pltpu.VMEM((24, tokens), jnp.float32),
@@ -548,21 +552,6 @@
         compiler_params=pltpu.CompilerParams(vmem_limit_bytes=16 << 20),
         name="vocabulary_scores",
     )(place, *sets, pltpu.with_memory_space_constraint(head, pltpu.VMEM))
-
-
-def zero_kernel(after_ref, head_ref, out_ref):
-    out_ref[0] = 0
-
-
-def zero_after(after, head):
-    return pl.pallas_call(
-        zero_kernel,
-        in_specs=[ANYWHERE, INSIDE],
-        out_specs=SCALARS,
-        out_shape=jax.ShapeDtypeStruct((1,), jnp.int32),
-        compiler_params=pltpu.CompilerParams(vmem_limit_bytes=16 << 20),
-        name="vocabulary_rows",
-    )(after, pltpu.with_memory_space_constraint(head, pltpu.VMEM))
 
 
 def spread_kernel(sections, groups, widths, place_ref, slot_ref, *refs):
@@ -690,18 +679,17 @@
     half = own.shape[0] // 2
     by_x = swap(own, "section", 1)
     by_y = swap(own, "tm", 2)
-    zero = zero_after(own, head)
+    first, zero = vocabulary_stats(place, [own, swap(own, "tm", 1)], head)
     across = [
         swap(lax.dynamic_slice_in_dim(by_x, zero[0], half, 0), "tm", 2),
         swap(lax.dynamic_slice_in_dim(by_y, zero[0] + half, half, 0), "section", 1),
     ]
-    stats = [
-        vocabulary_stats(place, [own, swap(own, "tm", 1), by_y, swap(by_y, "tm", 1)], head)
-    ]
+    second, _ = vocabulary_stats(
+        place, [by_y, swap(by_y, "tm", 1), by_x, swap(by_x, "tm", 1)], head
+    )
     across = jnp.concatenate(across)
-    stats.append(
-        vocabulary_stats(place, [by_x, swap(by_x, "tm", 1), across, swap(across, "tm", 1)], head)
-    )
+    third, _ = vocabulary_stats(place, [across, swap(across, "tm", 1)], head)
+    stats = [first, second, third]
 
     every = exchange(
         spread_stats(place, slot_utt, stats, section_count, group_count, width_count), ALL

time: 129 us -> 132 us (1.023)
  Pallas kernels: 35.3 us -> 40.1 us
    pallas_call x2 -> x3, Pallas kernels: 13.1 us -> 18.5 us  [vocabulary_stats(): pl.pallas_call(functools.partial(vocabulary_kernel, head.shape[0] // 2, c...]
  transfers between devices with their start and end apart: 24 -> 24, of which waited for: 14 -> 14; matrix products, arithmetic and copies ran while one was open for 2% -> 2% of each run, Pallas kernels for 11% -> 15%
where the time goes in v16:
time: 132 us; the launch traced here: 131 us
  Pallas kernels  40.1 us (30%)
  starting transfers between devices  30 us (23%)
  waiting for transfers between devices  29.3 us (22%)
  local copies, waits for them, and re-layouts  12.7 us (10%)
  blocking collectives  11.4 us (9%)
  loops' own time  3.36 us (3%)
  between operations  2.62 us (2%)
  other arithmetic  1.6 us (1%)
    ppermute x22, waiting for transfers between devices, swap(): return lax.ppermute(values, axis, pairs)  27.3 us
    ppermute x22, starting transfers between devices, swap(): return lax.ppermute(values, axis, pairs)  18.8 us
    pallas_call x3, Pallas kernels, vocabulary_stats(): pl.pallas_call(functools.partial(vocabulary_kernel, head.shape[0] // 2, c...  18.5 us
    all_to_all x1, blocking collectives, exchange(): return lax.all_to_all(blocks, axis, split_axis=0, concat_axis=0, tiled=True)  11.4 us
    cond x7, local copies, waits for them, and re-layouts  11.4 us
    all_to_all x2, starting transfers between devices, exchange(): return lax.all_to_all(blocks, axis, split_axis=0, concat_axis=0, tiled=True)  11.3 us
    pallas_call x1, Pallas kernels, ffn(): pl.pallas_call(functools.partial(ffn_kernel, tile), in_specs=[SCALARS] +...  6.3 us
    pallas_call x1, Pallas kernels, queries_of(): pl.pallas_call(functools.partial(query_kernel, count, depth), in_specs=[S...  6.13 us
  transfers between devices with their start and end apart: 24, of which 14 were waited for; matrix products, arithmetic and copies ran while one was open for 2% of the time, Pallas kernels for 15%

profile of v16, /device:TPU:0, one launch (start us, length us, event | category | flops | bytes accessed | tf_op | source)
XLA Modules:
  0.0 131.2 jit_solution(13353114430121062540)
XLA Ops:
  0.0 0.1 stack.23.place_ref.after_ref
  0.1 6.3 %encoder_ffn.1 = (bf16[4,32,1280]{2,1,0:T(8,128)(2,1)}, bf16[32,1280]{1,0:T(8,128)(2,1)S(1)}) custom-call(s32[5]{0:T(128)S(1)} %stack.23.place_ref.after_ref, bf16[32,4,1280]{2,1,0:T(4,128)(2,1)} %x_ref.1, bf16[1280,1280]{1,0:T(8,128)(2,1)} %up_ref.1, bf16[1280,1280]{1,0:T(8,128)(2,1)} %down_ref.1), custom_call_target="tpu_custom_call" | custom-call | flops 838860800 | bytes 6553600 | tf_op jit(solution)/shard_map/encoder_ffn/pallas_call | solution.py:121
  6.4 6.3 %all-to-all-start.2 = ((bf16[4,32,1280]{2,1,0:T(8,128)(2,1)}), bf16[4,32,1280]{2,1,0:T(8,128)(2,1)S(1)}, u32[]{:S(2)}, u32[]{:S(2)}) async-start(bf16[4,32,1280]{2,1,0:T(8,128)(2,1)} %get-tuple-element.106), calls=%async_computation.2 | async-start | bytes 655360 | tf_op jit(solution)/shard_map/all_to_all | solution.py:31
  12.7 0.1 reshape.27.tok_ref
  12.8 6.1 %hypothesis_queries.1 = (bf16[272,512]{1,0:T(8,128)(2,1)}, bf16[272,512]{1,0:T(8,128)(2,1)S(1)}, bf16[272,512]{1,0:T(8,128)(2,1)S(1)}, bf16[272,512]{1,0:T(8,128)(2,1)S(1)}) custom-call(s32[5]{0:T(128)S(1)} %stack.23.place_ref.after_ref, s32[8]{0:T(128)S(1)} %copy-done.7, s32[2,8]{1,0:T(2,128)S(1)} %copy-done.8, s32[5]{0:T(128)S(1)} %stack.23.place_ref.after_ref, ...), custom_call_target="tpu_custom_call" | custom-call | flops 1073741824 | bytes 6291456 | tf_op jit(solution)/shard_map/hypothesis_queries/pallas_call | solution.py:228
  19.0 0.1 collective-permute-start.36
  19.1 0.5 collective-permute-start.35
  19.6 1.0 collective-permute-done.36
  20.6 0.8 add.67
  21.4 1.5 %collective-permute-start.37 = (bf16[272,512]{1,0:T(8,128)(2,1)}, bf16[272,512]{1,0:T(8,128)(2,1)}, u32[]{:S(2)}, u32[]{:S(2)}) collective-permute-start(bf16[272,512]{1,0:T(8,128)(2,1)} %add.67), channel_id=1, source_target_pairs={{0,8},{4,12},{8,0},{12,4},{1,9},{5,13},{9,1},{13,5},{2,10},{6,14},... | collective-permute-start | bytes 835592 | tf_op jit(solution)/shard_map/ppermute | solution.py:41
  22.9 0.2 all-to-all-done.2.refs_0_
  23.1 1.5 %frame_keys_values.1 = bf16[256,256]{1,0:T(8,128)(2,1)} custom-call(bf16[4,32,1280]{2,1,0:T(8,128)(2,1)S(1)} %all-to-all-done.2.refs_0_, bf16[32,1280]{1,0:T(8,128)(2,1)S(1)} %get-tuple-element.107.refs_1_, bf16[1280,1024]{1,0:T(8,128)(2,1)S(1)} %copy-done.4, bf16[272,512]{1,0:T(8,128)(2,1)} %get-tuple-element.102.refs_3_), custom_call_target="tpu_custom_call" | custom-call | flops 83886080 | bytes 2621440 | tf_op jit(solution)/shard_map/frame_keys_values/pallas_call | solution.py:287
  24.6 5.0 %all-to-all-start.3 = ((bf16[32,8,256]{2,1,0:T(8,128)(2,1)}), bf16[32,8,256]{2,1,0:T(8,128)(2,1)S(1)}, u32[]{:S(2)}, u32[]{:S(2)}) async-start(bf16[32,8,256]{2,1,0:T(8,128)(2,1)} %bitcast.22), calls=%async_computation.3 | async-start | bytes 262144 | tf_op jit(solution)/shard_map/all_to_all | solution.py:31
  29.6 0.1 reduce_sum.9
  29.7 0.7 fusion
  30.4 0.3 collective-permute-start.32
  30.6 1.7 %collective-permute-start.33 = (s32[1]{0:T(128)}, s32[1]{0:T(128)}, u32[]{:S(2)}, u32[]{:S(2)}) collective-permute-start(s32[1]{0:T(128)} %bitcast.14), channel_id=1, source_target_pairs={{0,8},{4,12},{8,0},{12,4},{1,9},{5,13},{9,1},{13,5},{2,10},{6,14},... | collective-permute-start | bytes 20 | tf_op jit(solution)/shard_map/ppermute | solution.py:41
  33.6 0.8 collective-permute-done.33
  35.1 0.5 collective-permute-done.34
  36.1 1.8 %all-to-all-done.3 = bf16[32,8,256]{2,1,0:T(8,128)(2,1)S(1)} async-done(((bf16[32,8,256]{2,1,0:T(8,128)(2,1)}), bf16[32,8,256]{2,1,0:T(8,128)(2,1)S(1)}, u32[]{:S(2)}, u32[]{:S(2)}) %all-to-all-start.3) | async-done | bytes 131104 | tf_op jit(solution)/shard_map/all_to_all | solution.py:31
  38.0 92.7 %conditional.1 = (f32[2,8]{1,0:T(2,128)S(1)}) conditional(s32[]{:T(128)} %bitcast.15, (s32[5]{0:T(128)S(1)}, s32[8]{0:T(128)S(1)}, s32[4]{0:T(128)S(1)}, bf16[272,512]{1,0:T(8,128)(2,1)}, bf16[272,512]{1,0:T(8,128)(2,1)}, /*index=5*/bf16[272,512]{1,0:T(8,128)(2,1)}, bf16[32,8,256]{2,1,0:T(8,128)(2,1)S(1)}, bf16[512,4096]{1,0:T(8,128)(2,1)}, ...), branch_computations={%region_2.3_spmd, %region_3.4_spmd} | conditional | flops 13186891776 | bytes 166102016 | solution.py:767
  38.0 3.8 %attention_projection.3 = (bf16[32,4096]{1,0:T(8,128)(2,1)S(1)}, bf16[32,4096]{1,0:T(8,128)(2,1)S(1)}, bf16[16,4096]{1,0:T(8,128)(2,1)S(1)}, bf16[16,4096]{1,0:T(8,128)(2,1)S(1)}) custom-call(s32[5]{0:T(128)S(1)} %get-tuple-element.72.refs_0_.place_ref.first_ref, s32[8]{0:T(128)S(1)} %get-tuple-element.73.refs_1_.slot_ref, s32[4]{0:T(128)S(1)} %get-tuple-element.118.refs_2_, ...), custom_call_target="tpu_custom_call" | custom-call | flops 452984832 | bytes 4980736 | tf_op jit(solution)/shard_map/cond/branch_1_fun/attention_projection/pallas_call | solution.py:375
  41.8 0.8 collective-permute-start.16
  42.6 0.6 collective-permute-start.17
  43.2 4.4 %collective-permute-done.17.refs_3_ = bf16[16,4096]{1,0:T(8,128)(2,1)S(1)} collective-permute-done((bf16[16,4096]{1,0:T(8,128)(2,1)S(1)}, bf16[16,4096]{1,0:T(8,128)(2,1)S(1)}, u32[]{:S(2)}, u32[]{:S(2)}) %collective-permute-start.17) | collective-permute-done | bytes 131104 | tf_op jit(solution)/shard_map/cond/branch_1_fun/ppermute | solution.py:41
  47.6 1.6 %collective-permute-done.16.refs_1_ = bf16[32,4096]{1,0:T(8,128)(2,1)S(1)} collective-permute-done((bf16[32,4096]{1,0:T(8,128)(2,1)S(1)}, bf16[32,4096]{1,0:T(8,128)(2,1)S(1)}, u32[]{:S(2)}, u32[]{:S(2)}) %collective-permute-start.16) | collective-permute-done | bytes 262176 | tf_op jit(solution)/shard_map/cond/branch_1_fun/ppermute | solution.py:41
  49.2 0.7 sum_phase.6
  49.9 1.2 collective-permute-start.18
  51.1 1.2 collective-permute-start.19
  52.3 3.1 %collective-permute-done.19.refs_3_ = bf16[8,4096]{1,0:T(8,128)(2,1)S(1)} collective-permute-done((bf16[8,4096]{1,0:T(8,128)(2,1)S(1)}, bf16[8,4096]{1,0:T(8,128)(2,1)S(1)}, u32[]{:S(2)}, u32[]{:S(2)}) %collective-permute-start.19) | collective-permute-done | bytes 65568 | tf_op jit(solution)/shard_map/cond/branch_1_fun/ppermute | solution.py:41
  55.4 0.6 sum_phase.7
  56.0 2.3 %collective-permute-start.20 = (bf16[12,4096]{1,0:T(8,128)(2,1)S(1)}, bf16[12,4096]{1,0:T(8,128)(2,1)S(1)}, u32[]{:S(2)}, u32[]{:S(2)}) collective-permute-start(bf16[12,4096]{1,0:T(8,128)(2,1)S(1)} %get-tuple-element.90), channel_id=1, source_target_pairs={{0,2},{1,3},{2,0},{3,1},{4,6},{5,7},{6,4},{7,5},{8,10},{9,11},{10,... | collective-permute-start | bytes 294920 | tf_op jit(solution)/shard_map/cond/branch_1_fun/ppermute | solution.py:41
  58.3 5.3 %collective-permute-done.20.refs_4_ = bf16[12,4096]{1,0:T(8,128)(2,1)S(1)} collective-permute-done((bf16[12,4096]{1,0:T(8,128)(2,1)S(1)}, bf16[12,4096]{1,0:T(8,128)(2,1)S(1)}, u32[]{:S(2)}, u32[]{:S(2)}) %collective-permute-start.20) | collective-permute-done | bytes 98336 | tf_op jit(solution)/shard_map/cond/branch_1_fun/ppermute | solution.py:41
  63.7 1.3 token_rows.3
  64.9 0.1 collective-permute-start.21
  65.0 2.7 %collective-permute-start.22 = (bf16[3,4,4224]{2,1,0:T(4,128)(2,1)S(1)}, bf16[3,4,4224]{2,1,0:T(4,128)(2,1)S(1)}, u32[]{:S(2)}, u32[]{:S(2)}) collective-permute-start(bf16[3,4,4224]{2,1,0:T(4,128)(2,1)S(1)} %token_rows.3), channel_id=1, source_target_pairs={{0,2},{1,3},{2,0},{3,1},{4,6},{5,7},{6,4},{7,5},{8,10},{9,11},{10,... | collective-permute-start | bytes 304136 | tf_op jit(solution)/shard_map/cond/branch_1_fun/ppermute | solution.py:41
  67.8 1.6 %collective-permute-start.23 = (bf16[3,4,4224]{2,1,0:T(4,128)(2,1)S(1)}, bf16[3,4,4224]{2,1,0:T(4,128)(2,1)S(1)}, u32[]{:S(2)}, u32[]{:S(2)}) collective-permute-start(bf16[3,4,4224]{2,1,0:T(4,128)(2,1)S(1)} %token_rows.3), channel_id=1, source_target_pairs={{0,3},{1,2},{2,1},{3,0},{4,7},{5,6},{6,5},{7,4},{8,11},{9,10},{10,... | collective-permute-start | bytes 304136 | tf_op jit(solution)/shard_map/cond/branch_1_fun/ppermute | solution.py:41
  69.4 0.1 broadcast.7
  69.6 0.3 collective-permute-done.21
  69.9 5.3 %collective-permute-done.22 = bf16[3,4,4224]{2,1,0:T(4,128)(2,1)S(1)} collective-permute-done((bf16[3,4,4224]{2,1,0:T(4,128)(2,1)S(1)}, bf16[3,4,4224]{2,1,0:T(4,128)(2,1)S(1)}, u32[]{:S(2)}, u32[]{:S(2)}) %collective-permute-start.22) | collective-permute-done | bytes 101408 | tf_op jit(solution)/shard_map/cond/branch_1_fun/ppermute | solution.py:41
  75.3 0.1 bitcast_dynamic-update-slice_fusion.4
  75.3 0.1 collective-permute-start.24
  75.4 0.1 collective-permute-start.27
  75.5 0.9 collective-permute-start.25
  76.4 0.8 collective-permute-done.24.refs_1_
  77.1 5.7 %copy-done.2 = bf16[2000,4096]{1,0:T(8,128)(2,1)S(1)} copy-done((bf16[2000,4096]{1,0:T(8,128)(2,1)S(1)}, bf16[2000,4096]{1,0:T(8,128)(2,1)}, u32[]{:S(2)}) %copy-start.2) | copy-done | bytes 16384024 | tf_op jit(solution)/shard_map/cond
  82.8 6.0 %vocabulary_scores.9 = (f32[2,8,48]{2,1,0:T(8,128)S(1)}, s32[1]{0:T(128)}) custom-call(s32[5]{0:T(128)S(1)} %get-tuple-element.72.refs_0_.place_ref.first_ref, bf16[12,4,4224]{2,1,0:T(4,128)(2,1)S(1)} %bitcast.38, bf16[12,4,4224]{2,1,0:T(4,128)(2,1)S(1)} %collective-permute-done.24.refs_1_, bf16[2000,4096]{1,0:T(8,128)(2,1)S(1)} %copy-done.2), custom_call_target="tpu_custom_call" | custom-call | flops 2359296000 | bytes 786432 | tf_op jit(solution)/shard_map/cond/branch_1_fun/vocabulary_scores/pallas_call | solution.py:535
  90.7 0.1 constant_dynamic-slice_fusion.3
  90.8 0.5 collective-permute-start.29
  92.5 0.1 constant_dynamic-slice_fusion.2
  92.6 2.0 %collective-permute-start.30 = (bf16[6,4,4224]{2,1,0:T(4,128)(2,1)S(1)}, bf16[6,4,4224]{2,1,0:T(4,128)(2,1)S(1)}, u32[]{:S(2)}, u32[]{:S(2)}) collective-permute-start(bf16[6,4,4224]{2,1,0:T(4,128)(2,1)S(1)} %constant_dynamic-slice_fusion.2), channel_id=1, source_target_pairs={{0,16},{16,0},{1,17},{17,1},{2,18},{18,2},{3,19},{19,3},{4,20},{20... | collective-permute-start | bytes 608264 | tf_op jit(solution)/shard_map/cond/branch_1_fun/ppermute | solution.py:41
  94.6 0.5 collective-permute-start.28
  95.2 2.7 %collective-permute-done.29 = bf16[6,4,4224]{2,1,0:T(4,128)(2,1)S(1)} collective-permute-done((bf16[6,4,4224]{2,1,0:T(4,128)(2,1)S(1)}, bf16[6,4,4224]{2,1,0:T(4,128)(2,1)S(1)}, u32[]{:S(2)}, u32[]{:S(2)}) %collective-permute-start.29) | collective-permute-done | bytes 202784 | tf_op jit(solution)/shard_map/cond/branch_1_fun/ppermute | solution.py:41
  97.9 0.1 constant_dynamic-update-slice_fusion.3
  98.0 1.5 %collective-permute-done.30 = bf16[6,4,4224]{2,1,0:T(4,128)(2,1)S(1)} collective-permute-done((bf16[6,4,4224]{2,1,0:T(4,128)(2,1)S(1)}, bf16[6,4,4224]{2,1,0:T(4,128)(2,1)S(1)}, u32[]{:S(2)}, u32[]{:S(2)}) %collective-permute-start.30) | collective-permute-done | bytes 202784 | tf_op jit(solution)/shard_map/cond/branch_1_fun/ppermute | solution.py:41
  99.4 0.1 constant_dynamic-update-slice_fusion.2.refs_0_
  99.5 0.1 collective-permute-start.31
  99.7 5.6 %copy-done.3 = bf16[2000,4096]{1,0:T(8,128)(2,1)S(1)} copy-done((bf16[2000,4096]{1,0:T(8,128)(2,1)S(1)}, bf16[2000,4096]{1,0:T(8,128)(2,1)}, u32[]{:S(2)}) %copy-start.3) | copy-done | bytes 16384024 | tf_op jit(solution)/shard_map/cond
  105.3 6.6 %vocabulary_scores.10 = (f32[4,8,48]{2,1,0:T(8,128)S(1)}, s32[1]{0:T(128)}) custom-call(s32[5]{0:T(128)S(1)} %get-tuple-element.72.refs_0_.place_ref.first_ref, bf16[12,4,4224]{2,1,0:T(4,128)(2,1)S(1)} %collective-permute-done.25.refs_0_, bf16[12,4,4224]{2,1,0:T(4,128)(2,1)S(1)} %collective-permute-done.26.refs_1_, ...), custom_call_target="tpu_custom_call" | custom-call | flops 4718592000 | bytes 1572864 | tf_op jit(solution)/shard_map/cond/branch_1_fun/vocabulary_scores/pallas_call | solution.py:535
  111.9 6.0 %vocabulary_scores.11 = (f32[2,8,48]{2,1,0:T(8,128)S(1)}, s32[1]{0:T(128)}) custom-call(s32[5]{0:T(128)S(1)} %get-tuple-element.72.refs_0_.place_ref.first_ref, bf16[12,4,4224]{2,1,0:T(4,128)(2,1)S(1)} %constant_dynamic-update-slice_fusion.2.refs_0_, bf16[12,4,4224]{2,1,0:T(4,128)(2,1)S(1)} %collective-permute-done.31.refs_1_, bf16[2000,4096]{1,0:T(8,128)(2,1)S(1)} %copy-done.3), custom_call_target="tpu_custom_call" | custom-call | flops 2359296000 | bytes 786432 | tf_op jit(solution)/shard_map/cond/branch_1_fun/vocabulary_scores/pallas_call | solution.py:535
  117.8 0.6 statistics_by_group.3
  118.5 11.4 %all_to_all.19.every_ref = f32[32,8,96]{2,1,0:T(8,128)S(1)} all-to-all(f32[32,8,96]{2,1,0:T(8,128)S(1)} %statistics_by_group.3), channel_id=1, replica_groups=mesh['section'=2,'tm'=4,'mp'=4] {'section','tm','mp'}, dimensions={0} | all-to-all | bytes 196608 | tf_op jit(solution)/shard_map/cond/branch_1_fun/all_to_all | solution.py:31
  129.9 0.7 hypothesis_scores.3
  130.7 0.6 copy-done.11
  (30 shorter events, 0.2 us)
Async XLA Ops:
  0.1 12.6 %copy-start.9 = (s32[2,8,16]{2,1,0:T(8,128)S(1)}, s32[2,8,16]{2,1,0:T(8,128)}, u32[]{:S(2)}) copy-start(s32[2,8,16]{2,1,0:T(8,128)} %param.21) | copy-start | bytes 3076
  0.1 12.7 %copy-start.7 = (s32[8]{0:T(128)S(1)}, s32[8]{0:T(128)}, u32[]{:S(2)}) copy-start(s32[8]{0:T(128)} %slot_ref.1) | copy-start | bytes 100
  0.1 12.7 %copy-start.8 = (s32[2,8]{1,0:T(2,128)S(1)}, s32[2,8]{1,0:T(2,128)}, u32[]{:S(2)}) copy-start(s32[2,8]{1,0:T(2,128)} %length_ref.1) | copy-start | bytes 196
  6.4 16.7 %all-to-all-start.2 = ((bf16[4,32,1280]{2,1,0:T(8,128)(2,1)}), bf16[4,32,1280]{2,1,0:T(8,128)(2,1)S(1)}, u32[]{:S(2)}, u32[]{:S(2)}) async-start(bf16[4,32,1280]{2,1,0:T(8,128)(2,1)} %get-tuple-element.106), calls=%async_computation.2 | async-start | bytes 655360 | tf_op jit(solution)/shard_map/all_to_all | solution.py:31
  12.8 10.2 %copy-start.4 = (bf16[1280,1024]{1,0:T(8,128)(2,1)S(1)}, bf16[1280,1024]{1,0:T(8,128)(2,1)}, u32[]{:S(2)}) copy-start(bf16[1280,1024]{1,0:T(8,128)(2,1)} %refs_2_.1) | copy-start | bytes 7864324
  19.0 19.0 %copy-start.10 = (s32[4]{0:T(128)S(1)}, s32[4]{0:T(128)}, u32[]{:S(2)}) copy-start(s32[4]{0:T(128)} %param.14) | copy-start | bytes 52
  19.0 1.6 %collective-permute-start.36 = (bf16[272,512]{1,0:T(8,128)(2,1)S(1)}, bf16[272,512]{1,0:T(8,128)(2,1)S(1)}, u32[]{:S(2)}, u32[]{:S(2)}) collective-permute-start(bf16[272,512]{1,0:T(8,128)(2,1)S(1)} %get-tuple-element.105), channel_id=1, source_target_pairs={{0,4},{4,0},{8,12},{12,8},{1,5},{5,1},{9,13},{13,9},{2,6},{6,2},{1... | collective-permute-start | bytes 835592 | tf_op jit(solution)/shard_map/ppermute | solution.py:41
  19.1 17.0 %collective-permute-start.35 = (bf16[272,512]{1,0:T(8,128)(2,1)S(1)}, bf16[272,512]{1,0:T(8,128)(2,1)}, u32[]{:S(2)}, u32[]{:S(2)}) collective-permute-start(bf16[272,512]{1,0:T(8,128)(2,1)S(1)} %get-tuple-element.103), channel_id=1, source_target_pairs={{0,4},{4,0},{8,12},{12,8},{1,5},{5,1},{9,13},{13,9},{2,6},{6,2},{1... | collective-permute-start | bytes 835592 | tf_op jit(solution)/shard_map/ppermute | solution.py:41
  21.4 14.7 %collective-permute-start.37 = (bf16[272,512]{1,0:T(8,128)(2,1)}, bf16[272,512]{1,0:T(8,128)(2,1)}, u32[]{:S(2)}, u32[]{:S(2)}) collective-permute-start(bf16[272,512]{1,0:T(8,128)(2,1)} %add.67), channel_id=1, source_target_pairs={{0,8},{4,12},{8,0},{12,4},{1,9},{5,13},{9,1},{13,5},{2,10},{6,14},... | collective-permute-start | bytes 835592 | tf_op jit(solution)/shard_map/ppermute | solution.py:41
  24.6 13.4 %all-to-all-start.3 = ((bf16[32,8,256]{2,1,0:T(8,128)(2,1)}), bf16[32,8,256]{2,1,0:T(8,128)(2,1)S(1)}, u32[]{:S(2)}, u32[]{:S(2)}) async-start(bf16[32,8,256]{2,1,0:T(8,128)(2,1)} %bitcast.22), calls=%async_computation.3 | async-start | bytes 262144 | tf_op jit(solution)/shard_map/all_to_all | solution.py:31
  30.4 1.9 %collective-permute-start.32 = (s32[1]{0:T(128)}, s32[1]{0:T(128)}, u32[]{:S(2)}, u32[]{:S(2)}) collective-permute-start(s32[1]{0:T(128)} %bitcast.14), channel_id=1, source_target_pairs={{0,4},{4,0},{8,12},{12,8},{1,5},{5,1},{9,13},{13,9},{2,6},{6,2},{1... | collective-permute-start | bytes 20 | tf_op jit(solution)/shard_map/ppermute | solution.py:41
  30.6 3.8 %collective-permute-start.33 = (s32[1]{0:T(128)}, s32[1]{0:T(128)}, u32[]{:S(2)}, u32[]{:S(2)}) collective-permute-start(s32[1]{0:T(128)} %bitcast.14), channel_id=1, source_target_pairs={{0,8},{4,12},{8,0},{12,4},{1,9},{5,13},{9,1},{13,5},{2,10},{6,14},... | collective-permute-start | bytes 20 | tf_op jit(solution)/shard_map/ppermute | solution.py:41
  32.3 3.2 %collective-permute-start.34 = (s32[1]{0:T(128)}, s32[1]{0:T(128)}, u32[]{:S(2)}, u32[]{:S(2)}) collective-permute-start(s32[1]{0:T(128)} %bitcast.14), channel_id=1, source_target_pairs={{0,12},{4,8},{8,4},{12,0},{1,13},{5,9},{9,5},{13,1},{2,14},{6,10},... | collective-permute-start | bytes 20 | tf_op jit(solution)/shard_map/ppermute | solution.py:41
  38.0 25.7 %copy-start.6 = (bf16[272,512]{1,0:T(8,128)(2,1)S(1)}, bf16[272,512]{1,0:T(8,128)(2,1)}, u32[]{:S(2)}) copy-start(bf16[272,512]{1,0:T(8,128)(2,1)} %get-tuple-element.75.refs_3_.refs_0_) | copy-start | bytes 835588 | tf_op jit(solution)/shard_map/cond
  41.8 7.4 %collective-permute-start.16 = (bf16[32,4096]{1,0:T(8,128)(2,1)S(1)}, bf16[32,4096]{1,0:T(8,128)(2,1)S(1)}, u32[]{:S(2)}, u32[]{:S(2)}) collective-permute-start(bf16[32,4096]{1,0:T(8,128)(2,1)S(1)} %get-tuple-element.82), channel_id=1, source_target_pairs={{0,16},{16,0},{1,17},{17,1},{2,18},{18,2},{3,19},{19,3},{4,20},{20... | collective-permute-start | bytes 786440 | tf_op jit(solution)/shard_map/cond/branch_1_fun/ppermute | solution.py:41
  42.6 5.0 %collective-permute-start.17 = (bf16[16,4096]{1,0:T(8,128)(2,1)S(1)}, bf16[16,4096]{1,0:T(8,128)(2,1)S(1)}, u32[]{:S(2)}, u32[]{:S(2)}) collective-permute-start(bf16[16,4096]{1,0:T(8,128)(2,1)S(1)} %get-tuple-element.84), channel_id=1, source_target_pairs={{0,1},{1,0},{2,3},{3,2},{4,5},{5,4},{6,7},{7,6},{8,9},{9,8},{10,11... | collective-permute-start | bytes 393224 | tf_op jit(solution)/shard_map/cond/branch_1_fun/ppermute | solution.py:41
  49.9 5.5 %collective-permute-start.18 = (bf16[16,4096]{1,0:T(8,128)(2,1)S(1)}, bf16[16,4096]{1,0:T(8,128)(2,1)S(1)}, u32[]{:S(2)}, u32[]{:S(2)}) collective-permute-start(bf16[16,4096]{1,0:T(8,128)(2,1)S(1)} %get-tuple-element.86), channel_id=1, source_target_pairs={{0,1},{1,0},{2,3},{3,2},{4,5},{5,4},{6,7},{7,6},{8,9},{9,8},{10,11... | collective-permute-start | bytes 393224 | tf_op jit(solution)/shard_map/cond/branch_1_fun/ppermute | solution.py:41
  51.1 4.3 %collective-permute-start.19 = (bf16[8,4096]{1,0:T(8,128)(2,1)S(1)}, bf16[8,4096]{1,0:T(8,128)(2,1)S(1)}, u32[]{:S(2)}, u32[]{:S(2)}) collective-permute-start(bf16[8,4096]{1,0:T(8,128)(2,1)S(1)} %get-tuple-element.88), channel_id=1, source_target_pairs={{0,16},{16,0},{1,17},{17,1},{2,18},{18,2},{3,19},{19,3},{4,20},{20... | collective-permute-start | bytes 196616 | tf_op jit(solution)/shard_map/cond/branch_1_fun/ppermute | solution.py:41
  56.0 7.7 %collective-permute-start.20 = (bf16[12,4096]{1,0:T(8,128)(2,1)S(1)}, bf16[12,4096]{1,0:T(8,128)(2,1)S(1)}, u32[]{:S(2)}, u32[]{:S(2)}) collective-permute-start(bf16[12,4096]{1,0:T(8,128)(2,1)S(1)} %get-tuple-element.90), channel_id=1, source_target_pairs={{0,2},{1,3},{2,0},{3,1},{4,6},{5,7},{6,4},{7,5},{8,10},{9,11},{10,... | collective-permute-start | bytes 294920 | tf_op jit(solution)/shard_map/cond/branch_1_fun/ppermute | solution.py:41
  64.9 5.0 %collective-permute-start.21 = (bf16[3,4,4224]{2,1,0:T(4,128)(2,1)S(1)}, bf16[3,4,4224]{2,1,0:T(4,128)(2,1)S(1)}, u32[]{:S(2)}, u32[]{:S(2)}) collective-permute-start(bf16[3,4,4224]{2,1,0:T(4,128)(2,1)S(1)} %token_rows.3), channel_id=1, source_target_pairs={{0,1},{1,0},{2,3},{3,2},{4,5},{5,4},{6,7},{7,6},{8,9},{9,8},{10,11... | collective-permute-start | bytes 304136 | tf_op jit(solution)/shard_map/cond/branch_1_fun/ppermute | solution.py:41
  65.0 10.2 %collective-permute-start.22 = (bf16[3,4,4224]{2,1,0:T(4,128)(2,1)S(1)}, bf16[3,4,4224]{2,1,0:T(4,128)(2,1)S(1)}, u32[]{:S(2)}, u32[]{:S(2)}) collective-permute-start(bf16[3,4,4224]{2,1,0:T(4,128)(2,1)S(1)} %token_rows.3), channel_id=1, source_target_pairs={{0,2},{1,3},{2,0},{3,1},{4,6},{5,7},{6,4},{7,5},{8,10},{9,11},{10,... | collective-permute-start | bytes 304136 | tf_op jit(solution)/shard_map/cond/branch_1_fun/ppermute | solution.py:41
  67.8 7.5 %collective-permute-start.23 = (bf16[3,4,4224]{2,1,0:T(4,128)(2,1)S(1)}, bf16[3,4,4224]{2,1,0:T(4,128)(2,1)S(1)}, u32[]{:S(2)}, u32[]{:S(2)}) collective-permute-start(bf16[3,4,4224]{2,1,0:T(4,128)(2,1)S(1)} %token_rows.3), channel_id=1, source_target_pairs={{0,3},{1,2},{2,1},{3,0},{4,7},{5,6},{6,5},{7,4},{8,11},{9,10},{10,... | collective-permute-start | bytes 304136 | tf_op jit(solution)/shard_map/cond/branch_1_fun/ppermute | solution.py:41
  75.3 1.8 %collective-permute-start.24 = (bf16[12,4,4224]{2,1,0:T(4,128)(2,1)S(1)}, bf16[12,4,4224]{2,1,0:T(4,128)(2,1)S(1)}, u32[]{:S(2)}, u32[]{:S(2)}) collective-permute-start(bf16[12,4,4224]{2,1,0:T(4,128)(2,1)S(1)} %bitcast.35), channel_id=1, source_target_pairs={{0,4},{4,0},{8,12},{12,8},{1,5},{5,1},{9,13},{13,9},{2,6},{6,2},{1... | collective-permute-start | bytes 1216520 | tf_op jit(solution)/shard_map/cond/branch_1_fun/ppermute | solution.py:41
  75.4 15.3 %collective-permute-start.27 = (bf16[12,4,4224]{2,1,0:T(4,128)(2,1)S(1)}, bf16[12,4,4224]{2,1,0:T(4,128)(2,1)S(1)}, u32[]{:S(2)}, u32[]{:S(2)}) collective-permute-start(bf16[12,4,4224]{2,1,0:T(4,128)(2,1)S(1)} %bitcast.36), channel_id=1, source_target_pairs={{0,16},{16,0},{1,17},{17,1},{2,18},{18,2},{3,19},{19,3},{4,20},{20... | collective-permute-start | bytes 1216520 | tf_op jit(solution)/shard_map/cond/branch_1_fun/ppermute | solution.py:41
  75.5 17.1 %collective-permute-start.25 = (bf16[12,4,4224]{2,1,0:T(4,128)(2,1)S(1)}, bf16[12,4,4224]{2,1,0:T(4,128)(2,1)S(1)}, u32[]{:S(2)}, u32[]{:S(2)}) collective-permute-start(bf16[12,4,4224]{2,1,0:T(4,128)(2,1)S(1)} %bitcast.37), channel_id=1, source_target_pairs={{0,8},{4,12},{8,0},{12,4},{1,9},{5,13},{9,1},{13,5},{2,10},{6,14},... | collective-permute-start | bytes 1216520 | tf_op jit(solution)/shard_map/cond/branch_1_fun/ppermute | solution.py:41
  77.1 5.7 %copy-start.2 = (bf16[2000,4096]{1,0:T(8,128)(2,1)S(1)}, bf16[2000,4096]{1,0:T(8,128)(2,1)}, u32[]{:S(2)}) copy-start(bf16[2000,4096]{1,0:T(8,128)(2,1)} %get-tuple-element.122.refs_2_.refs_4_) | copy-start | bytes 49152004 | tf_op jit(solution)/shard_map/cond
  90.8 7.1 %collective-permute-start.29 = (bf16[6,4,4224]{2,1,0:T(4,128)(2,1)S(1)}, bf16[6,4,4224]{2,1,0:T(4,128)(2,1)S(1)}, u32[]{:S(2)}, u32[]{:S(2)}) collective-permute-start(bf16[6,4,4224]{2,1,0:T(4,128)(2,1)S(1)} %constant_dynamic-slice_fusion.3), channel_id=1, source_target_pairs={{0,8},{4,12},{8,0},{12,4},{1,9},{5,13},{9,1},{13,5},{2,10},{6,14},... | collective-permute-start | bytes 608264 | tf_op jit(solution)/shard_map/cond/branch_1_fun/ppermute | solution.py:41
  92.6 6.8 %collective-permute-start.30 = (bf16[6,4,4224]{2,1,0:T(4,128)(2,1)S(1)}, bf16[6,4,4224]{2,1,0:T(4,128)(2,1)S(1)}, u32[]{:S(2)}, u32[]{:S(2)}) collective-permute-start(bf16[6,4,4224]{2,1,0:T(4,128)(2,1)S(1)} %constant_dynamic-slice_fusion.2), channel_id=1, source_target_pairs={{0,16},{16,0},{1,17},{17,1},{2,18},{18,2},{3,19},{19,3},{4,20},{20... | collective-permute-start | bytes 608264 | tf_op jit(solution)/shard_map/cond/branch_1_fun/ppermute | solution.py:41
  94.6 5.0 %collective-permute-start.26 = (bf16[12,4,4224]{2,1,0:T(4,128)(2,1)S(1)}, bf16[12,4,4224]{2,1,0:T(4,128)(2,1)S(1)}, u32[]{:S(2)}, u32[]{:S(2)}) collective-permute-start(bf16[12,4,4224]{2,1,0:T(4,128)(2,1)S(1)} %collective-permute-done.25.refs_0_), channel_id=1, source_target_pairs={{0,4},{4,0},{8,12},{12,8},{1,5},{5,1},{9,13},{13,9},{2,6},{6,2},{1... | collective-permute-start | bytes 1216520 | tf_op jit(solution)/shard_map/cond/branch_1_fun/ppermute | solution.py:41
  94.6 5.0 %collective-permute-start.28 = (bf16[12,4,4224]{2,1,0:T(4,128)(2,1)S(1)}, bf16[12,4,4224]{2,1,0:T(4,128)(2,1)S(1)}, u32[]{:S(2)}, u32[]{:S(2)}) collective-permute-start(bf16[12,4,4224]{2,1,0:T(4,128)(2,1)S(1)} %collective-permute-done.27.refs_2_), channel_id=1, source_target_pairs={{0,4},{4,0},{8,12},{12,8},{1,5},{5,1},{9,13},{13,9},{2,6},{6,2},{1... | collective-permute-start | bytes 1216520 | tf_op jit(solution)/shard_map/cond/branch_1_fun/ppermute | solution.py:41
  99.5 12.3 %collective-permute-start.31 = (bf16[12,4,4224]{2,1,0:T(4,128)(2,1)S(1)}, bf16[12,4,4224]{2,1,0:T(4,128)(2,1)S(1)}, u32[]{:S(2)}, u32[]{:S(2)}) collective-permute-start(bf16[12,4,4224]{2,1,0:T(4,128)(2,1)S(1)} %constant_dynamic-update-slice_fusion.2.refs_0_), channel_id=1, source_target_pairs={{0,4},{4,0},{8,12},{12,8},{1,5},{5,1},{9,13},{13,9},{2,6},{6,2},{1... | collective-permute-start | bytes 1216520 | tf_op jit(solution)/shard_map/cond/branch_1_fun/ppermute | solution.py:41
  99.6 5.7 %copy-start.3 = (bf16[2000,4096]{1,0:T(8,128)(2,1)S(1)}, bf16[2000,4096]{1,0:T(8,128)(2,1)}, u32[]{:S(2)}) copy-start(bf16[2000,4096]{1,0:T(8,128)(2,1)} %get-tuple-element.122.refs_2_.refs_4_) | copy-start | bytes 49152004 | tf_op jit(solution)/shard_map/cond
  130.6 0.6 copy-start.11

commit v17 on v16

--- a/solution.py
+++ b/solution.py
@@ -492,8 +492,7 @@
 
 
 def vocabulary_kernel(tile, count, first_ref, *refs):
-    sets, (head_ref, out_ref, zero_ref, rows_ref, stat) = refs[:count], refs[count:]
-    zero_ref[0] = 0
+    sets, (head_ref, out_ref, rows_ref, stat) = refs[:count], refs[count:]
     vocab_rows, width = head_ref.shape
     share = sets[0].shape[0] * FOLD
     tokens = share * len(sets)
@@ -535,11 +534,8 @@
     return pl.pallas_call(
         functools.partial(vocabulary_kernel, head.shape[0] // 2, count),
         in_specs=[SCALARS] + [INSIDE] * (count + 1),
-        out_specs=[INSIDE, SCALARS],
-        out_shape=[
-            jax.ShapeDtypeStruct((count, 8, share), jnp.float32),
-            jax.ShapeDtypeStruct((1,), jnp.int32),
-        ],
+        out_specs=INSIDE,
+        out_shape=jax.ShapeDtypeStruct((count, 8, share), jnp.float32),
         scratch_shapes=[
             pltpu.VMEM((tokens, width + LANES), jnp.bfloat16),
             pltpu.VMEM((24, tokens), jnp.float32),
@@ -679,17 +675,15 @@
     half = own.shape[0] // 2
     by_x = swap(own, "section", 1)
     by_y = swap(own, "tm", 2)
-    first, zero = vocabulary_stats(place, [own, swap(own, "tm", 1)], head)
-    across = [
-        swap(lax.dynamic_slice_in_dim(by_x, zero[0], half, 0), "tm", 2),
-        swap(lax.dynamic_slice_in_dim(by_y, zero[0] + half, half, 0), "section", 1),
-    ]
-    second, _ = vocabulary_stats(
-        place, [by_y, swap(by_y, "tm", 1), by_x, swap(by_x, "tm", 1)], head
-    )
+    stats = [vocabulary_stats(place, [own, swap(own, "tm", 1)], head)]
+    by_x, by_y, stats[0] = lax.optimization_barrier((by_x, by_y, stats[0]))
+    across = [swap(by_x[:half], "tm", 2), swap(by_y[half:], "section", 1)]
+    stats.append(
+        vocabulary_stats(place, [by_y, swap(by_y, "tm", 1), by_x, swap(by_x, "tm", 1)], head)
+    )
+    *across, stats[1] = lax.optimization_barrier((*across, stats[1]))
     across = jnp.concatenate(across)
-    third, _ = vocabulary_stats(place, [across, swap(across, "tm", 1)], head)
-    stats = [first, second, third]
+    stats.append(vocabulary_stats(place, [across, swap(across, "tm", 1)], head))
 
     every = exchange(
         spread_stats(place, slot_utt, stats, section_count, group_count, width_count), ALL

time: 132 us -> 120 us (0.909)
  local copies, waits for them, and re-layouts: 12.7 us -> 7.04 us
  loops' own time: 3.36 us -> 0.13 us
  waiting for transfers between devices: 29.3 us -> 26.7 us
    cond x7 -> x5, local copies, waits for them, and re-layouts: 11.4 us -> 5.73 us
    another operation x1, loops' own time: 3.36 us -> 0.13 us  [near_device(): lax.cond(most[0] <= few * head_devices, functools.partial(rest, (few - fe...]
    ppermute x22, waiting for transfers between devices: 27.3 us -> 24.8 us  [swap(): return lax.ppermute(values, axis, pairs)]
  transfers between devices with their start and end apart: 24 -> 24, of which waited for: 14 -> 13; matrix products, arithmetic and copies ran while one was open for 2% -> 2% of each run, Pallas kernels for 15% -> 17%
where the time goes in v17:
time: 120 us; the launch traced here: 119 us
  Pallas kernels  40.1 us (33%)
  starting transfers between devices  30.1 us (25%)
  waiting for transfers between devices  26.7 us (22%)
  blocking collectives  10.7 us (9%)
  local copies, waits for them, and re-layouts  7.04 us (6%)
  between operations  2.65 us (2%)
  other arithmetic  1.63 us (1%)
    ppermute x22, waiting for transfers between devices, swap(): return lax.ppermute(values, axis, pairs)  24.8 us
    ppermute x22, starting transfers between devices, swap(): return lax.ppermute(values, axis, pairs)  18.8 us
    pallas_call x3, Pallas kernels, vocabulary_stats(): pl.pallas_call(functools.partial(vocabulary_kernel, head.shape[0] // 2, c...  18.4 us
    all_to_all x2, starting transfers between devices, exchange(): return lax.all_to_all(blocks, axis, split_axis=0, concat_axis=0, tiled=True)  11.3 us
    all_to_all x1, blocking collectives, exchange(): return lax.all_to_all(blocks, axis, split_axis=0, concat_axis=0, tiled=True)  10.7 us
    pallas_call x1, Pallas kernels, ffn(): pl.pallas_call(functools.partial(ffn_kernel, tile), in_specs=[SCALARS] +...  6.31 us
    pallas_call x1, Pallas kernels, queries_of(): pl.pallas_call(functools.partial(query_kernel, count, depth), in_specs=[S...  6.14 us
    cond x5, local copies, waits for them, and re-layouts  5.73 us
  transfers between devices with their start and end apart: 24, of which 13 were waited for; matrix products, arithmetic and copies ran while one was open for 2% of the time, Pallas kernels for 17%

profile of v17, /device:TPU:0, one launch (start us, length us, event | category | flops | bytes accessed | tf_op | source)
XLA Modules:
  0.0 119.1 jit_solution(14888895728323234645)
XLA Ops:
  0.0 0.1 stack.23.place_ref.after_ref
  0.1 6.3 %encoder_ffn.1 = (bf16[4,32,1280]{2,1,0:T(8,128)(2,1)}, bf16[32,1280]{1,0:T(8,128)(2,1)S(1)}) custom-call(s32[5]{0:T(128)S(1)} %stack.23.place_ref.after_ref, bf16[32,4,1280]{2,1,0:T(4,128)(2,1)} %x_ref.1, bf16[1280,1280]{1,0:T(8,128)(2,1)} %up_ref.1, bf16[1280,1280]{1,0:T(8,128)(2,1)} %down_ref.1), custom_call_target="tpu_custom_call" | custom-call | flops 838860800 | bytes 6553600 | tf_op jit(solution)/shard_map/encoder_ffn/pallas_call | solution.py:121
  6.4 6.3 %all-to-all-start.2 = ((bf16[4,32,1280]{2,1,0:T(8,128)(2,1)}), bf16[4,32,1280]{2,1,0:T(8,128)(2,1)S(1)}, u32[]{:S(2)}, u32[]{:S(2)}) async-start(bf16[4,32,1280]{2,1,0:T(8,128)(2,1)} %get-tuple-element.110), calls=%async_computation.2 | async-start | bytes 655360 | tf_op jit(solution)/shard_map/all_to_all | solution.py:31
  12.7 0.1 reshape.27.tok_ref
  12.8 6.1 %hypothesis_queries.1 = (bf16[272,512]{1,0:T(8,128)(2,1)}, bf16[272,512]{1,0:T(8,128)(2,1)S(1)}, bf16[272,512]{1,0:T(8,128)(2,1)S(1)}, bf16[272,512]{1,0:T(8,128)(2,1)S(1)}) custom-call(s32[5]{0:T(128)S(1)} %stack.23.place_ref.after_ref, s32[8]{0:T(128)S(1)} %copy-done.5, s32[2,8]{1,0:T(2,128)S(1)} %copy-done.6, s32[5]{0:T(128)S(1)} %stack.23.place_ref.after_ref, ...), custom_call_target="tpu_custom_call" | custom-call | flops 1073741824 | bytes 6291456 | tf_op jit(solution)/shard_map/hypothesis_queries/pallas_call | solution.py:228
  19.0 0.1 collective-permute-start.36
  19.1 0.5 collective-permute-start.35
  19.6 1.0 collective-permute-done.36
  20.6 0.8 add.45
  21.4 1.5 %collective-permute-start.37 = (bf16[272,512]{1,0:T(8,128)(2,1)}, bf16[272,512]{1,0:T(8,128)(2,1)}, u32[]{:S(2)}, u32[]{:S(2)}) collective-permute-start(bf16[272,512]{1,0:T(8,128)(2,1)} %add.45), channel_id=1, source_target_pairs={{0,8},{4,12},{8,0},{12,4},{1,9},{5,13},{9,1},{13,5},{2,10},{6,14},... | collective-permute-start | bytes 835592 | tf_op jit(solution)/shard_map/ppermute | solution.py:41
  23.0 0.1 all-to-all-done.2.refs_0_
  23.1 1.5 %frame_keys_values.1 = bf16[256,256]{1,0:T(8,128)(2,1)} custom-call(bf16[4,32,1280]{2,1,0:T(8,128)(2,1)S(1)} %all-to-all-done.2.refs_0_, bf16[32,1280]{1,0:T(8,128)(2,1)S(1)} %get-tuple-element.111.refs_1_, bf16[1280,1024]{1,0:T(8,128)(2,1)S(1)} %copy-done.2, bf16[272,512]{1,0:T(8,128)(2,1)} %get-tuple-element.106.refs_3_), custom_call_target="tpu_custom_call" | custom-call | flops 83886080 | bytes 2621440 | tf_op jit(solution)/shard_map/frame_keys_values/pallas_call | solution.py:287
  24.6 5.0 %all-to-all-start.3 = ((bf16[32,8,256]{2,1,0:T(8,128)(2,1)}), bf16[32,8,256]{2,1,0:T(8,128)(2,1)S(1)}, u32[]{:S(2)}, u32[]{:S(2)}) async-start(bf16[32,8,256]{2,1,0:T(8,128)(2,1)} %bitcast.20), calls=%async_computation.3 | async-start | bytes 262144 | tf_op jit(solution)/shard_map/all_to_all | solution.py:31
  29.6 0.1 reduce_sum.9
  29.8 0.7 fusion
  30.5 0.3 collective-permute-start.32
  30.7 1.7 %collective-permute-start.33 = (s32[1]{0:T(128)}, s32[1]{0:T(128)}, u32[]{:S(2)}, u32[]{:S(2)}) collective-permute-start(s32[1]{0:T(128)} %bitcast.12), channel_id=1, source_target_pairs={{0,8},{4,12},{8,0},{12,4},{1,9},{5,13},{9,1},{13,5},{2,10},{6,14},... | collective-permute-start | bytes 20 | tf_op jit(solution)/shard_map/ppermute | solution.py:41
  33.8 0.6 collective-permute-done.33
  35.0 0.6 collective-permute-done.34
  36.2 1.8 %all-to-all-done.3 = bf16[32,8,256]{2,1,0:T(8,128)(2,1)S(1)} async-done(((bf16[32,8,256]{2,1,0:T(8,128)(2,1)}), bf16[32,8,256]{2,1,0:T(8,128)(2,1)S(1)}, u32[]{:S(2)}, u32[]{:S(2)}) %all-to-all-start.3) | async-done | bytes 131104 | tf_op jit(solution)/shard_map/all_to_all | solution.py:31
  38.0 80.5 %conditional.1 = (f32[2,8]{1,0:T(2,128)S(1)}) conditional(s32[]{:T(128)} %bitcast.13, (s32[5]{0:T(128)S(1)}, s32[8]{0:T(128)S(1)}, s32[4]{0:T(128)S(1)}, bf16[272,512]{1,0:T(8,128)(2,1)}, bf16[272,512]{1,0:T(8,128)(2,1)}, /*index=5*/bf16[272,512]{1,0:T(8,128)(2,1)}, bf16[32,8,256]{2,1,0:T(8,128)(2,1)S(1)}, bf16[512,4096]{1,0:T(8,128)(2,1)}, ...), branch_computations={%region_2.3_spmd, %region_3.4_spmd} | conditional | flops 13186891776 | bytes 100565904 | solution.py:761
  38.0 3.8 %attention_projection.3 = (bf16[32,4096]{1,0:T(8,128)(2,1)S(1)}, bf16[32,4096]{1,0:T(8,128)(2,1)S(1)}, bf16[16,4096]{1,0:T(8,128)(2,1)S(1)}, bf16[16,4096]{1,0:T(8,128)(2,1)S(1)}) custom-call(s32[5]{0:T(128)S(1)} %get-tuple-element.74.refs_0_.place_ref.first_ref, s32[8]{0:T(128)S(1)} %get-tuple-element.75.refs_1_.slot_ref, s32[4]{0:T(128)S(1)} %get-tuple-element.122.refs_2_, ...), custom_call_target="tpu_custom_call" | custom-call | flops 452984832 | bytes 4980736 | tf_op jit(solution)/shard_map/cond/branch_1_fun/attention_projection/pallas_call | solution.py:375
  41.9 0.8 collective-permute-start.16
  42.7 0.6 collective-permute-start.17
  43.3 4.4 %collective-permute-done.17.refs_3_ = bf16[16,4096]{1,0:T(8,128)(2,1)S(1)} collective-permute-done((bf16[16,4096]{1,0:T(8,128)(2,1)S(1)}, bf16[16,4096]{1,0:T(8,128)(2,1)S(1)}, u32[]{:S(2)}, u32[]{:S(2)}) %collective-permute-start.17) | collective-permute-done | bytes 131104 | tf_op jit(solution)/shard_map/cond/branch_1_fun/ppermute | solution.py:41
  47.7 1.6 %collective-permute-done.16.refs_1_ = bf16[32,4096]{1,0:T(8,128)(2,1)S(1)} collective-permute-done((bf16[32,4096]{1,0:T(8,128)(2,1)S(1)}, bf16[32,4096]{1,0:T(8,128)(2,1)S(1)}, u32[]{:S(2)}, u32[]{:S(2)}) %collective-permute-start.16) | collective-permute-done | bytes 262176 | tf_op jit(solution)/shard_map/cond/branch_1_fun/ppermute | solution.py:41
  49.3 0.7 sum_phase.6
  50.0 1.2 %collective-permute-start.18 = (bf16[16,4096]{1,0:T(8,128)(2,1)S(1)}, bf16[16,4096]{1,0:T(8,128)(2,1)S(1)}, u32[]{:S(2)}, u32[]{:S(2)}) collective-permute-start(bf16[16,4096]{1,0:T(8,128)(2,1)S(1)} %get-tuple-element.88), channel_id=1, source_target_pairs={{0,1},{1,0},{2,3},{3,2},{4,5},{5,4},{6,7},{7,6},{8,9},{9,8},{10,11... | collective-permute-start | bytes 393224 | tf_op jit(solution)/shard_map/cond/branch_1_fun/ppermute | solution.py:41
  51.2 1.2 %collective-permute-start.19 = (bf16[8,4096]{1,0:T(8,128)(2,1)S(1)}, bf16[8,4096]{1,0:T(8,128)(2,1)S(1)}, u32[]{:S(2)}, u32[]{:S(2)}) collective-permute-start(bf16[8,4096]{1,0:T(8,128)(2,1)S(1)} %get-tuple-element.90), channel_id=1, source_target_pairs={{0,16},{16,0},{1,17},{17,1},{2,18},{18,2},{3,19},{19,3},{4,20},{20... | collective-permute-start | bytes 196616 | tf_op jit(solution)/shard_map/cond/branch_1_fun/ppermute | solution.py:41
  52.4 3.1 %collective-permute-done.19.refs_3_ = bf16[8,4096]{1,0:T(8,128)(2,1)S(1)} collective-permute-done((bf16[8,4096]{1,0:T(8,128)(2,1)S(1)}, bf16[8,4096]{1,0:T(8,128)(2,1)S(1)}, u32[]{:S(2)}, u32[]{:S(2)}) %collective-permute-start.19) | collective-permute-done | bytes 65568 | tf_op jit(solution)/shard_map/cond/branch_1_fun/ppermute | solution.py:41
  55.5 0.6 sum_phase.7
  56.1 2.3 %collective-permute-start.20 = (bf16[12,4096]{1,0:T(8,128)(2,1)S(1)}, bf16[12,4096]{1,0:T(8,128)(2,1)S(1)}, u32[]{:S(2)}, u32[]{:S(2)}) collective-permute-start(bf16[12,4096]{1,0:T(8,128)(2,1)S(1)} %get-tuple-element.92), channel_id=1, source_target_pairs={{0,2},{1,3},{2,0},{3,1},{4,6},{5,7},{6,4},{7,5},{8,10},{9,11},{10,... | collective-permute-start | bytes 294920 | tf_op jit(solution)/shard_map/cond/branch_1_fun/ppermute | solution.py:41
  58.4 5.3 %collective-permute-done.20.refs_4_ = bf16[12,4096]{1,0:T(8,128)(2,1)S(1)} collective-permute-done((bf16[12,4096]{1,0:T(8,128)(2,1)S(1)}, bf16[12,4096]{1,0:T(8,128)(2,1)S(1)}, u32[]{:S(2)}, u32[]{:S(2)}) %collective-permute-start.20) | collective-permute-done | bytes 98336 | tf_op jit(solution)/shard_map/cond/branch_1_fun/ppermute | solution.py:41
  63.7 1.3 %token_rows.3 = bf16[3,4,4224]{2,1,0:T(4,128)(2,1)S(1)} custom-call(s32[5]{0:T(128)S(1)} %get-tuple-element.74.refs_0_.place_ref.first_ref, s32[8]{0:T(128)S(1)} %get-tuple-element.75.refs_1_.slot_ref, bf16[272,512]{1,0:T(8,128)(2,1)S(1)} %copy-done.4, bf16[272,512]{1,0:T(8,128)(2,1)} %get-tuple-element.78.refs_4_.refs_1_, ...), custom_call_target="tpu_custom_call" | custom-call | tf_op jit(solution)/shard_map/cond/branch_1_fun/token_rows/pallas_call | solution.py:480
  65.0 0.1 collective-permute-start.21
  65.1 2.7 %collective-permute-start.22 = (bf16[3,4,4224]{2,1,0:T(4,128)(2,1)S(1)}, bf16[3,4,4224]{2,1,0:T(4,128)(2,1)S(1)}, u32[]{:S(2)}, u32[]{:S(2)}) collective-permute-start(bf16[3,4,4224]{2,1,0:T(4,128)(2,1)S(1)} %token_rows.3), channel_id=1, source_target_pairs={{0,2},{1,3},{2,0},{3,1},{4,6},{5,7},{6,4},{7,5},{8,10},{9,11},{10,... | collective-permute-start | bytes 304136 | tf_op jit(solution)/shard_map/cond/branch_1_fun/ppermute | solution.py:41
  67.8 1.6 %collective-permute-start.23 = (bf16[3,4,4224]{2,1,0:T(4,128)(2,1)S(1)}, bf16[3,4,4224]{2,1,0:T(4,128)(2,1)S(1)}, u32[]{:S(2)}, u32[]{:S(2)}) collective-permute-start(bf16[3,4,4224]{2,1,0:T(4,128)(2,1)S(1)} %token_rows.3), channel_id=1, source_target_pairs={{0,3},{1,2},{2,1},{3,0},{4,7},{5,6},{6,5},{7,4},{8,11},{9,10},{10,... | collective-permute-start | bytes 304136 | tf_op jit(solution)/shard_map/cond/branch_1_fun/ppermute | solution.py:41
  69.5 0.1 broadcast.7
  69.6 0.1 bitcast_dynamic-update-slice_fusion.7
  69.6 0.3 collective-permute-done.21
  70.0 5.3 %collective-permute-done.22 = bf16[3,4,4224]{2,1,0:T(4,128)(2,1)S(1)} collective-permute-done((bf16[3,4,4224]{2,1,0:T(4,128)(2,1)S(1)}, bf16[3,4,4224]{2,1,0:T(4,128)(2,1)S(1)}, u32[]{:S(2)}, u32[]{:S(2)}) %collective-permute-start.22) | collective-permute-done | bytes 101408 | tf_op jit(solution)/shard_map/cond/branch_1_fun/ppermute | solution.py:41
  75.3 0.1 bitcast_dynamic-update-slice_fusion.4
  75.4 0.1 collective-permute-start.26
  75.5 0.1 collective-permute-start.24
  75.6 0.9 collective-permute-start.25
  76.5 0.7 collective-permute-done.26.refs_1_
  77.2 5.7 %copy-done.1 = bf16[2000,4096]{1,0:T(8,128)(2,1)S(1)} copy-done((bf16[2000,4096]{1,0:T(8,128)(2,1)S(1)}, bf16[2000,4096]{1,0:T(8,128)(2,1)}, u32[]{:S(2)}) %copy-start.1) | copy-done | bytes 16384024 | tf_op jit(solution)/shard_map/cond
  82.9 5.9 %vocabulary_scores.9.refs_0_ = f32[2,8,48]{2,1,0:T(8,128)S(1)} custom-call(s32[5]{0:T(128)S(1)} %get-tuple-element.74.refs_0_.place_ref.first_ref, bf16[12,4,4224]{2,1,0:T(4,128)(2,1)S(1)} %bitcast.36, bf16[12,4,4224]{2,1,0:T(4,128)(2,1)S(1)} %collective-permute-done.26.refs_1_, bf16[2000,4096]{1,0:T(8,128)(2,1)S(1)} %copy-done.1), custom_call_target="tpu_custom_call" | custom-call | flops 2359296000 | bytes 786432 | tf_op jit(solution)/shard_map/cond/branch_1_fun/vocabulary_scores/pallas_call | solution.py:534
  88.8 0.2 collective-permute-start.29
  89.0 0.4 collective-permute-start.30
  89.4 0.1 slice.10
  89.4 0.1 slice.11
  89.5 0.5 collective-permute-start.27
  90.0 2.0 %collective-permute-start.28 = (bf16[6,4,4224]{2,1,0:T(4,128)(2,1)S(1)}, bf16[6,4,4224]{2,1,0:T(4,128)(2,1)S(1)}, u32[]{:S(2)}, u32[]{:S(2)}) collective-permute-start(bf16[6,4,4224]{2,1,0:T(4,128)(2,1)S(1)} %slice.11), channel_id=1, source_target_pairs={{0,16},{16,0},{1,17},{17,1},{2,18},{18,2},{3,19},{19,3},{4,20},{20... | collective-permute-start | bytes 608264 | tf_op jit(solution)/shard_map/cond/branch_1_fun/ppermute | solution.py:41
  92.0 6.5 %vocabulary_scores.10.refs_1_ = f32[4,8,48]{2,1,0:T(8,128)S(1)} custom-call(s32[5]{0:T(128)S(1)} %get-tuple-element.74.refs_0_.place_ref.first_ref, bf16[12,4,4224]{2,1,0:T(4,128)(2,1)S(1)} %collective-permute-done.25.refs_0_, bf16[12,4,4224]{2,1,0:T(4,128)(2,1)S(1)} %collective-permute-done.29.refs_1_, ...), custom_call_target="tpu_custom_call" | custom-call | flops 4718592000 | bytes 1572864 | tf_op jit(solution)/shard_map/cond/branch_1_fun/vocabulary_scores/pallas_call | solution.py:534
  98.6 0.1 constant_dynamic-update-slice_fusion.3
  98.6 0.1 constant_dynamic-update-slice_fusion.2.refs_0_
  98.7 0.1 collective-permute-start.31
  98.8 1.7 %collective-permute-done.31.refs_1_ = bf16[12,4,4224]{2,1,0:T(4,128)(2,1)S(1)} collective-permute-done((bf16[12,4,4224]{2,1,0:T(4,128)(2,1)S(1)}, bf16[12,4,4224]{2,1,0:T(4,128)(2,1)S(1)}, u32[]{:S(2)}, u32[]{:S(2)}) %collective-permute-start.31) | collective-permute-done | bytes 405536 | tf_op jit(solution)/shard_map/cond/branch_1_fun/ppermute | solution.py:41
  100.5 5.9 %vocabulary_scores.11.refs_2_ = f32[2,8,48]{2,1,0:T(8,128)S(1)} custom-call(s32[5]{0:T(128)S(1)} %get-tuple-element.74.refs_0_.place_ref.first_ref, bf16[12,4,4224]{2,1,0:T(4,128)(2,1)S(1)} %constant_dynamic-update-slice_fusion.2.refs_0_, bf16[12,4,4224]{2,1,0:T(4,128)(2,1)S(1)} %collective-permute-done.31.refs_1_, bf16[2000,4096]{1,0:T(8,128)(2,1)S(1)} %copy-done.1), custom_call_target="tpu_custom_call" | custom-call | flops 2359296000 | bytes 786432 | tf_op jit(solution)/shard_map/cond/branch_1_fun/vocabulary_scores/pallas_call | solution.py:534
  106.5 0.6 statistics_by_group.3
  107.1 10.7 %all_to_all.19.every_ref = f32[32,8,96]{2,1,0:T(8,128)S(1)} all-to-all(f32[32,8,96]{2,1,0:T(8,128)S(1)} %statistics_by_group.3), channel_id=1, replica_groups=mesh['section'=2,'tm'=4,'mp'=4] {'section','tm','mp'}, dimensions={0} | all-to-all | bytes 196608 | tf_op jit(solution)/shard_map/cond/branch_1_fun/all_to_all | solution.py:31
  117.8 0.7 hypothesis_scores.3
  118.6 0.6 copy-done.9
  (28 shorter events, 0.2 us)
Async XLA Ops:
  0.1 12.7 %copy-start.7 = (s32[2,8,16]{2,1,0:T(8,128)S(1)}, s32[2,8,16]{2,1,0:T(8,128)}, u32[]{:S(2)}) copy-start(s32[2,8,16]{2,1,0:T(8,128)} %param.21) | copy-start | bytes 3076
  0.1 12.7 %copy-start.5 = (s32[8]{0:T(128)S(1)}, s32[8]{0:T(128)}, u32[]{:S(2)}) copy-start(s32[8]{0:T(128)} %slot_ref.1) | copy-start | bytes 100
  0.1 12.7 %copy-start.6 = (s32[2,8]{1,0:T(2,128)S(1)}, s32[2,8]{1,0:T(2,128)}, u32[]{:S(2)}) copy-start(s32[2,8]{1,0:T(2,128)} %length_ref.1) | copy-start | bytes 196
  6.4 16.7 %all-to-all-start.2 = ((bf16[4,32,1280]{2,1,0:T(8,128)(2,1)}), bf16[4,32,1280]{2,1,0:T(8,128)(2,1)S(1)}, u32[]{:S(2)}, u32[]{:S(2)}) async-start(bf16[4,32,1280]{2,1,0:T(8,128)(2,1)} %get-tuple-element.110), calls=%async_computation.2 | async-start | bytes 655360 | tf_op jit(solution)/shard_map/all_to_all | solution.py:31
  12.8 10.2 %copy-start.2 = (bf16[1280,1024]{1,0:T(8,128)(2,1)S(1)}, bf16[1280,1024]{1,0:T(8,128)(2,1)}, u32[]{:S(2)}) copy-start(bf16[1280,1024]{1,0:T(8,128)(2,1)} %refs_2_.1) | copy-start | bytes 7864324
  19.0 19.1 %copy-start.8 = (s32[4]{0:T(128)S(1)}, s32[4]{0:T(128)}, u32[]{:S(2)}) copy-start(s32[4]{0:T(128)} %param.14) | copy-start | bytes 52
  19.0 1.6 %collective-permute-start.36 = (bf16[272,512]{1,0:T(8,128)(2,1)S(1)}, bf16[272,512]{1,0:T(8,128)(2,1)S(1)}, u32[]{:S(2)}, u32[]{:S(2)}) collective-permute-start(bf16[272,512]{1,0:T(8,128)(2,1)S(1)} %get-tuple-element.109), channel_id=1, source_target_pairs={{0,4},{4,0},{8,12},{12,8},{1,5},{5,1},{9,13},{13,9},{2,6},{6,2},{1... | collective-permute-start | bytes 835592 | tf_op jit(solution)/shard_map/ppermute | solution.py:41
  19.1 17.1 %collective-permute-start.35 = (bf16[272,512]{1,0:T(8,128)(2,1)S(1)}, bf16[272,512]{1,0:T(8,128)(2,1)}, u32[]{:S(2)}, u32[]{:S(2)}) collective-permute-start(bf16[272,512]{1,0:T(8,128)(2,1)S(1)} %get-tuple-element.107), channel_id=1, source_target_pairs={{0,4},{4,0},{8,12},{12,8},{1,5},{5,1},{9,13},{13,9},{2,6},{6,2},{1... | collective-permute-start | bytes 835592 | tf_op jit(solution)/shard_map/ppermute | solution.py:41
  21.4 14.8 %collective-permute-start.37 = (bf16[272,512]{1,0:T(8,128)(2,1)}, bf16[272,512]{1,0:T(8,128)(2,1)}, u32[]{:S(2)}, u32[]{:S(2)}) collective-permute-start(bf16[272,512]{1,0:T(8,128)(2,1)} %add.45), channel_id=1, source_target_pairs={{0,8},{4,12},{8,0},{12,4},{1,9},{5,13},{9,1},{13,5},{2,10},{6,14},... | collective-permute-start | bytes 835592 | tf_op jit(solution)/shard_map/ppermute | solution.py:41
  24.6 13.4 %all-to-all-start.3 = ((bf16[32,8,256]{2,1,0:T(8,128)(2,1)}), bf16[32,8,256]{2,1,0:T(8,128)(2,1)S(1)}, u32[]{:S(2)}, u32[]{:S(2)}) async-start(bf16[32,8,256]{2,1,0:T(8,128)(2,1)} %bitcast.20), calls=%async_computation.3 | async-start | bytes 262144 | tf_op jit(solution)/shard_map/all_to_all | solution.py:31
  30.5 1.9 %collective-permute-start.32 = (s32[1]{0:T(128)}, s32[1]{0:T(128)}, u32[]{:S(2)}, u32[]{:S(2)}) collective-permute-start(s32[1]{0:T(128)} %bitcast.12), channel_id=1, source_target_pairs={{0,4},{4,0},{8,12},{12,8},{1,5},{5,1},{9,13},{13,9},{2,6},{6,2},{1... | collective-permute-start | bytes 20 | tf_op jit(solution)/shard_map/ppermute | solution.py:41
  30.7 3.6 %collective-permute-start.33 = (s32[1]{0:T(128)}, s32[1]{0:T(128)}, u32[]{:S(2)}, u32[]{:S(2)}) collective-permute-start(s32[1]{0:T(128)} %bitcast.12), channel_id=1, source_target_pairs={{0,8},{4,12},{8,0},{12,4},{1,9},{5,13},{9,1},{13,5},{2,10},{6,14},... | collective-permute-start | bytes 20 | tf_op jit(solution)/shard_map/ppermute | solution.py:41
  32.4 3.2 %collective-permute-start.34 = (s32[1]{0:T(128)}, s32[1]{0:T(128)}, u32[]{:S(2)}, u32[]{:S(2)}) collective-permute-start(s32[1]{0:T(128)} %bitcast.12), channel_id=1, source_target_pairs={{0,12},{4,8},{8,4},{12,0},{1,13},{5,9},{9,5},{13,1},{2,14},{6,10},... | collective-permute-start | bytes 20 | tf_op jit(solution)/shard_map/ppermute | solution.py:41
  38.0 25.7 %copy-start.4 = (bf16[272,512]{1,0:T(8,128)(2,1)S(1)}, bf16[272,512]{1,0:T(8,128)(2,1)}, u32[]{:S(2)}) copy-start(bf16[272,512]{1,0:T(8,128)(2,1)} %get-tuple-element.77.refs_3_.refs_0_) | copy-start | bytes 835588 | tf_op jit(solution)/shard_map/cond
  41.9 7.4 %collective-permute-start.16 = (bf16[32,4096]{1,0:T(8,128)(2,1)S(1)}, bf16[32,4096]{1,0:T(8,128)(2,1)S(1)}, u32[]{:S(2)}, u32[]{:S(2)}) collective-permute-start(bf16[32,4096]{1,0:T(8,128)(2,1)S(1)} %get-tuple-element.84), channel_id=1, source_target_pairs={{0,16},{16,0},{1,17},{17,1},{2,18},{18,2},{3,19},{19,3},{4,20},{20... | collective-permute-start | bytes 786440 | tf_op jit(solution)/shard_map/cond/branch_1_fun/ppermute | solution.py:41
  42.7 5.0 %collective-permute-start.17 = (bf16[16,4096]{1,0:T(8,128)(2,1)S(1)}, bf16[16,4096]{1,0:T(8,128)(2,1)S(1)}, u32[]{:S(2)}, u32[]{:S(2)}) collective-permute-start(bf16[16,4096]{1,0:T(8,128)(2,1)S(1)} %get-tuple-element.86), channel_id=1, source_target_pairs={{0,1},{1,0},{2,3},{3,2},{4,5},{5,4},{6,7},{7,6},{8,9},{9,8},{10,11... | collective-permute-start | bytes 393224 | tf_op jit(solution)/shard_map/cond/branch_1_fun/ppermute | solution.py:41
  50.0 5.5 %collective-permute-start.18 = (bf16[16,4096]{1,0:T(8,128)(2,1)S(1)}, bf16[16,4096]{1,0:T(8,128)(2,1)S(1)}, u32[]{:S(2)}, u32[]{:S(2)}) collective-permute-start(bf16[16,4096]{1,0:T(8,128)(2,1)S(1)} %get-tuple-element.88), channel_id=1, source_target_pairs={{0,1},{1,0},{2,3},{3,2},{4,5},{5,4},{6,7},{7,6},{8,9},{9,8},{10,11... | collective-permute-start | bytes 393224 | tf_op jit(solution)/shard_map/cond/branch_1_fun/ppermute | solution.py:41
  51.2 4.3 %collective-permute-start.19 = (bf16[8,4096]{1,0:T(8,128)(2,1)S(1)}, bf16[8,4096]{1,0:T(8,128)(2,1)S(1)}, u32[]{:S(2)}, u32[]{:S(2)}) collective-permute-start(bf16[8,4096]{1,0:T(8,128)(2,1)S(1)} %get-tuple-element.90), channel_id=1, source_target_pairs={{0,16},{16,0},{1,17},{17,1},{2,18},{18,2},{3,19},{19,3},{4,20},{20... | collective-permute-start | bytes 196616 | tf_op jit(solution)/shard_map/cond/branch_1_fun/ppermute | solution.py:41
  56.1 7.7 %collective-permute-start.20 = (bf16[12,4096]{1,0:T(8,128)(2,1)S(1)}, bf16[12,4096]{1,0:T(8,128)(2,1)S(1)}, u32[]{:S(2)}, u32[]{:S(2)}) collective-permute-start(bf16[12,4096]{1,0:T(8,128)(2,1)S(1)} %get-tuple-element.92), channel_id=1, source_target_pairs={{0,2},{1,3},{2,0},{3,1},{4,6},{5,7},{6,4},{7,5},{8,10},{9,11},{10,... | collective-permute-start | bytes 294920 | tf_op jit(solution)/shard_map/cond/branch_1_fun/ppermute | solution.py:41
  65.0 5.0 %collective-permute-start.21 = (bf16[3,4,4224]{2,1,0:T(4,128)(2,1)S(1)}, bf16[3,4,4224]{2,1,0:T(4,128)(2,1)S(1)}, u32[]{:S(2)}, u32[]{:S(2)}) collective-permute-start(bf16[3,4,4224]{2,1,0:T(4,128)(2,1)S(1)} %token_rows.3), channel_id=1, source_target_pairs={{0,1},{1,0},{2,3},{3,2},{4,5},{5,4},{6,7},{7,6},{8,9},{9,8},{10,11... | collective-permute-start | bytes 304136 | tf_op jit(solution)/shard_map/cond/branch_1_fun/ppermute | solution.py:41
  65.1 10.2 %collective-permute-start.22 = (bf16[3,4,4224]{2,1,0:T(4,128)(2,1)S(1)}, bf16[3,4,4224]{2,1,0:T(4,128)(2,1)S(1)}, u32[]{:S(2)}, u32[]{:S(2)}) collective-permute-start(bf16[3,4,4224]{2,1,0:T(4,128)(2,1)S(1)} %token_rows.3), channel_id=1, source_target_pairs={{0,2},{1,3},{2,0},{3,1},{4,6},{5,7},{6,4},{7,5},{8,10},{9,11},{10,... | collective-permute-start | bytes 304136 | tf_op jit(solution)/shard_map/cond/branch_1_fun/ppermute | solution.py:41
  67.8 7.5 %collective-permute-start.23 = (bf16[3,4,4224]{2,1,0:T(4,128)(2,1)S(1)}, bf16[3,4,4224]{2,1,0:T(4,128)(2,1)S(1)}, u32[]{:S(2)}, u32[]{:S(2)}) collective-permute-start(bf16[3,4,4224]{2,1,0:T(4,128)(2,1)S(1)} %token_rows.3), channel_id=1, source_target_pairs={{0,3},{1,2},{2,1},{3,0},{4,7},{5,6},{6,5},{7,4},{8,11},{9,10},{10,... | collective-permute-start | bytes 304136 | tf_op jit(solution)/shard_map/cond/branch_1_fun/ppermute | solution.py:41
  75.4 1.8 %collective-permute-start.26 = (bf16[12,4,4224]{2,1,0:T(4,128)(2,1)S(1)}, bf16[12,4,4224]{2,1,0:T(4,128)(2,1)S(1)}, u32[]{:S(2)}, u32[]{:S(2)}) collective-permute-start(bf16[12,4,4224]{2,1,0:T(4,128)(2,1)S(1)} %bitcast.33), channel_id=1, source_target_pairs={{0,4},{4,0},{8,12},{12,8},{1,5},{5,1},{9,13},{13,9},{2,6},{6,2},{1... | collective-permute-start | bytes 1216520 | tf_op jit(solution)/shard_map/cond/branch_1_fun/ppermute | solution.py:41
  75.5 13.3 %collective-permute-start.24 = (bf16[12,4,4224]{2,1,0:T(4,128)(2,1)S(1)}, bf16[12,4,4224]{2,1,0:T(4,128)(2,1)S(1)}, u32[]{:S(2)}, u32[]{:S(2)}) collective-permute-start(bf16[12,4,4224]{2,1,0:T(4,128)(2,1)S(1)} %bitcast.34), channel_id=1, source_target_pairs={{0,16},{16,0},{1,17},{17,1},{2,18},{18,2},{3,19},{19,3},{4,20},{20... | collective-permute-start | bytes 1216520 | tf_op jit(solution)/shard_map/cond/branch_1_fun/ppermute | solution.py:41
  75.6 13.3 %collective-permute-start.25 = (bf16[12,4,4224]{2,1,0:T(4,128)(2,1)S(1)}, bf16[12,4,4224]{2,1,0:T(4,128)(2,1)S(1)}, u32[]{:S(2)}, u32[]{:S(2)}) collective-permute-start(bf16[12,4,4224]{2,1,0:T(4,128)(2,1)S(1)} %bitcast.35), channel_id=1, source_target_pairs={{0,8},{4,12},{8,0},{12,4},{1,9},{5,13},{9,1},{13,5},{2,10},{6,14},... | collective-permute-start | bytes 1216520 | tf_op jit(solution)/shard_map/cond/branch_1_fun/ppermute | solution.py:41
  77.2 5.7 %copy-start.1 = (bf16[2000,4096]{1,0:T(8,128)(2,1)S(1)}, bf16[2000,4096]{1,0:T(8,128)(2,1)}, u32[]{:S(2)}) copy-start(bf16[2000,4096]{1,0:T(8,128)(2,1)} %get-tuple-element.126.refs_2_.refs_4_) | copy-start | bytes 49152004 | tf_op jit(solution)/shard_map/cond
  88.8 3.2 %collective-permute-start.29 = (bf16[12,4,4224]{2,1,0:T(4,128)(2,1)S(1)}, bf16[12,4,4224]{2,1,0:T(4,128)(2,1)S(1)}, u32[]{:S(2)}, u32[]{:S(2)}) collective-permute-start(bf16[12,4,4224]{2,1,0:T(4,128)(2,1)S(1)} %collective-permute-done.25.refs_0_), channel_id=1, source_target_pairs={{0,4},{4,0},{8,12},{12,8},{1,5},{5,1},{9,13},{13,9},{2,6},{6,2},{1... | collective-permute-start | bytes 1216520 | tf_op jit(solution)/shard_map/cond/branch_1_fun/ppermute | solution.py:41
  89.0 3.0 %collective-permute-start.30 = (bf16[12,4,4224]{2,1,0:T(4,128)(2,1)S(1)}, bf16[12,4,4224]{2,1,0:T(4,128)(2,1)S(1)}, u32[]{:S(2)}, u32[]{:S(2)}) collective-permute-start(bf16[12,4,4224]{2,1,0:T(4,128)(2,1)S(1)} %collective-permute-done.24.refs_2_), channel_id=1, source_target_pairs={{0,4},{4,0},{8,12},{12,8},{1,5},{5,1},{9,13},{13,9},{2,6},{6,2},{1... | collective-permute-start | bytes 1216520 | tf_op jit(solution)/shard_map/cond/branch_1_fun/ppermute | solution.py:41
  89.5 9.0 %collective-permute-start.27 = (bf16[6,4,4224]{2,1,0:T(4,128)(2,1)S(1)}, bf16[6,4,4224]{2,1,0:T(4,128)(2,1)S(1)}, u32[]{:S(2)}, u32[]{:S(2)}) collective-permute-start(bf16[6,4,4224]{2,1,0:T(4,128)(2,1)S(1)} %slice.10), channel_id=1, source_target_pairs={{0,8},{4,12},{8,0},{12,4},{1,9},{5,13},{9,1},{13,5},{2,10},{6,14},... | collective-permute-start | bytes 608264 | tf_op jit(solution)/shard_map/cond/branch_1_fun/ppermute | solution.py:41
  90.0 8.5 %collective-permute-start.28 = (bf16[6,4,4224]{2,1,0:T(4,128)(2,1)S(1)}, bf16[6,4,4224]{2,1,0:T(4,128)(2,1)S(1)}, u32[]{:S(2)}, u32[]{:S(2)}) collective-permute-start(bf16[6,4,4224]{2,1,0:T(4,128)(2,1)S(1)} %slice.11), channel_id=1, source_target_pairs={{0,16},{16,0},{1,17},{17,1},{2,18},{18,2},{3,19},{19,3},{4,20},{20... | collective-permute-start | bytes 608264 | tf_op jit(solution)/shard_map/cond/branch_1_fun/ppermute | solution.py:41
  98.7 1.8 %collective-permute-start.31 = (bf16[12,4,4224]{2,1,0:T(4,128)(2,1)S(1)}, bf16[12,4,4224]{2,1,0:T(4,128)(2,1)S(1)}, u32[]{:S(2)}, u32[]{:S(2)}) collective-permute-start(bf16[12,4,4224]{2,1,0:T(4,128)(2,1)S(1)} %constant_dynamic-update-slice_fusion.2.refs_0_), channel_id=1, source_target_pairs={{0,4},{4,0},{8,12},{12,8},{1,5},{5,1},{9,13},{13,9},{2,6},{6,2},{1... | collective-permute-start | bytes 1216520 | tf_op jit(solution)/shard_map/cond/branch_1_fun/ppermute | solution.py:41
  118.6 0.6 copy-start.9

commit v18 on v17

--- a/solution.py
+++ b/solution.py
@@ -506,10 +506,8 @@
     stat[8:9, :] = jnp.zeros((1, tokens), jnp.float32)
     stat[16:17, :] = jnp.zeros((1, tokens), jnp.float32)
 
-    @pl.loop(0, vocab_rows // tile)
-    def _(step):
-        start = pl.multiple_of(step * tile, tile)
-        logits = dot_nt(head_ref[pl.ds(start, tile), :], rows_ref[:, :width])
+    for start in range(0, vocab_rows, tile):
+        logits = dot_nt(head_ref[start : start + tile, :], rows_ref[:, :width])
         vocab = lax.broadcasted_iota(jnp.int32, logits.shape, 0) + start
         before = stat[0:1, :]
         upper = jnp.maximum(before, jnp.max(logits, axis=0, keepdims=True))
@@ -532,7 +530,7 @@
     width = head.shape[1]
     tokens = share * count
     return pl.pallas_call(
-        functools.partial(vocabulary_kernel, head.shape[0] // 2, count),
+        functools.partial(vocabulary_kernel, head.shape[0], count),
         in_specs=[SCALARS] + [INSIDE] * (count + 1),
         out_specs=INSIDE,
         out_shape=jax.ShapeDtypeStruct((count, 8, share), jnp.float32),
@@ -550,13 +548,27 @@
     )(place, *sets, pltpu.with_memory_space_constraint(head, pltpu.VMEM))
 
 
-def spread_kernel(sections, groups, widths, place_ref, slot_ref, *refs):
+def zero_kernel(after_ref, head_ref, out_ref):
+    out_ref[...] = jnp.zeros_like(out_ref)
+
+
+def head_in_vmem(after, head):
+    return pl.pallas_call(
+        zero_kernel,
+        in_specs=[ANYWHERE, INSIDE],
+        out_specs=INSIDE,
+        out_shape=jax.ShapeDtypeStruct((8, LANES), jnp.float32),
+        compiler_params=pltpu.CompilerParams(vmem_limit_bytes=16 << 20),
+        name="vocabulary_rows",
+    )(after, pltpu.with_memory_space_constraint(head, pltpu.VMEM))
+
+
+def spread_kernel(order, sections, groups, widths, place_ref, slot_ref, *refs):
     stats, (out_ref, table, block) = refs[:-3], refs[-3:]
     share = table.shape[2]
-    first = 0
-    for stat in stats:
-        table[first : first + stat.shape[0]] = stat[...]
-        first += stat.shape[0]
+    for stat, places in zip(stats, order):
+        for number, at in enumerate(places):
+            table[at] = stat[number]
     slots = slot_ref.shape[0] // groups
     block[...] = jnp.zeros_like(block)
     for group in range(groups):
@@ -573,11 +585,11 @@
                 out_ref[(section * groups + group) * widths + width] = block[group]
 
 
-def spread_stats(place, slot_utt, stats, sections, groups, widths):
+def spread_stats(place, slot_utt, stats, order, sections, groups, widths):
     share = stats[0].shape[2]
     assert 3 * slot_utt.shape[0] // groups <= 8
     return pl.pallas_call(
-        functools.partial(spread_kernel, sections, groups, widths),
+        functools.partial(spread_kernel, order, sections, groups, widths),
         in_specs=[SCALARS] * 2 + [INSIDE] * len(stats),
         out_specs=INSIDE,
         out_shape=jax.ShapeDtypeStruct(
@@ -675,18 +687,18 @@
     half = own.shape[0] // 2
     by_x = swap(own, "section", 1)
     by_y = swap(own, "tm", 2)
-    stats = [vocabulary_stats(place, [own, swap(own, "tm", 1)], head)]
-    by_x, by_y, stats[0] = lax.optimization_barrier((by_x, by_y, stats[0]))
+    beside = swap(own, "tm", 1)
+    by_x, by_y, _ = lax.optimization_barrier((by_x, by_y, head_in_vmem(beside, head)))
     across = [swap(by_x[:half], "tm", 2), swap(by_y[half:], "section", 1)]
-    stats.append(
-        vocabulary_stats(place, [by_y, swap(by_y, "tm", 1), by_x, swap(by_x, "tm", 1)], head)
-    )
-    *across, stats[1] = lax.optimization_barrier((*across, stats[1]))
+    near = vocabulary_stats(place, [by_y, swap(by_y, "tm", 1), by_x, swap(by_x, "tm", 1)], head)
+    *across, near = lax.optimization_barrier((*across, near))
     across = jnp.concatenate(across)
-    stats.append(vocabulary_stats(place, [across, swap(across, "tm", 1)], head))
+    far = vocabulary_stats(place, [across, swap(across, "tm", 1), own, beside], head)
+    stats = [near, far]
+    order = ((2, 3, 4, 5), (6, 7, 0, 1))
 
     every = exchange(
-        spread_stats(place, slot_utt, stats, section_count, group_count, width_count), ALL
+        spread_stats(place, slot_utt, stats, order, section_count, group_count, width_count), ALL
     )
     return hypothesis_scores(
         place, slot_utt, hyp_len, every, slot_count, hyp_count, section_count, width_count

time: 120 us -> 121 us (level)
  waiting for transfers between devices: 26.7 us -> 33.8 us
  Pallas kernels: 40.1 us -> 33.6 us
  blocking collectives: 10.7 us -> 12.2 us
    ppermute x22, waiting for transfers between devices: 24.8 us -> 31.9 us  [swap(): return lax.ppermute(values, axis, pairs)]
    pallas_call x4 -> x3, Pallas kernels: 19.1 us -> 12.6 us  [the longest x2 11.9 us: vocabulary_stats(): pl.pallas_call(functools.partial(vocabulary_kernel, head.shape[0], count)...]
    all_to_all x1, blocking collectives: 10.7 us -> 12.2 us  [exchange(): return lax.all_to_all(blocks, axis, split_axis=0, concat_axis=0, tiled=True)]
  transfers between devices with their start and end apart: 24 -> 24, of which waited for: 13 -> 14; matrix products, arithmetic and copies ran while one was open for 2% -> 2% of each run, Pallas kernels for 17% -> 11%
where the time goes in v18:
time: 121 us
  waiting for transfers between devices  33.8 us (28%)
  Pallas kernels  33.6 us (28%)
  starting transfers between devices  29.6 us (24%)
  blocking collectives  12.2 us (10%)
  local copies, waits for them, and re-layouts  7.03 us (6%)
  between operations  2.65 us (2%)
  other arithmetic  1.63 us (1%)
    ppermute x22, waiting for transfers between devices, swap(): return lax.ppermute(values, axis, pairs)  31.9 us
    ppermute x22, starting transfers between devices, swap(): return lax.ppermute(values, axis, pairs)  18.3 us
    all_to_all x1, blocking collectives, exchange(): return lax.all_to_all(blocks, axis, split_axis=0, concat_axis=0, tiled=True)  12.2 us
    pallas_call x2, Pallas kernels, vocabulary_stats(): pl.pallas_call(functools.partial(vocabulary_kernel, head.shape[0], count)...  11.9 us
    all_to_all x2, starting transfers between devices, exchange(): return lax.all_to_all(blocks, axis, split_axis=0, concat_axis=0, tiled=True)  11.3 us
    pallas_call x1, Pallas kernels, ffn(): pl.pallas_call(functools.partial(ffn_kernel, tile), in_specs=[SCALARS] +...  6.31 us
    pallas_call x1, Pallas kernels, queries_of(): pl.pallas_call(functools.partial(query_kernel, count, depth), in_specs=[S...  6.15 us
    cond x5, local copies, waits for them, and re-layouts  5.73 us
  transfers between devices with their start and end apart: 24, of which 14 were waited for; matrix products, arithmetic and copies ran while one was open for 2% of the time, Pallas kernels for 11%

profile of v18, /device:TPU:0, one launch (start us, length us, event | category | flops | bytes accessed | tf_op | source)
XLA Modules:
  0.0 120.7 jit_solution(14567535545188891508)
XLA Ops:
  0.0 0.1 stack.23.place_ref.after_ref
  0.1 6.3 %encoder_ffn.1 = (bf16[4,32,1280]{2,1,0:T(8,128)(2,1)}, bf16[32,1280]{1,0:T(8,128)(2,1)S(1)}) custom-call(s32[5]{0:T(128)S(1)} %stack.23.place_ref.after_ref, bf16[32,4,1280]{2,1,0:T(4,128)(2,1)} %x_ref.1, bf16[1280,1280]{1,0:T(8,128)(2,1)} %up_ref.1, bf16[1280,1280]{1,0:T(8,128)(2,1)} %down_ref.1), custom_call_target="tpu_custom_call" | custom-call | flops 838860800 | bytes 6553600 | tf_op jit(solution)/shard_map/encoder_ffn/pallas_call | solution.py:121
  6.4 6.3 %all-to-all-start.2 = ((bf16[4,32,1280]{2,1,0:T(8,128)(2,1)}), bf16[4,32,1280]{2,1,0:T(8,128)(2,1)S(1)}, u32[]{:S(2)}, u32[]{:S(2)}) async-start(bf16[4,32,1280]{2,1,0:T(8,128)(2,1)} %get-tuple-element.108), calls=%async_computation.2 | async-start | bytes 655360 | tf_op jit(solution)/shard_map/all_to_all | solution.py:31
  12.7 0.1 reshape.27.tok_ref
  12.8 6.1 %hypothesis_queries.1 = (bf16[272,512]{1,0:T(8,128)(2,1)}, bf16[272,512]{1,0:T(8,128)(2,1)S(1)}, bf16[272,512]{1,0:T(8,128)(2,1)S(1)}, bf16[272,512]{1,0:T(8,128)(2,1)S(1)}) custom-call(s32[5]{0:T(128)S(1)} %stack.23.place_ref.after_ref, s32[8]{0:T(128)S(1)} %copy-done.5, s32[2,8]{1,0:T(2,128)S(1)} %copy-done.6, s32[5]{0:T(128)S(1)} %stack.23.place_ref.after_ref, ...), custom_call_target="tpu_custom_call" | custom-call | flops 1073741824 | bytes 6291456 | tf_op jit(solution)/shard_map/hypothesis_queries/pallas_call | solution.py:228
  19.0 0.1 collective-permute-start.36
  19.1 0.5 collective-permute-start.35
  19.6 1.0 collective-permute-done.36
  20.6 0.8 add.45
  21.4 1.5 %collective-permute-start.37 = (bf16[272,512]{1,0:T(8,128)(2,1)}, bf16[272,512]{1,0:T(8,128)(2,1)}, u32[]{:S(2)}, u32[]{:S(2)}) collective-permute-start(bf16[272,512]{1,0:T(8,128)(2,1)} %add.45), channel_id=1, source_target_pairs={{0,8},{4,12},{8,0},{12,4},{1,9},{5,13},{9,1},{13,5},{2,10},{6,14},... | collective-permute-start | bytes 835592 | tf_op jit(solution)/shard_map/ppermute | solution.py:41
  23.0 0.1 all-to-all-done.2.refs_0_
  23.1 1.5 %frame_keys_values.1 = bf16[256,256]{1,0:T(8,128)(2,1)} custom-call(bf16[4,32,1280]{2,1,0:T(8,128)(2,1)S(1)} %all-to-all-done.2.refs_0_, bf16[32,1280]{1,0:T(8,128)(2,1)S(1)} %get-tuple-element.109.refs_1_, bf16[1280,1024]{1,0:T(8,128)(2,1)S(1)} %copy-done.2, bf16[272,512]{1,0:T(8,128)(2,1)} %get-tuple-element.104.refs_3_), custom_call_target="tpu_custom_call" | custom-call | flops 83886080 | bytes 2621440 | tf_op jit(solution)/shard_map/frame_keys_values/pallas_call | solution.py:287
  24.6 5.0 %all-to-all-start.3 = ((bf16[32,8,256]{2,1,0:T(8,128)(2,1)}), bf16[32,8,256]{2,1,0:T(8,128)(2,1)S(1)}, u32[]{:S(2)}, u32[]{:S(2)}) async-start(bf16[32,8,256]{2,1,0:T(8,128)(2,1)} %bitcast.20), calls=%async_computation.3 | async-start | bytes 262144 | tf_op jit(solution)/shard_map/all_to_all | solution.py:31
  29.6 0.1 reduce_sum.9
  29.7 0.7 fusion
  30.5 0.3 collective-permute-start.32
  30.7 1.7 %collective-permute-start.33 = (s32[1]{0:T(128)}, s32[1]{0:T(128)}, u32[]{:S(2)}, u32[]{:S(2)}) collective-permute-start(s32[1]{0:T(128)} %bitcast.12), channel_id=1, source_target_pairs={{0,8},{4,12},{8,0},{12,4},{1,9},{5,13},{9,1},{13,5},{2,10},{6,14},... | collective-permute-start | bytes 20 | tf_op jit(solution)/shard_map/ppermute | solution.py:41
  33.7 0.6 collective-permute-done.33
  35.0 0.6 collective-permute-done.34
  36.2 1.8 %all-to-all-done.3 = bf16[32,8,256]{2,1,0:T(8,128)(2,1)S(1)} async-done(((bf16[32,8,256]{2,1,0:T(8,128)(2,1)}), bf16[32,8,256]{2,1,0:T(8,128)(2,1)S(1)}, u32[]{:S(2)}, u32[]{:S(2)}) %all-to-all-start.3) | async-done | bytes 131104 | tf_op jit(solution)/shard_map/all_to_all | solution.py:31
  38.0 82.1 %conditional.1 = (f32[2,8]{1,0:T(2,128)S(1)}) conditional(s32[]{:T(128)} %bitcast.13, (s32[5]{0:T(128)S(1)}, s32[8]{0:T(128)S(1)}, s32[4]{0:T(128)S(1)}, bf16[272,512]{1,0:T(8,128)(2,1)}, bf16[272,512]{1,0:T(8,128)(2,1)}, /*index=5*/bf16[272,512]{1,0:T(8,128)(2,1)}, bf16[32,8,256]{2,1,0:T(8,128)(2,1)S(1)}, bf16[512,4096]{1,0:T(8,128)(2,1)}, ...), branch_computations={%region_2.3_spmd, %region_3.4_spmd} | conditional | flops 13186891776 | bytes 100565904 | solution.py:773
  38.0 3.8 %attention_projection.3 = (bf16[32,4096]{1,0:T(8,128)(2,1)S(1)}, bf16[32,4096]{1,0:T(8,128)(2,1)S(1)}, bf16[16,4096]{1,0:T(8,128)(2,1)S(1)}, bf16[16,4096]{1,0:T(8,128)(2,1)S(1)}) custom-call(s32[5]{0:T(128)S(1)} %get-tuple-element.73.refs_0_.place_ref.first_ref, s32[8]{0:T(128)S(1)} %get-tuple-element.74.refs_1_.slot_ref, s32[4]{0:T(128)S(1)} %get-tuple-element.120.refs_2_, ...), custom_call_target="tpu_custom_call" | custom-call | flops 452984832 | bytes 4980736 | tf_op jit(solution)/shard_map/cond/branch_1_fun/attention_projection/pallas_call | solution.py:375
  41.9 0.8 collective-permute-start.16
  42.7 0.6 collective-permute-start.17
  43.3 4.4 %collective-permute-done.17.refs_3_ = bf16[16,4096]{1,0:T(8,128)(2,1)S(1)} collective-permute-done((bf16[16,4096]{1,0:T(8,128)(2,1)S(1)}, bf16[16,4096]{1,0:T(8,128)(2,1)S(1)}, u32[]{:S(2)}, u32[]{:S(2)}) %collective-permute-start.17) | collective-permute-done | bytes 131104 | tf_op jit(solution)/shard_map/cond/branch_1_fun/ppermute | solution.py:41
  47.7 1.6 %collective-permute-done.16.refs_1_ = bf16[32,4096]{1,0:T(8,128)(2,1)S(1)} collective-permute-done((bf16[32,4096]{1,0:T(8,128)(2,1)S(1)}, bf16[32,4096]{1,0:T(8,128)(2,1)S(1)}, u32[]{:S(2)}, u32[]{:S(2)}) %collective-permute-start.16) | collective-permute-done | bytes 262176 | tf_op jit(solution)/shard_map/cond/branch_1_fun/ppermute | solution.py:41
  49.3 0.7 sum_phase.6
  50.0 1.2 %collective-permute-start.18 = (bf16[16,4096]{1,0:T(8,128)(2,1)S(1)}, bf16[16,4096]{1,0:T(8,128)(2,1)S(1)}, u32[]{:S(2)}, u32[]{:S(2)}) collective-permute-start(bf16[16,4096]{1,0:T(8,128)(2,1)S(1)} %get-tuple-element.87), channel_id=1, source_target_pairs={{0,1},{1,0},{2,3},{3,2},{4,5},{5,4},{6,7},{7,6},{8,9},{9,8},{10,11... | collective-permute-start | bytes 393224 | tf_op jit(solution)/shard_map/cond/branch_1_fun/ppermute | solution.py:41
  51.2 1.2 %collective-permute-start.19 = (bf16[8,4096]{1,0:T(8,128)(2,1)S(1)}, bf16[8,4096]{1,0:T(8,128)(2,1)S(1)}, u32[]{:S(2)}, u32[]{:S(2)}) collective-permute-start(bf16[8,4096]{1,0:T(8,128)(2,1)S(1)} %get-tuple-element.89), channel_id=1, source_target_pairs={{0,16},{16,0},{1,17},{17,1},{2,18},{18,2},{3,19},{19,3},{4,20},{20... | collective-permute-start | bytes 196616 | tf_op jit(solution)/shard_map/cond/branch_1_fun/ppermute | solution.py:41
  52.4 3.1 %collective-permute-done.19.refs_3_ = bf16[8,4096]{1,0:T(8,128)(2,1)S(1)} collective-permute-done((bf16[8,4096]{1,0:T(8,128)(2,1)S(1)}, bf16[8,4096]{1,0:T(8,128)(2,1)S(1)}, u32[]{:S(2)}, u32[]{:S(2)}) %collective-permute-start.19) | collective-permute-done | bytes 65568 | tf_op jit(solution)/shard_map/cond/branch_1_fun/ppermute | solution.py:41
  55.4 0.6 sum_phase.7
  56.1 2.3 %collective-permute-start.20 = (bf16[12,4096]{1,0:T(8,128)(2,1)S(1)}, bf16[12,4096]{1,0:T(8,128)(2,1)S(1)}, u32[]{:S(2)}, u32[]{:S(2)}) collective-permute-start(bf16[12,4096]{1,0:T(8,128)(2,1)S(1)} %get-tuple-element.91), channel_id=1, source_target_pairs={{0,2},{1,3},{2,0},{3,1},{4,6},{5,7},{6,4},{7,5},{8,10},{9,11},{10,... | collective-permute-start | bytes 294920 | tf_op jit(solution)/shard_map/cond/branch_1_fun/ppermute | solution.py:41
  58.4 5.3 %collective-permute-done.20.refs_4_ = bf16[12,4096]{1,0:T(8,128)(2,1)S(1)} collective-permute-done((bf16[12,4096]{1,0:T(8,128)(2,1)S(1)}, bf16[12,4096]{1,0:T(8,128)(2,1)S(1)}, u32[]{:S(2)}, u32[]{:S(2)}) %collective-permute-start.20) | collective-permute-done | bytes 98336 | tf_op jit(solution)/shard_map/cond/branch_1_fun/ppermute | solution.py:41
  63.7 1.3 %token_rows.3 = bf16[3,4,4224]{2,1,0:T(4,128)(2,1)S(1)} custom-call(s32[5]{0:T(128)S(1)} %get-tuple-element.73.refs_0_.place_ref.first_ref, s32[8]{0:T(128)S(1)} %get-tuple-element.74.refs_1_.slot_ref, bf16[272,512]{1,0:T(8,128)(2,1)S(1)} %copy-done.4, bf16[272,512]{1,0:T(8,128)(2,1)} %get-tuple-element.77.refs_4_.refs_1_, ...), custom_call_target="tpu_custom_call" | custom-call | tf_op jit(solution)/shard_map/cond/branch_1_fun/token_rows/pallas_call | solution.py:480
  65.0 0.1 collective-permute-start.21
  65.1 2.7 %collective-permute-start.22 = (bf16[3,4,4224]{2,1,0:T(4,128)(2,1)S(1)}, bf16[3,4,4224]{2,1,0:T(4,128)(2,1)S(1)}, u32[]{:S(2)}, u32[]{:S(2)}) collective-permute-start(bf16[3,4,4224]{2,1,0:T(4,128)(2,1)S(1)} %token_rows.3), channel_id=1, source_target_pairs={{0,2},{1,3},{2,0},{3,1},{4,6},{5,7},{6,4},{7,5},{8,10},{9,11},{10,... | collective-permute-start | bytes 304136 | tf_op jit(solution)/shard_map/cond/branch_1_fun/ppermute | solution.py:41
  67.8 1.6 %collective-permute-start.23 = (bf16[3,4,4224]{2,1,0:T(4,128)(2,1)S(1)}, bf16[3,4,4224]{2,1,0:T(4,128)(2,1)S(1)}, u32[]{:S(2)}, u32[]{:S(2)}) collective-permute-start(bf16[3,4,4224]{2,1,0:T(4,128)(2,1)S(1)} %token_rows.3), channel_id=1, source_target_pairs={{0,3},{1,2},{2,1},{3,0},{4,7},{5,6},{6,5},{7,4},{8,11},{9,10},{10,... | collective-permute-start | bytes 304136 | tf_op jit(solution)/shard_map/cond/branch_1_fun/ppermute | solution.py:41
  69.5 0.1 broadcast.7
  69.6 0.1 bitcast_dynamic-update-slice_fusion.7
  69.6 0.3 collective-permute-done.21
  70.0 5.3 %collective-permute-done.22 = bf16[3,4,4224]{2,1,0:T(4,128)(2,1)S(1)} collective-permute-done((bf16[3,4,4224]{2,1,0:T(4,128)(2,1)S(1)}, bf16[3,4,4224]{2,1,0:T(4,128)(2,1)S(1)}, u32[]{:S(2)}, u32[]{:S(2)}) %collective-permute-start.22) | collective-permute-done | bytes 101408 | tf_op jit(solution)/shard_map/cond/branch_1_fun/ppermute | solution.py:41
  75.3 0.1 bitcast_dynamic-update-slice_fusion.5
  75.3 0.1 bitcast_dynamic-update-slice_fusion.4
  75.4 0.1 collective-permute-start.24
  75.5 0.9 collective-permute-start.25
  76.4 7.8 %collective-permute-done.24.refs_2_ = bf16[12,4,4224]{2,1,0:T(4,128)(2,1)S(1)} collective-permute-done((bf16[12,4,4224]{2,1,0:T(4,128)(2,1)S(1)}, bf16[12,4,4224]{2,1,0:T(4,128)(2,1)S(1)}, u32[]{:S(2)}, u32[]{:S(2)}) %collective-permute-start.24) | collective-permute-done | bytes 405536 | tf_op jit(solution)/shard_map/cond/branch_1_fun/ppermute | solution.py:41
  84.1 0.1 collective-permute-done.25.refs_0_
  84.2 0.5 collective-permute-start.29
  84.7 0.1 slice.10
  84.8 0.1 slice.11
  84.9 0.4 collective-permute-start.26
  85.2 1.7 %collective-permute-start.27 = (bf16[6,4,4224]{2,1,0:T(4,128)(2,1)S(1)}, bf16[6,4,4224]{2,1,0:T(4,128)(2,1)S(1)}, u32[]{:S(2)}, u32[]{:S(2)}) collective-permute-start(bf16[6,4,4224]{2,1,0:T(4,128)(2,1)S(1)} %slice.11), channel_id=1, source_target_pairs={{0,16},{16,0},{1,17},{17,1},{2,18},{18,2},{3,19},{19,3},{4,20},{20... | collective-permute-start | bytes 608264 | tf_op jit(solution)/shard_map/cond/branch_1_fun/ppermute | solution.py:41
  86.9 5.7 %copy-done.1 = bf16[2000,4096]{1,0:T(8,128)(2,1)S(1)} copy-done((bf16[2000,4096]{1,0:T(8,128)(2,1)S(1)}, bf16[2000,4096]{1,0:T(8,128)(2,1)}, u32[]{:S(2)}) %copy-start.1) | copy-done | bytes 16384024 | tf_op jit(solution)/shard_map/cond
  92.6 6.0 %vocabulary_scores.6.refs_0_ = f32[4,8,48]{2,1,0:T(8,128)S(1)} custom-call(s32[5]{0:T(128)S(1)} %get-tuple-element.73.refs_0_.place_ref.first_ref, bf16[12,4,4224]{2,1,0:T(4,128)(2,1)S(1)} %collective-permute-done.25.refs_0_, bf16[12,4,4224]{2,1,0:T(4,128)(2,1)S(1)} %collective-permute-done.28.refs_1_, ...), custom_call_target="tpu_custom_call" | custom-call | flops 4718592000 | bytes 1572864 | tf_op jit(solution)/shard_map/cond/branch_1_fun/vocabulary_scores/pallas_call | solution.py:532
  98.5 0.0 collective-permute-done.27
  98.5 0.1 constant_dynamic-update-slice_fusion.3
  98.6 0.1 constant_dynamic-update-slice_fusion.2.refs_0_
  98.7 0.1 collective-permute-start.30
  98.8 1.7 %collective-permute-done.30.refs_1_ = bf16[12,4,4224]{2,1,0:T(4,128)(2,1)S(1)} collective-permute-done((bf16[12,4,4224]{2,1,0:T(4,128)(2,1)S(1)}, bf16[12,4,4224]{2,1,0:T(4,128)(2,1)S(1)}, u32[]{:S(2)}, u32[]{:S(2)}) %collective-permute-start.30) | collective-permute-done | bytes 405536 | tf_op jit(solution)/shard_map/cond/branch_1_fun/ppermute | solution.py:41
  100.5 6.0 %vocabulary_scores.7.refs_1_ = f32[4,8,48]{2,1,0:T(8,128)S(1)} custom-call(s32[5]{0:T(128)S(1)} %get-tuple-element.73.refs_0_.place_ref.first_ref, bf16[12,4,4224]{2,1,0:T(4,128)(2,1)S(1)} %constant_dynamic-update-slice_fusion.2.refs_0_, bf16[12,4,4224]{2,1,0:T(4,128)(2,1)S(1)} %collective-permute-done.30.refs_1_, bf16[12,4,4224]{2,1,0:T(4,128)(2,1)S(1)} %bitcast.32, ...), custom_call_target="tpu_custom_call" | custom-call | flops 4718592000 | bytes 1572864 | tf_op jit(solution)/shard_map/cond/branch_1_fun/vocabulary_scores/pallas_call | solution.py:532
  106.5 0.6 statistics_by_group.3
  107.1 12.2 %all_to_all.19.every_ref = f32[32,8,96]{2,1,0:T(8,128)S(1)} all-to-all(f32[32,8,96]{2,1,0:T(8,128)S(1)} %statistics_by_group.3), channel_id=1, replica_groups=mesh['section'=2,'tm'=4,'mp'=4] {'section','tm','mp'}, dimensions={0} | all-to-all | bytes 196608 | tf_op jit(solution)/shard_map/cond/branch_1_fun/all_to_all | solution.py:31
  119.4 0.7 hypothesis_scores.3
  120.1 0.6 copy-done.9
  (27 shorter events, 0.1 us)
Async XLA Ops:
  0.1 12.7 %copy-start.7 = (s32[2,8,16]{2,1,0:T(8,128)S(1)}, s32[2,8,16]{2,1,0:T(8,128)}, u32[]{:S(2)}) copy-start(s32[2,8,16]{2,1,0:T(8,128)} %param.21) | copy-start | bytes 3076
  0.1 12.7 %copy-start.5 = (s32[8]{0:T(128)S(1)}, s32[8]{0:T(128)}, u32[]{:S(2)}) copy-start(s32[8]{0:T(128)} %slot_ref.1) | copy-start | bytes 100
  0.1 12.7 %copy-start.6 = (s32[2,8]{1,0:T(2,128)S(1)}, s32[2,8]{1,0:T(2,128)}, u32[]{:S(2)}) copy-start(s32[2,8]{1,0:T(2,128)} %length_ref.1) | copy-start | bytes 196
  6.4 16.7 %all-to-all-start.2 = ((bf16[4,32,1280]{2,1,0:T(8,128)(2,1)}), bf16[4,32,1280]{2,1,0:T(8,128)(2,1)S(1)}, u32[]{:S(2)}, u32[]{:S(2)}) async-start(bf16[4,32,1280]{2,1,0:T(8,128)(2,1)} %get-tuple-element.108), calls=%async_computation.2 | async-start | bytes 655360 | tf_op jit(solution)/shard_map/all_to_all | solution.py:31
  12.8 10.2 %copy-start.2 = (bf16[1280,1024]{1,0:T(8,128)(2,1)S(1)}, bf16[1280,1024]{1,0:T(8,128)(2,1)}, u32[]{:S(2)}) copy-start(bf16[1280,1024]{1,0:T(8,128)(2,1)} %refs_2_.1) | copy-start | bytes 7864324
  19.0 19.0 %copy-start.8 = (s32[4]{0:T(128)S(1)}, s32[4]{0:T(128)}, u32[]{:S(2)}) copy-start(s32[4]{0:T(128)} %param.14) | copy-start | bytes 52
  19.0 1.6 %collective-permute-start.36 = (bf16[272,512]{1,0:T(8,128)(2,1)S(1)}, bf16[272,512]{1,0:T(8,128)(2,1)S(1)}, u32[]{:S(2)}, u32[]{:S(2)}) collective-permute-start(bf16[272,512]{1,0:T(8,128)(2,1)S(1)} %get-tuple-element.107), channel_id=1, source_target_pairs={{0,4},{4,0},{8,12},{12,8},{1,5},{5,1},{9,13},{13,9},{2,6},{6,2},{1... | collective-permute-start | bytes 835592 | tf_op jit(solution)/shard_map/ppermute | solution.py:41
  19.1 17.1 %collective-permute-start.35 = (bf16[272,512]{1,0:T(8,128)(2,1)S(1)}, bf16[272,512]{1,0:T(8,128)(2,1)}, u32[]{:S(2)}, u32[]{:S(2)}) collective-permute-start(bf16[272,512]{1,0:T(8,128)(2,1)S(1)} %get-tuple-element.105), channel_id=1, source_target_pairs={{0,4},{4,0},{8,12},{12,8},{1,5},{5,1},{9,13},{13,9},{2,6},{6,2},{1... | collective-permute-start | bytes 835592 | tf_op jit(solution)/shard_map/ppermute | solution.py:41
  21.4 14.7 %collective-permute-start.37 = (bf16[272,512]{1,0:T(8,128)(2,1)}, bf16[272,512]{1,0:T(8,128)(2,1)}, u32[]{:S(2)}, u32[]{:S(2)}) collective-permute-start(bf16[272,512]{1,0:T(8,128)(2,1)} %add.45), channel_id=1, source_target_pairs={{0,8},{4,12},{8,0},{12,4},{1,9},{5,13},{9,1},{13,5},{2,10},{6,14},... | collective-permute-start | bytes 835592 | tf_op jit(solution)/shard_map/ppermute | solution.py:41
  24.6 13.4 %all-to-all-start.3 = ((bf16[32,8,256]{2,1,0:T(8,128)(2,1)}), bf16[32,8,256]{2,1,0:T(8,128)(2,1)S(1)}, u32[]{:S(2)}, u32[]{:S(2)}) async-start(bf16[32,8,256]{2,1,0:T(8,128)(2,1)} %bitcast.20), calls=%async_computation.3 | async-start | bytes 262144 | tf_op jit(solution)/shard_map/all_to_all | solution.py:31
  30.5 1.9 %collective-permute-start.32 = (s32[1]{0:T(128)}, s32[1]{0:T(128)}, u32[]{:S(2)}, u32[]{:S(2)}) collective-permute-start(s32[1]{0:T(128)} %bitcast.12), channel_id=1, source_target_pairs={{0,4},{4,0},{8,12},{12,8},{1,5},{5,1},{9,13},{13,9},{2,6},{6,2},{1... | collective-permute-start | bytes 20 | tf_op jit(solution)/shard_map/ppermute | solution.py:41
  30.7 3.6 %collective-permute-start.33 = (s32[1]{0:T(128)}, s32[1]{0:T(128)}, u32[]{:S(2)}, u32[]{:S(2)}) collective-permute-start(s32[1]{0:T(128)} %bitcast.12), channel_id=1, source_target_pairs={{0,8},{4,12},{8,0},{12,4},{1,9},{5,13},{9,1},{13,5},{2,10},{6,14},... | collective-permute-start | bytes 20 | tf_op jit(solution)/shard_map/ppermute | solution.py:41
  32.4 3.2 %collective-permute-start.34 = (s32[1]{0:T(128)}, s32[1]{0:T(128)}, u32[]{:S(2)}, u32[]{:S(2)}) collective-permute-start(s32[1]{0:T(128)} %bitcast.12), channel_id=1, source_target_pairs={{0,12},{4,8},{8,4},{12,0},{1,13},{5,9},{9,5},{13,1},{2,14},{6,10},... | collective-permute-start | bytes 20 | tf_op jit(solution)/shard_map/ppermute | solution.py:41
  38.0 25.7 %copy-start.4 = (bf16[272,512]{1,0:T(8,128)(2,1)S(1)}, bf16[272,512]{1,0:T(8,128)(2,1)}, u32[]{:S(2)}) copy-start(bf16[272,512]{1,0:T(8,128)(2,1)} %get-tuple-element.76.refs_3_.refs_0_) | copy-start | bytes 835588 | tf_op jit(solution)/shard_map/cond
  41.9 7.4 %collective-permute-start.16 = (bf16[32,4096]{1,0:T(8,128)(2,1)S(1)}, bf16[32,4096]{1,0:T(8,128)(2,1)S(1)}, u32[]{:S(2)}, u32[]{:S(2)}) collective-permute-start(bf16[32,4096]{1,0:T(8,128)(2,1)S(1)} %get-tuple-element.83), channel_id=1, source_target_pairs={{0,16},{16,0},{1,17},{17,1},{2,18},{18,2},{3,19},{19,3},{4,20},{20... | collective-permute-start | bytes 786440 | tf_op jit(solution)/shard_map/cond/branch_1_fun/ppermute | solution.py:41
  42.7 5.0 %collective-permute-start.17 = (bf16[16,4096]{1,0:T(8,128)(2,1)S(1)}, bf16[16,4096]{1,0:T(8,128)(2,1)S(1)}, u32[]{:S(2)}, u32[]{:S(2)}) collective-permute-start(bf16[16,4096]{1,0:T(8,128)(2,1)S(1)} %get-tuple-element.85), channel_id=1, source_target_pairs={{0,1},{1,0},{2,3},{3,2},{4,5},{5,4},{6,7},{7,6},{8,9},{9,8},{10,11... | collective-permute-start | bytes 393224 | tf_op jit(solution)/shard_map/cond/branch_1_fun/ppermute | solution.py:41
  50.0 5.5 %collective-permute-start.18 = (bf16[16,4096]{1,0:T(8,128)(2,1)S(1)}, bf16[16,4096]{1,0:T(8,128)(2,1)S(1)}, u32[]{:S(2)}, u32[]{:S(2)}) collective-permute-start(bf16[16,4096]{1,0:T(8,128)(2,1)S(1)} %get-tuple-element.87), channel_id=1, source_target_pairs={{0,1},{1,0},{2,3},{3,2},{4,5},{5,4},{6,7},{7,6},{8,9},{9,8},{10,11... | collective-permute-start | bytes 393224 | tf_op jit(solution)/shard_map/cond/branch_1_fun/ppermute | solution.py:41
  51.2 4.3 %collective-permute-start.19 = (bf16[8,4096]{1,0:T(8,128)(2,1)S(1)}, bf16[8,4096]{1,0:T(8,128)(2,1)S(1)}, u32[]{:S(2)}, u32[]{:S(2)}) collective-permute-start(bf16[8,4096]{1,0:T(8,128)(2,1)S(1)} %get-tuple-element.89), channel_id=1, source_target_pairs={{0,16},{16,0},{1,17},{17,1},{2,18},{18,2},{3,19},{19,3},{4,20},{20... | collective-permute-start | bytes 196616 | tf_op jit(solution)/shard_map/cond/branch_1_fun/ppermute | solution.py:41
  56.1 7.7 %collective-permute-start.20 = (bf16[12,4096]{1,0:T(8,128)(2,1)S(1)}, bf16[12,4096]{1,0:T(8,128)(2,1)S(1)}, u32[]{:S(2)}, u32[]{:S(2)}) collective-permute-start(bf16[12,4096]{1,0:T(8,128)(2,1)S(1)} %get-tuple-element.91), channel_id=1, source_target_pairs={{0,2},{1,3},{2,0},{3,1},{4,6},{5,7},{6,4},{7,5},{8,10},{9,11},{10,... | collective-permute-start | bytes 294920 | tf_op jit(solution)/shard_map/cond/branch_1_fun/ppermute | solution.py:41
  65.0 5.0 %collective-permute-start.21 = (bf16[3,4,4224]{2,1,0:T(4,128)(2,1)S(1)}, bf16[3,4,4224]{2,1,0:T(4,128)(2,1)S(1)}, u32[]{:S(2)}, u32[]{:S(2)}) collective-permute-start(bf16[3,4,4224]{2,1,0:T(4,128)(2,1)S(1)} %token_rows.3), channel_id=1, source_target_pairs={{0,1},{1,0},{2,3},{3,2},{4,5},{5,4},{6,7},{7,6},{8,9},{9,8},{10,11... | collective-permute-start | bytes 304136 | tf_op jit(solution)/shard_map/cond/branch_1_fun/ppermute | solution.py:41
  65.1 10.2 %collective-permute-start.22 = (bf16[3,4,4224]{2,1,0:T(4,128)(2,1)S(1)}, bf16[3,4,4224]{2,1,0:T(4,128)(2,1)S(1)}, u32[]{:S(2)}, u32[]{:S(2)}) collective-permute-start(bf16[3,4,4224]{2,1,0:T(4,128)(2,1)S(1)} %token_rows.3), channel_id=1, source_target_pairs={{0,2},{1,3},{2,0},{3,1},{4,6},{5,7},{6,4},{7,5},{8,10},{9,11},{10,... | collective-permute-start | bytes 304136 | tf_op jit(solution)/shard_map/cond/branch_1_fun/ppermute | solution.py:41
  67.8 7.5 %collective-permute-start.23 = (bf16[3,4,4224]{2,1,0:T(4,128)(2,1)S(1)}, bf16[3,4,4224]{2,1,0:T(4,128)(2,1)S(1)}, u32[]{:S(2)}, u32[]{:S(2)}) collective-permute-start(bf16[3,4,4224]{2,1,0:T(4,128)(2,1)S(1)} %token_rows.3), channel_id=1, source_target_pairs={{0,3},{1,2},{2,1},{3,0},{4,7},{5,6},{6,5},{7,4},{8,11},{9,10},{10,... | collective-permute-start | bytes 304136 | tf_op jit(solution)/shard_map/cond/branch_1_fun/ppermute | solution.py:41
  75.4 8.7 %collective-permute-start.24 = (bf16[12,4,4224]{2,1,0:T(4,128)(2,1)S(1)}, bf16[12,4,4224]{2,1,0:T(4,128)(2,1)S(1)}, u32[]{:S(2)}, u32[]{:S(2)}) collective-permute-start(bf16[12,4,4224]{2,1,0:T(4,128)(2,1)S(1)} %bitcast.29), channel_id=1, source_target_pairs={{0,16},{16,0},{1,17},{17,1},{2,18},{18,2},{3,19},{19,3},{4,20},{20... | collective-permute-start | bytes 1216520 | tf_op jit(solution)/shard_map/cond/branch_1_fun/ppermute | solution.py:41
  75.5 8.7 %collective-permute-start.25 = (bf16[12,4,4224]{2,1,0:T(4,128)(2,1)S(1)}, bf16[12,4,4224]{2,1,0:T(4,128)(2,1)S(1)}, u32[]{:S(2)}, u32[]{:S(2)}) collective-permute-start(bf16[12,4,4224]{2,1,0:T(4,128)(2,1)S(1)} %bitcast.30), channel_id=1, source_target_pairs={{0,8},{4,12},{8,0},{12,4},{1,9},{5,13},{9,1},{13,5},{2,10},{6,14},... | collective-permute-start | bytes 1216520 | tf_op jit(solution)/shard_map/cond/branch_1_fun/ppermute | solution.py:41
  84.2 2.7 %collective-permute-start.28 = (bf16[12,4,4224]{2,1,0:T(4,128)(2,1)S(1)}, bf16[12,4,4224]{2,1,0:T(4,128)(2,1)S(1)}, u32[]{:S(2)}, u32[]{:S(2)}) collective-permute-start(bf16[12,4,4224]{2,1,0:T(4,128)(2,1)S(1)} %collective-permute-done.25.refs_0_), channel_id=1, source_target_pairs={{0,4},{4,0},{8,12},{12,8},{1,5},{5,1},{9,13},{13,9},{2,6},{6,2},{1... | collective-permute-start | bytes 1216520 | tf_op jit(solution)/shard_map/cond/branch_1_fun/ppermute | solution.py:41
  84.2 2.7 %collective-permute-start.29 = (bf16[12,4,4224]{2,1,0:T(4,128)(2,1)S(1)}, bf16[12,4,4224]{2,1,0:T(4,128)(2,1)S(1)}, u32[]{:S(2)}, u32[]{:S(2)}) collective-permute-start(bf16[12,4,4224]{2,1,0:T(4,128)(2,1)S(1)} %collective-permute-done.24.refs_2_), channel_id=1, source_target_pairs={{0,4},{4,0},{8,12},{12,8},{1,5},{5,1},{9,13},{13,9},{2,6},{6,2},{1... | collective-permute-start | bytes 1216520 | tf_op jit(solution)/shard_map/cond/branch_1_fun/ppermute | solution.py:41
  84.7 14.1 %collective-permute-start.31 = (bf16[12,4,4224]{2,1,0:T(4,128)(2,1)S(1)}, bf16[12,4,4224]{2,1,0:T(4,128)(2,1)S(1)}, u32[]{:S(2)}, u32[]{:S(2)}) collective-permute-start(bf16[12,4,4224]{2,1,0:T(4,128)(2,1)S(1)} %bitcast.31), channel_id=1, source_target_pairs={{0,4},{4,0},{8,12},{12,8},{1,5},{5,1},{9,13},{13,9},{2,6},{6,2},{1... | collective-permute-start | bytes 1216520 | tf_op jit(solution)/shard_map/cond/branch_1_fun/ppermute | solution.py:41
  84.9 13.6 %collective-permute-start.26 = (bf16[6,4,4224]{2,1,0:T(4,128)(2,1)S(1)}, bf16[6,4,4224]{2,1,0:T(4,128)(2,1)S(1)}, u32[]{:S(2)}, u32[]{:S(2)}) collective-permute-start(bf16[6,4,4224]{2,1,0:T(4,128)(2,1)S(1)} %slice.10), channel_id=1, source_target_pairs={{0,8},{4,12},{8,0},{12,4},{1,9},{5,13},{9,1},{13,5},{2,10},{6,14},... | collective-permute-start | bytes 608264 | tf_op jit(solution)/shard_map/cond/branch_1_fun/ppermute | solution.py:41
  85.2 13.3 %collective-permute-start.27 = (bf16[6,4,4224]{2,1,0:T(4,128)(2,1)S(1)}, bf16[6,4,4224]{2,1,0:T(4,128)(2,1)S(1)}, u32[]{:S(2)}, u32[]{:S(2)}) collective-permute-start(bf16[6,4,4224]{2,1,0:T(4,128)(2,1)S(1)} %slice.11), channel_id=1, source_target_pairs={{0,16},{16,0},{1,17},{17,1},{2,18},{18,2},{3,19},{19,3},{4,20},{20... | collective-permute-start | bytes 608264 | tf_op jit(solution)/shard_map/cond/branch_1_fun/ppermute | solution.py:41
  86.9 5.7 %copy-start.1 = (bf16[2000,4096]{1,0:T(8,128)(2,1)S(1)}, bf16[2000,4096]{1,0:T(8,128)(2,1)}, u32[]{:S(2)}) copy-start(bf16[2000,4096]{1,0:T(8,128)(2,1)} %get-tuple-element.124.refs_4_) | copy-start | bytes 49152004 | tf_op jit(solution)/shard_map/cond
  98.7 1.8 %collective-permute-start.30 = (bf16[12,4,4224]{2,1,0:T(4,128)(2,1)S(1)}, bf16[12,4,4224]{2,1,0:T(4,128)(2,1)S(1)}, u32[]{:S(2)}, u32[]{:S(2)}) collective-permute-start(bf16[12,4,4224]{2,1,0:T(4,128)(2,1)S(1)} %constant_dynamic-update-slice_fusion.2.refs_0_), channel_id=1, source_target_pairs={{0,4},{4,0},{8,12},{12,8},{1,5},{5,1},{9,13},{13,9},{2,6},{6,2},{1... | collective-permute-start | bytes 1216520 | tf_op jit(solution)/shard_map/cond/branch_1_fun/ppermute | solution.py:41
  120.1 0.6 copy-start.9

commit v19 on v18

--- a/solution.py
+++ b/solution.py
@@ -491,7 +491,7 @@
     )(place, slot_utt, *payloads, *blocks)
 
 
-def vocabulary_kernel(tile, count, first_ref, *refs):
+def vocabulary_kernel(tile, count, first_ref, after_ref, *refs):
     sets, (head_ref, out_ref, rows_ref, stat) = refs[:count], refs[count:]
     vocab_rows, width = head_ref.shape
     share = sets[0].shape[0] * FOLD
@@ -524,14 +524,14 @@
             ]
 
 
-def vocabulary_stats(place, sets, head):
+def vocabulary_stats(place, after, sets, head):
     share = sets[0].shape[0] * FOLD
     count = len(sets)
     width = head.shape[1]
     tokens = share * count
     return pl.pallas_call(
         functools.partial(vocabulary_kernel, head.shape[0], count),
-        in_specs=[SCALARS] + [INSIDE] * (count + 1),
+        in_specs=[SCALARS, ANYWHERE] + [INSIDE] * (count + 1),
         out_specs=INSIDE,
         out_shape=jax.ShapeDtypeStruct((count, 8, share), jnp.float32),
         scratch_shapes=[
@@ -545,7 +545,7 @@
         ),
         compiler_params=pltpu.CompilerParams(vmem_limit_bytes=16 << 20),
         name="vocabulary_scores",
-    )(place, *sets, pltpu.with_memory_space_constraint(head, pltpu.VMEM))
+    )(place, after, *sets, pltpu.with_memory_space_constraint(head, pltpu.VMEM))
 
 
 def zero_kernel(after_ref, head_ref, out_ref):
@@ -688,12 +688,14 @@
     by_x = swap(own, "section", 1)
     by_y = swap(own, "tm", 2)
     beside = swap(own, "tm", 1)
-    by_x, by_y, _ = lax.optimization_barrier((by_x, by_y, head_in_vmem(beside, head)))
+    by_x, by_y, zeros = lax.optimization_barrier((by_x, by_y, head_in_vmem(beside, head)))
     across = [swap(by_x[:half], "tm", 2), swap(by_y[half:], "section", 1)]
-    near = vocabulary_stats(place, [by_y, swap(by_y, "tm", 1), by_x, swap(by_x, "tm", 1)], head)
+    near = vocabulary_stats(
+        place, zeros, [by_y, swap(by_y, "tm", 1), by_x, swap(by_x, "tm", 1)], head
+    )
     *across, near = lax.optimization_barrier((*across, near))
     across = jnp.concatenate(across)
-    far = vocabulary_stats(place, [across, swap(across, "tm", 1), own, beside], head)
+    far = vocabulary_stats(place, zeros, [across, swap(across, "tm", 1), own, beside], head)
     stats = [near, far]
     order = ((2, 3, 4, 5), (6, 7, 0, 1))
 

time: 121 us -> 118 us (0.975)
  waiting for transfers between devices: 33.8 us -> 31.1 us
    ppermute x22, waiting for transfers between devices: 31.9 us -> 29.2 us  [swap(): return lax.ppermute(values, axis, pairs)]
  transfers between devices with their start and end apart: 24 -> 24, of which waited for: 14 -> 14; matrix products, arithmetic and copies ran while one was open for 2% -> 2% of each run, Pallas kernels for 11% -> 12%
where the time goes in v19:
time: 118 us; the launch traced here: 117 us
  Pallas kernels  33.6 us (28%)
  waiting for transfers between devices  31.1 us (26%)
  starting transfers between devices  29.7 us (25%)
  blocking collectives  11.4 us (10%)
  local copies, waits for them, and re-layouts  7.03 us (6%)
  between operations  2.65 us (2%)
  other arithmetic  1.63 us (1%)
    ppermute x22, waiting for transfers between devices, swap(): return lax.ppermute(values, axis, pairs)  29.2 us
    ppermute x22, starting transfers between devices, swap(): return lax.ppermute(values, axis, pairs)  18.4 us
    pallas_call x2, Pallas kernels, vocabulary_stats(): pl.pallas_call(functools.partial(vocabulary_kernel, head.shape[0], count)...  11.9 us
    all_to_all x1, blocking collectives, exchange(): return lax.all_to_all(blocks, axis, split_axis=0, concat_axis=0, tiled=True)  11.4 us
    all_to_all x2, starting transfers between devices, exchange(): return lax.all_to_all(blocks, axis, split_axis=0, concat_axis=0, tiled=True)  11.3 us
    pallas_call x1, Pallas kernels, ffn(): pl.pallas_call(functools.partial(ffn_kernel, tile), in_specs=[SCALARS] +...  6.31 us
    pallas_call x1, Pallas kernels, queries_of(): pl.pallas_call(functools.partial(query_kernel, count, depth), in_specs=[S...  6.15 us
    cond x5, local copies, waits for them, and re-layouts  5.73 us
  transfers between devices with their start and end apart: 24, of which 14 were waited for; matrix products, arithmetic and copies ran while one was open for 2% of the time, Pallas kernels for 12%

profile of v19, /device:TPU:0, one launch (start us, length us, event | category | flops | bytes accessed | tf_op | source)
XLA Modules:
  0.0 117.4 jit_solution(4552966234490799524)
XLA Ops:
  0.0 0.1 stack.23.place_ref.after_ref
  0.1 6.3 %encoder_ffn.1 = (bf16[4,32,1280]{2,1,0:T(8,128)(2,1)}, bf16[32,1280]{1,0:T(8,128)(2,1)S(1)}) custom-call(s32[5]{0:T(128)S(1)} %stack.23.place_ref.after_ref, bf16[32,4,1280]{2,1,0:T(4,128)(2,1)} %x_ref.1, bf16[1280,1280]{1,0:T(8,128)(2,1)} %up_ref.1, bf16[1280,1280]{1,0:T(8,128)(2,1)} %down_ref.1), custom_call_target="tpu_custom_call" | custom-call | flops 838860800 | bytes 6553600 | tf_op jit(solution)/shard_map/encoder_ffn/pallas_call | solution.py:121
  6.4 6.3 %all-to-all-start.2 = ((bf16[4,32,1280]{2,1,0:T(8,128)(2,1)}), bf16[4,32,1280]{2,1,0:T(8,128)(2,1)S(1)}, u32[]{:S(2)}, u32[]{:S(2)}) async-start(bf16[4,32,1280]{2,1,0:T(8,128)(2,1)} %get-tuple-element.110), calls=%async_computation.2 | async-start | bytes 655360 | tf_op jit(solution)/shard_map/all_to_all | solution.py:31
  12.7 0.1 reshape.27.tok_ref
  12.8 6.1 %hypothesis_queries.1 = (bf16[272,512]{1,0:T(8,128)(2,1)}, bf16[272,512]{1,0:T(8,128)(2,1)S(1)}, bf16[272,512]{1,0:T(8,128)(2,1)S(1)}, bf16[272,512]{1,0:T(8,128)(2,1)S(1)}) custom-call(s32[5]{0:T(128)S(1)} %stack.23.place_ref.after_ref, s32[8]{0:T(128)S(1)} %copy-done.5, s32[2,8]{1,0:T(2,128)S(1)} %copy-done.6, s32[5]{0:T(128)S(1)} %stack.23.place_ref.after_ref, ...), custom_call_target="tpu_custom_call" | custom-call | flops 1073741824 | bytes 6291456 | tf_op jit(solution)/shard_map/hypothesis_queries/pallas_call | solution.py:228
  19.0 0.1 collective-permute-start.36
  19.1 0.5 collective-permute-start.35
  19.6 1.0 collective-permute-done.36
  20.6 0.8 add.45
  21.4 1.5 %collective-permute-start.37 = (bf16[272,512]{1,0:T(8,128)(2,1)}, bf16[272,512]{1,0:T(8,128)(2,1)}, u32[]{:S(2)}, u32[]{:S(2)}) collective-permute-start(bf16[272,512]{1,0:T(8,128)(2,1)} %add.45), channel_id=1, source_target_pairs={{0,8},{4,12},{8,0},{12,4},{1,9},{5,13},{9,1},{13,5},{2,10},{6,14},... | collective-permute-start | bytes 835592 | tf_op jit(solution)/shard_map/ppermute | solution.py:41
  23.0 0.1 all-to-all-done.2.refs_0_
  23.1 1.5 %frame_keys_values.1 = bf16[256,256]{1,0:T(8,128)(2,1)} custom-call(bf16[4,32,1280]{2,1,0:T(8,128)(2,1)S(1)} %all-to-all-done.2.refs_0_, bf16[32,1280]{1,0:T(8,128)(2,1)S(1)} %get-tuple-element.111.refs_1_, bf16[1280,1024]{1,0:T(8,128)(2,1)S(1)} %copy-done.2, bf16[272,512]{1,0:T(8,128)(2,1)} %get-tuple-element.106.refs_3_), custom_call_target="tpu_custom_call" | custom-call | flops 83886080 | bytes 2621440 | tf_op jit(solution)/shard_map/frame_keys_values/pallas_call | solution.py:287
  24.6 5.0 %all-to-all-start.3 = ((bf16[32,8,256]{2,1,0:T(8,128)(2,1)}), bf16[32,8,256]{2,1,0:T(8,128)(2,1)S(1)}, u32[]{:S(2)}, u32[]{:S(2)}) async-start(bf16[32,8,256]{2,1,0:T(8,128)(2,1)} %bitcast.20), calls=%async_computation.3 | async-start | bytes 262144 | tf_op jit(solution)/shard_map/all_to_all | solution.py:31
  29.6 0.1 reduce_sum.9
  29.7 0.7 fusion
  30.5 0.3 collective-permute-start.32
  30.7 1.7 %collective-permute-start.33 = (s32[1]{0:T(128)}, s32[1]{0:T(128)}, u32[]{:S(2)}, u32[]{:S(2)}) collective-permute-start(s32[1]{0:T(128)} %bitcast.12), channel_id=1, source_target_pairs={{0,8},{4,12},{8,0},{12,4},{1,9},{5,13},{9,1},{13,5},{2,10},{6,14},... | collective-permute-start | bytes 20 | tf_op jit(solution)/shard_map/ppermute | solution.py:41
  33.7 0.6 collective-permute-done.33
  35.0 0.6 collective-permute-done.34
  36.2 1.8 %all-to-all-done.3 = bf16[32,8,256]{2,1,0:T(8,128)(2,1)S(1)} async-done(((bf16[32,8,256]{2,1,0:T(8,128)(2,1)}), bf16[32,8,256]{2,1,0:T(8,128)(2,1)S(1)}, u32[]{:S(2)}, u32[]{:S(2)}) %all-to-all-start.3) | async-done | bytes 131104 | tf_op jit(solution)/shard_map/all_to_all | solution.py:31
  38.0 78.7 %conditional.1 = (f32[2,8]{1,0:T(2,128)S(1)}) conditional(s32[]{:T(128)} %bitcast.13, (s32[5]{0:T(128)S(1)}, s32[8]{0:T(128)S(1)}, s32[4]{0:T(128)S(1)}, bf16[272,512]{1,0:T(8,128)(2,1)}, bf16[272,512]{1,0:T(8,128)(2,1)}, /*index=5*/bf16[272,512]{1,0:T(8,128)(2,1)}, bf16[32,8,256]{2,1,0:T(8,128)(2,1)S(1)}, bf16[512,4096]{1,0:T(8,128)(2,1)}, ...), branch_computations={%region_2.3_spmd, %region_3.4_spmd} | conditional | flops 13186891776 | bytes 100565904 | solution.py:775
  38.0 3.8 %attention_projection.3 = (bf16[32,4096]{1,0:T(8,128)(2,1)S(1)}, bf16[32,4096]{1,0:T(8,128)(2,1)S(1)}, bf16[16,4096]{1,0:T(8,128)(2,1)S(1)}, bf16[16,4096]{1,0:T(8,128)(2,1)S(1)}) custom-call(s32[5]{0:T(128)S(1)} %get-tuple-element.74.refs_0_.place_ref.first_ref, s32[8]{0:T(128)S(1)} %get-tuple-element.75.refs_1_.slot_ref, s32[4]{0:T(128)S(1)} %get-tuple-element.122.refs_2_, ...), custom_call_target="tpu_custom_call" | custom-call | flops 452984832 | bytes 4980736 | tf_op jit(solution)/shard_map/cond/branch_1_fun/attention_projection/pallas_call | solution.py:375
  41.9 0.8 collective-permute-start.16
  42.7 0.6 collective-permute-start.17
  43.3 4.4 %collective-permute-done.17.refs_3_ = bf16[16,4096]{1,0:T(8,128)(2,1)S(1)} collective-permute-done((bf16[16,4096]{1,0:T(8,128)(2,1)S(1)}, bf16[16,4096]{1,0:T(8,128)(2,1)S(1)}, u32[]{:S(2)}, u32[]{:S(2)}) %collective-permute-start.17) | collective-permute-done | bytes 131104 | tf_op jit(solution)/shard_map/cond/branch_1_fun/ppermute | solution.py:41
  47.7 1.6 %collective-permute-done.16.refs_1_ = bf16[32,4096]{1,0:T(8,128)(2,1)S(1)} collective-permute-done((bf16[32,4096]{1,0:T(8,128)(2,1)S(1)}, bf16[32,4096]{1,0:T(8,128)(2,1)S(1)}, u32[]{:S(2)}, u32[]{:S(2)}) %collective-permute-start.16) | collective-permute-done | bytes 262176 | tf_op jit(solution)/shard_map/cond/branch_1_fun/ppermute | solution.py:41
  49.3 0.7 sum_phase.6
  50.0 1.2 %collective-permute-start.18 = (bf16[16,4096]{1,0:T(8,128)(2,1)S(1)}, bf16[16,4096]{1,0:T(8,128)(2,1)S(1)}, u32[]{:S(2)}, u32[]{:S(2)}) collective-permute-start(bf16[16,4096]{1,0:T(8,128)(2,1)S(1)} %get-tuple-element.88), channel_id=1, source_target_pairs={{0,1},{1,0},{2,3},{3,2},{4,5},{5,4},{6,7},{7,6},{8,9},{9,8},{10,11... | collective-permute-start | bytes 393224 | tf_op jit(solution)/shard_map/cond/branch_1_fun/ppermute | solution.py:41
  51.2 1.2 %collective-permute-start.19 = (bf16[8,4096]{1,0:T(8,128)(2,1)S(1)}, bf16[8,4096]{1,0:T(8,128)(2,1)S(1)}, u32[]{:S(2)}, u32[]{:S(2)}) collective-permute-start(bf16[8,4096]{1,0:T(8,128)(2,1)S(1)} %get-tuple-element.90), channel_id=1, source_target_pairs={{0,16},{16,0},{1,17},{17,1},{2,18},{18,2},{3,19},{19,3},{4,20},{20... | collective-permute-start | bytes 196616 | tf_op jit(solution)/shard_map/cond/branch_1_fun/ppermute | solution.py:41
  52.4 3.1 %collective-permute-done.19.refs_3_ = bf16[8,4096]{1,0:T(8,128)(2,1)S(1)} collective-permute-done((bf16[8,4096]{1,0:T(8,128)(2,1)S(1)}, bf16[8,4096]{1,0:T(8,128)(2,1)S(1)}, u32[]{:S(2)}, u32[]{:S(2)}) %collective-permute-start.19) | collective-permute-done | bytes 65568 | tf_op jit(solution)/shard_map/cond/branch_1_fun/ppermute | solution.py:41
  55.4 0.6 sum_phase.7
  56.1 2.3 %collective-permute-start.20 = (bf16[12,4096]{1,0:T(8,128)(2,1)S(1)}, bf16[12,4096]{1,0:T(8,128)(2,1)S(1)}, u32[]{:S(2)}, u32[]{:S(2)}) collective-permute-start(bf16[12,4096]{1,0:T(8,128)(2,1)S(1)} %get-tuple-element.92), channel_id=1, source_target_pairs={{0,2},{1,3},{2,0},{3,1},{4,6},{5,7},{6,4},{7,5},{8,10},{9,11},{10,... | collective-permute-start | bytes 294920 | tf_op jit(solution)/shard_map/cond/branch_1_fun/ppermute | solution.py:41
  58.4 5.3 %collective-permute-done.20.refs_4_ = bf16[12,4096]{1,0:T(8,128)(2,1)S(1)} collective-permute-done((bf16[12,4096]{1,0:T(8,128)(2,1)S(1)}, bf16[12,4096]{1,0:T(8,128)(2,1)S(1)}, u32[]{:S(2)}, u32[]{:S(2)}) %collective-permute-start.20) | collective-permute-done | bytes 98336 | tf_op jit(solution)/shard_map/cond/branch_1_fun/ppermute | solution.py:41
  63.7 1.3 %token_rows.3 = bf16[3,4,4224]{2,1,0:T(4,128)(2,1)S(1)} custom-call(s32[5]{0:T(128)S(1)} %get-tuple-element.74.refs_0_.place_ref.first_ref, s32[8]{0:T(128)S(1)} %get-tuple-element.75.refs_1_.slot_ref, bf16[272,512]{1,0:T(8,128)(2,1)S(1)} %copy-done.4, bf16[272,512]{1,0:T(8,128)(2,1)} %get-tuple-element.78.refs_4_.refs_1_, ...), custom_call_target="tpu_custom_call" | custom-call | tf_op jit(solution)/shard_map/cond/branch_1_fun/token_rows/pallas_call | solution.py:480
  65.0 0.1 collective-permute-start.21
  65.1 2.7 %collective-permute-start.22 = (bf16[3,4,4224]{2,1,0:T(4,128)(2,1)S(1)}, bf16[3,4,4224]{2,1,0:T(4,128)(2,1)S(1)}, u32[]{:S(2)}, u32[]{:S(2)}) collective-permute-start(bf16[3,4,4224]{2,1,0:T(4,128)(2,1)S(1)} %token_rows.3), channel_id=1, source_target_pairs={{0,2},{1,3},{2,0},{3,1},{4,6},{5,7},{6,4},{7,5},{8,10},{9,11},{10,... | collective-permute-start | bytes 304136 | tf_op jit(solution)/shard_map/cond/branch_1_fun/ppermute | solution.py:41
  67.8 1.6 %collective-permute-start.23 = (bf16[3,4,4224]{2,1,0:T(4,128)(2,1)S(1)}, bf16[3,4,4224]{2,1,0:T(4,128)(2,1)S(1)}, u32[]{:S(2)}, u32[]{:S(2)}) collective-permute-start(bf16[3,4,4224]{2,1,0:T(4,128)(2,1)S(1)} %token_rows.3), channel_id=1, source_target_pairs={{0,3},{1,2},{2,1},{3,0},{4,7},{5,6},{6,5},{7,4},{8,11},{9,10},{10,... | collective-permute-start | bytes 304136 | tf_op jit(solution)/shard_map/cond/branch_1_fun/ppermute | solution.py:41
  69.5 0.1 broadcast.7
  69.6 0.1 bitcast_dynamic-update-slice_fusion.7
  69.6 0.3 collective-permute-done.21
  70.0 5.3 %collective-permute-done.22 = bf16[3,4,4224]{2,1,0:T(4,128)(2,1)S(1)} collective-permute-done((bf16[3,4,4224]{2,1,0:T(4,128)(2,1)S(1)}, bf16[3,4,4224]{2,1,0:T(4,128)(2,1)S(1)}, u32[]{:S(2)}, u32[]{:S(2)}) %collective-permute-start.22) | collective-permute-done | bytes 101408 | tf_op jit(solution)/shard_map/cond/branch_1_fun/ppermute | solution.py:41
  75.3 0.1 bitcast_dynamic-update-slice_fusion.5
  75.3 0.1 bitcast_dynamic-update-slice_fusion.4
  75.4 0.1 collective-permute-start.26
  75.5 0.1 collective-permute-start.24
  75.5 0.9 collective-permute-start.25
  76.5 0.7 collective-permute-done.26.after_ref.refs_3_
  77.2 5.7 %copy-done.1 = bf16[2000,4096]{1,0:T(8,128)(2,1)S(1)} copy-done((bf16[2000,4096]{1,0:T(8,128)(2,1)S(1)}, bf16[2000,4096]{1,0:T(8,128)(2,1)}, u32[]{:S(2)}) %copy-start.1) | copy-done | bytes 16384024 | tf_op jit(solution)/shard_map/cond
  82.9 4.4 %collective-permute-done.24.refs_2_ = bf16[12,4,4224]{2,1,0:T(4,128)(2,1)S(1)} collective-permute-done((bf16[12,4,4224]{2,1,0:T(4,128)(2,1)S(1)}, bf16[12,4,4224]{2,1,0:T(4,128)(2,1)S(1)}, u32[]{:S(2)}, u32[]{:S(2)}) %collective-permute-start.24) | collective-permute-done | bytes 405536 | tf_op jit(solution)/shard_map/cond/branch_1_fun/ppermute | solution.py:41
  87.3 0.5 collective-permute-start.30
  87.8 0.1 slice.10
  87.9 0.1 slice.11
  87.9 0.7 collective-permute-start.27
  88.6 1.4 %collective-permute-start.28 = (bf16[6,4,4224]{2,1,0:T(4,128)(2,1)S(1)}, bf16[6,4,4224]{2,1,0:T(4,128)(2,1)S(1)}, u32[]{:S(2)}, u32[]{:S(2)}) collective-permute-start(bf16[6,4,4224]{2,1,0:T(4,128)(2,1)S(1)} %slice.11), channel_id=1, source_target_pairs={{0,16},{16,0},{1,17},{17,1},{2,18},{18,2},{3,19},{19,3},{4,20},{20... | collective-permute-start | bytes 608264 | tf_op jit(solution)/shard_map/cond/branch_1_fun/ppermute | solution.py:41
  90.0 6.0 %vocabulary_scores.6.refs_0_ = f32[4,8,48]{2,1,0:T(8,128)S(1)} custom-call(s32[5]{0:T(128)S(1)} %get-tuple-element.74.refs_0_.place_ref.first_ref, f32[8,128]{1,0:T(8,128)S(1)} %vocabulary_rows.3.after_ref, bf16[12,4,4224]{2,1,0:T(4,128)(2,1)S(1)} %collective-permute-done.25.refs_0_, bf16[12,4,4224]{2,1,0:T(4,128)(2,1)S(1)} %collective-permute-done.29.refs_1_, ...), custom_call_target="tpu_custom_call" | custom-call | flops 4718592000 | bytes 1572864 | tf_op jit(solution)/shard_map/cond/branch_1_fun/vocabulary_scores/pallas_call | solution.py:532
  96.0 0.1 constant_dynamic-update-slice_fusion.3
  96.1 0.1 constant_dynamic-update-slice_fusion.2.refs_0_
  96.2 0.1 collective-permute-start.31
  96.3 1.7 %collective-permute-done.31.refs_1_ = bf16[12,4,4224]{2,1,0:T(4,128)(2,1)S(1)} collective-permute-done((bf16[12,4,4224]{2,1,0:T(4,128)(2,1)S(1)}, bf16[12,4,4224]{2,1,0:T(4,128)(2,1)S(1)}, u32[]{:S(2)}, u32[]{:S(2)}) %collective-permute-start.31) | collective-permute-done | bytes 405536 | tf_op jit(solution)/shard_map/cond/branch_1_fun/ppermute | solution.py:41
  98.0 6.0 %vocabulary_scores.7.refs_1_ = f32[4,8,48]{2,1,0:T(8,128)S(1)} custom-call(s32[5]{0:T(128)S(1)} %get-tuple-element.74.refs_0_.place_ref.first_ref, f32[8,128]{1,0:T(8,128)S(1)} %vocabulary_rows.3.after_ref, bf16[12,4,4224]{2,1,0:T(4,128)(2,1)S(1)} %constant_dynamic-update-slice_fusion.2.refs_0_, bf16[12,4,4224]{2,1,0:T(4,128)(2,1)S(1)} %collective-permute-done.31.refs_1_, ...), custom_call_target="tpu_custom_call" | custom-call | flops 4718592000 | bytes 1572864 | tf_op jit(solution)/shard_map/cond/branch_1_fun/vocabulary_scores/pallas_call | solution.py:532
  103.9 0.6 statistics_by_group.3
  104.6 11.4 %all_to_all.19.every_ref = f32[32,8,96]{2,1,0:T(8,128)S(1)} all-to-all(f32[32,8,96]{2,1,0:T(8,128)S(1)} %statistics_by_group.3), channel_id=1, replica_groups=mesh['section'=2,'tm'=4,'mp'=4] {'section','tm','mp'}, dimensions={0} | all-to-all | bytes 196608 | tf_op jit(solution)/shard_map/cond/branch_1_fun/all_to_all | solution.py:31
  116.0 0.7 hypothesis_scores.3
  116.8 0.6 copy-done.9
  (28 shorter events, 0.1 us)
Async XLA Ops:
  0.1 12.7 %copy-start.7 = (s32[2,8,16]{2,1,0:T(8,128)S(1)}, s32[2,8,16]{2,1,0:T(8,128)}, u32[]{:S(2)}) copy-start(s32[2,8,16]{2,1,0:T(8,128)} %param.21) | copy-start | bytes 3076
  0.1 12.7 %copy-start.5 = (s32[8]{0:T(128)S(1)}, s32[8]{0:T(128)}, u32[]{:S(2)}) copy-start(s32[8]{0:T(128)} %slot_ref.1) | copy-start | bytes 100
  0.1 12.7 %copy-start.6 = (s32[2,8]{1,0:T(2,128)S(1)}, s32[2,8]{1,0:T(2,128)}, u32[]{:S(2)}) copy-start(s32[2,8]{1,0:T(2,128)} %length_ref.1) | copy-start | bytes 196
  6.4 16.7 %all-to-all-start.2 = ((bf16[4,32,1280]{2,1,0:T(8,128)(2,1)}), bf16[4,32,1280]{2,1,0:T(8,128)(2,1)S(1)}, u32[]{:S(2)}, u32[]{:S(2)}) async-start(bf16[4,32,1280]{2,1,0:T(8,128)(2,1)} %get-tuple-element.110), calls=%async_computation.2 | async-start | bytes 655360 | tf_op jit(solution)/shard_map/all_to_all | solution.py:31
  12.8 10.2 %copy-start.2 = (bf16[1280,1024]{1,0:T(8,128)(2,1)S(1)}, bf16[1280,1024]{1,0:T(8,128)(2,1)}, u32[]{:S(2)}) copy-start(bf16[1280,1024]{1,0:T(8,128)(2,1)} %refs_2_.1) | copy-start | bytes 7864324
  19.0 19.0 %copy-start.8 = (s32[4]{0:T(128)S(1)}, s32[4]{0:T(128)}, u32[]{:S(2)}) copy-start(s32[4]{0:T(128)} %param.14) | copy-start | bytes 52
  19.0 1.6 %collective-permute-start.36 = (bf16[272,512]{1,0:T(8,128)(2,1)S(1)}, bf16[272,512]{1,0:T(8,128)(2,1)S(1)}, u32[]{:S(2)}, u32[]{:S(2)}) collective-permute-start(bf16[272,512]{1,0:T(8,128)(2,1)S(1)} %get-tuple-element.109), channel_id=1, source_target_pairs={{0,4},{4,0},{8,12},{12,8},{1,5},{5,1},{9,13},{13,9},{2,6},{6,2},{1... | collective-permute-start | bytes 835592 | tf_op jit(solution)/shard_map/ppermute | solution.py:41
  19.1 17.1 %collective-permute-start.35 = (bf16[272,512]{1,0:T(8,128)(2,1)S(1)}, bf16[272,512]{1,0:T(8,128)(2,1)}, u32[]{:S(2)}, u32[]{:S(2)}) collective-permute-start(bf16[272,512]{1,0:T(8,128)(2,1)S(1)} %get-tuple-element.107), channel_id=1, source_target_pairs={{0,4},{4,0},{8,12},{12,8},{1,5},{5,1},{9,13},{13,9},{2,6},{6,2},{1... | collective-permute-start | bytes 835592 | tf_op jit(solution)/shard_map/ppermute | solution.py:41
  21.4 14.7 %collective-permute-start.37 = (bf16[272,512]{1,0:T(8,128)(2,1)}, bf16[272,512]{1,0:T(8,128)(2,1)}, u32[]{:S(2)}, u32[]{:S(2)}) collective-permute-start(bf16[272,512]{1,0:T(8,128)(2,1)} %add.45), channel_id=1, source_target_pairs={{0,8},{4,12},{8,0},{12,4},{1,9},{5,13},{9,1},{13,5},{2,10},{6,14},... | collective-permute-start | bytes 835592 | tf_op jit(solution)/shard_map/ppermute | solution.py:41
  24.6 13.4 %all-to-all-start.3 = ((bf16[32,8,256]{2,1,0:T(8,128)(2,1)}), bf16[32,8,256]{2,1,0:T(8,128)(2,1)S(1)}, u32[]{:S(2)}, u32[]{:S(2)}) async-start(bf16[32,8,256]{2,1,0:T(8,128)(2,1)} %bitcast.20), calls=%async_computation.3 | async-start | bytes 262144 | tf_op jit(solution)/shard_map/all_to_all | solution.py:31
  30.5 1.9 %collective-permute-start.32 = (s32[1]{0:T(128)}, s32[1]{0:T(128)}, u32[]{:S(2)}, u32[]{:S(2)}) collective-permute-start(s32[1]{0:T(128)} %bitcast.12), channel_id=1, source_target_pairs={{0,4},{4,0},{8,12},{12,8},{1,5},{5,1},{9,13},{13,9},{2,6},{6,2},{1... | collective-permute-start | bytes 20 | tf_op jit(solution)/shard_map/ppermute | solution.py:41
  30.7 3.6 %collective-permute-start.33 = (s32[1]{0:T(128)}, s32[1]{0:T(128)}, u32[]{:S(2)}, u32[]{:S(2)}) collective-permute-start(s32[1]{0:T(128)} %bitcast.12), channel_id=1, source_target_pairs={{0,8},{4,12},{8,0},{12,4},{1,9},{5,13},{9,1},{13,5},{2,10},{6,14},... | collective-permute-start | bytes 20 | tf_op jit(solution)/shard_map/ppermute | solution.py:41
  32.4 3.2 %collective-permute-start.34 = (s32[1]{0:T(128)}, s32[1]{0:T(128)}, u32[]{:S(2)}, u32[]{:S(2)}) collective-permute-start(s32[1]{0:T(128)} %bitcast.12), channel_id=1, source_target_pairs={{0,12},{4,8},{8,4},{12,0},{1,13},{5,9},{9,5},{13,1},{2,14},{6,10},... | collective-permute-start | bytes 20 | tf_op jit(solution)/shard_map/ppermute | solution.py:41
  38.0 25.7 %copy-start.4 = (bf16[272,512]{1,0:T(8,128)(2,1)S(1)}, bf16[272,512]{1,0:T(8,128)(2,1)}, u32[]{:S(2)}) copy-start(bf16[272,512]{1,0:T(8,128)(2,1)} %get-tuple-element.77.refs_3_.refs_0_) | copy-start | bytes 835588 | tf_op jit(solution)/shard_map/cond
  41.9 7.4 %collective-permute-start.16 = (bf16[32,4096]{1,0:T(8,128)(2,1)S(1)}, bf16[32,4096]{1,0:T(8,128)(2,1)S(1)}, u32[]{:S(2)}, u32[]{:S(2)}) collective-permute-start(bf16[32,4096]{1,0:T(8,128)(2,1)S(1)} %get-tuple-element.84), channel_id=1, source_target_pairs={{0,16},{16,0},{1,17},{17,1},{2,18},{18,2},{3,19},{19,3},{4,20},{20... | collective-permute-start | bytes 786440 | tf_op jit(solution)/shard_map/cond/branch_1_fun/ppermute | solution.py:41
  42.7 5.0 %collective-permute-start.17 = (bf16[16,4096]{1,0:T(8,128)(2,1)S(1)}, bf16[16,4096]{1,0:T(8,128)(2,1)S(1)}, u32[]{:S(2)}, u32[]{:S(2)}) collective-permute-start(bf16[16,4096]{1,0:T(8,128)(2,1)S(1)} %get-tuple-element.86), channel_id=1, source_target_pairs={{0,1},{1,0},{2,3},{3,2},{4,5},{5,4},{6,7},{7,6},{8,9},{9,8},{10,11... | collective-permute-start | bytes 393224 | tf_op jit(solution)/shard_map/cond/branch_1_fun/ppermute | solution.py:41
  50.0 5.5 %collective-permute-start.18 = (bf16[16,4096]{1,0:T(8,128)(2,1)S(1)}, bf16[16,4096]{1,0:T(8,128)(2,1)S(1)}, u32[]{:S(2)}, u32[]{:S(2)}) collective-permute-start(bf16[16,4096]{1,0:T(8,128)(2,1)S(1)} %get-tuple-element.88), channel_id=1, source_target_pairs={{0,1},{1,0},{2,3},{3,2},{4,5},{5,4},{6,7},{7,6},{8,9},{9,8},{10,11... | collective-permute-start | bytes 393224 | tf_op jit(solution)/shard_map/cond/branch_1_fun/ppermute | solution.py:41
  51.2 4.3 %collective-permute-start.19 = (bf16[8,4096]{1,0:T(8,128)(2,1)S(1)}, bf16[8,4096]{1,0:T(8,128)(2,1)S(1)}, u32[]{:S(2)}, u32[]{:S(2)}) collective-permute-start(bf16[8,4096]{1,0:T(8,128)(2,1)S(1)} %get-tuple-element.90), channel_id=1, source_target_pairs={{0,16},{16,0},{1,17},{17,1},{2,18},{18,2},{3,19},{19,3},{4,20},{20... | collective-permute-start | bytes 196616 | tf_op jit(solution)/shard_map/cond/branch_1_fun/ppermute | solution.py:41
  56.1 7.7 %collective-permute-start.20 = (bf16[12,4096]{1,0:T(8,128)(2,1)S(1)}, bf16[12,4096]{1,0:T(8,128)(2,1)S(1)}, u32[]{:S(2)}, u32[]{:S(2)}) collective-permute-start(bf16[12,4096]{1,0:T(8,128)(2,1)S(1)} %get-tuple-element.92), channel_id=1, source_target_pairs={{0,2},{1,3},{2,0},{3,1},{4,6},{5,7},{6,4},{7,5},{8,10},{9,11},{10,... | collective-permute-start | bytes 294920 | tf_op jit(solution)/shard_map/cond/branch_1_fun/ppermute | solution.py:41
  65.0 5.0 %collective-permute-start.21 = (bf16[3,4,4224]{2,1,0:T(4,128)(2,1)S(1)}, bf16[3,4,4224]{2,1,0:T(4,128)(2,1)S(1)}, u32[]{:S(2)}, u32[]{:S(2)}) collective-permute-start(bf16[3,4,4224]{2,1,0:T(4,128)(2,1)S(1)} %token_rows.3), channel_id=1, source_target_pairs={{0,1},{1,0},{2,3},{3,2},{4,5},{5,4},{6,7},{7,6},{8,9},{9,8},{10,11... | collective-permute-start | bytes 304136 | tf_op jit(solution)/shard_map/cond/branch_1_fun/ppermute | solution.py:41
  65.1 10.2 %collective-permute-start.22 = (bf16[3,4,4224]{2,1,0:T(4,128)(2,1)S(1)}, bf16[3,4,4224]{2,1,0:T(4,128)(2,1)S(1)}, u32[]{:S(2)}, u32[]{:S(2)}) collective-permute-start(bf16[3,4,4224]{2,1,0:T(4,128)(2,1)S(1)} %token_rows.3), channel_id=1, source_target_pairs={{0,2},{1,3},{2,0},{3,1},{4,6},{5,7},{6,4},{7,5},{8,10},{9,11},{10,... | collective-permute-start | bytes 304136 | tf_op jit(solution)/shard_map/cond/branch_1_fun/ppermute | solution.py:41
  67.8 7.5 %collective-permute-start.23 = (bf16[3,4,4224]{2,1,0:T(4,128)(2,1)S(1)}, bf16[3,4,4224]{2,1,0:T(4,128)(2,1)S(1)}, u32[]{:S(2)}, u32[]{:S(2)}) collective-permute-start(bf16[3,4,4224]{2,1,0:T(4,128)(2,1)S(1)} %token_rows.3), channel_id=1, source_target_pairs={{0,3},{1,2},{2,1},{3,0},{4,7},{5,6},{6,5},{7,4},{8,11},{9,10},{10,... | collective-permute-start | bytes 304136 | tf_op jit(solution)/shard_map/cond/branch_1_fun/ppermute | solution.py:41
  75.4 1.8 %collective-permute-start.26 = (bf16[12,4,4224]{2,1,0:T(4,128)(2,1)S(1)}, bf16[12,4,4224]{2,1,0:T(4,128)(2,1)S(1)}, u32[]{:S(2)}, u32[]{:S(2)}) collective-permute-start(bf16[12,4,4224]{2,1,0:T(4,128)(2,1)S(1)} %bitcast.29), channel_id=1, source_target_pairs={{0,4},{4,0},{8,12},{12,8},{1,5},{5,1},{9,13},{13,9},{2,6},{6,2},{1... | collective-permute-start | bytes 1216520 | tf_op jit(solution)/shard_map/cond/branch_1_fun/ppermute | solution.py:41
  75.5 11.8 %collective-permute-start.24 = (bf16[12,4,4224]{2,1,0:T(4,128)(2,1)S(1)}, bf16[12,4,4224]{2,1,0:T(4,128)(2,1)S(1)}, u32[]{:S(2)}, u32[]{:S(2)}) collective-permute-start(bf16[12,4,4224]{2,1,0:T(4,128)(2,1)S(1)} %bitcast.30), channel_id=1, source_target_pairs={{0,16},{16,0},{1,17},{17,1},{2,18},{18,2},{3,19},{19,3},{4,20},{20... | collective-permute-start | bytes 1216520 | tf_op jit(solution)/shard_map/cond/branch_1_fun/ppermute | solution.py:41
  75.5 11.7 %collective-permute-start.25 = (bf16[12,4,4224]{2,1,0:T(4,128)(2,1)S(1)}, bf16[12,4,4224]{2,1,0:T(4,128)(2,1)S(1)}, u32[]{:S(2)}, u32[]{:S(2)}) collective-permute-start(bf16[12,4,4224]{2,1,0:T(4,128)(2,1)S(1)} %bitcast.31), channel_id=1, source_target_pairs={{0,8},{4,12},{8,0},{12,4},{1,9},{5,13},{9,1},{13,5},{2,10},{6,14},... | collective-permute-start | bytes 1216520 | tf_op jit(solution)/shard_map/cond/branch_1_fun/ppermute | solution.py:41
  77.2 5.7 %copy-start.1 = (bf16[2000,4096]{1,0:T(8,128)(2,1)S(1)}, bf16[2000,4096]{1,0:T(8,128)(2,1)}, u32[]{:S(2)}) copy-start(bf16[2000,4096]{1,0:T(8,128)(2,1)} %get-tuple-element.126.head_ref.refs_4_) | copy-start | bytes 49152004 | tf_op jit(solution)/shard_map/cond
  87.3 2.8 %collective-permute-start.29 = (bf16[12,4,4224]{2,1,0:T(4,128)(2,1)S(1)}, bf16[12,4,4224]{2,1,0:T(4,128)(2,1)S(1)}, u32[]{:S(2)}, u32[]{:S(2)}) collective-permute-start(bf16[12,4,4224]{2,1,0:T(4,128)(2,1)S(1)} %collective-permute-done.25.refs_0_), channel_id=1, source_target_pairs={{0,4},{4,0},{8,12},{12,8},{1,5},{5,1},{9,13},{13,9},{2,6},{6,2},{1... | collective-permute-start | bytes 1216520 | tf_op jit(solution)/shard_map/cond/branch_1_fun/ppermute | solution.py:41
  87.3 2.8 %collective-permute-start.30 = (bf16[12,4,4224]{2,1,0:T(4,128)(2,1)S(1)}, bf16[12,4,4224]{2,1,0:T(4,128)(2,1)S(1)}, u32[]{:S(2)}, u32[]{:S(2)}) collective-permute-start(bf16[12,4,4224]{2,1,0:T(4,128)(2,1)S(1)} %collective-permute-done.24.refs_2_), channel_id=1, source_target_pairs={{0,4},{4,0},{8,12},{12,8},{1,5},{5,1},{9,13},{13,9},{2,6},{6,2},{1... | collective-permute-start | bytes 1216520 | tf_op jit(solution)/shard_map/cond/branch_1_fun/ppermute | solution.py:41
  87.9 8.1 %collective-permute-start.27 = (bf16[6,4,4224]{2,1,0:T(4,128)(2,1)S(1)}, bf16[6,4,4224]{2,1,0:T(4,128)(2,1)S(1)}, u32[]{:S(2)}, u32[]{:S(2)}) collective-permute-start(bf16[6,4,4224]{2,1,0:T(4,128)(2,1)S(1)} %slice.10), channel_id=1, source_target_pairs={{0,8},{4,12},{8,0},{12,4},{1,9},{5,13},{9,1},{13,5},{2,10},{6,14},... | collective-permute-start | bytes 608264 | tf_op jit(solution)/shard_map/cond/branch_1_fun/ppermute | solution.py:41
  88.6 7.4 %collective-permute-start.28 = (bf16[6,4,4224]{2,1,0:T(4,128)(2,1)S(1)}, bf16[6,4,4224]{2,1,0:T(4,128)(2,1)S(1)}, u32[]{:S(2)}, u32[]{:S(2)}) collective-permute-start(bf16[6,4,4224]{2,1,0:T(4,128)(2,1)S(1)} %slice.11), channel_id=1, source_target_pairs={{0,16},{16,0},{1,17},{17,1},{2,18},{18,2},{3,19},{19,3},{4,20},{20... | collective-permute-start | bytes 608264 | tf_op jit(solution)/shard_map/cond/branch_1_fun/ppermute | solution.py:41
  96.2 1.8 %collective-permute-start.31 = (bf16[12,4,4224]{2,1,0:T(4,128)(2,1)S(1)}, bf16[12,4,4224]{2,1,0:T(4,128)(2,1)S(1)}, u32[]{:S(2)}, u32[]{:S(2)}) collective-permute-start(bf16[12,4,4224]{2,1,0:T(4,128)(2,1)S(1)} %constant_dynamic-update-slice_fusion.2.refs_0_), channel_id=1, source_target_pairs={{0,4},{4,0},{8,12},{12,8},{1,5},{5,1},{9,13},{13,9},{2,6},{6,2},{1... | collective-permute-start | bytes 1216520 | tf_op jit(solution)/shard_map/cond/branch_1_fun/ppermute | solution.py:41
  116.8 0.6 copy-start.9

commit v20 on v19

--- a/solution.py
+++ b/solution.py
@@ -637,7 +637,7 @@
         functools.partial(score_kernel, sections, widths),
         in_specs=[SCALARS] * 3 + [INSIDE],
         out_specs=INSIDE,
-        out_shape=jax.ShapeDtypeStruct((slots, hyps), jnp.float32),
+        out_shape=pltpu.HBM((slots, hyps), jnp.float32),
         compiler_params=pltpu.CompilerParams(vmem_limit_bytes=16 << 20),
         name="hypothesis_scores",
     )(place, slot_utt, lengths, every)
@@ -774,7 +774,7 @@
     few = share_rows * 3 // 4
     return lax.cond(
         most[0] <= few * head_devices,
-        functools.partial(rest, (few - few // 3, few // 3), slot_tokens),
+        functools.partial(rest, (few // 2, few - few // 2), slot_tokens),
         functools.partial(rest, (share_rows // 2, share_rows - share_rows // 2), slot_tokens),
         *operands,
     )

time: 118 us -> 117 us (level)
  transfers between devices with their start and end apart: 24 -> 24, of which waited for: 14 -> 16; matrix products, arithmetic and copies ran while one was open for 2% -> 2% of each run, Pallas kernels for 12% -> 12%
where the time goes in v20:
time: 117 us
  Pallas kernels  34.4 us (29%)
  waiting for transfers between devices  30.6 us (26%)
  starting transfers between devices  29.8 us (25%)
  blocking collectives  10.9 us (9%)
  local copies, waits for them, and re-layouts  6.48 us (6%)
  between operations  2.63 us (2%)
  other arithmetic  1.64 us (1%)
    ppermute x22, waiting for transfers between devices, swap(): return lax.ppermute(values, axis, pairs)  28.5 us
    ppermute x22, starting transfers between devices, swap(): return lax.ppermute(values, axis, pairs)  18.5 us
    pallas_call x2, Pallas kernels, vocabulary_stats(): pl.pallas_call(functools.partial(vocabulary_kernel, head.shape[0], count)...  11.9 us
    all_to_all x2, starting transfers between devices, exchange(): return lax.all_to_all(blocks, axis, split_axis=0, concat_axis=0, tiled=True)  11.3 us
    all_to_all x1, blocking collectives, exchange(): return lax.all_to_all(blocks, axis, split_axis=0, concat_axis=0, tiled=True)  10.9 us
    pallas_call x1, Pallas kernels, ffn(): pl.pallas_call(functools.partial(ffn_kernel, tile), in_specs=[SCALARS] +...  6.32 us
    pallas_call x1, Pallas kernels, queries_of(): pl.pallas_call(functools.partial(query_kernel, count, depth), in_specs=[S...  6.16 us
    cond x5, local copies, waits for them, and re-layouts  5.73 us
  transfers between devices with their start and end apart: 24, of which 16 were waited for; matrix products, arithmetic and copies ran while one was open for 2% of the time, Pallas kernels for 12%

profile of v20, /device:TPU:0, one launch (start us, length us, event | category | flops | bytes accessed | tf_op | source)
XLA Modules:
  0.0 116.6 jit_solution(10610378458488682096)
XLA Ops:
  0.0 0.1 stack.23.place_ref.after_ref
  0.1 6.3 %encoder_ffn.1 = (bf16[4,32,1280]{2,1,0:T(8,128)(2,1)}, bf16[32,1280]{1,0:T(8,128)(2,1)S(1)}) custom-call(s32[5]{0:T(128)S(1)} %stack.23.place_ref.after_ref, bf16[32,4,1280]{2,1,0:T(4,128)(2,1)} %x_ref.1, bf16[1280,1280]{1,0:T(8,128)(2,1)} %up_ref.1, bf16[1280,1280]{1,0:T(8,128)(2,1)} %down_ref.1), custom_call_target="tpu_custom_call" | custom-call | flops 838860800 | bytes 6553600 | tf_op jit(solution)/shard_map/encoder_ffn/pallas_call | solution.py:121
  6.4 6.3 %all-to-all-start.2 = ((bf16[4,32,1280]{2,1,0:T(8,128)(2,1)}), bf16[4,32,1280]{2,1,0:T(8,128)(2,1)S(1)}, u32[]{:S(2)}, u32[]{:S(2)}) async-start(bf16[4,32,1280]{2,1,0:T(8,128)(2,1)} %get-tuple-element.110), calls=%async_computation.2 | async-start | bytes 655360 | tf_op jit(solution)/shard_map/all_to_all | solution.py:31
  12.7 0.1 reshape.27.tok_ref
  12.8 6.2 %hypothesis_queries.1 = (bf16[272,512]{1,0:T(8,128)(2,1)}, bf16[272,512]{1,0:T(8,128)(2,1)S(1)}, bf16[272,512]{1,0:T(8,128)(2,1)S(1)}, bf16[272,512]{1,0:T(8,128)(2,1)S(1)}) custom-call(s32[5]{0:T(128)S(1)} %stack.23.place_ref.after_ref, s32[8]{0:T(128)S(1)} %copy-done.5, s32[2,8]{1,0:T(2,128)S(1)} %copy-done.6, s32[5]{0:T(128)S(1)} %stack.23.place_ref.after_ref, ...), custom_call_target="tpu_custom_call" | custom-call | flops 1073741824 | bytes 6291456 | tf_op jit(solution)/shard_map/hypothesis_queries/pallas_call | solution.py:228
  19.0 0.1 collective-permute-start.36
  19.1 0.5 collective-permute-start.35
  19.6 1.0 collective-permute-done.36
  20.6 0.8 add.45
  21.5 1.5 %collective-permute-start.37 = (bf16[272,512]{1,0:T(8,128)(2,1)}, bf16[272,512]{1,0:T(8,128)(2,1)}, u32[]{:S(2)}, u32[]{:S(2)}) collective-permute-start(bf16[272,512]{1,0:T(8,128)(2,1)} %add.45), channel_id=1, source_target_pairs={{0,8},{4,12},{8,0},{12,4},{1,9},{5,13},{9,1},{13,5},{2,10},{6,14},... | collective-permute-start | bytes 835592 | tf_op jit(solution)/shard_map/ppermute | solution.py:41
  23.0 0.1 all-to-all-done.2.refs_0_
  23.1 1.5 %frame_keys_values.1 = bf16[256,256]{1,0:T(8,128)(2,1)} custom-call(bf16[4,32,1280]{2,1,0:T(8,128)(2,1)S(1)} %all-to-all-done.2.refs_0_, bf16[32,1280]{1,0:T(8,128)(2,1)S(1)} %get-tuple-element.111.refs_1_, bf16[1280,1024]{1,0:T(8,128)(2,1)S(1)} %copy-done.2, bf16[272,512]{1,0:T(8,128)(2,1)} %get-tuple-element.106.refs_3_), custom_call_target="tpu_custom_call" | custom-call | flops 83886080 | bytes 2621440 | tf_op jit(solution)/shard_map/frame_keys_values/pallas_call | solution.py:287
  24.6 5.0 %all-to-all-start.3 = ((bf16[32,8,256]{2,1,0:T(8,128)(2,1)}), bf16[32,8,256]{2,1,0:T(8,128)(2,1)S(1)}, u32[]{:S(2)}, u32[]{:S(2)}) async-start(bf16[32,8,256]{2,1,0:T(8,128)(2,1)} %bitcast.20), calls=%async_computation.3 | async-start | bytes 262144 | tf_op jit(solution)/shard_map/all_to_all | solution.py:31
  29.6 0.1 reduce_sum.9
  29.8 0.7 fusion
  30.5 0.3 collective-permute-start.32
  30.7 1.7 %collective-permute-start.33 = (s32[1]{0:T(128)}, s32[1]{0:T(128)}, u32[]{:S(2)}, u32[]{:S(2)}) collective-permute-start(s32[1]{0:T(128)} %bitcast.12), channel_id=1, source_target_pairs={{0,8},{4,12},{8,0},{12,4},{1,9},{5,13},{9,1},{13,5},{2,10},{6,14},... | collective-permute-start | bytes 20 | tf_op jit(solution)/shard_map/ppermute | solution.py:41
  33.7 0.8 collective-permute-done.33
  35.1 0.3 collective-permute-done.34
  36.1 1.9 %all-to-all-done.3 = bf16[32,8,256]{2,1,0:T(8,128)(2,1)S(1)} async-done(((bf16[32,8,256]{2,1,0:T(8,128)(2,1)}), bf16[32,8,256]{2,1,0:T(8,128)(2,1)S(1)}, u32[]{:S(2)}, u32[]{:S(2)}) %all-to-all-start.3) | async-done | bytes 131104 | tf_op jit(solution)/shard_map/all_to_all | solution.py:31
  38.1 78.5 %conditional.1 = (f32[2,8]{1,0:T(2,128)}) conditional(s32[]{:T(128)} %bitcast.13, (s32[5]{0:T(128)S(1)}, s32[8]{0:T(128)S(1)}, s32[4]{0:T(128)S(1)}, bf16[272,512]{1,0:T(8,128)(2,1)}, bf16[272,512]{1,0:T(8,128)(2,1)}, /*index=5*/bf16[272,512]{1,0:T(8,128)(2,1)}, bf16[32,8,256]{2,1,0:T(8,128)(2,1)S(1)}, bf16[512,4096]{1,0:T(8,128)(2,1)}, ...), branch_computations={%region_2.3_spmd, %region_3.4_spmd} | conditional | flops 13186891776 | bytes 100565904 | solution.py:775
  38.1 3.8 %attention_projection.3 = (bf16[24,4096]{1,0:T(8,128)(2,1)S(1)}, bf16[24,4096]{1,0:T(8,128)(2,1)S(1)}, bf16[24,4096]{1,0:T(8,128)(2,1)S(1)}, bf16[24,4096]{1,0:T(8,128)(2,1)S(1)}) custom-call(s32[5]{0:T(128)S(1)} %get-tuple-element.74.refs_0_.place_ref.first_ref, s32[8]{0:T(128)S(1)} %get-tuple-element.75.refs_1_.slot_ref, s32[4]{0:T(128)S(1)} %get-tuple-element.122.refs_2_, ...), custom_call_target="tpu_custom_call" | custom-call | flops 452984832 | bytes 4980736 | tf_op jit(solution)/shard_map/cond/branch_1_fun/attention_projection/pallas_call | solution.py:375
  41.9 0.9 collective-permute-start.16
  42.7 0.5 collective-permute-start.17
  43.2 4.7 %collective-permute-done.16.refs_1_ = bf16[24,4096]{1,0:T(8,128)(2,1)S(1)} collective-permute-done((bf16[24,4096]{1,0:T(8,128)(2,1)S(1)}, bf16[24,4096]{1,0:T(8,128)(2,1)S(1)}, u32[]{:S(2)}, u32[]{:S(2)}) %collective-permute-start.16) | collective-permute-done | bytes 196640 | tf_op jit(solution)/shard_map/cond/branch_1_fun/ppermute | solution.py:41
  47.9 0.9 collective-permute-done.17.refs_3_
  48.8 0.8 sum_phase.6
  49.6 1.3 %collective-permute-start.18 = (bf16[12,4096]{1,0:T(8,128)(2,1)S(1)}, bf16[12,4096]{1,0:T(8,128)(2,1)S(1)}, u32[]{:S(2)}, u32[]{:S(2)}) collective-permute-start(bf16[12,4096]{1,0:T(8,128)(2,1)S(1)} %get-tuple-element.88), channel_id=1, source_target_pairs={{0,1},{1,0},{2,3},{3,2},{4,5},{5,4},{6,7},{7,6},{8,9},{9,8},{10,11... | collective-permute-start | bytes 294920 | tf_op jit(solution)/shard_map/cond/branch_1_fun/ppermute | solution.py:41
  50.9 0.7 collective-permute-start.19
  51.6 3.0 %collective-permute-done.18.refs_1_ = bf16[12,4096]{1,0:T(8,128)(2,1)S(1)} collective-permute-done((bf16[12,4096]{1,0:T(8,128)(2,1)S(1)}, bf16[12,4096]{1,0:T(8,128)(2,1)S(1)}, u32[]{:S(2)}, u32[]{:S(2)}) %collective-permute-start.18) | collective-permute-done | bytes 98336 | tf_op jit(solution)/shard_map/cond/branch_1_fun/ppermute | solution.py:41
  54.6 1.2 %collective-permute-done.19.refs_3_ = bf16[12,4096]{1,0:T(8,128)(2,1)S(1)} collective-permute-done((bf16[12,4096]{1,0:T(8,128)(2,1)S(1)}, bf16[12,4096]{1,0:T(8,128)(2,1)S(1)}, u32[]{:S(2)}, u32[]{:S(2)}) %collective-permute-start.19) | collective-permute-done | bytes 98336 | tf_op jit(solution)/shard_map/cond/branch_1_fun/ppermute | solution.py:41
  55.9 0.7 sum_phase.7
  56.5 2.4 %collective-permute-start.20 = (bf16[12,4096]{1,0:T(8,128)(2,1)S(1)}, bf16[12,4096]{1,0:T(8,128)(2,1)S(1)}, u32[]{:S(2)}, u32[]{:S(2)}) collective-permute-start(bf16[12,4096]{1,0:T(8,128)(2,1)S(1)} %get-tuple-element.92), channel_id=1, source_target_pairs={{0,2},{1,3},{2,0},{3,1},{4,6},{5,7},{6,4},{7,5},{8,10},{9,11},{10,... | collective-permute-start | bytes 294920 | tf_op jit(solution)/shard_map/cond/branch_1_fun/ppermute | solution.py:41
  58.9 4.9 %collective-permute-done.20.refs_4_ = bf16[12,4096]{1,0:T(8,128)(2,1)S(1)} collective-permute-done((bf16[12,4096]{1,0:T(8,128)(2,1)S(1)}, bf16[12,4096]{1,0:T(8,128)(2,1)S(1)}, u32[]{:S(2)}, u32[]{:S(2)}) %collective-permute-start.20) | collective-permute-done | bytes 98336 | tf_op jit(solution)/shard_map/cond/branch_1_fun/ppermute | solution.py:41
  63.9 1.3 %token_rows.3 = bf16[3,4,4224]{2,1,0:T(4,128)(2,1)S(1)} custom-call(s32[5]{0:T(128)S(1)} %get-tuple-element.74.refs_0_.place_ref.first_ref, s32[8]{0:T(128)S(1)} %get-tuple-element.75.refs_1_.slot_ref, bf16[272,512]{1,0:T(8,128)(2,1)S(1)} %copy-done.4, bf16[272,512]{1,0:T(8,128)(2,1)} %get-tuple-element.78.refs_4_.refs_1_, ...), custom_call_target="tpu_custom_call" | custom-call | tf_op jit(solution)/shard_map/cond/branch_1_fun/token_rows/pallas_call | solution.py:480
  65.1 0.1 collective-permute-start.21
  65.2 2.8 %collective-permute-start.22 = (bf16[3,4,4224]{2,1,0:T(4,128)(2,1)S(1)}, bf16[3,4,4224]{2,1,0:T(4,128)(2,1)S(1)}, u32[]{:S(2)}, u32[]{:S(2)}) collective-permute-start(bf16[3,4,4224]{2,1,0:T(4,128)(2,1)S(1)} %token_rows.3), channel_id=1, source_target_pairs={{0,2},{1,3},{2,0},{3,1},{4,6},{5,7},{6,4},{7,5},{8,10},{9,11},{10,... | collective-permute-start | bytes 304136 | tf_op jit(solution)/shard_map/cond/branch_1_fun/ppermute | solution.py:41
  68.1 1.5 %collective-permute-start.23 = (bf16[3,4,4224]{2,1,0:T(4,128)(2,1)S(1)}, bf16[3,4,4224]{2,1,0:T(4,128)(2,1)S(1)}, u32[]{:S(2)}, u32[]{:S(2)}) collective-permute-start(bf16[3,4,4224]{2,1,0:T(4,128)(2,1)S(1)} %token_rows.3), channel_id=1, source_target_pairs={{0,3},{1,2},{2,1},{3,0},{4,7},{5,6},{6,5},{7,4},{8,11},{9,10},{10,... | collective-permute-start | bytes 304136 | tf_op jit(solution)/shard_map/cond/branch_1_fun/ppermute | solution.py:41
  69.6 0.1 broadcast.7
  69.7 0.1 bitcast_dynamic-update-slice_fusion.7
  69.8 2.0 %collective-permute-done.21 = bf16[3,4,4224]{2,1,0:T(4,128)(2,1)S(1)} collective-permute-done((bf16[3,4,4224]{2,1,0:T(4,128)(2,1)S(1)}, bf16[3,4,4224]{2,1,0:T(4,128)(2,1)S(1)}, u32[]{:S(2)}, u32[]{:S(2)}) %collective-permute-start.21) | collective-permute-done | bytes 101408 | tf_op jit(solution)/shard_map/cond/branch_1_fun/ppermute | solution.py:41
  71.8 0.1 bitcast_dynamic-update-slice_fusion.5
  71.9 2.6 %collective-permute-done.23 = bf16[3,4,4224]{2,1,0:T(4,128)(2,1)S(1)} collective-permute-done((bf16[3,4,4224]{2,1,0:T(4,128)(2,1)S(1)}, bf16[3,4,4224]{2,1,0:T(4,128)(2,1)S(1)}, u32[]{:S(2)}, u32[]{:S(2)}) %collective-permute-start.23) | collective-permute-done | bytes 101408 | tf_op jit(solution)/shard_map/cond/branch_1_fun/ppermute | solution.py:41
  74.6 0.1 collective-permute-start.26
  74.6 0.8 collective-permute-start.24
  75.5 0.6 collective-permute-start.25
  76.0 0.3 collective-permute-done.26.after_ref.refs_3_
  76.4 5.7 %copy-done.1 = bf16[2000,4096]{1,0:T(8,128)(2,1)S(1)} copy-done((bf16[2000,4096]{1,0:T(8,128)(2,1)S(1)}, bf16[2000,4096]{1,0:T(8,128)(2,1)}, u32[]{:S(2)}) %copy-start.1) | copy-done | bytes 16384024 | tf_op jit(solution)/shard_map/cond
  82.0 4.4 %collective-permute-done.24.refs_2_ = bf16[12,4,4224]{2,1,0:T(4,128)(2,1)S(1)} collective-permute-done((bf16[12,4,4224]{2,1,0:T(4,128)(2,1)S(1)}, bf16[12,4,4224]{2,1,0:T(4,128)(2,1)S(1)}, u32[]{:S(2)}, u32[]{:S(2)}) %collective-permute-start.24) | collective-permute-done | bytes 405536 | tf_op jit(solution)/shard_map/cond/branch_1_fun/ppermute | solution.py:41
  86.4 0.5 collective-permute-done.25.refs_0_
  86.9 0.5 collective-permute-start.30
  87.4 0.1 slice.10
  87.5 0.1 slice.11
  87.6 0.7 collective-permute-start.27
  88.2 1.5 %collective-permute-start.28 = (bf16[6,4,4224]{2,1,0:T(4,128)(2,1)S(1)}, bf16[6,4,4224]{2,1,0:T(4,128)(2,1)S(1)}, u32[]{:S(2)}, u32[]{:S(2)}) collective-permute-start(bf16[6,4,4224]{2,1,0:T(4,128)(2,1)S(1)} %slice.11), channel_id=1, source_target_pairs={{0,16},{16,0},{1,17},{17,1},{2,18},{18,2},{3,19},{19,3},{4,20},{20... | collective-permute-start | bytes 608264 | tf_op jit(solution)/shard_map/cond/branch_1_fun/ppermute | solution.py:41
  89.8 6.0 %vocabulary_scores.6.refs_0_ = f32[4,8,48]{2,1,0:T(8,128)S(1)} custom-call(s32[5]{0:T(128)S(1)} %get-tuple-element.74.refs_0_.place_ref.first_ref, f32[8,128]{1,0:T(8,128)S(1)} %vocabulary_rows.3.after_ref, bf16[12,4,4224]{2,1,0:T(4,128)(2,1)S(1)} %collective-permute-done.25.refs_0_, bf16[12,4,4224]{2,1,0:T(4,128)(2,1)S(1)} %collective-permute-done.29.refs_1_, ...), custom_call_target="tpu_custom_call" | custom-call | flops 4718592000 | bytes 1572864 | tf_op jit(solution)/shard_map/cond/branch_1_fun/vocabulary_scores/pallas_call | solution.py:532
  95.8 0.1 constant_dynamic-update-slice_fusion.3
  95.8 0.1 constant_dynamic-update-slice_fusion.2.refs_0_
  95.9 0.1 collective-permute-start.31
  96.0 1.7 %collective-permute-done.31.refs_1_ = bf16[12,4,4224]{2,1,0:T(4,128)(2,1)S(1)} collective-permute-done((bf16[12,4,4224]{2,1,0:T(4,128)(2,1)S(1)}, bf16[12,4,4224]{2,1,0:T(4,128)(2,1)S(1)}, u32[]{:S(2)}, u32[]{:S(2)}) %collective-permute-start.31) | collective-permute-done | bytes 405536 | tf_op jit(solution)/shard_map/cond/branch_1_fun/ppermute | solution.py:41
  97.7 6.0 %vocabulary_scores.7.refs_1_ = f32[4,8,48]{2,1,0:T(8,128)S(1)} custom-call(s32[5]{0:T(128)S(1)} %get-tuple-element.74.refs_0_.place_ref.first_ref, f32[8,128]{1,0:T(8,128)S(1)} %vocabulary_rows.3.after_ref, bf16[12,4,4224]{2,1,0:T(4,128)(2,1)S(1)} %constant_dynamic-update-slice_fusion.2.refs_0_, bf16[12,4,4224]{2,1,0:T(4,128)(2,1)S(1)} %collective-permute-done.31.refs_1_, ...), custom_call_target="tpu_custom_call" | custom-call | flops 4718592000 | bytes 1572864 | tf_op jit(solution)/shard_map/cond/branch_1_fun/vocabulary_scores/pallas_call | solution.py:532
  103.7 0.6 statistics_by_group.3
  104.3 10.9 %all_to_all.19.every_ref = f32[32,8,96]{2,1,0:T(8,128)S(1)} all-to-all(f32[32,8,96]{2,1,0:T(8,128)S(1)} %statistics_by_group.3), channel_id=1, replica_groups=mesh['section'=2,'tm'=4,'mp'=4] {'section','tm','mp'}, dimensions={0} | all-to-all | bytes 196608 | tf_op jit(solution)/shard_map/cond/branch_1_fun/all_to_all | solution.py:31
  115.3 1.3 %hypothesis_scores.3 = f32[2,8]{1,0:T(2,128)} custom-call(s32[5]{0:T(128)S(1)} %get-tuple-element.74.refs_0_.place_ref.first_ref, s32[8]{0:T(128)S(1)} %get-tuple-element.75.refs_1_.slot_ref, s32[2,8]{1,0:T(2,128)S(1)} %get-tuple-element.76.length_ref, f32[32,8,96]{2,1,0:T(8,128)S(1)} %all_to_all.19.every_ref), custom_call_target="tpu_custom_call" | custom-call | tf_op jit(solution)/shard_map/cond/branch_1_fun/hypothesis_scores/pallas_call | solution.py:636
  (26 shorter events, 0.2 us)
Async XLA Ops:
  0.1 12.7 %copy-start.7 = (s32[2,8,16]{2,1,0:T(8,128)S(1)}, s32[2,8,16]{2,1,0:T(8,128)}, u32[]{:S(2)}) copy-start(s32[2,8,16]{2,1,0:T(8,128)} %param.21) | copy-start | bytes 3076
  0.1 12.7 %copy-start.5 = (s32[8]{0:T(128)S(1)}, s32[8]{0:T(128)}, u32[]{:S(2)}) copy-start(s32[8]{0:T(128)} %slot_ref.1) | copy-start | bytes 100
  0.1 12.7 %copy-start.6 = (s32[2,8]{1,0:T(2,128)S(1)}, s32[2,8]{1,0:T(2,128)}, u32[]{:S(2)}) copy-start(s32[2,8]{1,0:T(2,128)} %length_ref.1) | copy-start | bytes 196
  6.4 16.7 %all-to-all-start.2 = ((bf16[4,32,1280]{2,1,0:T(8,128)(2,1)}), bf16[4,32,1280]{2,1,0:T(8,128)(2,1)S(1)}, u32[]{:S(2)}, u32[]{:S(2)}) async-start(bf16[4,32,1280]{2,1,0:T(8,128)(2,1)} %get-tuple-element.110), calls=%async_computation.2 | async-start | bytes 655360 | tf_op jit(solution)/shard_map/all_to_all | solution.py:31
  12.8 10.2 %copy-start.2 = (bf16[1280,1024]{1,0:T(8,128)(2,1)S(1)}, bf16[1280,1024]{1,0:T(8,128)(2,1)}, u32[]{:S(2)}) copy-start(bf16[1280,1024]{1,0:T(8,128)(2,1)} %refs_2_.1) | copy-start | bytes 7864324
  19.0 19.0 %copy-start.8 = (s32[4]{0:T(128)S(1)}, s32[4]{0:T(128)}, u32[]{:S(2)}) copy-start(s32[4]{0:T(128)} %param.14) | copy-start | bytes 52
  19.0 1.6 %collective-permute-start.36 = (bf16[272,512]{1,0:T(8,128)(2,1)S(1)}, bf16[272,512]{1,0:T(8,128)(2,1)S(1)}, u32[]{:S(2)}, u32[]{:S(2)}) collective-permute-start(bf16[272,512]{1,0:T(8,128)(2,1)S(1)} %get-tuple-element.109), channel_id=1, source_target_pairs={{0,4},{4,0},{8,12},{12,8},{1,5},{5,1},{9,13},{13,9},{2,6},{6,2},{1... | collective-permute-start | bytes 835592 | tf_op jit(solution)/shard_map/ppermute | solution.py:41
  19.1 17.0 %collective-permute-start.35 = (bf16[272,512]{1,0:T(8,128)(2,1)S(1)}, bf16[272,512]{1,0:T(8,128)(2,1)}, u32[]{:S(2)}, u32[]{:S(2)}) collective-permute-start(bf16[272,512]{1,0:T(8,128)(2,1)S(1)} %get-tuple-element.107), channel_id=1, source_target_pairs={{0,4},{4,0},{8,12},{12,8},{1,5},{5,1},{9,13},{13,9},{2,6},{6,2},{1... | collective-permute-start | bytes 835592 | tf_op jit(solution)/shard_map/ppermute | solution.py:41
  21.5 14.7 %collective-permute-start.37 = (bf16[272,512]{1,0:T(8,128)(2,1)}, bf16[272,512]{1,0:T(8,128)(2,1)}, u32[]{:S(2)}, u32[]{:S(2)}) collective-permute-start(bf16[272,512]{1,0:T(8,128)(2,1)} %add.45), channel_id=1, source_target_pairs={{0,8},{4,12},{8,0},{12,4},{1,9},{5,13},{9,1},{13,5},{2,10},{6,14},... | collective-permute-start | bytes 835592 | tf_op jit(solution)/shard_map/ppermute | solution.py:41
  24.6 13.4 %all-to-all-start.3 = ((bf16[32,8,256]{2,1,0:T(8,128)(2,1)}), bf16[32,8,256]{2,1,0:T(8,128)(2,1)S(1)}, u32[]{:S(2)}, u32[]{:S(2)}) async-start(bf16[32,8,256]{2,1,0:T(8,128)(2,1)} %bitcast.20), calls=%async_computation.3 | async-start | bytes 262144 | tf_op jit(solution)/shard_map/all_to_all | solution.py:31
  30.5 1.9 %collective-permute-start.32 = (s32[1]{0:T(128)}, s32[1]{0:T(128)}, u32[]{:S(2)}, u32[]{:S(2)}) collective-permute-start(s32[1]{0:T(128)} %bitcast.12), channel_id=1, source_target_pairs={{0,4},{4,0},{8,12},{12,8},{1,5},{5,1},{9,13},{13,9},{2,6},{6,2},{1... | collective-permute-start | bytes 20 | tf_op jit(solution)/shard_map/ppermute | solution.py:41
  30.7 3.8 %collective-permute-start.33 = (s32[1]{0:T(128)}, s32[1]{0:T(128)}, u32[]{:S(2)}, u32[]{:S(2)}) collective-permute-start(s32[1]{0:T(128)} %bitcast.12), channel_id=1, source_target_pairs={{0,8},{4,12},{8,0},{12,4},{1,9},{5,13},{9,1},{13,5},{2,10},{6,14},... | collective-permute-start | bytes 20 | tf_op jit(solution)/shard_map/ppermute | solution.py:41
  32.4 3.1 %collective-permute-start.34 = (s32[1]{0:T(128)}, s32[1]{0:T(128)}, u32[]{:S(2)}, u32[]{:S(2)}) collective-permute-start(s32[1]{0:T(128)} %bitcast.12), channel_id=1, source_target_pairs={{0,12},{4,8},{8,4},{12,0},{1,13},{5,9},{9,5},{13,1},{2,14},{6,10},... | collective-permute-start | bytes 20 | tf_op jit(solution)/shard_map/ppermute | solution.py:41
  38.1 25.8 %copy-start.4 = (bf16[272,512]{1,0:T(8,128)(2,1)S(1)}, bf16[272,512]{1,0:T(8,128)(2,1)}, u32[]{:S(2)}) copy-start(bf16[272,512]{1,0:T(8,128)(2,1)} %get-tuple-element.77.refs_3_.refs_0_) | copy-start | bytes 835588 | tf_op jit(solution)/shard_map/cond
  41.9 6.0 %collective-permute-start.16 = (bf16[24,4096]{1,0:T(8,128)(2,1)S(1)}, bf16[24,4096]{1,0:T(8,128)(2,1)S(1)}, u32[]{:S(2)}, u32[]{:S(2)}) collective-permute-start(bf16[24,4096]{1,0:T(8,128)(2,1)S(1)} %get-tuple-element.84), channel_id=1, source_target_pairs={{0,16},{16,0},{1,17},{17,1},{2,18},{18,2},{3,19},{19,3},{4,20},{20... | collective-permute-start | bytes 589832 | tf_op jit(solution)/shard_map/cond/branch_1_fun/ppermute | solution.py:41
  42.7 6.1 %collective-permute-start.17 = (bf16[24,4096]{1,0:T(8,128)(2,1)S(1)}, bf16[24,4096]{1,0:T(8,128)(2,1)S(1)}, u32[]{:S(2)}, u32[]{:S(2)}) collective-permute-start(bf16[24,4096]{1,0:T(8,128)(2,1)S(1)} %get-tuple-element.86), channel_id=1, source_target_pairs={{0,1},{1,0},{2,3},{3,2},{4,5},{5,4},{6,7},{7,6},{8,9},{9,8},{10,11... | collective-permute-start | bytes 589832 | tf_op jit(solution)/shard_map/cond/branch_1_fun/ppermute | solution.py:41
  49.6 5.0 %collective-permute-start.18 = (bf16[12,4096]{1,0:T(8,128)(2,1)S(1)}, bf16[12,4096]{1,0:T(8,128)(2,1)S(1)}, u32[]{:S(2)}, u32[]{:S(2)}) collective-permute-start(bf16[12,4096]{1,0:T(8,128)(2,1)S(1)} %get-tuple-element.88), channel_id=1, source_target_pairs={{0,1},{1,0},{2,3},{3,2},{4,5},{5,4},{6,7},{7,6},{8,9},{9,8},{10,11... | collective-permute-start | bytes 294920 | tf_op jit(solution)/shard_map/cond/branch_1_fun/ppermute | solution.py:41
  50.9 5.0 %collective-permute-start.19 = (bf16[12,4096]{1,0:T(8,128)(2,1)S(1)}, bf16[12,4096]{1,0:T(8,128)(2,1)S(1)}, u32[]{:S(2)}, u32[]{:S(2)}) collective-permute-start(bf16[12,4096]{1,0:T(8,128)(2,1)S(1)} %get-tuple-element.90), channel_id=1, source_target_pairs={{0,16},{16,0},{1,17},{17,1},{2,18},{18,2},{3,19},{19,3},{4,20},{20... | collective-permute-start | bytes 294920 | tf_op jit(solution)/shard_map/cond/branch_1_fun/ppermute | solution.py:41
  56.5 7.3 %collective-permute-start.20 = (bf16[12,4096]{1,0:T(8,128)(2,1)S(1)}, bf16[12,4096]{1,0:T(8,128)(2,1)S(1)}, u32[]{:S(2)}, u32[]{:S(2)}) collective-permute-start(bf16[12,4096]{1,0:T(8,128)(2,1)S(1)} %get-tuple-element.92), channel_id=1, source_target_pairs={{0,2},{1,3},{2,0},{3,1},{4,6},{5,7},{6,4},{7,5},{8,10},{9,11},{10,... | collective-permute-start | bytes 294920 | tf_op jit(solution)/shard_map/cond/branch_1_fun/ppermute | solution.py:41
  65.1 6.6 %collective-permute-start.21 = (bf16[3,4,4224]{2,1,0:T(4,128)(2,1)S(1)}, bf16[3,4,4224]{2,1,0:T(4,128)(2,1)S(1)}, u32[]{:S(2)}, u32[]{:S(2)}) collective-permute-start(bf16[3,4,4224]{2,1,0:T(4,128)(2,1)S(1)} %token_rows.3), channel_id=1, source_target_pairs={{0,1},{1,0},{2,3},{3,2},{4,5},{5,4},{6,7},{7,6},{8,9},{9,8},{10,11... | collective-permute-start | bytes 304136 | tf_op jit(solution)/shard_map/cond/branch_1_fun/ppermute | solution.py:41
  65.2 6.6 %collective-permute-start.22 = (bf16[3,4,4224]{2,1,0:T(4,128)(2,1)S(1)}, bf16[3,4,4224]{2,1,0:T(4,128)(2,1)S(1)}, u32[]{:S(2)}, u32[]{:S(2)}) collective-permute-start(bf16[3,4,4224]{2,1,0:T(4,128)(2,1)S(1)} %token_rows.3), channel_id=1, source_target_pairs={{0,2},{1,3},{2,0},{3,1},{4,6},{5,7},{6,4},{7,5},{8,10},{9,11},{10,... | collective-permute-start | bytes 304136 | tf_op jit(solution)/shard_map/cond/branch_1_fun/ppermute | solution.py:41
  68.1 6.4 %collective-permute-start.23 = (bf16[3,4,4224]{2,1,0:T(4,128)(2,1)S(1)}, bf16[3,4,4224]{2,1,0:T(4,128)(2,1)S(1)}, u32[]{:S(2)}, u32[]{:S(2)}) collective-permute-start(bf16[3,4,4224]{2,1,0:T(4,128)(2,1)S(1)} %token_rows.3), channel_id=1, source_target_pairs={{0,3},{1,2},{2,1},{3,0},{4,7},{5,6},{6,5},{7,4},{8,11},{9,10},{10,... | collective-permute-start | bytes 304136 | tf_op jit(solution)/shard_map/cond/branch_1_fun/ppermute | solution.py:41
  74.6 1.8 %collective-permute-start.26 = (bf16[12,4,4224]{2,1,0:T(4,128)(2,1)S(1)}, bf16[12,4,4224]{2,1,0:T(4,128)(2,1)S(1)}, u32[]{:S(2)}, u32[]{:S(2)}) collective-permute-start(bf16[12,4,4224]{2,1,0:T(4,128)(2,1)S(1)} %bitcast.29), channel_id=1, source_target_pairs={{0,4},{4,0},{8,12},{12,8},{1,5},{5,1},{9,13},{13,9},{2,6},{6,2},{1... | collective-permute-start | bytes 1216520 | tf_op jit(solution)/shard_map/cond/branch_1_fun/ppermute | solution.py:41
  74.6 11.8 %collective-permute-start.24 = (bf16[12,4,4224]{2,1,0:T(4,128)(2,1)S(1)}, bf16[12,4,4224]{2,1,0:T(4,128)(2,1)S(1)}, u32[]{:S(2)}, u32[]{:S(2)}) collective-permute-start(bf16[12,4,4224]{2,1,0:T(4,128)(2,1)S(1)} %bitcast.30), channel_id=1, source_target_pairs={{0,16},{16,0},{1,17},{17,1},{2,18},{18,2},{3,19},{19,3},{4,20},{20... | collective-permute-start | bytes 1216520 | tf_op jit(solution)/shard_map/cond/branch_1_fun/ppermute | solution.py:41
  75.5 11.4 %collective-permute-start.25 = (bf16[12,4,4224]{2,1,0:T(4,128)(2,1)S(1)}, bf16[12,4,4224]{2,1,0:T(4,128)(2,1)S(1)}, u32[]{:S(2)}, u32[]{:S(2)}) collective-permute-start(bf16[12,4,4224]{2,1,0:T(4,128)(2,1)S(1)} %bitcast.31), channel_id=1, source_target_pairs={{0,8},{4,12},{8,0},{12,4},{1,9},{5,13},{9,1},{13,5},{2,10},{6,14},... | collective-permute-start | bytes 1216520 | tf_op jit(solution)/shard_map/cond/branch_1_fun/ppermute | solution.py:41
  76.4 5.7 %copy-start.1 = (bf16[2000,4096]{1,0:T(8,128)(2,1)S(1)}, bf16[2000,4096]{1,0:T(8,128)(2,1)}, u32[]{:S(2)}) copy-start(bf16[2000,4096]{1,0:T(8,128)(2,1)} %get-tuple-element.126.head_ref.refs_4_) | copy-start | bytes 49152004 | tf_op jit(solution)/shard_map/cond
  86.9 2.9 %collective-permute-start.29 = (bf16[12,4,4224]{2,1,0:T(4,128)(2,1)S(1)}, bf16[12,4,4224]{2,1,0:T(4,128)(2,1)S(1)}, u32[]{:S(2)}, u32[]{:S(2)}) collective-permute-start(bf16[12,4,4224]{2,1,0:T(4,128)(2,1)S(1)} %collective-permute-done.25.refs_0_), channel_id=1, source_target_pairs={{0,4},{4,0},{8,12},{12,8},{1,5},{5,1},{9,13},{13,9},{2,6},{6,2},{1... | collective-permute-start | bytes 1216520 | tf_op jit(solution)/shard_map/cond/branch_1_fun/ppermute | solution.py:41
  86.9 2.9 %collective-permute-start.30 = (bf16[12,4,4224]{2,1,0:T(4,128)(2,1)S(1)}, bf16[12,4,4224]{2,1,0:T(4,128)(2,1)S(1)}, u32[]{:S(2)}, u32[]{:S(2)}) collective-permute-start(bf16[12,4,4224]{2,1,0:T(4,128)(2,1)S(1)} %collective-permute-done.24.refs_2_), channel_id=1, source_target_pairs={{0,4},{4,0},{8,12},{12,8},{1,5},{5,1},{9,13},{13,9},{2,6},{6,2},{1... | collective-permute-start | bytes 1216520 | tf_op jit(solution)/shard_map/cond/branch_1_fun/ppermute | solution.py:41
  87.6 8.2 %collective-permute-start.27 = (bf16[6,4,4224]{2,1,0:T(4,128)(2,1)S(1)}, bf16[6,4,4224]{2,1,0:T(4,128)(2,1)S(1)}, u32[]{:S(2)}, u32[]{:S(2)}) collective-permute-start(bf16[6,4,4224]{2,1,0:T(4,128)(2,1)S(1)} %slice.10), channel_id=1, source_target_pairs={{0,8},{4,12},{8,0},{12,4},{1,9},{5,13},{9,1},{13,5},{2,10},{6,14},... | collective-permute-start | bytes 608264 | tf_op jit(solution)/shard_map/cond/branch_1_fun/ppermute | solution.py:41
  88.2 7.5 %collective-permute-start.28 = (bf16[6,4,4224]{2,1,0:T(4,128)(2,1)S(1)}, bf16[6,4,4224]{2,1,0:T(4,128)(2,1)S(1)}, u32[]{:S(2)}, u32[]{:S(2)}) collective-permute-start(bf16[6,4,4224]{2,1,0:T(4,128)(2,1)S(1)} %slice.11), channel_id=1, source_target_pairs={{0,16},{16,0},{1,17},{17,1},{2,18},{18,2},{3,19},{19,3},{4,20},{20... | collective-permute-start | bytes 608264 | tf_op jit(solution)/shard_map/cond/branch_1_fun/ppermute | solution.py:41
  95.9 1.8 %collective-permute-start.31 = (bf16[12,4,4224]{2,1,0:T(4,128)(2,1)S(1)}, bf16[12,4,4224]{2,1,0:T(4,128)(2,1)S(1)}, u32[]{:S(2)}, u32[]{:S(2)}) collective-permute-start(bf16[12,4,4224]{2,1,0:T(4,128)(2,1)S(1)} %constant_dynamic-update-slice_fusion.2.refs_0_), channel_id=1, source_target_pairs={{0,4},{4,0},{8,12},{12,8},{1,5},{5,1},{9,13},{13,9},{2,6},{6,2},{1... | collective-permute-start | bytes 1216520 | tf_op jit(solution)/shard_map/cond/branch_1_fun/ppermute | solution.py:41

commit v21 on v20

--- a/solution.py
+++ b/solution.py
@@ -69,9 +69,10 @@
     return copies
 
 
-def ffn_kernel(tile, place_ref, x_ref, up_ref, down_ref, *refs):
-    out_ref, own_ref, inputs, rows, up, down, x_sem, up_sem, down_sem = refs
-    count, share, width = out_ref.shape
+def ffn_kernel(tile, count, place_ref, x_ref, up_ref, down_ref, *refs):
+    outs = refs[:count]
+    own_ref, inputs, rows, up, down, x_sem, up_sem, down_sem = refs[count:]
+    share = own_ref.shape[0]
     tiles = up_ref.shape[1] // tile
     x_copy = start_copies(lambda i: x_ref, lambda i: inputs, x_sem, 1)[0]
     up_copies = start_copies(
@@ -100,8 +101,10 @@
         down_copies[number].wait()
         product = dot(inner[number], down[number])
         total = product if total is None else total + product
-    for part in range(count):
-        out_ref[part] = total[part * share : (part + 1) * share, :].astype(jnp.bfloat16)
+    rows[...] = total
+    for distance in range(count):
+        start = pl.multiple_of((place_ref[2] ^ distance) * share, share)
+        outs[distance][...] = rows[pl.ds(start, share), :].astype(jnp.bfloat16)
 
 
 def in_hbm(values):
@@ -119,13 +122,10 @@
     tile = 256
     tiles = up.shape[1] // tile
     return pl.pallas_call(
-        functools.partial(ffn_kernel, tile),
+        functools.partial(ffn_kernel, tile, count),
         in_specs=[SCALARS] + [ANYWHERE] * 3,
-        out_specs=[INSIDE] * 2,
-        out_shape=[
-            jax.ShapeDtypeStruct((count, share, width), jnp.bfloat16),
-            jax.ShapeDtypeStruct((share, width), jnp.bfloat16),
-        ],
+        out_specs=[INSIDE] * (count + 1),
+        out_shape=[jax.ShapeDtypeStruct((share, width), jnp.bfloat16)] * (count + 1),
         scratch_shapes=[
             pltpu.VMEM(enc_in.shape, jnp.bfloat16),
             pltpu.VMEM((rows, width), jnp.float32),
@@ -250,13 +250,13 @@
 
 
 def kv_kernel(sections, utterances, widths, *refs):
-    parts_ref, own_ref, w_ref, after_ref, out_ref = refs
+    parts, (own_ref, w_ref, out_ref) = refs[:-3], refs[-3:]
     rows = own_ref.shape[0]
     frames = rows // utterances
     total = own_ref[...].astype(jnp.float32)
-    summed = parts_ref[0].astype(jnp.float32)
-    for part in range(1, parts_ref.shape[0]):
-        summed += parts_ref[part].astype(jnp.float32)
+    summed = parts[0][...].astype(jnp.float32)
+    for part in parts[1:]:
+        summed += part[...].astype(jnp.float32)
     states = layer_norm(total + summed).astype(jnp.bfloat16)
     to = lax.broadcasted_iota(jnp.int32, (rows, rows), 0)
     come = lax.broadcasted_iota(jnp.int32, (rows, rows), 1)
@@ -282,11 +282,11 @@
                 out_ref[start : start + per_kv * frames, :] = block
 
 
-def keys_values_of(parts, own, weights, after, sections, utterances, widths):
+def keys_values_of(parts, own, weights, sections, utterances, widths):
     rows = sections * widths * own.shape[0]
     return pl.pallas_call(
         functools.partial(kv_kernel, sections, utterances, widths),
-        in_specs=[INSIDE] * 3 + [ANYWHERE],
+        in_specs=[INSIDE] * (len(parts) + 2),
         out_specs=INSIDE,
         out_shape=jax.ShapeDtypeStruct((rows, 2 * HD), jnp.bfloat16),
         cost_estimate=pl.CostEstimate(
@@ -296,7 +296,7 @@
         ),
         compiler_params=pltpu.CompilerParams(vmem_limit_bytes=24 << 20),
         name="frame_keys_values",
-    )(parts, own, weights, after)
+    )(*parts, own, weights)
 
 
 def choice_of_payload(place_ref, slot_ref, slots):
@@ -741,8 +741,10 @@
     place = jnp.stack([section_pos, group_pos, width_pos, vocab_start, head_pos])
     place = place.astype(jnp.int32)
 
-    parts, own_frames = ffn(place, enc_in, ffn_up, ffn_down, width_count)
-    parts = exchange(parts, "mp")
+    *parts, own_frames = ffn(place, enc_in, ffn_up, ffn_down, width_count)
+    parts = [parts[0]] + [
+        swap(parts[distance], "mp", distance) for distance in range(1, width_count)
+    ]
 
     blocks = queries_of(
         place,
@@ -758,9 +760,7 @@
     crossing = blocks[2] + swap(blocks[3], "tm", 1)
     payloads = [blocks[0], swap(blocks[1], "tm", 1), swap(crossing, "tm", 2)]
 
-    sent = keys_values_of(
-        parts, own_frames, kv_proj, blocks[0], section_count, utterances, width_count
-    )
+    sent = keys_values_of(parts, own_frames, kv_proj, section_count, utterances, width_count)
     frames_all = all_devices * (frame_rows // width_count)
     keys_values = exchange(sent.reshape(all_devices, -1, 2 * HD), ALL).reshape(frames_all, 2 * HD)
 

time: 117 us -> 117 us (level)
  waiting for transfers between devices: 30.6 us -> 33.9 us
  Pallas kernels: 34.4 us -> 31.2 us
    all_to_all x2 -> x1, starting transfers between devices: 11.3 us -> 4.95 us  [exchange(): return lax.all_to_all(blocks, axis, split_axis=0, concat_axis=0, tiled=True)]
    ppermute x22 -> x25, starting transfers between devices: 18.5 us -> 24.4 us  [swap(): return lax.ppermute(values, axis, pairs)]
    ppermute x22 -> x25, waiting for transfers between devices: 28.5 us -> 32.1 us  [swap(): return lax.ppermute(values, axis, pairs)]
    cond x5 -> x3, local copies, waits for them, and re-layouts: 5.73 us -> 5.73 us
  transfers between devices with their start and end apart: 24 -> 26, of which waited for: 16 -> 14; matrix products, arithmetic and copies ran while one was open for 2% -> 1% of each run, Pallas kernels for 12% -> 11%
where the time goes in v21:
time: 117 us
  waiting for transfers between devices  33.9 us (29%)
  Pallas kernels  31.2 us (27%)
  starting transfers between devices  29.3 us (25%)
  blocking collectives  11.2 us (10%)
  local copies, waits for them, and re-layouts  7.17 us (6%)
  between operations  2.76 us (2%)
    ppermute x25, waiting for transfers between devices, swap(): return lax.ppermute(values, axis, pairs)  32.1 us
    ppermute x25, starting transfers between devices, swap(): return lax.ppermute(values, axis, pairs)  24.4 us
    pallas_call x2, Pallas kernels, vocabulary_stats(): pl.pallas_call(functools.partial(vocabulary_kernel, head.shape[0], count)...  11.4 us
    all_to_all x1, blocking collectives, exchange(): return lax.all_to_all(blocks, axis, split_axis=0, concat_axis=0, tiled=True)  11.2 us
    cond x3, local copies, waits for them, and re-layouts  5.73 us
    pallas_call x1, Pallas kernels, ffn(): pl.pallas_call(functools.partial(ffn_kernel, tile, count), in_specs=[SCAL...  5.61 us
    pallas_call x1, Pallas kernels, queries_of(): pl.pallas_call(functools.partial(query_kernel, count, depth), in_specs=[S...  5.37 us
    all_to_all x1, starting transfers between devices, exchange(): return lax.all_to_all(blocks, axis, split_axis=0, concat_axis=0, tiled=True)  4.95 us
  transfers between devices with their start and end apart: 26, of which 14 were waited for; matrix products, arithmetic and copies ran while one was open for 1% of the time, Pallas kernels for 11%

profile of v21, /device:TPU:0, one launch (start us, length us, event | category | flops | bytes accessed | tf_op | source)
XLA Modules:
  0.0 116.6 jit_solution(11187896947297001013)
XLA Ops:
  0.0 0.8 reshape.27.tok_ref
  0.8 0.1 stack.23.place_ref.after_ref
  0.9 5.4 %hypothesis_queries.1 = (bf16[272,512]{1,0:T(8,128)(2,1)S(1)}, bf16[272,512]{1,0:T(8,128)(2,1)S(1)}, bf16[272,512]{1,0:T(8,128)(2,1)S(1)}, bf16[272,512]{1,0:T(8,128)(2,1)S(1)}) custom-call(s32[5]{0:T(128)S(1)} %stack.23.place_ref.after_ref, s32[8]{0:T(128)} %slot_ref.1, s32[2,8]{1,0:T(2,128)} %length_ref.1, s32[5]{0:T(128)S(1)} %stack.23.place_ref.after_ref, ...), custom_call_target="tpu_custom_call" | custom-call | flops 1073741824 | bytes 6291456 | tf_op jit(solution)/shard_map/hypothesis_queries/pallas_call | solution.py:228
  6.2 0.5 collective-permute-start.36
  6.8 5.6 %encoder_ffn.1 = (bf16[32,1280]{1,0:T(8,128)(2,1)S(1)}, bf16[32,1280]{1,0:T(8,128)(2,1)S(1)}, bf16[32,1280]{1,0:T(8,128)(2,1)S(1)}, bf16[32,1280]{1,0:T(8,128)(2,1)S(1)}, bf16[32,1280]{1,0:T(8,128)(2,1)S(1)}) custom-call(s32[5]{0:T(128)S(1)} %stack.23.place_ref.after_ref, bf16[32,4,1280]{2,1,0:T(4,128)(2,1)} %x_ref.1, bf16[1280,1280]{1,0:T(8,128)(2,1)} %up_ref.1, ...), custom_call_target="tpu_custom_call" | custom-call | flops 838860800 | bytes 6553600 | tf_op jit(solution)/shard_map/encoder_ffn/pallas_call | solution.py:124
  12.4 2.8 %collective-permute-start.38 = (bf16[32,1280]{1,0:T(8,128)(2,1)S(1)}, bf16[32,1280]{1,0:T(8,128)(2,1)S(1)}, u32[]{:S(2)}, u32[]{:S(2)}) collective-permute-start(bf16[32,1280]{1,0:T(8,128)(2,1)S(1)} %get-tuple-element.114), channel_id=1, source_target_pairs={{0,1},{1,0},{2,3},{3,2},{4,5},{5,4},{6,7},{7,6},{8,9},{9,8},{10,11... | collective-permute-start | bytes 245768 | tf_op jit(solution)/shard_map/ppermute | solution.py:41
  15.2 2.6 %collective-permute-start.39 = (bf16[32,1280]{1,0:T(8,128)(2,1)S(1)}, bf16[32,1280]{1,0:T(8,128)(2,1)S(1)}, u32[]{:S(2)}, u32[]{:S(2)}) collective-permute-start(bf16[32,1280]{1,0:T(8,128)(2,1)S(1)} %get-tuple-element.115), channel_id=1, source_target_pairs={{0,2},{1,3},{2,0},{3,1},{4,6},{5,7},{6,4},{7,5},{8,10},{9,11},{10,... | collective-permute-start | bytes 245768 | tf_op jit(solution)/shard_map/ppermute | solution.py:41
  17.8 0.1 add.45
  17.9 1.8 %collective-permute-start.37 = (bf16[272,512]{1,0:T(8,128)(2,1)S(1)}, bf16[272,512]{1,0:T(8,128)(2,1)S(1)}, u32[]{:S(2)}, u32[]{:S(2)}) collective-permute-start(bf16[272,512]{1,0:T(8,128)(2,1)S(1)} %add.45), channel_id=1, source_target_pairs={{0,8},{4,12},{8,0},{12,4},{1,9},{5,13},{9,1},{13,5},{2,10},{6,14},... | collective-permute-start | bytes 835592 | tf_op jit(solution)/shard_map/ppermute | solution.py:41
  19.7 5.0 %collective-permute-done.39.refs_2_ = bf16[32,1280]{1,0:T(8,128)(2,1)S(1)} collective-permute-done((bf16[32,1280]{1,0:T(8,128)(2,1)S(1)}, bf16[32,1280]{1,0:T(8,128)(2,1)S(1)}, u32[]{:S(2)}, u32[]{:S(2)}) %collective-permute-start.39) | collective-permute-done | bytes 81952 | tf_op jit(solution)/shard_map/ppermute | solution.py:41
  24.7 1.5 %frame_keys_values.1 = bf16[256,256]{1,0:T(8,128)(2,1)} custom-call(bf16[32,1280]{1,0:T(8,128)(2,1)S(1)} %get-tuple-element.113.refs_0_, bf16[32,1280]{1,0:T(8,128)(2,1)S(1)} %collective-permute-done.38.refs_1_, bf16[32,1280]{1,0:T(8,128)(2,1)S(1)} %collective-permute-done.39.refs_2_, bf16[32,1280]{1,0:T(8,128)(2,1)S(1)} %collective-permute-done.40.refs_3_, ...), custom_call_target="tpu_custom_call" | custom-call | flops 83886080 | bytes 2621440 | tf_op jit(solution)/shard_map/frame_keys_values/pallas_call | solution.py:287
  26.2 4.9 %all-to-all-start.2 = ((bf16[32,8,256]{2,1,0:T(8,128)(2,1)}), bf16[32,8,256]{2,1,0:T(8,128)(2,1)S(1)}, u32[]{:S(2)}, u32[]{:S(2)}) async-start(bf16[32,8,256]{2,1,0:T(8,128)(2,1)} %bitcast.20), calls=%async_computation.2 | async-start | bytes 262144 | tf_op jit(solution)/shard_map/all_to_all | solution.py:31
  31.2 0.1 reduce_sum.9
  31.3 0.7 fusion
  32.0 0.3 collective-permute-start.32
  32.3 1.7 %collective-permute-start.33 = (s32[1]{0:T(128)}, s32[1]{0:T(128)}, u32[]{:S(2)}, u32[]{:S(2)}) collective-permute-start(s32[1]{0:T(128)} %bitcast.12), channel_id=1, source_target_pairs={{0,8},{4,12},{8,0},{12,4},{1,9},{5,13},{9,1},{13,5},{2,10},{6,14},... | collective-permute-start | bytes 20 | tf_op jit(solution)/shard_map/ppermute | solution.py:41
  35.4 0.5 collective-permute-done.33
  36.6 0.6 collective-permute-done.34
  37.8 1.8 %all-to-all-done.2 = bf16[32,8,256]{2,1,0:T(8,128)(2,1)S(1)} async-done(((bf16[32,8,256]{2,1,0:T(8,128)(2,1)}), bf16[32,8,256]{2,1,0:T(8,128)(2,1)S(1)}, u32[]{:S(2)}, u32[]{:S(2)}) %all-to-all-start.2) | async-done | bytes 131104 | tf_op jit(solution)/shard_map/all_to_all | solution.py:31
  39.6 77.0 %conditional.1 = (f32[2,8]{1,0:T(2,128)}) conditional(s32[]{:T(128)} %bitcast.13, (s32[5]{0:T(128)S(1)}, s32[8]{0:T(128)S(1)}, s32[4]{0:T(128)S(1)}, bf16[272,512]{1,0:T(8,128)(2,1)S(1)}, bf16[272,512]{1,0:T(8,128)(2,1)S(1)}, /*index=5*/bf16[272,512]{1,0:T(8,128)(2,1)S(1)}, bf16[32,8,256]{2,1,0:T(8,128)(2,1)S(1)}, bf16[512,4096]{1,0:T(8,128)(2,1)}, ...), branch_computations={%region_2.3_spmd, %region_3.4_spmd} | conditional | flops 13186891776 | bytes 99451768 | solution.py:775
  39.6 3.2 %attention_projection.3 = (bf16[24,4096]{1,0:T(8,128)(2,1)S(1)}, bf16[24,4096]{1,0:T(8,128)(2,1)S(1)}, bf16[24,4096]{1,0:T(8,128)(2,1)S(1)}, bf16[24,4096]{1,0:T(8,128)(2,1)S(1)}) custom-call(s32[5]{0:T(128)S(1)} %get-tuple-element.74.refs_0_.place_ref.first_ref, s32[8]{0:T(128)S(1)} %get-tuple-element.75.refs_1_.slot_ref, s32[4]{0:T(128)S(1)} %get-tuple-element.128.refs_2_, ...), custom_call_target="tpu_custom_call" | custom-call | flops 452984832 | bytes 4980736 | tf_op jit(solution)/shard_map/cond/branch_1_fun/attention_projection/pallas_call | solution.py:375
  42.8 0.8 collective-permute-start.16
  43.7 0.6 collective-permute-start.17
  44.2 4.6 %collective-permute-done.16.refs_1_ = bf16[24,4096]{1,0:T(8,128)(2,1)S(1)} collective-permute-done((bf16[24,4096]{1,0:T(8,128)(2,1)S(1)}, bf16[24,4096]{1,0:T(8,128)(2,1)S(1)}, u32[]{:S(2)}, u32[]{:S(2)}) %collective-permute-start.16) | collective-permute-done | bytes 196640 | tf_op jit(solution)/shard_map/cond/branch_1_fun/ppermute | solution.py:41
  48.8 0.9 collective-permute-done.17.refs_3_
  49.8 0.8 sum_phase.6
  50.5 1.2 %collective-permute-start.18 = (bf16[12,4096]{1,0:T(8,128)(2,1)S(1)}, bf16[12,4096]{1,0:T(8,128)(2,1)S(1)}, u32[]{:S(2)}, u32[]{:S(2)}) collective-permute-start(bf16[12,4096]{1,0:T(8,128)(2,1)S(1)} %get-tuple-element.88), channel_id=1, source_target_pairs={{0,1},{1,0},{2,3},{3,2},{4,5},{5,4},{6,7},{7,6},{8,9},{9,8},{10,11... | collective-permute-start | bytes 294920 | tf_op jit(solution)/shard_map/cond/branch_1_fun/ppermute | solution.py:41
  51.7 0.8 collective-permute-start.19
  52.6 3.0 %collective-permute-done.18.refs_1_ = bf16[12,4096]{1,0:T(8,128)(2,1)S(1)} collective-permute-done((bf16[12,4096]{1,0:T(8,128)(2,1)S(1)}, bf16[12,4096]{1,0:T(8,128)(2,1)S(1)}, u32[]{:S(2)}, u32[]{:S(2)}) %collective-permute-start.18) | collective-permute-done | bytes 98336 | tf_op jit(solution)/shard_map/cond/branch_1_fun/ppermute | solution.py:41
  55.6 1.1 collective-permute-done.19.refs_3_
  56.7 0.7 sum_phase.7
  57.4 2.3 %collective-permute-start.20 = (bf16[12,4096]{1,0:T(8,128)(2,1)S(1)}, bf16[12,4096]{1,0:T(8,128)(2,1)S(1)}, u32[]{:S(2)}, u32[]{:S(2)}) collective-permute-start(bf16[12,4096]{1,0:T(8,128)(2,1)S(1)} %get-tuple-element.92), channel_id=1, source_target_pairs={{0,2},{1,3},{2,0},{3,1},{4,6},{5,7},{6,4},{7,5},{8,10},{9,11},{10,... | collective-permute-start | bytes 294920 | tf_op jit(solution)/shard_map/cond/branch_1_fun/ppermute | solution.py:41
  59.7 5.1 %collective-permute-done.20.refs_4_ = bf16[12,4096]{1,0:T(8,128)(2,1)S(1)} collective-permute-done((bf16[12,4096]{1,0:T(8,128)(2,1)S(1)}, bf16[12,4096]{1,0:T(8,128)(2,1)S(1)}, u32[]{:S(2)}, u32[]{:S(2)}) %collective-permute-start.20) | collective-permute-done | bytes 98336 | tf_op jit(solution)/shard_map/cond/branch_1_fun/ppermute | solution.py:41
  64.8 0.7 token_rows.3
  65.5 0.1 collective-permute-start.21
  65.6 2.8 %collective-permute-start.22 = (bf16[3,4,4224]{2,1,0:T(4,128)(2,1)S(1)}, bf16[3,4,4224]{2,1,0:T(4,128)(2,1)S(1)}, u32[]{:S(2)}, u32[]{:S(2)}) collective-permute-start(bf16[3,4,4224]{2,1,0:T(4,128)(2,1)S(1)} %token_rows.3), channel_id=1, source_target_pairs={{0,2},{1,3},{2,0},{3,1},{4,6},{5,7},{6,4},{7,5},{8,10},{9,11},{10,... | collective-permute-start | bytes 304136 | tf_op jit(solution)/shard_map/cond/branch_1_fun/ppermute | solution.py:41
  68.4 1.6 %collective-permute-start.23 = (bf16[3,4,4224]{2,1,0:T(4,128)(2,1)S(1)}, bf16[3,4,4224]{2,1,0:T(4,128)(2,1)S(1)}, u32[]{:S(2)}, u32[]{:S(2)}) collective-permute-start(bf16[3,4,4224]{2,1,0:T(4,128)(2,1)S(1)} %token_rows.3), channel_id=1, source_target_pairs={{0,3},{1,2},{2,1},{3,0},{4,7},{5,6},{6,5},{7,4},{8,11},{9,10},{10,... | collective-permute-start | bytes 304136 | tf_op jit(solution)/shard_map/cond/branch_1_fun/ppermute | solution.py:41
  70.0 0.1 broadcast.7
  70.1 0.1 bitcast_dynamic-update-slice_fusion.7
  70.1 1.5 %collective-permute-done.21 = bf16[3,4,4224]{2,1,0:T(4,128)(2,1)S(1)} collective-permute-done((bf16[3,4,4224]{2,1,0:T(4,128)(2,1)S(1)}, bf16[3,4,4224]{2,1,0:T(4,128)(2,1)S(1)}, u32[]{:S(2)}, u32[]{:S(2)}) %collective-permute-start.21) | collective-permute-done | bytes 101408 | tf_op jit(solution)/shard_map/cond/branch_1_fun/ppermute | solution.py:41
  71.7 0.1 bitcast_dynamic-update-slice_fusion.5
  71.7 3.1 %collective-permute-done.23 = bf16[3,4,4224]{2,1,0:T(4,128)(2,1)S(1)} collective-permute-done((bf16[3,4,4224]{2,1,0:T(4,128)(2,1)S(1)}, bf16[3,4,4224]{2,1,0:T(4,128)(2,1)S(1)}, u32[]{:S(2)}, u32[]{:S(2)}) %collective-permute-start.23) | collective-permute-done | bytes 101408 | tf_op jit(solution)/shard_map/cond/branch_1_fun/ppermute | solution.py:41
  74.8 0.1 bitcast_dynamic-update-slice_fusion.4
  74.9 0.1 collective-permute-start.26
  74.9 0.8 collective-permute-start.24
  75.8 0.9 collective-permute-start.25
  76.7 0.0 collective-permute-done.26.after_ref.refs_3_
  76.7 5.7 %copy-done.1 = bf16[2000,4096]{1,0:T(8,128)(2,1)S(1)} copy-done((bf16[2000,4096]{1,0:T(8,128)(2,1)S(1)}, bf16[2000,4096]{1,0:T(8,128)(2,1)}, u32[]{:S(2)}) %copy-start.1) | copy-done | bytes 16384024 | tf_op jit(solution)/shard_map/cond
  82.3 4.4 %collective-permute-done.24.refs_2_ = bf16[12,4,4224]{2,1,0:T(4,128)(2,1)S(1)} collective-permute-done((bf16[12,4,4224]{2,1,0:T(4,128)(2,1)S(1)}, bf16[12,4,4224]{2,1,0:T(4,128)(2,1)S(1)}, u32[]{:S(2)}, u32[]{:S(2)}) %collective-permute-start.24) | collective-permute-done | bytes 405536 | tf_op jit(solution)/shard_map/cond/branch_1_fun/ppermute | solution.py:41
  86.7 0.5 collective-permute-done.25.refs_0_
  87.2 0.5 collective-permute-start.30
  87.7 0.1 slice.10
  87.8 0.1 slice.11
  87.9 0.9 collective-permute-start.27
  88.8 1.2 %collective-permute-start.28 = (bf16[6,4,4224]{2,1,0:T(4,128)(2,1)S(1)}, bf16[6,4,4224]{2,1,0:T(4,128)(2,1)S(1)}, u32[]{:S(2)}, u32[]{:S(2)}) collective-permute-start(bf16[6,4,4224]{2,1,0:T(4,128)(2,1)S(1)} %slice.11), channel_id=1, source_target_pairs={{0,16},{16,0},{1,17},{17,1},{2,18},{18,2},{3,19},{19,3},{4,20},{20... | collective-permute-start | bytes 608264 | tf_op jit(solution)/shard_map/cond/branch_1_fun/ppermute | solution.py:41
  90.1 5.7 %vocabulary_scores.6.refs_0_ = f32[4,8,48]{2,1,0:T(8,128)S(1)} custom-call(s32[5]{0:T(128)S(1)} %get-tuple-element.74.refs_0_.place_ref.first_ref, f32[8,128]{1,0:T(8,128)S(1)} %vocabulary_rows.3.after_ref, bf16[12,4,4224]{2,1,0:T(4,128)(2,1)S(1)} %collective-permute-done.25.refs_0_, bf16[12,4,4224]{2,1,0:T(4,128)(2,1)S(1)} %collective-permute-done.29.refs_1_, ...), custom_call_target="tpu_custom_call" | custom-call | flops 4718592000 | bytes 1572864 | tf_op jit(solution)/shard_map/cond/branch_1_fun/vocabulary_scores/pallas_call | solution.py:532
  95.8 0.1 constant_dynamic-update-slice_fusion.3
  95.8 0.1 constant_dynamic-update-slice_fusion.2.refs_0_
  95.9 0.1 collective-permute-start.31
  96.0 1.7 %collective-permute-done.31.refs_1_ = bf16[12,4,4224]{2,1,0:T(4,128)(2,1)S(1)} collective-permute-done((bf16[12,4,4224]{2,1,0:T(4,128)(2,1)S(1)}, bf16[12,4,4224]{2,1,0:T(4,128)(2,1)S(1)}, u32[]{:S(2)}, u32[]{:S(2)}) %collective-permute-start.31) | collective-permute-done | bytes 405536 | tf_op jit(solution)/shard_map/cond/branch_1_fun/ppermute | solution.py:41
  97.7 5.7 %vocabulary_scores.7.refs_1_ = f32[4,8,48]{2,1,0:T(8,128)S(1)} custom-call(s32[5]{0:T(128)S(1)} %get-tuple-element.74.refs_0_.place_ref.first_ref, f32[8,128]{1,0:T(8,128)S(1)} %vocabulary_rows.3.after_ref, bf16[12,4,4224]{2,1,0:T(4,128)(2,1)S(1)} %constant_dynamic-update-slice_fusion.2.refs_0_, bf16[12,4,4224]{2,1,0:T(4,128)(2,1)S(1)} %collective-permute-done.31.refs_1_, ...), custom_call_target="tpu_custom_call" | custom-call | flops 4718592000 | bytes 1572864 | tf_op jit(solution)/shard_map/cond/branch_1_fun/vocabulary_scores/pallas_call | solution.py:532
  103.4 0.6 statistics_by_group.3
  104.1 11.2 %all_to_all.14.every_ref = f32[32,8,96]{2,1,0:T(8,128)S(1)} all-to-all(f32[32,8,96]{2,1,0:T(8,128)S(1)} %statistics_by_group.3), channel_id=1, replica_groups=mesh['section'=2,'tm'=4,'mp'=4] {'section','tm','mp'}, dimensions={0} | all-to-all | bytes 196608 | tf_op jit(solution)/shard_map/cond/branch_1_fun/all_to_all | solution.py:31
  115.3 1.3 %hypothesis_scores.3 = f32[2,8]{1,0:T(2,128)} custom-call(s32[5]{0:T(128)S(1)} %get-tuple-element.74.refs_0_.place_ref.first_ref, s32[8]{0:T(128)S(1)} %get-tuple-element.75.refs_1_.slot_ref, s32[2,8]{1,0:T(2,128)S(1)} %get-tuple-element.76.length_ref, f32[32,8,96]{2,1,0:T(8,128)S(1)} %all_to_all.14.every_ref), custom_call_target="tpu_custom_call" | custom-call | tf_op jit(solution)/shard_map/cond/branch_1_fun/hypothesis_scores/pallas_call | solution.py:636
  (26 shorter events, 0.1 us)
Async XLA Ops:
  6.2 18.5 %copy-start.2 = (bf16[1280,1024]{1,0:T(8,128)(2,1)S(1)}, bf16[1280,1024]{1,0:T(8,128)(2,1)}, u32[]{:S(2)}) copy-start(bf16[1280,1024]{1,0:T(8,128)(2,1)} %refs_5_.1) | copy-start | bytes 7864324
  6.2 11.6 %collective-permute-start.36 = (bf16[272,512]{1,0:T(8,128)(2,1)S(1)}, bf16[272,512]{1,0:T(8,128)(2,1)S(1)}, u32[]{:S(2)}, u32[]{:S(2)}) collective-permute-start(bf16[272,512]{1,0:T(8,128)(2,1)S(1)} %get-tuple-element.112), channel_id=1, source_target_pairs={{0,4},{4,0},{8,12},{12,8},{1,5},{5,1},{9,13},{13,9},{2,6},{6,2},{1... | collective-permute-start | bytes 835592 | tf_op jit(solution)/shard_map/ppermute | solution.py:41
  12.4 18.8 %copy-start.4 = (s32[2,8]{1,0:T(2,128)S(1)}, s32[2,8]{1,0:T(2,128)}, u32[]{:S(2)}) copy-start(s32[2,8]{1,0:T(2,128)} %length_ref.1) | copy-start | bytes 196
  12.4 18.9 %copy-start.3 = (s32[8]{0:T(128)S(1)}, s32[8]{0:T(128)}, u32[]{:S(2)}) copy-start(s32[8]{0:T(128)} %slot_ref.1) | copy-start | bytes 100
  12.4 27.2 %copy-start.5 = (s32[4]{0:T(128)S(1)}, s32[4]{0:T(128)}, u32[]{:S(2)}) copy-start(s32[4]{0:T(128)} %param.14) | copy-start | bytes 52
  12.4 7.3 %collective-permute-start.38 = (bf16[32,1280]{1,0:T(8,128)(2,1)S(1)}, bf16[32,1280]{1,0:T(8,128)(2,1)S(1)}, u32[]{:S(2)}, u32[]{:S(2)}) collective-permute-start(bf16[32,1280]{1,0:T(8,128)(2,1)S(1)} %get-tuple-element.114), channel_id=1, source_target_pairs={{0,1},{1,0},{2,3},{3,2},{4,5},{5,4},{6,7},{7,6},{8,9},{9,8},{10,11... | collective-permute-start | bytes 245768 | tf_op jit(solution)/shard_map/ppermute | solution.py:41
  15.2 9.5 %collective-permute-start.39 = (bf16[32,1280]{1,0:T(8,128)(2,1)S(1)}, bf16[32,1280]{1,0:T(8,128)(2,1)S(1)}, u32[]{:S(2)}, u32[]{:S(2)}) collective-permute-start(bf16[32,1280]{1,0:T(8,128)(2,1)S(1)} %get-tuple-element.115), channel_id=1, source_target_pairs={{0,2},{1,3},{2,0},{3,1},{4,6},{5,7},{6,4},{7,5},{8,10},{9,11},{10,... | collective-permute-start | bytes 245768 | tf_op jit(solution)/shard_map/ppermute | solution.py:41
  17.8 6.9 %collective-permute-start.40 = (bf16[32,1280]{1,0:T(8,128)(2,1)S(1)}, bf16[32,1280]{1,0:T(8,128)(2,1)S(1)}, u32[]{:S(2)}, u32[]{:S(2)}) collective-permute-start(bf16[32,1280]{1,0:T(8,128)(2,1)S(1)} %get-tuple-element.116), channel_id=1, source_target_pairs={{0,3},{1,2},{2,1},{3,0},{4,7},{5,6},{6,5},{7,4},{8,11},{9,10},{10,... | collective-permute-start | bytes 245768 | tf_op jit(solution)/shard_map/ppermute | solution.py:41
  17.8 19.9 %collective-permute-start.35 = (bf16[272,512]{1,0:T(8,128)(2,1)S(1)}, bf16[272,512]{1,0:T(8,128)(2,1)S(1)}, u32[]{:S(2)}, u32[]{:S(2)}) collective-permute-start(bf16[272,512]{1,0:T(8,128)(2,1)S(1)} %get-tuple-element.110), channel_id=1, source_target_pairs={{0,4},{4,0},{8,12},{12,8},{1,5},{5,1},{9,13},{13,9},{2,6},{6,2},{1... | collective-permute-start | bytes 835592 | tf_op jit(solution)/shard_map/ppermute | solution.py:41
  17.9 21.7 %collective-permute-start.37 = (bf16[272,512]{1,0:T(8,128)(2,1)S(1)}, bf16[272,512]{1,0:T(8,128)(2,1)S(1)}, u32[]{:S(2)}, u32[]{:S(2)}) collective-permute-start(bf16[272,512]{1,0:T(8,128)(2,1)S(1)} %add.45), channel_id=1, source_target_pairs={{0,8},{4,12},{8,0},{12,4},{1,9},{5,13},{9,1},{13,5},{2,10},{6,14},... | collective-permute-start | bytes 835592 | tf_op jit(solution)/shard_map/ppermute | solution.py:41
  26.2 13.4 %all-to-all-start.2 = ((bf16[32,8,256]{2,1,0:T(8,128)(2,1)}), bf16[32,8,256]{2,1,0:T(8,128)(2,1)S(1)}, u32[]{:S(2)}, u32[]{:S(2)}) async-start(bf16[32,8,256]{2,1,0:T(8,128)(2,1)} %bitcast.20), calls=%async_computation.2 | async-start | bytes 262144 | tf_op jit(solution)/shard_map/all_to_all | solution.py:31
  32.0 1.9 %collective-permute-start.32 = (s32[1]{0:T(128)}, s32[1]{0:T(128)}, u32[]{:S(2)}, u32[]{:S(2)}) collective-permute-start(s32[1]{0:T(128)} %bitcast.12), channel_id=1, source_target_pairs={{0,4},{4,0},{8,12},{12,8},{1,5},{5,1},{9,13},{13,9},{2,6},{6,2},{1... | collective-permute-start | bytes 20 | tf_op jit(solution)/shard_map/ppermute | solution.py:41
  32.3 3.6 %collective-permute-start.33 = (s32[1]{0:T(128)}, s32[1]{0:T(128)}, u32[]{:S(2)}, u32[]{:S(2)}) collective-permute-start(s32[1]{0:T(128)} %bitcast.12), channel_id=1, source_target_pairs={{0,8},{4,12},{8,0},{12,4},{1,9},{5,13},{9,1},{13,5},{2,10},{6,14},... | collective-permute-start | bytes 20 | tf_op jit(solution)/shard_map/ppermute | solution.py:41
  34.0 3.2 %collective-permute-start.34 = (s32[1]{0:T(128)}, s32[1]{0:T(128)}, u32[]{:S(2)}, u32[]{:S(2)}) collective-permute-start(s32[1]{0:T(128)} %bitcast.12), channel_id=1, source_target_pairs={{0,12},{4,8},{8,4},{12,0},{1,13},{5,9},{9,5},{13,1},{2,14},{6,10},... | collective-permute-start | bytes 20 | tf_op jit(solution)/shard_map/ppermute | solution.py:41
  42.8 6.0 %collective-permute-start.16 = (bf16[24,4096]{1,0:T(8,128)(2,1)S(1)}, bf16[24,4096]{1,0:T(8,128)(2,1)S(1)}, u32[]{:S(2)}, u32[]{:S(2)}) collective-permute-start(bf16[24,4096]{1,0:T(8,128)(2,1)S(1)} %get-tuple-element.84), channel_id=1, source_target_pairs={{0,16},{16,0},{1,17},{17,1},{2,18},{18,2},{3,19},{19,3},{4,20},{20... | collective-permute-start | bytes 589832 | tf_op jit(solution)/shard_map/cond/branch_1_fun/ppermute | solution.py:41
  43.7 6.1 %collective-permute-start.17 = (bf16[24,4096]{1,0:T(8,128)(2,1)S(1)}, bf16[24,4096]{1,0:T(8,128)(2,1)S(1)}, u32[]{:S(2)}, u32[]{:S(2)}) collective-permute-start(bf16[24,4096]{1,0:T(8,128)(2,1)S(1)} %get-tuple-element.86), channel_id=1, source_target_pairs={{0,1},{1,0},{2,3},{3,2},{4,5},{5,4},{6,7},{7,6},{8,9},{9,8},{10,11... | collective-permute-start | bytes 589832 | tf_op jit(solution)/shard_map/cond/branch_1_fun/ppermute | solution.py:41
  50.5 5.0 %collective-permute-start.18 = (bf16[12,4096]{1,0:T(8,128)(2,1)S(1)}, bf16[12,4096]{1,0:T(8,128)(2,1)S(1)}, u32[]{:S(2)}, u32[]{:S(2)}) collective-permute-start(bf16[12,4096]{1,0:T(8,128)(2,1)S(1)} %get-tuple-element.88), channel_id=1, source_target_pairs={{0,1},{1,0},{2,3},{3,2},{4,5},{5,4},{6,7},{7,6},{8,9},{9,8},{10,11... | collective-permute-start | bytes 294920 | tf_op jit(solution)/shard_map/cond/branch_1_fun/ppermute | solution.py:41
  51.7 5.0 %collective-permute-start.19 = (bf16[12,4096]{1,0:T(8,128)(2,1)S(1)}, bf16[12,4096]{1,0:T(8,128)(2,1)S(1)}, u32[]{:S(2)}, u32[]{:S(2)}) collective-permute-start(bf16[12,4096]{1,0:T(8,128)(2,1)S(1)} %get-tuple-element.90), channel_id=1, source_target_pairs={{0,16},{16,0},{1,17},{17,1},{2,18},{18,2},{3,19},{19,3},{4,20},{20... | collective-permute-start | bytes 294920 | tf_op jit(solution)/shard_map/cond/branch_1_fun/ppermute | solution.py:41
  57.4 7.4 %collective-permute-start.20 = (bf16[12,4096]{1,0:T(8,128)(2,1)S(1)}, bf16[12,4096]{1,0:T(8,128)(2,1)S(1)}, u32[]{:S(2)}, u32[]{:S(2)}) collective-permute-start(bf16[12,4096]{1,0:T(8,128)(2,1)S(1)} %get-tuple-element.92), channel_id=1, source_target_pairs={{0,2},{1,3},{2,0},{3,1},{4,6},{5,7},{6,4},{7,5},{8,10},{9,11},{10,... | collective-permute-start | bytes 294920 | tf_op jit(solution)/shard_map/cond/branch_1_fun/ppermute | solution.py:41
  65.5 6.1 %collective-permute-start.21 = (bf16[3,4,4224]{2,1,0:T(4,128)(2,1)S(1)}, bf16[3,4,4224]{2,1,0:T(4,128)(2,1)S(1)}, u32[]{:S(2)}, u32[]{:S(2)}) collective-permute-start(bf16[3,4,4224]{2,1,0:T(4,128)(2,1)S(1)} %token_rows.3), channel_id=1, source_target_pairs={{0,1},{1,0},{2,3},{3,2},{4,5},{5,4},{6,7},{7,6},{8,9},{9,8},{10,11... | collective-permute-start | bytes 304136 | tf_op jit(solution)/shard_map/cond/branch_1_fun/ppermute | solution.py:41
  65.6 6.1 %collective-permute-start.22 = (bf16[3,4,4224]{2,1,0:T(4,128)(2,1)S(1)}, bf16[3,4,4224]{2,1,0:T(4,128)(2,1)S(1)}, u32[]{:S(2)}, u32[]{:S(2)}) collective-permute-start(bf16[3,4,4224]{2,1,0:T(4,128)(2,1)S(1)} %token_rows.3), channel_id=1, source_target_pairs={{0,2},{1,3},{2,0},{3,1},{4,6},{5,7},{6,4},{7,5},{8,10},{9,11},{10,... | collective-permute-start | bytes 304136 | tf_op jit(solution)/shard_map/cond/branch_1_fun/ppermute | solution.py:41
  68.4 6.4 %collective-permute-start.23 = (bf16[3,4,4224]{2,1,0:T(4,128)(2,1)S(1)}, bf16[3,4,4224]{2,1,0:T(4,128)(2,1)S(1)}, u32[]{:S(2)}, u32[]{:S(2)}) collective-permute-start(bf16[3,4,4224]{2,1,0:T(4,128)(2,1)S(1)} %token_rows.3), channel_id=1, source_target_pairs={{0,3},{1,2},{2,1},{3,0},{4,7},{5,6},{6,5},{7,4},{8,11},{9,10},{10,... | collective-permute-start | bytes 304136 | tf_op jit(solution)/shard_map/cond/branch_1_fun/ppermute | solution.py:41
  74.9 1.8 %collective-permute-start.26 = (bf16[12,4,4224]{2,1,0:T(4,128)(2,1)S(1)}, bf16[12,4,4224]{2,1,0:T(4,128)(2,1)S(1)}, u32[]{:S(2)}, u32[]{:S(2)}) collective-permute-start(bf16[12,4,4224]{2,1,0:T(4,128)(2,1)S(1)} %bitcast.29), channel_id=1, source_target_pairs={{0,4},{4,0},{8,12},{12,8},{1,5},{5,1},{9,13},{13,9},{2,6},{6,2},{1... | collective-permute-start | bytes 1216520 | tf_op jit(solution)/shard_map/cond/branch_1_fun/ppermute | solution.py:41
  74.9 11.8 %collective-permute-start.24 = (bf16[12,4,4224]{2,1,0:T(4,128)(2,1)S(1)}, bf16[12,4,4224]{2,1,0:T(4,128)(2,1)S(1)}, u32[]{:S(2)}, u32[]{:S(2)}) collective-permute-start(bf16[12,4,4224]{2,1,0:T(4,128)(2,1)S(1)} %bitcast.30), channel_id=1, source_target_pairs={{0,16},{16,0},{1,17},{17,1},{2,18},{18,2},{3,19},{19,3},{4,20},{20... | collective-permute-start | bytes 1216520 | tf_op jit(solution)/shard_map/cond/branch_1_fun/ppermute | solution.py:41
  75.8 11.4 %collective-permute-start.25 = (bf16[12,4,4224]{2,1,0:T(4,128)(2,1)S(1)}, bf16[12,4,4224]{2,1,0:T(4,128)(2,1)S(1)}, u32[]{:S(2)}, u32[]{:S(2)}) collective-permute-start(bf16[12,4,4224]{2,1,0:T(4,128)(2,1)S(1)} %bitcast.31), channel_id=1, source_target_pairs={{0,8},{4,12},{8,0},{12,4},{1,9},{5,13},{9,1},{13,5},{2,10},{6,14},... | collective-permute-start | bytes 1216520 | tf_op jit(solution)/shard_map/cond/branch_1_fun/ppermute | solution.py:41
  76.7 5.7 %copy-start.1 = (bf16[2000,4096]{1,0:T(8,128)(2,1)S(1)}, bf16[2000,4096]{1,0:T(8,128)(2,1)}, u32[]{:S(2)}) copy-start(bf16[2000,4096]{1,0:T(8,128)(2,1)} %get-tuple-element.132.head_ref.refs_4_) | copy-start | bytes 49152004 | tf_op jit(solution)/shard_map/cond
  87.2 2.8 %collective-permute-start.29 = (bf16[12,4,4224]{2,1,0:T(4,128)(2,1)S(1)}, bf16[12,4,4224]{2,1,0:T(4,128)(2,1)S(1)}, u32[]{:S(2)}, u32[]{:S(2)}) collective-permute-start(bf16[12,4,4224]{2,1,0:T(4,128)(2,1)S(1)} %collective-permute-done.25.refs_0_), channel_id=1, source_target_pairs={{0,4},{4,0},{8,12},{12,8},{1,5},{5,1},{9,13},{13,9},{2,6},{6,2},{1... | collective-permute-start | bytes 1216520 | tf_op jit(solution)/shard_map/cond/branch_1_fun/ppermute | solution.py:41
  87.2 2.8 %collective-permute-start.30 = (bf16[12,4,4224]{2,1,0:T(4,128)(2,1)S(1)}, bf16[12,4,4224]{2,1,0:T(4,128)(2,1)S(1)}, u32[]{:S(2)}, u32[]{:S(2)}) collective-permute-start(bf16[12,4,4224]{2,1,0:T(4,128)(2,1)S(1)} %collective-permute-done.24.refs_2_), channel_id=1, source_target_pairs={{0,4},{4,0},{8,12},{12,8},{1,5},{5,1},{9,13},{13,9},{2,6},{6,2},{1... | collective-permute-start | bytes 1216520 | tf_op jit(solution)/shard_map/cond/branch_1_fun/ppermute | solution.py:41
  87.9 7.8 %collective-permute-start.27 = (bf16[6,4,4224]{2,1,0:T(4,128)(2,1)S(1)}, bf16[6,4,4224]{2,1,0:T(4,128)(2,1)S(1)}, u32[]{:S(2)}, u32[]{:S(2)}) collective-permute-start(bf16[6,4,4224]{2,1,0:T(4,128)(2,1)S(1)} %slice.10), channel_id=1, source_target_pairs={{0,8},{4,12},{8,0},{12,4},{1,9},{5,13},{9,1},{13,5},{2,10},{6,14},... | collective-permute-start | bytes 608264 | tf_op jit(solution)/shard_map/cond/branch_1_fun/ppermute | solution.py:41
  88.8 6.9 %collective-permute-start.28 = (bf16[6,4,4224]{2,1,0:T(4,128)(2,1)S(1)}, bf16[6,4,4224]{2,1,0:T(4,128)(2,1)S(1)}, u32[]{:S(2)}, u32[]{:S(2)}) collective-permute-start(bf16[6,4,4224]{2,1,0:T(4,128)(2,1)S(1)} %slice.11), channel_id=1, source_target_pairs={{0,16},{16,0},{1,17},{17,1},{2,18},{18,2},{3,19},{19,3},{4,20},{20... | collective-permute-start | bytes 608264 | tf_op jit(solution)/shard_map/cond/branch_1_fun/ppermute | solution.py:41
  95.9 1.8 %collective-permute-start.31 = (bf16[12,4,4224]{2,1,0:T(4,128)(2,1)S(1)}, bf16[12,4,4224]{2,1,0:T(4,128)(2,1)S(1)}, u32[]{:S(2)}, u32[]{:S(2)}) collective-permute-start(bf16[12,4,4224]{2,1,0:T(4,128)(2,1)S(1)} %constant_dynamic-update-slice_fusion.2.refs_0_), channel_id=1, source_target_pairs={{0,4},{4,0},{8,12},{12,8},{1,5},{5,1},{9,13},{13,9},{2,6},{6,2},{1... | collective-permute-start | bytes 1216520 | tf_op jit(solution)/shard_map/cond/branch_1_fun/ppermute | solution.py:41

commit v22 on v21

--- a/solution.py
+++ b/solution.py
@@ -745,11 +745,12 @@
     parts = [parts[0]] + [
         swap(parts[distance], "mp", distance) for distance in range(1, width_count)
     ]
+    own_frames, lengths = lax.optimization_barrier((own_frames, hyp_len))
 
     blocks = queries_of(
         place,
         slot_utt,
-        hyp_len,
+        lengths,
         place,
         hyp_state.reshape(slot_count, slot_tokens, model_width),
         hyp_tok.reshape(slot_count, 1, slot_tokens),

time: 117 us -> 116 us (level)
  transfers between devices with their start and end apart: 26 -> 26, of which waited for: 14 -> 15; matrix products, arithmetic and copies ran while one was open for 1% -> 1% of each run, Pallas kernels for 11% -> 6%
where the time goes in v22:
time: 116 us
  waiting for transfers between devices  34.2 us (29%)
  Pallas kernels  31.3 us (27%)
  starting transfers between devices  28.9 us (25%)
  blocking collectives  11.4 us (10%)
  local copies, waits for them, and re-layouts  6.47 us (6%)
  between operations  2.69 us (2%)
    ppermute x25, waiting for transfers between devices, swap(): return lax.ppermute(values, axis, pairs)  32.4 us
    ppermute x25, starting transfers between devices, swap(): return lax.ppermute(values, axis, pairs)  23.9 us
    all_to_all x1, blocking collectives, exchange(): return lax.all_to_all(blocks, axis, split_axis=0, concat_axis=0, tiled=True)  11.4 us
    pallas_call x2, Pallas kernels, vocabulary_stats(): pl.pallas_call(functools.partial(vocabulary_kernel, head.shape[0], count)...  11.4 us
    cond x3, local copies, waits for them, and re-layouts  5.73 us
    pallas_call x1, Pallas kernels, ffn(): pl.pallas_call(functools.partial(ffn_kernel, tile, count), in_specs=[SCAL...  5.62 us
    pallas_call x1, Pallas kernels, queries_of(): pl.pallas_call(functools.partial(query_kernel, count, depth), in_specs=[S...  5.46 us
    all_to_all x1, starting transfers between devices, exchange(): return lax.all_to_all(blocks, axis, split_axis=0, concat_axis=0, tiled=True)  5.06 us
  transfers between devices with their start and end apart: 26, of which 15 were waited for; matrix products, arithmetic and copies ran while one was open for 1% of the time, Pallas kernels for 6%

profile of v22, /device:TPU:0, one launch (start us, length us, event | category | flops | bytes accessed | tf_op | source)
XLA Modules:
  0.0 116.0 jit_solution(17000199060950322819)
XLA Ops:
  0.0 0.1 stack.23.place_ref.after_ref
  0.1 5.6 %encoder_ffn.1 = (bf16[32,1280]{1,0:T(8,128)(2,1)S(1)}, bf16[32,1280]{1,0:T(8,128)(2,1)S(1)}, bf16[32,1280]{1,0:T(8,128)(2,1)S(1)}, bf16[32,1280]{1,0:T(8,128)(2,1)S(1)}, bf16[32,1280]{1,0:T(8,128)(2,1)S(1)}) custom-call(s32[5]{0:T(128)S(1)} %stack.23.place_ref.after_ref, bf16[32,4,1280]{2,1,0:T(4,128)(2,1)} %x_ref.1, bf16[1280,1280]{1,0:T(8,128)(2,1)} %up_ref.1, ...), custom_call_target="tpu_custom_call" | custom-call | flops 838860800 | bytes 6553600 | tf_op jit(solution)/shard_map/encoder_ffn/pallas_call | solution.py:124
  5.7 0.1 reshape.27.tok_ref
  5.8 5.5 %hypothesis_queries.1 = (bf16[272,512]{1,0:T(8,128)(2,1)S(1)}, bf16[272,512]{1,0:T(8,128)(2,1)S(1)}, bf16[272,512]{1,0:T(8,128)(2,1)S(1)}, bf16[272,512]{1,0:T(8,128)(2,1)S(1)}) custom-call(s32[5]{0:T(128)S(1)} %stack.23.place_ref.after_ref, s32[8]{0:T(128)S(1)} %copy-done.3, s32[2,8]{1,0:T(2,128)S(1)} %copy-done.4, s32[5]{0:T(128)S(1)} %stack.23.place_ref.after_ref, ...), custom_call_target="tpu_custom_call" | custom-call | flops 1073741824 | bytes 6291456 | tf_op jit(solution)/shard_map/hypothesis_queries/pallas_call | solution.py:228
  11.3 0.5 collective-permute-start.36
  11.8 2.7 %collective-permute-start.38 = (bf16[32,1280]{1,0:T(8,128)(2,1)S(1)}, bf16[32,1280]{1,0:T(8,128)(2,1)S(1)}, u32[]{:S(2)}, u32[]{:S(2)}) collective-permute-start(bf16[32,1280]{1,0:T(8,128)(2,1)S(1)} %get-tuple-element.118), channel_id=1, source_target_pairs={{0,1},{1,0},{2,3},{3,2},{4,5},{5,4},{6,7},{7,6},{8,9},{9,8},{10,11... | collective-permute-start | bytes 245768 | tf_op jit(solution)/shard_map/ppermute | solution.py:41
  14.5 2.6 %collective-permute-start.39 = (bf16[32,1280]{1,0:T(8,128)(2,1)S(1)}, bf16[32,1280]{1,0:T(8,128)(2,1)S(1)}, u32[]{:S(2)}, u32[]{:S(2)}) collective-permute-start(bf16[32,1280]{1,0:T(8,128)(2,1)S(1)} %get-tuple-element.119), channel_id=1, source_target_pairs={{0,2},{1,3},{2,0},{3,1},{4,6},{5,7},{6,4},{7,5},{8,10},{9,11},{10,... | collective-permute-start | bytes 245768 | tf_op jit(solution)/shard_map/ppermute | solution.py:41
  17.1 0.1 add.45
  17.1 1.8 %collective-permute-start.37 = (bf16[272,512]{1,0:T(8,128)(2,1)S(1)}, bf16[272,512]{1,0:T(8,128)(2,1)S(1)}, u32[]{:S(2)}, u32[]{:S(2)}) collective-permute-start(bf16[272,512]{1,0:T(8,128)(2,1)S(1)} %add.45), channel_id=1, source_target_pairs={{0,8},{4,12},{8,0},{12,4},{1,9},{5,13},{9,1},{13,5},{2,10},{6,14},... | collective-permute-start | bytes 835592 | tf_op jit(solution)/shard_map/ppermute | solution.py:41
  18.9 5.0 %collective-permute-done.39.refs_2_ = bf16[32,1280]{1,0:T(8,128)(2,1)S(1)} collective-permute-done((bf16[32,1280]{1,0:T(8,128)(2,1)S(1)}, bf16[32,1280]{1,0:T(8,128)(2,1)S(1)}, u32[]{:S(2)}, u32[]{:S(2)}) %collective-permute-start.39) | collective-permute-done | bytes 81952 | tf_op jit(solution)/shard_map/ppermute | solution.py:41
  23.9 1.6 %frame_keys_values.1 = bf16[256,256]{1,0:T(8,128)(2,1)} custom-call(bf16[32,1280]{1,0:T(8,128)(2,1)S(1)} %get-tuple-element.117.refs_0_, bf16[32,1280]{1,0:T(8,128)(2,1)S(1)} %collective-permute-done.38.refs_1_, bf16[32,1280]{1,0:T(8,128)(2,1)S(1)} %collective-permute-done.39.refs_2_, bf16[32,1280]{1,0:T(8,128)(2,1)S(1)} %collective-permute-done.40.refs_3_, ...), custom_call_target="tpu_custom_call" | custom-call | flops 83886080 | bytes 2621440 | tf_op jit(solution)/shard_map/frame_keys_values/pallas_call | solution.py:287
  25.5 5.1 %all-to-all-start.2 = ((bf16[32,8,256]{2,1,0:T(8,128)(2,1)}), bf16[32,8,256]{2,1,0:T(8,128)(2,1)S(1)}, u32[]{:S(2)}, u32[]{:S(2)}) async-start(bf16[32,8,256]{2,1,0:T(8,128)(2,1)} %bitcast.20), calls=%async_computation.2 | async-start | bytes 262144 | tf_op jit(solution)/shard_map/all_to_all | solution.py:31
  30.6 0.1 reduce_sum.9
  30.7 0.7 fusion
  31.4 0.3 collective-permute-start.32
  31.6 1.7 %collective-permute-start.33 = (s32[1]{0:T(128)}, s32[1]{0:T(128)}, u32[]{:S(2)}, u32[]{:S(2)}) collective-permute-start(s32[1]{0:T(128)} %bitcast.12), channel_id=1, source_target_pairs={{0,8},{4,12},{8,0},{12,4},{1,9},{5,13},{9,1},{13,5},{2,10},{6,14},... | collective-permute-start | bytes 20 | tf_op jit(solution)/shard_map/ppermute | solution.py:41
  34.7 0.7 collective-permute-done.33
  36.0 0.5 collective-permute-done.34
  37.2 1.8 %all-to-all-done.2 = bf16[32,8,256]{2,1,0:T(8,128)(2,1)S(1)} async-done(((bf16[32,8,256]{2,1,0:T(8,128)(2,1)}), bf16[32,8,256]{2,1,0:T(8,128)(2,1)S(1)}, u32[]{:S(2)}, u32[]{:S(2)}) %all-to-all-start.2) | async-done | bytes 131104 | tf_op jit(solution)/shard_map/all_to_all | solution.py:31
  39.0 77.1 %conditional.1 = (f32[2,8]{1,0:T(2,128)}) conditional(s32[]{:T(128)} %bitcast.13, (s32[5]{0:T(128)S(1)}, s32[8]{0:T(128)S(1)}, s32[4]{0:T(128)S(1)}, bf16[272,512]{1,0:T(8,128)(2,1)S(1)}, bf16[272,512]{1,0:T(8,128)(2,1)S(1)}, /*index=5*/bf16[272,512]{1,0:T(8,128)(2,1)S(1)}, bf16[32,8,256]{2,1,0:T(8,128)(2,1)S(1)}, bf16[512,4096]{1,0:T(8,128)(2,1)}, ...), branch_computations={%region_2.3_spmd, %region_3.4_spmd} | conditional | flops 13186891776 | bytes 99451768 | solution.py:776
  39.0 3.2 %attention_projection.3 = (bf16[24,4096]{1,0:T(8,128)(2,1)S(1)}, bf16[24,4096]{1,0:T(8,128)(2,1)S(1)}, bf16[24,4096]{1,0:T(8,128)(2,1)S(1)}, bf16[24,4096]{1,0:T(8,128)(2,1)S(1)}) custom-call(s32[5]{0:T(128)S(1)} %get-tuple-element.74.refs_0_.place_ref.first_ref, s32[8]{0:T(128)S(1)} %get-tuple-element.75.refs_1_.slot_ref, s32[4]{0:T(128)S(1)} %get-tuple-element.132.refs_2_, ...), custom_call_target="tpu_custom_call" | custom-call | flops 452984832 | bytes 4980736 | tf_op jit(solution)/shard_map/cond/branch_1_fun/attention_projection/pallas_call | solution.py:375
  42.2 0.8 collective-permute-start.16
  43.0 0.6 collective-permute-start.17
  43.6 4.6 %collective-permute-done.16.refs_1_ = bf16[24,4096]{1,0:T(8,128)(2,1)S(1)} collective-permute-done((bf16[24,4096]{1,0:T(8,128)(2,1)S(1)}, bf16[24,4096]{1,0:T(8,128)(2,1)S(1)}, u32[]{:S(2)}, u32[]{:S(2)}) %collective-permute-start.16) | collective-permute-done | bytes 196640 | tf_op jit(solution)/shard_map/cond/branch_1_fun/ppermute | solution.py:41
  48.2 0.9 collective-permute-done.17.refs_3_
  49.1 0.8 sum_phase.6
  49.9 1.3 %collective-permute-start.18 = (bf16[12,4096]{1,0:T(8,128)(2,1)S(1)}, bf16[12,4096]{1,0:T(8,128)(2,1)S(1)}, u32[]{:S(2)}, u32[]{:S(2)}) collective-permute-start(bf16[12,4096]{1,0:T(8,128)(2,1)S(1)} %get-tuple-element.88), channel_id=1, source_target_pairs={{0,1},{1,0},{2,3},{3,2},{4,5},{5,4},{6,7},{7,6},{8,9},{9,8},{10,11... | collective-permute-start | bytes 294920 | tf_op jit(solution)/shard_map/cond/branch_1_fun/ppermute | solution.py:41
  51.2 0.7 collective-permute-start.19
  51.9 3.0 %collective-permute-done.18.refs_1_ = bf16[12,4096]{1,0:T(8,128)(2,1)S(1)} collective-permute-done((bf16[12,4096]{1,0:T(8,128)(2,1)S(1)}, bf16[12,4096]{1,0:T(8,128)(2,1)S(1)}, u32[]{:S(2)}, u32[]{:S(2)}) %collective-permute-start.18) | collective-permute-done | bytes 98336 | tf_op jit(solution)/shard_map/cond/branch_1_fun/ppermute | solution.py:41
  54.9 1.2 %collective-permute-done.19.refs_3_ = bf16[12,4096]{1,0:T(8,128)(2,1)S(1)} collective-permute-done((bf16[12,4096]{1,0:T(8,128)(2,1)S(1)}, bf16[12,4096]{1,0:T(8,128)(2,1)S(1)}, u32[]{:S(2)}, u32[]{:S(2)}) %collective-permute-start.19) | collective-permute-done | bytes 98336 | tf_op jit(solution)/shard_map/cond/branch_1_fun/ppermute | solution.py:41
  56.1 0.7 sum_phase.7
  56.8 2.3 %collective-permute-start.20 = (bf16[12,4096]{1,0:T(8,128)(2,1)S(1)}, bf16[12,4096]{1,0:T(8,128)(2,1)S(1)}, u32[]{:S(2)}, u32[]{:S(2)}) collective-permute-start(bf16[12,4096]{1,0:T(8,128)(2,1)S(1)} %get-tuple-element.92), channel_id=1, source_target_pairs={{0,2},{1,3},{2,0},{3,1},{4,6},{5,7},{6,4},{7,5},{8,10},{9,11},{10,... | collective-permute-start | bytes 294920 | tf_op jit(solution)/shard_map/cond/branch_1_fun/ppermute | solution.py:41
  59.1 5.1 %collective-permute-done.20.refs_4_ = bf16[12,4096]{1,0:T(8,128)(2,1)S(1)} collective-permute-done((bf16[12,4096]{1,0:T(8,128)(2,1)S(1)}, bf16[12,4096]{1,0:T(8,128)(2,1)S(1)}, u32[]{:S(2)}, u32[]{:S(2)}) %collective-permute-start.20) | collective-permute-done | bytes 98336 | tf_op jit(solution)/shard_map/cond/branch_1_fun/ppermute | solution.py:41
  64.2 0.7 token_rows.3
  64.9 0.1 collective-permute-start.21
  65.0 2.8 %collective-permute-start.22 = (bf16[3,4,4224]{2,1,0:T(4,128)(2,1)S(1)}, bf16[3,4,4224]{2,1,0:T(4,128)(2,1)S(1)}, u32[]{:S(2)}, u32[]{:S(2)}) collective-permute-start(bf16[3,4,4224]{2,1,0:T(4,128)(2,1)S(1)} %token_rows.3), channel_id=1, source_target_pairs={{0,2},{1,3},{2,0},{3,1},{4,6},{5,7},{6,4},{7,5},{8,10},{9,11},{10,... | collective-permute-start | bytes 304136 | tf_op jit(solution)/shard_map/cond/branch_1_fun/ppermute | solution.py:41
  67.8 1.6 %collective-permute-start.23 = (bf16[3,4,4224]{2,1,0:T(4,128)(2,1)S(1)}, bf16[3,4,4224]{2,1,0:T(4,128)(2,1)S(1)}, u32[]{:S(2)}, u32[]{:S(2)}) collective-permute-start(bf16[3,4,4224]{2,1,0:T(4,128)(2,1)S(1)} %token_rows.3), channel_id=1, source_target_pairs={{0,3},{1,2},{2,1},{3,0},{4,7},{5,6},{6,5},{7,4},{8,11},{9,10},{10,... | collective-permute-start | bytes 304136 | tf_op jit(solution)/shard_map/cond/branch_1_fun/ppermute | solution.py:41
  69.4 0.1 broadcast.7
  69.5 0.1 bitcast_dynamic-update-slice_fusion.7
  69.6 1.5 %collective-permute-done.21 = bf16[3,4,4224]{2,1,0:T(4,128)(2,1)S(1)} collective-permute-done((bf16[3,4,4224]{2,1,0:T(4,128)(2,1)S(1)}, bf16[3,4,4224]{2,1,0:T(4,128)(2,1)S(1)}, u32[]{:S(2)}, u32[]{:S(2)}) %collective-permute-start.21) | collective-permute-done | bytes 101408 | tf_op jit(solution)/shard_map/cond/branch_1_fun/ppermute | solution.py:41
  71.1 0.1 bitcast_dynamic-update-slice_fusion.5
  71.1 3.1 %collective-permute-done.23 = bf16[3,4,4224]{2,1,0:T(4,128)(2,1)S(1)} collective-permute-done((bf16[3,4,4224]{2,1,0:T(4,128)(2,1)S(1)}, bf16[3,4,4224]{2,1,0:T(4,128)(2,1)S(1)}, u32[]{:S(2)}, u32[]{:S(2)}) %collective-permute-start.23) | collective-permute-done | bytes 101408 | tf_op jit(solution)/shard_map/cond/branch_1_fun/ppermute | solution.py:41
  74.2 0.1 bitcast_dynamic-update-slice_fusion.4
  74.3 0.1 collective-permute-start.26
  74.3 0.8 collective-permute-start.24
  75.2 0.7 collective-permute-start.25
  75.9 0.1 collective-permute-done.26.after_ref.refs_3_
  76.1 5.7 %copy-done.1 = bf16[2000,4096]{1,0:T(8,128)(2,1)S(1)} copy-done((bf16[2000,4096]{1,0:T(8,128)(2,1)S(1)}, bf16[2000,4096]{1,0:T(8,128)(2,1)}, u32[]{:S(2)}) %copy-start.1) | copy-done | bytes 16384024 | tf_op jit(solution)/shard_map/cond
  81.7 4.4 %collective-permute-done.24.refs_2_ = bf16[12,4,4224]{2,1,0:T(4,128)(2,1)S(1)} collective-permute-done((bf16[12,4,4224]{2,1,0:T(4,128)(2,1)S(1)}, bf16[12,4,4224]{2,1,0:T(4,128)(2,1)S(1)}, u32[]{:S(2)}, u32[]{:S(2)}) %collective-permute-start.24) | collective-permute-done | bytes 405536 | tf_op jit(solution)/shard_map/cond/branch_1_fun/ppermute | solution.py:41
  86.1 0.5 collective-permute-done.25.refs_0_
  86.7 0.5 collective-permute-start.30
  87.2 0.1 slice.10
  87.2 0.1 slice.11
  87.3 0.8 collective-permute-start.27
  88.1 1.2 %collective-permute-start.28 = (bf16[6,4,4224]{2,1,0:T(4,128)(2,1)S(1)}, bf16[6,4,4224]{2,1,0:T(4,128)(2,1)S(1)}, u32[]{:S(2)}, u32[]{:S(2)}) collective-permute-start(bf16[6,4,4224]{2,1,0:T(4,128)(2,1)S(1)} %slice.11), channel_id=1, source_target_pairs={{0,16},{16,0},{1,17},{17,1},{2,18},{18,2},{3,19},{19,3},{4,20},{20... | collective-permute-start | bytes 608264 | tf_op jit(solution)/shard_map/cond/branch_1_fun/ppermute | solution.py:41
  89.3 5.7 %vocabulary_scores.6.refs_0_ = f32[4,8,48]{2,1,0:T(8,128)S(1)} custom-call(s32[5]{0:T(128)S(1)} %get-tuple-element.74.refs_0_.place_ref.first_ref, f32[8,128]{1,0:T(8,128)S(1)} %vocabulary_rows.3.after_ref, bf16[12,4,4224]{2,1,0:T(4,128)(2,1)S(1)} %collective-permute-done.25.refs_0_, bf16[12,4,4224]{2,1,0:T(4,128)(2,1)S(1)} %collective-permute-done.29.refs_1_, ...), custom_call_target="tpu_custom_call" | custom-call | flops 4718592000 | bytes 1572864 | tf_op jit(solution)/shard_map/cond/branch_1_fun/vocabulary_scores/pallas_call | solution.py:532
  95.0 0.1 constant_dynamic-update-slice_fusion.3
  95.1 0.1 constant_dynamic-update-slice_fusion.2.refs_0_
  95.2 0.1 collective-permute-start.31
  95.2 1.7 %collective-permute-done.31.refs_1_ = bf16[12,4,4224]{2,1,0:T(4,128)(2,1)S(1)} collective-permute-done((bf16[12,4,4224]{2,1,0:T(4,128)(2,1)S(1)}, bf16[12,4,4224]{2,1,0:T(4,128)(2,1)S(1)}, u32[]{:S(2)}, u32[]{:S(2)}) %collective-permute-start.31) | collective-permute-done | bytes 405536 | tf_op jit(solution)/shard_map/cond/branch_1_fun/ppermute | solution.py:41
  97.0 5.7 %vocabulary_scores.7.refs_1_ = f32[4,8,48]{2,1,0:T(8,128)S(1)} custom-call(s32[5]{0:T(128)S(1)} %get-tuple-element.74.refs_0_.place_ref.first_ref, f32[8,128]{1,0:T(8,128)S(1)} %vocabulary_rows.3.after_ref, bf16[12,4,4224]{2,1,0:T(4,128)(2,1)S(1)} %constant_dynamic-update-slice_fusion.2.refs_0_, bf16[12,4,4224]{2,1,0:T(4,128)(2,1)S(1)} %collective-permute-done.31.refs_1_, ...), custom_call_target="tpu_custom_call" | custom-call | flops 4718592000 | bytes 1572864 | tf_op jit(solution)/shard_map/cond/branch_1_fun/vocabulary_scores/pallas_call | solution.py:532
  102.7 0.6 statistics_by_group.3
  103.3 11.4 %all_to_all.14.every_ref = f32[32,8,96]{2,1,0:T(8,128)S(1)} all-to-all(f32[32,8,96]{2,1,0:T(8,128)S(1)} %statistics_by_group.3), channel_id=1, replica_groups=mesh['section'=2,'tm'=4,'mp'=4] {'section','tm','mp'}, dimensions={0} | all-to-all | bytes 196608 | tf_op jit(solution)/shard_map/cond/branch_1_fun/all_to_all | solution.py:31
  114.7 1.3 %hypothesis_scores.3 = f32[2,8]{1,0:T(2,128)} custom-call(s32[5]{0:T(128)S(1)} %get-tuple-element.74.refs_0_.place_ref.first_ref, s32[8]{0:T(128)S(1)} %get-tuple-element.75.refs_1_.slot_ref, s32[2,8]{1,0:T(2,128)S(1)} %get-tuple-element.76.length_ref, f32[32,8,96]{2,1,0:T(8,128)S(1)} %all_to_all.14.every_ref), custom_call_target="tpu_custom_call" | custom-call | tf_op jit(solution)/shard_map/cond/branch_1_fun/hypothesis_scores/pallas_call | solution.py:636
  (28 shorter events, 0.1 us)
Async XLA Ops:
  0.1 5.6 %copy-start.5 = (s32[2,8,16]{2,1,0:T(8,128)S(1)}, s32[2,8,16]{2,1,0:T(8,128)}, u32[]{:S(2)}) copy-start(s32[2,8,16]{2,1,0:T(8,128)} %param.21) | copy-start | bytes 3076
  0.1 5.7 %copy-start.3 = (s32[8]{0:T(128)S(1)}, s32[8]{0:T(128)}, u32[]{:S(2)}) copy-start(s32[8]{0:T(128)} %slot_ref.1) | copy-start | bytes 100
  0.1 5.7 %copy-start.4 = (s32[2,8]{1,0:T(2,128)S(1)}, s32[2,8]{1,0:T(2,128)}, u32[]{:S(2)}) copy-start(s32[2,8]{1,0:T(2,128)} %length_ref) | copy-start | bytes 196
  5.8 18.1 %copy-start.2 = (bf16[1280,1024]{1,0:T(8,128)(2,1)S(1)}, bf16[1280,1024]{1,0:T(8,128)(2,1)}, u32[]{:S(2)}) copy-start(bf16[1280,1024]{1,0:T(8,128)(2,1)} %refs_5_.1) | copy-start | bytes 7864324
  11.3 27.7 %copy-start.6 = (s32[4]{0:T(128)S(1)}, s32[4]{0:T(128)}, u32[]{:S(2)}) copy-start(s32[4]{0:T(128)} %param.14) | copy-start | bytes 52
  11.3 5.8 %collective-permute-start.36 = (bf16[272,512]{1,0:T(8,128)(2,1)S(1)}, bf16[272,512]{1,0:T(8,128)(2,1)S(1)}, u32[]{:S(2)}, u32[]{:S(2)}) collective-permute-start(bf16[272,512]{1,0:T(8,128)(2,1)S(1)} %get-tuple-element.116), channel_id=1, source_target_pairs={{0,4},{4,0},{8,12},{12,8},{1,5},{5,1},{9,13},{13,9},{2,6},{6,2},{1... | collective-permute-start | bytes 835592 | tf_op jit(solution)/shard_map/ppermute | solution.py:41
  11.8 7.1 %collective-permute-start.38 = (bf16[32,1280]{1,0:T(8,128)(2,1)S(1)}, bf16[32,1280]{1,0:T(8,128)(2,1)S(1)}, u32[]{:S(2)}, u32[]{:S(2)}) collective-permute-start(bf16[32,1280]{1,0:T(8,128)(2,1)S(1)} %get-tuple-element.118), channel_id=1, source_target_pairs={{0,1},{1,0},{2,3},{3,2},{4,5},{5,4},{6,7},{7,6},{8,9},{9,8},{10,11... | collective-permute-start | bytes 245768 | tf_op jit(solution)/shard_map/ppermute | solution.py:41
  14.5 9.5 %collective-permute-start.39 = (bf16[32,1280]{1,0:T(8,128)(2,1)S(1)}, bf16[32,1280]{1,0:T(8,128)(2,1)S(1)}, u32[]{:S(2)}, u32[]{:S(2)}) collective-permute-start(bf16[32,1280]{1,0:T(8,128)(2,1)S(1)} %get-tuple-element.119), channel_id=1, source_target_pairs={{0,2},{1,3},{2,0},{3,1},{4,6},{5,7},{6,4},{7,5},{8,10},{9,11},{10,... | collective-permute-start | bytes 245768 | tf_op jit(solution)/shard_map/ppermute | solution.py:41
  17.0 6.9 %collective-permute-start.40 = (bf16[32,1280]{1,0:T(8,128)(2,1)S(1)}, bf16[32,1280]{1,0:T(8,128)(2,1)S(1)}, u32[]{:S(2)}, u32[]{:S(2)}) collective-permute-start(bf16[32,1280]{1,0:T(8,128)(2,1)S(1)} %get-tuple-element.120), channel_id=1, source_target_pairs={{0,3},{1,2},{2,1},{3,0},{4,7},{5,6},{6,5},{7,4},{8,11},{9,10},{10,... | collective-permute-start | bytes 245768 | tf_op jit(solution)/shard_map/ppermute | solution.py:41
  17.1 20.1 %collective-permute-start.35 = (bf16[272,512]{1,0:T(8,128)(2,1)S(1)}, bf16[272,512]{1,0:T(8,128)(2,1)S(1)}, u32[]{:S(2)}, u32[]{:S(2)}) collective-permute-start(bf16[272,512]{1,0:T(8,128)(2,1)S(1)} %get-tuple-element.114), channel_id=1, source_target_pairs={{0,4},{4,0},{8,12},{12,8},{1,5},{5,1},{9,13},{13,9},{2,6},{6,2},{1... | collective-permute-start | bytes 835592 | tf_op jit(solution)/shard_map/ppermute | solution.py:41
  17.1 21.8 %collective-permute-start.37 = (bf16[272,512]{1,0:T(8,128)(2,1)S(1)}, bf16[272,512]{1,0:T(8,128)(2,1)S(1)}, u32[]{:S(2)}, u32[]{:S(2)}) collective-permute-start(bf16[272,512]{1,0:T(8,128)(2,1)S(1)} %add.45), channel_id=1, source_target_pairs={{0,8},{4,12},{8,0},{12,4},{1,9},{5,13},{9,1},{13,5},{2,10},{6,14},... | collective-permute-start | bytes 835592 | tf_op jit(solution)/shard_map/ppermute | solution.py:41
  25.5 13.5 %all-to-all-start.2 = ((bf16[32,8,256]{2,1,0:T(8,128)(2,1)}), bf16[32,8,256]{2,1,0:T(8,128)(2,1)S(1)}, u32[]{:S(2)}, u32[]{:S(2)}) async-start(bf16[32,8,256]{2,1,0:T(8,128)(2,1)} %bitcast.20), calls=%async_computation.2 | async-start | bytes 262144 | tf_op jit(solution)/shard_map/all_to_all | solution.py:31
  31.4 1.9 %collective-permute-start.32 = (s32[1]{0:T(128)}, s32[1]{0:T(128)}, u32[]{:S(2)}, u32[]{:S(2)}) collective-permute-start(s32[1]{0:T(128)} %bitcast.12), channel_id=1, source_target_pairs={{0,4},{4,0},{8,12},{12,8},{1,5},{5,1},{9,13},{13,9},{2,6},{6,2},{1... | collective-permute-start | bytes 20 | tf_op jit(solution)/shard_map/ppermute | solution.py:41
  31.6 3.8 %collective-permute-start.33 = (s32[1]{0:T(128)}, s32[1]{0:T(128)}, u32[]{:S(2)}, u32[]{:S(2)}) collective-permute-start(s32[1]{0:T(128)} %bitcast.12), channel_id=1, source_target_pairs={{0,8},{4,12},{8,0},{12,4},{1,9},{5,13},{9,1},{13,5},{2,10},{6,14},... | collective-permute-start | bytes 20 | tf_op jit(solution)/shard_map/ppermute | solution.py:41
  33.3 3.2 %collective-permute-start.34 = (s32[1]{0:T(128)}, s32[1]{0:T(128)}, u32[]{:S(2)}, u32[]{:S(2)}) collective-permute-start(s32[1]{0:T(128)} %bitcast.12), channel_id=1, source_target_pairs={{0,12},{4,8},{8,4},{12,0},{1,13},{5,9},{9,5},{13,1},{2,14},{6,10},... | collective-permute-start | bytes 20 | tf_op jit(solution)/shard_map/ppermute | solution.py:41
  42.2 6.0 %collective-permute-start.16 = (bf16[24,4096]{1,0:T(8,128)(2,1)S(1)}, bf16[24,4096]{1,0:T(8,128)(2,1)S(1)}, u32[]{:S(2)}, u32[]{:S(2)}) collective-permute-start(bf16[24,4096]{1,0:T(8,128)(2,1)S(1)} %get-tuple-element.84), channel_id=1, source_target_pairs={{0,16},{16,0},{1,17},{17,1},{2,18},{18,2},{3,19},{19,3},{4,20},{20... | collective-permute-start | bytes 589832 | tf_op jit(solution)/shard_map/cond/branch_1_fun/ppermute | solution.py:41
  43.0 6.1 %collective-permute-start.17 = (bf16[24,4096]{1,0:T(8,128)(2,1)S(1)}, bf16[24,4096]{1,0:T(8,128)(2,1)S(1)}, u32[]{:S(2)}, u32[]{:S(2)}) collective-permute-start(bf16[24,4096]{1,0:T(8,128)(2,1)S(1)} %get-tuple-element.86), channel_id=1, source_target_pairs={{0,1},{1,0},{2,3},{3,2},{4,5},{5,4},{6,7},{7,6},{8,9},{9,8},{10,11... | collective-permute-start | bytes 589832 | tf_op jit(solution)/shard_map/cond/branch_1_fun/ppermute | solution.py:41
  49.9 5.0 %collective-permute-start.18 = (bf16[12,4096]{1,0:T(8,128)(2,1)S(1)}, bf16[12,4096]{1,0:T(8,128)(2,1)S(1)}, u32[]{:S(2)}, u32[]{:S(2)}) collective-permute-start(bf16[12,4096]{1,0:T(8,128)(2,1)S(1)} %get-tuple-element.88), channel_id=1, source_target_pairs={{0,1},{1,0},{2,3},{3,2},{4,5},{5,4},{6,7},{7,6},{8,9},{9,8},{10,11... | collective-permute-start | bytes 294920 | tf_op jit(solution)/shard_map/cond/branch_1_fun/ppermute | solution.py:41
  51.2 5.0 %collective-permute-start.19 = (bf16[12,4096]{1,0:T(8,128)(2,1)S(1)}, bf16[12,4096]{1,0:T(8,128)(2,1)S(1)}, u32[]{:S(2)}, u32[]{:S(2)}) collective-permute-start(bf16[12,4096]{1,0:T(8,128)(2,1)S(1)} %get-tuple-element.90), channel_id=1, source_target_pairs={{0,16},{16,0},{1,17},{17,1},{2,18},{18,2},{3,19},{19,3},{4,20},{20... | collective-permute-start | bytes 294920 | tf_op jit(solution)/shard_map/cond/branch_1_fun/ppermute | solution.py:41
  56.8 7.4 %collective-permute-start.20 = (bf16[12,4096]{1,0:T(8,128)(2,1)S(1)}, bf16[12,4096]{1,0:T(8,128)(2,1)S(1)}, u32[]{:S(2)}, u32[]{:S(2)}) collective-permute-start(bf16[12,4096]{1,0:T(8,128)(2,1)S(1)} %get-tuple-element.92), channel_id=1, source_target_pairs={{0,2},{1,3},{2,0},{3,1},{4,6},{5,7},{6,4},{7,5},{8,10},{9,11},{10,... | collective-permute-start | bytes 294920 | tf_op jit(solution)/shard_map/cond/branch_1_fun/ppermute | solution.py:41
  64.9 6.1 %collective-permute-start.21 = (bf16[3,4,4224]{2,1,0:T(4,128)(2,1)S(1)}, bf16[3,4,4224]{2,1,0:T(4,128)(2,1)S(1)}, u32[]{:S(2)}, u32[]{:S(2)}) collective-permute-start(bf16[3,4,4224]{2,1,0:T(4,128)(2,1)S(1)} %token_rows.3), channel_id=1, source_target_pairs={{0,1},{1,0},{2,3},{3,2},{4,5},{5,4},{6,7},{7,6},{8,9},{9,8},{10,11... | collective-permute-start | bytes 304136 | tf_op jit(solution)/shard_map/cond/branch_1_fun/ppermute | solution.py:41
  65.0 6.1 %collective-permute-start.22 = (bf16[3,4,4224]{2,1,0:T(4,128)(2,1)S(1)}, bf16[3,4,4224]{2,1,0:T(4,128)(2,1)S(1)}, u32[]{:S(2)}, u32[]{:S(2)}) collective-permute-start(bf16[3,4,4224]{2,1,0:T(4,128)(2,1)S(1)} %token_rows.3), channel_id=1, source_target_pairs={{0,2},{1,3},{2,0},{3,1},{4,6},{5,7},{6,4},{7,5},{8,10},{9,11},{10,... | collective-permute-start | bytes 304136 | tf_op jit(solution)/shard_map/cond/branch_1_fun/ppermute | solution.py:41
  67.8 6.4 %collective-permute-start.23 = (bf16[3,4,4224]{2,1,0:T(4,128)(2,1)S(1)}, bf16[3,4,4224]{2,1,0:T(4,128)(2,1)S(1)}, u32[]{:S(2)}, u32[]{:S(2)}) collective-permute-start(bf16[3,4,4224]{2,1,0:T(4,128)(2,1)S(1)} %token_rows.3), channel_id=1, source_target_pairs={{0,3},{1,2},{2,1},{3,0},{4,7},{5,6},{6,5},{7,4},{8,11},{9,10},{10,... | collective-permute-start | bytes 304136 | tf_op jit(solution)/shard_map/cond/branch_1_fun/ppermute | solution.py:41
  74.3 1.8 %collective-permute-start.26 = (bf16[12,4,4224]{2,1,0:T(4,128)(2,1)S(1)}, bf16[12,4,4224]{2,1,0:T(4,128)(2,1)S(1)}, u32[]{:S(2)}, u32[]{:S(2)}) collective-permute-start(bf16[12,4,4224]{2,1,0:T(4,128)(2,1)S(1)} %bitcast.29), channel_id=1, source_target_pairs={{0,4},{4,0},{8,12},{12,8},{1,5},{5,1},{9,13},{13,9},{2,6},{6,2},{1... | collective-permute-start | bytes 1216520 | tf_op jit(solution)/shard_map/cond/branch_1_fun/ppermute | solution.py:41
  74.3 11.8 %collective-permute-start.24 = (bf16[12,4,4224]{2,1,0:T(4,128)(2,1)S(1)}, bf16[12,4,4224]{2,1,0:T(4,128)(2,1)S(1)}, u32[]{:S(2)}, u32[]{:S(2)}) collective-permute-start(bf16[12,4,4224]{2,1,0:T(4,128)(2,1)S(1)} %bitcast.30), channel_id=1, source_target_pairs={{0,16},{16,0},{1,17},{17,1},{2,18},{18,2},{3,19},{19,3},{4,20},{20... | collective-permute-start | bytes 1216520 | tf_op jit(solution)/shard_map/cond/branch_1_fun/ppermute | solution.py:41
  75.2 11.4 %collective-permute-start.25 = (bf16[12,4,4224]{2,1,0:T(4,128)(2,1)S(1)}, bf16[12,4,4224]{2,1,0:T(4,128)(2,1)S(1)}, u32[]{:S(2)}, u32[]{:S(2)}) collective-permute-start(bf16[12,4,4224]{2,1,0:T(4,128)(2,1)S(1)} %bitcast.31), channel_id=1, source_target_pairs={{0,8},{4,12},{8,0},{12,4},{1,9},{5,13},{9,1},{13,5},{2,10},{6,14},... | collective-permute-start | bytes 1216520 | tf_op jit(solution)/shard_map/cond/branch_1_fun/ppermute | solution.py:41
  76.1 5.7 %copy-start.1 = (bf16[2000,4096]{1,0:T(8,128)(2,1)S(1)}, bf16[2000,4096]{1,0:T(8,128)(2,1)}, u32[]{:S(2)}) copy-start(bf16[2000,4096]{1,0:T(8,128)(2,1)} %get-tuple-element.136.head_ref.refs_4_) | copy-start | bytes 49152004 | tf_op jit(solution)/shard_map/cond
  86.6 2.6 %collective-permute-start.29 = (bf16[12,4,4224]{2,1,0:T(4,128)(2,1)S(1)}, bf16[12,4,4224]{2,1,0:T(4,128)(2,1)S(1)}, u32[]{:S(2)}, u32[]{:S(2)}) collective-permute-start(bf16[12,4,4224]{2,1,0:T(4,128)(2,1)S(1)} %collective-permute-done.25.refs_0_), channel_id=1, source_target_pairs={{0,4},{4,0},{8,12},{12,8},{1,5},{5,1},{9,13},{13,9},{2,6},{6,2},{1... | collective-permute-start | bytes 1216520 | tf_op jit(solution)/shard_map/cond/branch_1_fun/ppermute | solution.py:41
  86.7 2.6 %collective-permute-start.30 = (bf16[12,4,4224]{2,1,0:T(4,128)(2,1)S(1)}, bf16[12,4,4224]{2,1,0:T(4,128)(2,1)S(1)}, u32[]{:S(2)}, u32[]{:S(2)}) collective-permute-start(bf16[12,4,4224]{2,1,0:T(4,128)(2,1)S(1)} %collective-permute-done.24.refs_2_), channel_id=1, source_target_pairs={{0,4},{4,0},{8,12},{12,8},{1,5},{5,1},{9,13},{13,9},{2,6},{6,2},{1... | collective-permute-start | bytes 1216520 | tf_op jit(solution)/shard_map/cond/branch_1_fun/ppermute | solution.py:41
  87.3 7.7 %collective-permute-start.27 = (bf16[6,4,4224]{2,1,0:T(4,128)(2,1)S(1)}, bf16[6,4,4224]{2,1,0:T(4,128)(2,1)S(1)}, u32[]{:S(2)}, u32[]{:S(2)}) collective-permute-start(bf16[6,4,4224]{2,1,0:T(4,128)(2,1)S(1)} %slice.10), channel_id=1, source_target_pairs={{0,8},{4,12},{8,0},{12,4},{1,9},{5,13},{9,1},{13,5},{2,10},{6,14},... | collective-permute-start | bytes 608264 | tf_op jit(solution)/shard_map/cond/branch_1_fun/ppermute | solution.py:41
  88.1 6.9 %collective-permute-start.28 = (bf16[6,4,4224]{2,1,0:T(4,128)(2,1)S(1)}, bf16[6,4,4224]{2,1,0:T(4,128)(2,1)S(1)}, u32[]{:S(2)}, u32[]{:S(2)}) collective-permute-start(bf16[6,4,4224]{2,1,0:T(4,128)(2,1)S(1)} %slice.11), channel_id=1, source_target_pairs={{0,16},{16,0},{1,17},{17,1},{2,18},{18,2},{3,19},{19,3},{4,20},{20... | collective-permute-start | bytes 608264 | tf_op jit(solution)/shard_map/cond/branch_1_fun/ppermute | solution.py:41
  95.2 1.8 %collective-permute-start.31 = (bf16[12,4,4224]{2,1,0:T(4,128)(2,1)S(1)}, bf16[12,4,4224]{2,1,0:T(4,128)(2,1)S(1)}, u32[]{:S(2)}, u32[]{:S(2)}) collective-permute-start(bf16[12,4,4224]{2,1,0:T(4,128)(2,1)S(1)} %constant_dynamic-update-slice_fusion.2.refs_0_), channel_id=1, source_target_pairs={{0,4},{4,0},{8,12},{12,8},{1,5},{5,1},{9,13},{13,9},{2,6},{6,2},{1... | collective-permute-start | bytes 1216520 | tf_op jit(solution)/shard_map/cond/branch_1_fun/ppermute | solution.py:41
